TPU v7x, 32 devices: a whole 2x2x4 slice. The times are simulated.
32 devices in a mesh: groups: 2 (over y), seq: 4 (over z), cuts: 4 (over x, core).
Axes of the slice: x: 2, y: 2, z: 4, core: 2. Of those that a mesh axis runs over, the one named last changes fastest.
Arguments:
- queries: bfloat16 [2048, 2048], P(('groups', 'seq'), 'cuts'), parts along dimension 0, may hold values from -56 to 56
- keyvals: bfloat16 [2048, 1024], P(('groups', 'seq'), 'cuts'), parts along dimension 0, may hold values from -5 to 5
- preceding_keyvalues: bfloat16 [256, 1024], P('groups', 'cuts'), parts along dimension 0, may hold values from -5 to 5
- attention_sink_logits: float32 [32], P('cuts'), may hold values from 3 to 7
- residual: bfloat16 [2048, 2880], P(('groups', 'seq'), 'cuts'), parts along dimension 0, may hold values from -24 to 24
- w_out: bfloat16 [2048, 2880], P(None, 'cuts'), may hold values from -0.75 to 0.75
- norm_gain: float32 [2880], replicated, may hold values from 0.5 to 1.5
- expert_ids: int32 [2048, 4], P(('groups', 'seq')), parts along dimension 0, may hold values from 0 to 127, all different within a row; in each aligned block of 256 rows (0 to 255, 256 to 511, ...) at most 16 rows name the same one
- route_weights: float32 [2048, 4], P(('groups', 'seq')), parts along dimension 0, may hold values from 0.1 to 1
- w_gate: bfloat16 [4, 2880, 1440], P('seq', None, 'cuts'), may hold values from -0.109375 to 0.109375
- w_up: bfloat16 [4, 2880, 1440], P('seq', None, 'cuts'), may hold values from -0.109375 to 0.109375
- w_down: bfloat16 [4, 1440, 2880], P('seq', 'cuts'), may hold values from -0.15625 to 0.15625
Outputs:
- layer_out: bfloat16 [2048, 2880], P(('groups', 'seq'), 'cuts'), parts along dimension 0
There are 2 independent parts, one for each index of `groups`. A program takes and returns all parts, laid end to end along the dimension named above; an argument that names none is the same for every part. Nothing has to cross between parts.
Inputs may be any that keep to these rules, and one draw needn't show every extreme that they name: `expert_ids`: the 4 experts of a token differ. Among the 256 rows of one device no expert is named by more than 16 rows, and in every draw some expert is named by exactly 16 rows of some device.
All inputs are finite; a program needn't handle non-finite values.
Results may differ from a plain program's by a relative error of at most 0.0038.
Values may be sent and summed in bfloat16 or wider, within the bound.
No kernel may reach another device: no remote copies, remote signals or barrier semaphores. Data moves between devices by JAX's collectives and lax.ppermute only.
A program may use at most 64 MiB of HBM per device.

v0:
```python
import jax
import jax.numpy as jnp
from jax import lax
from jax.sharding import PartitionSpec as P

D = 2880
HEAD_SIZE = 64
KEYS_SEEN = 128
CAP = 16


norm_eps = 1e-05
glu_alpha = 1.702


def passed_along(block, axis, distance):
    devices = range(lax.axis_size(axis))
    route = [(i - distance, i) for i in devices if i - distance in devices]
    return lax.ppermute(block, axis, route)


def attend(queries, keyvals, rim_rows, attention_sink_logits):
    tok_rows = queries.shape[0]
    kv_heads = keyvals.shape[1] // (2 * HEAD_SIZE)
    queries_per_group = queries.shape[1] // (kv_heads * HEAD_SIZE)
    head_scale = HEAD_SIZE ** (-0.5)
    joined_keys = jnp.concatenate([rim_rows, keyvals], axis=0).reshape(
        KEYS_SEEN + tok_rows, kv_heads, 2, HEAD_SIZE
    )
    query_head_rows = queries.reshape(tok_rows, kv_heads, queries_per_group, HEAD_SIZE)
    scores = (
        jnp.einsum(
            "tkgd,skd->kgts",
            query_head_rows,
            joined_keys[:, :, 0, :],
            preferred_element_type=jnp.float32,
        )
        * head_scale
    )
    row_ids = jnp.arange(tok_rows, dtype=jnp.int32)[:, None]
    col_ids = jnp.arange(KEYS_SEEN + tok_rows, dtype=jnp.int32)[None, :]
    allowed = (col_ids > row_ids) & (col_ids <= row_ids + KEYS_SEEN)
    scores = jnp.where(allowed[None, None, :, :], scores, -jnp.inf)
    local_sink_logit = attention_sink_logits.reshape(kv_heads, queries_per_group)[:, :, None]
    peak = jnp.maximum(jnp.max(scores, axis=3), local_sink_logit)
    exp_terms = jnp.exp(scores - peak[..., None])
    denom = jnp.sum(exp_terms, axis=3) + jnp.exp(local_sink_logit - peak)
    probs = (exp_terms / denom[..., None]).astype(jnp.bfloat16)
    outputs = jnp.einsum(
        "kgts,skd->tkgd", probs, joined_keys[:, :, 1, :], preferred_element_type=jnp.float32
    )
    return outputs.astype(jnp.bfloat16).reshape(tok_rows, kv_heads * queries_per_group * HEAD_SIZE)


def slot_tables(expert_ids, route_weights, live_count):
    experts_held = jnp.arange(live_count, dtype=jnp.int32)
    is_named = expert_ids[:, :, None] == experts_held[None, None, :]
    chosen = jnp.any(is_named, axis=1).astype(jnp.int32)
    before = jnp.cumsum(chosen, axis=0, dtype=jnp.int32) - chosen
    ranking = jnp.sum(jnp.where(is_named, before[:, None, :], 0), axis=2, dtype=jnp.int32)
    target = jnp.where(expert_ids < live_count, expert_ids * CAP + ranking, -1)
    slot_ids = jnp.arange(live_count * CAP, dtype=jnp.int32)
    matches = target[None, :, :] == slot_ids[:, None, None]
    placing = jnp.any(matches, axis=2).astype(jnp.bfloat16)
    mixing = jnp.sum(jnp.where(matches, route_weights[None, :, :], 0.0), axis=2)
    return (placing, mixing)


def shards(
    queries,
    keyvals,
    preceding_keyvalues,
    attention_sink_logits,
    residual,
    w_out,
    norm_gain,
    expert_ids,
    route_weights,
    w_gate,
    w_up,
    w_down,
):
    feat_dev = residual.shape[1]
    live_count = w_gate.shape[0] * lax.axis_size("seq")
    tail_rows = keyvals[keyvals.shape[0] - KEYS_SEEN :]
    shifted = passed_along(tail_rows, "seq", 1)
    rim_rows = jnp.where(lax.axis_index("seq") == 0, preceding_keyvalues, shifted)
    attended = attend(queries, keyvals, rim_rows, attention_sink_logits)
    projected = jnp.dot(
        lax.all_gather(attended, "cuts", axis=1, tiled=True),
        w_out,
        preferred_element_type=jnp.float32,
    )
    resid_rows = (residual.astype(jnp.float32) + projected).astype(jnp.bfloat16)
    placing, mixing = slot_tables(expert_ids, route_weights, live_count)
    gate_here = w_gate[0]
    up_here = w_up[0]
    down_here = w_down[0]
    full_rows = lax.all_gather(resid_rows, "cuts", axis=1, tiled=True)
    wide_rows = full_rows.astype(jnp.float32)
    row_scale = lax.rsqrt(jnp.mean(wide_rows * wide_rows, axis=1, keepdims=True) + norm_eps)
    normed = (wide_rows * row_scale * norm_gain[None, :]).astype(jnp.bfloat16)
    outgoing = jnp.dot(placing, normed, preferred_element_type=jnp.float32).astype(jnp.bfloat16)
    arrived = lax.all_to_all(
        outgoing.reshape(live_count, CAP, D), "seq", split_axis=0, concat_axis=0, tiled=True
    )
    arrived = arrived.reshape(live_count * CAP, D)
    gate_sum = jnp.dot(arrived, gate_here, preferred_element_type=jnp.float32)
    up_sum = jnp.dot(arrived, up_here, preferred_element_type=jnp.float32)
    activated = ((up_sum + 1.0) * gate_sum * jax.nn.sigmoid(glu_alpha * gate_sum)).astype(
        jnp.bfloat16
    )
    summed = lax.psum_scatter(
        lax.dot_general(
            down_here, activated, (((0,), (1,)), ((), ())), preferred_element_type=jnp.float32
        ).astype(jnp.bfloat16),
        "cuts",
        scatter_dimension=0,
        tiled=True,
    )
    expert_out = summed.reshape(feat_dev, live_count, CAP)
    returned = lax.all_to_all(expert_out, "seq", split_axis=1, concat_axis=1, tiled=True).reshape(
        feat_dev, live_count * CAP
    )
    mixed_in = lax.dot_general(
        mixing,
        returned.astype(jnp.float32),
        (((0,), (1,)), ((), ())),
        precision=lax.Precision.HIGHEST,
        preferred_element_type=jnp.float32,
    )
    return (resid_rows.astype(jnp.float32) + mixed_in).astype(jnp.bfloat16)


def solution(mesh):
    placed = (
        P(("groups", "seq"), "cuts"),
        P(("groups", "seq"), "cuts"),
        P("groups", "cuts"),
        P("cuts"),
        P(("groups", "seq"), "cuts"),
        P(None, "cuts"),
        P(),
        P(("groups", "seq"), None),
        P(("groups", "seq"), None),
        P("seq", None, "cuts"),
        P("seq", None, "cuts"),
        P("seq", "cuts", None),
    )
    return jax.shard_map(
        shards, mesh=mesh, in_specs=placed, out_specs=P(("groups", "seq"), "cuts"), check_vma=False
    )
```

profile of v0, /device:TPU:0, one launch (start us, length us, event | category | flops | bytes accessed | tf_op | source)
XLA Modules:
  0.0 130.4 jit_solution(1180500122743205695)
XLA Ops:
  6.5 0.0 copy-start
  6.5 0.0 all-gather.3.cloned.1.call-start
  6.5 1.2 copy.47
  7.7 0.6 slice.20
  8.3 5.5 %collective-permute-start = (bf16[128,256]{0,1:T(8,128)(2,1)}, bf16[128,256]{0,1:T(8,128)(2,1)}, u32[]{:S(2)}, u32[]{:S(2)}) collective-permute-start(bf16[128,256]{0,1:T(8,128)(2,1)} %slice.20), channel_id=1, source_target_pairs={{0,4},{4,8},{8,12},{1,5},{5,9},{9,13},{2,6},{6,10},{10,14},{3,7},{... | collective-permute-start | bytes 196616 | tf_op jit(solution)/shard_map/ppermute | solution.py:19
  13.9 0.1 fusion.32
  14.0 1.0 copy.48
  14.9 1.1 copy.52
  16.0 0.7 max.17
  16.7 0.0 collective-permute-done
  16.8 0.7 fusion.5
  17.5 0.1 broadcast_maximum_fusion
  17.5 0.7 fusion.4
  18.2 0.1 exponential_add_fusion
  18.3 1.7 %fusion.17 = bf16[2,64,4,256]{3,1,2,0:T(8,128)(2,1)} fusion(f32[2,384,256,4]{2,1,3,0:T(8,128)S(1)} %get-tuple-element.6, f32[2,4,256]{2,1,0:T(4,128)S(1)} %exponential_add_fusion, f32[2,4,256]{2,1,0:T(4,128)S(1)} %broadcast_maximum_fusion, pred[256,384]{0,1:T(8,128)(4,1)S(1)} %fusion.32, bf16[384,2,2,64]{0,3,2,1:T(8,128)(2,1)S(1)} %bitcast.85), kind=kOutput, calls=%fused_computation.25 | convolution fusion | flops 104726528 | bytes 3620864 | tf_op jit(solution)/shard_map/kgts,skd->tkgd/dot_general | solution.py:49
  20.0 0.0 all-gather.3.cloned.1.call-update
  20.0 0.0 copy-start.2
  20.0 0.0 copy-start.4
  20.0 0.0 all-gather.5.cloned.1.call-start
  20.1 18.4 %all-gather.3.cloned.1.call-done = bf16[256,2048]{0,1:T(8,128)(2,1)} async-done(((bf16[256,512]{0,1:T(8,128)(2,1)}), bf16[256,2048]{0,1:T(8,128)(2,1)}) %all-gather.3.cloned.1.call-update) | async-done | bytes 1048592 | tf_op jit(solution)/shard_map/all_gather | solution.py:90
  38.5 0.0 copy-done
  38.5 3.0 %fusion.15 = bf16[256,720]{0,1:T(8,128)(2,1)} fusion(bf16[2048,720]{0,1:T(8,128)(2,1)S(1)} %copy-done, bf16[256,2048]{0,1:T(8,128)(2,1)} %all-gather.3.cloned.1.call-done, bf16[256,720]{0,1:T(8,128)(2,1)} %param.16), kind=kOutput, calls=%fused_computation.23 | convolution fusion | flops 755527680 | bytes 4734976 | tf_op jit(solution)/shard_map/dot_general | solution.py:89
  41.4 0.0 all-gather.5.cloned.1.call-update
  41.5 0.0 reduce-scatter.4.cloned.1.call-start
  41.5 0.0 copy-done.2
  41.6 1.2 reduce-window.6
  42.8 0.1 slice.23
  42.9 0.1 copy.54
  43.0 0.1 copy.55
  43.1 0.1 add_bitcast_fusion
  43.3 17.5 %all-gather.5.cloned.1.call-done = bf16[256,2880]{0,1:T(8,128)(2,1)} async-done(((bf16[256,720]{0,1:T(8,128)(2,1)}), bf16[256,2880]{0,1:T(8,128)(2,1)}) %all-gather.5.cloned.1.call-update) | async-done | bytes 1474576 | tf_op jit(solution)/shard_map/all_gather | solution.py:99
  60.7 0.0 copy-start.1
  60.7 1.9 %fusion.1 = f32[256]{0:T(256)S(1)} fusion(bf16[256,2880]{0,1:T(8,128)(2,1)} %all-gather.5.cloned.1.call-done), kind=kLoop, calls=%fused_computation.8 | loop fusion | flops 2211584 | bytes 1475584 | tf_op jit(solution)/shard_map/reduce_sum | solution.py:101
  62.7 0.0 copy-done.4
  62.7 2.0 %convolution_convert_fusion.1 = bf16[64,2880]{1,0:T(8,128)(2,1)S(1)} fusion(pred[64,256]{1,0:T(8,128)(4,1)S(1)} %fusion.33, bf16[256,2880]{0,1:T(8,128)(2,1)} %all-gather.5.cloned.1.call-done, f32[2880]{0:T(1024)S(1)} %copy-done.4, f32[256]{0:T(256)S(1)} %add_rsqrt_fusion), kind=kOutput, calls=%fused_computation.3 | convolution fusion | flops 97505280 | bytes 1872128 | tf_op jit(solution)/shard_map/dot_general | solution.py:103
  64.7 16.1 %all_to_all.10 = bf16[4,16,2880]{2,1,0:T(8,128)(2,1)S(1)} all-to-all(bf16[4,16,2880]{2,1,0:T(8,128)(2,1)S(1)} %bitcast.87), channel_id=1, replica_groups=mesh['groups'=2,'seq'=4,'cuts'=4] {'seq'}, dimensions={0} | all-to-all | bytes 737280 | tf_op jit(solution)/shard_map/all_to_all | solution.py:104
  80.8 0.0 copy-done.1
  80.8 0.7 fusion.7
  81.6 0.0 copy-start.3
  81.6 4.6 %fusion = bf16[2880,64]{0,1:T(8,128)(2,1)} fusion(bf16[1,360,2880]{2,1,0:T(8,128)(2,1)} %param.23, f32[64,360]{1,0:T(8,128)S(1)} %fusion.7, bf16[64,2880]{1,0:T(8,128)(2,1)S(1)} %bitcast.82, bf16[1,2880,360]{1,2,0:T(8,128)(2,1)} %param.22), kind=kOutput, calls=%fused_computation.4 | convolution fusion | flops 265789440 | bytes 4976640 | tf_op jit(solution)/shard_map/dot_general | solution.py:114
  86.1 2.1 %copy.59 = bf16[2880,64]{1,0:T(8,128)(2,1)} copy(bf16[2880,64]{0,1:T(8,128)(2,1)} %fusion) | data formatting | bytes 737280
  88.3 0.0 reduce-scatter.4.cloned.1.call-update
  88.3 21.2 %reduce-scatter.4.cloned.1.call-done = bf16[720,64]{1,0:T(8,128)(2,1)} async-done(((bf16[2880,64]{1,0:T(8,128)(2,1)}), bf16[720,64]{1,0:T(8,128)(2,1)}) %reduce-scatter.4.cloned.1.call-update) | async-done | bytes 92176
  109.5 1.7 %copy.60 = bf16[720,64]{0,1:T(8,128)(2,1)} copy(bf16[720,64]{1,0:T(8,128)(2,1)} %reduce-scatter.4.cloned.1.call-done) | data formatting | bytes 184320
  111.2 4.6 %all-to-all-start.1 = ((bf16[720,4,16]{0,2,1:T(8,128)(2,1)}), bf16[720,4,16]{0,2,1:T(8,128)(2,1)S(1)}, u32[]{:S(2)}, u32[]{:S(2)}) async-start(bf16[720,4,16]{0,2,1:T(8,128)(2,1)} %bitcast.20), calls=%async_computation.1 | async-start | bytes 196608 | tf_op jit(solution)/shard_map/all_to_all | solution.py:122
  115.8 0.0 copy-done.3
  115.8 5.8 %all-to-all-done.1 = bf16[720,4,16]{0,2,1:T(8,128)(2,1)S(1)} async-done(((bf16[720,4,16]{0,2,1:T(8,128)(2,1)}), bf16[720,4,16]{0,2,1:T(8,128)(2,1)S(1)}, u32[]{:S(2)}, u32[]{:S(2)}) %all-to-all-start.1) | async-done | bytes 92192 | tf_op jit(solution)/shard_map/all_to_all | solution.py:122
  121.6 2.2 %fusion.16 = bf16[256,720]{0,1:T(8,128)(2,1)} fusion(f32[64,256]{1,0:T(8,128)S(1)} %select_reduce_fusion, bf16[720,64]{0,1:T(8,128)(2,1)S(1)} %bitcast.86, bf16[256,720]{0,1:T(8,128)(2,1)} %fusion.15), kind=kOutput, calls=%fused_computation.24 | convolution fusion | flops 142110720 | bytes 894976 | tf_op jit(solution)/shard_map/dot_general | solution.py:125
  (14 shorter events, 0.2 us)
Async XLA Ops:
  6.5 31.9 %copy-start = (bf16[2048,720]{0,1:T(8,128)(2,1)S(1)}, bf16[2048,720]{0,1:T(8,128)(2,1)}, u32[]{:S(2)}) copy-start(bf16[2048,720]{0,1:T(8,128)(2,1)} %param.17) | copy-start | bytes 8847364
  6.5 31.9 %all-gather.3.cloned.1.call-start = ((), (), s32[]{:S(2)}) async-start(), calls=%async_computation.3 | async-start | bytes 1310720 | tf_op jit(solution)/shard_map/all_gather | solution.py:90
  8.3 8.4 %collective-permute-start = (bf16[128,256]{0,1:T(8,128)(2,1)}, bf16[128,256]{0,1:T(8,128)(2,1)}, u32[]{:S(2)}, u32[]{:S(2)}) collective-permute-start(bf16[128,256]{0,1:T(8,128)(2,1)} %slice.20), channel_id=1, source_target_pairs={{0,4},{4,8},{8,12},{1,5},{5,9},{9,13},{2,6},{6,10},{10,14},{3,7},{... | collective-permute-start | bytes 196616 | tf_op jit(solution)/shard_map/ppermute | solution.py:19
  20.0 21.5 %copy-start.2 = (s32[256,4]{0,1:T(4,128)S(1)}, s32[256,4]{0,1:T(4,128)}, u32[]{:S(2)}) copy-start(s32[256,4]{0,1:T(4,128)} %param.19) | copy-start | bytes 12292
  20.0 42.7 %copy-start.4 = (f32[2880]{0:T(1024)S(1)}, f32[2880]{0:T(1024)}, u32[]{:S(2)}) copy-start(f32[2880]{0:T(1024)} %param.18) | copy-start | bytes 34564
  20.0 40.7 %all-gather.5.cloned.1.call-start = ((), (), s32[]{:S(2)}) async-start(), calls=%async_computation.4 | async-start | bytes 1843200 | tf_op jit(solution)/shard_map/all_gather | solution.py:99
  41.5 68.1 %reduce-scatter.4.cloned.1.call-start = ((), (), s32[]{:S(2)}) async-start(), calls=%async_computation.5 | async-start | bytes 921600
  60.7 20.1 %copy-start.1 = (bf16[1,2880,360]{1,2,0:T(8,128)(2,1)S(1)}, bf16[1,2880,360]{1,2,0:T(8,128)(2,1)}, u32[]{:S(2)}) copy-start(bf16[1,2880,360]{1,2,0:T(8,128)(2,1)} %param.21) | copy-start | bytes 6220804
  81.6 34.3 %copy-start.3 = (f32[256,4]{0,1:T(4,128)S(1)}, f32[256,4]{0,1:T(4,128)}, u32[]{:S(2)}) copy-start(f32[256,4]{0,1:T(4,128)} %param.20) | copy-start | bytes 12292
  111.2 10.4 %all-to-all-start.1 = ((bf16[720,4,16]{0,2,1:T(8,128)(2,1)}), bf16[720,4,16]{0,2,1:T(8,128)(2,1)S(1)}, u32[]{:S(2)}, u32[]{:S(2)}) async-start(bf16[720,4,16]{0,2,1:T(8,128)(2,1)} %bitcast.20), calls=%async_computation.1 | async-start | bytes 196608 | tf_op jit(solution)/shard_map/all_to_all | solution.py:122
Sparse Core Ops, SparseCore 0:
  20.1 18.2 all-gather.2
  41.6 19.0 all-gather.4
  88.4 21.0 reduce-scatter.3
where the time goes:
time: 131 us; the launch traced here: 130 us
  waiting for transfers between devices  62.9 us (48%)
  blocking collectives  16.1 us (12%)
  matrix products  14.9 us (11%)
  between operations  13.2 us (10%)
  starting transfers between devices  10.2 us (8%)
  local copies, waits for them, and re-layouts  8.68 us (7%)
  other arithmetic  4.33 us (3%)
    unnamed x4, waiting for transfers between devices  21.3 us
    all_gather x1, waiting for transfers between devices, shards(): lax.all_gather(attended, 'cuts', axis=1, tiled=True)  18.4 us
    all_gather x1, waiting for transfers between devices, shards(): full_rows = lax.all_gather(resid_rows, 'cuts', axis=1, tiled=True)  17.5 us
    all_to_all x1, blocking collectives, shards(): lax.all_to_all(outgoing.reshape(live_count, CAP, D), 'seq', split_axis=0,...  16.1 us
    unnamed x15, local copies, waits for them, and re-layouts  7.01 us
    all_to_all x1, waiting for transfers between devices, shards(): lax.all_to_all(expert_out, 'seq', split_axis=1, concat_axis=1, tiled=True)  5.8 us
    ppermute x1, starting transfers between devices, passed_along(): return lax.ppermute(block, axis, route)  5.54 us
    all_to_all x1, starting transfers between devices, shards(): lax.all_to_all(expert_out, 'seq', split_axis=1, concat_axis=1, tiled=True)  4.61 us
  transfers between devices with their start and end apart: 5, of which 4 were waited for; matrix products, arithmetic and copies ran while one was open for 4% of the time, Pallas kernels for 0%

commit v1 on v0

v1 whole, which is shorter than its diff:
```python
import functools

import jax
import jax.numpy as jnp
from jax import lax
from jax.experimental import pallas as pl
from jax.experimental.pallas import tpu as pltpu
from jax.sharding import PartitionSpec as P

HEAD_SIZE = 64
KEYS_SEEN = 128
CAP = 16
CORES = 2

norm_eps = 1e-05
glu_alpha = 1.702

NT = (((1,), (1,)), ((), ()))
NN = (((1,), (0,)), ((), ()))
TN = (((0,), (0,)), ((), ()))
VMEM_LIMIT = 40 * 1024 * 1024


def dot(a, b, dims):
    return lax.dot_general(a, b, dims, preferred_element_type=jnp.float32)


def call(kernel, outs, scratch=(), smem=(), n_in=0, flops=0, moved=0):
    specs = [
        pl.BlockSpec(memory_space=pltpu.SMEM if i in smem else pltpu.VMEM) for i in range(n_in)
    ]
    return pl.pallas_call(
        kernel,
        out_shape=outs,
        in_specs=specs,
        out_specs=jax.tree.map(lambda _: pl.BlockSpec(memory_space=pltpu.VMEM), outs),
        scratch_shapes=list(scratch),
        compiler_params=pltpu.CompilerParams(vmem_limit_bytes=VMEM_LIMIT),
        cost_estimate=pl.CostEstimate(flops=flops, bytes_accessed=moved, transcendentals=0),
    )


def bf16(*shape):
    return jax.ShapeDtypeStruct(shape, jnp.bfloat16)


def tables_kernel(live, ids_ref, weights_ref, placing_ref, mix_hi_ref, mix_lo_ref):
    top, toks = ids_ref.shape
    ids = ids_ref[...]
    weights = weights_ref[...]
    chosen = jnp.concatenate(
        [jnp.max((ids == e).astype(jnp.float32), axis=0, keepdims=True) for e in range(live)], axis=0
    )
    earlier = lax.broadcasted_iota(jnp.int32, (toks, toks), 0)
    later = lax.broadcasted_iota(jnp.int32, (toks, toks), 1)
    strict = (earlier < later).astype(jnp.bfloat16)
    before = dot(chosen.astype(jnp.bfloat16), strict, NN)
    slot = lax.broadcasted_iota(jnp.int32, (CAP, toks), 0).astype(jnp.float32)
    for e in range(live):
        weight = jnp.sum(jnp.where(ids == e, weights, 0.0), axis=0, keepdims=True)
        fills = (before[e : e + 1] == slot) & (chosen[e : e + 1] > 0.0)
        mix = jnp.where(fills, weight, 0.0)
        hi = mix.astype(jnp.bfloat16)
        rows = slice(e * CAP, (e + 1) * CAP)
        placing_ref[rows] = fills.astype(jnp.bfloat16)
        mix_hi_ref[rows] = hi
        mix_lo_ref[rows] = (mix - hi.astype(jnp.float32)).astype(jnp.bfloat16)


def attend_kernel(q_ref, kv_ref, before_ref, rim_ref, sinks_ref, out_ref, joined_ref):
    toks = q_ref.shape[0]
    groups = kv_ref.shape[1] // (2 * HEAD_SIZE)
    pairs = q_ref.shape[1] // (2 * HEAD_SIZE)
    per_group = pairs // groups
    first = lax.axis_index("seq") == 0
    joined_ref[:KEYS_SEEN] = jnp.where(first, before_ref[...], rim_ref[...])
    joined_ref[KEYS_SEEN:] = kv_ref[...]
    span = 2 * KEYS_SEEN
    row = lax.broadcasted_iota(jnp.int32, (KEYS_SEEN, span), 0)
    col = lax.broadcasted_iota(jnp.int32, (KEYS_SEEN, span), 1)
    allowed = (col > row) & (col <= row + KEYS_SEEN)
    low = lax.broadcasted_iota(jnp.int32, (span, 2 * HEAD_SIZE), 1) < HEAD_SIZE
    for g in range(groups):
        for b in range(toks // KEYS_SEEN):
            lanes = slice(g * 2 * HEAD_SIZE, (g + 1) * 2 * HEAD_SIZE)
            both = joined_ref[b * KEYS_SEEN : b * KEYS_SEEN + span, lanes].astype(jnp.float32)
            turned = pltpu.roll(both, HEAD_SIZE, 1)
            keys = jnp.concatenate([jnp.where(low, both, 0.0), jnp.where(low, 0.0, turned)], axis=0)
            values = jnp.concatenate([jnp.where(low, turned, 0.0), jnp.where(low, 0.0, both)], axis=0)
            keys = keys.astype(jnp.bfloat16)
            values = values.astype(jnp.bfloat16)
            for p in range(g * per_group, (g + 1) * per_group):
                rows = slice(b * KEYS_SEEN, (b + 1) * KEYS_SEEN)
                heads = slice(p * 2 * HEAD_SIZE, (p + 1) * 2 * HEAD_SIZE)
                scores = dot(q_ref[rows, heads], keys, NT) * (HEAD_SIZE**-0.5)
                probs = []
                for i in range(2):
                    sink = sinks_ref[2 * p + i]
                    part = jnp.where(allowed, scores[:, i * span : (i + 1) * span], -jnp.inf)
                    peak = jnp.maximum(jnp.max(part, axis=1, keepdims=True), sink)
                    terms = jnp.exp(part - peak)
                    denom = jnp.sum(terms, axis=1, keepdims=True) + jnp.exp(sink - peak)
                    probs.append((terms / denom).astype(jnp.bfloat16))
                mixed = dot(jnp.concatenate(probs, axis=1), values, NN)
                out_ref[rows, heads] = mixed.astype(jnp.bfloat16)


def origin(k, steps, sibling):
    me = lax.axis_index("cuts")
    chip = lax.rem(lax.div(me, CORES) - k + steps, steps)
    core = lax.rem(me, CORES)
    return chip * CORES + (1 - core if sibling else core)


def project_kernel(steps, *refs):
    mine, theirs = refs[:steps], refs[steps : 2 * steps]
    w_ref, residual_ref, placing_ref, resid_ref = refs[2 * steps : 2 * steps + 4]
    outgoing = refs[2 * steps + 4 : -1]
    rows_ref = refs[-1]
    width = mine[0].shape[1]
    total = residual_ref[...].astype(jnp.float32)
    for k in range(steps):
        for sibling in (False, True):
            block = (theirs if sibling else mine)[k][...]
            at = pl.multiple_of(origin(k, steps, sibling) * width, 128)
            total += dot(w_ref[:, pl.ds(at, width)], block, NT)
    resid = total.astype(jnp.bfloat16)
    resid_ref[...] = resid
    live = len(outgoing)
    rows = dot(placing_ref[...], resid, NT).astype(jnp.bfloat16)
    rows_ref[...] = rows.reshape(rows_ref.shape)
    me = lax.axis_index("seq")
    for k in range(live):
        outgoing[k][...] = rows_ref[lax.rem(me + k, live)]


def expert_kernel(steps, *refs):
    mine, theirs = refs[:steps], refs[steps : 2 * steps]
    gain_ref, gate_ref, up_ref, down_ref, kept_ref, given_ref, blocks_ref, rows_ref = refs[2 * steps :]
    cuts = CORES * steps
    width = mine[0].shape[1]
    for k in range(steps):
        blocks_ref[origin(k, steps, False)] = mine[k][...]
        blocks_ref[origin(k, steps, True)] = theirs[k][...]
    blocks = [blocks_ref[p].astype(jnp.float32) for p in range(cuts)]
    squares = sum(jnp.sum(b * b, axis=1, keepdims=True) for b in blocks)
    scale = lax.rsqrt(squares / (cuts * width) + norm_eps)
    gain = gain_ref[...].reshape(1, cuts * width)
    wide = jnp.concatenate(blocks, axis=1)
    rows_ref[...] = (wide * scale * gain).astype(jnp.bfloat16)
    rows = rows_ref[...]
    gate = dot(rows, gate_ref[...], NT)
    up = dot(rows, up_ref[...], NT)
    activated = ((up + 1.0) * gate * jax.nn.sigmoid(glu_alpha * gate)).astype(jnp.bfloat16)
    out = dot(activated, down_ref[...], NN).astype(jnp.bfloat16)
    for p in range(cuts):
        blocks_ref[p] = out[:, p * width : (p + 1) * width]
    for k in range(steps):
        kept_ref[k] = blocks_ref[origin(k, steps, False)]
        given_ref[k] = blocks_ref[origin(k, steps, True)]


def add_pair_kernel(kept_ref, given_ref, *out_refs):
    for k, out_ref in enumerate(out_refs):
        total = kept_ref[k].astype(jnp.float32) + given_ref[k].astype(jnp.float32)
        out_ref[...] = total.astype(jnp.bfloat16)


def add_chips_kernel(steps, *refs):
    total = sum(r[...].astype(jnp.float32) for r in refs[:steps])
    for k, out_ref in enumerate(refs[steps:]):
        out_ref[...] = total[k * CAP : (k + 1) * CAP].astype(jnp.bfloat16)


def combine_kernel(live, *refs):
    blocks = refs[:live]
    mix_hi_ref, mix_lo_ref, resid_ref, out_ref, rows_ref = refs[live:]
    me = lax.axis_index("seq")
    for k in range(live):
        rows_ref[lax.rem(me + k, live)] = blocks[k][...]
    rows = rows_ref[...].reshape(live * CAP, -1)
    mixed = dot(rows, mix_hi_ref[...], TN) + dot(rows, mix_lo_ref[...], TN)
    out_ref[...] = (resid_ref[...].astype(jnp.float32) + mixed).astype(jnp.bfloat16)


def shift_seq(block, distance):
    size = lax.axis_size("seq")
    return lax.ppermute(block, "seq", [(i, (i + distance) % size) for i in range(size)])


def shift_chips(block, distance):
    size = lax.axis_size("cuts")
    return lax.ppermute(block, "cuts", [(i, (i + CORES * distance) % size) for i in range(size)])


def swap_cores(block):
    return lax.ppermute(block, "cuts", [(i, i ^ 1) for i in range(lax.axis_size("cuts"))])


def gather_cuts(block):
    steps = lax.axis_size("cuts") // CORES
    mine = [block] + [shift_chips(block, k) for k in range(1, steps)]
    return mine, [swap_cores(b) for b in mine]


def shards(
    queries,
    keyvals,
    preceding_keyvalues,
    attention_sink_logits,
    residual,
    w_out,
    norm_gain,
    expert_ids,
    route_weights,
    w_gate,
    w_up,
    w_down,
):
    toks, feats = residual.shape
    live = w_gate.shape[0] * lax.axis_size("seq")
    cuts = lax.axis_size("cuts")
    steps = cuts // CORES
    slots = live * CAP
    hidden = w_gate.shape[2]
    width = norm_gain.shape[0]

    size = lax.axis_size("seq")
    rim = lax.ppermute(keyvals[toks - KEYS_SEEN :], "seq", [(i, i + 1) for i in range(size - 1)])
    placing, mix_hi, mix_lo = call(
        functools.partial(tables_kernel, live), (bf16(slots, toks),) * 3, n_in=2
    )(expert_ids.T, route_weights.T)
    attended = call(
        attend_kernel,
        bf16(*queries.shape),
        scratch=[pltpu.VMEM((KEYS_SEEN + toks, keyvals.shape[1]), jnp.bfloat16)],
        smem=(4,),
        n_in=5,
    )(queries, keyvals, preceding_keyvalues, rim, attention_sink_logits)
    mine, theirs = gather_cuts(attended)
    resid, *outgoing = call(
        functools.partial(project_kernel, steps),
        (bf16(feats, toks),) + (bf16(CAP, feats),) * live,
        scratch=[pltpu.VMEM((live, CAP, feats), jnp.bfloat16)],
        n_in=2 * steps + 3,
    )(*mine, *theirs, w_out.T, residual.T, placing)
    arrived = [outgoing[0]] + [shift_seq(outgoing[k], k) for k in range(1, live)]
    mine, theirs = gather_cuts(jnp.concatenate(arrived, axis=0))
    kept, given = call(
        functools.partial(expert_kernel, steps),
        (bf16(steps, slots, feats),) * 2,
        scratch=[
            pltpu.VMEM((cuts, slots, feats), jnp.bfloat16),
            pltpu.VMEM((slots, width), jnp.bfloat16),
        ],
        n_in=2 * steps + 4,
    )(*mine, *theirs, norm_gain, w_gate[0].T, w_up[0].T, w_down[0])
    sums = call(add_pair_kernel, (bf16(slots, feats),) * steps, n_in=2)(kept, swap_cores(given))
    sums = [sums[0]] + [shift_chips(sums[k], steps - k) for k in range(1, steps)]
    returned = call(
        functools.partial(add_chips_kernel, steps),
        (bf16(CAP, feats),) * live,
        n_in=steps,
    )(*sums)
    returned = [returned[0]] + [shift_seq(returned[k], live - k) for k in range(1, live)]
    out = call(
        functools.partial(combine_kernel, live),
        bf16(feats, toks),
        scratch=[pltpu.VMEM((live, CAP, feats), jnp.bfloat16)],
        n_in=live + 3,
    )(*returned, mix_hi, mix_lo, resid)
    return out.T


def solution(mesh):
    placed = (
        P(("groups", "seq"), "cuts"),
        P(("groups", "seq"), "cuts"),
        P("groups", "cuts"),
        P("cuts"),
        P(("groups", "seq"), "cuts"),
        P(None, "cuts"),
        P(),
        P(("groups", "seq"), None),
        P(("groups", "seq"), None),
        P("seq", None, "cuts"),
        P("seq", None, "cuts"),
        P("seq", "cuts", None),
    )
    return jax.shard_map(
        shards, mesh=mesh, in_specs=placed, out_specs=P(("groups", "seq"), "cuts"), check_vma=False
    )
```

time: 131 us -> 62.6 us (0.48)
  waiting for transfers between devices: 62.9 us -> 24.1 us
  blocking collectives: 16.1 us -> 0 us
  matrix products: 14.9 us -> 0 us
  between operations: 13.2 us -> 0.1 us
  starting transfers between devices: 10.2 us -> 19.7 us
  Pallas kernels: 0 us -> 8.3 us
  other arithmetic: 4.33 us -> 0 us
  local copies, waits for them, and re-layouts: 8.68 us -> 9.99 us
    all_gather x2 -> x0, waiting for transfers between devices: 35.8 us -> none  [the longest x1 18.4 us: shards(): lax.all_gather(attended, 'cuts', axis=1, tiled=True)]
    ppermute x1 -> x15, waiting for transfers between devices: 0.01 us -> 24.1 us  [the longest x3 12.1 us: shift_chips(): lax.ppermute(block, 'cuts', [(i, (i + CORES * distance) % size) for i in...]
    unnamed x4 -> x0, waiting for transfers between devices: 21.3 us -> none
    all_to_all x1 -> x0, blocking collectives: 16.1 us -> none  [shards(): lax.all_to_all(outgoing.reshape(live_count, CAP, D), 'seq', split_axis=0,...]
    dot_general x7 -> x0, matrix products: 14.9 us -> none  [the longest x1 4.57 us: shards(): lax.dot_general(down_here, activated, (((0,), (1,)), ((), ())), preferred...]
    ppermute x1 -> x15, starting transfers between devices: 5.54 us -> 19.7 us  [the longest x6 9.9 us: shift_seq(): lax.ppermute(block, 'seq', [(i, (i + distance) % size) for i in range(siz...]
    pallas_call x0 -> x7, Pallas kernels: none -> 8.3 us  [the longest x1 3.68 us: shards(): call(attend_kernel, bf16(*queries.shape), scratch=[pltpu.VMEM((KEYS_SEEN...]
    all_to_all x1 -> x0, waiting for transfers between devices: 5.8 us -> none  [shards(): lax.all_to_all(expert_out, 'seq', split_axis=1, concat_axis=1, tiled=True)]
  transfers between devices with their start and end apart: 5 -> 15, of which waited for: 4 -> 11; matrix products, arithmetic and copies ran while one was open for 4% -> 0% of each run, Pallas kernels for 0% -> 0%
where the time goes in v1:
time: 62.6 us; the launch traced here: 62.1 us
  waiting for transfers between devices  24.1 us (38%)
  starting transfers between devices  19.7 us (31%)
  local copies, waits for them, and re-layouts  9.99 us (16%)
  Pallas kernels  8.3 us (13%)
    ppermute x3, waiting for transfers between devices, shift_chips(): lax.ppermute(block, 'cuts', [(i, (i + CORES * distance) % size) for i in...  12.1 us
    ppermute x6, starting transfers between devices, shift_seq(): lax.ppermute(block, 'seq', [(i, (i + distance) % size) for i in range(siz...  9.9 us
    unnamed x27, local copies, waits for them, and re-layouts  9.15 us
    ppermute x6, waiting for transfers between devices, shift_seq(): lax.ppermute(block, 'seq', [(i, (i + distance) % size) for i in range(siz...  7.44 us
    ppermute x1, starting transfers between devices, shards(): lax.ppermute(keyvals[toks - KEYS_SEEN:], 'seq', [(i, i + 1) for i in rang...  4.92 us
    ppermute x3, starting transfers between devices, shift_chips(): lax.ppermute(block, 'cuts', [(i, (i + CORES * distance) % size) for i in...  4.64 us
    pallas_call x1, Pallas kernels, shards(): call(attend_kernel, bf16(*queries.shape), scratch=[pltpu.VMEM((KEYS_SEEN...  3.68 us
    ppermute x5, waiting for transfers between devices, swap_cores(): lax.ppermute(block, 'cuts', [(i, i ^ 1) for i in range(lax.axis_size('cut...  2.6 us
  transfers between devices with their start and end apart: 15, of which 11 were waited for; matrix products, arithmetic and copies ran while one was open for 0% of the time, Pallas kernels for 0%

profile of v1, /device:TPU:0, one launch (start us, length us, event | category | flops | bytes accessed | tf_op | source)
XLA Modules:
  0.0 62.1 jit_solution(17677417884929490505)
XLA Ops:
  0.0 0.8 %slice.3 = bf16[128,256]{1,0:T(8,128)(2,1)S(1)} slice(bf16[256,256]{1,0:T(8,128)(2,1)} %kv_ref.1), slice={[128:256], [0:256]} | slice | bytes 131072 | tf_op jit(solution)/shard_map/slice | solution.py:229
  0.8 4.9 %collective-permute-start = (bf16[128,256]{1,0:T(8,128)(2,1)S(1)}, bf16[128,256]{1,0:T(8,128)(2,1)S(1)}, u32[]{:S(2)}, u32[]{:S(2)}) collective-permute-start(bf16[128,256]{1,0:T(8,128)(2,1)S(1)} %slice.3), channel_id=1, source_target_pairs={{0,4},{4,8},{8,12},{1,5},{5,9},{9,13},{2,6},{6,10},{10,14},{3,7},{... | collective-permute-start | bytes 196616 | tf_op jit(solution)/shard_map/ppermute | solution.py:229
  5.8 1.9 %collective-permute-done.rim_ref = bf16[128,256]{1,0:T(8,128)(2,1)S(1)} collective-permute-done((bf16[128,256]{1,0:T(8,128)(2,1)S(1)}, bf16[128,256]{1,0:T(8,128)(2,1)S(1)}, u32[]{:S(2)}, u32[]{:S(2)}) %collective-permute-start) | collective-permute-done | bytes 65568 | tf_op jit(solution)/shard_map/ppermute | solution.py:229
  7.7 0.9 %copy-done.5 = bf16[256,256]{1,0:T(8,128)(2,1)S(1)} copy-done((bf16[256,256]{1,0:T(8,128)(2,1)S(1)}, bf16[256,256]{1,0:T(8,128)(2,1)}, u32[]{:S(2)}) %copy-start.5) | copy-done | bytes 131096
  8.6 0.9 %copy-done.6 = bf16[256,512]{1,0:T(8,128)(2,1)S(1)} copy-done((bf16[256,512]{1,0:T(8,128)(2,1)S(1)}, bf16[256,512]{1,0:T(8,128)(2,1)}, u32[]{:S(2)}) %copy-start.6) | copy-done | bytes 262168
  9.5 0.8 %copy-done.7 = bf16[128,256]{1,0:T(8,128)(2,1)S(1)} copy-done((bf16[128,256]{1,0:T(8,128)(2,1)S(1)}, bf16[128,256]{1,0:T(8,128)(2,1)}, u32[]{:S(2)}) %copy-start.7) | copy-done | bytes 65560
  10.4 0.7 %copy-done.11 = f32[8]{0:T(128)S(1)} copy-done((f32[8]{0:T(128)S(1)}, f32[8]{0:T(128)}, u32[]{:S(2)}) %copy-start.11) | copy-done | bytes 56
  11.0 3.7 %shard_map.118.refs_0_ = bf16[256,512]{1,0:T(8,128)(2,1)S(1)} custom-call(bf16[256,512]{1,0:T(8,128)(2,1)S(1)} %copy-done.6, bf16[256,256]{1,0:T(8,128)(2,1)S(1)} %copy-done.5, bf16[128,256]{1,0:T(8,128)(2,1)S(1)} %copy-done.7, bf16[128,256]{1,0:T(8,128)(2,1)S(1)} %collective-permute-done.rim_ref, f32[8]{0:T(128)S(1)} %copy-done.11), custom_call_target="tpu_custom_call" | custom-call | tf_op jit(solution)/shard_map/pallas_call | solution.py:233
  14.7 1.6 %collective-permute-start.1 = (bf16[256,512]{1,0:T(8,128)(2,1)S(1)}, bf16[256,512]{1,0:T(8,128)(2,1)S(1)}, u32[]{:S(2)}, u32[]{:S(2)}) collective-permute-start(bf16[256,512]{1,0:T(8,128)(2,1)S(1)} %shard_map.118.refs_0_), channel_id=1, source_target_pairs={{0,2},{1,3},{2,0},{3,1},{4,6},{5,7},{6,4},{7,5},{8,10},{9,11},{10,... | collective-permute-start | bytes 786440 | tf_op jit(solution)/shard_map/ppermute | solution.py:193
  16.3 0.0 collective-permute-start.2
  16.3 5.7 %collective-permute-done.1.refs_1_ = bf16[256,512]{1,0:T(8,128)(2,1)S(1)} collective-permute-done((bf16[256,512]{1,0:T(8,128)(2,1)S(1)}, bf16[256,512]{1,0:T(8,128)(2,1)S(1)}, u32[]{:S(2)}, u32[]{:S(2)}) %collective-permute-start.1) | collective-permute-done | bytes 262176 | tf_op jit(solution)/shard_map/ppermute | solution.py:193
  22.0 0.0 collective-permute-start.3
  22.0 0.7 %copy-done.9 = s32[256,4]{0,1:T(4,128)S(1)} copy-done((s32[256,4]{0,1:T(4,128)S(1)}, s32[256,4]{0,1:T(4,128)}, u32[]{:S(2)}) %copy-start.9) | copy-done | bytes 4120
  22.7 0.7 %copy-done.10 = f32[256,4]{0,1:T(4,128)S(1)} copy-done((f32[256,4]{0,1:T(4,128)S(1)}, f32[256,4]{0,1:T(4,128)}, u32[]{:S(2)}) %copy-start.10) | copy-done | bytes 4120
  23.3 0.2 shard_map.119
  23.5 0.0 collective-permute-done.2.refs_2_
  23.5 0.0 collective-permute-done.3.refs_3_
  23.5 0.0 copy-start
  23.5 1.8 %copy-done = bf16[2048,720]{0,1:T(8,128)(2,1)S(1)} copy-done((bf16[2048,720]{0,1:T(8,128)(2,1)S(1)}, bf16[2048,720]{0,1:T(8,128)(2,1)}, u32[]{:S(2)}) %copy-start) | copy-done | bytes 2949144
  25.4 1.0 %copy-done.4 = bf16[256,720]{0,1:T(8,128)(2,1)S(1)} copy-done((bf16[256,720]{0,1:T(8,128)(2,1)S(1)}, bf16[256,720]{0,1:T(8,128)(2,1)}, u32[]{:S(2)}) %copy-start.4) | copy-done | bytes 368664
  26.4 1.2 %shard_map.120 = (bf16[720,256]{1,0:T(8,128)(2,1)S(1)}, bf16[16,720]{1,0:T(8,128)(2,1)S(1)}, bf16[16,720]{1,0:T(8,128)(2,1)S(1)}, bf16[16,720]{1,0:T(8,128)(2,1)S(1)}, bf16[16,720]{1,0:T(8,128)(2,1)S(1)}) custom-call(bf16[256,512]{1,0:T(8,128)(2,1)S(1)} %shard_map.118.refs_0_, bf16[256,512]{1,0:T(8,128)(2,1)S(1)} %collective-permute-done.1.refs_1_, ...), custom_call_target="tpu_custom_call" | custom-call | tf_op jit(solution)/shard_map/pallas_call | solution.py:241
  27.5 2.1 %collective-permute-start.4 = (bf16[16,720]{1,0:T(8,128)(2,1)S(1)}, bf16[16,720]{1,0:T(8,128)(2,1)S(1)}, u32[]{:S(2)}, u32[]{:S(2)}) collective-permute-start(bf16[16,720]{1,0:T(8,128)(2,1)S(1)} %get-tuple-element.23), channel_id=1, source_target_pairs={{0,4},{4,8},{8,12},{12,0},{1,5},{5,9},{9,13},{13,1},{2,6},{6,10},{... | collective-permute-start | bytes 69128 | tf_op jit(solution)/shard_map/ppermute | solution.py:188
  29.7 2.6 %collective-permute-start.5 = (bf16[16,720]{1,0:T(8,128)(2,1)S(1)}, bf16[16,720]{1,0:T(8,128)(2,1)S(1)}, u32[]{:S(2)}, u32[]{:S(2)}) collective-permute-start(bf16[16,720]{1,0:T(8,128)(2,1)S(1)} %get-tuple-element.24), channel_id=1, source_target_pairs={{0,8},{4,12},{8,0},{12,4},{1,9},{5,13},{9,1},{13,5},{2,10},{6,14},... | collective-permute-start | bytes 69128 | tf_op jit(solution)/shard_map/ppermute | solution.py:188
  32.2 1.4 %collective-permute-start.6 = (bf16[16,720]{1,0:T(8,128)(2,1)S(1)}, bf16[16,720]{1,0:T(8,128)(2,1)S(1)}, u32[]{:S(2)}, u32[]{:S(2)}) collective-permute-start(bf16[16,720]{1,0:T(8,128)(2,1)S(1)} %get-tuple-element.25), channel_id=1, source_target_pairs={{0,12},{4,0},{8,4},{12,8},{1,13},{5,1},{9,5},{13,9},{2,14},{6,2},{... | collective-permute-start | bytes 69128 | tf_op jit(solution)/shard_map/ppermute | solution.py:188
  33.6 0.0 collective-permute-done.4
  33.6 0.8 %collective-permute-done.5 = bf16[16,720]{1,0:T(8,128)(2,1)S(1)} collective-permute-done((bf16[16,720]{1,0:T(8,128)(2,1)S(1)}, bf16[16,720]{1,0:T(8,128)(2,1)S(1)}, u32[]{:S(2)}, u32[]{:S(2)}) %collective-permute-start.5) | collective-permute-done | bytes 23072 | tf_op jit(solution)/shard_map/ppermute | solution.py:188
  34.4 1.7 %collective-permute-done.6 = bf16[16,720]{1,0:T(8,128)(2,1)S(1)} collective-permute-done((bf16[16,720]{1,0:T(8,128)(2,1)S(1)}, bf16[16,720]{1,0:T(8,128)(2,1)S(1)}, u32[]{:S(2)}, u32[]{:S(2)}) %collective-permute-start.6) | collective-permute-done | bytes 23072 | tf_op jit(solution)/shard_map/ppermute | solution.py:188
  36.1 1.5 %collective-permute-start.7 = (bf16[64,720]{1,0:T(8,128)(2,1)S(1)}, bf16[64,720]{1,0:T(8,128)(2,1)S(1)}, u32[]{:S(2)}, u32[]{:S(2)}) collective-permute-start(bf16[64,720]{1,0:T(8,128)(2,1)S(1)} %constant_dynamic-update-slice_fusion.refs_0_), channel_id=1, source_target_pairs={{0,2},{1,3},{2,0},{3,1},{4,6},{5,7},{6,4},{7,5},{8,10},{9,11},{10,... | collective-permute-start | bytes 276488 | tf_op jit(solution)/shard_map/ppermute | solution.py:193
  37.6 0.0 collective-permute-start.8
  37.6 3.1 %collective-permute-done.7.refs_1_ = bf16[64,720]{1,0:T(8,128)(2,1)S(1)} collective-permute-done((bf16[64,720]{1,0:T(8,128)(2,1)S(1)}, bf16[64,720]{1,0:T(8,128)(2,1)S(1)}, u32[]{:S(2)}, u32[]{:S(2)}) %collective-permute-start.7) | collective-permute-done | bytes 92192 | tf_op jit(solution)/shard_map/ppermute | solution.py:193
  40.7 0.0 collective-permute-start.9
  40.7 0.0 collective-permute-done.8.refs_2_
  40.7 1.3 %collective-permute-done.9.refs_3_ = bf16[64,720]{1,0:T(8,128)(2,1)S(1)} collective-permute-done((bf16[64,720]{1,0:T(8,128)(2,1)S(1)}, bf16[64,720]{1,0:T(8,128)(2,1)S(1)}, u32[]{:S(2)}, u32[]{:S(2)}) %collective-permute-start.9) | collective-permute-done | bytes 92192 | tf_op jit(solution)/shard_map/ppermute | solution.py:197
  42.0 0.0 copy-done.1
  42.0 0.0 copy-start.3
  42.0 1.6 %copy-done.3 = bf16[1,360,2880]{2,1,0:T(8,128)(2,1)S(1)} copy-done((bf16[1,360,2880]{2,1,0:T(8,128)(2,1)S(1)}, bf16[1,360,2880]{2,1,0:T(8,128)(2,1)}, u32[]{:S(2)}) %copy-start.3) | copy-done | bytes 2073624
  43.6 2.1 %shard_map.121 = (bf16[2,64,720]{2,1,0:T(8,128)(2,1)S(1)}, bf16[2,64,720]{2,1,0:T(8,128)(2,1)S(1)}) custom-call(bf16[64,720]{1,0:T(8,128)(2,1)S(1)} %constant_dynamic-update-slice_fusion.refs_0_, bf16[64,720]{1,0:T(8,128)(2,1)S(1)} %collective-permute-done.7.refs_1_, bf16[64,720]{1,0:T(8,128)(2,1)S(1)} %collective-permute-done.8.refs_2_, ...), custom_call_target="tpu_custom_call" | custom-call | tf_op jit(solution)/shard_map/pallas_call | solution.py:249
  45.7 0.2 collective-permute-start.10
  45.9 1.3 %collective-permute-done.10.given_ref = bf16[2,64,720]{2,1,0:T(8,128)(2,1)S(1)} collective-permute-done((bf16[2,64,720]{2,1,0:T(8,128)(2,1)S(1)}, bf16[2,64,720]{2,1,0:T(8,128)(2,1)S(1)}, u32[]{:S(2)}, u32[]{:S(2)}) %collective-permute-start.10) | collective-permute-done | bytes 184352 | tf_op jit(solution)/shard_map/ppermute | solution.py:197
  47.2 1.6 %collective-permute-start.11 = (bf16[64,720]{1,0:T(8,128)(2,1)S(1)}, bf16[64,720]{1,0:T(8,128)(2,1)S(1)}, u32[]{:S(2)}, u32[]{:S(2)}) collective-permute-start(bf16[64,720]{1,0:T(8,128)(2,1)S(1)} %get-tuple-element.29), channel_id=1, source_target_pairs={{0,2},{1,3},{2,0},{3,1},{4,6},{5,7},{6,4},{7,5},{8,10},{9,11},{10,... | collective-permute-start | bytes 276488 | tf_op jit(solution)/shard_map/ppermute | solution.py:193
  48.8 3.3 %collective-permute-done.11.refs_1_ = bf16[64,720]{1,0:T(8,128)(2,1)S(1)} collective-permute-done((bf16[64,720]{1,0:T(8,128)(2,1)S(1)}, bf16[64,720]{1,0:T(8,128)(2,1)S(1)}, u32[]{:S(2)}, u32[]{:S(2)}) %collective-permute-start.11) | collective-permute-done | bytes 92192 | tf_op jit(solution)/shard_map/ppermute | solution.py:193
  52.2 3.2 %collective-permute-start.12 = (bf16[16,720]{1,0:T(8,128)(2,1)S(1)}, bf16[16,720]{1,0:T(8,128)(2,1)S(1)}, u32[]{:S(2)}, u32[]{:S(2)}) collective-permute-start(bf16[16,720]{1,0:T(8,128)(2,1)S(1)} %get-tuple-element.31), channel_id=1, source_target_pairs={{0,12},{4,0},{8,4},{12,8},{1,13},{5,1},{9,5},{13,9},{2,14},{6,2},{... | collective-permute-start | bytes 69128 | tf_op jit(solution)/shard_map/ppermute | solution.py:188
  55.4 0.0 collective-permute-start.13
  55.4 0.6 %collective-permute-start.14 = (bf16[16,720]{1,0:T(8,128)(2,1)S(1)}, bf16[16,720]{1,0:T(8,128)(2,1)S(1)}, u32[]{:S(2)}, u32[]{:S(2)}) collective-permute-start(bf16[16,720]{1,0:T(8,128)(2,1)S(1)} %get-tuple-element.33), channel_id=1, source_target_pairs={{0,4},{4,8},{8,12},{12,0},{1,5},{5,9},{9,13},{13,1},{2,6},{6,10},{... | collective-permute-start | bytes 69128 | tf_op jit(solution)/shard_map/ppermute | solution.py:188
  56.0 0.9 %collective-permute-done.12.refs_1_ = bf16[16,720]{1,0:T(8,128)(2,1)S(1)} collective-permute-done((bf16[16,720]{1,0:T(8,128)(2,1)S(1)}, bf16[16,720]{1,0:T(8,128)(2,1)S(1)}, u32[]{:S(2)}, u32[]{:S(2)}) %collective-permute-start.12) | collective-permute-done | bytes 23072 | tf_op jit(solution)/shard_map/ppermute | solution.py:188
  56.9 3.2 %collective-permute-done.13.refs_2_ = bf16[16,720]{1,0:T(8,128)(2,1)S(1)} collective-permute-done((bf16[16,720]{1,0:T(8,128)(2,1)S(1)}, bf16[16,720]{1,0:T(8,128)(2,1)S(1)}, u32[]{:S(2)}, u32[]{:S(2)}) %collective-permute-start.13) | collective-permute-done | bytes 23072 | tf_op jit(solution)/shard_map/ppermute | solution.py:188
  60.1 0.9 %collective-permute-done.14.refs_3_ = bf16[16,720]{1,0:T(8,128)(2,1)S(1)} collective-permute-done((bf16[16,720]{1,0:T(8,128)(2,1)S(1)}, bf16[16,720]{1,0:T(8,128)(2,1)S(1)}, u32[]{:S(2)}, u32[]{:S(2)}) %collective-permute-start.14) | collective-permute-done | bytes 23072 | tf_op jit(solution)/shard_map/ppermute | solution.py:188
  61.0 1.1 %shard_map.124 = bf16[720,256]{1,0:T(8,128)(2,1)} custom-call(bf16[16,720]{1,0:T(8,128)(2,1)S(1)} %get-tuple-element.30.refs_0_, bf16[16,720]{1,0:T(8,128)(2,1)S(1)} %collective-permute-done.12.refs_1_, bf16[16,720]{1,0:T(8,128)(2,1)S(1)} %collective-permute-done.13.refs_2_, bf16[16,720]{1,0:T(8,128)(2,1)S(1)} %collective-permute-done.14.refs_3_, ...), custom_call_target="tpu_custom_call" | custom-call | tf_op jit(solution)/shard_map/pallas_call | solution.py:266
  (18 shorter events, 0.1 us)
Async XLA Ops:
  0.8 6.8 %collective-permute-start = (bf16[128,256]{1,0:T(8,128)(2,1)S(1)}, bf16[128,256]{1,0:T(8,128)(2,1)S(1)}, u32[]{:S(2)}, u32[]{:S(2)}) collective-permute-start(bf16[128,256]{1,0:T(8,128)(2,1)S(1)} %slice.3), channel_id=1, source_target_pairs={{0,4},{4,8},{8,12},{1,5},{5,9},{9,13},{2,6},{6,10},{10,14},{3,7},{... | collective-permute-start | bytes 196616 | tf_op jit(solution)/shard_map/ppermute | solution.py:229
  7.7 0.9 %copy-start.5 = (bf16[256,256]{1,0:T(8,128)(2,1)S(1)}, bf16[256,256]{1,0:T(8,128)(2,1)}, u32[]{:S(2)}) copy-start(bf16[256,256]{1,0:T(8,128)(2,1)} %kv_ref.1) | copy-start | bytes 393220
  8.6 0.9 %copy-start.6 = (bf16[256,512]{1,0:T(8,128)(2,1)S(1)}, bf16[256,512]{1,0:T(8,128)(2,1)}, u32[]{:S(2)}) copy-start(bf16[256,512]{1,0:T(8,128)(2,1)} %q_ref.1) | copy-start | bytes 786436
  9.5 0.8 %copy-start.7 = (bf16[128,256]{1,0:T(8,128)(2,1)S(1)}, bf16[128,256]{1,0:T(8,128)(2,1)}, u32[]{:S(2)}) copy-start(bf16[128,256]{1,0:T(8,128)(2,1)} %before_ref.1) | copy-start | bytes 196612
  10.4 0.7 %copy-start.11 = (f32[8]{0:T(128)S(1)}, f32[8]{0:T(128)}, u32[]{:S(2)}) copy-start(f32[8]{0:T(128)} %sinks_ref.1) | copy-start | bytes 100
  14.7 7.3 %collective-permute-start.1 = (bf16[256,512]{1,0:T(8,128)(2,1)S(1)}, bf16[256,512]{1,0:T(8,128)(2,1)S(1)}, u32[]{:S(2)}, u32[]{:S(2)}) collective-permute-start(bf16[256,512]{1,0:T(8,128)(2,1)S(1)} %shard_map.118.refs_0_), channel_id=1, source_target_pairs={{0,2},{1,3},{2,0},{3,1},{4,6},{5,7},{6,4},{7,5},{8,10},{9,11},{10,... | collective-permute-start | bytes 786440 | tf_op jit(solution)/shard_map/ppermute | solution.py:193
  16.3 7.3 %collective-permute-start.2 = (bf16[256,512]{1,0:T(8,128)(2,1)S(1)}, bf16[256,512]{1,0:T(8,128)(2,1)S(1)}, u32[]{:S(2)}, u32[]{:S(2)}) collective-permute-start(bf16[256,512]{1,0:T(8,128)(2,1)S(1)} %shard_map.118.refs_0_), channel_id=1, source_target_pairs={{0,1},{1,0},{2,3},{3,2},{4,5},{5,4},{6,7},{7,6},{8,9},{9,8},{10,11... | collective-permute-start | bytes 786440 | tf_op jit(solution)/shard_map/ppermute | solution.py:197
  22.0 1.6 %collective-permute-start.3 = (bf16[256,512]{1,0:T(8,128)(2,1)S(1)}, bf16[256,512]{1,0:T(8,128)(2,1)S(1)}, u32[]{:S(2)}, u32[]{:S(2)}) collective-permute-start(bf16[256,512]{1,0:T(8,128)(2,1)S(1)} %collective-permute-done.1.refs_1_), channel_id=1, source_target_pairs={{0,1},{1,0},{2,3},{3,2},{4,5},{5,4},{6,7},{7,6},{8,9},{9,8},{10,11... | collective-permute-start | bytes 786440 | tf_op jit(solution)/shard_map/ppermute | solution.py:197
  22.0 0.7 %copy-start.9 = (s32[256,4]{0,1:T(4,128)S(1)}, s32[256,4]{0,1:T(4,128)}, u32[]{:S(2)}) copy-start(s32[256,4]{0,1:T(4,128)} %param.19) | copy-start | bytes 12292
  22.6 0.7 %copy-start.10 = (f32[256,4]{0,1:T(4,128)S(1)}, f32[256,4]{0,1:T(4,128)}, u32[]{:S(2)}) copy-start(f32[256,4]{0,1:T(4,128)} %param.20) | copy-start | bytes 12292
  23.5 1.8 %copy-start = (bf16[2048,720]{0,1:T(8,128)(2,1)S(1)}, bf16[2048,720]{0,1:T(8,128)(2,1)}, u32[]{:S(2)}) copy-start(bf16[2048,720]{0,1:T(8,128)(2,1)} %param.17) | copy-start | bytes 8847364
  25.4 1.0 %copy-start.4 = (bf16[256,720]{0,1:T(8,128)(2,1)S(1)}, bf16[256,720]{0,1:T(8,128)(2,1)}, u32[]{:S(2)}) copy-start(bf16[256,720]{0,1:T(8,128)(2,1)} %param.16) | copy-start | bytes 1105924
  26.4 15.6 %copy-start.1 = (bf16[1,2880,360]{1,2,0:T(8,128)(2,1)S(1)}, bf16[1,2880,360]{1,2,0:T(8,128)(2,1)}, u32[]{:S(2)}) copy-start(bf16[1,2880,360]{1,2,0:T(8,128)(2,1)} %param.21) | copy-start | bytes 6220804
  26.4 15.6 %copy-start.2 = (bf16[1,2880,360]{1,2,0:T(8,128)(2,1)S(1)}, bf16[1,2880,360]{1,2,0:T(8,128)(2,1)}, u32[]{:S(2)}) copy-start(bf16[1,2880,360]{1,2,0:T(8,128)(2,1)} %param.22) | copy-start | bytes 6220804
  26.4 15.6 %copy-start.8 = (f32[2880]{0:T(1024)S(1)}, f32[2880]{0:T(1024)}, u32[]{:S(2)}) copy-start(f32[2880]{0:T(1024)} %refs_4_.1) | copy-start | bytes 34564
  27.5 6.1 %collective-permute-start.4 = (bf16[16,720]{1,0:T(8,128)(2,1)S(1)}, bf16[16,720]{1,0:T(8,128)(2,1)S(1)}, u32[]{:S(2)}, u32[]{:S(2)}) collective-permute-start(bf16[16,720]{1,0:T(8,128)(2,1)S(1)} %get-tuple-element.23), channel_id=1, source_target_pairs={{0,4},{4,8},{8,12},{12,0},{1,5},{5,9},{9,13},{13,1},{2,6},{6,10},{... | collective-permute-start | bytes 69128 | tf_op jit(solution)/shard_map/ppermute | solution.py:188
  29.7 4.7 %collective-permute-start.5 = (bf16[16,720]{1,0:T(8,128)(2,1)S(1)}, bf16[16,720]{1,0:T(8,128)(2,1)S(1)}, u32[]{:S(2)}, u32[]{:S(2)}) collective-permute-start(bf16[16,720]{1,0:T(8,128)(2,1)S(1)} %get-tuple-element.24), channel_id=1, source_target_pairs={{0,8},{4,12},{8,0},{12,4},{1,9},{5,13},{9,1},{13,5},{2,10},{6,14},... | collective-permute-start | bytes 69128 | tf_op jit(solution)/shard_map/ppermute | solution.py:188
  32.2 3.8 %collective-permute-start.6 = (bf16[16,720]{1,0:T(8,128)(2,1)S(1)}, bf16[16,720]{1,0:T(8,128)(2,1)S(1)}, u32[]{:S(2)}, u32[]{:S(2)}) collective-permute-start(bf16[16,720]{1,0:T(8,128)(2,1)S(1)} %get-tuple-element.25), channel_id=1, source_target_pairs={{0,12},{4,0},{8,4},{12,8},{1,13},{5,1},{9,5},{13,9},{2,14},{6,2},{... | collective-permute-start | bytes 69128 | tf_op jit(solution)/shard_map/ppermute | solution.py:188
  36.1 4.6 %collective-permute-start.7 = (bf16[64,720]{1,0:T(8,128)(2,1)S(1)}, bf16[64,720]{1,0:T(8,128)(2,1)S(1)}, u32[]{:S(2)}, u32[]{:S(2)}) collective-permute-start(bf16[64,720]{1,0:T(8,128)(2,1)S(1)} %constant_dynamic-update-slice_fusion.refs_0_), channel_id=1, source_target_pairs={{0,2},{1,3},{2,0},{3,1},{4,6},{5,7},{6,4},{7,5},{8,10},{9,11},{10,... | collective-permute-start | bytes 276488 | tf_op jit(solution)/shard_map/ppermute | solution.py:193
  37.6 3.1 %collective-permute-start.8 = (bf16[64,720]{1,0:T(8,128)(2,1)S(1)}, bf16[64,720]{1,0:T(8,128)(2,1)S(1)}, u32[]{:S(2)}, u32[]{:S(2)}) collective-permute-start(bf16[64,720]{1,0:T(8,128)(2,1)S(1)} %constant_dynamic-update-slice_fusion.refs_0_), channel_id=1, source_target_pairs={{0,1},{1,0},{2,3},{3,2},{4,5},{5,4},{6,7},{7,6},{8,9},{9,8},{10,11... | collective-permute-start | bytes 276488 | tf_op jit(solution)/shard_map/ppermute | solution.py:197
  40.7 1.3 %collective-permute-start.9 = (bf16[64,720]{1,0:T(8,128)(2,1)S(1)}, bf16[64,720]{1,0:T(8,128)(2,1)S(1)}, u32[]{:S(2)}, u32[]{:S(2)}) collective-permute-start(bf16[64,720]{1,0:T(8,128)(2,1)S(1)} %collective-permute-done.7.refs_1_), channel_id=1, source_target_pairs={{0,1},{1,0},{2,3},{3,2},{4,5},{5,4},{6,7},{7,6},{8,9},{9,8},{10,11... | collective-permute-start | bytes 276488 | tf_op jit(solution)/shard_map/ppermute | solution.py:197
  42.0 1.6 %copy-start.3 = (bf16[1,360,2880]{2,1,0:T(8,128)(2,1)S(1)}, bf16[1,360,2880]{2,1,0:T(8,128)(2,1)}, u32[]{:S(2)}) copy-start(bf16[1,360,2880]{2,1,0:T(8,128)(2,1)} %param.23) | copy-start | bytes 6220804
  45.7 1.5 %collective-permute-start.10 = (bf16[2,64,720]{2,1,0:T(8,128)(2,1)S(1)}, bf16[2,64,720]{2,1,0:T(8,128)(2,1)S(1)}, u32[]{:S(2)}, u32[]{:S(2)}) collective-permute-start(bf16[2,64,720]{2,1,0:T(8,128)(2,1)S(1)} %get-tuple-element.27), channel_id=1, source_target_pairs={{0,1},{1,0},{2,3},{3,2},{4,5},{5,4},{6,7},{7,6},{8,9},{9,8},{10,11... | collective-permute-start | bytes 552968 | tf_op jit(solution)/shard_map/ppermute | solution.py:197
  47.2 4.9 %collective-permute-start.11 = (bf16[64,720]{1,0:T(8,128)(2,1)S(1)}, bf16[64,720]{1,0:T(8,128)(2,1)S(1)}, u32[]{:S(2)}, u32[]{:S(2)}) collective-permute-start(bf16[64,720]{1,0:T(8,128)(2,1)S(1)} %get-tuple-element.29), channel_id=1, source_target_pairs={{0,2},{1,3},{2,0},{3,1},{4,6},{5,7},{6,4},{7,5},{8,10},{9,11},{10,... | collective-permute-start | bytes 276488 | tf_op jit(solution)/shard_map/ppermute | solution.py:193
  52.2 4.7 %collective-permute-start.12 = (bf16[16,720]{1,0:T(8,128)(2,1)S(1)}, bf16[16,720]{1,0:T(8,128)(2,1)S(1)}, u32[]{:S(2)}, u32[]{:S(2)}) collective-permute-start(bf16[16,720]{1,0:T(8,128)(2,1)S(1)} %get-tuple-element.31), channel_id=1, source_target_pairs={{0,12},{4,0},{8,4},{12,8},{1,13},{5,1},{9,5},{13,9},{2,14},{6,2},{... | collective-permute-start | bytes 69128 | tf_op jit(solution)/shard_map/ppermute | solution.py:188
  55.4 4.7 %collective-permute-start.13 = (bf16[16,720]{1,0:T(8,128)(2,1)S(1)}, bf16[16,720]{1,0:T(8,128)(2,1)S(1)}, u32[]{:S(2)}, u32[]{:S(2)}) collective-permute-start(bf16[16,720]{1,0:T(8,128)(2,1)S(1)} %get-tuple-element.32), channel_id=1, source_target_pairs={{0,8},{4,12},{8,0},{12,4},{1,9},{5,13},{9,1},{13,5},{2,10},{6,14},... | collective-permute-start | bytes 69128 | tf_op jit(solution)/shard_map/ppermute | solution.py:188
  55.4 5.6 %collective-permute-start.14 = (bf16[16,720]{1,0:T(8,128)(2,1)S(1)}, bf16[16,720]{1,0:T(8,128)(2,1)S(1)}, u32[]{:S(2)}, u32[]{:S(2)}) collective-permute-start(bf16[16,720]{1,0:T(8,128)(2,1)S(1)} %get-tuple-element.33), channel_id=1, source_target_pairs={{0,4},{4,8},{8,12},{12,0},{1,5},{5,9},{9,13},{13,1},{2,6},{6,10},{... | collective-permute-start | bytes 69128 | tf_op jit(solution)/shard_map/ppermute | solution.py:188

commit v2 on v1

v2 whole, which is shorter than its diff:
```python
import functools
import math

import jax
import jax.numpy as jnp
from jax import lax
from jax.experimental import pallas as pl
from jax.experimental.pallas import tpu as pltpu
from jax.sharding import PartitionSpec as P

HEAD_SIZE = 64
KEYS_SEEN = 128
PAIR = 2 * HEAD_SIZE
SPAN = 2 * KEYS_SEEN
CAP = 16
CORES = 2

norm_eps = 1e-05
glu_alpha = 1.702

NT = (((1,), (1,)), ((), ()))
NN = (((1,), (0,)), ((), ()))
TN = (((0,), (0,)), ((), ()))
VMEM_LIMIT = 32 * 1024 * 1024


def dot(a, b, dims):
    return lax.dot_general(a, b, dims, preferred_element_type=jnp.float32)


def call(kernel, outs, n_in, scratch=(), hbm=(), smem=(), flops=0, moved=0):
    spaces = [pltpu.HBM if i in hbm else pltpu.SMEM if i in smem else pltpu.VMEM for i in range(n_in)]
    return pl.pallas_call(
        kernel,
        out_shape=outs,
        in_specs=[pl.BlockSpec(memory_space=space) for space in spaces],
        out_specs=jax.tree.map(lambda _: pl.BlockSpec(memory_space=pltpu.VMEM), outs),
        scratch_shapes=list(scratch),
        compiler_params=pltpu.CompilerParams(vmem_limit_bytes=VMEM_LIMIT),
        cost_estimate=pl.CostEstimate(flops=flops, bytes_accessed=moved, transcendentals=0),
    )


def bf16(*shape):
    return jax.ShapeDtypeStruct(shape, jnp.bfloat16)


def visible():
    key = lax.broadcasted_iota(jnp.int32, (SPAN, KEYS_SEEN), 0)
    query = lax.broadcasted_iota(jnp.int32, (SPAN, KEYS_SEEN), 1)
    return (key > query) & (key <= query + KEYS_SEEN)


def attend_block(pairs, both, sinks, allowed):
    both = both.astype(jnp.float32)
    low = lax.broadcasted_iota(jnp.int32, both.shape, 1) < HEAD_SIZE
    turned = pltpu.roll(both, HEAD_SIZE, 1)
    keys = jnp.concatenate([jnp.where(low, both, 0.0), jnp.where(low, 0.0, turned)], axis=0)
    values = jnp.concatenate([jnp.where(low, turned, 0.0), jnp.where(low, 0.0, both)], axis=0)
    keys, values = keys.astype(jnp.bfloat16), values.astype(jnp.bfloat16)
    scores = dot(keys, jnp.concatenate(pairs, axis=0), NT) * (HEAD_SIZE**-0.5 * math.log2(math.e))
    allowed = jnp.concatenate([allowed] * len(pairs), axis=1)
    probs = []
    for i in range(2):
        sink = jnp.concatenate([sinks[2 * p + i] for p in range(len(pairs))], axis=1)
        part = jnp.where(allowed, scores[i * SPAN : (i + 1) * SPAN], -jnp.inf)
        peak = jnp.maximum(jnp.max(part, axis=0, keepdims=True), sink)
        terms = jnp.exp2(part - peak)
        denom = jnp.sum(terms, axis=0, keepdims=True) + jnp.exp2(sink - peak)
        probs.append((terms * (1.0 / denom)).astype(jnp.bfloat16))
    mixed = dot(values, jnp.concatenate(probs, axis=0), TN).astype(jnp.bfloat16)
    return [mixed[:, p * KEYS_SEEN : (p + 1) * KEYS_SEEN] for p in range(len(pairs))]


def attend_tokens(block, q_ref, rows_of, sinks, out_ref, lanes):
    groups = len(rows_of)
    per_group = q_ref.shape[1] // PAIR // groups
    allowed = visible()
    toks = slice(block * KEYS_SEEN, (block + 1) * KEYS_SEEN)
    for g, both in enumerate(rows_of):
        first = g * per_group
        pairs = [q_ref[toks, (first + p) * PAIR : (first + p + 1) * PAIR] for p in range(per_group)]
        outs = attend_block(pairs, both, sinks[2 * first : 2 * (first + per_group)], allowed)
        for p, out in enumerate(outs):
            out_ref[(first + p) * PAIR : (first + p + 1) * PAIR, lanes] = out


def fill_tables(live, ids, weights, placing_ref, mix_hi_ref, mix_lo_ref):
    toks = ids.shape[1]
    chosen = jnp.concatenate(
        [jnp.max((ids == e).astype(jnp.float32), axis=0, keepdims=True) for e in range(live)], axis=0
    )
    earlier = lax.broadcasted_iota(jnp.int32, (toks, toks), 0)
    later = lax.broadcasted_iota(jnp.int32, (toks, toks), 1)
    strict = (earlier < later).astype(jnp.bfloat16)
    before = dot(chosen.astype(jnp.bfloat16), strict, NN)
    slot = lax.broadcasted_iota(jnp.int32, (CAP, toks), 0).astype(jnp.float32)
    for e in range(live):
        weight = jnp.sum(jnp.where(ids == e, weights, 0.0), axis=0, keepdims=True)
        fills = (before[e : e + 1] == slot) & (chosen[e : e + 1] > 0.0)
        mix = jnp.where(fills, weight, 0.0)
        hi = mix.astype(jnp.bfloat16)
        rows = slice(e * CAP, (e + 1) * CAP)
        placing_ref[rows] = fills.astype(jnp.bfloat16)
        mix_hi_ref[rows] = hi
        mix_lo_ref[rows] = (mix - hi.astype(jnp.float32)).astype(jnp.bfloat16)


def first_kernel(live, sinks_ref, *refs):
    loaded, (ids_ref, weights_ref) = refs[:5], refs[5:7]
    held = refs[7:12]
    placing_ref, mix_hi_ref, mix_lo_ref, sinks_out, late_ref, ids_vmem, weights_vmem, sems = refs[12:]
    copies = [
        pltpu.make_async_copy(source, target, sems.at[i])
        for i, (source, target) in enumerate(
            zip((*loaded[:2], ids_ref, weights_ref, *loaded[2:]), (*held[:2], ids_vmem, weights_vmem, *held[2:]))
        )
    ]
    for copy in copies:
        copy.start()
    q_ref, kv_ref = held[:2]
    heads = sinks_ref.shape[0]
    sinks = [jnp.full((1, KEYS_SEEN), sinks_ref[h], jnp.float32) * math.log2(math.e) for h in range(heads)]
    sinks_out[...] = jnp.concatenate(sinks, axis=0)
    for copy in copies[2:4]:
        copy.wait()
    fill_tables(live, ids_vmem[...], weights_vmem[...], placing_ref, mix_hi_ref, mix_lo_ref)
    for copy in copies[:2]:
        copy.wait()
    groups = kv_ref.shape[1] // PAIR
    for b in range(1, q_ref.shape[0] // KEYS_SEEN):
        span = slice((b - 1) * KEYS_SEEN, (b + 1) * KEYS_SEEN)
        rows_of = [kv_ref[span, g * PAIR : (g + 1) * PAIR] for g in range(groups)]
        attend_tokens(b, q_ref, rows_of, sinks, late_ref, slice((b - 1) * KEYS_SEEN, b * KEYS_SEEN))
    for copy in copies[4:]:
        copy.wait()


def second_kernel(q_ref, kv_ref, before_ref, rim_ref, sinks_ref, late_ref, placing_ref, all_ref, rows_ref):
    first = lax.axis_index("seq") == 0
    rim = jnp.where(first, before_ref[...], rim_ref[...])
    groups = kv_ref.shape[1] // PAIR
    rows_of = []
    for g in range(groups):
        lanes = slice(g * PAIR, (g + 1) * PAIR)
        rows_of.append(jnp.concatenate([rim[:, lanes], kv_ref[:KEYS_SEEN, lanes]], axis=0))
    sinks = [sinks_ref[h : h + 1] for h in range(sinks_ref.shape[0])]
    attend_tokens(0, q_ref, rows_of, sinks, all_ref, slice(0, KEYS_SEEN))
    all_ref[:, KEYS_SEEN:] = late_ref[...]
    rows_ref[...] = dot(placing_ref[...], all_ref[...], NT).astype(jnp.bfloat16)


def origin(k, sibling):
    me = lax.axis_index("cuts")
    return lax.bitwise_xor(me, CORES * k + (1 if sibling else 0))


def project_rows_kernel(steps, *refs):
    blocks = refs[: 2 * steps]
    w_ref, residual_ref, placing_ref = refs[2 * steps : 2 * steps + 3]
    outgoing, rows_ref = refs[2 * steps + 3 : -1], refs[-1]
    width = blocks[0].shape[1]
    total = dot(placing_ref[...], residual_ref[...], NT)
    for i, block in enumerate(blocks):
        at = pl.multiple_of(origin(i % steps, i >= steps) * width, 128)
        total += dot(block[...], w_ref[:, pl.ds(at, width)], NT)
    rows_ref[...] = total.astype(jnp.bfloat16).reshape(rows_ref.shape)
    me = lax.axis_index("seq")
    for k, out_ref in enumerate(outgoing):
        out_ref[...] = rows_ref[lax.bitwise_xor(me, k)]


def project_kernel(steps, *refs):
    blocks = refs[: 2 * steps]
    w_ref, residual_ref, resid_ref = refs[2 * steps :]
    width = blocks[0].shape[0]
    total = residual_ref[...].astype(jnp.float32)
    for i, block in enumerate(blocks):
        at = pl.multiple_of(origin(i % steps, i >= steps) * width, 128)
        total += dot(w_ref[:, pl.ds(at, width)], block[...], NN)
    resid_ref[...] = total.astype(jnp.bfloat16)


def expert_kernel(steps, *refs):
    blocks = refs[: 2 * steps]
    gain_ref, gate_ref, up_ref, down_ref, kept_ref, given_ref, blocks_ref, rows_ref = refs[2 * steps :]
    cuts = CORES * steps
    width = blocks[0].shape[1]
    for i, block in enumerate(blocks):
        blocks_ref[origin(i % steps, i >= steps)] = block[...]
    wide = [blocks_ref[p].astype(jnp.float32) for p in range(cuts)]
    squares = sum(jnp.sum(b * b, axis=1, keepdims=True) for b in wide)
    scale = lax.rsqrt(squares / (cuts * width) + norm_eps)
    gain = gain_ref[...].reshape(1, cuts * width)
    rows_ref[...] = (jnp.concatenate(wide, axis=1) * scale * gain).astype(jnp.bfloat16)
    rows = rows_ref[...]
    gate = dot(rows, gate_ref[...], NT)
    up = dot(rows, up_ref[...], NT)
    activated = ((up + 1.0) * gate * jax.nn.sigmoid(glu_alpha * gate)).astype(jnp.bfloat16)
    out = dot(activated, down_ref[...], NN).astype(jnp.bfloat16)
    for p in range(cuts):
        blocks_ref[p] = out[:, p * width : (p + 1) * width]
    for k in range(steps):
        kept_ref[k] = blocks_ref[origin(k, False)]
        given_ref[k] = blocks_ref[origin(k, True)]


def add_cores_kernel(kept_ref, given_ref, *out_refs):
    for k, out_ref in enumerate(out_refs):
        total = kept_ref[k].astype(jnp.float32) + given_ref[k].astype(jnp.float32)
        out_ref[...] = total.astype(jnp.bfloat16)


def add_chips_kernel(steps, *refs):
    total = sum(r[...].astype(jnp.float32) for r in refs[:steps])
    for k, out_ref in enumerate(refs[steps:]):
        out_ref[...] = total[k * CAP : (k + 1) * CAP].astype(jnp.bfloat16)


def combine_kernel(live, *refs):
    blocks = refs[:live]
    mix_hi_ref, mix_lo_ref, resid_ref, out_ref, rows_ref = refs[live:]
    me = lax.axis_index("seq")
    for k in range(live):
        rows_ref[lax.bitwise_xor(me, k)] = blocks[k][...]
    rows = rows_ref[...].reshape(live * CAP, -1)
    mixed = dot(rows, mix_hi_ref[...], TN) + dot(rows, mix_lo_ref[...], TN)
    out_ref[...] = (resid_ref[...].astype(jnp.float32) + mixed).astype(jnp.bfloat16)


def swap(block, axis, mask):
    return lax.ppermute(block, axis, [(i, i ^ mask) for i in range(lax.axis_size(axis))])


def gather_cuts(block):
    steps = lax.axis_size("cuts") // CORES
    mine = [block] + [swap(block, "cuts", CORES * k) for k in range(1, steps)]
    return mine + [swap(b, "cuts", 1) for b in mine]


def shards(
    queries,
    keyvals,
    preceding_keyvalues,
    attention_sink_logits,
    residual,
    w_out,
    norm_gain,
    expert_ids,
    route_weights,
    w_gate,
    w_up,
    w_down,
):
    toks, feats = residual.shape
    size = lax.axis_size("seq")
    live = w_gate.shape[0] * size
    cuts = lax.axis_size("cuts")
    steps = cuts // CORES
    slots = live * CAP
    head_rows = queries.shape[1]
    heads = head_rows // HEAD_SIZE
    width = norm_gain.shape[0]

    rim = lax.ppermute(keyvals[toks - KEYS_SEEN :], "seq", [(i, i + 1) for i in range(size - 1)])
    loads = (queries, keyvals, preceding_keyvalues, w_out.T, residual.T)
    q, kv, before, w_t, residual_t, placing, mix_hi, mix_lo, sinks, late = call(
        functools.partial(first_kernel, live),
        (
            *(bf16(*a.shape) for a in loads),
            *(bf16(slots, toks),) * 3,
            jax.ShapeDtypeStruct((heads, KEYS_SEEN), jnp.float32),
            bf16(head_rows, toks - KEYS_SEEN),
        ),
        n_in=8,
        scratch=[
            pltpu.VMEM(expert_ids.T.shape, jnp.int32),
            pltpu.VMEM(expert_ids.T.shape, jnp.float32),
            pltpu.SemaphoreType.DMA((7,)),
        ],
        smem=(0,),
        hbm=range(1, 8),
        flops=4 * toks * SPAN * head_rows,
        moved=2 * (w_out.size + residual.size + queries.size),
    )(attention_sink_logits, *loads, expert_ids.T, route_weights.T)
    attended, rows = call(
        second_kernel,
        (bf16(head_rows, toks), bf16(slots, head_rows)),
        n_in=7,
        flops=2 * toks * SPAN * head_rows,
        moved=2 * queries.size,
    )(q, kv, before, rim, sinks, late, placing)

    outgoing = call(
        functools.partial(project_rows_kernel, steps),
        (bf16(CAP, feats),) * live,
        n_in=cuts + 3,
        scratch=[pltpu.VMEM((live, CAP, feats), jnp.bfloat16)],
        flops=2 * slots * w_out.size,
        moved=2 * w_out.size,
    )(*gather_cuts(rows), w_t, residual_t, placing)
    arrived = [outgoing[0]] + [swap(outgoing[k], "seq", k) for k in range(1, live)]

    resid = call(
        functools.partial(project_kernel, steps),
        bf16(feats, toks),
        n_in=cuts + 2,
        flops=2 * toks * w_out.size,
        moved=2 * w_out.size,
    )(*gather_cuts(attended), w_t, residual_t)

    kept, given = call(
        functools.partial(expert_kernel, steps),
        (bf16(steps, slots, feats),) * 2,
        n_in=cuts + 4,
        scratch=[
            pltpu.VMEM((cuts, slots, feats), jnp.bfloat16),
            pltpu.VMEM((slots, width), jnp.bfloat16),
        ],
        flops=6 * slots * w_gate.size,
        moved=6 * w_gate.size,
    )(*gather_cuts(jnp.concatenate(arrived, axis=0)), norm_gain, w_gate[0].T, w_up[0].T, w_down[0])
    sums = call(add_cores_kernel, (bf16(slots, feats),) * steps, n_in=2)(kept, swap(given, "cuts", 1))
    sums = [sums[0]] + [swap(sums[k], "cuts", CORES * k) for k in range(1, steps)]
    returned = call(functools.partial(add_chips_kernel, steps), (bf16(CAP, feats),) * live, n_in=steps)(*sums)
    returned = [returned[0]] + [swap(returned[k], "seq", k) for k in range(1, live)]
    out = call(
        functools.partial(combine_kernel, live),
        bf16(feats, toks),
        n_in=live + 3,
        scratch=[pltpu.VMEM((live, CAP, feats), jnp.bfloat16)],
    )(*returned, mix_hi, mix_lo, resid)
    return out.T


def solution(mesh):
    placed = (
        P(("groups", "seq"), "cuts"),
        P(("groups", "seq"), "cuts"),
        P("groups", "cuts"),
        P("cuts"),
        P(("groups", "seq"), "cuts"),
        P(None, "cuts"),
        P(),
        P(("groups", "seq"), None),
        P(("groups", "seq"), None),
        P("seq", None, "cuts"),
        P("seq", None, "cuts"),
        P("seq", "cuts", None),
    )
    return jax.shard_map(
        shards, mesh=mesh, in_specs=placed, out_specs=P(("groups", "seq"), "cuts"), check_vma=False
    )
```

time: 62.6 us -> 56.4 us (0.901)
  waiting for transfers between devices: 24.1 us -> 18.3 us
  local copies, waits for them, and re-layouts: 9.99 us -> 8.41 us
  Pallas kernels: 8.3 us -> 8.93 us
    ppermute x14 -> x17, waiting for transfers between devices: 22.2 us -> 18.3 us  [swap(): lax.ppermute(block, axis, [(i, i ^ mask) for i in range(lax.axis_size(axi...]
    ppermute x1, waiting for transfers between devices: 1.88 us -> 0.01 us  [shards(): lax.ppermute(keyvals[toks - KEYS_SEEN:], 'seq', [(i, i + 1) for i in rang...]
    unnamed x27, local copies, waits for them, and re-layouts: 9.15 us -> 7.57 us
    pallas_call x5 -> x6, Pallas kernels: 6.2 us -> 6.86 us  [the longest x1 2.5 us: shards(): call(functools.partial(first_kernel, live), (*(bf16(*a.shape) for a in lo...]
    ppermute x14 -> x17, starting transfers between devices: 14.8 us -> 15.3 us  [swap(): lax.ppermute(block, axis, [(i, i ^ mask) for i in range(lax.axis_size(axi...]
  transfers between devices with their start and end apart: 15 -> 18, of which waited for: 11 -> 8; matrix products, arithmetic and copies ran while one was open for 0% -> 0% of each run, Pallas kernels for 0% -> 12%
where the time goes in v2:
time: 56.4 us; the launch traced here: 55.9 us
  starting transfers between devices  20.2 us (36%)
  waiting for transfers between devices  18.3 us (32%)
  Pallas kernels  8.93 us (16%)
  local copies, waits for them, and re-layouts  8.41 us (15%)
    ppermute x17, waiting for transfers between devices, swap(): lax.ppermute(block, axis, [(i, i ^ mask) for i in range(lax.axis_size(axi...  18.3 us
    ppermute x17, starting transfers between devices, swap(): lax.ppermute(block, axis, [(i, i ^ mask) for i in range(lax.axis_size(axi...  15.3 us
    unnamed x27, local copies, waits for them, and re-layouts  7.57 us
    ppermute x1, starting transfers between devices, shards(): lax.ppermute(keyvals[toks - KEYS_SEEN:], 'seq', [(i, i + 1) for i in rang...  4.92 us
    pallas_call x1, Pallas kernels, shards(): call(functools.partial(first_kernel, live), (*(bf16(*a.shape) for a in lo...  2.5 us
    pallas_call x1, Pallas kernels, shards(): call(functools.partial(expert_kernel, steps), (bf16(steps, slots, feats),...  2.05 us
    pallas_call x1, Pallas kernels, shards(): call(second_kernel, (bf16(head_rows, toks), bf16(slots, head_rows)), n_in...  1.18 us
    pallas_call x1, Pallas kernels, shards(): call(functools.partial(combine_kernel, live), bf16(feats, toks), n_in=liv...  1.14 us
  transfers between devices with their start and end apart: 18, of which 8 were waited for; matrix products, arithmetic and copies ran while one was open for 0% of the time, Pallas kernels for 12%

profile of v2, /device:TPU:0, one launch (start us, length us, event | category | flops | bytes accessed | tf_op | source)
XLA Modules:
  0.0 55.9 jit_solution(9782484173455354318)
XLA Ops:
  0.0 0.8 %slice.3 = bf16[128,256]{1,0:T(8,128)(2,1)S(1)} slice(bf16[256,256]{1,0:T(8,128)(2,1)} %refs_1_.1), slice={[128:256], [0:256]} | slice | bytes 131072 | tf_op jit(solution)/shard_map/slice | solution.py:265
  0.8 4.9 %collective-permute-start = (bf16[128,256]{1,0:T(8,128)(2,1)S(1)}, bf16[128,256]{1,0:T(8,128)(2,1)S(1)}, u32[]{:S(2)}, u32[]{:S(2)}) collective-permute-start(bf16[128,256]{1,0:T(8,128)(2,1)S(1)} %slice.3), channel_id=1, source_target_pairs={{0,4},{4,8},{8,12},{1,5},{5,9},{9,13},{2,6},{6,10},{10,14},{3,7},{... | collective-permute-start | bytes 196616 | tf_op jit(solution)/shard_map/ppermute | solution.py:265
  5.8 0.0 copy-start
  5.8 1.8 %copy-done = bf16[2048,720]{0,1:T(8,128)(2,1)S(1)} copy-done((bf16[2048,720]{0,1:T(8,128)(2,1)S(1)}, bf16[2048,720]{0,1:T(8,128)(2,1)}, u32[]{:S(2)}) %copy-start) | copy-done | bytes 2949144
  7.6 1.0 %copy-done.4 = bf16[256,720]{0,1:T(8,128)(2,1)S(1)} copy-done((bf16[256,720]{0,1:T(8,128)(2,1)S(1)}, bf16[256,720]{0,1:T(8,128)(2,1)}, u32[]{:S(2)}) %copy-start.4) | copy-done | bytes 368664
  8.6 0.9 %copy-done.5 = bf16[256,256]{1,0:T(8,128)(2,1)S(1)} copy-done((bf16[256,256]{1,0:T(8,128)(2,1)S(1)}, bf16[256,256]{1,0:T(8,128)(2,1)}, u32[]{:S(2)}) %copy-start.5) | copy-done | bytes 131096
  9.5 0.9 %copy-done.6 = bf16[256,512]{1,0:T(8,128)(2,1)S(1)} copy-done((bf16[256,512]{1,0:T(8,128)(2,1)S(1)}, bf16[256,512]{1,0:T(8,128)(2,1)}, u32[]{:S(2)}) %copy-start.6) | copy-done | bytes 262168
  10.5 0.8 %copy-done.7 = bf16[128,256]{1,0:T(8,128)(2,1)S(1)} copy-done((bf16[128,256]{1,0:T(8,128)(2,1)S(1)}, bf16[128,256]{1,0:T(8,128)(2,1)}, u32[]{:S(2)}) %copy-start.7) | copy-done | bytes 65560
  11.3 0.7 %copy-done.9 = s32[256,4]{0,1:T(4,128)S(1)} copy-done((s32[256,4]{0,1:T(4,128)S(1)}, s32[256,4]{0,1:T(4,128)}, u32[]{:S(2)}) %copy-start.9) | copy-done | bytes 4120
  12.0 0.7 %copy-done.10 = f32[256,4]{0,1:T(4,128)S(1)} copy-done((f32[256,4]{0,1:T(4,128)S(1)}, f32[256,4]{0,1:T(4,128)}, u32[]{:S(2)}) %copy-start.10) | copy-done | bytes 4120
  12.7 0.7 %copy-done.11 = f32[8]{0:T(128)S(1)} copy-done((f32[8]{0:T(128)S(1)}, f32[8]{0:T(128)}, u32[]{:S(2)}) %copy-start.11) | copy-done | bytes 56
  13.3 2.5 %shard_map.118 = (bf16[256,512]{1,0:T(8,128)(2,1)S(1)}, bf16[256,256]{1,0:T(8,128)(2,1)S(1)}, bf16[128,256]{1,0:T(8,128)(2,1)S(1)}, bf16[720,2048]{1,0:T(8,128)(...) custom-call(f32[8]{0:T(128)S(1)} %copy-done.11, ...), custom_call_target="tpu_custom_call" | custom-call | flops 134217728 | bytes 3579904 | tf_op jit(solution)/shard_map/pallas_call | solution.py:267
  15.8 0.0 collective-permute-done.rim_ref
  15.8 0.0 copy-start.1
  15.9 0.0 copy-start.2
  15.9 0.0 copy-start.8
  15.9 1.2 %shard_map.119 = (bf16[512,256]{1,0:T(8,128)(2,1)S(1)}, bf16[64,512]{1,0:T(8,128)(2,1)S(1)}) custom-call(bf16[256,512]{1,0:T(8,128)(2,1)S(1)} %get-tuple-element.29.q_ref, bf16[256,256]{1,0:T(8,128)(2,1)S(1)} %get-tuple-element.30.kv_ref, bf16[128,256]{1,0:T(8,128)(2,1)S(1)} %get-tuple-element.31.before_ref, ...), custom_call_target="tpu_custom_call" | custom-call | flops 67108864 | bytes 262144 | tf_op jit(solution)/shard_map/pallas_call | solution.py:286
  17.1 1.6 %collective-permute-start.1 = (bf16[64,512]{1,0:T(8,128)(2,1)S(1)}, bf16[64,512]{1,0:T(8,128)(2,1)S(1)}, u32[]{:S(2)}, u32[]{:S(2)}) collective-permute-start(bf16[64,512]{1,0:T(8,128)(2,1)S(1)} %get-tuple-element.35.refs_0_), channel_id=1, source_target_pairs={{0,2},{1,3},{2,0},{3,1},{4,6},{5,7},{6,4},{7,5},{8,10},{9,11},{10,... | collective-permute-start | bytes 196616 | tf_op jit(solution)/shard_map/ppermute | solution.py:232
  18.6 0.0 collective-permute-start.2
  18.6 2.8 %collective-permute-done.1.refs_1_ = bf16[64,512]{1,0:T(8,128)(2,1)S(1)} collective-permute-done((bf16[64,512]{1,0:T(8,128)(2,1)S(1)}, bf16[64,512]{1,0:T(8,128)(2,1)S(1)}, u32[]{:S(2)}, u32[]{:S(2)}) %collective-permute-start.1) | collective-permute-done | bytes 65568 | tf_op jit(solution)/shard_map/ppermute | solution.py:232
  21.4 0.0 collective-permute-start.3
  21.4 1.5 %collective-permute-start.15 = (bf16[512,256]{1,0:T(8,128)(2,1)S(1)}, bf16[512,256]{1,0:T(8,128)(2,1)S(1)}, u32[]{:S(2)}, u32[]{:S(2)}) collective-permute-start(bf16[512,256]{1,0:T(8,128)(2,1)S(1)} %get-tuple-element.52.refs_0_), channel_id=1, source_target_pairs={{0,2},{1,3},{2,0},{3,1},{4,6},{5,7},{6,4},{7,5},{8,10},{9,11},{10,... | collective-permute-start | bytes 786440 | tf_op jit(solution)/shard_map/ppermute | solution.py:232
  22.9 1.1 %shard_map.120 = (bf16[16,720]{1,0:T(8,128)(2,1)S(1)}, bf16[16,720]{1,0:T(8,128)(2,1)S(1)}, bf16[16,720]{1,0:T(8,128)(2,1)S(1)}, bf16[16,720]{1,0:T(8,128)(2,1)S(1)}) custom-call(bf16[64,512]{1,0:T(8,128)(2,1)S(1)} %get-tuple-element.35.refs_0_, bf16[64,512]{1,0:T(8,128)(2,1)S(1)} %collective-permute-done.1.refs_1_, ...), custom_call_target="tpu_custom_call" | custom-call | flops 188743680 | bytes 2949120 | tf_op jit(solution)/shard_map/pallas_call | solution.py:294
  24.0 1.6 %collective-permute-start.4 = (bf16[16,720]{1,0:T(8,128)(2,1)S(1)}, bf16[16,720]{1,0:T(8,128)(2,1)S(1)}, u32[]{:S(2)}, u32[]{:S(2)}) collective-permute-start(bf16[16,720]{1,0:T(8,128)(2,1)S(1)} %get-tuple-element.39), channel_id=1, source_target_pairs={{0,4},{4,0},{8,12},{12,8},{1,5},{5,1},{9,13},{13,9},{2,6},{6,2},{1... | collective-permute-start | bytes 69128 | tf_op jit(solution)/shard_map/ppermute | solution.py:232
  25.6 1.1 %collective-permute-start.5 = (bf16[16,720]{1,0:T(8,128)(2,1)S(1)}, bf16[16,720]{1,0:T(8,128)(2,1)S(1)}, u32[]{:S(2)}, u32[]{:S(2)}) collective-permute-start(bf16[16,720]{1,0:T(8,128)(2,1)S(1)} %get-tuple-element.40), channel_id=1, source_target_pairs={{0,8},{4,12},{8,0},{12,4},{1,9},{5,13},{9,1},{13,5},{2,10},{6,14},... | collective-permute-start | bytes 69128 | tf_op jit(solution)/shard_map/ppermute | solution.py:232
  26.7 1.7 %collective-permute-start.6 = (bf16[16,720]{1,0:T(8,128)(2,1)S(1)}, bf16[16,720]{1,0:T(8,128)(2,1)S(1)}, u32[]{:S(2)}, u32[]{:S(2)}) collective-permute-start(bf16[16,720]{1,0:T(8,128)(2,1)S(1)} %get-tuple-element.41), channel_id=1, source_target_pairs={{0,12},{4,8},{8,4},{12,0},{1,13},{5,9},{9,5},{13,1},{2,14},{6,10},... | collective-permute-start | bytes 69128 | tf_op jit(solution)/shard_map/ppermute | solution.py:232
  28.4 2.2 %collective-permute-done.5 = bf16[16,720]{1,0:T(8,128)(2,1)S(1)} collective-permute-done((bf16[16,720]{1,0:T(8,128)(2,1)S(1)}, bf16[16,720]{1,0:T(8,128)(2,1)S(1)}, u32[]{:S(2)}, u32[]{:S(2)}) %collective-permute-start.5) | collective-permute-done | bytes 23072 | tf_op jit(solution)/shard_map/ppermute | solution.py:232
  30.6 1.7 %collective-permute-done.6 = bf16[16,720]{1,0:T(8,128)(2,1)S(1)} collective-permute-done((bf16[16,720]{1,0:T(8,128)(2,1)S(1)}, bf16[16,720]{1,0:T(8,128)(2,1)S(1)}, u32[]{:S(2)}, u32[]{:S(2)}) %collective-permute-start.6) | collective-permute-done | bytes 23072 | tf_op jit(solution)/shard_map/ppermute | solution.py:232
  32.3 1.2 %collective-permute-start.7 = (bf16[64,720]{1,0:T(8,128)(2,1)S(1)}, bf16[64,720]{1,0:T(8,128)(2,1)S(1)}, u32[]{:S(2)}, u32[]{:S(2)}) collective-permute-start(bf16[64,720]{1,0:T(8,128)(2,1)S(1)} %constant_dynamic-update-slice_fusion.refs_0_), channel_id=1, source_target_pairs={{0,2},{1,3},{2,0},{3,1},{4,6},{5,7},{6,4},{7,5},{8,10},{9,11},{10,... | collective-permute-start | bytes 276488 | tf_op jit(solution)/shard_map/ppermute | solution.py:232
  33.6 3.4 %collective-permute-done.7.refs_1_ = bf16[64,720]{1,0:T(8,128)(2,1)S(1)} collective-permute-done((bf16[64,720]{1,0:T(8,128)(2,1)S(1)}, bf16[64,720]{1,0:T(8,128)(2,1)S(1)}, u32[]{:S(2)}, u32[]{:S(2)}) %collective-permute-start.7) | collective-permute-done | bytes 92192 | tf_op jit(solution)/shard_map/ppermute | solution.py:232
  37.0 0.0 collective-permute-start.9
  37.0 0.0 collective-permute-done.8.refs_2_
  37.0 1.3 %collective-permute-done.9.refs_3_ = bf16[64,720]{1,0:T(8,128)(2,1)S(1)} collective-permute-done((bf16[64,720]{1,0:T(8,128)(2,1)S(1)}, bf16[64,720]{1,0:T(8,128)(2,1)S(1)}, u32[]{:S(2)}, u32[]{:S(2)}) %collective-permute-start.9) | collective-permute-done | bytes 92192 | tf_op jit(solution)/shard_map/ppermute | solution.py:232
  38.3 2.0 %shard_map.121 = (bf16[2,64,720]{2,1,0:T(8,128)(2,1)S(1)}, bf16[2,64,720]{2,1,0:T(8,128)(2,1)S(1)}) custom-call(bf16[64,720]{1,0:T(8,128)(2,1)S(1)} %constant_dynamic-update-slice_fusion.refs_0_, bf16[64,720]{1,0:T(8,128)(2,1)S(1)} %collective-permute-done.7.refs_1_, bf16[64,720]{1,0:T(8,128)(2,1)S(1)} %collective-permute-done.8.refs_2_, ...), custom_call_target="tpu_custom_call" | custom-call | flops 398131200 | bytes 6220800 | tf_op jit(solution)/shard_map/pallas_call | solution.py:312
  40.3 0.2 collective-permute-start.10
  40.6 0.4 collective-permute-start.16
  40.9 0.0 collective-permute-done.15.refs_1_
  40.9 0.2 collective-permute-start.17
  41.1 0.8 %collective-permute-done.10.given_ref = bf16[2,64,720]{2,1,0:T(8,128)(2,1)S(1)} collective-permute-done((bf16[2,64,720]{2,1,0:T(8,128)(2,1)S(1)}, bf16[2,64,720]{2,1,0:T(8,128)(2,1)S(1)}, u32[]{:S(2)}, u32[]{:S(2)}) %collective-permute-start.10) | collective-permute-done | bytes 184352 | tf_op jit(solution)/shard_map/ppermute | solution.py:232
  41.9 1.3 %collective-permute-start.11 = (bf16[64,720]{1,0:T(8,128)(2,1)S(1)}, bf16[64,720]{1,0:T(8,128)(2,1)S(1)}, u32[]{:S(2)}, u32[]{:S(2)}) collective-permute-start(bf16[64,720]{1,0:T(8,128)(2,1)S(1)} %get-tuple-element.45), channel_id=1, source_target_pairs={{0,2},{1,3},{2,0},{3,1},{4,6},{5,7},{6,4},{7,5},{8,10},{9,11},{10,... | collective-permute-start | bytes 276488 | tf_op jit(solution)/shard_map/ppermute | solution.py:232
  43.2 3.6 %collective-permute-done.11.refs_1_ = bf16[64,720]{1,0:T(8,128)(2,1)S(1)} collective-permute-done((bf16[64,720]{1,0:T(8,128)(2,1)S(1)}, bf16[64,720]{1,0:T(8,128)(2,1)S(1)}, u32[]{:S(2)}, u32[]{:S(2)}) %collective-permute-start.11) | collective-permute-done | bytes 92192 | tf_op jit(solution)/shard_map/ppermute | solution.py:232
  46.8 0.2 collective-permute-start.12
  47.0 2.1 %collective-permute-start.13 = (bf16[16,720]{1,0:T(8,128)(2,1)S(1)}, bf16[16,720]{1,0:T(8,128)(2,1)S(1)}, u32[]{:S(2)}, u32[]{:S(2)}) collective-permute-start(bf16[16,720]{1,0:T(8,128)(2,1)S(1)} %get-tuple-element.48), channel_id=1, source_target_pairs={{0,8},{4,12},{8,0},{12,4},{1,9},{5,13},{9,1},{13,5},{2,10},{6,14},... | collective-permute-start | bytes 69128 | tf_op jit(solution)/shard_map/ppermute | solution.py:232
  49.2 2.1 %collective-permute-start.14 = (bf16[16,720]{1,0:T(8,128)(2,1)S(1)}, bf16[16,720]{1,0:T(8,128)(2,1)S(1)}, u32[]{:S(2)}, u32[]{:S(2)}) collective-permute-start(bf16[16,720]{1,0:T(8,128)(2,1)S(1)} %get-tuple-element.49), channel_id=1, source_target_pairs={{0,12},{4,8},{8,4},{12,0},{1,13},{5,9},{9,5},{13,1},{2,14},{6,10},... | collective-permute-start | bytes 69128 | tf_op jit(solution)/shard_map/ppermute | solution.py:232
  51.3 0.9 %shard_map.124.refs_6_ = bf16[720,256]{1,0:T(8,128)(2,1)S(1)} custom-call(bf16[512,256]{1,0:T(8,128)(2,1)S(1)} %get-tuple-element.52.refs_0_, bf16[512,256]{1,0:T(8,128)(2,1)S(1)} %collective-permute-done.15.refs_1_, bf16[512,256]{1,0:T(8,128)(2,1)S(1)} %collective-permute-done.16.refs_2_, bf16[512,256]{1,0:T(8,128)(2,1)S(1)} %collective-permute-done.17.refs_3_, ...), custom_call_target="tpu_custom_call" | custom-call | flops 754974720 | bytes 2949120 | tf_op jit(solution)/shard_map/pallas_call | solution.py:304
  52.2 0.0 collective-permute-done.12.refs_1_
  52.3 2.5 %collective-permute-done.14.refs_3_ = bf16[16,720]{1,0:T(8,128)(2,1)S(1)} collective-permute-done((bf16[16,720]{1,0:T(8,128)(2,1)S(1)}, bf16[16,720]{1,0:T(8,128)(2,1)S(1)}, u32[]{:S(2)}, u32[]{:S(2)}) %collective-permute-start.14) | collective-permute-done | bytes 23072 | tf_op jit(solution)/shard_map/ppermute | solution.py:232
  54.8 1.1 %shard_map.125 = bf16[720,256]{1,0:T(8,128)(2,1)} custom-call(bf16[16,720]{1,0:T(8,128)(2,1)S(1)} %get-tuple-element.46.refs_0_, bf16[16,720]{1,0:T(8,128)(2,1)S(1)} %collective-permute-done.12.refs_1_, bf16[16,720]{1,0:T(8,128)(2,1)S(1)} %collective-permute-done.13.refs_2_, bf16[16,720]{1,0:T(8,128)(2,1)S(1)} %collective-permute-done.14.refs_3_, ...), custom_call_target="tpu_custom_call" | custom-call | tf_op jit(solution)/shard_map/pallas_call | solution.py:327
  (25 shorter events, 0.1 us)
Async XLA Ops:
  0.8 15.0 %collective-permute-start = (bf16[128,256]{1,0:T(8,128)(2,1)S(1)}, bf16[128,256]{1,0:T(8,128)(2,1)S(1)}, u32[]{:S(2)}, u32[]{:S(2)}) collective-permute-start(bf16[128,256]{1,0:T(8,128)(2,1)S(1)} %slice.3), channel_id=1, source_target_pairs={{0,4},{4,8},{8,12},{1,5},{5,9},{9,13},{2,6},{6,10},{10,14},{3,7},{... | collective-permute-start | bytes 196616 | tf_op jit(solution)/shard_map/ppermute | solution.py:265
  5.8 1.8 %copy-start = (bf16[2048,720]{0,1:T(8,128)(2,1)S(1)}, bf16[2048,720]{0,1:T(8,128)(2,1)}, u32[]{:S(2)}) copy-start(bf16[2048,720]{0,1:T(8,128)(2,1)} %param.17) | copy-start | bytes 8847364
  7.6 1.0 %copy-start.4 = (bf16[256,720]{0,1:T(8,128)(2,1)S(1)}, bf16[256,720]{0,1:T(8,128)(2,1)}, u32[]{:S(2)}) copy-start(bf16[256,720]{0,1:T(8,128)(2,1)} %param.16) | copy-start | bytes 1105924
  8.6 0.9 %copy-start.5 = (bf16[256,256]{1,0:T(8,128)(2,1)S(1)}, bf16[256,256]{1,0:T(8,128)(2,1)}, u32[]{:S(2)}) copy-start(bf16[256,256]{1,0:T(8,128)(2,1)} %refs_1_.1) | copy-start | bytes 393220
  9.5 0.9 %copy-start.6 = (bf16[256,512]{1,0:T(8,128)(2,1)S(1)}, bf16[256,512]{1,0:T(8,128)(2,1)}, u32[]{:S(2)}) copy-start(bf16[256,512]{1,0:T(8,128)(2,1)} %refs_0_.1) | copy-start | bytes 786436
  10.5 0.8 %copy-start.7 = (bf16[128,256]{1,0:T(8,128)(2,1)S(1)}, bf16[128,256]{1,0:T(8,128)(2,1)}, u32[]{:S(2)}) copy-start(bf16[128,256]{1,0:T(8,128)(2,1)} %refs_2_.1) | copy-start | bytes 196612
  11.3 0.7 %copy-start.9 = (s32[256,4]{0,1:T(4,128)S(1)}, s32[256,4]{0,1:T(4,128)}, u32[]{:S(2)}) copy-start(s32[256,4]{0,1:T(4,128)} %param.19) | copy-start | bytes 12292
  12.0 0.7 %copy-start.10 = (f32[256,4]{0,1:T(4,128)S(1)}, f32[256,4]{0,1:T(4,128)}, u32[]{:S(2)}) copy-start(f32[256,4]{0,1:T(4,128)} %param.20) | copy-start | bytes 12292
  12.7 0.7 %copy-start.11 = (f32[8]{0:T(128)S(1)}, f32[8]{0:T(128)}, u32[]{:S(2)}) copy-start(f32[8]{0:T(128)} %sinks_ref.1) | copy-start | bytes 100
  13.3 24.9 %copy-start.3 = (bf16[1,360,2880]{2,1,0:T(8,128)(2,1)S(1)}, bf16[1,360,2880]{2,1,0:T(8,128)(2,1)}, u32[]{:S(2)}) copy-start(bf16[1,360,2880]{2,1,0:T(8,128)(2,1)} %param.23) | copy-start | bytes 6220804
  15.8 22.4 %copy-start.1 = (bf16[1,2880,360]{1,2,0:T(8,128)(2,1)S(1)}, bf16[1,2880,360]{1,2,0:T(8,128)(2,1)}, u32[]{:S(2)}) copy-start(bf16[1,2880,360]{1,2,0:T(8,128)(2,1)} %param.21) | copy-start | bytes 6220804
  15.9 22.4 %copy-start.2 = (bf16[1,2880,360]{1,2,0:T(8,128)(2,1)S(1)}, bf16[1,2880,360]{1,2,0:T(8,128)(2,1)}, u32[]{:S(2)}) copy-start(bf16[1,2880,360]{1,2,0:T(8,128)(2,1)} %param.22) | copy-start | bytes 6220804
  15.9 22.4 %copy-start.8 = (f32[2880]{0:T(1024)S(1)}, f32[2880]{0:T(1024)}, u32[]{:S(2)}) copy-start(f32[2880]{0:T(1024)} %refs_4_.1) | copy-start | bytes 34564
  17.1 4.3 %collective-permute-start.1 = (bf16[64,512]{1,0:T(8,128)(2,1)S(1)}, bf16[64,512]{1,0:T(8,128)(2,1)S(1)}, u32[]{:S(2)}, u32[]{:S(2)}) collective-permute-start(bf16[64,512]{1,0:T(8,128)(2,1)S(1)} %get-tuple-element.35.refs_0_), channel_id=1, source_target_pairs={{0,2},{1,3},{2,0},{3,1},{4,6},{5,7},{6,4},{7,5},{8,10},{9,11},{10,... | collective-permute-start | bytes 196616 | tf_op jit(solution)/shard_map/ppermute | solution.py:232
  18.6 4.3 %collective-permute-start.2 = (bf16[64,512]{1,0:T(8,128)(2,1)S(1)}, bf16[64,512]{1,0:T(8,128)(2,1)S(1)}, u32[]{:S(2)}, u32[]{:S(2)}) collective-permute-start(bf16[64,512]{1,0:T(8,128)(2,1)S(1)} %get-tuple-element.35.refs_0_), channel_id=1, source_target_pairs={{0,1},{1,0},{2,3},{3,2},{4,5},{5,4},{6,7},{7,6},{8,9},{9,8},{10,11... | collective-permute-start | bytes 196616 | tf_op jit(solution)/shard_map/ppermute | solution.py:232
  21.4 1.5 %collective-permute-start.3 = (bf16[64,512]{1,0:T(8,128)(2,1)S(1)}, bf16[64,512]{1,0:T(8,128)(2,1)S(1)}, u32[]{:S(2)}, u32[]{:S(2)}) collective-permute-start(bf16[64,512]{1,0:T(8,128)(2,1)S(1)} %collective-permute-done.1.refs_1_), channel_id=1, source_target_pairs={{0,1},{1,0},{2,3},{3,2},{4,5},{5,4},{6,7},{7,6},{8,9},{9,8},{10,11... | collective-permute-start | bytes 196616 | tf_op jit(solution)/shard_map/ppermute | solution.py:232
  21.4 19.5 %collective-permute-start.15 = (bf16[512,256]{1,0:T(8,128)(2,1)S(1)}, bf16[512,256]{1,0:T(8,128)(2,1)S(1)}, u32[]{:S(2)}, u32[]{:S(2)}) collective-permute-start(bf16[512,256]{1,0:T(8,128)(2,1)S(1)} %get-tuple-element.52.refs_0_), channel_id=1, source_target_pairs={{0,2},{1,3},{2,0},{3,1},{4,6},{5,7},{6,4},{7,5},{8,10},{9,11},{10,... | collective-permute-start | bytes 786440 | tf_op jit(solution)/shard_map/ppermute | solution.py:232
  24.0 4.5 %collective-permute-start.4 = (bf16[16,720]{1,0:T(8,128)(2,1)S(1)}, bf16[16,720]{1,0:T(8,128)(2,1)S(1)}, u32[]{:S(2)}, u32[]{:S(2)}) collective-permute-start(bf16[16,720]{1,0:T(8,128)(2,1)S(1)} %get-tuple-element.39), channel_id=1, source_target_pairs={{0,4},{4,0},{8,12},{12,8},{1,5},{5,1},{9,13},{13,9},{2,6},{6,2},{1... | collective-permute-start | bytes 69128 | tf_op jit(solution)/shard_map/ppermute | solution.py:232
  25.6 5.0 %collective-permute-start.5 = (bf16[16,720]{1,0:T(8,128)(2,1)S(1)}, bf16[16,720]{1,0:T(8,128)(2,1)S(1)}, u32[]{:S(2)}, u32[]{:S(2)}) collective-permute-start(bf16[16,720]{1,0:T(8,128)(2,1)S(1)} %get-tuple-element.40), channel_id=1, source_target_pairs={{0,8},{4,12},{8,0},{12,4},{1,9},{5,13},{9,1},{13,5},{2,10},{6,14},... | collective-permute-start | bytes 69128 | tf_op jit(solution)/shard_map/ppermute | solution.py:232
  26.7 5.6 %collective-permute-start.6 = (bf16[16,720]{1,0:T(8,128)(2,1)S(1)}, bf16[16,720]{1,0:T(8,128)(2,1)S(1)}, u32[]{:S(2)}, u32[]{:S(2)}) collective-permute-start(bf16[16,720]{1,0:T(8,128)(2,1)S(1)} %get-tuple-element.41), channel_id=1, source_target_pairs={{0,12},{4,8},{8,4},{12,0},{1,13},{5,9},{9,5},{13,1},{2,14},{6,10},... | collective-permute-start | bytes 69128 | tf_op jit(solution)/shard_map/ppermute | solution.py:232
  32.3 4.6 %collective-permute-start.7 = (bf16[64,720]{1,0:T(8,128)(2,1)S(1)}, bf16[64,720]{1,0:T(8,128)(2,1)S(1)}, u32[]{:S(2)}, u32[]{:S(2)}) collective-permute-start(bf16[64,720]{1,0:T(8,128)(2,1)S(1)} %constant_dynamic-update-slice_fusion.refs_0_), channel_id=1, source_target_pairs={{0,2},{1,3},{2,0},{3,1},{4,6},{5,7},{6,4},{7,5},{8,10},{9,11},{10,... | collective-permute-start | bytes 276488 | tf_op jit(solution)/shard_map/ppermute | solution.py:232
  33.6 3.4 %collective-permute-start.8 = (bf16[64,720]{1,0:T(8,128)(2,1)S(1)}, bf16[64,720]{1,0:T(8,128)(2,1)S(1)}, u32[]{:S(2)}, u32[]{:S(2)}) collective-permute-start(bf16[64,720]{1,0:T(8,128)(2,1)S(1)} %constant_dynamic-update-slice_fusion.refs_0_), channel_id=1, source_target_pairs={{0,1},{1,0},{2,3},{3,2},{4,5},{5,4},{6,7},{7,6},{8,9},{9,8},{10,11... | collective-permute-start | bytes 276488 | tf_op jit(solution)/shard_map/ppermute | solution.py:232
  37.0 1.3 %collective-permute-start.9 = (bf16[64,720]{1,0:T(8,128)(2,1)S(1)}, bf16[64,720]{1,0:T(8,128)(2,1)S(1)}, u32[]{:S(2)}, u32[]{:S(2)}) collective-permute-start(bf16[64,720]{1,0:T(8,128)(2,1)S(1)} %collective-permute-done.7.refs_1_), channel_id=1, source_target_pairs={{0,1},{1,0},{2,3},{3,2},{4,5},{5,4},{6,7},{7,6},{8,9},{9,8},{10,11... | collective-permute-start | bytes 276488 | tf_op jit(solution)/shard_map/ppermute | solution.py:232
  40.3 1.5 %collective-permute-start.10 = (bf16[2,64,720]{2,1,0:T(8,128)(2,1)S(1)}, bf16[2,64,720]{2,1,0:T(8,128)(2,1)S(1)}, u32[]{:S(2)}, u32[]{:S(2)}) collective-permute-start(bf16[2,64,720]{2,1,0:T(8,128)(2,1)S(1)} %get-tuple-element.43), channel_id=1, source_target_pairs={{0,1},{1,0},{2,3},{3,2},{4,5},{5,4},{6,7},{7,6},{8,9},{9,8},{10,11... | collective-permute-start | bytes 552968 | tf_op jit(solution)/shard_map/ppermute | solution.py:232
  40.6 10.7 %collective-permute-start.16 = (bf16[512,256]{1,0:T(8,128)(2,1)S(1)}, bf16[512,256]{1,0:T(8,128)(2,1)S(1)}, u32[]{:S(2)}, u32[]{:S(2)}) collective-permute-start(bf16[512,256]{1,0:T(8,128)(2,1)S(1)} %get-tuple-element.52.refs_0_), channel_id=1, source_target_pairs={{0,1},{1,0},{2,3},{3,2},{4,5},{5,4},{6,7},{7,6},{8,9},{9,8},{10,11... | collective-permute-start | bytes 786440 | tf_op jit(solution)/shard_map/ppermute | solution.py:232
  40.9 10.4 %collective-permute-start.17 = (bf16[512,256]{1,0:T(8,128)(2,1)S(1)}, bf16[512,256]{1,0:T(8,128)(2,1)S(1)}, u32[]{:S(2)}, u32[]{:S(2)}) collective-permute-start(bf16[512,256]{1,0:T(8,128)(2,1)S(1)} %collective-permute-done.15.refs_1_), channel_id=1, source_target_pairs={{0,1},{1,0},{2,3},{3,2},{4,5},{5,4},{6,7},{7,6},{8,9},{9,8},{10,11... | collective-permute-start | bytes 786440 | tf_op jit(solution)/shard_map/ppermute | solution.py:232
  41.9 4.9 %collective-permute-start.11 = (bf16[64,720]{1,0:T(8,128)(2,1)S(1)}, bf16[64,720]{1,0:T(8,128)(2,1)S(1)}, u32[]{:S(2)}, u32[]{:S(2)}) collective-permute-start(bf16[64,720]{1,0:T(8,128)(2,1)S(1)} %get-tuple-element.45), channel_id=1, source_target_pairs={{0,2},{1,3},{2,0},{3,1},{4,6},{5,7},{6,4},{7,5},{8,10},{9,11},{10,... | collective-permute-start | bytes 276488 | tf_op jit(solution)/shard_map/ppermute | solution.py:232
  46.8 5.4 %collective-permute-start.12 = (bf16[16,720]{1,0:T(8,128)(2,1)S(1)}, bf16[16,720]{1,0:T(8,128)(2,1)S(1)}, u32[]{:S(2)}, u32[]{:S(2)}) collective-permute-start(bf16[16,720]{1,0:T(8,128)(2,1)S(1)} %get-tuple-element.47), channel_id=1, source_target_pairs={{0,4},{4,0},{8,12},{12,8},{1,5},{5,1},{9,13},{13,9},{2,6},{6,2},{1... | collective-permute-start | bytes 69128 | tf_op jit(solution)/shard_map/ppermute | solution.py:232
  47.0 5.2 %collective-permute-start.13 = (bf16[16,720]{1,0:T(8,128)(2,1)S(1)}, bf16[16,720]{1,0:T(8,128)(2,1)S(1)}, u32[]{:S(2)}, u32[]{:S(2)}) collective-permute-start(bf16[16,720]{1,0:T(8,128)(2,1)S(1)} %get-tuple-element.48), channel_id=1, source_target_pairs={{0,8},{4,12},{8,0},{12,4},{1,9},{5,13},{9,1},{13,5},{2,10},{6,14},... | collective-permute-start | bytes 69128 | tf_op jit(solution)/shard_map/ppermute | solution.py:232
  49.2 5.6 %collective-permute-start.14 = (bf16[16,720]{1,0:T(8,128)(2,1)S(1)}, bf16[16,720]{1,0:T(8,128)(2,1)S(1)}, u32[]{:S(2)}, u32[]{:S(2)}) collective-permute-start(bf16[16,720]{1,0:T(8,128)(2,1)S(1)} %get-tuple-element.49), channel_id=1, source_target_pairs={{0,12},{4,8},{8,4},{12,0},{1,13},{5,9},{9,5},{13,1},{2,14},{6,10},... | collective-permute-start | bytes 69128 | tf_op jit(solution)/shard_map/ppermute | solution.py:232

commit v3 on v2

--- a/solution.py
+++ b/solution.py
@@ -39,6 +39,10 @@
         compiler_params=pltpu.CompilerParams(vmem_limit_bytes=VMEM_LIMIT),
         cost_estimate=pl.CostEstimate(flops=flops, bytes_accessed=moved, transcendentals=0),
     )
+
+
+def in_hbm(array):
+    return pltpu.with_memory_space_constraint(array, pltpu.HBM)
 
 
 def bf16(*shape):
@@ -138,7 +142,7 @@
 
 def second_kernel(q_ref, kv_ref, before_ref, rim_ref, sinks_ref, late_ref, placing_ref, all_ref, rows_ref):
     first = lax.axis_index("seq") == 0
-    rim = jnp.where(first, before_ref[...], rim_ref[...])
+    rim = jnp.where(first, before_ref[...], rim_ref[rim_ref.shape[0] - KEYS_SEEN :])
     groups = kv_ref.shape[1] // PAIR
     rows_of = []
     for g in range(groups):
@@ -155,39 +159,59 @@
     return lax.bitwise_xor(me, CORES * k + (1 if sibling else 0))
 
 
-def project_rows_kernel(steps, *refs):
-    blocks = refs[: 2 * steps]
-    w_ref, residual_ref, placing_ref = refs[2 * steps : 2 * steps + 3]
-    outgoing, rows_ref = refs[2 * steps + 3 : -1], refs[-1]
-    width = blocks[0].shape[1]
+def add_products(total, first, blocks, w_ref, steps, dims, swapped=False):
+    width = blocks[0].shape[0 if swapped else 1] if blocks else 0
+    for i, block in enumerate(blocks, first):
+        at = pl.multiple_of(origin(i % steps, i >= steps) * width, 128)
+        w = w_ref[:, pl.ds(at, width)]
+        total += dot(w, block[...], dims) if swapped else dot(block[...], w, dims)
+    return total
+
+
+def rows_near_kernel(steps, mine_ref, theirs_ref, w_ref, residual_ref, placing_ref, total_ref):
     total = dot(placing_ref[...], residual_ref[...], NT)
-    for i, block in enumerate(blocks):
-        at = pl.multiple_of(origin(i % steps, i >= steps) * width, 128)
-        total += dot(block[...], w_ref[:, pl.ds(at, width)], NT)
+    total = add_products(total, 0, [mine_ref], w_ref, steps, NT)
+    total_ref[...] = add_products(total, steps, [theirs_ref], w_ref, steps, NT)
+
+
+def rows_chips_kernel(steps, *refs):
+    blocks, (before_ref, w_ref, total_ref) = refs[: steps - 1], refs[steps - 1 :]
+    total_ref[...] = add_products(before_ref[...], 1, blocks, w_ref, steps, NT)
+
+
+def rows_last_kernel(steps, *refs):
+    blocks, (before_ref, w_ref) = refs[: steps - 1], refs[steps - 1 : steps + 1]
+    outgoing, rows_ref = refs[steps + 1 : -1], refs[-1]
+    total = add_products(before_ref[...], steps + 1, blocks, w_ref, steps, NT)
     rows_ref[...] = total.astype(jnp.bfloat16).reshape(rows_ref.shape)
     me = lax.axis_index("seq")
     for k, out_ref in enumerate(outgoing):
         out_ref[...] = rows_ref[lax.bitwise_xor(me, k)]
 
 
+def stack_kernel(*refs):
+    for i, block in enumerate(refs[:-1]):
+        refs[-1][i * CAP : (i + 1) * CAP] = block[...]
+
+
 def project_kernel(steps, *refs):
     blocks = refs[: 2 * steps]
     w_ref, residual_ref, resid_ref = refs[2 * steps :]
-    width = blocks[0].shape[0]
-    total = residual_ref[...].astype(jnp.float32)
-    for i, block in enumerate(blocks):
-        at = pl.multiple_of(origin(i % steps, i >= steps) * width, 128)
-        total += dot(w_ref[:, pl.ds(at, width)], block[...], NN)
+    total = add_products(residual_ref[...].astype(jnp.float32), 0, blocks, w_ref, steps, NN, True)
     resid_ref[...] = total.astype(jnp.bfloat16)
 
 
-def expert_kernel(steps, *refs):
-    blocks = refs[: 2 * steps]
-    gain_ref, gate_ref, up_ref, down_ref, kept_ref, given_ref, blocks_ref, rows_ref = refs[2 * steps :]
+def expert_kernel(live, steps, *refs):
     cuts = CORES * steps
-    width = blocks[0].shape[1]
-    for i, block in enumerate(blocks):
-        blocks_ref[origin(i % steps, i >= steps)] = block[...]
+    most, rest = refs[:cuts], refs[cuts : 2 * cuts]
+    gain_ref, gate_ref, up_ref, down_ref, kept_ref, given_ref, blocks_ref, rows_ref = refs[2 * cuts :]
+    width = most[0].shape[1]
+    far = (live - 2) * CAP
+    for i in range(cuts):
+        p = origin(i % steps, i >= steps)
+        blocks_ref[p, :far] = most[i][:far]
+        blocks_ref[p, far : far + CAP] = rest[i][...]
+        blocks_ref[p, far + CAP :] = most[i][far:]
     wide = [blocks_ref[p].astype(jnp.float32) for p in range(cuts)]
     squares = sum(jnp.sum(b * b, axis=1, keepdims=True) for b in wide)
     scale = lax.rsqrt(squares / (cuts * width) + norm_eps)
@@ -206,8 +230,10 @@
 
 
 def add_cores_kernel(kept_ref, given_ref, *out_refs):
-    for k, out_ref in enumerate(out_refs):
-        total = kept_ref[k].astype(jnp.float32) + given_ref[k].astype(jnp.float32)
+    half = out_refs[0].shape[0]
+    for i, out_ref in enumerate(out_refs):
+        rows = slice(i % 2 * half, (i % 2 + 1) * half)
+        total = kept_ref[i // 2, rows].astype(jnp.float32) + given_ref[i // 2, rows].astype(jnp.float32)
         out_ref[...] = total.astype(jnp.bfloat16)
 
 
@@ -222,7 +248,7 @@
     mix_hi_ref, mix_lo_ref, resid_ref, out_ref, rows_ref = refs[live:]
     me = lax.axis_index("seq")
     for k in range(live):
-        rows_ref[lax.bitwise_xor(me, k)] = blocks[k][...]
+        rows_ref[lax.bitwise_xor(me, live - 1 - k)] = blocks[k][...]
     rows = rows_ref[...].reshape(live * CAP, -1)
     mixed = dot(rows, mix_hi_ref[...], TN) + dot(rows, mix_lo_ref[...], TN)
     out_ref[...] = (resid_ref[...].astype(jnp.float32) + mixed).astype(jnp.bfloat16)
@@ -235,7 +261,7 @@
 def gather_cuts(block):
     steps = lax.axis_size("cuts") // CORES
     mine = [block] + [swap(block, "cuts", CORES * k) for k in range(1, steps)]
-    return mine + [swap(b, "cuts", 1) for b in mine]
+    return mine, [swap(b, "cuts", 1) for b in mine]
 
 
 def shards(
@@ -262,7 +288,7 @@
     heads = head_rows // HEAD_SIZE
     width = norm_gain.shape[0]
 
-    rim = lax.ppermute(keyvals[toks - KEYS_SEEN :], "seq", [(i, i + 1) for i in range(size - 1)])
+    rim = lax.ppermute(keyvals, "seq", [(i, i + 1) for i in range(size - 1)])
     loads = (queries, keyvals, preceding_keyvalues, w_out.T, residual.T)
     q, kv, before, w_t, residual_t, placing, mix_hi, mix_lo, sinks, late = call(
         functools.partial(first_kernel, live),
@@ -282,7 +308,7 @@
         hbm=range(1, 8),
         flops=4 * toks * SPAN * head_rows,
         moved=2 * (w_out.size + residual.size + queries.size),
-    )(attention_sink_logits, *loads, expert_ids.T, route_weights.T)
+    )(attention_sink_logits, *(in_hbm(a) for a in (*loads, expert_ids.T, route_weights.T)))
     attended, rows = call(
         second_kernel,
         (bf16(head_rows, toks), bf16(slots, head_rows)),
@@ -291,39 +317,60 @@
         moved=2 * queries.size,
     )(q, kv, before, rim, sinks, late, placing)
 
+    mine, theirs = gather_cuts(rows)
+    total = jax.ShapeDtypeStruct((slots, feats), jnp.float32)
+    part = dict(flops=slots * w_out.size // 2, moved=w_out.size // 2)
+    near = call(functools.partial(rows_near_kernel, steps), total, n_in=5, **part)(
+        mine[0], theirs[0], w_t, residual_t, placing
+    )
+    chips = call(functools.partial(rows_chips_kernel, steps), total, n_in=steps + 1, **part)(
+        *mine[1:], near, w_t
+    )
     outgoing = call(
-        functools.partial(project_rows_kernel, steps),
+        functools.partial(rows_last_kernel, steps),
         (bf16(CAP, feats),) * live,
-        n_in=cuts + 3,
+        n_in=steps + 1,
         scratch=[pltpu.VMEM((live, CAP, feats), jnp.bfloat16)],
-        flops=2 * slots * w_out.size,
-        moved=2 * w_out.size,
-    )(*gather_cuts(rows), w_t, residual_t, placing)
-    arrived = [outgoing[0]] + [swap(outgoing[k], "seq", k) for k in range(1, live)]
-
+        **part,
+    )(*theirs[1:], chips, w_t)
+
+    arrived = [swap(outgoing[k], "seq", k) for k in range(live - 1, 0, -1)] + [outgoing[0]]
+    most = call(stack_kernel, bf16(slots - CAP, feats), n_in=live - 1)(*arrived[:-2], arrived[-1])
+    most_mine, most_theirs = gather_cuts(most)
+    rest_mine, rest_theirs = gather_cuts(arrived[-2])
+
+    mine, theirs = gather_cuts(attended)
     resid = call(
         functools.partial(project_kernel, steps),
         bf16(feats, toks),
         n_in=cuts + 2,
         flops=2 * toks * w_out.size,
         moved=2 * w_out.size,
-    )(*gather_cuts(attended), w_t, residual_t)
+    )(*mine, *theirs, w_t, residual_t)
 
     kept, given = call(
-        functools.partial(expert_kernel, steps),
+        functools.partial(expert_kernel, live, steps),
         (bf16(steps, slots, feats),) * 2,
-        n_in=cuts + 4,
+        n_in=2 * cuts + 4,
         scratch=[
             pltpu.VMEM((cuts, slots, feats), jnp.bfloat16),
             pltpu.VMEM((slots, width), jnp.bfloat16),
         ],
         flops=6 * slots * w_gate.size,
         moved=6 * w_gate.size,
-    )(*gather_cuts(jnp.concatenate(arrived, axis=0)), norm_gain, w_gate[0].T, w_up[0].T, w_down[0])
-    sums = call(add_cores_kernel, (bf16(slots, feats),) * steps, n_in=2)(kept, swap(given, "cuts", 1))
-    sums = [sums[0]] + [swap(sums[k], "cuts", CORES * k) for k in range(1, steps)]
-    returned = call(functools.partial(add_chips_kernel, steps), (bf16(CAP, feats),) * live, n_in=steps)(*sums)
-    returned = [returned[0]] + [swap(returned[k], "seq", k) for k in range(1, live)]
+    )(*most_mine, *most_theirs, *rest_mine, *rest_theirs, norm_gain, w_gate[0].T, w_up[0].T, w_down[0])
+    sums = call(add_cores_kernel, (bf16(slots // 2, feats),) * (2 * steps), n_in=2)(
+        kept, swap(given, "cuts", 1)
+    )
+    returned = []
+    for half in range(2):
+        parts = [sums[half]] + [swap(sums[2 * k + half], "cuts", CORES * k) for k in range(1, steps)]
+        blocks = call(functools.partial(add_chips_kernel, steps), (bf16(CAP, feats),) * (live // 2), n_in=steps)(
+            *parts
+        )
+        for block in blocks:
+            k = live - 1 - len(returned)
+            returned.append(swap(block, "seq", k) if k else block)
     out = call(
         functools.partial(combine_kernel, live),
         bf16(feats, toks),

time: 56.4 us -> 51.4 us (0.911)
  local copies, waits for them, and re-layouts: 8.41 us -> 0.67 us
  waiting for transfers between devices: 18.3 us -> 19.9 us
  starting transfers between devices: 20.2 us -> 21 us
    unnamed x27 -> x10, local copies, waits for them, and re-layouts: 7.57 us -> 0.67 us
    ppermute x17 -> x21, waiting for transfers between devices: 18.3 us -> 19.9 us  [swap(): lax.ppermute(block, axis, [(i, i ^ mask) for i in range(lax.axis_size(axi...]
    slice x1 -> x0, local copies, waits for them, and re-layouts: 0.84 us -> none  [shards(): keyvals[toks - KEYS_SEEN:]]
    ppermute x17 -> x21, starting transfers between devices: 15.3 us -> 16.1 us  [swap(): lax.ppermute(block, axis, [(i, i ^ mask) for i in range(lax.axis_size(axi...]
    pallas_call x4 -> x8, Pallas kernels: 3.19 us -> 3.51 us  [the longest x1 2.07 us: shards(): call(functools.partial(expert_kernel, live, steps), (bf16(steps, slots, f...]
  transfers between devices with their start and end apart: 18 -> 22, of which waited for: 8 -> 13; matrix products, arithmetic and copies ran while one was open for 0% -> 0% of each run, Pallas kernels for 12% -> 14%
where the time goes in v3:
time: 51.4 us; the launch traced here: 51.2 us
  starting transfers between devices  21 us (41%)
  waiting for transfers between devices  19.9 us (39%)
  Pallas kernels  9.45 us (18%)
  local copies, waits for them, and re-layouts  0.67 us (1%)
    ppermute x21, waiting for transfers between devices, swap(): lax.ppermute(block, axis, [(i, i ^ mask) for i in range(lax.axis_size(axi...  19.9 us
    ppermute x21, starting transfers between devices, swap(): lax.ppermute(block, axis, [(i, i ^ mask) for i in range(lax.axis_size(axi...  16.1 us
    ppermute x1, starting transfers between devices, shards(): rim = lax.ppermute(keyvals, 'seq', [(i, i + 1) for i in range(size - 1)])  4.92 us
    pallas_call x1, Pallas kernels, shards(): call(functools.partial(first_kernel, live), (*(bf16(*a.shape) for a in lo...  2.68 us
    pallas_call x1, Pallas kernels, shards(): call(functools.partial(expert_kernel, live, steps), (bf16(steps, slots, f...  2.07 us
    pallas_call x1, Pallas kernels, shards(): call(second_kernel, (bf16(head_rows, toks), bf16(slots, head_rows)), n_in...  1.18 us
    pallas_call x1, Pallas kernels, shards(): call(functools.partial(combine_kernel, live), bf16(feats, toks), n_in=liv...  1.14 us
  transfers between devices with their start and end apart: 22, of which 13 were waited for; matrix products, arithmetic and copies ran while one was open for 0% of the time, Pallas kernels for 14%

profile of v3, /device:TPU:0, one launch (start us, length us, event | category | flops | bytes accessed | tf_op | source)
XLA Modules:
  0.0 51.2 jit_solution(3004402444141612892)
XLA Ops:
  0.0 4.9 %collective-permute-start = (bf16[256,256]{1,0:T(8,128)(2,1)}, bf16[256,256]{1,0:T(8,128)(2,1)S(1)}, u32[]{:S(2)}, u32[]{:S(2)}) collective-permute-start(bf16[256,256]{1,0:T(8,128)(2,1)} %refs_1_.1), channel_id=1, source_target_pairs={{0,4},{4,8},{8,12},{1,5},{5,9},{9,13},{2,6},{6,10},{10,14},{3,7},{... | collective-permute-start | bytes 393224 | tf_op jit(solution)/shard_map/ppermute | solution.py:291
  4.9 0.6 %copy-done.4 = f32[8]{0:T(128)S(1)} copy-done((f32[8]{0:T(128)S(1)}, f32[8]{0:T(128)}, u32[]{:S(2)}) %copy-start.4) | copy-done | bytes 56
  5.6 2.7 %shard_map.118 = (bf16[256,512]{1,0:T(8,128)(2,1)S(1)}, bf16[256,256]{1,0:T(8,128)(2,1)S(1)}, bf16[128,256]{1,0:T(8,128)(2,1)S(1)}, bf16[720,2048]{1,0:T(8,128)(...) custom-call(f32[8]{0:T(128)S(1)} %copy-done.4, ...), custom_call_target="tpu_custom_call" | custom-call | flops 134217728 | bytes 3579904 | tf_op jit(solution)/shard_map/pallas_call | solution.py:293
  8.3 0.0 collective-permute-done.rim_ref
  8.3 1.2 %shard_map.119 = (bf16[512,256]{1,0:T(8,128)(2,1)S(1)}, bf16[64,512]{1,0:T(8,128)(2,1)S(1)}) custom-call(bf16[256,512]{1,0:T(8,128)(2,1)S(1)} %get-tuple-element.31.q_ref, bf16[256,256]{1,0:T(8,128)(2,1)S(1)} %get-tuple-element.32.kv_ref, bf16[128,256]{1,0:T(8,128)(2,1)S(1)} %get-tuple-element.33.before_ref, ...), custom_call_target="tpu_custom_call" | custom-call | flops 67108864 | bytes 262144 | tf_op jit(solution)/shard_map/pallas_call | solution.py:312
  9.5 1.6 %collective-permute-start.1 = (bf16[64,512]{1,0:T(8,128)(2,1)S(1)}, bf16[64,512]{1,0:T(8,128)(2,1)S(1)}, u32[]{:S(2)}, u32[]{:S(2)}) collective-permute-start(bf16[64,512]{1,0:T(8,128)(2,1)S(1)} %get-tuple-element.37.mine_ref), channel_id=1, source_target_pairs={{0,2},{1,3},{2,0},{3,1},{4,6},{5,7},{6,4},{7,5},{8,10},{9,11},{10,... | collective-permute-start | bytes 196616 | tf_op jit(solution)/shard_map/ppermute | solution.py:258
  11.0 0.5 %collective-permute-start.19 = (bf16[512,256]{1,0:T(8,128)(2,1)S(1)}, bf16[512,256]{1,0:T(8,128)(2,1)S(1)}, u32[]{:S(2)}, u32[]{:S(2)}) collective-permute-start(bf16[512,256]{1,0:T(8,128)(2,1)S(1)} %get-tuple-element.56.refs_0_), channel_id=1, source_target_pairs={{0,2},{1,3},{2,0},{3,1},{4,6},{5,7},{6,4},{7,5},{8,10},{9,11},{10,... | collective-permute-start | bytes 786440 | tf_op jit(solution)/shard_map/ppermute | solution.py:258
  11.6 2.9 %collective-permute-done.1.refs_0_ = bf16[64,512]{1,0:T(8,128)(2,1)S(1)} collective-permute-done((bf16[64,512]{1,0:T(8,128)(2,1)S(1)}, bf16[64,512]{1,0:T(8,128)(2,1)S(1)}, u32[]{:S(2)}, u32[]{:S(2)}) %collective-permute-start.1) | collective-permute-done | bytes 65568 | tf_op jit(solution)/shard_map/ppermute | solution.py:258
  14.5 0.0 collective-permute-done.3.theirs_ref
  14.5 0.6 %shard_map.120.refs_1_ = f32[64,720]{1,0:T(8,128)S(1)} custom-call(bf16[64,512]{1,0:T(8,128)(2,1)S(1)} %get-tuple-element.37.mine_ref, bf16[64,512]{1,0:T(8,128)(2,1)S(1)} %collective-permute-done.3.theirs_ref, bf16[720,2048]{1,0:T(8,128)(2,1)S(1)} %get-tuple-element.38.w_ref.refs_2_.refs_4_, bf16[720,256]{1,0:T(8,128)(2,1)S(1)} %get-tuple-element.39.residual_ref.refs_5_, ...), custom_call_target="tpu_custom_call" | custom-call | flops 47185920 | bytes 737280 | tf_op jit(solution)/shard_map/pallas_call | solution.py:323
  15.2 0.0 copy-start.2
  15.2 0.4 shard_map.121.refs_1_
  15.5 0.0 copy-start
  15.6 0.0 copy-start.3
  15.6 0.2 collective-permute-done.2.refs_0_
  15.8 0.4 shard_map.122
  16.1 4.1 %collective-permute-start.4 = (bf16[16,720]{1,0:T(8,128)(2,1)S(1)}, bf16[16,720]{1,0:T(8,128)(2,1)S(1)}, u32[]{:S(2)}, u32[]{:S(2)}) collective-permute-start(bf16[16,720]{1,0:T(8,128)(2,1)S(1)} %get-tuple-element.40), channel_id=1, source_target_pairs={{0,12},{4,8},{8,4},{12,0},{1,13},{5,9},{9,5},{13,1},{2,14},{6,10},... | collective-permute-start | bytes 69128 | tf_op jit(solution)/shard_map/ppermute | solution.py:258
  20.3 0.0 collective-permute-start.5
  20.3 1.8 %collective-permute-done.4.refs_0_ = bf16[16,720]{1,0:T(8,128)(2,1)S(1)} collective-permute-done((bf16[16,720]{1,0:T(8,128)(2,1)S(1)}, bf16[16,720]{1,0:T(8,128)(2,1)S(1)}, u32[]{:S(2)}, u32[]{:S(2)}) %collective-permute-start.4) | collective-permute-done | bytes 23072 | tf_op jit(solution)/shard_map/ppermute | solution.py:258
  22.1 2.9 %collective-permute-done.5.refs_1_ = bf16[16,720]{1,0:T(8,128)(2,1)S(1)} collective-permute-done((bf16[16,720]{1,0:T(8,128)(2,1)S(1)}, bf16[16,720]{1,0:T(8,128)(2,1)S(1)}, u32[]{:S(2)}, u32[]{:S(2)}) %collective-permute-start.5) | collective-permute-done | bytes 23072 | tf_op jit(solution)/shard_map/ppermute | solution.py:258
  25.0 1.7 %collective-permute-start.6 = (bf16[48,720]{1,0:T(8,128)(2,1)S(1)}, bf16[48,720]{1,0:T(8,128)(2,1)S(1)}, u32[]{:S(2)}, u32[]{:S(2)}) collective-permute-start(bf16[48,720]{1,0:T(8,128)(2,1)S(1)} %shard_map.123.refs_0_), channel_id=1, source_target_pairs={{0,2},{1,3},{2,0},{3,1},{4,6},{5,7},{6,4},{7,5},{8,10},{9,11},{10,... | collective-permute-start | bytes 207368 | tf_op jit(solution)/shard_map/ppermute | solution.py:258
  26.6 0.0 collective-permute-start.7
  26.6 2.8 %collective-permute-done.6.refs_1_ = bf16[48,720]{1,0:T(8,128)(2,1)S(1)} collective-permute-done((bf16[48,720]{1,0:T(8,128)(2,1)S(1)}, bf16[48,720]{1,0:T(8,128)(2,1)S(1)}, u32[]{:S(2)}, u32[]{:S(2)}) %collective-permute-start.6) | collective-permute-done | bytes 69152 | tf_op jit(solution)/shard_map/ppermute | solution.py:258
  29.4 0.0 collective-permute-start.8
  29.4 1.1 %collective-permute-done.9.refs_4_ = bf16[16,720]{1,0:T(8,128)(2,1)S(1)} collective-permute-done((bf16[16,720]{1,0:T(8,128)(2,1)S(1)}, bf16[16,720]{1,0:T(8,128)(2,1)S(1)}, u32[]{:S(2)}, u32[]{:S(2)}) %collective-permute-start.9) | collective-permute-done | bytes 23072 | tf_op jit(solution)/shard_map/ppermute | solution.py:258
  30.5 0.5 %collective-permute-start.10 = (bf16[16,720]{1,0:T(8,128)(2,1)S(1)}, bf16[16,720]{1,0:T(8,128)(2,1)S(1)}, u32[]{:S(2)}, u32[]{:S(2)}) collective-permute-start(bf16[16,720]{1,0:T(8,128)(2,1)S(1)} %collective-permute-done.9.refs_4_), channel_id=1, source_target_pairs={{0,2},{1,3},{2,0},{3,1},{4,6},{5,7},{6,4},{7,5},{8,10},{9,11},{10,... | collective-permute-start | bytes 69128 | tf_op jit(solution)/shard_map/ppermute | solution.py:258
  31.0 0.2 collective-permute-start.11
  31.2 3.1 %collective-permute-done.10.refs_5_ = bf16[16,720]{1,0:T(8,128)(2,1)S(1)} collective-permute-done((bf16[16,720]{1,0:T(8,128)(2,1)S(1)}, bf16[16,720]{1,0:T(8,128)(2,1)S(1)}, u32[]{:S(2)}, u32[]{:S(2)}) %collective-permute-start.10) | collective-permute-done | bytes 23072 | tf_op jit(solution)/shard_map/ppermute | solution.py:258
  34.3 0.0 collective-permute-start.12
  34.3 0.0 collective-permute-done.11.refs_6_
  34.3 0.5 collective-permute-start.20
  34.8 0.1 collective-permute-start.21
  34.9 0.6 %collective-permute-done.12.refs_7_ = bf16[16,720]{1,0:T(8,128)(2,1)S(1)} collective-permute-done((bf16[16,720]{1,0:T(8,128)(2,1)S(1)}, bf16[16,720]{1,0:T(8,128)(2,1)S(1)}, u32[]{:S(2)}, u32[]{:S(2)}) %collective-permute-start.12) | collective-permute-done | bytes 23072 | tf_op jit(solution)/shard_map/ppermute | solution.py:258
  35.5 2.1 %shard_map.124 = (bf16[2,64,720]{2,1,0:T(8,128)(2,1)S(1)}, bf16[2,64,720]{2,1,0:T(8,128)(2,1)S(1)}) custom-call(bf16[48,720]{1,0:T(8,128)(2,1)S(1)} %shard_map.123.refs_0_, bf16[48,720]{1,0:T(8,128)(2,1)S(1)} %collective-permute-done.6.refs_1_, bf16[48,720]{1,0:T(8,128)(2,1)S(1)} %collective-permute-done.7.refs_2_, ...), custom_call_target="tpu_custom_call" | custom-call | flops 398131200 | bytes 6220800 | tf_op jit(solution)/shard_map/pallas_call | solution.py:351
  37.6 0.2 collective-permute-start.13
  37.8 1.3 %collective-permute-done.13.given_ref = bf16[2,64,720]{2,1,0:T(8,128)(2,1)S(1)} collective-permute-done((bf16[2,64,720]{2,1,0:T(8,128)(2,1)S(1)}, bf16[2,64,720]{2,1,0:T(8,128)(2,1)S(1)}, u32[]{:S(2)}, u32[]{:S(2)}) %collective-permute-start.13) | collective-permute-done | bytes 184352 | tf_op jit(solution)/shard_map/ppermute | solution.py:258
  39.1 0.1 shard_map.125
  39.2 0.6 %collective-permute-start.14 = (bf16[32,720]{1,0:T(8,128)(2,1)S(1)}, bf16[32,720]{1,0:T(8,128)(2,1)S(1)}, u32[]{:S(2)}, u32[]{:S(2)}) collective-permute-start(bf16[32,720]{1,0:T(8,128)(2,1)S(1)} %get-tuple-element.47), channel_id=1, source_target_pairs={{0,2},{1,3},{2,0},{3,1},{4,6},{5,7},{6,4},{7,5},{8,10},{9,11},{10,... | collective-permute-start | bytes 138248 | tf_op jit(solution)/shard_map/ppermute | solution.py:258
  39.8 1.5 %collective-permute-start.17 = (bf16[32,720]{1,0:T(8,128)(2,1)S(1)}, bf16[32,720]{1,0:T(8,128)(2,1)S(1)}, u32[]{:S(2)}, u32[]{:S(2)}) collective-permute-start(bf16[32,720]{1,0:T(8,128)(2,1)S(1)} %get-tuple-element.51), channel_id=1, source_target_pairs={{0,2},{1,3},{2,0},{3,1},{4,6},{5,7},{6,4},{7,5},{8,10},{9,11},{10,... | collective-permute-start | bytes 138248 | tf_op jit(solution)/shard_map/ppermute | solution.py:258
  41.3 2.3 %collective-permute-done.14.refs_1_ = bf16[32,720]{1,0:T(8,128)(2,1)S(1)} collective-permute-done((bf16[32,720]{1,0:T(8,128)(2,1)S(1)}, bf16[32,720]{1,0:T(8,128)(2,1)S(1)}, u32[]{:S(2)}, u32[]{:S(2)}) %collective-permute-start.14) | collective-permute-done | bytes 46112 | tf_op jit(solution)/shard_map/ppermute | solution.py:258
  43.6 1.0 %collective-permute-start.15 = (bf16[16,720]{1,0:T(8,128)(2,1)S(1)}, bf16[16,720]{1,0:T(8,128)(2,1)S(1)}, u32[]{:S(2)}, u32[]{:S(2)}) collective-permute-start(bf16[16,720]{1,0:T(8,128)(2,1)S(1)} %get-tuple-element.48), channel_id=1, source_target_pairs={{0,12},{4,8},{8,4},{12,0},{1,13},{5,9},{9,5},{13,1},{2,14},{6,10},... | collective-permute-start | bytes 69128 | tf_op jit(solution)/shard_map/ppermute | solution.py:258
  44.6 0.6 %collective-permute-start.16 = (bf16[16,720]{1,0:T(8,128)(2,1)S(1)}, bf16[16,720]{1,0:T(8,128)(2,1)S(1)}, u32[]{:S(2)}, u32[]{:S(2)}) collective-permute-start(bf16[16,720]{1,0:T(8,128)(2,1)S(1)} %get-tuple-element.49), channel_id=1, source_target_pairs={{0,8},{4,12},{8,0},{12,4},{1,9},{5,13},{9,1},{13,5},{2,10},{6,14},... | collective-permute-start | bytes 69128 | tf_op jit(solution)/shard_map/ppermute | solution.py:258
  45.1 3.0 %collective-permute-start.18 = (bf16[16,720]{1,0:T(8,128)(2,1)S(1)}, bf16[16,720]{1,0:T(8,128)(2,1)S(1)}, u32[]{:S(2)}, u32[]{:S(2)}) collective-permute-start(bf16[16,720]{1,0:T(8,128)(2,1)S(1)} %get-tuple-element.52), channel_id=1, source_target_pairs={{0,4},{4,0},{8,12},{12,8},{1,5},{5,1},{9,13},{13,9},{2,6},{6,2},{1... | collective-permute-start | bytes 69128 | tf_op jit(solution)/shard_map/ppermute | solution.py:258
  48.1 0.9 %shard_map.128.refs_6_ = bf16[720,256]{1,0:T(8,128)(2,1)S(1)} custom-call(bf16[512,256]{1,0:T(8,128)(2,1)S(1)} %get-tuple-element.56.refs_0_, bf16[512,256]{1,0:T(8,128)(2,1)S(1)} %collective-permute-done.19.refs_1_, bf16[512,256]{1,0:T(8,128)(2,1)S(1)} %collective-permute-done.20.refs_2_, bf16[512,256]{1,0:T(8,128)(2,1)S(1)} %collective-permute-done.21.refs_3_, ...), custom_call_target="tpu_custom_call" | custom-call | flops 754974720 | bytes 2949120 | tf_op jit(solution)/shard_map/pallas_call | solution.py:343
  49.1 0.2 collective-permute-done.15.refs_0_
  49.3 0.5 collective-permute-done.16.refs_1_
  49.8 0.3 collective-permute-done.18.refs_2_
  50.1 1.1 %shard_map.129 = bf16[720,256]{1,0:T(8,128)(2,1)} custom-call(bf16[16,720]{1,0:T(8,128)(2,1)S(1)} %collective-permute-done.15.refs_0_, bf16[16,720]{1,0:T(8,128)(2,1)S(1)} %collective-permute-done.16.refs_1_, bf16[16,720]{1,0:T(8,128)(2,1)S(1)} %collective-permute-done.18.refs_2_, bf16[16,720]{1,0:T(8,128)(2,1)S(1)} %get-tuple-element.53.refs_3_, ...), custom_call_target="tpu_custom_call" | custom-call | tf_op jit(solution)/shard_map/pallas_call | solution.py:374
  (18 shorter events, 0.1 us)
Async XLA Ops:
  0.0 8.3 %collective-permute-start = (bf16[256,256]{1,0:T(8,128)(2,1)}, bf16[256,256]{1,0:T(8,128)(2,1)S(1)}, u32[]{:S(2)}, u32[]{:S(2)}) collective-permute-start(bf16[256,256]{1,0:T(8,128)(2,1)} %refs_1_.1), channel_id=1, source_target_pairs={{0,4},{4,8},{8,12},{1,5},{5,9},{9,13},{2,6},{6,10},{10,14},{3,7},{... | collective-permute-start | bytes 393224 | tf_op jit(solution)/shard_map/ppermute | solution.py:291
  4.9 0.7 %copy-start.4 = (f32[8]{0:T(128)S(1)}, f32[8]{0:T(128)}, u32[]{:S(2)}) copy-start(f32[8]{0:T(128)} %sinks_ref.1) | copy-start | bytes 100
  9.5 5.0 %collective-permute-start.1 = (bf16[64,512]{1,0:T(8,128)(2,1)S(1)}, bf16[64,512]{1,0:T(8,128)(2,1)S(1)}, u32[]{:S(2)}, u32[]{:S(2)}) collective-permute-start(bf16[64,512]{1,0:T(8,128)(2,1)S(1)} %get-tuple-element.37.mine_ref), channel_id=1, source_target_pairs={{0,2},{1,3},{2,0},{3,1},{4,6},{5,7},{6,4},{7,5},{8,10},{9,11},{10,... | collective-permute-start | bytes 196616 | tf_op jit(solution)/shard_map/ppermute | solution.py:258
  11.0 23.8 %collective-permute-start.19 = (bf16[512,256]{1,0:T(8,128)(2,1)S(1)}, bf16[512,256]{1,0:T(8,128)(2,1)S(1)}, u32[]{:S(2)}, u32[]{:S(2)}) collective-permute-start(bf16[512,256]{1,0:T(8,128)(2,1)S(1)} %get-tuple-element.56.refs_0_), channel_id=1, source_target_pairs={{0,2},{1,3},{2,0},{3,1},{4,6},{5,7},{6,4},{7,5},{8,10},{9,11},{10,... | collective-permute-start | bytes 786440 | tf_op jit(solution)/shard_map/ppermute | solution.py:258
  11.6 2.9 %collective-permute-start.3 = (bf16[64,512]{1,0:T(8,128)(2,1)S(1)}, bf16[64,512]{1,0:T(8,128)(2,1)S(1)}, u32[]{:S(2)}, u32[]{:S(2)}) collective-permute-start(bf16[64,512]{1,0:T(8,128)(2,1)S(1)} %get-tuple-element.37.mine_ref), channel_id=1, source_target_pairs={{0,1},{1,0},{2,3},{3,2},{4,5},{5,4},{6,7},{7,6},{8,9},{9,8},{10,11... | collective-permute-start | bytes 196616 | tf_op jit(solution)/shard_map/ppermute | solution.py:258
  14.5 1.3 %collective-permute-start.2 = (bf16[64,512]{1,0:T(8,128)(2,1)S(1)}, bf16[64,512]{1,0:T(8,128)(2,1)S(1)}, u32[]{:S(2)}, u32[]{:S(2)}) collective-permute-start(bf16[64,512]{1,0:T(8,128)(2,1)S(1)} %collective-permute-done.1.refs_0_), channel_id=1, source_target_pairs={{0,1},{1,0},{2,3},{3,2},{4,5},{5,4},{6,7},{7,6},{8,9},{9,8},{10,11... | collective-permute-start | bytes 196616 | tf_op jit(solution)/shard_map/ppermute | solution.py:258
  15.2 20.3 %copy-start.1 = (bf16[1,2880,360]{1,2,0:T(8,128)(2,1)S(1)}, bf16[1,2880,360]{1,2,0:T(8,128)(2,1)}, u32[]{:S(2)}) copy-start(bf16[1,2880,360]{1,2,0:T(8,128)(2,1)} %param.22) | copy-start | bytes 6220804
  15.2 20.3 %copy-start.2 = (bf16[1,360,2880]{2,1,0:T(8,128)(2,1)S(1)}, bf16[1,360,2880]{2,1,0:T(8,128)(2,1)}, u32[]{:S(2)}) copy-start(bf16[1,360,2880]{2,1,0:T(8,128)(2,1)} %param.23) | copy-start | bytes 6220804
  15.5 20.0 %copy-start = (bf16[1,2880,360]{1,2,0:T(8,128)(2,1)S(1)}, bf16[1,2880,360]{1,2,0:T(8,128)(2,1)}, u32[]{:S(2)}) copy-start(bf16[1,2880,360]{1,2,0:T(8,128)(2,1)} %param.21) | copy-start | bytes 6220804
  15.6 20.0 %copy-start.3 = (f32[2880]{0:T(1024)S(1)}, f32[2880]{0:T(1024)}, u32[]{:S(2)}) copy-start(f32[2880]{0:T(1024)} %refs_8_.1) | copy-start | bytes 34564
  16.1 5.9 %collective-permute-start.4 = (bf16[16,720]{1,0:T(8,128)(2,1)S(1)}, bf16[16,720]{1,0:T(8,128)(2,1)S(1)}, u32[]{:S(2)}, u32[]{:S(2)}) collective-permute-start(bf16[16,720]{1,0:T(8,128)(2,1)S(1)} %get-tuple-element.40), channel_id=1, source_target_pairs={{0,12},{4,8},{8,4},{12,0},{1,13},{5,9},{9,5},{13,1},{2,14},{6,10},... | collective-permute-start | bytes 69128 | tf_op jit(solution)/shard_map/ppermute | solution.py:258
  20.3 4.7 %collective-permute-start.5 = (bf16[16,720]{1,0:T(8,128)(2,1)S(1)}, bf16[16,720]{1,0:T(8,128)(2,1)S(1)}, u32[]{:S(2)}, u32[]{:S(2)}) collective-permute-start(bf16[16,720]{1,0:T(8,128)(2,1)S(1)} %get-tuple-element.41), channel_id=1, source_target_pairs={{0,8},{4,12},{8,0},{12,4},{1,9},{5,13},{9,1},{13,5},{2,10},{6,14},... | collective-permute-start | bytes 69128 | tf_op jit(solution)/shard_map/ppermute | solution.py:258
  25.0 4.4 %collective-permute-start.6 = (bf16[48,720]{1,0:T(8,128)(2,1)S(1)}, bf16[48,720]{1,0:T(8,128)(2,1)S(1)}, u32[]{:S(2)}, u32[]{:S(2)}) collective-permute-start(bf16[48,720]{1,0:T(8,128)(2,1)S(1)} %shard_map.123.refs_0_), channel_id=1, source_target_pairs={{0,2},{1,3},{2,0},{3,1},{4,6},{5,7},{6,4},{7,5},{8,10},{9,11},{10,... | collective-permute-start | bytes 207368 | tf_op jit(solution)/shard_map/ppermute | solution.py:258
  26.6 3.8 %collective-permute-start.9 = (bf16[16,720]{1,0:T(8,128)(2,1)S(1)}, bf16[16,720]{1,0:T(8,128)(2,1)S(1)}, u32[]{:S(2)}, u32[]{:S(2)}) collective-permute-start(bf16[16,720]{1,0:T(8,128)(2,1)S(1)} %get-tuple-element.43), channel_id=1, source_target_pairs={{0,4},{4,0},{8,12},{12,8},{1,5},{5,1},{9,13},{13,9},{2,6},{6,2},{1... | collective-permute-start | bytes 69128 | tf_op jit(solution)/shard_map/ppermute | solution.py:258
  26.6 8.9 %collective-permute-start.7 = (bf16[48,720]{1,0:T(8,128)(2,1)S(1)}, bf16[48,720]{1,0:T(8,128)(2,1)S(1)}, u32[]{:S(2)}, u32[]{:S(2)}) collective-permute-start(bf16[48,720]{1,0:T(8,128)(2,1)S(1)} %shard_map.123.refs_0_), channel_id=1, source_target_pairs={{0,1},{1,0},{2,3},{3,2},{4,5},{5,4},{6,7},{7,6},{8,9},{9,8},{10,11... | collective-permute-start | bytes 207368 | tf_op jit(solution)/shard_map/ppermute | solution.py:258
  29.4 6.1 %collective-permute-start.8 = (bf16[48,720]{1,0:T(8,128)(2,1)S(1)}, bf16[48,720]{1,0:T(8,128)(2,1)S(1)}, u32[]{:S(2)}, u32[]{:S(2)}) collective-permute-start(bf16[48,720]{1,0:T(8,128)(2,1)S(1)} %collective-permute-done.6.refs_1_), channel_id=1, source_target_pairs={{0,1},{1,0},{2,3},{3,2},{4,5},{5,4},{6,7},{7,6},{8,9},{9,8},{10,11... | collective-permute-start | bytes 207368 | tf_op jit(solution)/shard_map/ppermute | solution.py:258
  30.5 3.8 %collective-permute-start.10 = (bf16[16,720]{1,0:T(8,128)(2,1)S(1)}, bf16[16,720]{1,0:T(8,128)(2,1)S(1)}, u32[]{:S(2)}, u32[]{:S(2)}) collective-permute-start(bf16[16,720]{1,0:T(8,128)(2,1)S(1)} %collective-permute-done.9.refs_4_), channel_id=1, source_target_pairs={{0,2},{1,3},{2,0},{3,1},{4,6},{5,7},{6,4},{7,5},{8,10},{9,11},{10,... | collective-permute-start | bytes 69128 | tf_op jit(solution)/shard_map/ppermute | solution.py:258
  31.0 3.3 %collective-permute-start.11 = (bf16[16,720]{1,0:T(8,128)(2,1)S(1)}, bf16[16,720]{1,0:T(8,128)(2,1)S(1)}, u32[]{:S(2)}, u32[]{:S(2)}) collective-permute-start(bf16[16,720]{1,0:T(8,128)(2,1)S(1)} %collective-permute-done.9.refs_4_), channel_id=1, source_target_pairs={{0,1},{1,0},{2,3},{3,2},{4,5},{5,4},{6,7},{7,6},{8,9},{9,8},{10,11... | collective-permute-start | bytes 69128 | tf_op jit(solution)/shard_map/ppermute | solution.py:258
  34.3 1.2 %collective-permute-start.12 = (bf16[16,720]{1,0:T(8,128)(2,1)S(1)}, bf16[16,720]{1,0:T(8,128)(2,1)S(1)}, u32[]{:S(2)}, u32[]{:S(2)}) collective-permute-start(bf16[16,720]{1,0:T(8,128)(2,1)S(1)} %collective-permute-done.10.refs_5_), channel_id=1, source_target_pairs={{0,1},{1,0},{2,3},{3,2},{4,5},{5,4},{6,7},{7,6},{8,9},{9,8},{10,11... | collective-permute-start | bytes 69128 | tf_op jit(solution)/shard_map/ppermute | solution.py:258
  34.3 13.8 %collective-permute-start.20 = (bf16[512,256]{1,0:T(8,128)(2,1)S(1)}, bf16[512,256]{1,0:T(8,128)(2,1)S(1)}, u32[]{:S(2)}, u32[]{:S(2)}) collective-permute-start(bf16[512,256]{1,0:T(8,128)(2,1)S(1)} %get-tuple-element.56.refs_0_), channel_id=1, source_target_pairs={{0,1},{1,0},{2,3},{3,2},{4,5},{5,4},{6,7},{7,6},{8,9},{9,8},{10,11... | collective-permute-start | bytes 786440 | tf_op jit(solution)/shard_map/ppermute | solution.py:258
  34.8 13.3 %collective-permute-start.21 = (bf16[512,256]{1,0:T(8,128)(2,1)S(1)}, bf16[512,256]{1,0:T(8,128)(2,1)S(1)}, u32[]{:S(2)}, u32[]{:S(2)}) collective-permute-start(bf16[512,256]{1,0:T(8,128)(2,1)S(1)} %collective-permute-done.19.refs_1_), channel_id=1, source_target_pairs={{0,1},{1,0},{2,3},{3,2},{4,5},{5,4},{6,7},{7,6},{8,9},{9,8},{10,11... | collective-permute-start | bytes 786440 | tf_op jit(solution)/shard_map/ppermute | solution.py:258
  37.6 1.5 %collective-permute-start.13 = (bf16[2,64,720]{2,1,0:T(8,128)(2,1)S(1)}, bf16[2,64,720]{2,1,0:T(8,128)(2,1)S(1)}, u32[]{:S(2)}, u32[]{:S(2)}) collective-permute-start(bf16[2,64,720]{2,1,0:T(8,128)(2,1)S(1)} %get-tuple-element.45), channel_id=1, source_target_pairs={{0,1},{1,0},{2,3},{3,2},{4,5},{5,4},{6,7},{7,6},{8,9},{9,8},{10,11... | collective-permute-start | bytes 552968 | tf_op jit(solution)/shard_map/ppermute | solution.py:258
  39.2 4.4 %collective-permute-start.14 = (bf16[32,720]{1,0:T(8,128)(2,1)S(1)}, bf16[32,720]{1,0:T(8,128)(2,1)S(1)}, u32[]{:S(2)}, u32[]{:S(2)}) collective-permute-start(bf16[32,720]{1,0:T(8,128)(2,1)S(1)} %get-tuple-element.47), channel_id=1, source_target_pairs={{0,2},{1,3},{2,0},{3,1},{4,6},{5,7},{6,4},{7,5},{8,10},{9,11},{10,... | collective-permute-start | bytes 138248 | tf_op jit(solution)/shard_map/ppermute | solution.py:258
  39.8 5.4 %collective-permute-start.17 = (bf16[32,720]{1,0:T(8,128)(2,1)S(1)}, bf16[32,720]{1,0:T(8,128)(2,1)S(1)}, u32[]{:S(2)}, u32[]{:S(2)}) collective-permute-start(bf16[32,720]{1,0:T(8,128)(2,1)S(1)} %get-tuple-element.51), channel_id=1, source_target_pairs={{0,2},{1,3},{2,0},{3,1},{4,6},{5,7},{6,4},{7,5},{8,10},{9,11},{10,... | collective-permute-start | bytes 138248 | tf_op jit(solution)/shard_map/ppermute | solution.py:258
  43.6 5.7 %collective-permute-start.15 = (bf16[16,720]{1,0:T(8,128)(2,1)S(1)}, bf16[16,720]{1,0:T(8,128)(2,1)S(1)}, u32[]{:S(2)}, u32[]{:S(2)}) collective-permute-start(bf16[16,720]{1,0:T(8,128)(2,1)S(1)} %get-tuple-element.48), channel_id=1, source_target_pairs={{0,12},{4,8},{8,4},{12,0},{1,13},{5,9},{9,5},{13,1},{2,14},{6,10},... | collective-permute-start | bytes 69128 | tf_op jit(solution)/shard_map/ppermute | solution.py:258
  44.6 5.3 %collective-permute-start.16 = (bf16[16,720]{1,0:T(8,128)(2,1)S(1)}, bf16[16,720]{1,0:T(8,128)(2,1)S(1)}, u32[]{:S(2)}, u32[]{:S(2)}) collective-permute-start(bf16[16,720]{1,0:T(8,128)(2,1)S(1)} %get-tuple-element.49), channel_id=1, source_target_pairs={{0,8},{4,12},{8,0},{12,4},{1,9},{5,13},{9,1},{13,5},{2,10},{6,14},... | collective-permute-start | bytes 69128 | tf_op jit(solution)/shard_map/ppermute | solution.py:258
  45.1 4.9 %collective-permute-start.18 = (bf16[16,720]{1,0:T(8,128)(2,1)S(1)}, bf16[16,720]{1,0:T(8,128)(2,1)S(1)}, u32[]{:S(2)}, u32[]{:S(2)}) collective-permute-start(bf16[16,720]{1,0:T(8,128)(2,1)S(1)} %get-tuple-element.52), channel_id=1, source_target_pairs={{0,4},{4,0},{8,12},{12,8},{1,5},{5,1},{9,13},{13,9},{2,6},{6,2},{1... | collective-permute-start | bytes 69128 | tf_op jit(solution)/shard_map/ppermute | solution.py:258

commit v4 on v3

--- a/solution.py
+++ b/solution.py
@@ -110,39 +110,37 @@
         mix_lo_ref[rows] = (mix - hi.astype(jnp.float32)).astype(jnp.bfloat16)
 
 
-def first_kernel(live, sinks_ref, *refs):
-    loaded, (ids_ref, weights_ref) = refs[:5], refs[5:7]
-    held = refs[7:12]
-    placing_ref, mix_hi_ref, mix_lo_ref, sinks_out, late_ref, ids_vmem, weights_vmem, sems = refs[12:]
-    copies = [
-        pltpu.make_async_copy(source, target, sems.at[i])
-        for i, (source, target) in enumerate(
-            zip((*loaded[:2], ids_ref, weights_ref, *loaded[2:]), (*held[:2], ids_vmem, weights_vmem, *held[2:]))
-        )
-    ]
+def first_kernel(live, *refs):
+    loaded, held = refs[:8], refs[8:13]
+    placing_ref, mix_hi_ref, mix_lo_ref, sinks_out, late_ref, ids_ref, weights_ref, sinks_ref, sems = refs[13:]
+    targets = (ids_ref, weights_ref, sinks_ref, *held)
+    copies = [pltpu.make_async_copy(*pair, sems.at[i]) for i, pair in enumerate(zip(loaded, targets))]
     for copy in copies:
         copy.start()
     q_ref, kv_ref = held[:2]
+    for copy in copies[:2]:
+        copy.wait()
+    fill_tables(live, ids_ref[...], weights_ref[...], placing_ref, mix_hi_ref, mix_lo_ref)
+    for copy in copies[2:5]:
+        copy.wait()
     heads = sinks_ref.shape[0]
     sinks = [jnp.full((1, KEYS_SEEN), sinks_ref[h], jnp.float32) * math.log2(math.e) for h in range(heads)]
     sinks_out[...] = jnp.concatenate(sinks, axis=0)
-    for copy in copies[2:4]:
-        copy.wait()
-    fill_tables(live, ids_vmem[...], weights_vmem[...], placing_ref, mix_hi_ref, mix_lo_ref)
-    for copy in copies[:2]:
-        copy.wait()
     groups = kv_ref.shape[1] // PAIR
     for b in range(1, q_ref.shape[0] // KEYS_SEEN):
         span = slice((b - 1) * KEYS_SEEN, (b + 1) * KEYS_SEEN)
         rows_of = [kv_ref[span, g * PAIR : (g + 1) * PAIR] for g in range(groups)]
         attend_tokens(b, q_ref, rows_of, sinks, late_ref, slice((b - 1) * KEYS_SEEN, b * KEYS_SEEN))
-    for copy in copies[4:]:
+    for copy in copies[5:]:
         copy.wait()
 
 
-def second_kernel(q_ref, kv_ref, before_ref, rim_ref, sinks_ref, late_ref, placing_ref, all_ref, rows_ref):
+def second_kernel(
+    q_ref, kv_ref, before_ref, to_even_ref, to_odd_ref, sinks_ref, late_ref, placing_ref, all_ref, rows_ref
+):
     first = lax.axis_index("seq") == 0
-    rim = jnp.where(first, before_ref[...], rim_ref[rim_ref.shape[0] - KEYS_SEEN :])
+    odd = lax.rem(lax.axis_index("seq"), 2) == 1
+    rim = jnp.where(first, before_ref[...], jnp.where(odd, to_odd_ref[...], to_even_ref[...]))
     groups = kv_ref.shape[1] // PAIR
     rows_of = []
     for g in range(groups):
@@ -201,17 +199,12 @@
     resid_ref[...] = total.astype(jnp.bfloat16)
 
 
-def expert_kernel(live, steps, *refs):
+def expert_kernel(steps, *refs):
     cuts = CORES * steps
-    most, rest = refs[:cuts], refs[cuts : 2 * cuts]
-    gain_ref, gate_ref, up_ref, down_ref, kept_ref, given_ref, blocks_ref, rows_ref = refs[2 * cuts :]
-    width = most[0].shape[1]
-    far = (live - 2) * CAP
+    gain_ref, gate_ref, up_ref, down_ref, kept_ref, given_ref, blocks_ref, rows_ref = refs[cuts:]
+    width = refs[0].shape[1]
     for i in range(cuts):
-        p = origin(i % steps, i >= steps)
-        blocks_ref[p, :far] = most[i][:far]
-        blocks_ref[p, far : far + CAP] = rest[i][...]
-        blocks_ref[p, far + CAP :] = most[i][far:]
+        blocks_ref[origin(i % steps, i >= steps)] = refs[i][...]
     wide = [blocks_ref[p].astype(jnp.float32) for p in range(cuts)]
     squares = sum(jnp.sum(b * b, axis=1, keepdims=True) for b in wide)
     scale = lax.rsqrt(squares / (cuts * width) + norm_eps)
@@ -288,7 +281,8 @@
     heads = head_rows // HEAD_SIZE
     width = norm_gain.shape[0]
 
-    rim = lax.ppermute(keyvals, "seq", [(i, i + 1) for i in range(size - 1)])
+    tail = keyvals[toks - KEYS_SEEN :]
+    rims = [lax.ppermute(tail, "seq", [(i, i + 1) for i in range(odd, size - 1, 2)]) for odd in (1, 0)]
     loads = (queries, keyvals, preceding_keyvalues, w_out.T, residual.T)
     q, kv, before, w_t, residual_t, placing, mix_hi, mix_lo, sinks, late = call(
         functools.partial(first_kernel, live),
@@ -302,20 +296,20 @@
         scratch=[
             pltpu.VMEM(expert_ids.T.shape, jnp.int32),
             pltpu.VMEM(expert_ids.T.shape, jnp.float32),
-            pltpu.SemaphoreType.DMA((7,)),
+            pltpu.SMEM(attention_sink_logits.shape, jnp.float32),
+            pltpu.SemaphoreType.DMA((8,)),
         ],
-        smem=(0,),
-        hbm=range(1, 8),
+        hbm=range(8),
         flops=4 * toks * SPAN * head_rows,
         moved=2 * (w_out.size + residual.size + queries.size),
-    )(attention_sink_logits, *(in_hbm(a) for a in (*loads, expert_ids.T, route_weights.T)))
+    )(*(in_hbm(a) for a in (expert_ids.T, route_weights.T, attention_sink_logits, *loads)))
     attended, rows = call(
         second_kernel,
         (bf16(head_rows, toks), bf16(slots, head_rows)),
-        n_in=7,
+        n_in=8,
         flops=2 * toks * SPAN * head_rows,
         moved=2 * queries.size,
-    )(q, kv, before, rim, sinks, late, placing)
+    )(q, kv, before, *rims, sinks, late, placing)
 
     mine, theirs = gather_cuts(rows)
     total = jax.ShapeDtypeStruct((slots, feats), jnp.float32)
@@ -335,10 +329,10 @@
     )(*theirs[1:], chips, w_t)
 
     arrived = [swap(outgoing[k], "seq", k) for k in range(live - 1, 0, -1)] + [outgoing[0]]
-    most = call(stack_kernel, bf16(slots - CAP, feats), n_in=live - 1)(*arrived[:-2], arrived[-1])
-    most_mine, most_theirs = gather_cuts(most)
-    rest_mine, rest_theirs = gather_cuts(arrived[-2])
-
+    stacked = call(stack_kernel, bf16(slots, feats), n_in=live)(*arrived)
+    expert_mine, expert_theirs = gather_cuts(stacked)
+
+    attended, _ = lax.optimization_barrier((attended, chips))
     mine, theirs = gather_cuts(attended)
     resid = call(
         functools.partial(project_kernel, steps),
@@ -349,16 +343,16 @@
     )(*mine, *theirs, w_t, residual_t)
 
     kept, given = call(
-        functools.partial(expert_kernel, live, steps),
+        functools.partial(expert_kernel, steps),
         (bf16(steps, slots, feats),) * 2,
-        n_in=2 * cuts + 4,
+        n_in=cuts + 4,
         scratch=[
             pltpu.VMEM((cuts, slots, feats), jnp.bfloat16),
             pltpu.VMEM((slots, width), jnp.bfloat16),
         ],
         flops=6 * slots * w_gate.size,
         moved=6 * w_gate.size,
-    )(*most_mine, *most_theirs, *rest_mine, *rest_theirs, norm_gain, w_gate[0].T, w_up[0].T, w_down[0])
+    )(*expert_mine, *expert_theirs, norm_gain, w_gate[0].T, w_up[0].T, w_down[0])
     sums = call(add_cores_kernel, (bf16(slots // 2, feats),) * (2 * steps), n_in=2)(
         kept, swap(given, "cuts", 1)
     )

time: 51.4 us -> 50 us (0.973)
  waiting for transfers between devices: 19.9 us -> 16.7 us
  starting transfers between devices: 21 us -> 23.2 us
  Pallas kernels: 9.45 us -> 8.92 us
    ppermute x21 -> x18, waiting for transfers between devices: 19.9 us -> 16.7 us  [swap(): lax.ppermute(block, axis, [(i, i ^ mask) for i in range(lax.axis_size(axi...]
    ppermute x21 -> x18, starting transfers between devices: 16.1 us -> 17.6 us  [swap(): lax.ppermute(block, axis, [(i, i ^ mask) for i in range(lax.axis_size(axi...]
    slice x0 -> x1, local copies, waits for them, and re-layouts: none -> 0.84 us  [shards(): tail = keyvals[toks - KEYS_SEEN:]]
    ppermute x1 -> x2, starting transfers between devices: 4.92 us -> 5.58 us  [shards(): lax.ppermute(tail, 'seq', [(i, i + 1) for i in range(odd, size - 1, 2)])]
    unnamed x10 -> x8, local copies, waits for them, and re-layouts: 0.67 us -> 0.02 us
    pallas_call x1, Pallas kernels: 2.68 us -> 2.16 us  [shards(): call(functools.partial(first_kernel, live), (*(bf16(*a.shape) for a in lo...]
  transfers between devices with their start and end apart: 22 -> 20, of which waited for: 13 -> 9; matrix products, arithmetic and copies ran while one was open for 0% -> 0% of each run, Pallas kernels for 14% -> 13%
where the time goes in v4:
time: 50 us; the launch traced here: 49.8 us
  starting transfers between devices  23.2 us (46%)
  waiting for transfers between devices  16.7 us (33%)
  Pallas kernels  8.92 us (18%)
  local copies, waits for them, and re-layouts  0.87 us (2%)
    ppermute x18, starting transfers between devices, swap(): lax.ppermute(block, axis, [(i, i ^ mask) for i in range(lax.axis_size(axi...  17.6 us
    ppermute x18, waiting for transfers between devices, swap(): lax.ppermute(block, axis, [(i, i ^ mask) for i in range(lax.axis_size(axi...  16.7 us
    ppermute x2, starting transfers between devices, shards(): lax.ppermute(tail, 'seq', [(i, i + 1) for i in range(odd, size - 1, 2)])  5.58 us
    pallas_call x1, Pallas kernels, shards(): call(functools.partial(first_kernel, live), (*(bf16(*a.shape) for a in lo...  2.16 us
    pallas_call x1, Pallas kernels, shards(): call(functools.partial(expert_kernel, steps), (bf16(steps, slots, feats),...  2.06 us
    pallas_call x1, Pallas kernels, shards(): call(second_kernel, (bf16(head_rows, toks), bf16(slots, head_rows)), n_in...  1.18 us
    pallas_call x1, Pallas kernels, shards(): call(functools.partial(combine_kernel, live), bf16(feats, toks), n_in=liv...  1.13 us
  transfers between devices with their start and end apart: 20, of which 9 were waited for; matrix products, arithmetic and copies ran while one was open for 0% of the time, Pallas kernels for 13%

profile of v4, /device:TPU:0, one launch (start us, length us, event | category | flops | bytes accessed | tf_op | source)
XLA Modules:
  0.0 49.8 jit_solution(9938339712796478615)
XLA Ops:
  0.0 0.8 %slice.3 = bf16[128,256]{1,0:T(8,128)(2,1)S(1)} slice(bf16[256,256]{1,0:T(8,128)(2,1)} %refs_4_.2), slice={[128:256], [0:256]} | slice | bytes 131072 | tf_op jit(solution)/shard_map/slice | solution.py:284
  0.8 4.9 %collective-permute-start.1 = (bf16[128,256]{1,0:T(8,128)(2,1)S(1)}, bf16[128,256]{1,0:T(8,128)(2,1)S(1)}, u32[]{:S(2)}, u32[]{:S(2)}) collective-permute-start(bf16[128,256]{1,0:T(8,128)(2,1)S(1)} %slice.3), channel_id=1, source_target_pairs={{0,4},{8,12},{1,5},{9,13},{2,6},{10,14},{3,7},{11,15},{16,20},{24,... | collective-permute-start | bytes 196616 | tf_op jit(solution)/shard_map/ppermute | solution.py:285
  5.8 0.7 %collective-permute-start = (bf16[128,256]{1,0:T(8,128)(2,1)S(1)}, bf16[128,256]{1,0:T(8,128)(2,1)S(1)}, u32[]{:S(2)}, u32[]{:S(2)}) collective-permute-start(bf16[128,256]{1,0:T(8,128)(2,1)S(1)} %slice.3), channel_id=1, source_target_pairs={{4,8},{5,9},{6,10},{7,11},{20,24},{21,25},{22,26},{23,27}} | collective-permute-start | bytes 196616 | tf_op jit(solution)/shard_map/ppermute | solution.py:285
  6.4 2.2 %shard_map.118 = (bf16[256,512]{1,0:T(8,128)(2,1)S(1)}, bf16[256,256]{1,0:T(8,128)(2,1)S(1)}, bf16[128,256]{1,0:T(8,128)(2,1)S(1)}, bf16[720,2048]{1,0:T(8,128)(...) custom-call(s32[4,256]{1,0:T(4,128)} %bitcast.17, ...), custom_call_target="tpu_custom_call" | custom-call | flops 134217728 | bytes 3579904 | tf_op jit(solution)/shard_map/pallas_call | solution.py:287
  8.6 0.0 collective-permute-done.1.to_odd_ref
  8.6 0.0 collective-permute-done.to_even_ref
  8.6 1.2 %shard_map.119 = (bf16[512,256]{1,0:T(8,128)(2,1)S(1)}, bf16[64,512]{1,0:T(8,128)(2,1)S(1)}) custom-call(bf16[256,512]{1,0:T(8,128)(2,1)S(1)} %get-tuple-element.32.q_ref, bf16[256,256]{1,0:T(8,128)(2,1)S(1)} %get-tuple-element.33.kv_ref, bf16[128,256]{1,0:T(8,128)(2,1)S(1)} %get-tuple-element.34.before_ref, ...), custom_call_target="tpu_custom_call" | custom-call | flops 67108864 | bytes 262144 | tf_op jit(solution)/shard_map/pallas_call | solution.py:306
  9.8 1.6 %collective-permute-start.2 = (bf16[64,512]{1,0:T(8,128)(2,1)S(1)}, bf16[64,512]{1,0:T(8,128)(2,1)S(1)}, u32[]{:S(2)}, u32[]{:S(2)}) collective-permute-start(bf16[64,512]{1,0:T(8,128)(2,1)S(1)} %get-tuple-element.38.mine_ref), channel_id=1, source_target_pairs={{0,2},{1,3},{2,0},{3,1},{4,6},{5,7},{6,4},{7,5},{8,10},{9,11},{10,... | collective-permute-start | bytes 196616 | tf_op jit(solution)/shard_map/ppermute | solution.py:251
  11.4 0.0 collective-permute-start.4
  11.4 2.8 %collective-permute-done.2.refs_0_ = bf16[64,512]{1,0:T(8,128)(2,1)S(1)} collective-permute-done((bf16[64,512]{1,0:T(8,128)(2,1)S(1)}, bf16[64,512]{1,0:T(8,128)(2,1)S(1)}, u32[]{:S(2)}, u32[]{:S(2)}) %collective-permute-start.2) | collective-permute-done | bytes 65568 | tf_op jit(solution)/shard_map/ppermute | solution.py:251
  14.2 0.0 collective-permute-start.3
  14.2 0.0 collective-permute-done.4.theirs_ref
  14.2 0.6 %shard_map.120.refs_1_ = f32[64,720]{1,0:T(8,128)S(1)} custom-call(bf16[64,512]{1,0:T(8,128)(2,1)S(1)} %get-tuple-element.38.mine_ref, bf16[64,512]{1,0:T(8,128)(2,1)S(1)} %collective-permute-done.4.theirs_ref, bf16[720,2048]{1,0:T(8,128)(2,1)S(1)} %get-tuple-element.39.w_ref.refs_2_.refs_4_, bf16[720,256]{1,0:T(8,128)(2,1)S(1)} %get-tuple-element.40.residual_ref.refs_5_, ...), custom_call_target="tpu_custom_call" | custom-call | flops 47185920 | bytes 737280 | tf_op jit(solution)/shard_map/pallas_call | solution.py:317
  14.8 0.0 copy-start.2
  14.8 0.4 shard_map.121.refs_1_
  15.2 0.0 copy-start
  15.2 0.0 copy-start.3
  15.2 1.6 %collective-permute-start.17 = (bf16[512,256]{1,0:T(8,128)(2,1)S(1)}, bf16[512,256]{1,0:T(8,128)(2,1)S(1)}, u32[]{:S(2)}, u32[]{:S(2)}) collective-permute-start(bf16[512,256]{1,0:T(8,128)(2,1)S(1)} %get-tuple-element.58.refs_0_), channel_id=1, source_target_pairs={{0,2},{1,3},{2,0},{3,1},{4,6},{5,7},{6,4},{7,5},{8,10},{9,11},{10,... | collective-permute-start | bytes 786440 | tf_op jit(solution)/shard_map/ppermute | solution.py:251
  16.8 0.0 collective-permute-done.3.refs_0_
  16.8 0.4 shard_map.122
  17.1 3.5 %collective-permute-start.5 = (bf16[16,720]{1,0:T(8,128)(2,1)S(1)}, bf16[16,720]{1,0:T(8,128)(2,1)S(1)}, u32[]{:S(2)}, u32[]{:S(2)}) collective-permute-start(bf16[16,720]{1,0:T(8,128)(2,1)S(1)} %get-tuple-element.41), channel_id=1, source_target_pairs={{0,12},{4,8},{8,4},{12,0},{1,13},{5,9},{9,5},{13,1},{2,14},{6,10},... | collective-permute-start | bytes 69128 | tf_op jit(solution)/shard_map/ppermute | solution.py:251
  20.6 2.5 %collective-permute-start.6 = (bf16[16,720]{1,0:T(8,128)(2,1)S(1)}, bf16[16,720]{1,0:T(8,128)(2,1)S(1)}, u32[]{:S(2)}, u32[]{:S(2)}) collective-permute-start(bf16[16,720]{1,0:T(8,128)(2,1)S(1)} %get-tuple-element.42), channel_id=1, source_target_pairs={{0,8},{4,12},{8,0},{12,4},{1,9},{5,13},{9,1},{13,5},{2,10},{6,14},... | collective-permute-start | bytes 69128 | tf_op jit(solution)/shard_map/ppermute | solution.py:251
  23.2 0.5 collective-permute-start.7
  23.6 1.7 %collective-permute-done.6.refs_1_ = bf16[16,720]{1,0:T(8,128)(2,1)S(1)} collective-permute-done((bf16[16,720]{1,0:T(8,128)(2,1)S(1)}, bf16[16,720]{1,0:T(8,128)(2,1)S(1)}, u32[]{:S(2)}, u32[]{:S(2)}) %collective-permute-start.6) | collective-permute-done | bytes 23072 | tf_op jit(solution)/shard_map/ppermute | solution.py:251
  25.3 1.6 %collective-permute-done.7.refs_2_ = bf16[16,720]{1,0:T(8,128)(2,1)S(1)} collective-permute-done((bf16[16,720]{1,0:T(8,128)(2,1)S(1)}, bf16[16,720]{1,0:T(8,128)(2,1)S(1)}, u32[]{:S(2)}, u32[]{:S(2)}) %collective-permute-start.7) | collective-permute-done | bytes 23072 | tf_op jit(solution)/shard_map/ppermute | solution.py:251
  27.0 0.6 %collective-permute-start.8 = (bf16[64,720]{1,0:T(8,128)(2,1)S(1)}, bf16[64,720]{1,0:T(8,128)(2,1)S(1)}, u32[]{:S(2)}, u32[]{:S(2)}) collective-permute-start(bf16[64,720]{1,0:T(8,128)(2,1)S(1)} %shard_map.123.refs_0_), channel_id=1, source_target_pairs={{0,2},{1,3},{2,0},{3,1},{4,6},{5,7},{6,4},{7,5},{8,10},{9,11},{10,... | collective-permute-start | bytes 276488 | tf_op jit(solution)/shard_map/ppermute | solution.py:251
  27.6 4.1 %collective-permute-done.8.refs_1_ = bf16[64,720]{1,0:T(8,128)(2,1)S(1)} collective-permute-done((bf16[64,720]{1,0:T(8,128)(2,1)S(1)}, bf16[64,720]{1,0:T(8,128)(2,1)S(1)}, u32[]{:S(2)}, u32[]{:S(2)}) %collective-permute-start.8) | collective-permute-done | bytes 92192 | tf_op jit(solution)/shard_map/ppermute | solution.py:251
  31.7 0.0 collective-permute-start.10
  31.7 0.5 %collective-permute-start.18 = (bf16[512,256]{1,0:T(8,128)(2,1)S(1)}, bf16[512,256]{1,0:T(8,128)(2,1)S(1)}, u32[]{:S(2)}, u32[]{:S(2)}) collective-permute-start(bf16[512,256]{1,0:T(8,128)(2,1)S(1)} %get-tuple-element.58.refs_0_), channel_id=1, source_target_pairs={{0,1},{1,0},{2,3},{3,2},{4,5},{5,4},{6,7},{7,6},{8,9},{9,8},{10,11... | collective-permute-start | bytes 786440 | tf_op jit(solution)/shard_map/ppermute | solution.py:251
  32.2 0.0 collective-permute-start.19
  32.2 0.0 collective-permute-done.9.refs_2_
  32.2 0.8 %collective-permute-done.10.refs_3_ = bf16[64,720]{1,0:T(8,128)(2,1)S(1)} collective-permute-done((bf16[64,720]{1,0:T(8,128)(2,1)S(1)}, bf16[64,720]{1,0:T(8,128)(2,1)S(1)}, u32[]{:S(2)}, u32[]{:S(2)}) %collective-permute-start.10) | collective-permute-done | bytes 92192 | tf_op jit(solution)/shard_map/ppermute | solution.py:251
  33.0 2.1 %shard_map.124 = (bf16[2,64,720]{2,1,0:T(8,128)(2,1)S(1)}, bf16[2,64,720]{2,1,0:T(8,128)(2,1)S(1)}) custom-call(bf16[64,720]{1,0:T(8,128)(2,1)S(1)} %shard_map.123.refs_0_, bf16[64,720]{1,0:T(8,128)(2,1)S(1)} %collective-permute-done.8.refs_1_, bf16[64,720]{1,0:T(8,128)(2,1)S(1)} %collective-permute-done.9.refs_2_, ...), custom_call_target="tpu_custom_call" | custom-call | flops 398131200 | bytes 6220800 | tf_op jit(solution)/shard_map/pallas_call | solution.py:345
  35.1 0.2 collective-permute-start.11
  35.3 1.3 %collective-permute-done.11.given_ref = bf16[2,64,720]{2,1,0:T(8,128)(2,1)S(1)} collective-permute-done((bf16[2,64,720]{2,1,0:T(8,128)(2,1)S(1)}, bf16[2,64,720]{2,1,0:T(8,128)(2,1)S(1)}, u32[]{:S(2)}, u32[]{:S(2)}) %collective-permute-start.11) | collective-permute-done | bytes 184352 | tf_op jit(solution)/shard_map/ppermute | solution.py:251
  36.6 0.1 shard_map.125
  36.6 0.6 %collective-permute-start.12 = (bf16[32,720]{1,0:T(8,128)(2,1)S(1)}, bf16[32,720]{1,0:T(8,128)(2,1)S(1)}, u32[]{:S(2)}, u32[]{:S(2)}) collective-permute-start(bf16[32,720]{1,0:T(8,128)(2,1)S(1)} %get-tuple-element.48), channel_id=1, source_target_pairs={{0,2},{1,3},{2,0},{3,1},{4,6},{5,7},{6,4},{7,5},{8,10},{9,11},{10,... | collective-permute-start | bytes 138248 | tf_op jit(solution)/shard_map/ppermute | solution.py:251
  37.2 1.5 %collective-permute-start.15 = (bf16[32,720]{1,0:T(8,128)(2,1)S(1)}, bf16[32,720]{1,0:T(8,128)(2,1)S(1)}, u32[]{:S(2)}, u32[]{:S(2)}) collective-permute-start(bf16[32,720]{1,0:T(8,128)(2,1)S(1)} %get-tuple-element.52), channel_id=1, source_target_pairs={{0,2},{1,3},{2,0},{3,1},{4,6},{5,7},{6,4},{7,5},{8,10},{9,11},{10,... | collective-permute-start | bytes 138248 | tf_op jit(solution)/shard_map/ppermute | solution.py:251
  38.7 2.3 %collective-permute-done.12.refs_1_ = bf16[32,720]{1,0:T(8,128)(2,1)S(1)} collective-permute-done((bf16[32,720]{1,0:T(8,128)(2,1)S(1)}, bf16[32,720]{1,0:T(8,128)(2,1)S(1)}, u32[]{:S(2)}, u32[]{:S(2)}) %collective-permute-start.12) | collective-permute-done | bytes 46112 | tf_op jit(solution)/shard_map/ppermute | solution.py:251
  41.0 2.9 %collective-permute-start.13 = (bf16[16,720]{1,0:T(8,128)(2,1)S(1)}, bf16[16,720]{1,0:T(8,128)(2,1)S(1)}, u32[]{:S(2)}, u32[]{:S(2)}) collective-permute-start(bf16[16,720]{1,0:T(8,128)(2,1)S(1)} %get-tuple-element.49), channel_id=1, source_target_pairs={{0,12},{4,8},{8,4},{12,0},{1,13},{5,9},{9,5},{13,1},{2,14},{6,10},... | collective-permute-start | bytes 69128 | tf_op jit(solution)/shard_map/ppermute | solution.py:251
  44.0 0.0 collective-permute-done.15.refs_1_
  44.0 1.6 %collective-permute-start.16 = (bf16[16,720]{1,0:T(8,128)(2,1)S(1)}, bf16[16,720]{1,0:T(8,128)(2,1)S(1)}, u32[]{:S(2)}, u32[]{:S(2)}) collective-permute-start(bf16[16,720]{1,0:T(8,128)(2,1)S(1)} %get-tuple-element.53), channel_id=1, source_target_pairs={{0,4},{4,0},{8,12},{12,8},{1,5},{5,1},{9,13},{13,9},{2,6},{6,2},{1... | collective-permute-start | bytes 69128 | tf_op jit(solution)/shard_map/ppermute | solution.py:251
  45.6 0.0 collective-permute-done.19.refs_3_
  45.6 0.9 %shard_map.128.refs_6_ = bf16[720,256]{1,0:T(8,128)(2,1)S(1)} custom-call(bf16[512,256]{1,0:T(8,128)(2,1)S(1)} %get-tuple-element.58.refs_0_, bf16[512,256]{1,0:T(8,128)(2,1)S(1)} %collective-permute-done.17.refs_1_, bf16[512,256]{1,0:T(8,128)(2,1)S(1)} %collective-permute-done.18.refs_2_, bf16[512,256]{1,0:T(8,128)(2,1)S(1)} %collective-permute-done.19.refs_3_, ...), custom_call_target="tpu_custom_call" | custom-call | flops 754974720 | bytes 2949120 | tf_op jit(solution)/shard_map/pallas_call | solution.py:337
  46.5 0.2 collective-permute-done.13.refs_0_
  46.7 1.9 %collective-permute-done.14.refs_1_ = bf16[16,720]{1,0:T(8,128)(2,1)S(1)} collective-permute-done((bf16[16,720]{1,0:T(8,128)(2,1)S(1)}, bf16[16,720]{1,0:T(8,128)(2,1)S(1)}, u32[]{:S(2)}, u32[]{:S(2)}) %collective-permute-start.14) | collective-permute-done | bytes 23072 | tf_op jit(solution)/shard_map/ppermute | solution.py:251
  48.7 0.0 collective-permute-done.16.refs_2_
  48.7 1.1 %shard_map.129 = bf16[720,256]{1,0:T(8,128)(2,1)} custom-call(bf16[16,720]{1,0:T(8,128)(2,1)S(1)} %collective-permute-done.13.refs_0_, bf16[16,720]{1,0:T(8,128)(2,1)S(1)} %collective-permute-done.14.refs_1_, bf16[16,720]{1,0:T(8,128)(2,1)S(1)} %collective-permute-done.16.refs_2_, bf16[16,720]{1,0:T(8,128)(2,1)S(1)} %get-tuple-element.54.refs_3_, ...), custom_call_target="tpu_custom_call" | custom-call | tf_op jit(solution)/shard_map/pallas_call | solution.py:368
  (13 shorter events, 0.1 us)
Async XLA Ops:
  0.8 7.8 %collective-permute-start.1 = (bf16[128,256]{1,0:T(8,128)(2,1)S(1)}, bf16[128,256]{1,0:T(8,128)(2,1)S(1)}, u32[]{:S(2)}, u32[]{:S(2)}) collective-permute-start(bf16[128,256]{1,0:T(8,128)(2,1)S(1)} %slice.3), channel_id=1, source_target_pairs={{0,4},{8,12},{1,5},{9,13},{2,6},{10,14},{3,7},{11,15},{16,20},{24,... | collective-permute-start | bytes 196616 | tf_op jit(solution)/shard_map/ppermute | solution.py:285
  5.8 2.9 %collective-permute-start = (bf16[128,256]{1,0:T(8,128)(2,1)S(1)}, bf16[128,256]{1,0:T(8,128)(2,1)S(1)}, u32[]{:S(2)}, u32[]{:S(2)}) collective-permute-start(bf16[128,256]{1,0:T(8,128)(2,1)S(1)} %slice.3), channel_id=1, source_target_pairs={{4,8},{5,9},{6,10},{7,11},{20,24},{21,25},{22,26},{23,27}} | collective-permute-start | bytes 196616 | tf_op jit(solution)/shard_map/ppermute | solution.py:285
  9.8 4.3 %collective-permute-start.2 = (bf16[64,512]{1,0:T(8,128)(2,1)S(1)}, bf16[64,512]{1,0:T(8,128)(2,1)S(1)}, u32[]{:S(2)}, u32[]{:S(2)}) collective-permute-start(bf16[64,512]{1,0:T(8,128)(2,1)S(1)} %get-tuple-element.38.mine_ref), channel_id=1, source_target_pairs={{0,2},{1,3},{2,0},{3,1},{4,6},{5,7},{6,4},{7,5},{8,10},{9,11},{10,... | collective-permute-start | bytes 196616 | tf_op jit(solution)/shard_map/ppermute | solution.py:251
  11.4 2.8 %collective-permute-start.4 = (bf16[64,512]{1,0:T(8,128)(2,1)S(1)}, bf16[64,512]{1,0:T(8,128)(2,1)S(1)}, u32[]{:S(2)}, u32[]{:S(2)}) collective-permute-start(bf16[64,512]{1,0:T(8,128)(2,1)S(1)} %get-tuple-element.38.mine_ref), channel_id=1, source_target_pairs={{0,1},{1,0},{2,3},{3,2},{4,5},{5,4},{6,7},{7,6},{8,9},{9,8},{10,11... | collective-permute-start | bytes 196616 | tf_op jit(solution)/shard_map/ppermute | solution.py:251
  14.2 2.6 %collective-permute-start.3 = (bf16[64,512]{1,0:T(8,128)(2,1)S(1)}, bf16[64,512]{1,0:T(8,128)(2,1)S(1)}, u32[]{:S(2)}, u32[]{:S(2)}) collective-permute-start(bf16[64,512]{1,0:T(8,128)(2,1)S(1)} %collective-permute-done.2.refs_0_), channel_id=1, source_target_pairs={{0,1},{1,0},{2,3},{3,2},{4,5},{5,4},{6,7},{7,6},{8,9},{9,8},{10,11... | collective-permute-start | bytes 196616 | tf_op jit(solution)/shard_map/ppermute | solution.py:251
  14.8 18.2 %copy-start.1 = (bf16[1,2880,360]{1,2,0:T(8,128)(2,1)S(1)}, bf16[1,2880,360]{1,2,0:T(8,128)(2,1)}, u32[]{:S(2)}) copy-start(bf16[1,2880,360]{1,2,0:T(8,128)(2,1)} %param.22) | copy-start | bytes 6220804
  14.8 18.2 %copy-start.2 = (bf16[1,360,2880]{2,1,0:T(8,128)(2,1)S(1)}, bf16[1,360,2880]{2,1,0:T(8,128)(2,1)}, u32[]{:S(2)}) copy-start(bf16[1,360,2880]{2,1,0:T(8,128)(2,1)} %param.23) | copy-start | bytes 6220804
  15.2 17.8 %copy-start = (bf16[1,2880,360]{1,2,0:T(8,128)(2,1)S(1)}, bf16[1,2880,360]{1,2,0:T(8,128)(2,1)}, u32[]{:S(2)}) copy-start(bf16[1,2880,360]{1,2,0:T(8,128)(2,1)} %param.21) | copy-start | bytes 6220804
  15.2 17.8 %copy-start.3 = (f32[2880]{0:T(1024)S(1)}, f32[2880]{0:T(1024)}, u32[]{:S(2)}) copy-start(f32[2880]{0:T(1024)} %refs_4_.3) | copy-start | bytes 34564
  15.2 17.0 %collective-permute-start.17 = (bf16[512,256]{1,0:T(8,128)(2,1)S(1)}, bf16[512,256]{1,0:T(8,128)(2,1)S(1)}, u32[]{:S(2)}, u32[]{:S(2)}) collective-permute-start(bf16[512,256]{1,0:T(8,128)(2,1)S(1)} %get-tuple-element.58.refs_0_), channel_id=1, source_target_pairs={{0,2},{1,3},{2,0},{3,1},{4,6},{5,7},{6,4},{7,5},{8,10},{9,11},{10,... | collective-permute-start | bytes 786440 | tf_op jit(solution)/shard_map/ppermute | solution.py:251
  17.1 6.5 %collective-permute-start.5 = (bf16[16,720]{1,0:T(8,128)(2,1)S(1)}, bf16[16,720]{1,0:T(8,128)(2,1)S(1)}, u32[]{:S(2)}, u32[]{:S(2)}) collective-permute-start(bf16[16,720]{1,0:T(8,128)(2,1)S(1)} %get-tuple-element.41), channel_id=1, source_target_pairs={{0,12},{4,8},{8,4},{12,0},{1,13},{5,9},{9,5},{13,1},{2,14},{6,10},... | collective-permute-start | bytes 69128 | tf_op jit(solution)/shard_map/ppermute | solution.py:251
  20.6 4.7 %collective-permute-start.6 = (bf16[16,720]{1,0:T(8,128)(2,1)S(1)}, bf16[16,720]{1,0:T(8,128)(2,1)S(1)}, u32[]{:S(2)}, u32[]{:S(2)}) collective-permute-start(bf16[16,720]{1,0:T(8,128)(2,1)S(1)} %get-tuple-element.42), channel_id=1, source_target_pairs={{0,8},{4,12},{8,0},{12,4},{1,9},{5,13},{9,1},{13,5},{2,10},{6,14},... | collective-permute-start | bytes 69128 | tf_op jit(solution)/shard_map/ppermute | solution.py:251
  23.2 3.8 %collective-permute-start.7 = (bf16[16,720]{1,0:T(8,128)(2,1)S(1)}, bf16[16,720]{1,0:T(8,128)(2,1)S(1)}, u32[]{:S(2)}, u32[]{:S(2)}) collective-permute-start(bf16[16,720]{1,0:T(8,128)(2,1)S(1)} %get-tuple-element.43), channel_id=1, source_target_pairs={{0,4},{4,0},{8,12},{12,8},{1,5},{5,1},{9,13},{13,9},{2,6},{6,2},{1... | collective-permute-start | bytes 69128 | tf_op jit(solution)/shard_map/ppermute | solution.py:251
  27.0 4.7 %collective-permute-start.8 = (bf16[64,720]{1,0:T(8,128)(2,1)S(1)}, bf16[64,720]{1,0:T(8,128)(2,1)S(1)}, u32[]{:S(2)}, u32[]{:S(2)}) collective-permute-start(bf16[64,720]{1,0:T(8,128)(2,1)S(1)} %shard_map.123.refs_0_), channel_id=1, source_target_pairs={{0,2},{1,3},{2,0},{3,1},{4,6},{5,7},{6,4},{7,5},{8,10},{9,11},{10,... | collective-permute-start | bytes 276488 | tf_op jit(solution)/shard_map/ppermute | solution.py:251
  27.6 4.6 %collective-permute-start.9 = (bf16[64,720]{1,0:T(8,128)(2,1)S(1)}, bf16[64,720]{1,0:T(8,128)(2,1)S(1)}, u32[]{:S(2)}, u32[]{:S(2)}) collective-permute-start(bf16[64,720]{1,0:T(8,128)(2,1)S(1)} %shard_map.123.refs_0_), channel_id=1, source_target_pairs={{0,1},{1,0},{2,3},{3,2},{4,5},{5,4},{6,7},{7,6},{8,9},{9,8},{10,11... | collective-permute-start | bytes 276488 | tf_op jit(solution)/shard_map/ppermute | solution.py:251
  31.7 1.3 %collective-permute-start.10 = (bf16[64,720]{1,0:T(8,128)(2,1)S(1)}, bf16[64,720]{1,0:T(8,128)(2,1)S(1)}, u32[]{:S(2)}, u32[]{:S(2)}) collective-permute-start(bf16[64,720]{1,0:T(8,128)(2,1)S(1)} %collective-permute-done.8.refs_1_), channel_id=1, source_target_pairs={{0,1},{1,0},{2,3},{3,2},{4,5},{5,4},{6,7},{7,6},{8,9},{9,8},{10,11... | collective-permute-start | bytes 276488 | tf_op jit(solution)/shard_map/ppermute | solution.py:251
  31.7 13.9 %collective-permute-start.18 = (bf16[512,256]{1,0:T(8,128)(2,1)S(1)}, bf16[512,256]{1,0:T(8,128)(2,1)S(1)}, u32[]{:S(2)}, u32[]{:S(2)}) collective-permute-start(bf16[512,256]{1,0:T(8,128)(2,1)S(1)} %get-tuple-element.58.refs_0_), channel_id=1, source_target_pairs={{0,1},{1,0},{2,3},{3,2},{4,5},{5,4},{6,7},{7,6},{8,9},{9,8},{10,11... | collective-permute-start | bytes 786440 | tf_op jit(solution)/shard_map/ppermute | solution.py:251
  32.2 13.4 %collective-permute-start.19 = (bf16[512,256]{1,0:T(8,128)(2,1)S(1)}, bf16[512,256]{1,0:T(8,128)(2,1)S(1)}, u32[]{:S(2)}, u32[]{:S(2)}) collective-permute-start(bf16[512,256]{1,0:T(8,128)(2,1)S(1)} %collective-permute-done.17.refs_1_), channel_id=1, source_target_pairs={{0,1},{1,0},{2,3},{3,2},{4,5},{5,4},{6,7},{7,6},{8,9},{9,8},{10,11... | collective-permute-start | bytes 786440 | tf_op jit(solution)/shard_map/ppermute | solution.py:251
  35.1 1.5 %collective-permute-start.11 = (bf16[2,64,720]{2,1,0:T(8,128)(2,1)S(1)}, bf16[2,64,720]{2,1,0:T(8,128)(2,1)S(1)}, u32[]{:S(2)}, u32[]{:S(2)}) collective-permute-start(bf16[2,64,720]{2,1,0:T(8,128)(2,1)S(1)} %get-tuple-element.46), channel_id=1, source_target_pairs={{0,1},{1,0},{2,3},{3,2},{4,5},{5,4},{6,7},{7,6},{8,9},{9,8},{10,11... | collective-permute-start | bytes 552968 | tf_op jit(solution)/shard_map/ppermute | solution.py:251
  36.6 4.4 %collective-permute-start.12 = (bf16[32,720]{1,0:T(8,128)(2,1)S(1)}, bf16[32,720]{1,0:T(8,128)(2,1)S(1)}, u32[]{:S(2)}, u32[]{:S(2)}) collective-permute-start(bf16[32,720]{1,0:T(8,128)(2,1)S(1)} %get-tuple-element.48), channel_id=1, source_target_pairs={{0,2},{1,3},{2,0},{3,1},{4,6},{5,7},{6,4},{7,5},{8,10},{9,11},{10,... | collective-permute-start | bytes 138248 | tf_op jit(solution)/shard_map/ppermute | solution.py:251
  37.2 6.7 %collective-permute-start.15 = (bf16[32,720]{1,0:T(8,128)(2,1)S(1)}, bf16[32,720]{1,0:T(8,128)(2,1)S(1)}, u32[]{:S(2)}, u32[]{:S(2)}) collective-permute-start(bf16[32,720]{1,0:T(8,128)(2,1)S(1)} %get-tuple-element.52), channel_id=1, source_target_pairs={{0,2},{1,3},{2,0},{3,1},{4,6},{5,7},{6,4},{7,5},{8,10},{9,11},{10,... | collective-permute-start | bytes 138248 | tf_op jit(solution)/shard_map/ppermute | solution.py:251
  41.0 5.7 %collective-permute-start.13 = (bf16[16,720]{1,0:T(8,128)(2,1)S(1)}, bf16[16,720]{1,0:T(8,128)(2,1)S(1)}, u32[]{:S(2)}, u32[]{:S(2)}) collective-permute-start(bf16[16,720]{1,0:T(8,128)(2,1)S(1)} %get-tuple-element.49), channel_id=1, source_target_pairs={{0,12},{4,8},{8,4},{12,0},{1,13},{5,9},{9,5},{13,1},{2,14},{6,10},... | collective-permute-start | bytes 69128 | tf_op jit(solution)/shard_map/ppermute | solution.py:251
  44.0 4.7 %collective-permute-start.14 = (bf16[16,720]{1,0:T(8,128)(2,1)S(1)}, bf16[16,720]{1,0:T(8,128)(2,1)S(1)}, u32[]{:S(2)}, u32[]{:S(2)}) collective-permute-start(bf16[16,720]{1,0:T(8,128)(2,1)S(1)} %get-tuple-element.50), channel_id=1, source_target_pairs={{0,8},{4,12},{8,0},{12,4},{1,9},{5,13},{9,1},{13,5},{2,10},{6,14},... | collective-permute-start | bytes 69128 | tf_op jit(solution)/shard_map/ppermute | solution.py:251
  44.0 4.7 %collective-permute-start.16 = (bf16[16,720]{1,0:T(8,128)(2,1)S(1)}, bf16[16,720]{1,0:T(8,128)(2,1)S(1)}, u32[]{:S(2)}, u32[]{:S(2)}) collective-permute-start(bf16[16,720]{1,0:T(8,128)(2,1)S(1)} %get-tuple-element.53), channel_id=1, source_target_pairs={{0,4},{4,0},{8,12},{12,8},{1,5},{5,1},{9,13},{13,9},{2,6},{6,2},{1... | collective-permute-start | bytes 69128 | tf_op jit(solution)/shard_map/ppermute | solution.py:251

commit v5 on v4

--- a/solution.py
+++ b/solution.py
@@ -135,12 +135,9 @@
         copy.wait()
 
 
-def second_kernel(
-    q_ref, kv_ref, before_ref, to_even_ref, to_odd_ref, sinks_ref, late_ref, placing_ref, all_ref, rows_ref
-):
+def second_kernel(q_ref, kv_ref, before_ref, rim_ref, sinks_ref, late_ref, placing_ref, all_ref, rows_ref):
     first = lax.axis_index("seq") == 0
-    odd = lax.rem(lax.axis_index("seq"), 2) == 1
-    rim = jnp.where(first, before_ref[...], jnp.where(odd, to_odd_ref[...], to_even_ref[...]))
+    rim = jnp.where(first, before_ref[...], rim_ref[...])
     groups = kv_ref.shape[1] // PAIR
     rows_of = []
     for g in range(groups):
@@ -282,7 +279,7 @@
     width = norm_gain.shape[0]
 
     tail = keyvals[toks - KEYS_SEEN :]
-    rims = [lax.ppermute(tail, "seq", [(i, i + 1) for i in range(odd, size - 1, 2)]) for odd in (1, 0)]
+    rim = lax.ppermute(tail, "seq", [(i, (i + 1) % size) for i in range(size)])
     loads = (queries, keyvals, preceding_keyvalues, w_out.T, residual.T)
     q, kv, before, w_t, residual_t, placing, mix_hi, mix_lo, sinks, late = call(
         functools.partial(first_kernel, live),
@@ -306,10 +303,10 @@
     attended, rows = call(
         second_kernel,
         (bf16(head_rows, toks), bf16(slots, head_rows)),
-        n_in=8,
+        n_in=7,
         flops=2 * toks * SPAN * head_rows,
         moved=2 * queries.size,
-    )(q, kv, before, *rims, sinks, late, placing)
+    )(q, kv, before, rim, sinks, late, placing)
 
     mine, theirs = gather_cuts(rows)
     total = jax.ShapeDtypeStruct((slots, feats), jnp.float32)
@@ -332,7 +329,7 @@
     stacked = call(stack_kernel, bf16(slots, feats), n_in=live)(*arrived)
     expert_mine, expert_theirs = gather_cuts(stacked)
 
-    attended, _ = lax.optimization_barrier((attended, chips))
+    attended, _ = lax.optimization_barrier((attended, arrived[0]))
     mine, theirs = gather_cuts(attended)
     resid = call(
         functools.partial(project_kernel, steps),

time: 50 us -> 49.7 us (level)
  starting transfers between devices: 23.2 us -> 18.7 us
  waiting for transfers between devices: 16.7 us -> 20.9 us
    ppermute x2 -> x1, starting transfers between devices: 5.58 us -> 3.02 us  [shards(): rim = lax.ppermute(tail, 'seq', [(i, (i + 1) % size) for i in range(size)])]
    ppermute x2 -> x1, waiting for transfers between devices: 0.01 us -> 2.11 us  [shards(): rim = lax.ppermute(tail, 'seq', [(i, (i + 1) % size) for i in range(size)])]
    ppermute x18, waiting for transfers between devices: 16.7 us -> 18.8 us  [swap(): lax.ppermute(block, axis, [(i, i ^ mask) for i in range(lax.axis_size(axi...]
    ppermute x18, starting transfers between devices: 17.6 us -> 15.7 us  [swap(): lax.ppermute(block, axis, [(i, i ^ mask) for i in range(lax.axis_size(axi...]
  transfers between devices with their start and end apart: 20 -> 19, of which waited for: 9 -> 12; matrix products, arithmetic and copies ran while one was open for 0% -> 0% of each run, Pallas kernels for 13% -> 13%
where the time goes in v5:
time: 49.7 us; the launch traced here: 49.5 us
  waiting for transfers between devices  20.9 us (42%)
  starting transfers between devices  18.7 us (38%)
  Pallas kernels  8.91 us (18%)
  local copies, waits for them, and re-layouts  0.87 us (2%)
    ppermute x18, waiting for transfers between devices, swap(): lax.ppermute(block, axis, [(i, i ^ mask) for i in range(lax.axis_size(axi...  18.8 us
    ppermute x18, starting transfers between devices, swap(): lax.ppermute(block, axis, [(i, i ^ mask) for i in range(lax.axis_size(axi...  15.7 us
    ppermute x1, starting transfers between devices, shards(): rim = lax.ppermute(tail, 'seq', [(i, (i + 1) % size) for i in range(size)])  3.02 us
    pallas_call x1, Pallas kernels, shards(): call(functools.partial(first_kernel, live), (*(bf16(*a.shape) for a in lo...  2.15 us
    ppermute x1, waiting for transfers between devices, shards(): rim = lax.ppermute(tail, 'seq', [(i, (i + 1) % size) for i in range(size)])  2.11 us
    pallas_call x1, Pallas kernels, shards(): call(functools.partial(expert_kernel, steps), (bf16(steps, slots, feats),...  2.06 us
    pallas_call x1, Pallas kernels, shards(): call(second_kernel, (bf16(head_rows, toks), bf16(slots, head_rows)), n_in...  1.18 us
    pallas_call x1, Pallas kernels, shards(): call(functools.partial(combine_kernel, live), bf16(feats, toks), n_in=liv...  1.13 us
  transfers between devices with their start and end apart: 19, of which 12 were waited for; matrix products, arithmetic and copies ran while one was open for 0% of the time, Pallas kernels for 13%

profile of v5, /device:TPU:0, one launch (start us, length us, event | category | flops | bytes accessed | tf_op | source)
XLA Modules:
  0.0 49.5 jit_solution(9496770817503435680)
XLA Ops:
  0.0 0.8 %slice.3 = bf16[128,256]{1,0:T(8,128)(2,1)S(1)} slice(bf16[256,256]{1,0:T(8,128)(2,1)} %refs_4_.2), slice={[128:256], [0:256]} | slice | bytes 131072 | tf_op jit(solution)/shard_map/slice | solution.py:281
  0.8 3.0 %collective-permute-start = (bf16[128,256]{1,0:T(8,128)(2,1)S(1)}, bf16[128,256]{1,0:T(8,128)(2,1)S(1)}, u32[]{:S(2)}, u32[]{:S(2)}) collective-permute-start(bf16[128,256]{1,0:T(8,128)(2,1)S(1)} %slice.3), channel_id=1, source_target_pairs={{0,4},{4,8},{8,12},{12,0},{1,5},{5,9},{9,13},{13,1},{2,6},{6,10},{... | collective-permute-start | bytes 196616 | tf_op jit(solution)/shard_map/ppermute | solution.py:282
  3.9 2.1 %shard_map.118 = (bf16[256,512]{1,0:T(8,128)(2,1)S(1)}, bf16[256,256]{1,0:T(8,128)(2,1)S(1)}, bf16[128,256]{1,0:T(8,128)(2,1)S(1)}, bf16[720,2048]{1,0:T(8,128)(...) custom-call(s32[4,256]{1,0:T(4,128)} %bitcast.17, ...), custom_call_target="tpu_custom_call" | custom-call | flops 134217728 | bytes 3579904 | tf_op jit(solution)/shard_map/pallas_call | solution.py:284
  6.0 2.1 %collective-permute-done.rim_ref = bf16[128,256]{1,0:T(8,128)(2,1)S(1)} collective-permute-done((bf16[128,256]{1,0:T(8,128)(2,1)S(1)}, bf16[128,256]{1,0:T(8,128)(2,1)S(1)}, u32[]{:S(2)}, u32[]{:S(2)}) %collective-permute-start) | collective-permute-done | bytes 65568 | tf_op jit(solution)/shard_map/ppermute | solution.py:282
  8.1 1.2 %shard_map.119 = (bf16[512,256]{1,0:T(8,128)(2,1)S(1)}, bf16[64,512]{1,0:T(8,128)(2,1)S(1)}) custom-call(bf16[256,512]{1,0:T(8,128)(2,1)S(1)} %get-tuple-element.32.q_ref, bf16[256,256]{1,0:T(8,128)(2,1)S(1)} %get-tuple-element.33.kv_ref, bf16[128,256]{1,0:T(8,128)(2,1)S(1)} %get-tuple-element.34.before_ref, ...), custom_call_target="tpu_custom_call" | custom-call | flops 67108864 | bytes 262144 | tf_op jit(solution)/shard_map/pallas_call | solution.py:303
  9.3 1.8 %collective-permute-start.1 = (bf16[64,512]{1,0:T(8,128)(2,1)S(1)}, bf16[64,512]{1,0:T(8,128)(2,1)S(1)}, u32[]{:S(2)}, u32[]{:S(2)}) collective-permute-start(bf16[64,512]{1,0:T(8,128)(2,1)S(1)} %get-tuple-element.38.mine_ref), channel_id=1, source_target_pairs={{0,2},{1,3},{2,0},{3,1},{4,6},{5,7},{6,4},{7,5},{8,10},{9,11},{10,... | collective-permute-start | bytes 196616 | tf_op jit(solution)/shard_map/ppermute | solution.py:248
  11.1 0.0 collective-permute-start.3
  11.1 2.5 %collective-permute-done.1.refs_0_ = bf16[64,512]{1,0:T(8,128)(2,1)S(1)} collective-permute-done((bf16[64,512]{1,0:T(8,128)(2,1)S(1)}, bf16[64,512]{1,0:T(8,128)(2,1)S(1)}, u32[]{:S(2)}, u32[]{:S(2)}) %collective-permute-start.1) | collective-permute-done | bytes 65568 | tf_op jit(solution)/shard_map/ppermute | solution.py:248
  13.7 0.0 collective-permute-start.2
  13.7 0.0 collective-permute-done.3.theirs_ref
  13.7 0.6 %shard_map.120.refs_1_ = f32[64,720]{1,0:T(8,128)S(1)} custom-call(bf16[64,512]{1,0:T(8,128)(2,1)S(1)} %get-tuple-element.38.mine_ref, bf16[64,512]{1,0:T(8,128)(2,1)S(1)} %collective-permute-done.3.theirs_ref, bf16[720,2048]{1,0:T(8,128)(2,1)S(1)} %get-tuple-element.39.w_ref.refs_2_.refs_4_, bf16[720,256]{1,0:T(8,128)(2,1)S(1)} %get-tuple-element.40.residual_ref.refs_5_, ...), custom_call_target="tpu_custom_call" | custom-call | flops 47185920 | bytes 737280 | tf_op jit(solution)/shard_map/pallas_call | solution.py:314
  14.3 0.0 copy-start.2
  14.3 0.4 shard_map.121.refs_1_
  14.7 0.0 copy-start
  14.7 0.0 copy-start.3
  14.7 0.2 collective-permute-done.2.refs_0_
  14.9 0.4 shard_map.122
  15.3 2.1 %collective-permute-start.4 = (bf16[16,720]{1,0:T(8,128)(2,1)S(1)}, bf16[16,720]{1,0:T(8,128)(2,1)S(1)}, u32[]{:S(2)}, u32[]{:S(2)}) collective-permute-start(bf16[16,720]{1,0:T(8,128)(2,1)S(1)} %get-tuple-element.41), channel_id=1, source_target_pairs={{0,12},{4,8},{8,4},{12,0},{1,13},{5,9},{9,5},{13,1},{2,14},{6,10},... | collective-permute-start | bytes 69128 | tf_op jit(solution)/shard_map/ppermute | solution.py:248
  17.4 3.6 %collective-permute-done.4.refs_0_ = bf16[16,720]{1,0:T(8,128)(2,1)S(1)} collective-permute-done((bf16[16,720]{1,0:T(8,128)(2,1)S(1)}, bf16[16,720]{1,0:T(8,128)(2,1)S(1)}, u32[]{:S(2)}, u32[]{:S(2)}) %collective-permute-start.4) | collective-permute-done | bytes 23072 | tf_op jit(solution)/shard_map/ppermute | solution.py:248
  21.0 1.7 %collective-permute-start.16 = (bf16[512,256]{1,0:T(8,128)(2,1)S(1)}, bf16[512,256]{1,0:T(8,128)(2,1)S(1)}, u32[]{:S(2)}, u32[]{:S(2)}) collective-permute-start(bf16[512,256]{1,0:T(8,128)(2,1)S(1)} %get-tuple-element.58.refs_0_), channel_id=1, source_target_pairs={{0,2},{1,3},{2,0},{3,1},{4,6},{5,7},{6,4},{7,5},{8,10},{9,11},{10,... | collective-permute-start | bytes 786440 | tf_op jit(solution)/shard_map/ppermute | solution.py:248
  22.7 0.0 collective-permute-start.5
  22.7 2.4 %collective-permute-start.6 = (bf16[16,720]{1,0:T(8,128)(2,1)S(1)}, bf16[16,720]{1,0:T(8,128)(2,1)S(1)}, u32[]{:S(2)}, u32[]{:S(2)}) collective-permute-start(bf16[16,720]{1,0:T(8,128)(2,1)S(1)} %get-tuple-element.43), channel_id=1, source_target_pairs={{0,4},{4,0},{8,12},{12,8},{1,5},{5,1},{9,13},{13,9},{2,6},{6,2},{1... | collective-permute-start | bytes 69128 | tf_op jit(solution)/shard_map/ppermute | solution.py:248
  25.1 2.4 %collective-permute-done.5.refs_1_ = bf16[16,720]{1,0:T(8,128)(2,1)S(1)} collective-permute-done((bf16[16,720]{1,0:T(8,128)(2,1)S(1)}, bf16[16,720]{1,0:T(8,128)(2,1)S(1)}, u32[]{:S(2)}, u32[]{:S(2)}) %collective-permute-start.5) | collective-permute-done | bytes 23072 | tf_op jit(solution)/shard_map/ppermute | solution.py:248
  27.4 0.0 collective-permute-done.6.refs_2_
  27.4 0.4 collective-permute-start.7
  27.8 0.0 collective-permute-start.8
  27.8 4.3 %collective-permute-done.7.refs_1_ = bf16[64,720]{1,0:T(8,128)(2,1)S(1)} collective-permute-done((bf16[64,720]{1,0:T(8,128)(2,1)S(1)}, bf16[64,720]{1,0:T(8,128)(2,1)S(1)}, u32[]{:S(2)}, u32[]{:S(2)}) %collective-permute-start.7) | collective-permute-done | bytes 92192 | tf_op jit(solution)/shard_map/ppermute | solution.py:248
  32.1 0.0 collective-permute-start.9
  32.1 0.5 %collective-permute-start.17 = (bf16[512,256]{1,0:T(8,128)(2,1)S(1)}, bf16[512,256]{1,0:T(8,128)(2,1)S(1)}, u32[]{:S(2)}, u32[]{:S(2)}) collective-permute-start(bf16[512,256]{1,0:T(8,128)(2,1)S(1)} %get-tuple-element.58.refs_0_), channel_id=1, source_target_pairs={{0,1},{1,0},{2,3},{3,2},{4,5},{5,4},{6,7},{7,6},{8,9},{9,8},{10,11... | collective-permute-start | bytes 786440 | tf_op jit(solution)/shard_map/ppermute | solution.py:248
  32.6 0.0 collective-permute-done.16.refs_1_
  32.6 0.0 collective-permute-start.18
  32.6 0.8 %collective-permute-done.9.refs_3_ = bf16[64,720]{1,0:T(8,128)(2,1)S(1)} collective-permute-done((bf16[64,720]{1,0:T(8,128)(2,1)S(1)}, bf16[64,720]{1,0:T(8,128)(2,1)S(1)}, u32[]{:S(2)}, u32[]{:S(2)}) %collective-permute-start.9) | collective-permute-done | bytes 92192 | tf_op jit(solution)/shard_map/ppermute | solution.py:248
  33.4 2.1 %shard_map.124 = (bf16[2,64,720]{2,1,0:T(8,128)(2,1)S(1)}, bf16[2,64,720]{2,1,0:T(8,128)(2,1)S(1)}) custom-call(bf16[64,720]{1,0:T(8,128)(2,1)S(1)} %shard_map.123.refs_0_, bf16[64,720]{1,0:T(8,128)(2,1)S(1)} %collective-permute-done.7.refs_1_, bf16[64,720]{1,0:T(8,128)(2,1)S(1)} %collective-permute-done.8.refs_2_, ...), custom_call_target="tpu_custom_call" | custom-call | flops 398131200 | bytes 6220800 | tf_op jit(solution)/shard_map/pallas_call | solution.py:342
  35.5 0.2 collective-permute-start.10
  35.7 1.3 %collective-permute-done.10.given_ref = bf16[2,64,720]{2,1,0:T(8,128)(2,1)S(1)} collective-permute-done((bf16[2,64,720]{2,1,0:T(8,128)(2,1)S(1)}, bf16[2,64,720]{2,1,0:T(8,128)(2,1)S(1)}, u32[]{:S(2)}, u32[]{:S(2)}) %collective-permute-start.10) | collective-permute-done | bytes 184352 | tf_op jit(solution)/shard_map/ppermute | solution.py:248
  37.0 0.1 shard_map.125
  37.1 0.4 collective-permute-start.11
  37.4 1.7 %collective-permute-start.14 = (bf16[32,720]{1,0:T(8,128)(2,1)S(1)}, bf16[32,720]{1,0:T(8,128)(2,1)S(1)}, u32[]{:S(2)}, u32[]{:S(2)}) collective-permute-start(bf16[32,720]{1,0:T(8,128)(2,1)S(1)} %get-tuple-element.52), channel_id=1, source_target_pairs={{0,2},{1,3},{2,0},{3,1},{4,6},{5,7},{6,4},{7,5},{8,10},{9,11},{10,... | collective-permute-start | bytes 138248 | tf_op jit(solution)/shard_map/ppermute | solution.py:248
  39.1 2.3 %collective-permute-done.11.refs_1_ = bf16[32,720]{1,0:T(8,128)(2,1)S(1)} collective-permute-done((bf16[32,720]{1,0:T(8,128)(2,1)S(1)}, bf16[32,720]{1,0:T(8,128)(2,1)S(1)}, u32[]{:S(2)}, u32[]{:S(2)}) %collective-permute-start.11) | collective-permute-done | bytes 46112 | tf_op jit(solution)/shard_map/ppermute | solution.py:248
  41.5 1.9 %collective-permute-start.12 = (bf16[16,720]{1,0:T(8,128)(2,1)S(1)}, bf16[16,720]{1,0:T(8,128)(2,1)S(1)}, u32[]{:S(2)}, u32[]{:S(2)}) collective-permute-start(bf16[16,720]{1,0:T(8,128)(2,1)S(1)} %get-tuple-element.49), channel_id=1, source_target_pairs={{0,12},{4,8},{8,4},{12,0},{1,13},{5,9},{9,5},{13,1},{2,14},{6,10},... | collective-permute-start | bytes 69128 | tf_op jit(solution)/shard_map/ppermute | solution.py:248
  43.3 1.1 %collective-permute-start.13 = (bf16[16,720]{1,0:T(8,128)(2,1)S(1)}, bf16[16,720]{1,0:T(8,128)(2,1)S(1)}, u32[]{:S(2)}, u32[]{:S(2)}) collective-permute-start(bf16[16,720]{1,0:T(8,128)(2,1)S(1)} %get-tuple-element.50), channel_id=1, source_target_pairs={{0,8},{4,12},{8,0},{12,4},{1,9},{5,13},{9,1},{13,5},{2,10},{6,14},... | collective-permute-start | bytes 69128 | tf_op jit(solution)/shard_map/ppermute | solution.py:248
  44.5 1.5 %collective-permute-start.15 = (bf16[16,720]{1,0:T(8,128)(2,1)S(1)}, bf16[16,720]{1,0:T(8,128)(2,1)S(1)}, u32[]{:S(2)}, u32[]{:S(2)}) collective-permute-start(bf16[16,720]{1,0:T(8,128)(2,1)S(1)} %get-tuple-element.53), channel_id=1, source_target_pairs={{0,4},{4,0},{8,12},{12,8},{1,5},{5,1},{9,13},{13,9},{2,6},{6,2},{1... | collective-permute-start | bytes 69128 | tf_op jit(solution)/shard_map/ppermute | solution.py:248
  46.0 0.0 collective-permute-done.17.refs_2_
  46.0 0.9 %shard_map.128.refs_6_ = bf16[720,256]{1,0:T(8,128)(2,1)S(1)} custom-call(bf16[512,256]{1,0:T(8,128)(2,1)S(1)} %get-tuple-element.58.refs_0_, bf16[512,256]{1,0:T(8,128)(2,1)S(1)} %collective-permute-done.16.refs_1_, bf16[512,256]{1,0:T(8,128)(2,1)S(1)} %collective-permute-done.17.refs_2_, bf16[512,256]{1,0:T(8,128)(2,1)S(1)} %collective-permute-done.18.refs_3_, ...), custom_call_target="tpu_custom_call" | custom-call | flops 754974720 | bytes 2949120 | tf_op jit(solution)/shard_map/pallas_call | solution.py:334
  47.0 0.2 collective-permute-done.12.refs_0_
  47.2 0.9 %collective-permute-done.13.refs_1_ = bf16[16,720]{1,0:T(8,128)(2,1)S(1)} collective-permute-done((bf16[16,720]{1,0:T(8,128)(2,1)S(1)}, bf16[16,720]{1,0:T(8,128)(2,1)S(1)}, u32[]{:S(2)}, u32[]{:S(2)}) %collective-permute-start.13) | collective-permute-done | bytes 23072 | tf_op jit(solution)/shard_map/ppermute | solution.py:248
  48.1 0.3 collective-permute-done.15.refs_2_
  48.4 1.1 %shard_map.129 = bf16[720,256]{1,0:T(8,128)(2,1)} custom-call(bf16[16,720]{1,0:T(8,128)(2,1)S(1)} %collective-permute-done.12.refs_0_, bf16[16,720]{1,0:T(8,128)(2,1)S(1)} %collective-permute-done.13.refs_1_, bf16[16,720]{1,0:T(8,128)(2,1)S(1)} %collective-permute-done.15.refs_2_, bf16[16,720]{1,0:T(8,128)(2,1)S(1)} %get-tuple-element.54.refs_3_, ...), custom_call_target="tpu_custom_call" | custom-call | tf_op jit(solution)/shard_map/pallas_call | solution.py:365
  (11 shorter events, 0.1 us)
Async XLA Ops:
  0.8 7.3 %collective-permute-start = (bf16[128,256]{1,0:T(8,128)(2,1)S(1)}, bf16[128,256]{1,0:T(8,128)(2,1)S(1)}, u32[]{:S(2)}, u32[]{:S(2)}) collective-permute-start(bf16[128,256]{1,0:T(8,128)(2,1)S(1)} %slice.3), channel_id=1, source_target_pairs={{0,4},{4,8},{8,12},{12,0},{1,5},{5,9},{9,13},{13,1},{2,6},{6,10},{... | collective-permute-start | bytes 196616 | tf_op jit(solution)/shard_map/ppermute | solution.py:282
  9.3 4.3 %collective-permute-start.1 = (bf16[64,512]{1,0:T(8,128)(2,1)S(1)}, bf16[64,512]{1,0:T(8,128)(2,1)S(1)}, u32[]{:S(2)}, u32[]{:S(2)}) collective-permute-start(bf16[64,512]{1,0:T(8,128)(2,1)S(1)} %get-tuple-element.38.mine_ref), channel_id=1, source_target_pairs={{0,2},{1,3},{2,0},{3,1},{4,6},{5,7},{6,4},{7,5},{8,10},{9,11},{10,... | collective-permute-start | bytes 196616 | tf_op jit(solution)/shard_map/ppermute | solution.py:248
  11.1 2.6 %collective-permute-start.3 = (bf16[64,512]{1,0:T(8,128)(2,1)S(1)}, bf16[64,512]{1,0:T(8,128)(2,1)S(1)}, u32[]{:S(2)}, u32[]{:S(2)}) collective-permute-start(bf16[64,512]{1,0:T(8,128)(2,1)S(1)} %get-tuple-element.38.mine_ref), channel_id=1, source_target_pairs={{0,1},{1,0},{2,3},{3,2},{4,5},{5,4},{6,7},{7,6},{8,9},{9,8},{10,11... | collective-permute-start | bytes 196616 | tf_op jit(solution)/shard_map/ppermute | solution.py:248
  13.7 1.3 %collective-permute-start.2 = (bf16[64,512]{1,0:T(8,128)(2,1)S(1)}, bf16[64,512]{1,0:T(8,128)(2,1)S(1)}, u32[]{:S(2)}, u32[]{:S(2)}) collective-permute-start(bf16[64,512]{1,0:T(8,128)(2,1)S(1)} %collective-permute-done.1.refs_0_), channel_id=1, source_target_pairs={{0,1},{1,0},{2,3},{3,2},{4,5},{5,4},{6,7},{7,6},{8,9},{9,8},{10,11... | collective-permute-start | bytes 196616 | tf_op jit(solution)/shard_map/ppermute | solution.py:248
  14.3 19.1 %copy-start.1 = (bf16[1,2880,360]{1,2,0:T(8,128)(2,1)S(1)}, bf16[1,2880,360]{1,2,0:T(8,128)(2,1)}, u32[]{:S(2)}) copy-start(bf16[1,2880,360]{1,2,0:T(8,128)(2,1)} %param.22) | copy-start | bytes 6220804
  14.3 19.1 %copy-start.2 = (bf16[1,360,2880]{2,1,0:T(8,128)(2,1)S(1)}, bf16[1,360,2880]{2,1,0:T(8,128)(2,1)}, u32[]{:S(2)}) copy-start(bf16[1,360,2880]{2,1,0:T(8,128)(2,1)} %param.23) | copy-start | bytes 6220804
  14.7 18.7 %copy-start = (bf16[1,2880,360]{1,2,0:T(8,128)(2,1)S(1)}, bf16[1,2880,360]{1,2,0:T(8,128)(2,1)}, u32[]{:S(2)}) copy-start(bf16[1,2880,360]{1,2,0:T(8,128)(2,1)} %param.21) | copy-start | bytes 6220804
  14.7 18.7 %copy-start.3 = (f32[2880]{0:T(1024)S(1)}, f32[2880]{0:T(1024)}, u32[]{:S(2)}) copy-start(f32[2880]{0:T(1024)} %refs_4_.3) | copy-start | bytes 34564
  15.3 5.7 %collective-permute-start.4 = (bf16[16,720]{1,0:T(8,128)(2,1)S(1)}, bf16[16,720]{1,0:T(8,128)(2,1)S(1)}, u32[]{:S(2)}, u32[]{:S(2)}) collective-permute-start(bf16[16,720]{1,0:T(8,128)(2,1)S(1)} %get-tuple-element.41), channel_id=1, source_target_pairs={{0,12},{4,8},{8,4},{12,0},{1,13},{5,9},{9,5},{13,1},{2,14},{6,10},... | collective-permute-start | bytes 69128 | tf_op jit(solution)/shard_map/ppermute | solution.py:248
  21.0 11.7 %collective-permute-start.16 = (bf16[512,256]{1,0:T(8,128)(2,1)S(1)}, bf16[512,256]{1,0:T(8,128)(2,1)S(1)}, u32[]{:S(2)}, u32[]{:S(2)}) collective-permute-start(bf16[512,256]{1,0:T(8,128)(2,1)S(1)} %get-tuple-element.58.refs_0_), channel_id=1, source_target_pairs={{0,2},{1,3},{2,0},{3,1},{4,6},{5,7},{6,4},{7,5},{8,10},{9,11},{10,... | collective-permute-start | bytes 786440 | tf_op jit(solution)/shard_map/ppermute | solution.py:248
  22.7 4.7 %collective-permute-start.5 = (bf16[16,720]{1,0:T(8,128)(2,1)S(1)}, bf16[16,720]{1,0:T(8,128)(2,1)S(1)}, u32[]{:S(2)}, u32[]{:S(2)}) collective-permute-start(bf16[16,720]{1,0:T(8,128)(2,1)S(1)} %get-tuple-element.42), channel_id=1, source_target_pairs={{0,8},{4,12},{8,0},{12,4},{1,9},{5,13},{9,1},{13,5},{2,10},{6,14},... | collective-permute-start | bytes 69128 | tf_op jit(solution)/shard_map/ppermute | solution.py:248
  22.7 4.7 %collective-permute-start.6 = (bf16[16,720]{1,0:T(8,128)(2,1)S(1)}, bf16[16,720]{1,0:T(8,128)(2,1)S(1)}, u32[]{:S(2)}, u32[]{:S(2)}) collective-permute-start(bf16[16,720]{1,0:T(8,128)(2,1)S(1)} %get-tuple-element.43), channel_id=1, source_target_pairs={{0,4},{4,0},{8,12},{12,8},{1,5},{5,1},{9,13},{13,9},{2,6},{6,2},{1... | collective-permute-start | bytes 69128 | tf_op jit(solution)/shard_map/ppermute | solution.py:248
  27.4 4.7 %collective-permute-start.7 = (bf16[64,720]{1,0:T(8,128)(2,1)S(1)}, bf16[64,720]{1,0:T(8,128)(2,1)S(1)}, u32[]{:S(2)}, u32[]{:S(2)}) collective-permute-start(bf16[64,720]{1,0:T(8,128)(2,1)S(1)} %shard_map.123.refs_0_), channel_id=1, source_target_pairs={{0,2},{1,3},{2,0},{3,1},{4,6},{5,7},{6,4},{7,5},{8,10},{9,11},{10,... | collective-permute-start | bytes 276488 | tf_op jit(solution)/shard_map/ppermute | solution.py:248
  27.8 4.8 %collective-permute-start.8 = (bf16[64,720]{1,0:T(8,128)(2,1)S(1)}, bf16[64,720]{1,0:T(8,128)(2,1)S(1)}, u32[]{:S(2)}, u32[]{:S(2)}) collective-permute-start(bf16[64,720]{1,0:T(8,128)(2,1)S(1)} %shard_map.123.refs_0_), channel_id=1, source_target_pairs={{0,1},{1,0},{2,3},{3,2},{4,5},{5,4},{6,7},{7,6},{8,9},{9,8},{10,11... | collective-permute-start | bytes 276488 | tf_op jit(solution)/shard_map/ppermute | solution.py:248
  32.1 1.3 %collective-permute-start.9 = (bf16[64,720]{1,0:T(8,128)(2,1)S(1)}, bf16[64,720]{1,0:T(8,128)(2,1)S(1)}, u32[]{:S(2)}, u32[]{:S(2)}) collective-permute-start(bf16[64,720]{1,0:T(8,128)(2,1)S(1)} %collective-permute-done.7.refs_1_), channel_id=1, source_target_pairs={{0,1},{1,0},{2,3},{3,2},{4,5},{5,4},{6,7},{7,6},{8,9},{9,8},{10,11... | collective-permute-start | bytes 276488 | tf_op jit(solution)/shard_map/ppermute | solution.py:248
  32.1 13.9 %collective-permute-start.17 = (bf16[512,256]{1,0:T(8,128)(2,1)S(1)}, bf16[512,256]{1,0:T(8,128)(2,1)S(1)}, u32[]{:S(2)}, u32[]{:S(2)}) collective-permute-start(bf16[512,256]{1,0:T(8,128)(2,1)S(1)} %get-tuple-element.58.refs_0_), channel_id=1, source_target_pairs={{0,1},{1,0},{2,3},{3,2},{4,5},{5,4},{6,7},{7,6},{8,9},{9,8},{10,11... | collective-permute-start | bytes 786440 | tf_op jit(solution)/shard_map/ppermute | solution.py:248
  32.6 13.4 %collective-permute-start.18 = (bf16[512,256]{1,0:T(8,128)(2,1)S(1)}, bf16[512,256]{1,0:T(8,128)(2,1)S(1)}, u32[]{:S(2)}, u32[]{:S(2)}) collective-permute-start(bf16[512,256]{1,0:T(8,128)(2,1)S(1)} %collective-permute-done.16.refs_1_), channel_id=1, source_target_pairs={{0,1},{1,0},{2,3},{3,2},{4,5},{5,4},{6,7},{7,6},{8,9},{9,8},{10,11... | collective-permute-start | bytes 786440 | tf_op jit(solution)/shard_map/ppermute | solution.py:248
  35.5 1.5 %collective-permute-start.10 = (bf16[2,64,720]{2,1,0:T(8,128)(2,1)S(1)}, bf16[2,64,720]{2,1,0:T(8,128)(2,1)S(1)}, u32[]{:S(2)}, u32[]{:S(2)}) collective-permute-start(bf16[2,64,720]{2,1,0:T(8,128)(2,1)S(1)} %get-tuple-element.46), channel_id=1, source_target_pairs={{0,1},{1,0},{2,3},{3,2},{4,5},{5,4},{6,7},{7,6},{8,9},{9,8},{10,11... | collective-permute-start | bytes 552968 | tf_op jit(solution)/shard_map/ppermute | solution.py:248
  37.1 4.4 %collective-permute-start.11 = (bf16[32,720]{1,0:T(8,128)(2,1)S(1)}, bf16[32,720]{1,0:T(8,128)(2,1)S(1)}, u32[]{:S(2)}, u32[]{:S(2)}) collective-permute-start(bf16[32,720]{1,0:T(8,128)(2,1)S(1)} %get-tuple-element.48), channel_id=1, source_target_pairs={{0,2},{1,3},{2,0},{3,1},{4,6},{5,7},{6,4},{7,5},{8,10},{9,11},{10,... | collective-permute-start | bytes 138248 | tf_op jit(solution)/shard_map/ppermute | solution.py:248
  37.4 7.0 %collective-permute-start.14 = (bf16[32,720]{1,0:T(8,128)(2,1)S(1)}, bf16[32,720]{1,0:T(8,128)(2,1)S(1)}, u32[]{:S(2)}, u32[]{:S(2)}) collective-permute-start(bf16[32,720]{1,0:T(8,128)(2,1)S(1)} %get-tuple-element.52), channel_id=1, source_target_pairs={{0,2},{1,3},{2,0},{3,1},{4,6},{5,7},{6,4},{7,5},{8,10},{9,11},{10,... | collective-permute-start | bytes 138248 | tf_op jit(solution)/shard_map/ppermute | solution.py:248
  41.5 5.7 %collective-permute-start.12 = (bf16[16,720]{1,0:T(8,128)(2,1)S(1)}, bf16[16,720]{1,0:T(8,128)(2,1)S(1)}, u32[]{:S(2)}, u32[]{:S(2)}) collective-permute-start(bf16[16,720]{1,0:T(8,128)(2,1)S(1)} %get-tuple-element.49), channel_id=1, source_target_pairs={{0,12},{4,8},{8,4},{12,0},{1,13},{5,9},{9,5},{13,1},{2,14},{6,10},... | collective-permute-start | bytes 69128 | tf_op jit(solution)/shard_map/ppermute | solution.py:248
  43.3 4.7 %collective-permute-start.13 = (bf16[16,720]{1,0:T(8,128)(2,1)S(1)}, bf16[16,720]{1,0:T(8,128)(2,1)S(1)}, u32[]{:S(2)}, u32[]{:S(2)}) collective-permute-start(bf16[16,720]{1,0:T(8,128)(2,1)S(1)} %get-tuple-element.50), channel_id=1, source_target_pairs={{0,8},{4,12},{8,0},{12,4},{1,9},{5,13},{9,1},{13,5},{2,10},{6,14},... | collective-permute-start | bytes 69128 | tf_op jit(solution)/shard_map/ppermute | solution.py:248
  44.5 3.9 %collective-permute-start.15 = (bf16[16,720]{1,0:T(8,128)(2,1)S(1)}, bf16[16,720]{1,0:T(8,128)(2,1)S(1)}, u32[]{:S(2)}, u32[]{:S(2)}) collective-permute-start(bf16[16,720]{1,0:T(8,128)(2,1)S(1)} %get-tuple-element.53), channel_id=1, source_target_pairs={{0,4},{4,0},{8,12},{12,8},{1,5},{5,1},{9,13},{13,9},{2,6},{6,2},{1... | collective-permute-start | bytes 69128 | tf_op jit(solution)/shard_map/ppermute | solution.py:248

commit v6 on v5

--- a/solution.py
+++ b/solution.py
@@ -196,27 +196,72 @@
     resid_ref[...] = total.astype(jnp.bfloat16)
 
 
-def expert_kernel(steps, *refs):
-    cuts = CORES * steps
-    gain_ref, gate_ref, up_ref, down_ref, kept_ref, given_ref, blocks_ref, rows_ref = refs[cuts:]
-    width = refs[0].shape[1]
-    for i in range(cuts):
-        blocks_ref[origin(i % steps, i >= steps)] = refs[i][...]
-    wide = [blocks_ref[p].astype(jnp.float32) for p in range(cuts)]
-    squares = sum(jnp.sum(b * b, axis=1, keepdims=True) for b in wide)
+def weights_kernel(gate_ref, up_ref, down_ref, gain_ref, gates_ref, ups_ref, downs_ref, gains_ref, *scratch):
+    held, sems = scratch[:3], scratch[3]
+    copies = [
+        pltpu.make_async_copy(source, target, sems.at[i])
+        for i, (source, target) in enumerate(zip((gate_ref, up_ref, down_ref), held))
+    ]
+    for copy in copies:
+        copy.start()
+    cuts, _, width = gates_ref.shape
+    gain = gain_ref[...].reshape(1, cuts * width)
+    for p in range(cuts):
+        gains_ref[p] = gain[:, p * width : (p + 1) * width]
+    for copy, source, target in zip(copies, held, (gates_ref, ups_ref, downs_ref)):
+        copy.wait()
+        for p in range(cuts):
+            target[p] = source[:, p * width : (p + 1) * width]
+
+
+def add_features(sums, first, blocks, gains_ref, gates_ref, ups_ref, steps):
+    gate, up, squares = sums
+    for i, block in enumerate(blocks, first):
+        p = origin(i % steps, i >= steps)
+        wide = block[...].astype(jnp.float32)
+        squares += jnp.sum(wide * wide, axis=1, keepdims=True)
+        rows = (wide * gains_ref[p]).astype(jnp.bfloat16)
+        gate += dot(rows, gates_ref[p], NT)
+        up += dot(rows, ups_ref[p], NT)
+    return gate, up, squares
+
+
+def store_sums(sums, refs):
+    for ref, value in zip(refs, sums):
+        ref[...] = jnp.broadcast_to(value, ref.shape)
+
+
+def expert_near_kernel(steps, mine_ref, theirs_ref, gains_ref, gates_ref, ups_ref, *out_refs):
+    zeros = jnp.zeros(out_refs[0].shape, jnp.float32)
+    sums = (zeros, zeros, jnp.zeros((zeros.shape[0], 1), jnp.float32))
+    for first, block in ((0, mine_ref), (steps, theirs_ref)):
+        sums = add_features(sums, first, [block], gains_ref, gates_ref, ups_ref, steps)
+    store_sums(sums, out_refs)
+
+
+def expert_chips_kernel(steps, *refs):
+    blocks, refs = refs[: steps - 1], refs[steps - 1 :]
+    sums = (refs[0][...], refs[1][...], refs[2][:, :1])
+    store_sums(add_features(sums, 1, blocks, *refs[3:6], steps), refs[6:])
+
+
+def expert_last_kernel(steps, *refs):
+    blocks, refs = refs[: steps - 1], refs[steps - 1 :]
+    sums = (refs[0][...], refs[1][...], refs[2][:, :1])
+    gains_ref, gates_ref, ups_ref, downs_ref, given_ref, activated_ref = refs[3:]
+    gate, up, squares = add_features(sums, steps + 1, blocks, gains_ref, gates_ref, ups_ref, steps)
+    cuts, _, width = gates_ref.shape
     scale = lax.rsqrt(squares / (cuts * width) + norm_eps)
-    gain = gain_ref[...].reshape(1, cuts * width)
-    rows_ref[...] = (jnp.concatenate(wide, axis=1) * scale * gain).astype(jnp.bfloat16)
-    rows = rows_ref[...]
-    gate = dot(rows, gate_ref[...], NT)
-    up = dot(rows, up_ref[...], NT)
+    gate, up = gate * scale, up * scale
     activated = ((up + 1.0) * gate * jax.nn.sigmoid(glu_alpha * gate)).astype(jnp.bfloat16)
-    out = dot(activated, down_ref[...], NN).astype(jnp.bfloat16)
-    for p in range(cuts):
-        blocks_ref[p] = out[:, p * width : (p + 1) * width]
+    activated_ref[...] = activated
     for k in range(steps):
-        kept_ref[k] = blocks_ref[origin(k, False)]
-        given_ref[k] = blocks_ref[origin(k, True)]
+        given_ref[k] = dot(activated, downs_ref[origin(k, True)], NN).astype(jnp.bfloat16)
+
+
+def expert_kept_kernel(activated_ref, downs_ref, kept_ref):
+    for k in range(kept_ref.shape[0]):
+        kept_ref[k] = dot(activated_ref[...], downs_ref[origin(k, False)], NN).astype(jnp.bfloat16)
 
 
 def add_cores_kernel(kept_ref, given_ref, *out_refs):
@@ -248,10 +293,16 @@
     return lax.ppermute(block, axis, [(i, i ^ mask) for i in range(lax.axis_size(axis))])
 
 
-def gather_cuts(block):
-    steps = lax.axis_size("cuts") // CORES
-    mine = [block] + [swap(block, "cuts", CORES * k) for k in range(1, steps)]
-    return mine, [swap(b, "cuts", 1) for b in mine]
+def from_chips(block):
+    return [swap(block, "cuts", CORES * k) for k in range(1, lax.axis_size("cuts") // CORES)]
+
+
+def from_sibling(block):
+    return swap(block, "cuts", 1)
+
+
+def after(arrays, others):
+    return lax.optimization_barrier((arrays, others))[0]
 
 
 def shards(
@@ -277,6 +328,7 @@
     head_rows = queries.shape[1]
     heads = head_rows // HEAD_SIZE
     width = norm_gain.shape[0]
+    hidden = w_gate.shape[2]
 
     tail = keyvals[toks - KEYS_SEEN :]
     rim = lax.ppermute(tail, "seq", [(i, (i + 1) % size) for i in range(size)])
@@ -308,14 +360,17 @@
         moved=2 * queries.size,
     )(q, kv, before, rim, sinks, late, placing)
 
-    mine, theirs = gather_cuts(rows)
+    chip_rows = from_chips(rows)
+    sibling_rows = from_sibling(rows)
     total = jax.ShapeDtypeStruct((slots, feats), jnp.float32)
     part = dict(flops=slots * w_out.size // 2, moved=w_out.size // 2)
     near = call(functools.partial(rows_near_kernel, steps), total, n_in=5, **part)(
-        mine[0], theirs[0], w_t, residual_t, placing
-    )
+        rows, sibling_rows, w_t, residual_t, placing
+    )
+    chip_rows = after(chip_rows, near)
+    relayed_rows = [from_sibling(b) for b in chip_rows]
     chips = call(functools.partial(rows_chips_kernel, steps), total, n_in=steps + 1, **part)(
-        *mine[1:], near, w_t
+        *chip_rows, near, w_t
     )
     outgoing = call(
         functools.partial(rows_last_kernel, steps),
@@ -323,33 +378,52 @@
         n_in=steps + 1,
         scratch=[pltpu.VMEM((live, CAP, feats), jnp.bfloat16)],
         **part,
-    )(*theirs[1:], chips, w_t)
+    )(*relayed_rows, chips, w_t)
 
     arrived = [swap(outgoing[k], "seq", k) for k in range(live - 1, 0, -1)] + [outgoing[0]]
-    stacked = call(stack_kernel, bf16(slots, feats), n_in=live)(*arrived)
-    expert_mine, expert_theirs = gather_cuts(stacked)
-
-    attended, _ = lax.optimization_barrier((attended, arrived[0]))
-    mine, theirs = gather_cuts(attended)
+
+    w_gate_t, w_up_t, w_down_t, _ = lax.optimization_barrier((w_gate[0].T, w_up[0].T, w_down[0], outgoing[0]))
+    weights = call(
+        weights_kernel,
+        (*(bf16(cuts, hidden, feats),) * 3, jax.ShapeDtypeStruct((cuts, 1, feats), jnp.float32)),
+        n_in=4,
+        hbm=range(3),
+        scratch=[*(pltpu.VMEM((hidden, width), jnp.bfloat16),) * 3, pltpu.SemaphoreType.DMA((3,))],
+        moved=6 * w_gate.size,
+    )(in_hbm(w_gate_t), in_hbm(w_up_t), in_hbm(w_down_t), norm_gain)
+    gates, ups, downs, gains = weights
+    sums = (
+        *(jax.ShapeDtypeStruct((slots, hidden), jnp.float32),) * 2,
+        jax.ShapeDtypeStruct((slots, KEYS_SEEN), jnp.float32),
+    )
+    part = dict(flops=slots * w_gate.size, moved=w_gate.size)
+    stacked = call(stack_kernel, bf16(slots, feats), n_in=live)(*after(arrived, gains))
+    chip_rows = from_chips(stacked)
+    near = call(functools.partial(expert_near_kernel, steps), sums, n_in=5, **part)(
+        stacked, from_sibling(stacked), gains, gates, ups
+    )
+    chip_rows = after(chip_rows, near)
+    relayed_rows = [from_sibling(b) for b in chip_rows]
+    chips = call(functools.partial(expert_chips_kernel, steps), sums, n_in=steps + 5, **part)(
+        *chip_rows, *near, gains, gates, ups
+    )
+    given, activated = call(
+        functools.partial(expert_last_kernel, steps),
+        (bf16(steps, slots, feats), bf16(slots, hidden)),
+        n_in=steps + 6,
+        **part,
+    )(*relayed_rows, *chips, gains, gates, ups, downs)
+    kept = call(expert_kept_kernel, bf16(steps, slots, feats), n_in=2, **part)(activated, downs)
+    chip_blocks = from_chips(attended)
+    blocks = [attended, *chip_blocks, *(from_sibling(b) for b in (attended, *chip_blocks))]
     resid = call(
         functools.partial(project_kernel, steps),
         bf16(feats, toks),
         n_in=cuts + 2,
         flops=2 * toks * w_out.size,
         moved=2 * w_out.size,
-    )(*mine, *theirs, w_t, residual_t)
-
-    kept, given = call(
-        functools.partial(expert_kernel, steps),
-        (bf16(steps, slots, feats),) * 2,
-        n_in=cuts + 4,
-        scratch=[
-            pltpu.VMEM((cuts, slots, feats), jnp.bfloat16),
-            pltpu.VMEM((slots, width), jnp.bfloat16),
-        ],
-        flops=6 * slots * w_gate.size,
-        moved=6 * w_gate.size,
-    )(*expert_mine, *expert_theirs, norm_gain, w_gate[0].T, w_up[0].T, w_down[0])
+    )(*blocks, w_t, residual_t)
+
     sums = call(add_cores_kernel, (bf16(slots // 2, feats),) * (2 * steps), n_in=2)(
         kept, swap(given, "cuts", 1)
     )

time: 49.7 us -> 45 us (0.905)
  waiting for transfers between devices: 20.9 us -> 11.9 us
  Pallas kernels: 8.91 us -> 12.6 us
  starting transfers between devices: 18.7 us -> 19.3 us
    ppermute x18, waiting for transfers between devices: 18.8 us -> 9.74 us  [swap(): lax.ppermute(block, axis, [(i, i ^ mask) for i in range(lax.axis_size(axi...]
    pallas_call x2 -> x6, Pallas kernels: 2.07 us -> 5.83 us  [the longest x1 3.53 us: shards(): call(weights_kernel, (*(bf16(cuts, hidden, feats),) * 3, jax.ShapeDtypeSt...]
    ppermute x18, starting transfers between devices: 15.7 us -> 16.3 us  [swap(): lax.ppermute(block, axis, [(i, i ^ mask) for i in range(lax.axis_size(axi...]
  transfers between devices with their start and end apart: 19 -> 19, of which waited for: 12 -> 9; matrix products, arithmetic and copies ran while one was open for 0% -> 0% of each run, Pallas kernels for 13% -> 23%
where the time goes in v6:
time: 45 us; the launch traced here: 44.8 us
  starting transfers between devices  19.3 us (43%)
  Pallas kernels  12.6 us (28%)
  waiting for transfers between devices  11.9 us (26%)
  local copies, waits for them, and re-layouts  0.85 us (2%)
    ppermute x18, starting transfers between devices, swap(): lax.ppermute(block, axis, [(i, i ^ mask) for i in range(lax.axis_size(axi...  16.3 us
    ppermute x18, waiting for transfers between devices, swap(): lax.ppermute(block, axis, [(i, i ^ mask) for i in range(lax.axis_size(axi...  9.74 us
    pallas_call x1, Pallas kernels, shards(): call(weights_kernel, (*(bf16(cuts, hidden, feats),) * 3, jax.ShapeDtypeSt...  3.53 us
    ppermute x1, starting transfers between devices, shards(): rim = lax.ppermute(tail, 'seq', [(i, (i + 1) % size) for i in range(size)])  3.02 us
    pallas_call x1, Pallas kernels, shards(): call(functools.partial(first_kernel, live), (*(bf16(*a.shape) for a in lo...  2.15 us
    ppermute x1, waiting for transfers between devices, shards(): rim = lax.ppermute(tail, 'seq', [(i, (i + 1) % size) for i in range(size)])  2.11 us
    pallas_call x1, Pallas kernels, shards(): call(second_kernel, (bf16(head_rows, toks), bf16(slots, head_rows)), n_in...  1.18 us
    pallas_call x1, Pallas kernels, shards(): call(functools.partial(combine_kernel, live), bf16(feats, toks), n_in=liv...  1.14 us
  transfers between devices with their start and end apart: 19, of which 9 were waited for; matrix products, arithmetic and copies ran while one was open for 0% of the time, Pallas kernels for 23%

profile of v6, /device:TPU:0, one launch (start us, length us, event | category | flops | bytes accessed | tf_op | source)
XLA Modules:
  0.0 44.8 jit_solution(13157070576042319558)
XLA Ops:
  0.0 0.8 %slice.3 = bf16[128,256]{1,0:T(8,128)(2,1)S(1)} slice(bf16[256,256]{1,0:T(8,128)(2,1)} %refs_4_.1), slice={[128:256], [0:256]} | slice | bytes 131072 | tf_op jit(solution)/shard_map/slice | solution.py:333
  0.8 3.0 %collective-permute-start = (bf16[128,256]{1,0:T(8,128)(2,1)S(1)}, bf16[128,256]{1,0:T(8,128)(2,1)S(1)}, u32[]{:S(2)}, u32[]{:S(2)}) collective-permute-start(bf16[128,256]{1,0:T(8,128)(2,1)S(1)} %slice.3), channel_id=1, source_target_pairs={{0,4},{4,8},{8,12},{12,0},{1,5},{5,9},{9,13},{13,1},{2,6},{6,10},{... | collective-permute-start | bytes 196616 | tf_op jit(solution)/shard_map/ppermute | solution.py:334
  3.9 2.1 %shard_map.118 = (bf16[256,512]{1,0:T(8,128)(2,1)S(1)}, bf16[256,256]{1,0:T(8,128)(2,1)S(1)}, bf16[128,256]{1,0:T(8,128)(2,1)S(1)}, bf16[720,2048]{1,0:T(8,128)(...) custom-call(s32[4,256]{1,0:T(4,128)} %bitcast.17, ...), custom_call_target="tpu_custom_call" | custom-call | flops 134217728 | bytes 3579904 | tf_op jit(solution)/shard_map/pallas_call | solution.py:336
  6.0 2.1 %collective-permute-done.rim_ref = bf16[128,256]{1,0:T(8,128)(2,1)S(1)} collective-permute-done((bf16[128,256]{1,0:T(8,128)(2,1)S(1)}, bf16[128,256]{1,0:T(8,128)(2,1)S(1)}, u32[]{:S(2)}, u32[]{:S(2)}) %collective-permute-start) | collective-permute-done | bytes 65568 | tf_op jit(solution)/shard_map/ppermute | solution.py:334
  8.1 1.2 %shard_map.119 = (bf16[512,256]{1,0:T(8,128)(2,1)S(1)}, bf16[64,512]{1,0:T(8,128)(2,1)S(1)}) custom-call(bf16[256,512]{1,0:T(8,128)(2,1)S(1)} %get-tuple-element.50.q_ref, bf16[256,256]{1,0:T(8,128)(2,1)S(1)} %get-tuple-element.51.kv_ref, bf16[128,256]{1,0:T(8,128)(2,1)S(1)} %get-tuple-element.52.before_ref, ...), custom_call_target="tpu_custom_call" | custom-call | flops 67108864 | bytes 262144 | tf_op jit(solution)/shard_map/pallas_call | solution.py:355
  9.3 0.1 collective-permute-start.2
  9.4 1.8 %collective-permute-start.1 = (bf16[64,512]{1,0:T(8,128)(2,1)S(1)}, bf16[64,512]{1,0:T(8,128)(2,1)S(1)}, u32[]{:S(2)}, u32[]{:S(2)}) collective-permute-start(bf16[64,512]{1,0:T(8,128)(2,1)S(1)} %get-tuple-element.56.mine_ref), channel_id=1, source_target_pairs={{0,2},{1,3},{2,0},{3,1},{4,6},{5,7},{6,4},{7,5},{8,10},{9,11},{10,... | collective-permute-start | bytes 196616 | tf_op jit(solution)/shard_map/ppermute | solution.py:293
  11.2 0.3 collective-permute-start.16
  11.5 0.0 collective-permute-done.2.theirs_ref
  11.5 0.6 %shard_map.120.refs_1_ = f32[64,720]{1,0:T(8,128)S(1)} custom-call(bf16[64,512]{1,0:T(8,128)(2,1)S(1)} %get-tuple-element.56.mine_ref, bf16[64,512]{1,0:T(8,128)(2,1)S(1)} %collective-permute-done.2.theirs_ref, bf16[720,2048]{1,0:T(8,128)(2,1)S(1)} %get-tuple-element.57.w_ref.refs_2_.refs_4_, bf16[720,256]{1,0:T(8,128)(2,1)S(1)} %get-tuple-element.58.residual_ref.refs_5_, ...), custom_call_target="tpu_custom_call" | custom-call | flops 47185920 | bytes 737280 | tf_op jit(solution)/shard_map/pallas_call | solution.py:367
  12.1 1.8 %collective-permute-done.1.refs_0_ = bf16[64,512]{1,0:T(8,128)(2,1)S(1)} collective-permute-done((bf16[64,512]{1,0:T(8,128)(2,1)S(1)}, bf16[64,512]{1,0:T(8,128)(2,1)S(1)}, u32[]{:S(2)}, u32[]{:S(2)}) %collective-permute-start.1) | collective-permute-done | bytes 65568 | tf_op jit(solution)/shard_map/ppermute | solution.py:293
  13.9 0.0 collective-permute-start.3
  13.9 0.3 shard_map.121.refs_1_
  14.3 0.0 copy-start
  14.3 0.9 %collective-permute-done.3.refs_0_ = bf16[64,512]{1,0:T(8,128)(2,1)S(1)} collective-permute-done((bf16[64,512]{1,0:T(8,128)(2,1)S(1)}, bf16[64,512]{1,0:T(8,128)(2,1)S(1)}, u32[]{:S(2)}, u32[]{:S(2)}) %collective-permute-start.3) | collective-permute-done | bytes 65568 | tf_op jit(solution)/shard_map/ppermute | solution.py:293
  15.2 0.4 shard_map.122
  15.5 2.3 %collective-permute-start.4 = (bf16[16,720]{1,0:T(8,128)(2,1)S(1)}, bf16[16,720]{1,0:T(8,128)(2,1)S(1)}, u32[]{:S(2)}, u32[]{:S(2)}) collective-permute-start(bf16[16,720]{1,0:T(8,128)(2,1)S(1)} %get-tuple-element.60), channel_id=1, source_target_pairs={{0,12},{4,8},{8,4},{12,0},{1,13},{5,9},{9,5},{13,1},{2,14},{6,10},... | collective-permute-start | bytes 69128 | tf_op jit(solution)/shard_map/ppermute | solution.py:293
  17.8 0.0 collective-permute-start.5
  17.8 2.1 %collective-permute-start.6 = (bf16[16,720]{1,0:T(8,128)(2,1)S(1)}, bf16[16,720]{1,0:T(8,128)(2,1)S(1)}, u32[]{:S(2)}, u32[]{:S(2)}) collective-permute-start(bf16[16,720]{1,0:T(8,128)(2,1)S(1)} %get-tuple-element.62), channel_id=1, source_target_pairs={{0,4},{4,0},{8,12},{12,8},{1,5},{5,1},{9,13},{13,9},{2,6},{6,2},{1... | collective-permute-start | bytes 69128 | tf_op jit(solution)/shard_map/ppermute | solution.py:293
  20.0 3.5 %shard_map.123 = (bf16[4,360,720]{2,1,0:T(8,128)(2,1)S(1)}, bf16[4,360,720]{2,1,0:T(8,128)(2,1)S(1)}, bf16[4,360,720]{2,1,0:T(8,128)(2,1)S(1)}, f32[4,1,720]{2,1,0:T(1,128)S(1)}) custom-call(bf16[360,2880]{1,0:T(8,128)(2,1)} %bitcast.13, bf16[360,2880]{1,0:T(8,128)(2,1)} %bitcast.14, bf16[360,2880]{1,0:T(8,128)(2,1)} %bitcast.15, f32[2880]{0:T(1024)S(1)} %copy-done), custom_call_target="tpu_custom_call" | custom-call | bytes 6220800 | tf_op jit(solution)/shard_map/pallas_call | solution.py:386
  23.5 0.0 collective-permute-done.4.refs_0_
  23.5 0.0 collective-permute-done.5.refs_1_
  23.5 0.0 collective-permute-done.6.refs_2_
  23.6 0.1 collective-permute-start.8
  23.6 2.2 %collective-permute-start.7 = (bf16[64,720]{1,0:T(8,128)(2,1)S(1)}, bf16[64,720]{1,0:T(8,128)(2,1)S(1)}, u32[]{:S(2)}, u32[]{:S(2)}) collective-permute-start(bf16[64,720]{1,0:T(8,128)(2,1)S(1)} %shard_map.124.mine_ref), channel_id=1, source_target_pairs={{0,2},{1,3},{2,0},{3,1},{4,6},{5,7},{6,4},{7,5},{8,10},{9,11},{10,... | collective-permute-start | bytes 276488 | tf_op jit(solution)/shard_map/ppermute | solution.py:293
  25.9 0.8 %shard_map.125 = (f32[64,360]{1,0:T(8,128)S(1)}, f32[64,360]{1,0:T(8,128)S(1)}, f32[64,128]{1,0:T(8,128)S(1)}) custom-call(bf16[64,720]{1,0:T(8,128)(2,1)S(1)} %shard_map.124.mine_ref, bf16[64,720]{1,0:T(8,128)(2,1)S(1)} %collective-permute-done.8.theirs_ref, f32[4,1,720]{2,1,0:T(1,128)S(1)} %get-tuple-element.67.gains_ref.refs_4_, ...), custom_call_target="tpu_custom_call" | custom-call | flops 66355200 | bytes 1036800 | tf_op jit(solution)/shard_map/pallas_call | solution.py:402
  26.7 2.6 %collective-permute-done.7.refs_0_ = bf16[64,720]{1,0:T(8,128)(2,1)S(1)} collective-permute-done((bf16[64,720]{1,0:T(8,128)(2,1)S(1)}, bf16[64,720]{1,0:T(8,128)(2,1)S(1)}, u32[]{:S(2)}, u32[]{:S(2)}) %collective-permute-start.7) | collective-permute-done | bytes 92192 | tf_op jit(solution)/shard_map/ppermute | solution.py:293
  29.3 0.0 collective-permute-start.9
  29.3 0.5 %collective-permute-start.17 = (bf16[512,256]{1,0:T(8,128)(2,1)S(1)}, bf16[512,256]{1,0:T(8,128)(2,1)S(1)}, u32[]{:S(2)}, u32[]{:S(2)}) collective-permute-start(bf16[512,256]{1,0:T(8,128)(2,1)S(1)} %get-tuple-element.94.refs_0_), channel_id=1, source_target_pairs={{0,1},{1,0},{2,3},{3,2},{4,5},{5,4},{6,7},{7,6},{8,9},{9,8},{10,11... | collective-permute-start | bytes 786440 | tf_op jit(solution)/shard_map/ppermute | solution.py:293
  29.8 0.0 collective-permute-start.18
  29.8 0.4 shard_map.126
  30.2 0.3 collective-permute-done.9.refs_0_
  30.6 0.7 %shard_map.127 = (bf16[2,64,720]{2,1,0:T(8,128)(2,1)S(1)}, bf16[64,360]{1,0:T(8,128)(2,1)S(1)}) custom-call(bf16[64,720]{1,0:T(8,128)(2,1)S(1)} %collective-permute-done.9.refs_0_, f32[64,360]{1,0:T(8,128)S(1)} %get-tuple-element.78.refs_1_, f32[64,360]{1,0:T(8,128)S(1)} %get-tuple-element.79.refs_2_, f32[64,128]{1,0:T(8,128)S(1)} %get-tuple-element.80.refs_3_, ...), custom_call_target="tpu_custom_call" | custom-call | flops 66355200 | bytes 1036800 | tf_op jit(solution)/shard_map/pallas_call | solution.py:410
  31.3 0.3 collective-permute-start.10
  31.6 0.3 shard_map.128.kept_ref
  31.9 0.9 %collective-permute-done.10.given_ref = bf16[2,64,720]{2,1,0:T(8,128)(2,1)S(1)} collective-permute-done((bf16[2,64,720]{2,1,0:T(8,128)(2,1)S(1)}, bf16[2,64,720]{2,1,0:T(8,128)(2,1)S(1)}, u32[]{:S(2)}, u32[]{:S(2)}) %collective-permute-start.10) | collective-permute-done | bytes 184352 | tf_op jit(solution)/shard_map/ppermute | solution.py:293
  32.9 1.8 %collective-permute-start.11 = (bf16[32,720]{1,0:T(8,128)(2,1)S(1)}, bf16[32,720]{1,0:T(8,128)(2,1)S(1)}, u32[]{:S(2)}, u32[]{:S(2)}) collective-permute-start(bf16[32,720]{1,0:T(8,128)(2,1)S(1)} %get-tuple-element.85), channel_id=1, source_target_pairs={{0,2},{1,3},{2,0},{3,1},{4,6},{5,7},{6,4},{7,5},{8,10},{9,11},{10,... | collective-permute-start | bytes 138248 | tf_op jit(solution)/shard_map/ppermute | solution.py:293
  34.7 0.3 collective-permute-start.14
  35.0 2.1 %collective-permute-done.11.refs_1_ = bf16[32,720]{1,0:T(8,128)(2,1)S(1)} collective-permute-done((bf16[32,720]{1,0:T(8,128)(2,1)S(1)}, bf16[32,720]{1,0:T(8,128)(2,1)S(1)}, u32[]{:S(2)}, u32[]{:S(2)}) %collective-permute-start.11) | collective-permute-done | bytes 46112 | tf_op jit(solution)/shard_map/ppermute | solution.py:293
  37.0 1.9 %collective-permute-start.12 = (bf16[16,720]{1,0:T(8,128)(2,1)S(1)}, bf16[16,720]{1,0:T(8,128)(2,1)S(1)}, u32[]{:S(2)}, u32[]{:S(2)}) collective-permute-start(bf16[16,720]{1,0:T(8,128)(2,1)S(1)} %get-tuple-element.86), channel_id=1, source_target_pairs={{0,12},{4,8},{8,4},{12,0},{1,13},{5,9},{9,5},{13,1},{2,14},{6,10},... | collective-permute-start | bytes 69128 | tf_op jit(solution)/shard_map/ppermute | solution.py:293
  38.9 0.0 collective-permute-start.13
  39.0 0.0 collective-permute-done.14.refs_1_
  39.0 2.6 %collective-permute-start.15 = (bf16[16,720]{1,0:T(8,128)(2,1)S(1)}, bf16[16,720]{1,0:T(8,128)(2,1)S(1)}, u32[]{:S(2)}, u32[]{:S(2)}) collective-permute-start(bf16[16,720]{1,0:T(8,128)(2,1)S(1)} %get-tuple-element.90), channel_id=1, source_target_pairs={{0,4},{4,0},{8,12},{12,8},{1,5},{5,1},{9,13},{13,9},{2,6},{6,2},{1... | collective-permute-start | bytes 69128 | tf_op jit(solution)/shard_map/ppermute | solution.py:293
  41.6 0.9 %shard_map.132.refs_6_ = bf16[720,256]{1,0:T(8,128)(2,1)S(1)} custom-call(bf16[512,256]{1,0:T(8,128)(2,1)S(1)} %get-tuple-element.94.refs_0_, bf16[512,256]{1,0:T(8,128)(2,1)S(1)} %collective-permute-done.16.refs_1_, bf16[512,256]{1,0:T(8,128)(2,1)S(1)} %collective-permute-done.17.refs_2_, bf16[512,256]{1,0:T(8,128)(2,1)S(1)} %collective-permute-done.18.refs_3_, ...), custom_call_target="tpu_custom_call" | custom-call | flops 754974720 | bytes 2949120 | tf_op jit(solution)/shard_map/pallas_call | solution.py:419
  42.5 0.5 %collective-permute-done.12.refs_0_ = bf16[16,720]{1,0:T(8,128)(2,1)S(1)} collective-permute-done((bf16[16,720]{1,0:T(8,128)(2,1)S(1)}, bf16[16,720]{1,0:T(8,128)(2,1)S(1)}, u32[]{:S(2)}, u32[]{:S(2)}) %collective-permute-start.12) | collective-permute-done | bytes 23072 | tf_op jit(solution)/shard_map/ppermute | solution.py:293
  43.0 0.7 %collective-permute-done.13.refs_1_ = bf16[16,720]{1,0:T(8,128)(2,1)S(1)} collective-permute-done((bf16[16,720]{1,0:T(8,128)(2,1)S(1)}, bf16[16,720]{1,0:T(8,128)(2,1)S(1)}, u32[]{:S(2)}, u32[]{:S(2)}) %collective-permute-start.13) | collective-permute-done | bytes 23072 | tf_op jit(solution)/shard_map/ppermute | solution.py:293
  43.7 0.0 collective-permute-done.15.refs_2_
  43.7 1.1 %shard_map.133 = bf16[720,256]{1,0:T(8,128)(2,1)} custom-call(bf16[16,720]{1,0:T(8,128)(2,1)S(1)} %collective-permute-done.12.refs_0_, bf16[16,720]{1,0:T(8,128)(2,1)S(1)} %collective-permute-done.13.refs_1_, bf16[16,720]{1,0:T(8,128)(2,1)S(1)} %collective-permute-done.15.refs_2_, bf16[16,720]{1,0:T(8,128)(2,1)S(1)} %get-tuple-element.91.refs_3_, ...), custom_call_target="tpu_custom_call" | custom-call | tf_op jit(solution)/shard_map/pallas_call | solution.py:439
  (9 shorter events, 0.1 us)
Async XLA Ops:
  0.8 7.3 %collective-permute-start = (bf16[128,256]{1,0:T(8,128)(2,1)S(1)}, bf16[128,256]{1,0:T(8,128)(2,1)S(1)}, u32[]{:S(2)}, u32[]{:S(2)}) collective-permute-start(bf16[128,256]{1,0:T(8,128)(2,1)S(1)} %slice.3), channel_id=1, source_target_pairs={{0,4},{4,8},{8,12},{12,0},{1,5},{5,9},{9,13},{13,1},{2,6},{6,10},{... | collective-permute-start | bytes 196616 | tf_op jit(solution)/shard_map/ppermute | solution.py:334
  9.3 2.2 %collective-permute-start.2 = (bf16[64,512]{1,0:T(8,128)(2,1)S(1)}, bf16[64,512]{1,0:T(8,128)(2,1)S(1)}, u32[]{:S(2)}, u32[]{:S(2)}) collective-permute-start(bf16[64,512]{1,0:T(8,128)(2,1)S(1)} %get-tuple-element.56.mine_ref), channel_id=1, source_target_pairs={{0,1},{1,0},{2,3},{3,2},{4,5},{5,4},{6,7},{7,6},{8,9},{9,8},{10,11... | collective-permute-start | bytes 196616 | tf_op jit(solution)/shard_map/ppermute | solution.py:293
  9.4 4.5 %collective-permute-start.1 = (bf16[64,512]{1,0:T(8,128)(2,1)S(1)}, bf16[64,512]{1,0:T(8,128)(2,1)S(1)}, u32[]{:S(2)}, u32[]{:S(2)}) collective-permute-start(bf16[64,512]{1,0:T(8,128)(2,1)S(1)} %get-tuple-element.56.mine_ref), channel_id=1, source_target_pairs={{0,2},{1,3},{2,0},{3,1},{4,6},{5,7},{6,4},{7,5},{8,10},{9,11},{10,... | collective-permute-start | bytes 196616 | tf_op jit(solution)/shard_map/ppermute | solution.py:293
  11.2 18.6 %collective-permute-start.16 = (bf16[512,256]{1,0:T(8,128)(2,1)S(1)}, bf16[512,256]{1,0:T(8,128)(2,1)S(1)}, u32[]{:S(2)}, u32[]{:S(2)}) collective-permute-start(bf16[512,256]{1,0:T(8,128)(2,1)S(1)} %get-tuple-element.94.refs_0_), channel_id=1, source_target_pairs={{0,2},{1,3},{2,0},{3,1},{4,6},{5,7},{6,4},{7,5},{8,10},{9,11},{10,... | collective-permute-start | bytes 786440 | tf_op jit(solution)/shard_map/ppermute | solution.py:293
  13.9 1.3 %collective-permute-start.3 = (bf16[64,512]{1,0:T(8,128)(2,1)S(1)}, bf16[64,512]{1,0:T(8,128)(2,1)S(1)}, u32[]{:S(2)}, u32[]{:S(2)}) collective-permute-start(bf16[64,512]{1,0:T(8,128)(2,1)S(1)} %collective-permute-done.1.refs_0_), channel_id=1, source_target_pairs={{0,1},{1,0},{2,3},{3,2},{4,5},{5,4},{6,7},{7,6},{8,9},{9,8},{10,11... | collective-permute-start | bytes 196616 | tf_op jit(solution)/shard_map/ppermute | solution.py:293
  14.3 5.7 %copy-start = (f32[2880]{0:T(1024)S(1)}, f32[2880]{0:T(1024)}, u32[]{:S(2)}) copy-start(f32[2880]{0:T(1024)} %gain_ref.1) | copy-start | bytes 34564
  15.5 8.0 %collective-permute-start.4 = (bf16[16,720]{1,0:T(8,128)(2,1)S(1)}, bf16[16,720]{1,0:T(8,128)(2,1)S(1)}, u32[]{:S(2)}, u32[]{:S(2)}) collective-permute-start(bf16[16,720]{1,0:T(8,128)(2,1)S(1)} %get-tuple-element.60), channel_id=1, source_target_pairs={{0,12},{4,8},{8,4},{12,0},{1,13},{5,9},{9,5},{13,1},{2,14},{6,10},... | collective-permute-start | bytes 69128 | tf_op jit(solution)/shard_map/ppermute | solution.py:293
  17.8 5.7 %collective-permute-start.5 = (bf16[16,720]{1,0:T(8,128)(2,1)S(1)}, bf16[16,720]{1,0:T(8,128)(2,1)S(1)}, u32[]{:S(2)}, u32[]{:S(2)}) collective-permute-start(bf16[16,720]{1,0:T(8,128)(2,1)S(1)} %get-tuple-element.61), channel_id=1, source_target_pairs={{0,8},{4,12},{8,0},{12,4},{1,9},{5,13},{9,1},{13,5},{2,10},{6,14},... | collective-permute-start | bytes 69128 | tf_op jit(solution)/shard_map/ppermute | solution.py:293
  17.8 5.7 %collective-permute-start.6 = (bf16[16,720]{1,0:T(8,128)(2,1)S(1)}, bf16[16,720]{1,0:T(8,128)(2,1)S(1)}, u32[]{:S(2)}, u32[]{:S(2)}) collective-permute-start(bf16[16,720]{1,0:T(8,128)(2,1)S(1)} %get-tuple-element.62), channel_id=1, source_target_pairs={{0,4},{4,0},{8,12},{12,8},{1,5},{5,1},{9,13},{13,9},{2,6},{6,2},{1... | collective-permute-start | bytes 69128 | tf_op jit(solution)/shard_map/ppermute | solution.py:293
  23.6 2.3 %collective-permute-start.8 = (bf16[64,720]{1,0:T(8,128)(2,1)S(1)}, bf16[64,720]{1,0:T(8,128)(2,1)S(1)}, u32[]{:S(2)}, u32[]{:S(2)}) collective-permute-start(bf16[64,720]{1,0:T(8,128)(2,1)S(1)} %shard_map.124.mine_ref), channel_id=1, source_target_pairs={{0,1},{1,0},{2,3},{3,2},{4,5},{5,4},{6,7},{7,6},{8,9},{9,8},{10,11... | collective-permute-start | bytes 276488 | tf_op jit(solution)/shard_map/ppermute | solution.py:293
  23.6 5.6 %collective-permute-start.7 = (bf16[64,720]{1,0:T(8,128)(2,1)S(1)}, bf16[64,720]{1,0:T(8,128)(2,1)S(1)}, u32[]{:S(2)}, u32[]{:S(2)}) collective-permute-start(bf16[64,720]{1,0:T(8,128)(2,1)S(1)} %shard_map.124.mine_ref), channel_id=1, source_target_pairs={{0,2},{1,3},{2,0},{3,1},{4,6},{5,7},{6,4},{7,5},{8,10},{9,11},{10,... | collective-permute-start | bytes 276488 | tf_op jit(solution)/shard_map/ppermute | solution.py:293
  29.3 1.3 %collective-permute-start.9 = (bf16[64,720]{1,0:T(8,128)(2,1)S(1)}, bf16[64,720]{1,0:T(8,128)(2,1)S(1)}, u32[]{:S(2)}, u32[]{:S(2)}) collective-permute-start(bf16[64,720]{1,0:T(8,128)(2,1)S(1)} %collective-permute-done.7.refs_0_), channel_id=1, source_target_pairs={{0,1},{1,0},{2,3},{3,2},{4,5},{5,4},{6,7},{7,6},{8,9},{9,8},{10,11... | collective-permute-start | bytes 276488 | tf_op jit(solution)/shard_map/ppermute | solution.py:293
  29.3 12.3 %collective-permute-start.17 = (bf16[512,256]{1,0:T(8,128)(2,1)S(1)}, bf16[512,256]{1,0:T(8,128)(2,1)S(1)}, u32[]{:S(2)}, u32[]{:S(2)}) collective-permute-start(bf16[512,256]{1,0:T(8,128)(2,1)S(1)} %get-tuple-element.94.refs_0_), channel_id=1, source_target_pairs={{0,1},{1,0},{2,3},{3,2},{4,5},{5,4},{6,7},{7,6},{8,9},{9,8},{10,11... | collective-permute-start | bytes 786440 | tf_op jit(solution)/shard_map/ppermute | solution.py:293
  29.8 11.8 %collective-permute-start.18 = (bf16[512,256]{1,0:T(8,128)(2,1)S(1)}, bf16[512,256]{1,0:T(8,128)(2,1)S(1)}, u32[]{:S(2)}, u32[]{:S(2)}) collective-permute-start(bf16[512,256]{1,0:T(8,128)(2,1)S(1)} %collective-permute-done.16.refs_1_), channel_id=1, source_target_pairs={{0,1},{1,0},{2,3},{3,2},{4,5},{5,4},{6,7},{7,6},{8,9},{9,8},{10,11... | collective-permute-start | bytes 786440 | tf_op jit(solution)/shard_map/ppermute | solution.py:293
  31.3 1.5 %collective-permute-start.10 = (bf16[2,64,720]{2,1,0:T(8,128)(2,1)S(1)}, bf16[2,64,720]{2,1,0:T(8,128)(2,1)S(1)}, u32[]{:S(2)}, u32[]{:S(2)}) collective-permute-start(bf16[2,64,720]{2,1,0:T(8,128)(2,1)S(1)} %get-tuple-element.83), channel_id=1, source_target_pairs={{0,1},{1,0},{2,3},{3,2},{4,5},{5,4},{6,7},{7,6},{8,9},{9,8},{10,11... | collective-permute-start | bytes 552968 | tf_op jit(solution)/shard_map/ppermute | solution.py:293
  32.9 4.2 %collective-permute-start.11 = (bf16[32,720]{1,0:T(8,128)(2,1)S(1)}, bf16[32,720]{1,0:T(8,128)(2,1)S(1)}, u32[]{:S(2)}, u32[]{:S(2)}) collective-permute-start(bf16[32,720]{1,0:T(8,128)(2,1)S(1)} %get-tuple-element.85), channel_id=1, source_target_pairs={{0,2},{1,3},{2,0},{3,1},{4,6},{5,7},{6,4},{7,5},{8,10},{9,11},{10,... | collective-permute-start | bytes 138248 | tf_op jit(solution)/shard_map/ppermute | solution.py:293
  34.7 4.3 %collective-permute-start.14 = (bf16[32,720]{1,0:T(8,128)(2,1)S(1)}, bf16[32,720]{1,0:T(8,128)(2,1)S(1)}, u32[]{:S(2)}, u32[]{:S(2)}) collective-permute-start(bf16[32,720]{1,0:T(8,128)(2,1)S(1)} %get-tuple-element.89), channel_id=1, source_target_pairs={{0,2},{1,3},{2,0},{3,1},{4,6},{5,7},{6,4},{7,5},{8,10},{9,11},{10,... | collective-permute-start | bytes 138248 | tf_op jit(solution)/shard_map/ppermute | solution.py:293
  37.0 5.9 %collective-permute-start.12 = (bf16[16,720]{1,0:T(8,128)(2,1)S(1)}, bf16[16,720]{1,0:T(8,128)(2,1)S(1)}, u32[]{:S(2)}, u32[]{:S(2)}) collective-permute-start(bf16[16,720]{1,0:T(8,128)(2,1)S(1)} %get-tuple-element.86), channel_id=1, source_target_pairs={{0,12},{4,8},{8,4},{12,0},{1,13},{5,9},{9,5},{13,1},{2,14},{6,10},... | collective-permute-start | bytes 69128 | tf_op jit(solution)/shard_map/ppermute | solution.py:293
  38.9 4.7 %collective-permute-start.13 = (bf16[16,720]{1,0:T(8,128)(2,1)S(1)}, bf16[16,720]{1,0:T(8,128)(2,1)S(1)}, u32[]{:S(2)}, u32[]{:S(2)}) collective-permute-start(bf16[16,720]{1,0:T(8,128)(2,1)S(1)} %get-tuple-element.87), channel_id=1, source_target_pairs={{0,8},{4,12},{8,0},{12,4},{1,9},{5,13},{9,1},{13,5},{2,10},{6,14},... | collective-permute-start | bytes 69128 | tf_op jit(solution)/shard_map/ppermute | solution.py:293
  39.0 4.7 %collective-permute-start.15 = (bf16[16,720]{1,0:T(8,128)(2,1)S(1)}, bf16[16,720]{1,0:T(8,128)(2,1)S(1)}, u32[]{:S(2)}, u32[]{:S(2)}) collective-permute-start(bf16[16,720]{1,0:T(8,128)(2,1)S(1)} %get-tuple-element.90), channel_id=1, source_target_pairs={{0,4},{4,0},{8,12},{12,8},{1,5},{5,1},{9,13},{13,9},{2,6},{6,2},{1... | collective-permute-start | bytes 69128 | tf_op jit(solution)/shard_map/ppermute | solution.py:293

commit v7 on v6

--- a/solution.py
+++ b/solution.py
@@ -154,30 +154,29 @@
     return lax.bitwise_xor(me, CORES * k + (1 if sibling else 0))
 
 
-def add_products(total, first, blocks, w_ref, steps, dims, swapped=False):
+def add_products(total, places, blocks, w_ref, steps, dims, swapped=False):
     width = blocks[0].shape[0 if swapped else 1] if blocks else 0
-    for i, block in enumerate(blocks, first):
+    for i, block in zip(places, blocks):
         at = pl.multiple_of(origin(i % steps, i >= steps) * width, 128)
         w = w_ref[:, pl.ds(at, width)]
         total += dot(w, block[...], dims) if swapped else dot(block[...], w, dims)
     return total
 
 
-def rows_near_kernel(steps, mine_ref, theirs_ref, w_ref, residual_ref, placing_ref, total_ref):
+def rows_own_kernel(steps, rows_ref, w_ref, residual_ref, placing_ref, total_ref):
     total = dot(placing_ref[...], residual_ref[...], NT)
-    total = add_products(total, 0, [mine_ref], w_ref, steps, NT)
-    total_ref[...] = add_products(total, steps, [theirs_ref], w_ref, steps, NT)
-
-
-def rows_chips_kernel(steps, *refs):
-    blocks, (before_ref, w_ref, total_ref) = refs[: steps - 1], refs[steps - 1 :]
-    total_ref[...] = add_products(before_ref[...], 1, blocks, w_ref, steps, NT)
+    total_ref[...] = add_products(total, [0], [rows_ref], w_ref, steps, NT)
+
+
+def rows_more_kernel(places, steps, *refs):
+    blocks, (before_ref, w_ref, total_ref) = refs[:-3], refs[-3:]
+    total_ref[...] = add_products(before_ref[...], places, blocks, w_ref, steps, NT)
 
 
 def rows_last_kernel(steps, *refs):
     blocks, (before_ref, w_ref) = refs[: steps - 1], refs[steps - 1 : steps + 1]
     outgoing, rows_ref = refs[steps + 1 : -1], refs[-1]
-    total = add_products(before_ref[...], steps + 1, blocks, w_ref, steps, NT)
+    total = add_products(before_ref[...], range(steps + 1, 2 * steps), blocks, w_ref, steps, NT)
     rows_ref[...] = total.astype(jnp.bfloat16).reshape(rows_ref.shape)
     me = lax.axis_index("seq")
     for k, out_ref in enumerate(outgoing):
@@ -192,31 +191,27 @@
 def project_kernel(steps, *refs):
     blocks = refs[: 2 * steps]
     w_ref, residual_ref, resid_ref = refs[2 * steps :]
-    total = add_products(residual_ref[...].astype(jnp.float32), 0, blocks, w_ref, steps, NN, True)
+    total = residual_ref[...].astype(jnp.float32)
+    total = add_products(total, range(2 * steps), blocks, w_ref, steps, NN, True)
     resid_ref[...] = total.astype(jnp.bfloat16)
 
 
-def weights_kernel(gate_ref, up_ref, down_ref, gain_ref, gates_ref, ups_ref, downs_ref, gains_ref, *scratch):
-    held, sems = scratch[:3], scratch[3]
-    copies = [
-        pltpu.make_async_copy(source, target, sems.at[i])
-        for i, (source, target) in enumerate(zip((gate_ref, up_ref, down_ref), held))
-    ]
-    for copy in copies:
-        copy.start()
-    cuts, _, width = gates_ref.shape
+def spread_kernel(source_ref, blocks_ref):
+    cuts, _, width = blocks_ref.shape
+    for p in range(cuts):
+        blocks_ref[p] = source_ref[:, p * width : (p + 1) * width]
+
+
+def spread_gain_kernel(gain_ref, blocks_ref):
+    cuts, _, width = blocks_ref.shape
     gain = gain_ref[...].reshape(1, cuts * width)
     for p in range(cuts):
-        gains_ref[p] = gain[:, p * width : (p + 1) * width]
-    for copy, source, target in zip(copies, held, (gates_ref, ups_ref, downs_ref)):
-        copy.wait()
-        for p in range(cuts):
-            target[p] = source[:, p * width : (p + 1) * width]
-
-
-def add_features(sums, first, blocks, gains_ref, gates_ref, ups_ref, steps):
+        blocks_ref[p] = gain[:, p * width : (p + 1) * width]
+
+
+def add_features(sums, places, blocks, gains_ref, gates_ref, ups_ref, steps):
     gate, up, squares = sums
-    for i, block in enumerate(blocks, first):
+    for i, block in zip(places, blocks):
         p = origin(i % steps, i >= steps)
         wide = block[...].astype(jnp.float32)
         squares += jnp.sum(wide * wide, axis=1, keepdims=True)
@@ -231,25 +226,24 @@
         ref[...] = jnp.broadcast_to(value, ref.shape)
 
 
-def expert_near_kernel(steps, mine_ref, theirs_ref, gains_ref, gates_ref, ups_ref, *out_refs):
+def expert_own_kernel(steps, block_ref, gains_ref, gates_ref, ups_ref, *out_refs):
     zeros = jnp.zeros(out_refs[0].shape, jnp.float32)
     sums = (zeros, zeros, jnp.zeros((zeros.shape[0], 1), jnp.float32))
-    for first, block in ((0, mine_ref), (steps, theirs_ref)):
-        sums = add_features(sums, first, [block], gains_ref, gates_ref, ups_ref, steps)
-    store_sums(sums, out_refs)
-
-
-def expert_chips_kernel(steps, *refs):
-    blocks, refs = refs[: steps - 1], refs[steps - 1 :]
+    store_sums(add_features(sums, [0], [block_ref], gains_ref, gates_ref, ups_ref, steps), out_refs)
+
+
+def expert_more_kernel(places, steps, *refs):
+    blocks, refs = refs[:-9], refs[-9:]
     sums = (refs[0][...], refs[1][...], refs[2][:, :1])
-    store_sums(add_features(sums, 1, blocks, *refs[3:6], steps), refs[6:])
+    store_sums(add_features(sums, places, blocks, *refs[3:6], steps), refs[6:])
 
 
 def expert_last_kernel(steps, *refs):
     blocks, refs = refs[: steps - 1], refs[steps - 1 :]
     sums = (refs[0][...], refs[1][...], refs[2][:, :1])
     gains_ref, gates_ref, ups_ref, downs_ref, given_ref, activated_ref = refs[3:]
-    gate, up, squares = add_features(sums, steps + 1, blocks, gains_ref, gates_ref, ups_ref, steps)
+    places = range(steps + 1, 2 * steps)
+    gate, up, squares = add_features(sums, places, blocks, gains_ref, gates_ref, ups_ref, steps)
     cuts, _, width = gates_ref.shape
     scale = lax.rsqrt(squares / (cuts * width) + norm_eps)
     gate, up = gate * scale, up * scale
@@ -361,16 +355,21 @@
     )(q, kv, before, rim, sinks, late, placing)
 
     chip_rows = from_chips(rows)
-    sibling_rows = from_sibling(rows)
     total = jax.ShapeDtypeStruct((slots, feats), jnp.float32)
     part = dict(flops=slots * w_out.size // 2, moved=w_out.size // 2)
-    near = call(functools.partial(rows_near_kernel, steps), total, n_in=5, **part)(
-        rows, sibling_rows, w_t, residual_t, placing
-    )
-    chip_rows = after(chip_rows, near)
+    own = call(functools.partial(rows_own_kernel, steps), total, n_in=4, **part)(
+        rows, w_t, residual_t, placing
+    )
+    sibling_rows = from_sibling(rows)
+    places = [steps, *range(1, steps)]
+    spread = functools.partial(
+        call, spread_kernel, bf16(cuts, hidden, feats), n_in=1, moved=4 * w_gate.size
+    )
+    gates = spread()(after(w_gate[0].T, rows))
+    chip_rows = after(chip_rows, (own, gates))
     relayed_rows = [from_sibling(b) for b in chip_rows]
-    chips = call(functools.partial(rows_chips_kernel, steps), total, n_in=steps + 1, **part)(
-        *chip_rows, near, w_t
+    chips = call(functools.partial(rows_more_kernel, places, steps), total, n_in=steps + 2, **part)(
+        sibling_rows, *chip_rows, own, w_t
     )
     outgoing = call(
         functools.partial(rows_last_kernel, steps),
@@ -382,30 +381,25 @@
 
     arrived = [swap(outgoing[k], "seq", k) for k in range(live - 1, 0, -1)] + [outgoing[0]]
 
-    w_gate_t, w_up_t, w_down_t, _ = lax.optimization_barrier((w_gate[0].T, w_up[0].T, w_down[0], outgoing[0]))
-    weights = call(
-        weights_kernel,
-        (*(bf16(cuts, hidden, feats),) * 3, jax.ShapeDtypeStruct((cuts, 1, feats), jnp.float32)),
-        n_in=4,
-        hbm=range(3),
-        scratch=[*(pltpu.VMEM((hidden, width), jnp.bfloat16),) * 3, pltpu.SemaphoreType.DMA((3,))],
-        moved=6 * w_gate.size,
-    )(in_hbm(w_gate_t), in_hbm(w_up_t), in_hbm(w_down_t), norm_gain)
-    gates, ups, downs, gains = weights
+    ups = spread()(after(w_up[0].T, outgoing[0]))
+    gains = call(spread_gain_kernel, jax.ShapeDtypeStruct((cuts, 1, feats), jnp.float32), n_in=1)(norm_gain)
     sums = (
         *(jax.ShapeDtypeStruct((slots, hidden), jnp.float32),) * 2,
         jax.ShapeDtypeStruct((slots, KEYS_SEEN), jnp.float32),
     )
     part = dict(flops=slots * w_gate.size, moved=w_gate.size)
-    stacked = call(stack_kernel, bf16(slots, feats), n_in=live)(*after(arrived, gains))
+    stacked = call(stack_kernel, bf16(slots, feats), n_in=live)(*after(arrived, (ups, gains)))
     chip_rows = from_chips(stacked)
-    near = call(functools.partial(expert_near_kernel, steps), sums, n_in=5, **part)(
-        stacked, from_sibling(stacked), gains, gates, ups
-    )
-    chip_rows = after(chip_rows, near)
+    own = call(functools.partial(expert_own_kernel, steps), sums, n_in=4, **part)(stacked, gains, gates, ups)
+    sibling_rows = from_sibling(stacked)
+    downs = spread()(after(w_down[0], stacked))
+    chip_blocks = from_chips(after(attended, gates))
+    blocks = [attended, *chip_blocks]
+    blocks += [from_sibling(b) for b in blocks]
+    chip_rows = after(chip_rows, (own, downs))
     relayed_rows = [from_sibling(b) for b in chip_rows]
-    chips = call(functools.partial(expert_chips_kernel, steps), sums, n_in=steps + 5, **part)(
-        *chip_rows, *near, gains, gates, ups
+    chips = call(functools.partial(expert_more_kernel, places, steps), sums, n_in=steps + 6, **part)(
+        sibling_rows, *chip_rows, *own, gains, gates, ups
     )
     given, activated = call(
         functools.partial(expert_last_kernel, steps),
@@ -414,8 +408,6 @@
         **part,
     )(*relayed_rows, *chips, gains, gates, ups, downs)
     kept = call(expert_kept_kernel, bf16(steps, slots, feats), n_in=2, **part)(activated, downs)
-    chip_blocks = from_chips(attended)
-    blocks = [attended, *chip_blocks, *(from_sibling(b) for b in (attended, *chip_blocks))]
     resid = call(
         functools.partial(project_kernel, steps),
         bf16(feats, toks),

time: 45 us -> 43.6 us (0.969)
  Pallas kernels: 12.6 us -> 11.1 us
    pallas_call x6 -> x9, Pallas kernels: 5.76 us -> 4.08 us  [the longest x1 0.77 us: shards(): call(functools.partial(expert_more_kernel, places, steps), sums, n_in=ste...]
    ppermute x18, waiting for transfers between devices: 9.74 us -> 10.3 us  [swap(): lax.ppermute(block, axis, [(i, i ^ mask) for i in range(lax.axis_size(axi...]
  transfers between devices with their start and end apart: 19 -> 19, of which waited for: 9 -> 10; matrix products, arithmetic and copies ran while one was open for 0% -> 0% of each run, Pallas kernels for 23% -> 20%
where the time goes in v7:
time: 43.6 us; the launch traced here: 43.5 us
  starting transfers between devices  19 us (44%)
  waiting for transfers between devices  12.3 us (28%)
  Pallas kernels  11.1 us (25%)
  local copies, waits for them, and re-layouts  0.86 us (2%)
    ppermute x18, starting transfers between devices, swap(): lax.ppermute(block, axis, [(i, i ^ mask) for i in range(lax.axis_size(axi...  16 us
    ppermute x18, waiting for transfers between devices, swap(): lax.ppermute(block, axis, [(i, i ^ mask) for i in range(lax.axis_size(axi...  10.3 us
    ppermute x1, starting transfers between devices, shards(): rim = lax.ppermute(tail, 'seq', [(i, (i + 1) % size) for i in range(size)])  3.02 us
    pallas_call x1, Pallas kernels, shards(): call(functools.partial(first_kernel, live), (*(bf16(*a.shape) for a in lo...  2.3 us
    ppermute x1, waiting for transfers between devices, shards(): rim = lax.ppermute(tail, 'seq', [(i, (i + 1) % size) for i in range(size)])  1.96 us
    pallas_call x1, Pallas kernels, shards(): call(second_kernel, (bf16(head_rows, toks), bf16(slots, head_rows)), n_in...  1.18 us
    pallas_call x1, Pallas kernels, shards(): call(functools.partial(combine_kernel, live), bf16(feats, toks), n_in=liv...  1.14 us
    pallas_call x1, Pallas kernels, shards(): call(functools.partial(project_kernel, steps), bf16(feats, toks), n_in=cu...  0.93 us
  transfers between devices with their start and end apart: 19, of which 10 were waited for; matrix products, arithmetic and copies ran while one was open for 0% of the time, Pallas kernels for 20%

profile of v7, /device:TPU:0, one launch (start us, length us, event | category | flops | bytes accessed | tf_op | source)
XLA Modules:
  0.0 43.5 jit_solution(13419681395813968072)
XLA Ops:
  0.0 0.8 %slice.3 = bf16[128,256]{1,0:T(8,128)(2,1)S(1)} slice(bf16[256,256]{1,0:T(8,128)(2,1)} %refs_4_.1), slice={[128:256], [0:256]} | slice | bytes 131072 | tf_op jit(solution)/shard_map/slice | solution.py:327
  0.8 3.0 %collective-permute-start = (bf16[128,256]{1,0:T(8,128)(2,1)S(1)}, bf16[128,256]{1,0:T(8,128)(2,1)S(1)}, u32[]{:S(2)}, u32[]{:S(2)}) collective-permute-start(bf16[128,256]{1,0:T(8,128)(2,1)S(1)} %slice.3), channel_id=1, source_target_pairs={{0,4},{4,8},{8,12},{12,0},{1,5},{5,9},{9,13},{13,1},{2,6},{6,10},{... | collective-permute-start | bytes 196616 | tf_op jit(solution)/shard_map/ppermute | solution.py:328
  3.9 2.3 %shard_map.118 = (bf16[256,512]{1,0:T(8,128)(2,1)S(1)}, bf16[256,256]{1,0:T(8,128)(2,1)S(1)}, bf16[128,256]{1,0:T(8,128)(2,1)S(1)}, bf16[720,2048]{1,0:T(8,128)(...) custom-call(s32[4,256]{1,0:T(4,128)} %bitcast.17, ...), custom_call_target="tpu_custom_call" | custom-call | flops 134217728 | bytes 3579904 | tf_op jit(solution)/shard_map/pallas_call | solution.py:330
  6.2 2.0 %collective-permute-done.rim_ref = bf16[128,256]{1,0:T(8,128)(2,1)S(1)} collective-permute-done((bf16[128,256]{1,0:T(8,128)(2,1)S(1)}, bf16[128,256]{1,0:T(8,128)(2,1)S(1)}, u32[]{:S(2)}, u32[]{:S(2)}) %collective-permute-start) | collective-permute-done | bytes 65568 | tf_op jit(solution)/shard_map/ppermute | solution.py:328
  8.1 1.2 %shard_map.119 = (bf16[512,256]{1,0:T(8,128)(2,1)S(1)}, bf16[64,512]{1,0:T(8,128)(2,1)S(1)}) custom-call(bf16[256,512]{1,0:T(8,128)(2,1)S(1)} %get-tuple-element.47.q_ref, bf16[256,256]{1,0:T(8,128)(2,1)S(1)} %get-tuple-element.48.kv_ref, bf16[128,256]{1,0:T(8,128)(2,1)S(1)} %get-tuple-element.49.before_ref, ...), custom_call_target="tpu_custom_call" | custom-call | flops 67108864 | bytes 262144 | tf_op jit(solution)/shard_map/pallas_call | solution.py:349
  9.3 1.8 %collective-permute-start.1 = (bf16[64,512]{1,0:T(8,128)(2,1)S(1)}, bf16[64,512]{1,0:T(8,128)(2,1)S(1)}, u32[]{:S(2)}, u32[]{:S(2)}) collective-permute-start(bf16[64,512]{1,0:T(8,128)(2,1)S(1)} %get-tuple-element.53.rows_ref), channel_id=1, source_target_pairs={{0,2},{1,3},{2,0},{3,1},{4,6},{5,7},{6,4},{7,5},{8,10},{9,11},{10,... | collective-permute-start | bytes 196616 | tf_op jit(solution)/shard_map/ppermute | solution.py:287
  11.1 0.6 %shard_map.121.gates_ref.refs_6_.refs_5_ = bf16[4,360,720]{2,1,0:T(8,128)(2,1)S(1)} custom-call(bf16[360,2880]{1,0:T(8,128)(2,1)S(1)} %bitcast.12), custom_call_target="tpu_custom_call" | custom-call | bytes 4147200 | tf_op jit(solution)/shard_map/pallas_call | solution.py:368
  11.7 0.4 collective-permute-start.16
  12.1 0.0 collective-permute-start.3
  12.1 0.4 %shard_map.120.refs_2_ = f32[64,720]{1,0:T(8,128)S(1)} custom-call(bf16[64,512]{1,0:T(8,128)(2,1)S(1)} %get-tuple-element.53.rows_ref, bf16[720,2048]{1,0:T(8,128)(2,1)S(1)} %get-tuple-element.54.w_ref.refs_3_.refs_2_.refs_4_, bf16[720,256]{1,0:T(8,128)(2,1)S(1)} %get-tuple-element.55.residual_ref.refs_5_, bf16[64,256]{1,0:T(8,128)(2,1)S(1)} %get-tuple-element.52.placing_ref), custom_call_target="tpu_custom_call" | custom-call | flops 47185920 | bytes 737280 | tf_op jit(solution)/shard_map/pallas_call | solution.py:360
  12.5 1.8 %collective-permute-done.1.refs_1_ = bf16[64,512]{1,0:T(8,128)(2,1)S(1)} collective-permute-done((bf16[64,512]{1,0:T(8,128)(2,1)S(1)}, bf16[64,512]{1,0:T(8,128)(2,1)S(1)}, u32[]{:S(2)}, u32[]{:S(2)}) %collective-permute-start.1) | collective-permute-done | bytes 65568 | tf_op jit(solution)/shard_map/ppermute | solution.py:287
  14.4 0.6 %shard_map.122.refs_1_ = f32[64,720]{1,0:T(8,128)S(1)} custom-call(bf16[64,512]{1,0:T(8,128)(2,1)S(1)} %collective-permute-done.3.refs_0_, bf16[64,512]{1,0:T(8,128)(2,1)S(1)} %collective-permute-done.1.refs_1_, f32[64,720]{1,0:T(8,128)S(1)} %shard_map.120.refs_2_, bf16[720,2048]{1,0:T(8,128)(2,1)S(1)} %get-tuple-element.54.w_ref.refs_3_.refs_2_.refs_4_), custom_call_target="tpu_custom_call" | custom-call | flops 47185920 | bytes 737280 | tf_op jit(solution)/shard_map/pallas_call | solution.py:371
  14.9 0.0 copy-start.3
  15.0 0.0 copy-start.1
  15.0 0.6 %collective-permute-done.2.refs_0_ = bf16[64,512]{1,0:T(8,128)(2,1)S(1)} collective-permute-done((bf16[64,512]{1,0:T(8,128)(2,1)S(1)}, bf16[64,512]{1,0:T(8,128)(2,1)S(1)}, u32[]{:S(2)}, u32[]{:S(2)}) %collective-permute-start.2) | collective-permute-done | bytes 65568 | tf_op jit(solution)/shard_map/ppermute | solution.py:287
  15.6 0.4 shard_map.123
  16.0 2.0 %collective-permute-start.4 = (bf16[16,720]{1,0:T(8,128)(2,1)S(1)}, bf16[16,720]{1,0:T(8,128)(2,1)S(1)}, u32[]{:S(2)}, u32[]{:S(2)}) collective-permute-start(bf16[16,720]{1,0:T(8,128)(2,1)S(1)} %get-tuple-element.58), channel_id=1, source_target_pairs={{0,12},{4,8},{8,4},{12,0},{1,13},{5,9},{9,5},{13,1},{2,14},{6,10},... | collective-permute-start | bytes 69128 | tf_op jit(solution)/shard_map/ppermute | solution.py:287
  18.0 0.0 collective-permute-start.5
  18.0 2.4 %collective-permute-start.6 = (bf16[16,720]{1,0:T(8,128)(2,1)S(1)}, bf16[16,720]{1,0:T(8,128)(2,1)S(1)}, u32[]{:S(2)}, u32[]{:S(2)}) collective-permute-start(bf16[16,720]{1,0:T(8,128)(2,1)S(1)} %get-tuple-element.60), channel_id=1, source_target_pairs={{0,4},{4,0},{8,12},{12,8},{1,5},{5,1},{9,13},{13,9},{2,6},{6,2},{1... | collective-permute-start | bytes 69128 | tf_op jit(solution)/shard_map/ppermute | solution.py:287
  20.4 0.1 shard_map.125.gains_ref.refs_5_.refs_4_
  20.5 0.6 %shard_map.124.ups_ref.refs_7_.refs_6_ = bf16[4,360,720]{2,1,0:T(8,128)(2,1)S(1)} custom-call(bf16[360,2880]{1,0:T(8,128)(2,1)S(1)} %bitcast.13), custom_call_target="tpu_custom_call" | custom-call | bytes 4147200 | tf_op jit(solution)/shard_map/pallas_call | solution.py:384
  21.1 0.7 %collective-permute-done.4.refs_0_ = bf16[16,720]{1,0:T(8,128)(2,1)S(1)} collective-permute-done((bf16[16,720]{1,0:T(8,128)(2,1)S(1)}, bf16[16,720]{1,0:T(8,128)(2,1)S(1)}, u32[]{:S(2)}, u32[]{:S(2)}) %collective-permute-start.4) | collective-permute-done | bytes 23072 | tf_op jit(solution)/shard_map/ppermute | solution.py:287
  21.8 0.9 %collective-permute-done.5.refs_1_ = bf16[16,720]{1,0:T(8,128)(2,1)S(1)} collective-permute-done((bf16[16,720]{1,0:T(8,128)(2,1)S(1)}, bf16[16,720]{1,0:T(8,128)(2,1)S(1)}, u32[]{:S(2)}, u32[]{:S(2)}) %collective-permute-start.5) | collective-permute-done | bytes 23072 | tf_op jit(solution)/shard_map/ppermute | solution.py:287
  22.7 0.0 collective-permute-done.6.refs_2_
  22.7 1.7 %collective-permute-start.7 = (bf16[64,720]{1,0:T(8,128)(2,1)S(1)}, bf16[64,720]{1,0:T(8,128)(2,1)S(1)}, u32[]{:S(2)}, u32[]{:S(2)}) collective-permute-start(bf16[64,720]{1,0:T(8,128)(2,1)S(1)} %shard_map.126.block_ref), channel_id=1, source_target_pairs={{0,2},{1,3},{2,0},{3,1},{4,6},{5,7},{6,4},{7,5},{8,10},{9,11},{10,... | collective-permute-start | bytes 276488 | tf_op jit(solution)/shard_map/ppermute | solution.py:287
  24.4 0.6 %shard_map.128.refs_7_.downs_ref = bf16[4,360,720]{2,1,0:T(8,128)(2,1)S(1)} custom-call(bf16[360,2880]{1,0:T(8,128)(2,1)S(1)} %bitcast.14), custom_call_target="tpu_custom_call" | custom-call | bytes 4147200 | tf_op jit(solution)/shard_map/pallas_call | solution.py:395
  25.0 0.4 %shard_map.127 = (f32[64,360]{1,0:T(8,128)S(1)}, f32[64,360]{1,0:T(8,128)S(1)}, f32[64,128]{1,0:T(8,128)S(1)}) custom-call(bf16[64,720]{1,0:T(8,128)(2,1)S(1)} %shard_map.126.block_ref, f32[4,1,720]{2,1,0:T(1,128)S(1)} %shard_map.125.gains_ref.refs_5_.refs_4_, bf16[4,360,720]{2,1,0:T(8,128)(2,1)S(1)} %shard_map.121.gates_ref.refs_6_.refs_5_, ...), custom_call_target="tpu_custom_call" | custom-call | flops 66355200 | bytes 1036800 | tf_op jit(solution)/shard_map/pallas_call | solution.py:393
  25.5 1.9 %collective-permute-done.7.refs_1_ = bf16[64,720]{1,0:T(8,128)(2,1)S(1)} collective-permute-done((bf16[64,720]{1,0:T(8,128)(2,1)S(1)}, bf16[64,720]{1,0:T(8,128)(2,1)S(1)}, u32[]{:S(2)}, u32[]{:S(2)}) %collective-permute-start.7) | collective-permute-done | bytes 92192 | tf_op jit(solution)/shard_map/ppermute | solution.py:287
  27.4 0.0 collective-permute-start.8
  27.4 0.5 %collective-permute-start.17 = (bf16[512,256]{1,0:T(8,128)(2,1)S(1)}, bf16[512,256]{1,0:T(8,128)(2,1)S(1)}, u32[]{:S(2)}, u32[]{:S(2)}) collective-permute-start(bf16[512,256]{1,0:T(8,128)(2,1)S(1)} %get-tuple-element.88.refs_0_), channel_id=1, source_target_pairs={{0,1},{1,0},{2,3},{3,2},{4,5},{5,4},{6,7},{7,6},{8,9},{9,8},{10,11... | collective-permute-start | bytes 786440 | tf_op jit(solution)/shard_map/ppermute | solution.py:287
  27.9 0.0 collective-permute-done.16.refs_1_
  27.9 0.0 collective-permute-start.18
  27.9 0.8 %shard_map.129 = (f32[64,360]{1,0:T(8,128)S(1)}, f32[64,360]{1,0:T(8,128)S(1)}, f32[64,128]{1,0:T(8,128)S(1)}) custom-call(bf16[64,720]{1,0:T(8,128)(2,1)S(1)} %collective-permute-done.9.refs_0_, bf16[64,720]{1,0:T(8,128)(2,1)S(1)} %collective-permute-done.7.refs_1_, f32[64,360]{1,0:T(8,128)S(1)} %get-tuple-element.67.refs_2_, ...), custom_call_target="tpu_custom_call" | custom-call | flops 66355200 | bytes 1036800 | tf_op jit(solution)/shard_map/pallas_call | solution.py:401
  28.7 0.7 %shard_map.130 = (bf16[2,64,720]{2,1,0:T(8,128)(2,1)S(1)}, bf16[64,360]{1,0:T(8,128)(2,1)S(1)}) custom-call(bf16[64,720]{1,0:T(8,128)(2,1)S(1)} %collective-permute-done.8.refs_0_, f32[64,360]{1,0:T(8,128)S(1)} %get-tuple-element.72.refs_1_, f32[64,360]{1,0:T(8,128)S(1)} %get-tuple-element.73.refs_2_, f32[64,128]{1,0:T(8,128)S(1)} %get-tuple-element.74.refs_3_, ...), custom_call_target="tpu_custom_call" | custom-call | flops 66355200 | bytes 1036800 | tf_op jit(solution)/shard_map/pallas_call | solution.py:404
  29.5 0.6 %collective-permute-start.10 = (bf16[2,64,720]{2,1,0:T(8,128)(2,1)S(1)}, bf16[2,64,720]{2,1,0:T(8,128)(2,1)S(1)}, u32[]{:S(2)}, u32[]{:S(2)}) collective-permute-start(bf16[2,64,720]{2,1,0:T(8,128)(2,1)S(1)} %get-tuple-element.76), channel_id=1, source_target_pairs={{0,1},{1,0},{2,3},{3,2},{4,5},{5,4},{6,7},{7,6},{8,9},{9,8},{10,11... | collective-permute-start | bytes 552968 | tf_op jit(solution)/shard_map/ppermute | solution.py:287
  30.0 0.3 shard_map.131.kept_ref
  30.4 0.7 %collective-permute-done.10.given_ref = bf16[2,64,720]{2,1,0:T(8,128)(2,1)S(1)} collective-permute-done((bf16[2,64,720]{2,1,0:T(8,128)(2,1)S(1)}, bf16[2,64,720]{2,1,0:T(8,128)(2,1)S(1)}, u32[]{:S(2)}, u32[]{:S(2)}) %collective-permute-start.10) | collective-permute-done | bytes 184352 | tf_op jit(solution)/shard_map/ppermute | solution.py:287
  31.1 0.1 shard_map.132
  31.2 1.7 %collective-permute-start.11 = (bf16[32,720]{1,0:T(8,128)(2,1)S(1)}, bf16[32,720]{1,0:T(8,128)(2,1)S(1)}, u32[]{:S(2)}, u32[]{:S(2)}) collective-permute-start(bf16[32,720]{1,0:T(8,128)(2,1)S(1)} %get-tuple-element.78), channel_id=1, source_target_pairs={{0,2},{1,3},{2,0},{3,1},{4,6},{5,7},{6,4},{7,5},{8,10},{9,11},{10,... | collective-permute-start | bytes 138248 | tf_op jit(solution)/shard_map/ppermute | solution.py:287
  32.9 0.4 collective-permute-start.14
  33.3 2.1 %collective-permute-done.11.refs_1_ = bf16[32,720]{1,0:T(8,128)(2,1)S(1)} collective-permute-done((bf16[32,720]{1,0:T(8,128)(2,1)S(1)}, bf16[32,720]{1,0:T(8,128)(2,1)S(1)}, u32[]{:S(2)}, u32[]{:S(2)}) %collective-permute-start.11) | collective-permute-done | bytes 46112 | tf_op jit(solution)/shard_map/ppermute | solution.py:287
  35.3 1.9 %collective-permute-start.12 = (bf16[16,720]{1,0:T(8,128)(2,1)S(1)}, bf16[16,720]{1,0:T(8,128)(2,1)S(1)}, u32[]{:S(2)}, u32[]{:S(2)}) collective-permute-start(bf16[16,720]{1,0:T(8,128)(2,1)S(1)} %get-tuple-element.79), channel_id=1, source_target_pairs={{0,12},{4,8},{8,4},{12,0},{1,13},{5,9},{9,5},{13,1},{2,14},{6,10},... | collective-permute-start | bytes 69128 | tf_op jit(solution)/shard_map/ppermute | solution.py:287
  37.3 1.1 %collective-permute-start.13 = (bf16[16,720]{1,0:T(8,128)(2,1)S(1)}, bf16[16,720]{1,0:T(8,128)(2,1)S(1)}, u32[]{:S(2)}, u32[]{:S(2)}) collective-permute-start(bf16[16,720]{1,0:T(8,128)(2,1)S(1)} %get-tuple-element.80), channel_id=1, source_target_pairs={{0,8},{4,12},{8,0},{12,4},{1,9},{5,13},{9,1},{13,5},{2,10},{6,14},... | collective-permute-start | bytes 69128 | tf_op jit(solution)/shard_map/ppermute | solution.py:287
  38.4 1.5 %collective-permute-start.15 = (bf16[16,720]{1,0:T(8,128)(2,1)S(1)}, bf16[16,720]{1,0:T(8,128)(2,1)S(1)}, u32[]{:S(2)}, u32[]{:S(2)}) collective-permute-start(bf16[16,720]{1,0:T(8,128)(2,1)S(1)} %get-tuple-element.83), channel_id=1, source_target_pairs={{0,4},{4,0},{8,12},{12,8},{1,5},{5,1},{9,13},{13,9},{2,6},{6,2},{1... | collective-permute-start | bytes 69128 | tf_op jit(solution)/shard_map/ppermute | solution.py:287
  39.9 0.9 %shard_map.135.refs_6_ = bf16[720,256]{1,0:T(8,128)(2,1)S(1)} custom-call(bf16[512,256]{1,0:T(8,128)(2,1)S(1)} %get-tuple-element.88.refs_0_, bf16[512,256]{1,0:T(8,128)(2,1)S(1)} %collective-permute-done.16.refs_1_, bf16[512,256]{1,0:T(8,128)(2,1)S(1)} %collective-permute-done.17.refs_2_, bf16[512,256]{1,0:T(8,128)(2,1)S(1)} %collective-permute-done.18.refs_3_, ...), custom_call_target="tpu_custom_call" | custom-call | flops 754974720 | bytes 2949120 | tf_op jit(solution)/shard_map/pallas_call | solution.py:411
  40.8 0.2 collective-permute-done.12.refs_0_
  41.1 1.3 %collective-permute-done.13.refs_1_ = bf16[16,720]{1,0:T(8,128)(2,1)S(1)} collective-permute-done((bf16[16,720]{1,0:T(8,128)(2,1)S(1)}, bf16[16,720]{1,0:T(8,128)(2,1)S(1)}, u32[]{:S(2)}, u32[]{:S(2)}) %collective-permute-start.13) | collective-permute-done | bytes 23072 | tf_op jit(solution)/shard_map/ppermute | solution.py:287
  42.4 1.1 %shard_map.136 = bf16[720,256]{1,0:T(8,128)(2,1)} custom-call(bf16[16,720]{1,0:T(8,128)(2,1)S(1)} %collective-permute-done.12.refs_0_, bf16[16,720]{1,0:T(8,128)(2,1)S(1)} %collective-permute-done.13.refs_1_, bf16[16,720]{1,0:T(8,128)(2,1)S(1)} %collective-permute-done.15.refs_2_, bf16[16,720]{1,0:T(8,128)(2,1)S(1)} %get-tuple-element.84.refs_3_, ...), custom_call_target="tpu_custom_call" | custom-call | tf_op jit(solution)/shard_map/pallas_call | solution.py:431
  (18 shorter events, 0.1 us)
Async XLA Ops:
  0.8 7.3 %collective-permute-start = (bf16[128,256]{1,0:T(8,128)(2,1)S(1)}, bf16[128,256]{1,0:T(8,128)(2,1)S(1)}, u32[]{:S(2)}, u32[]{:S(2)}) collective-permute-start(bf16[128,256]{1,0:T(8,128)(2,1)S(1)} %slice.3), channel_id=1, source_target_pairs={{0,4},{4,8},{8,12},{12,0},{1,5},{5,9},{9,13},{13,1},{2,6},{6,10},{... | collective-permute-start | bytes 196616 | tf_op jit(solution)/shard_map/ppermute | solution.py:328
  3.9 7.2 %copy-start = (bf16[1,2880,360]{1,2,0:T(8,128)(2,1)S(1)}, bf16[1,2880,360]{1,2,0:T(8,128)(2,1)}, u32[]{:S(2)}) copy-start(bf16[1,2880,360]{1,2,0:T(8,128)(2,1)} %param.21) | copy-start | bytes 6220804
  9.3 5.0 %collective-permute-start.1 = (bf16[64,512]{1,0:T(8,128)(2,1)S(1)}, bf16[64,512]{1,0:T(8,128)(2,1)S(1)}, u32[]{:S(2)}, u32[]{:S(2)}) collective-permute-start(bf16[64,512]{1,0:T(8,128)(2,1)S(1)} %get-tuple-element.53.rows_ref), channel_id=1, source_target_pairs={{0,2},{1,3},{2,0},{3,1},{4,6},{5,7},{6,4},{7,5},{8,10},{9,11},{10,... | collective-permute-start | bytes 196616 | tf_op jit(solution)/shard_map/ppermute | solution.py:287
  11.7 16.2 %collective-permute-start.16 = (bf16[512,256]{1,0:T(8,128)(2,1)S(1)}, bf16[512,256]{1,0:T(8,128)(2,1)S(1)}, u32[]{:S(2)}, u32[]{:S(2)}) collective-permute-start(bf16[512,256]{1,0:T(8,128)(2,1)S(1)} %get-tuple-element.88.refs_0_), channel_id=1, source_target_pairs={{0,2},{1,3},{2,0},{3,1},{4,6},{5,7},{6,4},{7,5},{8,10},{9,11},{10,... | collective-permute-start | bytes 786440 | tf_op jit(solution)/shard_map/ppermute | solution.py:287
  12.1 2.3 %collective-permute-start.3 = (bf16[64,512]{1,0:T(8,128)(2,1)S(1)}, bf16[64,512]{1,0:T(8,128)(2,1)S(1)}, u32[]{:S(2)}, u32[]{:S(2)}) collective-permute-start(bf16[64,512]{1,0:T(8,128)(2,1)S(1)} %get-tuple-element.53.rows_ref), channel_id=1, source_target_pairs={{0,1},{1,0},{2,3},{3,2},{4,5},{5,4},{6,7},{7,6},{8,9},{9,8},{10,11... | collective-permute-start | bytes 196616 | tf_op jit(solution)/shard_map/ppermute | solution.py:287
  14.4 1.3 %collective-permute-start.2 = (bf16[64,512]{1,0:T(8,128)(2,1)S(1)}, bf16[64,512]{1,0:T(8,128)(2,1)S(1)}, u32[]{:S(2)}, u32[]{:S(2)}) collective-permute-start(bf16[64,512]{1,0:T(8,128)(2,1)S(1)} %collective-permute-done.1.refs_1_), channel_id=1, source_target_pairs={{0,1},{1,0},{2,3},{3,2},{4,5},{5,4},{6,7},{7,6},{8,9},{9,8},{10,11... | collective-permute-start | bytes 196616 | tf_op jit(solution)/shard_map/ppermute | solution.py:287
  14.9 5.5 %copy-start.3 = (f32[2880]{0:T(1024)S(1)}, f32[2880]{0:T(1024)}, u32[]{:S(2)}) copy-start(f32[2880]{0:T(1024)} %gain_ref.1) | copy-start | bytes 34564
  15.0 5.5 %copy-start.1 = (bf16[1,2880,360]{1,2,0:T(8,128)(2,1)S(1)}, bf16[1,2880,360]{1,2,0:T(8,128)(2,1)}, u32[]{:S(2)}) copy-start(bf16[1,2880,360]{1,2,0:T(8,128)(2,1)} %param.22) | copy-start | bytes 6220804
  16.0 5.8 %collective-permute-start.4 = (bf16[16,720]{1,0:T(8,128)(2,1)S(1)}, bf16[16,720]{1,0:T(8,128)(2,1)S(1)}, u32[]{:S(2)}, u32[]{:S(2)}) collective-permute-start(bf16[16,720]{1,0:T(8,128)(2,1)S(1)} %get-tuple-element.58), channel_id=1, source_target_pairs={{0,12},{4,8},{8,4},{12,0},{1,13},{5,9},{9,5},{13,1},{2,14},{6,10},... | collective-permute-start | bytes 69128 | tf_op jit(solution)/shard_map/ppermute | solution.py:287
  18.0 4.7 %collective-permute-start.5 = (bf16[16,720]{1,0:T(8,128)(2,1)S(1)}, bf16[16,720]{1,0:T(8,128)(2,1)S(1)}, u32[]{:S(2)}, u32[]{:S(2)}) collective-permute-start(bf16[16,720]{1,0:T(8,128)(2,1)S(1)} %get-tuple-element.59), channel_id=1, source_target_pairs={{0,8},{4,12},{8,0},{12,4},{1,9},{5,13},{9,1},{13,5},{2,10},{6,14},... | collective-permute-start | bytes 69128 | tf_op jit(solution)/shard_map/ppermute | solution.py:287
  18.0 4.7 %collective-permute-start.6 = (bf16[16,720]{1,0:T(8,128)(2,1)S(1)}, bf16[16,720]{1,0:T(8,128)(2,1)S(1)}, u32[]{:S(2)}, u32[]{:S(2)}) collective-permute-start(bf16[16,720]{1,0:T(8,128)(2,1)S(1)} %get-tuple-element.60), channel_id=1, source_target_pairs={{0,4},{4,0},{8,12},{12,8},{1,5},{5,1},{9,13},{13,9},{2,6},{6,2},{1... | collective-permute-start | bytes 69128 | tf_op jit(solution)/shard_map/ppermute | solution.py:287
  20.5 3.9 %copy-start.2 = (bf16[1,360,2880]{2,1,0:T(8,128)(2,1)S(1)}, bf16[1,360,2880]{2,1,0:T(8,128)(2,1)}, u32[]{:S(2)}) copy-start(bf16[1,360,2880]{2,1,0:T(8,128)(2,1)} %param.23) | copy-start | bytes 6220804
  22.7 4.7 %collective-permute-start.7 = (bf16[64,720]{1,0:T(8,128)(2,1)S(1)}, bf16[64,720]{1,0:T(8,128)(2,1)S(1)}, u32[]{:S(2)}, u32[]{:S(2)}) collective-permute-start(bf16[64,720]{1,0:T(8,128)(2,1)S(1)} %shard_map.126.block_ref), channel_id=1, source_target_pairs={{0,2},{1,3},{2,0},{3,1},{4,6},{5,7},{6,4},{7,5},{8,10},{9,11},{10,... | collective-permute-start | bytes 276488 | tf_op jit(solution)/shard_map/ppermute | solution.py:287
  24.4 3.5 %collective-permute-start.9 = (bf16[64,720]{1,0:T(8,128)(2,1)S(1)}, bf16[64,720]{1,0:T(8,128)(2,1)S(1)}, u32[]{:S(2)}, u32[]{:S(2)}) collective-permute-start(bf16[64,720]{1,0:T(8,128)(2,1)S(1)} %shard_map.126.block_ref), channel_id=1, source_target_pairs={{0,1},{1,0},{2,3},{3,2},{4,5},{5,4},{6,7},{7,6},{8,9},{9,8},{10,11... | collective-permute-start | bytes 276488 | tf_op jit(solution)/shard_map/ppermute | solution.py:287
  27.4 1.3 %collective-permute-start.8 = (bf16[64,720]{1,0:T(8,128)(2,1)S(1)}, bf16[64,720]{1,0:T(8,128)(2,1)S(1)}, u32[]{:S(2)}, u32[]{:S(2)}) collective-permute-start(bf16[64,720]{1,0:T(8,128)(2,1)S(1)} %collective-permute-done.7.refs_1_), channel_id=1, source_target_pairs={{0,1},{1,0},{2,3},{3,2},{4,5},{5,4},{6,7},{7,6},{8,9},{9,8},{10,11... | collective-permute-start | bytes 276488 | tf_op jit(solution)/shard_map/ppermute | solution.py:287
  27.4 12.5 %collective-permute-start.17 = (bf16[512,256]{1,0:T(8,128)(2,1)S(1)}, bf16[512,256]{1,0:T(8,128)(2,1)S(1)}, u32[]{:S(2)}, u32[]{:S(2)}) collective-permute-start(bf16[512,256]{1,0:T(8,128)(2,1)S(1)} %get-tuple-element.88.refs_0_), channel_id=1, source_target_pairs={{0,1},{1,0},{2,3},{3,2},{4,5},{5,4},{6,7},{7,6},{8,9},{9,8},{10,11... | collective-permute-start | bytes 786440 | tf_op jit(solution)/shard_map/ppermute | solution.py:287
  27.9 12.0 %collective-permute-start.18 = (bf16[512,256]{1,0:T(8,128)(2,1)S(1)}, bf16[512,256]{1,0:T(8,128)(2,1)S(1)}, u32[]{:S(2)}, u32[]{:S(2)}) collective-permute-start(bf16[512,256]{1,0:T(8,128)(2,1)S(1)} %collective-permute-done.16.refs_1_), channel_id=1, source_target_pairs={{0,1},{1,0},{2,3},{3,2},{4,5},{5,4},{6,7},{7,6},{8,9},{9,8},{10,11... | collective-permute-start | bytes 786440 | tf_op jit(solution)/shard_map/ppermute | solution.py:287
  29.5 1.6 %collective-permute-start.10 = (bf16[2,64,720]{2,1,0:T(8,128)(2,1)S(1)}, bf16[2,64,720]{2,1,0:T(8,128)(2,1)S(1)}, u32[]{:S(2)}, u32[]{:S(2)}) collective-permute-start(bf16[2,64,720]{2,1,0:T(8,128)(2,1)S(1)} %get-tuple-element.76), channel_id=1, source_target_pairs={{0,1},{1,0},{2,3},{3,2},{4,5},{5,4},{6,7},{7,6},{8,9},{9,8},{10,11... | collective-permute-start | bytes 552968 | tf_op jit(solution)/shard_map/ppermute | solution.py:287
  31.2 4.2 %collective-permute-start.11 = (bf16[32,720]{1,0:T(8,128)(2,1)S(1)}, bf16[32,720]{1,0:T(8,128)(2,1)S(1)}, u32[]{:S(2)}, u32[]{:S(2)}) collective-permute-start(bf16[32,720]{1,0:T(8,128)(2,1)S(1)} %get-tuple-element.78), channel_id=1, source_target_pairs={{0,2},{1,3},{2,0},{3,1},{4,6},{5,7},{6,4},{7,5},{8,10},{9,11},{10,... | collective-permute-start | bytes 138248 | tf_op jit(solution)/shard_map/ppermute | solution.py:287
  32.9 5.5 %collective-permute-start.14 = (bf16[32,720]{1,0:T(8,128)(2,1)S(1)}, bf16[32,720]{1,0:T(8,128)(2,1)S(1)}, u32[]{:S(2)}, u32[]{:S(2)}) collective-permute-start(bf16[32,720]{1,0:T(8,128)(2,1)S(1)} %get-tuple-element.82), channel_id=1, source_target_pairs={{0,2},{1,3},{2,0},{3,1},{4,6},{5,7},{6,4},{7,5},{8,10},{9,11},{10,... | collective-permute-start | bytes 138248 | tf_op jit(solution)/shard_map/ppermute | solution.py:287
  35.3 5.7 %collective-permute-start.12 = (bf16[16,720]{1,0:T(8,128)(2,1)S(1)}, bf16[16,720]{1,0:T(8,128)(2,1)S(1)}, u32[]{:S(2)}, u32[]{:S(2)}) collective-permute-start(bf16[16,720]{1,0:T(8,128)(2,1)S(1)} %get-tuple-element.79), channel_id=1, source_target_pairs={{0,12},{4,8},{8,4},{12,0},{1,13},{5,9},{9,5},{13,1},{2,14},{6,10},... | collective-permute-start | bytes 69128 | tf_op jit(solution)/shard_map/ppermute | solution.py:287
  37.3 5.1 %collective-permute-start.13 = (bf16[16,720]{1,0:T(8,128)(2,1)S(1)}, bf16[16,720]{1,0:T(8,128)(2,1)S(1)}, u32[]{:S(2)}, u32[]{:S(2)}) collective-permute-start(bf16[16,720]{1,0:T(8,128)(2,1)S(1)} %get-tuple-element.80), channel_id=1, source_target_pairs={{0,8},{4,12},{8,0},{12,4},{1,9},{5,13},{9,1},{13,5},{2,10},{6,14},... | collective-permute-start | bytes 69128 | tf_op jit(solution)/shard_map/ppermute | solution.py:287
  38.4 3.9 %collective-permute-start.15 = (bf16[16,720]{1,0:T(8,128)(2,1)S(1)}, bf16[16,720]{1,0:T(8,128)(2,1)S(1)}, u32[]{:S(2)}, u32[]{:S(2)}) collective-permute-start(bf16[16,720]{1,0:T(8,128)(2,1)S(1)} %get-tuple-element.83), channel_id=1, source_target_pairs={{0,4},{4,0},{8,12},{12,8},{1,5},{5,1},{9,13},{13,9},{2,6},{6,2},{1... | collective-permute-start | bytes 69128 | tf_op jit(solution)/shard_map/ppermute | solution.py:287

commit v8 on v7

--- a/solution.py
+++ b/solution.py
@@ -196,10 +196,17 @@
     resid_ref[...] = total.astype(jnp.bfloat16)
 
 
-def spread_kernel(source_ref, blocks_ref):
-    cuts, _, width = blocks_ref.shape
-    for p in range(cuts):
-        blocks_ref[p] = source_ref[:, p * width : (p + 1) * width]
+def spread_kernel(*refs):
+    sources, targets = refs[:CORES], refs[CORES:]
+    steps, _, width = targets[0].shape
+    chip, core = lax.div(lax.axis_index("cuts"), CORES), lax.rem(lax.axis_index("cuts"), CORES)
+    for value in range(CORES):
+
+        @pl.when(core == value)
+        def _():
+            for source, target in zip(sources, targets):
+                for p in range(value, CORES * steps, CORES):
+                    target[lax.bitwise_xor(chip, p // CORES)] = source[:, p * width : (p + 1) * width]
 
 
 def spread_gain_kernel(gain_ref, blocks_ref):
@@ -209,61 +216,58 @@
         blocks_ref[p] = gain[:, p * width : (p + 1) * width]
 
 
-def add_features(sums, places, blocks, gains_ref, gates_ref, ups_ref, steps):
-    gate, up, squares = sums
-    for i, block in zip(places, blocks):
-        p = origin(i % steps, i >= steps)
-        wide = block[...].astype(jnp.float32)
-        squares += jnp.sum(wide * wide, axis=1, keepdims=True)
-        rows = (wide * gains_ref[p]).astype(jnp.bfloat16)
-        gate += dot(rows, gates_ref[p], NT)
-        up += dot(rows, ups_ref[p], NT)
-    return gate, up, squares
-
-
-def store_sums(sums, refs):
-    for ref, value in zip(refs, sums):
-        ref[...] = jnp.broadcast_to(value, ref.shape)
-
-
-def expert_own_kernel(steps, block_ref, gains_ref, gates_ref, ups_ref, *out_refs):
-    zeros = jnp.zeros(out_refs[0].shape, jnp.float32)
-    sums = (zeros, zeros, jnp.zeros((zeros.shape[0], 1), jnp.float32))
-    store_sums(add_features(sums, [0], [block_ref], gains_ref, gates_ref, ups_ref, steps), out_refs)
-
-
-def expert_more_kernel(places, steps, *refs):
-    blocks, refs = refs[:-9], refs[-9:]
-    sums = (refs[0][...], refs[1][...], refs[2][:, :1])
-    store_sums(add_features(sums, places, blocks, *refs[3:6], steps), refs[6:])
-
-
-def expert_last_kernel(steps, *refs):
+def add_features(totals, k, block, gains_ref, weights):
+    wide = block[...].astype(jnp.float32)
+    rows = (wide * gains_ref[origin(k, False)]).astype(jnp.bfloat16)
+    totals = [total + dot(rows, w[k], NT) for total, w in zip(totals, weights)] + totals[len(weights) :]
+    totals[-1] += jnp.sum(wide * wide, axis=1, keepdims=True)
+    return totals
+
+
+def expert_own_kernel(block_ref, gains_ref, *refs):
+    weights, totals_ref = refs[:-1], refs[-1]
+    totals = [jnp.zeros(totals_ref.shape[1:], jnp.float32)] * totals_ref.shape[0]
+    for i, total in enumerate(add_features(totals, 0, block_ref, gains_ref, weights)):
+        totals_ref[i] = total
+
+
+def expert_chips_kernel(steps, *refs):
     blocks, refs = refs[: steps - 1], refs[steps - 1 :]
-    sums = (refs[0][...], refs[1][...], refs[2][:, :1])
-    gains_ref, gates_ref, ups_ref, downs_ref, given_ref, activated_ref = refs[3:]
-    places = range(steps + 1, 2 * steps)
-    gate, up, squares = add_features(sums, places, blocks, gains_ref, gates_ref, ups_ref, steps)
-    cuts, _, width = gates_ref.shape
-    scale = lax.rsqrt(squares / (cuts * width) + norm_eps)
-    gate, up = gate * scale, up * scale
-    activated = ((up + 1.0) * gate * jax.nn.sigmoid(glu_alpha * gate)).astype(jnp.bfloat16)
-    activated_ref[...] = activated
-    for k in range(steps):
-        given_ref[k] = dot(activated, downs_ref[origin(k, True)], NN).astype(jnp.bfloat16)
-
-
-def expert_kept_kernel(activated_ref, downs_ref, kept_ref):
-    for k in range(kept_ref.shape[0]):
-        kept_ref[k] = dot(activated_ref[...], downs_ref[origin(k, False)], NN).astype(jnp.bfloat16)
-
-
-def add_cores_kernel(kept_ref, given_ref, *out_refs):
+    before_ref, gains_ref, *weights, totals_ref, sums_ref, squares_ref = refs
+    totals = [before_ref[i] for i in range(totals_ref.shape[0])]
+    for k, block in enumerate(blocks, 1):
+        totals = add_features(totals, k, block, gains_ref, weights)
+    for i, total in enumerate(totals):
+        totals_ref[i] = total
+    for i in range(2 * CORES):
+        sums_ref[i] = totals[i].astype(jnp.bfloat16)
+    squares_ref[...] = totals[-1][:, : squares_ref.shape[1]]
+
+
+def expert_last_kernel(features, mine_ref, sums_ref, squares_ref, down_mine_ref, down_theirs_ref, *out_refs):
+    gates = [mine_ref[i] + sums_ref[1 - i].astype(jnp.float32) for i in range(CORES)]
+    ups = [mine_ref[CORES + i] + sums_ref[CORES + 1 - i].astype(jnp.float32) for i in range(CORES)]
+    squares = mine_ref[2 * CORES][:, :1] + squares_ref[:, :1]
+    scale = lax.rsqrt(squares / features + norm_eps)
+    activated = []
+    for gate, up in zip(gates, ups):
+        gate, up = gate * scale, up * scale
+        activated.append(((up + 1.0) * gate * jax.nn.sigmoid(glu_alpha * gate)).astype(jnp.bfloat16))
+    for i in range(CORES):
+        out_refs[i][...] = activated[i]
+    store_products(range(1, down_mine_ref.shape[0]), out_refs[:CORES], down_mine_ref, down_theirs_ref, out_refs[CORES:])
+
+
+def store_products(chips, activated, down_mine_ref, down_theirs_ref, out_refs):
     half = out_refs[0].shape[0]
-    for i, out_ref in enumerate(out_refs):
-        rows = slice(i % 2 * half, (i % 2 + 1) * half)
-        total = kept_ref[i // 2, rows].astype(jnp.float32) + given_ref[i // 2, rows].astype(jnp.float32)
-        out_ref[...] = total.astype(jnp.bfloat16)
+    for k, firsts in zip(chips, range(0, len(out_refs), 2)):
+        out = dot(activated[0][...], down_mine_ref[k], NN) + dot(activated[1][...], down_theirs_ref[k], NN)
+        for i in range(2):
+            out_refs[firsts + i][...] = out[i * half : (i + 1) * half].astype(jnp.bfloat16)
+
+
+def expert_kept_kernel(mine_ref, theirs_ref, down_mine_ref, down_theirs_ref, *out_refs):
+    store_products([0], (mine_ref, theirs_ref), down_mine_ref, down_theirs_ref, out_refs)
 
 
 def add_chips_kernel(steps, *refs):
@@ -279,7 +283,8 @@
     for k in range(live):
         rows_ref[lax.bitwise_xor(me, live - 1 - k)] = blocks[k][...]
     rows = rows_ref[...].reshape(live * CAP, -1)
-    mixed = dot(rows, mix_hi_ref[...], TN) + dot(rows, mix_lo_ref[...], TN)
+    mix = jnp.concatenate([mix_hi_ref[...], mix_lo_ref[...]], axis=0)
+    mixed = dot(jnp.concatenate([rows, rows], axis=0), mix, TN)
     out_ref[...] = (resid_ref[...].astype(jnp.float32) + mixed).astype(jnp.bfloat16)
 
 
@@ -346,6 +351,8 @@
         flops=4 * toks * SPAN * head_rows,
         moved=2 * (w_out.size + residual.size + queries.size),
     )(*(in_hbm(a) for a in (expert_ids.T, route_weights.T, attention_sink_logits, *loads)))
+    pairs = [(w, from_sibling(w)) for w in (w_gate[0].T, w_up[0].T, w_down[0])]
+    spread = call(spread_kernel, (bf16(steps, hidden, feats),) * CORES, n_in=CORES, moved=4 * w_gate.size)
     attended, rows = call(
         second_kernel,
         (bf16(head_rows, toks), bf16(slots, head_rows)),
@@ -354,6 +361,8 @@
         moved=2 * queries.size,
     )(q, kv, before, rim, sinks, late, placing)
 
+    gate_pair, up_pair, down_pair = pairs
+    rows, attended = after((rows, attended), pairs)
     chip_rows = from_chips(rows)
     total = jax.ShapeDtypeStruct((slots, feats), jnp.float32)
     part = dict(flops=slots * w_out.size // 2, moved=w_out.size // 2)
@@ -362,10 +371,7 @@
     )
     sibling_rows = from_sibling(rows)
     places = [steps, *range(1, steps)]
-    spread = functools.partial(
-        call, spread_kernel, bf16(cuts, hidden, feats), n_in=1, moved=4 * w_gate.size
-    )
-    gates = spread()(after(w_gate[0].T, rows))
+    gates = spread(*after(gate_pair, rows))
     chip_rows = after(chip_rows, (own, gates))
     relayed_rows = [from_sibling(b) for b in chip_rows]
     chips = call(functools.partial(rows_more_kernel, places, steps), total, n_in=steps + 2, **part)(
@@ -381,33 +387,35 @@
 
     arrived = [swap(outgoing[k], "seq", k) for k in range(live - 1, 0, -1)] + [outgoing[0]]
 
-    ups = spread()(after(w_up[0].T, outgoing[0]))
     gains = call(spread_gain_kernel, jax.ShapeDtypeStruct((cuts, 1, feats), jnp.float32), n_in=1)(norm_gain)
-    sums = (
-        *(jax.ShapeDtypeStruct((slots, hidden), jnp.float32),) * 2,
-        jax.ShapeDtypeStruct((slots, KEYS_SEEN), jnp.float32),
-    )
-    part = dict(flops=slots * w_gate.size, moved=w_gate.size)
-    stacked = call(stack_kernel, bf16(slots, feats), n_in=live)(*after(arrived, (ups, gains)))
+    ups = spread(*after(up_pair, outgoing[0]))
+    weights = (*gates, *ups)
+    totals = jax.ShapeDtypeStruct((2 * CORES + 1, slots, hidden), jnp.float32)
+    part = dict(flops=4 * slots * hidden * feats, moved=8 * hidden * feats)
+    chip_blocks = from_chips(after(attended, outgoing[0]))
+    stacked = call(stack_kernel, bf16(slots, feats), n_in=live)(*after(arrived, (gains, ups)))
     chip_rows = from_chips(stacked)
-    own = call(functools.partial(expert_own_kernel, steps), sums, n_in=4, **part)(stacked, gains, gates, ups)
-    sibling_rows = from_sibling(stacked)
-    downs = spread()(after(w_down[0], stacked))
-    chip_blocks = from_chips(after(attended, gates))
+    own = call(expert_own_kernel, totals, n_in=6, **part)(stacked, gains, *weights)
     blocks = [attended, *chip_blocks]
-    blocks += [from_sibling(b) for b in blocks]
+    blocks += [from_sibling(b) for b in after(blocks, stacked)]
+    downs = spread(*after(down_pair, stacked))
     chip_rows = after(chip_rows, (own, downs))
-    relayed_rows = [from_sibling(b) for b in chip_rows]
-    chips = call(functools.partial(expert_more_kernel, places, steps), sums, n_in=steps + 6, **part)(
-        sibling_rows, *chip_rows, *own, gains, gates, ups
-    )
-    given, activated = call(
-        functools.partial(expert_last_kernel, steps),
-        (bf16(steps, slots, feats), bf16(slots, hidden)),
-        n_in=steps + 6,
+    chips, *theirs = call(
+        functools.partial(expert_chips_kernel, steps),
+        (totals, bf16(2 * CORES, slots, hidden), jax.ShapeDtypeStruct((slots, KEYS_SEEN), jnp.float32)),
+        n_in=steps + 5,
         **part,
-    )(*relayed_rows, *chips, gains, gates, ups, downs)
-    kept = call(expert_kept_kernel, bf16(steps, slots, feats), n_in=2, **part)(activated, downs)
+    )(
+        *chip_rows, own, gains, *weights
+    )
+    half = bf16(slots // 2, feats)
+    act_mine, act_theirs, *sums = call(
+        functools.partial(expert_last_kernel, width),
+        (*(bf16(slots, hidden),) * CORES, *(half,) * (2 * steps - 2)),
+        n_in=5,
+    )(chips, *(from_sibling(a) for a in theirs), *downs)
+    kept = call(expert_kept_kernel, (half,) * 2, n_in=4)(act_mine, act_theirs, *downs)
+    sums = [*kept, *sums]
     resid = call(
         functools.partial(project_kernel, steps),
         bf16(feats, toks),
@@ -416,9 +424,6 @@
         moved=2 * w_out.size,
     )(*blocks, w_t, residual_t)
 
-    sums = call(add_cores_kernel, (bf16(slots // 2, feats),) * (2 * steps), n_in=2)(
-        kept, swap(given, "cuts", 1)
-    )
     returned = []
     for half in range(2):
         parts = [sums[half]] + [swap(sums[2 * k + half], "cuts", CORES * k) for k in range(1, steps)]

time: 43.6 us -> 47.3 us (1.085)
  waiting for transfers between devices: 12.3 us -> 14.8 us
  starting transfers between devices: 19 us -> 21 us
  Pallas kernels: 11.1 us -> 10.3 us
    ppermute x18 -> x20, starting transfers between devices: 16 us -> 18.4 us  [swap(): lax.ppermute(block, axis, [(i, i ^ mask) for i in range(lax.axis_size(axi...]
    ppermute x18 -> x20, waiting for transfers between devices: 10.3 us -> 12.3 us  [swap(): lax.ppermute(block, axis, [(i, i ^ mask) for i in range(lax.axis_size(axi...]
    pallas_call x8 -> x7, Pallas kernels: 4.1 us -> 3.39 us  [the longest x1 0.77 us: shards(): call(functools.partial(expert_chips_kernel, steps), (totals, bf16(2 * COR...]
    ppermute x1, waiting for transfers between devices: 1.96 us -> 2.48 us  [shards(): rim = lax.ppermute(tail, 'seq', [(i, (i + 1) % size) for i in range(size)])]
  transfers between devices with their start and end apart: 19 -> 21, of which waited for: 10 -> 12; matrix products, arithmetic and copies ran while one was open for 0% -> 2% of each run, Pallas kernels for 20% -> 19%
where the time goes in v8:
time: 47.3 us; the launch traced here: 47.2 us
  starting transfers between devices  21 us (44%)
  waiting for transfers between devices  14.8 us (31%)
  Pallas kernels  10.3 us (22%)
  local copies, waits for them, and re-layouts  0.86 us (2%)
    ppermute x20, starting transfers between devices, swap(): lax.ppermute(block, axis, [(i, i ^ mask) for i in range(lax.axis_size(axi...  18.4 us
    ppermute x20, waiting for transfers between devices, swap(): lax.ppermute(block, axis, [(i, i ^ mask) for i in range(lax.axis_size(axi...  12.3 us
    ppermute x1, starting transfers between devices, shards(): rim = lax.ppermute(tail, 'seq', [(i, (i + 1) % size) for i in range(size)])  2.57 us
    ppermute x1, waiting for transfers between devices, shards(): rim = lax.ppermute(tail, 'seq', [(i, (i + 1) % size) for i in range(size)])  2.48 us
    pallas_call x1, Pallas kernels, shards(): call(functools.partial(first_kernel, live), (*(bf16(*a.shape) for a in lo...  2.3 us
    pallas_call x1, Pallas kernels, shards(): call(second_kernel, (bf16(head_rows, toks), bf16(slots, head_rows)), n_in...  1.18 us
    pallas_call x1, Pallas kernels, shards(): call(functools.partial(combine_kernel, live), bf16(feats, toks), n_in=liv...  1.05 us
  transfers between devices with their start and end apart: 21, of which 12 were waited for; matrix products, arithmetic and copies ran while one was open for 2% of the time, Pallas kernels for 19%

profile of v8, /device:TPU:0, one launch (start us, length us, event | category | flops | bytes accessed | tf_op | source)
XLA Modules:
  0.0 47.2 jit_solution(14024410243690359757)
XLA Ops:
  0.0 0.5 collective-permute-start.1
  0.5 0.1 collective-permute-start.2
  0.5 0.5 collective-permute-start.3
  1.0 0.8 %slice.3 = bf16[128,256]{1,0:T(8,128)(2,1)S(1)} slice(bf16[256,256]{1,0:T(8,128)(2,1)} %refs_4_.1), slice={[128:256], [0:256]} | slice | bytes 131072 | tf_op jit(solution)/shard_map/slice | solution.py:332
  1.8 2.6 %collective-permute-start = (bf16[128,256]{1,0:T(8,128)(2,1)S(1)}, bf16[128,256]{1,0:T(8,128)(2,1)S(1)}, u32[]{:S(2)}, u32[]{:S(2)}) collective-permute-start(bf16[128,256]{1,0:T(8,128)(2,1)S(1)} %slice.3), channel_id=1, source_target_pairs={{0,4},{4,8},{8,12},{12,0},{1,5},{5,9},{9,13},{13,1},{2,6},{6,10},{... | collective-permute-start | bytes 196616 | tf_op jit(solution)/shard_map/ppermute | solution.py:333
  4.4 2.3 %shard_map.118 = (bf16[256,512]{1,0:T(8,128)(2,1)S(1)}, bf16[256,256]{1,0:T(8,128)(2,1)S(1)}, bf16[128,256]{1,0:T(8,128)(2,1)S(1)}, bf16[720,2048]{1,0:T(8,128)(...) custom-call(s32[4,256]{1,0:T(4,128)} %bitcast.20, ...), custom_call_target="tpu_custom_call" | custom-call | flops 134217728 | bytes 3579904 | tf_op jit(solution)/shard_map/pallas_call | solution.py:335
  6.7 2.5 %collective-permute-done.rim_ref = bf16[128,256]{1,0:T(8,128)(2,1)S(1)} collective-permute-done((bf16[128,256]{1,0:T(8,128)(2,1)S(1)}, bf16[128,256]{1,0:T(8,128)(2,1)S(1)}, u32[]{:S(2)}, u32[]{:S(2)}) %collective-permute-start) | collective-permute-done | bytes 65568 | tf_op jit(solution)/shard_map/ppermute | solution.py:333
  9.2 1.2 %shard_map.119 = (bf16[512,256]{1,0:T(8,128)(2,1)S(1)}, bf16[64,512]{1,0:T(8,128)(2,1)S(1)}) custom-call(bf16[256,512]{1,0:T(8,128)(2,1)S(1)} %get-tuple-element.57.q_ref, bf16[256,256]{1,0:T(8,128)(2,1)S(1)} %get-tuple-element.58.kv_ref, bf16[128,256]{1,0:T(8,128)(2,1)S(1)} %get-tuple-element.59.before_ref, ...), custom_call_target="tpu_custom_call" | custom-call | flops 67108864 | bytes 262144 | tf_op jit(solution)/shard_map/pallas_call | solution.py:356
  10.4 0.0 collective-permute-done.1.refs_1_
  10.4 0.2 collective-permute-done.3.refs_1_
  10.5 2.9 %collective-permute-start.4 = (bf16[64,512]{1,0:T(8,128)(2,1)S(1)}, bf16[64,512]{1,0:T(8,128)(2,1)S(1)}, u32[]{:S(2)}, u32[]{:S(2)}) collective-permute-start(bf16[64,512]{1,0:T(8,128)(2,1)S(1)} %get-tuple-element.65.rows_ref), channel_id=1, source_target_pairs={{0,2},{1,3},{2,0},{3,1},{4,6},{5,7},{6,4},{7,5},{8,10},{9,11},{10,... | collective-permute-start | bytes 196616 | tf_op jit(solution)/shard_map/ppermute | solution.py:292
  13.4 0.4 shard_map.121
  13.8 0.5 shard_map.120.refs_2_
  14.3 1.5 %collective-permute-done.4.refs_1_ = bf16[64,512]{1,0:T(8,128)(2,1)S(1)} collective-permute-done((bf16[64,512]{1,0:T(8,128)(2,1)S(1)}, bf16[64,512]{1,0:T(8,128)(2,1)S(1)}, u32[]{:S(2)}, u32[]{:S(2)}) %collective-permute-start.4) | collective-permute-done | bytes 65568 | tf_op jit(solution)/shard_map/ppermute | solution.py:292
  15.8 0.6 %shard_map.122.refs_1_ = f32[64,720]{1,0:T(8,128)S(1)} custom-call(bf16[64,512]{1,0:T(8,128)(2,1)S(1)} %collective-permute-done.6.refs_0_, bf16[64,512]{1,0:T(8,128)(2,1)S(1)} %collective-permute-done.4.refs_1_, f32[64,720]{1,0:T(8,128)S(1)} %shard_map.120.refs_2_, bf16[720,2048]{1,0:T(8,128)(2,1)S(1)} %get-tuple-element.66.w_ref.refs_3_.refs_2_.refs_4_), custom_call_target="tpu_custom_call" | custom-call | flops 47185920 | bytes 737280 | tf_op jit(solution)/shard_map/pallas_call | solution.py:377
  16.4 0.0 copy-start.3
  16.4 0.0 copy-start.1
  16.4 0.6 %collective-permute-done.5.refs_0_ = bf16[64,512]{1,0:T(8,128)(2,1)S(1)} collective-permute-done((bf16[64,512]{1,0:T(8,128)(2,1)S(1)}, bf16[64,512]{1,0:T(8,128)(2,1)S(1)}, u32[]{:S(2)}, u32[]{:S(2)}) %collective-permute-start.5) | collective-permute-done | bytes 65568 | tf_op jit(solution)/shard_map/ppermute | solution.py:292
  17.1 0.3 shard_map.123
  17.4 1.9 %collective-permute-start.18 = (bf16[512,256]{1,0:T(8,128)(2,1)S(1)}, bf16[512,256]{1,0:T(8,128)(2,1)S(1)}, u32[]{:S(2)}, u32[]{:S(2)}) collective-permute-start(bf16[512,256]{1,0:T(8,128)(2,1)S(1)} %get-tuple-element.107.refs_0_), channel_id=1, source_target_pairs={{0,2},{1,3},{2,0},{3,1},{4,6},{5,7},{6,4},{7,5},{8,10},{9,11},{10,... | collective-permute-start | bytes 786440 | tf_op jit(solution)/shard_map/ppermute | solution.py:292
  19.4 3.6 %collective-permute-start.7 = (bf16[16,720]{1,0:T(8,128)(2,1)S(1)}, bf16[16,720]{1,0:T(8,128)(2,1)S(1)}, u32[]{:S(2)}, u32[]{:S(2)}) collective-permute-start(bf16[16,720]{1,0:T(8,128)(2,1)S(1)} %get-tuple-element.73), channel_id=1, source_target_pairs={{0,12},{4,8},{8,4},{12,0},{1,13},{5,9},{9,5},{13,1},{2,14},{6,10},... | collective-permute-start | bytes 69128 | tf_op jit(solution)/shard_map/ppermute | solution.py:292
  23.0 0.8 %collective-permute-start.9 = (bf16[16,720]{1,0:T(8,128)(2,1)S(1)}, bf16[16,720]{1,0:T(8,128)(2,1)S(1)}, u32[]{:S(2)}, u32[]{:S(2)}) collective-permute-start(bf16[16,720]{1,0:T(8,128)(2,1)S(1)} %get-tuple-element.75), channel_id=1, source_target_pairs={{0,4},{4,0},{8,12},{12,8},{1,5},{5,1},{9,13},{13,9},{2,6},{6,2},{1... | collective-permute-start | bytes 69128 | tf_op jit(solution)/shard_map/ppermute | solution.py:292
  23.7 0.1 shard_map.124.gains_ref.refs_2_
  23.8 0.4 shard_map.125
  24.2 0.8 %collective-permute-done.7.refs_0_ = bf16[16,720]{1,0:T(8,128)(2,1)S(1)} collective-permute-done((bf16[16,720]{1,0:T(8,128)(2,1)S(1)}, bf16[16,720]{1,0:T(8,128)(2,1)S(1)}, u32[]{:S(2)}, u32[]{:S(2)}) %collective-permute-start.7) | collective-permute-done | bytes 23072 | tf_op jit(solution)/shard_map/ppermute | solution.py:292
  25.0 2.7 %collective-permute-done.8.refs_1_ = bf16[16,720]{1,0:T(8,128)(2,1)S(1)} collective-permute-done((bf16[16,720]{1,0:T(8,128)(2,1)S(1)}, bf16[16,720]{1,0:T(8,128)(2,1)S(1)}, u32[]{:S(2)}, u32[]{:S(2)}) %collective-permute-start.8) | collective-permute-done | bytes 23072 | tf_op jit(solution)/shard_map/ppermute | solution.py:292
  27.7 0.6 %collective-permute-start.10 = (bf16[64,720]{1,0:T(8,128)(2,1)S(1)}, bf16[64,720]{1,0:T(8,128)(2,1)S(1)}, u32[]{:S(2)}, u32[]{:S(2)}) collective-permute-start(bf16[64,720]{1,0:T(8,128)(2,1)S(1)} %shard_map.126.block_ref), channel_id=1, source_target_pairs={{0,2},{1,3},{2,0},{3,1},{4,6},{5,7},{6,4},{7,5},{8,10},{9,11},{10,... | collective-permute-start | bytes 276488 | tf_op jit(solution)/shard_map/ppermute | solution.py:292
  28.3 0.5 %collective-permute-start.20 = (bf16[512,256]{1,0:T(8,128)(2,1)S(1)}, bf16[512,256]{1,0:T(8,128)(2,1)S(1)}, u32[]{:S(2)}, u32[]{:S(2)}) collective-permute-start(bf16[512,256]{1,0:T(8,128)(2,1)S(1)} %collective-permute-done.18.refs_1_), channel_id=1, source_target_pairs={{0,1},{1,0},{2,3},{3,2},{4,5},{5,4},{6,7},{7,6},{8,9},{9,8},{10,11... | collective-permute-start | bytes 786440 | tf_op jit(solution)/shard_map/ppermute | solution.py:292
  28.8 0.4 shard_map.128
  29.2 0.8 %shard_map.127.refs_1_ = f32[5,64,360]{2,1,0:T(8,128)S(1)} custom-call(bf16[64,720]{1,0:T(8,128)(2,1)S(1)} %shard_map.126.block_ref, f32[4,1,720]{2,1,0:T(1,128)S(1)} %shard_map.124.gains_ref.refs_2_, bf16[2,360,720]{2,1,0:T(8,128)(2,1)S(1)} %get-tuple-element.70.refs_0_.refs_3_, bf16[2,360,720]{2,1,0:T(8,128)(2,1)S(1)} %get-tuple-element.71.refs_1_.refs_4_, ...), custom_call_target="tpu_custom_call" | custom-call | flops 66355200 | bytes 2073600 | tf_op jit(solution)/shard_map/pallas_call | solution.py:398
  30.0 2.4 %collective-permute-done.10.refs_0_ = bf16[64,720]{1,0:T(8,128)(2,1)S(1)} collective-permute-done((bf16[64,720]{1,0:T(8,128)(2,1)S(1)}, bf16[64,720]{1,0:T(8,128)(2,1)S(1)}, u32[]{:S(2)}, u32[]{:S(2)}) %collective-permute-start.10) | collective-permute-done | bytes 92192 | tf_op jit(solution)/shard_map/ppermute | solution.py:292
  32.4 0.8 %shard_map.129 = (f32[5,64,360]{2,1,0:T(8,128)S(1)}, bf16[4,64,360]{2,1,0:T(8,128)(2,1)S(1)}, f32[64,128]{1,0:T(8,128)S(1)}) custom-call(bf16[64,720]{1,0:T(8,128)(2,1)S(1)} %collective-permute-done.10.refs_0_, f32[5,64,360]{2,1,0:T(8,128)S(1)} %shard_map.127.refs_1_, f32[4,1,720]{2,1,0:T(1,128)S(1)} %shard_map.124.gains_ref.refs_2_, ...), custom_call_target="tpu_custom_call" | custom-call | flops 66355200 | bytes 2073600 | tf_op jit(solution)/shard_map/pallas_call | solution.py:403
  33.2 0.1 collective-permute-start.11
  33.2 0.5 %collective-permute-start.12 = (f32[64,128]{1,0:T(8,128)S(1)}, f32[64,128]{1,0:T(8,128)S(1)}, u32[]{:S(2)}, u32[]{:S(2)}) collective-permute-start(f32[64,128]{1,0:T(8,128)S(1)} %get-tuple-element.92), channel_id=1, source_target_pairs={{0,1},{1,0},{2,3},{3,2},{4,5},{5,4},{6,7},{7,6},{8,9},{9,8},{10,11... | collective-permute-start | bytes 98312 | tf_op jit(solution)/shard_map/ppermute | solution.py:292
  33.7 1.0 %collective-permute-done.12.squares_ref = f32[64,128]{1,0:T(8,128)S(1)} collective-permute-done((f32[64,128]{1,0:T(8,128)S(1)}, f32[64,128]{1,0:T(8,128)S(1)}, u32[]{:S(2)}, u32[]{:S(2)}) %collective-permute-start.12) | collective-permute-done | bytes 32800 | tf_op jit(solution)/shard_map/ppermute | solution.py:292
  34.7 0.4 shard_map.130
  35.1 0.6 %collective-permute-start.13 = (bf16[32,720]{1,0:T(8,128)(2,1)S(1)}, bf16[32,720]{1,0:T(8,128)(2,1)S(1)}, u32[]{:S(2)}, u32[]{:S(2)}) collective-permute-start(bf16[32,720]{1,0:T(8,128)(2,1)S(1)} %get-tuple-element.96), channel_id=1, source_target_pairs={{0,2},{1,3},{2,0},{3,1},{4,6},{5,7},{6,4},{7,5},{8,10},{9,11},{10,... | collective-permute-start | bytes 138248 | tf_op jit(solution)/shard_map/ppermute | solution.py:292
  35.7 1.5 %collective-permute-start.16 = (bf16[32,720]{1,0:T(8,128)(2,1)S(1)}, bf16[32,720]{1,0:T(8,128)(2,1)S(1)}, u32[]{:S(2)}, u32[]{:S(2)}) collective-permute-start(bf16[32,720]{1,0:T(8,128)(2,1)S(1)} %get-tuple-element.100), channel_id=1, source_target_pairs={{0,2},{1,3},{2,0},{3,1},{4,6},{5,7},{6,4},{7,5},{8,10},{9,11},{10,... | collective-permute-start | bytes 138248 | tf_op jit(solution)/shard_map/ppermute | solution.py:292
  37.2 0.3 shard_map.131
  37.6 2.0 %collective-permute-done.13.refs_1_ = bf16[32,720]{1,0:T(8,128)(2,1)S(1)} collective-permute-done((bf16[32,720]{1,0:T(8,128)(2,1)S(1)}, bf16[32,720]{1,0:T(8,128)(2,1)S(1)}, u32[]{:S(2)}, u32[]{:S(2)}) %collective-permute-start.13) | collective-permute-done | bytes 46112 | tf_op jit(solution)/shard_map/ppermute | solution.py:292
  39.6 1.5 %collective-permute-start.14 = (bf16[16,720]{1,0:T(8,128)(2,1)S(1)}, bf16[16,720]{1,0:T(8,128)(2,1)S(1)}, u32[]{:S(2)}, u32[]{:S(2)}) collective-permute-start(bf16[16,720]{1,0:T(8,128)(2,1)S(1)} %get-tuple-element.97), channel_id=1, source_target_pairs={{0,12},{4,8},{8,4},{12,0},{1,13},{5,9},{9,5},{13,1},{2,14},{6,10},... | collective-permute-start | bytes 69128 | tf_op jit(solution)/shard_map/ppermute | solution.py:292
  41.2 0.6 %collective-permute-start.15 = (bf16[16,720]{1,0:T(8,128)(2,1)S(1)}, bf16[16,720]{1,0:T(8,128)(2,1)S(1)}, u32[]{:S(2)}, u32[]{:S(2)}) collective-permute-start(bf16[16,720]{1,0:T(8,128)(2,1)S(1)} %get-tuple-element.98), channel_id=1, source_target_pairs={{0,8},{4,12},{8,0},{12,4},{1,9},{5,13},{9,1},{13,5},{2,10},{6,14},... | collective-permute-start | bytes 69128 | tf_op jit(solution)/shard_map/ppermute | solution.py:292
  41.8 2.4 %collective-permute-start.17 = (bf16[16,720]{1,0:T(8,128)(2,1)S(1)}, bf16[16,720]{1,0:T(8,128)(2,1)S(1)}, u32[]{:S(2)}, u32[]{:S(2)}) collective-permute-start(bf16[16,720]{1,0:T(8,128)(2,1)S(1)} %get-tuple-element.101), channel_id=1, source_target_pairs={{0,4},{4,0},{8,12},{12,8},{1,5},{5,1},{9,13},{13,9},{2,6},{6,2},{1... | collective-permute-start | bytes 69128 | tf_op jit(solution)/shard_map/ppermute | solution.py:292
  44.2 0.9 %shard_map.134.refs_6_ = bf16[720,256]{1,0:T(8,128)(2,1)S(1)} custom-call(bf16[512,256]{1,0:T(8,128)(2,1)S(1)} %get-tuple-element.107.refs_0_, bf16[512,256]{1,0:T(8,128)(2,1)S(1)} %collective-permute-done.18.refs_1_, bf16[512,256]{1,0:T(8,128)(2,1)S(1)} %collective-permute-done.19.refs_2_, bf16[512,256]{1,0:T(8,128)(2,1)S(1)} %collective-permute-done.20.refs_3_, ...), custom_call_target="tpu_custom_call" | custom-call | flops 754974720 | bytes 2949120 | tf_op jit(solution)/shard_map/pallas_call | solution.py:419
  45.1 0.2 collective-permute-done.14.refs_0_
  45.3 0.6 %collective-permute-done.15.refs_1_ = bf16[16,720]{1,0:T(8,128)(2,1)S(1)} collective-permute-done((bf16[16,720]{1,0:T(8,128)(2,1)S(1)}, bf16[16,720]{1,0:T(8,128)(2,1)S(1)}, u32[]{:S(2)}, u32[]{:S(2)}) %collective-permute-start.15) | collective-permute-done | bytes 23072 | tf_op jit(solution)/shard_map/ppermute | solution.py:292
  45.9 0.2 collective-permute-done.17.refs_2_
  46.1 1.0 %shard_map.135 = bf16[720,256]{1,0:T(8,128)(2,1)} custom-call(bf16[16,720]{1,0:T(8,128)(2,1)S(1)} %collective-permute-done.14.refs_0_, bf16[16,720]{1,0:T(8,128)(2,1)S(1)} %collective-permute-done.15.refs_1_, bf16[16,720]{1,0:T(8,128)(2,1)S(1)} %collective-permute-done.17.refs_2_, bf16[16,720]{1,0:T(8,128)(2,1)S(1)} %get-tuple-element.102.refs_3_, ...), custom_call_target="tpu_custom_call" | custom-call | tf_op jit(solution)/shard_map/pallas_call | solution.py:436
  (21 shorter events, 0.1 us)
Async XLA Ops:
  0.0 10.4 %collective-permute-start.1 = (bf16[360,2880]{1,0:T(8,128)(2,1)}, bf16[360,2880]{1,0:T(8,128)(2,1)S(1)}, u32[]{:S(2)}, u32[]{:S(2)}) collective-permute-start(bf16[360,2880]{1,0:T(8,128)(2,1)} %bitcast.12), channel_id=1, source_target_pairs={{0,1},{1,0},{2,3},{3,2},{4,5},{5,4},{6,7},{7,6},{8,9},{9,8},{10,11... | collective-permute-start | bytes 6220808 | tf_op jit(solution)/shard_map/ppermute | solution.py:292
  0.5 9.9 %collective-permute-start.2 = (bf16[360,2880]{1,0:T(8,128)(2,1)}, bf16[360,2880]{1,0:T(8,128)(2,1)S(1)}, u32[]{:S(2)}, u32[]{:S(2)}) collective-permute-start(bf16[360,2880]{1,0:T(8,128)(2,1)} %bitcast.14), channel_id=1, source_target_pairs={{0,1},{1,0},{2,3},{3,2},{4,5},{5,4},{6,7},{7,6},{8,9},{9,8},{10,11... | collective-permute-start | bytes 6220808 | tf_op jit(solution)/shard_map/ppermute | solution.py:292
  0.5 10.0 %collective-permute-start.3 = (bf16[360,2880]{1,0:T(8,128)(2,1)}, bf16[360,2880]{1,0:T(8,128)(2,1)S(1)}, u32[]{:S(2)}, u32[]{:S(2)}) collective-permute-start(bf16[360,2880]{1,0:T(8,128)(2,1)} %bitcast.16), channel_id=1, source_target_pairs={{0,1},{1,0},{2,3},{3,2},{4,5},{5,4},{6,7},{7,6},{8,9},{9,8},{10,11... | collective-permute-start | bytes 6220808 | tf_op jit(solution)/shard_map/ppermute | solution.py:292
  1.8 7.4 %collective-permute-start = (bf16[128,256]{1,0:T(8,128)(2,1)S(1)}, bf16[128,256]{1,0:T(8,128)(2,1)S(1)}, u32[]{:S(2)}, u32[]{:S(2)}) collective-permute-start(bf16[128,256]{1,0:T(8,128)(2,1)S(1)} %slice.3), channel_id=1, source_target_pairs={{0,4},{4,8},{8,12},{12,0},{1,5},{5,9},{9,13},{13,1},{2,6},{6,10},{... | collective-permute-start | bytes 196616 | tf_op jit(solution)/shard_map/ppermute | solution.py:333
  4.4 9.0 %copy-start = (bf16[1,2880,360]{1,2,0:T(8,128)(2,1)S(1)}, bf16[1,2880,360]{1,2,0:T(8,128)(2,1)}, u32[]{:S(2)}) copy-start(bf16[1,2880,360]{1,2,0:T(8,128)(2,1)} %param.21) | copy-start | bytes 6220804
  10.5 5.3 %collective-permute-start.4 = (bf16[64,512]{1,0:T(8,128)(2,1)S(1)}, bf16[64,512]{1,0:T(8,128)(2,1)S(1)}, u32[]{:S(2)}, u32[]{:S(2)}) collective-permute-start(bf16[64,512]{1,0:T(8,128)(2,1)S(1)} %get-tuple-element.65.rows_ref), channel_id=1, source_target_pairs={{0,2},{1,3},{2,0},{3,1},{4,6},{5,7},{6,4},{7,5},{8,10},{9,11},{10,... | collective-permute-start | bytes 196616 | tf_op jit(solution)/shard_map/ppermute | solution.py:292
  13.4 2.4 %collective-permute-start.6 = (bf16[64,512]{1,0:T(8,128)(2,1)S(1)}, bf16[64,512]{1,0:T(8,128)(2,1)S(1)}, u32[]{:S(2)}, u32[]{:S(2)}) collective-permute-start(bf16[64,512]{1,0:T(8,128)(2,1)S(1)} %get-tuple-element.65.rows_ref), channel_id=1, source_target_pairs={{0,1},{1,0},{2,3},{3,2},{4,5},{5,4},{6,7},{7,6},{8,9},{9,8},{10,11... | collective-permute-start | bytes 196616 | tf_op jit(solution)/shard_map/ppermute | solution.py:292
  15.8 1.3 %collective-permute-start.5 = (bf16[64,512]{1,0:T(8,128)(2,1)S(1)}, bf16[64,512]{1,0:T(8,128)(2,1)S(1)}, u32[]{:S(2)}, u32[]{:S(2)}) collective-permute-start(bf16[64,512]{1,0:T(8,128)(2,1)S(1)} %collective-permute-done.4.refs_1_), channel_id=1, source_target_pairs={{0,1},{1,0},{2,3},{3,2},{4,5},{5,4},{6,7},{7,6},{8,9},{9,8},{10,11... | collective-permute-start | bytes 196616 | tf_op jit(solution)/shard_map/ppermute | solution.py:292
  16.4 7.4 %copy-start.3 = (f32[2880]{0:T(1024)S(1)}, f32[2880]{0:T(1024)}, u32[]{:S(2)}) copy-start(f32[2880]{0:T(1024)} %gain_ref.1) | copy-start | bytes 34564
  16.4 7.4 %copy-start.1 = (bf16[1,2880,360]{1,2,0:T(8,128)(2,1)S(1)}, bf16[1,2880,360]{1,2,0:T(8,128)(2,1)}, u32[]{:S(2)}) copy-start(bf16[1,2880,360]{1,2,0:T(8,128)(2,1)} %param.22) | copy-start | bytes 6220804
  17.4 10.9 %collective-permute-start.18 = (bf16[512,256]{1,0:T(8,128)(2,1)S(1)}, bf16[512,256]{1,0:T(8,128)(2,1)S(1)}, u32[]{:S(2)}, u32[]{:S(2)}) collective-permute-start(bf16[512,256]{1,0:T(8,128)(2,1)S(1)} %get-tuple-element.107.refs_0_), channel_id=1, source_target_pairs={{0,2},{1,3},{2,0},{3,1},{4,6},{5,7},{6,4},{7,5},{8,10},{9,11},{10,... | collective-permute-start | bytes 786440 | tf_op jit(solution)/shard_map/ppermute | solution.py:292
  19.4 5.6 %collective-permute-start.7 = (bf16[16,720]{1,0:T(8,128)(2,1)S(1)}, bf16[16,720]{1,0:T(8,128)(2,1)S(1)}, u32[]{:S(2)}, u32[]{:S(2)}) collective-permute-start(bf16[16,720]{1,0:T(8,128)(2,1)S(1)} %get-tuple-element.73), channel_id=1, source_target_pairs={{0,12},{4,8},{8,4},{12,0},{1,13},{5,9},{9,5},{13,1},{2,14},{6,10},... | collective-permute-start | bytes 69128 | tf_op jit(solution)/shard_map/ppermute | solution.py:292
  23.0 4.7 %collective-permute-start.8 = (bf16[16,720]{1,0:T(8,128)(2,1)S(1)}, bf16[16,720]{1,0:T(8,128)(2,1)S(1)}, u32[]{:S(2)}, u32[]{:S(2)}) collective-permute-start(bf16[16,720]{1,0:T(8,128)(2,1)S(1)} %get-tuple-element.74), channel_id=1, source_target_pairs={{0,8},{4,12},{8,0},{12,4},{1,9},{5,13},{9,1},{13,5},{2,10},{6,14},... | collective-permute-start | bytes 69128 | tf_op jit(solution)/shard_map/ppermute | solution.py:292
  23.0 4.7 %collective-permute-start.9 = (bf16[16,720]{1,0:T(8,128)(2,1)S(1)}, bf16[16,720]{1,0:T(8,128)(2,1)S(1)}, u32[]{:S(2)}, u32[]{:S(2)}) collective-permute-start(bf16[16,720]{1,0:T(8,128)(2,1)S(1)} %get-tuple-element.75), channel_id=1, source_target_pairs={{0,4},{4,0},{8,12},{12,8},{1,5},{5,1},{9,13},{13,9},{2,6},{6,2},{1... | collective-permute-start | bytes 69128 | tf_op jit(solution)/shard_map/ppermute | solution.py:292
  23.8 5.0 %copy-start.2 = (bf16[1,360,2880]{2,1,0:T(8,128)(2,1)S(1)}, bf16[1,360,2880]{2,1,0:T(8,128)(2,1)}, u32[]{:S(2)}) copy-start(bf16[1,360,2880]{2,1,0:T(8,128)(2,1)} %param.23) | copy-start | bytes 6220804
  27.7 4.7 %collective-permute-start.10 = (bf16[64,720]{1,0:T(8,128)(2,1)S(1)}, bf16[64,720]{1,0:T(8,128)(2,1)S(1)}, u32[]{:S(2)}, u32[]{:S(2)}) collective-permute-start(bf16[64,720]{1,0:T(8,128)(2,1)S(1)} %shard_map.126.block_ref), channel_id=1, source_target_pairs={{0,2},{1,3},{2,0},{3,1},{4,6},{5,7},{6,4},{7,5},{8,10},{9,11},{10,... | collective-permute-start | bytes 276488 | tf_op jit(solution)/shard_map/ppermute | solution.py:292
  28.3 15.9 %collective-permute-start.19 = (bf16[512,256]{1,0:T(8,128)(2,1)S(1)}, bf16[512,256]{1,0:T(8,128)(2,1)S(1)}, u32[]{:S(2)}, u32[]{:S(2)}) collective-permute-start(bf16[512,256]{1,0:T(8,128)(2,1)S(1)} %get-tuple-element.107.refs_0_), channel_id=1, source_target_pairs={{0,1},{1,0},{2,3},{3,2},{4,5},{5,4},{6,7},{7,6},{8,9},{9,8},{10,11... | collective-permute-start | bytes 786440 | tf_op jit(solution)/shard_map/ppermute | solution.py:292
  28.3 15.9 %collective-permute-start.20 = (bf16[512,256]{1,0:T(8,128)(2,1)S(1)}, bf16[512,256]{1,0:T(8,128)(2,1)S(1)}, u32[]{:S(2)}, u32[]{:S(2)}) collective-permute-start(bf16[512,256]{1,0:T(8,128)(2,1)S(1)} %collective-permute-done.18.refs_1_), channel_id=1, source_target_pairs={{0,1},{1,0},{2,3},{3,2},{4,5},{5,4},{6,7},{7,6},{8,9},{9,8},{10,11... | collective-permute-start | bytes 786440 | tf_op jit(solution)/shard_map/ppermute | solution.py:292
  33.2 1.6 %collective-permute-start.11 = (bf16[4,64,360]{2,1,0:T(8,128)(2,1)S(1)}, bf16[4,64,360]{2,1,0:T(8,128)(2,1)S(1)}, u32[]{:S(2)}, u32[]{:S(2)}) collective-permute-start(bf16[4,64,360]{2,1,0:T(8,128)(2,1)S(1)} %get-tuple-element.91), channel_id=1, source_target_pairs={{0,1},{1,0},{2,3},{3,2},{4,5},{5,4},{6,7},{7,6},{8,9},{9,8},{10,11... | collective-permute-start | bytes 552968 | tf_op jit(solution)/shard_map/ppermute | solution.py:292
  33.2 1.5 %collective-permute-start.12 = (f32[64,128]{1,0:T(8,128)S(1)}, f32[64,128]{1,0:T(8,128)S(1)}, u32[]{:S(2)}, u32[]{:S(2)}) collective-permute-start(f32[64,128]{1,0:T(8,128)S(1)} %get-tuple-element.92), channel_id=1, source_target_pairs={{0,1},{1,0},{2,3},{3,2},{4,5},{5,4},{6,7},{7,6},{8,9},{9,8},{10,11... | collective-permute-start | bytes 98312 | tf_op jit(solution)/shard_map/ppermute | solution.py:292
  35.1 4.5 %collective-permute-start.13 = (bf16[32,720]{1,0:T(8,128)(2,1)S(1)}, bf16[32,720]{1,0:T(8,128)(2,1)S(1)}, u32[]{:S(2)}, u32[]{:S(2)}) collective-permute-start(bf16[32,720]{1,0:T(8,128)(2,1)S(1)} %get-tuple-element.96), channel_id=1, source_target_pairs={{0,2},{1,3},{2,0},{3,1},{4,6},{5,7},{6,4},{7,5},{8,10},{9,11},{10,... | collective-permute-start | bytes 138248 | tf_op jit(solution)/shard_map/ppermute | solution.py:292
  35.7 6.1 %collective-permute-start.16 = (bf16[32,720]{1,0:T(8,128)(2,1)S(1)}, bf16[32,720]{1,0:T(8,128)(2,1)S(1)}, u32[]{:S(2)}, u32[]{:S(2)}) collective-permute-start(bf16[32,720]{1,0:T(8,128)(2,1)S(1)} %get-tuple-element.100), channel_id=1, source_target_pairs={{0,2},{1,3},{2,0},{3,1},{4,6},{5,7},{6,4},{7,5},{8,10},{9,11},{10,... | collective-permute-start | bytes 138248 | tf_op jit(solution)/shard_map/ppermute | solution.py:292
  39.6 5.7 %collective-permute-start.14 = (bf16[16,720]{1,0:T(8,128)(2,1)S(1)}, bf16[16,720]{1,0:T(8,128)(2,1)S(1)}, u32[]{:S(2)}, u32[]{:S(2)}) collective-permute-start(bf16[16,720]{1,0:T(8,128)(2,1)S(1)} %get-tuple-element.97), channel_id=1, source_target_pairs={{0,12},{4,8},{8,4},{12,0},{1,13},{5,9},{9,5},{13,1},{2,14},{6,10},... | collective-permute-start | bytes 69128 | tf_op jit(solution)/shard_map/ppermute | solution.py:292
  41.2 4.7 %collective-permute-start.15 = (bf16[16,720]{1,0:T(8,128)(2,1)S(1)}, bf16[16,720]{1,0:T(8,128)(2,1)S(1)}, u32[]{:S(2)}, u32[]{:S(2)}) collective-permute-start(bf16[16,720]{1,0:T(8,128)(2,1)S(1)} %get-tuple-element.98), channel_id=1, source_target_pairs={{0,8},{4,12},{8,0},{12,4},{1,9},{5,13},{9,1},{13,5},{2,10},{6,14},... | collective-permute-start | bytes 69128 | tf_op jit(solution)/shard_map/ppermute | solution.py:292
  41.8 4.3 %collective-permute-start.17 = (bf16[16,720]{1,0:T(8,128)(2,1)S(1)}, bf16[16,720]{1,0:T(8,128)(2,1)S(1)}, u32[]{:S(2)}, u32[]{:S(2)}) collective-permute-start(bf16[16,720]{1,0:T(8,128)(2,1)S(1)} %get-tuple-element.101), channel_id=1, source_target_pairs={{0,4},{4,0},{8,12},{12,8},{1,5},{5,1},{9,13},{13,9},{2,6},{6,2},{1... | collective-permute-start | bytes 69128 | tf_op jit(solution)/shard_map/ppermute | solution.py:292

commit v9 on v7

--- a/solution.py
+++ b/solution.py
@@ -279,7 +279,8 @@
     for k in range(live):
         rows_ref[lax.bitwise_xor(me, live - 1 - k)] = blocks[k][...]
     rows = rows_ref[...].reshape(live * CAP, -1)
-    mixed = dot(rows, mix_hi_ref[...], TN) + dot(rows, mix_lo_ref[...], TN)
+    mix = jnp.concatenate([mix_hi_ref[...], mix_lo_ref[...]], axis=0)
+    mixed = dot(jnp.concatenate([rows, rows], axis=0), mix, TN)
     out_ref[...] = (resid_ref[...].astype(jnp.float32) + mixed).astype(jnp.bfloat16)
 
 
@@ -393,9 +394,9 @@
     own = call(functools.partial(expert_own_kernel, steps), sums, n_in=4, **part)(stacked, gains, gates, ups)
     sibling_rows = from_sibling(stacked)
     downs = spread()(after(w_down[0], stacked))
-    chip_blocks = from_chips(after(attended, gates))
+    chip_blocks = from_chips(after(attended, outgoing[0]))
     blocks = [attended, *chip_blocks]
-    blocks += [from_sibling(b) for b in blocks]
+    blocks += [from_sibling(b) for b in after(blocks, stacked)]
     chip_rows = after(chip_rows, (own, downs))
     relayed_rows = [from_sibling(b) for b in chip_rows]
     chips = call(functools.partial(expert_more_kernel, places, steps), sums, n_in=steps + 6, **part)(
@@ -419,13 +420,13 @@
     sums = call(add_cores_kernel, (bf16(slots // 2, feats),) * (2 * steps), n_in=2)(
         kept, swap(given, "cuts", 1)
     )
-    returned = []
+    returned, added = [], []
     for half in range(2):
         parts = [sums[half]] + [swap(sums[2 * k + half], "cuts", CORES * k) for k in range(1, steps)]
-        blocks = call(functools.partial(add_chips_kernel, steps), (bf16(CAP, feats),) * (live // 2), n_in=steps)(
-            *parts
+        added = call(functools.partial(add_chips_kernel, steps), (bf16(CAP, feats),) * (live // 2), n_in=steps)(
+            *after(parts, added)
         )
-        for block in blocks:
+        for block in added:
             k = live - 1 - len(returned)
             returned.append(swap(block, "seq", k) if k else block)
     out = call(

time: 43.6 us -> 45.2 us (1.037)
  waiting for transfers between devices: 12.3 us -> 13.7 us
    ppermute x18, waiting for transfers between devices: 10.3 us -> 11.7 us  [swap(): lax.ppermute(block, axis, [(i, i ^ mask) for i in range(lax.axis_size(axi...]
  transfers between devices with their start and end apart: 19 -> 19, of which waited for: 10 -> 9; matrix products, arithmetic and copies ran while one was open for 0% -> 0% of each run, Pallas kernels for 20% -> 19%
where the time goes in v9:
time: 45.2 us; the launch traced here: 45 us
  starting transfers between devices  19.3 us (43%)
  waiting for transfers between devices  13.7 us (30%)
  Pallas kernels  11.1 us (25%)
  local copies, waits for them, and re-layouts  0.86 us (2%)
    ppermute x18, starting transfers between devices, swap(): lax.ppermute(block, axis, [(i, i ^ mask) for i in range(lax.axis_size(axi...  16.3 us
    ppermute x18, waiting for transfers between devices, swap(): lax.ppermute(block, axis, [(i, i ^ mask) for i in range(lax.axis_size(axi...  11.7 us
    ppermute x1, starting transfers between devices, shards(): rim = lax.ppermute(tail, 'seq', [(i, (i + 1) % size) for i in range(size)])  3.02 us
    pallas_call x1, Pallas kernels, shards(): call(functools.partial(first_kernel, live), (*(bf16(*a.shape) for a in lo...  2.3 us
    ppermute x1, waiting for transfers between devices, shards(): rim = lax.ppermute(tail, 'seq', [(i, (i + 1) % size) for i in range(size)])  1.96 us
    pallas_call x1, Pallas kernels, shards(): call(second_kernel, (bf16(head_rows, toks), bf16(slots, head_rows)), n_in...  1.18 us
    pallas_call x1, Pallas kernels, shards(): call(functools.partial(combine_kernel, live), bf16(feats, toks), n_in=liv...  1.05 us
    pallas_call x1, Pallas kernels, shards(): call(functools.partial(project_kernel, steps), bf16(feats, toks), n_in=cu...  0.93 us
  transfers between devices with their start and end apart: 19, of which 9 were waited for; matrix products, arithmetic and copies ran while one was open for 0% of the time, Pallas kernels for 19%

profile of v9, /device:TPU:0, one launch (start us, length us, event | category | flops | bytes accessed | tf_op | source)
XLA Modules:
  0.0 45.0 jit_solution(10082156024871608488)
XLA Ops:
  0.0 0.8 %slice.3 = bf16[128,256]{1,0:T(8,128)(2,1)S(1)} slice(bf16[256,256]{1,0:T(8,128)(2,1)} %refs_4_.1), slice={[128:256], [0:256]} | slice | bytes 131072 | tf_op jit(solution)/shard_map/slice | solution.py:328
  0.8 3.0 %collective-permute-start = (bf16[128,256]{1,0:T(8,128)(2,1)S(1)}, bf16[128,256]{1,0:T(8,128)(2,1)S(1)}, u32[]{:S(2)}, u32[]{:S(2)}) collective-permute-start(bf16[128,256]{1,0:T(8,128)(2,1)S(1)} %slice.3), channel_id=1, source_target_pairs={{0,4},{4,8},{8,12},{12,0},{1,5},{5,9},{9,13},{13,1},{2,6},{6,10},{... | collective-permute-start | bytes 196616 | tf_op jit(solution)/shard_map/ppermute | solution.py:329
  3.9 2.3 %shard_map.118 = (bf16[256,512]{1,0:T(8,128)(2,1)S(1)}, bf16[256,256]{1,0:T(8,128)(2,1)S(1)}, bf16[128,256]{1,0:T(8,128)(2,1)S(1)}, bf16[720,2048]{1,0:T(8,128)(...) custom-call(s32[4,256]{1,0:T(4,128)} %bitcast.17, ...), custom_call_target="tpu_custom_call" | custom-call | flops 134217728 | bytes 3579904 | tf_op jit(solution)/shard_map/pallas_call | solution.py:331
  6.2 2.0 %collective-permute-done.rim_ref = bf16[128,256]{1,0:T(8,128)(2,1)S(1)} collective-permute-done((bf16[128,256]{1,0:T(8,128)(2,1)S(1)}, bf16[128,256]{1,0:T(8,128)(2,1)S(1)}, u32[]{:S(2)}, u32[]{:S(2)}) %collective-permute-start) | collective-permute-done | bytes 65568 | tf_op jit(solution)/shard_map/ppermute | solution.py:329
  8.1 1.2 %shard_map.119 = (bf16[512,256]{1,0:T(8,128)(2,1)S(1)}, bf16[64,512]{1,0:T(8,128)(2,1)S(1)}) custom-call(bf16[256,512]{1,0:T(8,128)(2,1)S(1)} %get-tuple-element.53.q_ref, bf16[256,256]{1,0:T(8,128)(2,1)S(1)} %get-tuple-element.54.kv_ref, bf16[128,256]{1,0:T(8,128)(2,1)S(1)} %get-tuple-element.55.before_ref, ...), custom_call_target="tpu_custom_call" | custom-call | flops 67108864 | bytes 262144 | tf_op jit(solution)/shard_map/pallas_call | solution.py:350
  9.3 1.8 %collective-permute-start.1 = (bf16[64,512]{1,0:T(8,128)(2,1)S(1)}, bf16[64,512]{1,0:T(8,128)(2,1)S(1)}, u32[]{:S(2)}, u32[]{:S(2)}) collective-permute-start(bf16[64,512]{1,0:T(8,128)(2,1)S(1)} %get-tuple-element.59.rows_ref), channel_id=1, source_target_pairs={{0,2},{1,3},{2,0},{3,1},{4,6},{5,7},{6,4},{7,5},{8,10},{9,11},{10,... | collective-permute-start | bytes 196616 | tf_op jit(solution)/shard_map/ppermute | solution.py:288
  11.1 0.6 %shard_map.121.gates_ref.refs_6_.refs_5_ = bf16[4,360,720]{2,1,0:T(8,128)(2,1)S(1)} custom-call(bf16[360,2880]{1,0:T(8,128)(2,1)S(1)} %bitcast.12), custom_call_target="tpu_custom_call" | custom-call | bytes 4147200 | tf_op jit(solution)/shard_map/pallas_call | solution.py:369
  11.7 0.5 %shard_map.120.refs_2_ = f32[64,720]{1,0:T(8,128)S(1)} custom-call(bf16[64,512]{1,0:T(8,128)(2,1)S(1)} %get-tuple-element.59.rows_ref, bf16[720,2048]{1,0:T(8,128)(2,1)S(1)} %get-tuple-element.60.w_ref.refs_3_.refs_2_.refs_4_, bf16[720,256]{1,0:T(8,128)(2,1)S(1)} %get-tuple-element.61.residual_ref.refs_5_, bf16[64,256]{1,0:T(8,128)(2,1)S(1)} %get-tuple-element.58.placing_ref), custom_call_target="tpu_custom_call" | custom-call | flops 47185920 | bytes 737280 | tf_op jit(solution)/shard_map/pallas_call | solution.py:361
  12.2 1.5 %collective-permute-done.1.refs_1_ = bf16[64,512]{1,0:T(8,128)(2,1)S(1)} collective-permute-done((bf16[64,512]{1,0:T(8,128)(2,1)S(1)}, bf16[64,512]{1,0:T(8,128)(2,1)S(1)}, u32[]{:S(2)}, u32[]{:S(2)}) %collective-permute-start.1) | collective-permute-done | bytes 65568 | tf_op jit(solution)/shard_map/ppermute | solution.py:288
  13.7 0.0 collective-permute-start.2
  13.7 0.0 collective-permute-done.3.refs_0_
  13.7 0.6 %shard_map.122.refs_1_ = f32[64,720]{1,0:T(8,128)S(1)} custom-call(bf16[64,512]{1,0:T(8,128)(2,1)S(1)} %collective-permute-done.3.refs_0_, bf16[64,512]{1,0:T(8,128)(2,1)S(1)} %collective-permute-done.1.refs_1_, f32[64,720]{1,0:T(8,128)S(1)} %shard_map.120.refs_2_, bf16[720,2048]{1,0:T(8,128)(2,1)S(1)} %get-tuple-element.60.w_ref.refs_3_.refs_2_.refs_4_), custom_call_target="tpu_custom_call" | custom-call | flops 47185920 | bytes 737280 | tf_op jit(solution)/shard_map/pallas_call | solution.py:372
  14.2 0.0 copy-start.3
  14.3 0.0 copy-start.1
  14.3 0.6 %collective-permute-done.2.refs_0_ = bf16[64,512]{1,0:T(8,128)(2,1)S(1)} collective-permute-done((bf16[64,512]{1,0:T(8,128)(2,1)S(1)}, bf16[64,512]{1,0:T(8,128)(2,1)S(1)}, u32[]{:S(2)}, u32[]{:S(2)}) %collective-permute-start.2) | collective-permute-done | bytes 65568 | tf_op jit(solution)/shard_map/ppermute | solution.py:288
  14.9 0.4 shard_map.123
  15.3 1.8 %collective-permute-start.16 = (bf16[512,256]{1,0:T(8,128)(2,1)S(1)}, bf16[512,256]{1,0:T(8,128)(2,1)S(1)}, u32[]{:S(2)}, u32[]{:S(2)}) collective-permute-start(bf16[512,256]{1,0:T(8,128)(2,1)S(1)} %get-tuple-element.99.refs_0_), channel_id=1, source_target_pairs={{0,2},{1,3},{2,0},{3,1},{4,6},{5,7},{6,4},{7,5},{8,10},{9,11},{10,... | collective-permute-start | bytes 786440 | tf_op jit(solution)/shard_map/ppermute | solution.py:288
  17.1 1.8 %collective-permute-start.4 = (bf16[16,720]{1,0:T(8,128)(2,1)S(1)}, bf16[16,720]{1,0:T(8,128)(2,1)S(1)}, u32[]{:S(2)}, u32[]{:S(2)}) collective-permute-start(bf16[16,720]{1,0:T(8,128)(2,1)S(1)} %get-tuple-element.64), channel_id=1, source_target_pairs={{0,12},{4,8},{8,4},{12,0},{1,13},{5,9},{9,5},{13,1},{2,14},{6,10},... | collective-permute-start | bytes 69128 | tf_op jit(solution)/shard_map/ppermute | solution.py:288
  18.9 0.0 collective-permute-start.5
  18.9 2.6 %collective-permute-start.6 = (bf16[16,720]{1,0:T(8,128)(2,1)S(1)}, bf16[16,720]{1,0:T(8,128)(2,1)S(1)}, u32[]{:S(2)}, u32[]{:S(2)}) collective-permute-start(bf16[16,720]{1,0:T(8,128)(2,1)S(1)} %get-tuple-element.66), channel_id=1, source_target_pairs={{0,4},{4,0},{8,12},{12,8},{1,5},{5,1},{9,13},{13,9},{2,6},{6,2},{1... | collective-permute-start | bytes 69128 | tf_op jit(solution)/shard_map/ppermute | solution.py:288
  21.4 0.1 shard_map.125.gains_ref.refs_5_.refs_4_
  21.5 0.6 %shard_map.124.ups_ref.refs_7_.refs_6_ = bf16[4,360,720]{2,1,0:T(8,128)(2,1)S(1)} custom-call(bf16[360,2880]{1,0:T(8,128)(2,1)S(1)} %bitcast.13), custom_call_target="tpu_custom_call" | custom-call | bytes 4147200 | tf_op jit(solution)/shard_map/pallas_call | solution.py:385
  22.1 0.6 %collective-permute-done.4.refs_0_ = bf16[16,720]{1,0:T(8,128)(2,1)S(1)} collective-permute-done((bf16[16,720]{1,0:T(8,128)(2,1)S(1)}, bf16[16,720]{1,0:T(8,128)(2,1)S(1)}, u32[]{:S(2)}, u32[]{:S(2)}) %collective-permute-start.4) | collective-permute-done | bytes 23072 | tf_op jit(solution)/shard_map/ppermute | solution.py:288
  22.7 0.9 %collective-permute-done.5.refs_1_ = bf16[16,720]{1,0:T(8,128)(2,1)S(1)} collective-permute-done((bf16[16,720]{1,0:T(8,128)(2,1)S(1)}, bf16[16,720]{1,0:T(8,128)(2,1)S(1)}, u32[]{:S(2)}, u32[]{:S(2)}) %collective-permute-start.5) | collective-permute-done | bytes 23072 | tf_op jit(solution)/shard_map/ppermute | solution.py:288
  23.6 0.0 collective-permute-done.6.refs_2_
  23.6 0.6 %collective-permute-start.7 = (bf16[64,720]{1,0:T(8,128)(2,1)S(1)}, bf16[64,720]{1,0:T(8,128)(2,1)S(1)}, u32[]{:S(2)}, u32[]{:S(2)}) collective-permute-start(bf16[64,720]{1,0:T(8,128)(2,1)S(1)} %shard_map.126.block_ref), channel_id=1, source_target_pairs={{0,2},{1,3},{2,0},{3,1},{4,6},{5,7},{6,4},{7,5},{8,10},{9,11},{10,... | collective-permute-start | bytes 276488 | tf_op jit(solution)/shard_map/ppermute | solution.py:288
  24.2 0.6 %shard_map.128.refs_7_.downs_ref = bf16[4,360,720]{2,1,0:T(8,128)(2,1)S(1)} custom-call(bf16[360,2880]{1,0:T(8,128)(2,1)S(1)} %bitcast.14), custom_call_target="tpu_custom_call" | custom-call | bytes 4147200 | tf_op jit(solution)/shard_map/pallas_call | solution.py:396
  24.8 0.4 shard_map.127
  25.3 3.0 %collective-permute-done.7.refs_1_ = bf16[64,720]{1,0:T(8,128)(2,1)S(1)} collective-permute-done((bf16[64,720]{1,0:T(8,128)(2,1)S(1)}, bf16[64,720]{1,0:T(8,128)(2,1)S(1)}, u32[]{:S(2)}, u32[]{:S(2)}) %collective-permute-start.7) | collective-permute-done | bytes 92192 | tf_op jit(solution)/shard_map/ppermute | solution.py:288
  28.3 0.0 collective-permute-start.8
  28.3 0.5 %collective-permute-start.17 = (bf16[512,256]{1,0:T(8,128)(2,1)S(1)}, bf16[512,256]{1,0:T(8,128)(2,1)S(1)}, u32[]{:S(2)}, u32[]{:S(2)}) collective-permute-start(bf16[512,256]{1,0:T(8,128)(2,1)S(1)} %get-tuple-element.99.refs_0_), channel_id=1, source_target_pairs={{0,1},{1,0},{2,3},{3,2},{4,5},{5,4},{6,7},{7,6},{8,9},{9,8},{10,11... | collective-permute-start | bytes 786440 | tf_op jit(solution)/shard_map/ppermute | solution.py:288
  28.8 0.0 collective-permute-start.18
  28.8 0.8 %shard_map.129 = (f32[64,360]{1,0:T(8,128)S(1)}, f32[64,360]{1,0:T(8,128)S(1)}, f32[64,128]{1,0:T(8,128)S(1)}) custom-call(bf16[64,720]{1,0:T(8,128)(2,1)S(1)} %collective-permute-done.9.refs_0_, bf16[64,720]{1,0:T(8,128)(2,1)S(1)} %collective-permute-done.7.refs_1_, f32[64,360]{1,0:T(8,128)S(1)} %get-tuple-element.73.refs_2_, ...), custom_call_target="tpu_custom_call" | custom-call | flops 66355200 | bytes 1036800 | tf_op jit(solution)/shard_map/pallas_call | solution.py:402
  29.6 0.0 collective-permute-done.8.refs_0_
  29.6 0.7 %shard_map.130 = (bf16[2,64,720]{2,1,0:T(8,128)(2,1)S(1)}, bf16[64,360]{1,0:T(8,128)(2,1)S(1)}) custom-call(bf16[64,720]{1,0:T(8,128)(2,1)S(1)} %collective-permute-done.8.refs_0_, f32[64,360]{1,0:T(8,128)S(1)} %get-tuple-element.78.refs_1_, f32[64,360]{1,0:T(8,128)S(1)} %get-tuple-element.79.refs_2_, f32[64,128]{1,0:T(8,128)S(1)} %get-tuple-element.80.refs_3_, ...), custom_call_target="tpu_custom_call" | custom-call | flops 66355200 | bytes 1036800 | tf_op jit(solution)/shard_map/pallas_call | solution.py:405
  30.3 0.6 %collective-permute-start.10 = (bf16[2,64,720]{2,1,0:T(8,128)(2,1)S(1)}, bf16[2,64,720]{2,1,0:T(8,128)(2,1)S(1)}, u32[]{:S(2)}, u32[]{:S(2)}) collective-permute-start(bf16[2,64,720]{2,1,0:T(8,128)(2,1)S(1)} %get-tuple-element.82), channel_id=1, source_target_pairs={{0,1},{1,0},{2,3},{3,2},{4,5},{5,4},{6,7},{7,6},{8,9},{9,8},{10,11... | collective-permute-start | bytes 552968 | tf_op jit(solution)/shard_map/ppermute | solution.py:288
  30.9 0.3 shard_map.131.kept_ref
  31.2 0.7 %collective-permute-done.10.given_ref = bf16[2,64,720]{2,1,0:T(8,128)(2,1)S(1)} collective-permute-done((bf16[2,64,720]{2,1,0:T(8,128)(2,1)S(1)}, bf16[2,64,720]{2,1,0:T(8,128)(2,1)S(1)}, u32[]{:S(2)}, u32[]{:S(2)}) %collective-permute-start.10) | collective-permute-done | bytes 184352 | tf_op jit(solution)/shard_map/ppermute | solution.py:288
  32.0 0.1 shard_map.132
  32.0 0.6 %collective-permute-start.11 = (bf16[32,720]{1,0:T(8,128)(2,1)S(1)}, bf16[32,720]{1,0:T(8,128)(2,1)S(1)}, u32[]{:S(2)}, u32[]{:S(2)}) collective-permute-start(bf16[32,720]{1,0:T(8,128)(2,1)S(1)} %get-tuple-element.84), channel_id=1, source_target_pairs={{0,2},{1,3},{2,0},{3,1},{4,6},{5,7},{6,4},{7,5},{8,10},{9,11},{10,... | collective-permute-start | bytes 138248 | tf_op jit(solution)/shard_map/ppermute | solution.py:288
  32.7 1.5 %collective-permute-start.14 = (bf16[32,720]{1,0:T(8,128)(2,1)S(1)}, bf16[32,720]{1,0:T(8,128)(2,1)S(1)}, u32[]{:S(2)}, u32[]{:S(2)}) collective-permute-start(bf16[32,720]{1,0:T(8,128)(2,1)S(1)} %get-tuple-element.90), channel_id=1, source_target_pairs={{0,2},{1,3},{2,0},{3,1},{4,6},{5,7},{6,4},{7,5},{8,10},{9,11},{10,... | collective-permute-start | bytes 138248 | tf_op jit(solution)/shard_map/ppermute | solution.py:288
  34.1 2.5 %collective-permute-done.11.refs_1_ = bf16[32,720]{1,0:T(8,128)(2,1)S(1)} collective-permute-done((bf16[32,720]{1,0:T(8,128)(2,1)S(1)}, bf16[32,720]{1,0:T(8,128)(2,1)S(1)}, u32[]{:S(2)}, u32[]{:S(2)}) %collective-permute-start.11) | collective-permute-done | bytes 46112 | tf_op jit(solution)/shard_map/ppermute | solution.py:288
  36.7 2.1 %collective-permute-start.12 = (bf16[16,720]{1,0:T(8,128)(2,1)S(1)}, bf16[16,720]{1,0:T(8,128)(2,1)S(1)}, u32[]{:S(2)}, u32[]{:S(2)}) collective-permute-start(bf16[16,720]{1,0:T(8,128)(2,1)S(1)} %get-tuple-element.87), channel_id=1, source_target_pairs={{0,12},{4,8},{8,4},{12,0},{1,13},{5,9},{9,5},{13,1},{2,14},{6,10},... | collective-permute-start | bytes 69128 | tf_op jit(solution)/shard_map/ppermute | solution.py:288
  38.8 1.1 %collective-permute-start.13 = (bf16[16,720]{1,0:T(8,128)(2,1)S(1)}, bf16[16,720]{1,0:T(8,128)(2,1)S(1)}, u32[]{:S(2)}, u32[]{:S(2)}) collective-permute-start(bf16[16,720]{1,0:T(8,128)(2,1)S(1)} %get-tuple-element.88), channel_id=1, source_target_pairs={{0,8},{4,12},{8,0},{12,4},{1,9},{5,13},{9,1},{13,5},{2,10},{6,14},... | collective-permute-start | bytes 69128 | tf_op jit(solution)/shard_map/ppermute | solution.py:288
  39.9 1.3 %collective-permute-start.15 = (bf16[16,720]{1,0:T(8,128)(2,1)S(1)}, bf16[16,720]{1,0:T(8,128)(2,1)S(1)}, u32[]{:S(2)}, u32[]{:S(2)}) collective-permute-start(bf16[16,720]{1,0:T(8,128)(2,1)S(1)} %get-tuple-element.93), channel_id=1, source_target_pairs={{0,4},{4,0},{8,12},{12,8},{1,5},{5,1},{9,13},{13,9},{2,6},{6,2},{1... | collective-permute-start | bytes 69128 | tf_op jit(solution)/shard_map/ppermute | solution.py:288
  41.2 0.9 %shard_map.135.refs_6_ = bf16[720,256]{1,0:T(8,128)(2,1)S(1)} custom-call(bf16[512,256]{1,0:T(8,128)(2,1)S(1)} %get-tuple-element.99.refs_0_, bf16[512,256]{1,0:T(8,128)(2,1)S(1)} %collective-permute-done.16.refs_1_, bf16[512,256]{1,0:T(8,128)(2,1)S(1)} %collective-permute-done.17.refs_2_, bf16[512,256]{1,0:T(8,128)(2,1)S(1)} %collective-permute-done.18.refs_3_, ...), custom_call_target="tpu_custom_call" | custom-call | flops 754974720 | bytes 2949120 | tf_op jit(solution)/shard_map/pallas_call | solution.py:412
  42.2 1.8 %collective-permute-done.15.refs_2_ = bf16[16,720]{1,0:T(8,128)(2,1)S(1)} collective-permute-done((bf16[16,720]{1,0:T(8,128)(2,1)S(1)}, bf16[16,720]{1,0:T(8,128)(2,1)S(1)}, u32[]{:S(2)}, u32[]{:S(2)}) %collective-permute-start.15) | collective-permute-done | bytes 23072 | tf_op jit(solution)/shard_map/ppermute | solution.py:288
  44.0 1.0 %shard_map.136 = bf16[720,256]{1,0:T(8,128)(2,1)} custom-call(bf16[16,720]{1,0:T(8,128)(2,1)S(1)} %collective-permute-done.12.refs_0_, bf16[16,720]{1,0:T(8,128)(2,1)S(1)} %collective-permute-done.13.refs_1_, bf16[16,720]{1,0:T(8,128)(2,1)S(1)} %collective-permute-done.15.refs_2_, bf16[16,720]{1,0:T(8,128)(2,1)S(1)} %get-tuple-element.94.refs_3_, ...), custom_call_target="tpu_custom_call" | custom-call | tf_op jit(solution)/shard_map/pallas_call | solution.py:432
  (18 shorter events, 0.1 us)
Async XLA Ops:
  0.8 7.3 %collective-permute-start = (bf16[128,256]{1,0:T(8,128)(2,1)S(1)}, bf16[128,256]{1,0:T(8,128)(2,1)S(1)}, u32[]{:S(2)}, u32[]{:S(2)}) collective-permute-start(bf16[128,256]{1,0:T(8,128)(2,1)S(1)} %slice.3), channel_id=1, source_target_pairs={{0,4},{4,8},{8,12},{12,0},{1,5},{5,9},{9,13},{13,1},{2,6},{6,10},{... | collective-permute-start | bytes 196616 | tf_op jit(solution)/shard_map/ppermute | solution.py:329
  3.9 7.2 %copy-start = (bf16[1,2880,360]{1,2,0:T(8,128)(2,1)S(1)}, bf16[1,2880,360]{1,2,0:T(8,128)(2,1)}, u32[]{:S(2)}) copy-start(bf16[1,2880,360]{1,2,0:T(8,128)(2,1)} %param.21) | copy-start | bytes 6220804
  9.3 4.3 %collective-permute-start.1 = (bf16[64,512]{1,0:T(8,128)(2,1)S(1)}, bf16[64,512]{1,0:T(8,128)(2,1)S(1)}, u32[]{:S(2)}, u32[]{:S(2)}) collective-permute-start(bf16[64,512]{1,0:T(8,128)(2,1)S(1)} %get-tuple-element.59.rows_ref), channel_id=1, source_target_pairs={{0,2},{1,3},{2,0},{3,1},{4,6},{5,7},{6,4},{7,5},{8,10},{9,11},{10,... | collective-permute-start | bytes 196616 | tf_op jit(solution)/shard_map/ppermute | solution.py:288
  11.1 2.6 %collective-permute-start.3 = (bf16[64,512]{1,0:T(8,128)(2,1)S(1)}, bf16[64,512]{1,0:T(8,128)(2,1)S(1)}, u32[]{:S(2)}, u32[]{:S(2)}) collective-permute-start(bf16[64,512]{1,0:T(8,128)(2,1)S(1)} %get-tuple-element.59.rows_ref), channel_id=1, source_target_pairs={{0,1},{1,0},{2,3},{3,2},{4,5},{5,4},{6,7},{7,6},{8,9},{9,8},{10,11... | collective-permute-start | bytes 196616 | tf_op jit(solution)/shard_map/ppermute | solution.py:288
  13.7 1.3 %collective-permute-start.2 = (bf16[64,512]{1,0:T(8,128)(2,1)S(1)}, bf16[64,512]{1,0:T(8,128)(2,1)S(1)}, u32[]{:S(2)}, u32[]{:S(2)}) collective-permute-start(bf16[64,512]{1,0:T(8,128)(2,1)S(1)} %collective-permute-done.1.refs_1_), channel_id=1, source_target_pairs={{0,1},{1,0},{2,3},{3,2},{4,5},{5,4},{6,7},{7,6},{8,9},{9,8},{10,11... | collective-permute-start | bytes 196616 | tf_op jit(solution)/shard_map/ppermute | solution.py:288
  14.2 7.2 %copy-start.3 = (f32[2880]{0:T(1024)S(1)}, f32[2880]{0:T(1024)}, u32[]{:S(2)}) copy-start(f32[2880]{0:T(1024)} %gain_ref.1) | copy-start | bytes 34564
  14.3 7.3 %copy-start.1 = (bf16[1,2880,360]{1,2,0:T(8,128)(2,1)S(1)}, bf16[1,2880,360]{1,2,0:T(8,128)(2,1)}, u32[]{:S(2)}) copy-start(bf16[1,2880,360]{1,2,0:T(8,128)(2,1)} %param.22) | copy-start | bytes 6220804
  15.3 13.0 %collective-permute-start.16 = (bf16[512,256]{1,0:T(8,128)(2,1)S(1)}, bf16[512,256]{1,0:T(8,128)(2,1)S(1)}, u32[]{:S(2)}, u32[]{:S(2)}) collective-permute-start(bf16[512,256]{1,0:T(8,128)(2,1)S(1)} %get-tuple-element.99.refs_0_), channel_id=1, source_target_pairs={{0,2},{1,3},{2,0},{3,1},{4,6},{5,7},{6,4},{7,5},{8,10},{9,11},{10,... | collective-permute-start | bytes 786440 | tf_op jit(solution)/shard_map/ppermute | solution.py:288
  17.1 5.6 %collective-permute-start.4 = (bf16[16,720]{1,0:T(8,128)(2,1)S(1)}, bf16[16,720]{1,0:T(8,128)(2,1)S(1)}, u32[]{:S(2)}, u32[]{:S(2)}) collective-permute-start(bf16[16,720]{1,0:T(8,128)(2,1)S(1)} %get-tuple-element.64), channel_id=1, source_target_pairs={{0,12},{4,8},{8,4},{12,0},{1,13},{5,9},{9,5},{13,1},{2,14},{6,10},... | collective-permute-start | bytes 69128 | tf_op jit(solution)/shard_map/ppermute | solution.py:288
  18.9 4.7 %collective-permute-start.5 = (bf16[16,720]{1,0:T(8,128)(2,1)S(1)}, bf16[16,720]{1,0:T(8,128)(2,1)S(1)}, u32[]{:S(2)}, u32[]{:S(2)}) collective-permute-start(bf16[16,720]{1,0:T(8,128)(2,1)S(1)} %get-tuple-element.65), channel_id=1, source_target_pairs={{0,8},{4,12},{8,0},{12,4},{1,9},{5,13},{9,1},{13,5},{2,10},{6,14},... | collective-permute-start | bytes 69128 | tf_op jit(solution)/shard_map/ppermute | solution.py:288
  18.9 4.7 %collective-permute-start.6 = (bf16[16,720]{1,0:T(8,128)(2,1)S(1)}, bf16[16,720]{1,0:T(8,128)(2,1)S(1)}, u32[]{:S(2)}, u32[]{:S(2)}) collective-permute-start(bf16[16,720]{1,0:T(8,128)(2,1)S(1)} %get-tuple-element.66), channel_id=1, source_target_pairs={{0,4},{4,0},{8,12},{12,8},{1,5},{5,1},{9,13},{13,9},{2,6},{6,2},{1... | collective-permute-start | bytes 69128 | tf_op jit(solution)/shard_map/ppermute | solution.py:288
  21.5 2.7 %copy-start.2 = (bf16[1,360,2880]{2,1,0:T(8,128)(2,1)S(1)}, bf16[1,360,2880]{2,1,0:T(8,128)(2,1)}, u32[]{:S(2)}) copy-start(bf16[1,360,2880]{2,1,0:T(8,128)(2,1)} %param.23) | copy-start | bytes 6220804
  23.6 4.7 %collective-permute-start.7 = (bf16[64,720]{1,0:T(8,128)(2,1)S(1)}, bf16[64,720]{1,0:T(8,128)(2,1)S(1)}, u32[]{:S(2)}, u32[]{:S(2)}) collective-permute-start(bf16[64,720]{1,0:T(8,128)(2,1)S(1)} %shard_map.126.block_ref), channel_id=1, source_target_pairs={{0,2},{1,3},{2,0},{3,1},{4,6},{5,7},{6,4},{7,5},{8,10},{9,11},{10,... | collective-permute-start | bytes 276488 | tf_op jit(solution)/shard_map/ppermute | solution.py:288
  24.2 4.6 %collective-permute-start.9 = (bf16[64,720]{1,0:T(8,128)(2,1)S(1)}, bf16[64,720]{1,0:T(8,128)(2,1)S(1)}, u32[]{:S(2)}, u32[]{:S(2)}) collective-permute-start(bf16[64,720]{1,0:T(8,128)(2,1)S(1)} %shard_map.126.block_ref), channel_id=1, source_target_pairs={{0,1},{1,0},{2,3},{3,2},{4,5},{5,4},{6,7},{7,6},{8,9},{9,8},{10,11... | collective-permute-start | bytes 276488 | tf_op jit(solution)/shard_map/ppermute | solution.py:288
  28.3 1.3 %collective-permute-start.8 = (bf16[64,720]{1,0:T(8,128)(2,1)S(1)}, bf16[64,720]{1,0:T(8,128)(2,1)S(1)}, u32[]{:S(2)}, u32[]{:S(2)}) collective-permute-start(bf16[64,720]{1,0:T(8,128)(2,1)S(1)} %collective-permute-done.7.refs_1_), channel_id=1, source_target_pairs={{0,1},{1,0},{2,3},{3,2},{4,5},{5,4},{6,7},{7,6},{8,9},{9,8},{10,11... | collective-permute-start | bytes 276488 | tf_op jit(solution)/shard_map/ppermute | solution.py:288
  28.3 12.9 %collective-permute-start.17 = (bf16[512,256]{1,0:T(8,128)(2,1)S(1)}, bf16[512,256]{1,0:T(8,128)(2,1)S(1)}, u32[]{:S(2)}, u32[]{:S(2)}) collective-permute-start(bf16[512,256]{1,0:T(8,128)(2,1)S(1)} %get-tuple-element.99.refs_0_), channel_id=1, source_target_pairs={{0,1},{1,0},{2,3},{3,2},{4,5},{5,4},{6,7},{7,6},{8,9},{9,8},{10,11... | collective-permute-start | bytes 786440 | tf_op jit(solution)/shard_map/ppermute | solution.py:288
  28.8 12.4 %collective-permute-start.18 = (bf16[512,256]{1,0:T(8,128)(2,1)S(1)}, bf16[512,256]{1,0:T(8,128)(2,1)S(1)}, u32[]{:S(2)}, u32[]{:S(2)}) collective-permute-start(bf16[512,256]{1,0:T(8,128)(2,1)S(1)} %collective-permute-done.16.refs_1_), channel_id=1, source_target_pairs={{0,1},{1,0},{2,3},{3,2},{4,5},{5,4},{6,7},{7,6},{8,9},{9,8},{10,11... | collective-permute-start | bytes 786440 | tf_op jit(solution)/shard_map/ppermute | solution.py:288
  30.3 1.6 %collective-permute-start.10 = (bf16[2,64,720]{2,1,0:T(8,128)(2,1)S(1)}, bf16[2,64,720]{2,1,0:T(8,128)(2,1)S(1)}, u32[]{:S(2)}, u32[]{:S(2)}) collective-permute-start(bf16[2,64,720]{2,1,0:T(8,128)(2,1)S(1)} %get-tuple-element.82), channel_id=1, source_target_pairs={{0,1},{1,0},{2,3},{3,2},{4,5},{5,4},{6,7},{7,6},{8,9},{9,8},{10,11... | collective-permute-start | bytes 552968 | tf_op jit(solution)/shard_map/ppermute | solution.py:288
  32.0 4.6 %collective-permute-start.11 = (bf16[32,720]{1,0:T(8,128)(2,1)S(1)}, bf16[32,720]{1,0:T(8,128)(2,1)S(1)}, u32[]{:S(2)}, u32[]{:S(2)}) collective-permute-start(bf16[32,720]{1,0:T(8,128)(2,1)S(1)} %get-tuple-element.84), channel_id=1, source_target_pairs={{0,2},{1,3},{2,0},{3,1},{4,6},{5,7},{6,4},{7,5},{8,10},{9,11},{10,... | collective-permute-start | bytes 138248 | tf_op jit(solution)/shard_map/ppermute | solution.py:288
  32.7 7.2 %collective-permute-start.14 = (bf16[32,720]{1,0:T(8,128)(2,1)S(1)}, bf16[32,720]{1,0:T(8,128)(2,1)S(1)}, u32[]{:S(2)}, u32[]{:S(2)}) collective-permute-start(bf16[32,720]{1,0:T(8,128)(2,1)S(1)} %get-tuple-element.90), channel_id=1, source_target_pairs={{0,2},{1,3},{2,0},{3,1},{4,6},{5,7},{6,4},{7,5},{8,10},{9,11},{10,... | collective-permute-start | bytes 138248 | tf_op jit(solution)/shard_map/ppermute | solution.py:288
  36.7 7.3 %collective-permute-start.12 = (bf16[16,720]{1,0:T(8,128)(2,1)S(1)}, bf16[16,720]{1,0:T(8,128)(2,1)S(1)}, u32[]{:S(2)}, u32[]{:S(2)}) collective-permute-start(bf16[16,720]{1,0:T(8,128)(2,1)S(1)} %get-tuple-element.87), channel_id=1, source_target_pairs={{0,12},{4,8},{8,4},{12,0},{1,13},{5,9},{9,5},{13,1},{2,14},{6,10},... | collective-permute-start | bytes 69128 | tf_op jit(solution)/shard_map/ppermute | solution.py:288
  38.8 5.2 %collective-permute-start.13 = (bf16[16,720]{1,0:T(8,128)(2,1)S(1)}, bf16[16,720]{1,0:T(8,128)(2,1)S(1)}, u32[]{:S(2)}, u32[]{:S(2)}) collective-permute-start(bf16[16,720]{1,0:T(8,128)(2,1)S(1)} %get-tuple-element.88), channel_id=1, source_target_pairs={{0,8},{4,12},{8,0},{12,4},{1,9},{5,13},{9,1},{13,5},{2,10},{6,14},... | collective-permute-start | bytes 69128 | tf_op jit(solution)/shard_map/ppermute | solution.py:288
  39.9 4.1 %collective-permute-start.15 = (bf16[16,720]{1,0:T(8,128)(2,1)S(1)}, bf16[16,720]{1,0:T(8,128)(2,1)S(1)}, u32[]{:S(2)}, u32[]{:S(2)}) collective-permute-start(bf16[16,720]{1,0:T(8,128)(2,1)S(1)} %get-tuple-element.93), channel_id=1, source_target_pairs={{0,4},{4,0},{8,12},{12,8},{1,5},{5,1},{9,13},{13,9},{2,6},{6,2},{1... | collective-permute-start | bytes 69128 | tf_op jit(solution)/shard_map/ppermute | solution.py:288

commit v10 on v7

--- a/solution.py
+++ b/solution.py
@@ -49,44 +49,59 @@
     return jax.ShapeDtypeStruct(shape, jnp.bfloat16)
 
 
-def visible():
-    key = lax.broadcasted_iota(jnp.int32, (SPAN, KEYS_SEEN), 0)
-    query = lax.broadcasted_iota(jnp.int32, (SPAN, KEYS_SEEN), 1)
-    return (key > query) & (key <= query + KEYS_SEEN)
-
-
-def attend_block(pairs, both, sinks, allowed):
+def split_pair(both):
     both = both.astype(jnp.float32)
     low = lax.broadcasted_iota(jnp.int32, both.shape, 1) < HEAD_SIZE
     turned = pltpu.roll(both, HEAD_SIZE, 1)
     keys = jnp.concatenate([jnp.where(low, both, 0.0), jnp.where(low, 0.0, turned)], axis=0)
     values = jnp.concatenate([jnp.where(low, turned, 0.0), jnp.where(low, 0.0, both)], axis=0)
-    keys, values = keys.astype(jnp.bfloat16), values.astype(jnp.bfloat16)
+    return keys.astype(jnp.bfloat16), values.astype(jnp.bfloat16)
+
+
+def score(pairs, keys, allowed):
     scores = dot(keys, jnp.concatenate(pairs, axis=0), NT) * (HEAD_SIZE**-0.5 * math.log2(math.e))
     allowed = jnp.concatenate([allowed] * len(pairs), axis=1)
+    span = allowed.shape[0]
+    return [jnp.where(allowed, scores[i * span : (i + 1) * span], -jnp.inf) for i in range(2)]
+
+
+def sink_row(sinks, i, pairs):
+    return jnp.concatenate([sinks[2 * p + i] for p in range(pairs)], axis=1)
+
+
+def attend_block(pairs, both, sinks, allowed):
+    keys, values = split_pair(both)
     probs = []
-    for i in range(2):
-        sink = jnp.concatenate([sinks[2 * p + i] for p in range(len(pairs))], axis=1)
-        part = jnp.where(allowed, scores[i * SPAN : (i + 1) * SPAN], -jnp.inf)
+    for i, part in enumerate(score(pairs, keys, allowed)):
+        sink = sink_row(sinks, i, len(pairs))
         peak = jnp.maximum(jnp.max(part, axis=0, keepdims=True), sink)
         terms = jnp.exp2(part - peak)
         denom = jnp.sum(terms, axis=0, keepdims=True) + jnp.exp2(sink - peak)
         probs.append((terms * (1.0 / denom)).astype(jnp.bfloat16))
-    mixed = dot(values, jnp.concatenate(probs, axis=0), TN).astype(jnp.bfloat16)
-    return [mixed[:, p * KEYS_SEEN : (p + 1) * KEYS_SEEN] for p in range(len(pairs))]
-
-
-def attend_tokens(block, q_ref, rows_of, sinks, out_ref, lanes):
-    groups = len(rows_of)
+    return dot(values, jnp.concatenate(probs, axis=0), TN).astype(jnp.bfloat16)
+
+
+def group_queries(q_ref, g, groups, block):
     per_group = q_ref.shape[1] // PAIR // groups
-    allowed = visible()
+    first = g * per_group
     toks = slice(block * KEYS_SEEN, (block + 1) * KEYS_SEEN)
-    for g, both in enumerate(rows_of):
-        first = g * per_group
-        pairs = [q_ref[toks, (first + p) * PAIR : (first + p + 1) * PAIR] for p in range(per_group)]
-        outs = attend_block(pairs, both, sinks[2 * first : 2 * (first + per_group)], allowed)
-        for p, out in enumerate(outs):
-            out_ref[(first + p) * PAIR : (first + p + 1) * PAIR, lanes] = out
+    pairs = [q_ref[toks, (first + p) * PAIR : (first + p + 1) * PAIR] for p in range(per_group)]
+    return first, pairs
+
+
+def store_pairs(mixed, first, out_ref, lanes):
+    for p in range(mixed.shape[1] // KEYS_SEEN):
+        rows = slice((first + p) * PAIR, (first + p + 1) * PAIR)
+        out_ref[rows, lanes] = mixed[:, p * KEYS_SEEN : (p + 1) * KEYS_SEEN]
+
+
+def key_query(span):
+    key = lax.broadcasted_iota(jnp.int32, (span, KEYS_SEEN), 0)
+    return key, lax.broadcasted_iota(jnp.int32, (span, KEYS_SEEN), 1)
+
+
+def per_head(pair):
+    return jnp.concatenate([jnp.broadcast_to(row, (HEAD_SIZE, row.shape[1])) for row in pair], axis=0)
 
 
 def fill_tables(live, ids, weights, placing_ref, mix_hi_ref, mix_lo_ref):
@@ -112,7 +127,8 @@
 
 def first_kernel(live, *refs):
     loaded, held = refs[:8], refs[8:13]
-    placing_ref, mix_hi_ref, mix_lo_ref, sinks_out, late_ref, ids_ref, weights_ref, sinks_ref, sems = refs[13:]
+    placing_ref, mix_hi_ref, mix_lo_ref, sinks_out, late_ref, rows_ref, mixed_ref, peaks_ref, sums_ref = refs[13:22]
+    ids_ref, weights_ref, sinks_ref, sems = refs[22:]
     targets = (ids_ref, weights_ref, sinks_ref, *held)
     copies = [pltpu.make_async_copy(*pair, sems.at[i]) for i, pair in enumerate(zip(loaded, targets))]
     for copy in copies:
@@ -127,26 +143,57 @@
     sinks = [jnp.full((1, KEYS_SEEN), sinks_ref[h], jnp.float32) * math.log2(math.e) for h in range(heads)]
     sinks_out[...] = jnp.concatenate(sinks, axis=0)
     groups = kv_ref.shape[1] // PAIR
+    key, query = key_query(SPAN)
+    allowed = (key > query) & (key <= query + KEYS_SEEN)
     for b in range(1, q_ref.shape[0] // KEYS_SEEN):
         span = slice((b - 1) * KEYS_SEEN, (b + 1) * KEYS_SEEN)
-        rows_of = [kv_ref[span, g * PAIR : (g + 1) * PAIR] for g in range(groups)]
-        attend_tokens(b, q_ref, rows_of, sinks, late_ref, slice((b - 1) * KEYS_SEEN, b * KEYS_SEEN))
+        for g in range(groups):
+            first, pairs = group_queries(q_ref, g, groups, b)
+            part = sinks[2 * first : 2 * (first + len(pairs))]
+            mixed = attend_block(pairs, kv_ref[span, g * PAIR : (g + 1) * PAIR], part, allowed)
+            store_pairs(mixed, first, late_ref, slice((b - 1) * KEYS_SEEN, b * KEYS_SEEN))
+    key, query = key_query(KEYS_SEEN)
+    for g in range(groups):
+        _, pairs = group_queries(q_ref, g, groups, 0)
+        keys, values = split_pair(kv_ref[:KEYS_SEEN, g * PAIR : (g + 1) * PAIR])
+        terms = []
+        for i, part in enumerate(score(pairs, keys, key <= query)):
+            peak = jnp.max(part, axis=0, keepdims=True)
+            terms.append(jnp.exp2(part - peak))
+            peaks_ref[2 * g + i : 2 * g + i + 1] = peak
+            sums_ref[2 * g + i : 2 * g + i + 1] = jnp.sum(terms[-1], axis=0, keepdims=True)
+        mixed_ref[g] = dot(values, jnp.concatenate(terms, axis=0).astype(jnp.bfloat16), TN)
+    rows_ref[...] = dot(placing_ref[:, KEYS_SEEN:], late_ref[...], NT)
     for copy in copies[5:]:
         copy.wait()
 
 
-def second_kernel(q_ref, kv_ref, before_ref, rim_ref, sinks_ref, late_ref, placing_ref, all_ref, rows_ref):
-    first = lax.axis_index("seq") == 0
-    rim = jnp.where(first, before_ref[...], rim_ref[...])
-    groups = kv_ref.shape[1] // PAIR
-    rows_of = []
+def second_kernel(q_ref, before_ref, rim_ref, sinks_ref, late_ref, placing_ref, *refs):
+    late_rows_ref, mixed_ref, peaks_ref, sums_ref, all_ref, rows_ref = refs
+    rim = jnp.where(lax.axis_index("seq") == 0, before_ref[...], rim_ref[...])
+    groups = mixed_ref.shape[0]
+    key, query = key_query(KEYS_SEEN)
     for g in range(groups):
-        lanes = slice(g * PAIR, (g + 1) * PAIR)
-        rows_of.append(jnp.concatenate([rim[:, lanes], kv_ref[:KEYS_SEEN, lanes]], axis=0))
-    sinks = [sinks_ref[h : h + 1] for h in range(sinks_ref.shape[0])]
-    attend_tokens(0, q_ref, rows_of, sinks, all_ref, slice(0, KEYS_SEEN))
+        first, pairs = group_queries(q_ref, g, groups, 0)
+        sinks = [sinks_ref[h : h + 1] for h in range(2 * first, 2 * (first + len(pairs)))]
+        keys, values = split_pair(rim[:, g * PAIR : (g + 1) * PAIR])
+        terms, scales, inverses = [], [], []
+        for i, part in enumerate(score(pairs, keys, key > query)):
+            sink = sink_row(sinks, i, len(pairs))
+            own_peak = peaks_ref[2 * g + i : 2 * g + i + 1]
+            peak = jnp.maximum(jnp.max(part, axis=0, keepdims=True), jnp.maximum(own_peak, sink))
+            scale = jnp.exp2(own_peak - peak)
+            terms.append(jnp.exp2(part - peak))
+            denom = jnp.sum(terms[-1], axis=0, keepdims=True) + jnp.exp2(sink - peak)
+            denom += sums_ref[2 * g + i : 2 * g + i + 1] * scale
+            inverses.append(1.0 / denom)
+            scales.append(scale)
+        mixed = dot(values, jnp.concatenate(terms, axis=0).astype(jnp.bfloat16), TN)
+        mixed = (mixed + mixed_ref[g] * per_head(scales)) * per_head(inverses)
+        store_pairs(mixed.astype(jnp.bfloat16), first, all_ref, slice(0, KEYS_SEEN))
+    rows = late_rows_ref[...] + dot(placing_ref[:, :KEYS_SEEN], all_ref[:, :KEYS_SEEN], NT)
+    rows_ref[...] = rows.astype(jnp.bfloat16)
     all_ref[:, KEYS_SEEN:] = late_ref[...]
-    rows_ref[...] = dot(placing_ref[...], all_ref[...], NT).astype(jnp.bfloat16)
 
 
 def origin(k, sibling):
@@ -327,13 +374,20 @@
     tail = keyvals[toks - KEYS_SEEN :]
     rim = lax.ppermute(tail, "seq", [(i, (i + 1) % size) for i in range(size)])
     loads = (queries, keyvals, preceding_keyvalues, w_out.T, residual.T)
-    q, kv, before, w_t, residual_t, placing, mix_hi, mix_lo, sinks, late = call(
+    groups = keyvals.shape[1] // PAIR
+    across = head_rows // PAIR // groups * KEYS_SEEN
+    part_sums = jax.ShapeDtypeStruct((2 * groups, across), jnp.float32)
+    q, _, before, w_t, residual_t, placing, mix_hi, mix_lo, sinks, late, *parts = call(
         functools.partial(first_kernel, live),
         (
             *(bf16(*a.shape) for a in loads),
             *(bf16(slots, toks),) * 3,
             jax.ShapeDtypeStruct((heads, KEYS_SEEN), jnp.float32),
             bf16(head_rows, toks - KEYS_SEEN),
+            jax.ShapeDtypeStruct((slots, head_rows), jnp.float32),
+            jax.ShapeDtypeStruct((groups, PAIR, across), jnp.float32),
+            part_sums,
+            part_sums,
         ),
         n_in=8,
         scratch=[
@@ -349,10 +403,10 @@
     attended, rows = call(
         second_kernel,
         (bf16(head_rows, toks), bf16(slots, head_rows)),
-        n_in=7,
+        n_in=10,
         flops=2 * toks * SPAN * head_rows,
         moved=2 * queries.size,
-    )(q, kv, before, rim, sinks, late, placing)
+    )(q, before, rim, sinks, late, placing, *parts)
 
     chip_rows = from_chips(rows)
     total = jax.ShapeDtypeStruct((slots, feats), jnp.float32)

time: 43.6 us -> 43.3 us (level)
  waiting for transfers between devices: 12.3 us -> 11.3 us
  Pallas kernels: 11.1 us -> 11.9 us
    ppermute x1, waiting for transfers between devices: 1.96 us -> 0.81 us  [shards(): rim = lax.ppermute(tail, 'seq', [(i, (i + 1) % size) for i in range(size)])]
    pallas_call x1, Pallas kernels: 2.3 us -> 3.45 us  [shards(): call(functools.partial(first_kernel, live), (*(bf16(*a.shape) for a in lo...]
  transfers between devices with their start and end apart: 19 -> 19, of which waited for: 10 -> 11; matrix products, arithmetic and copies ran while one was open for 0% -> 0% of each run, Pallas kernels for 20% -> 23%
where the time goes in v10:
time: 43.3 us; the launch traced here: 43.1 us
  starting transfers between devices  18.9 us (44%)
  Pallas kernels  11.9 us (27%)
  waiting for transfers between devices  11.3 us (26%)
  local copies, waits for them, and re-layouts  0.86 us (2%)
    ppermute x18, starting transfers between devices, swap(): lax.ppermute(block, axis, [(i, i ^ mask) for i in range(lax.axis_size(axi...  15.9 us
    ppermute x18, waiting for transfers between devices, swap(): lax.ppermute(block, axis, [(i, i ^ mask) for i in range(lax.axis_size(axi...  10.4 us
    pallas_call x1, Pallas kernels, shards(): call(functools.partial(first_kernel, live), (*(bf16(*a.shape) for a in lo...  3.45 us
    ppermute x1, starting transfers between devices, shards(): rim = lax.ppermute(tail, 'seq', [(i, (i + 1) % size) for i in range(size)])  3.02 us
    pallas_call x1, Pallas kernels, shards(): call(functools.partial(combine_kernel, live), bf16(feats, toks), n_in=liv...  1.13 us
    pallas_call x1, Pallas kernels, shards(): call(functools.partial(project_kernel, steps), bf16(feats, toks), n_in=cu...  0.93 us
  transfers between devices with their start and end apart: 19, of which 11 were waited for; matrix products, arithmetic and copies ran while one was open for 0% of the time, Pallas kernels for 23%

profile of v10, /device:TPU:0, one launch (start us, length us, event | category | flops | bytes accessed | tf_op | source)
XLA Modules:
  0.0 43.1 jit_solution(6552957012099458949)
XLA Ops:
  0.0 0.8 %slice.3 = bf16[128,256]{1,0:T(8,128)(2,1)S(1)} slice(bf16[256,256]{1,0:T(8,128)(2,1)} %refs_4_.1), slice={[128:256], [0:256]} | slice | bytes 131072 | tf_op jit(solution)/shard_map/slice | solution.py:374
  0.8 3.0 %collective-permute-start = (bf16[128,256]{1,0:T(8,128)(2,1)S(1)}, bf16[128,256]{1,0:T(8,128)(2,1)S(1)}, u32[]{:S(2)}, u32[]{:S(2)}) collective-permute-start(bf16[128,256]{1,0:T(8,128)(2,1)S(1)} %slice.3), channel_id=1, source_target_pairs={{0,4},{4,8},{8,12},{12,0},{1,5},{5,9},{9,13},{13,1},{2,6},{6,10},{... | collective-permute-start | bytes 196616 | tf_op jit(solution)/shard_map/ppermute | solution.py:375
  3.9 3.5 %shard_map.118 = (bf16[256,512]{1,0:T(8,128)(2,1)S(1)}, bf16[256,256]{1,0:T(8,128)(2,1)}, bf16[128,256]{1,0:T(8,128)(2,1)S(1)}, bf16[720,2048]{1,0:T(8,128)(2,1)...) custom-call(s32[4,256]{1,0:T(4,128)} %bitcast.17, ...), custom_call_target="tpu_custom_call" | custom-call | flops 134217728 | bytes 3579904 | tf_op jit(solution)/shard_map/pallas_call | solution.py:380
  7.3 0.8 %collective-permute-done.rim_ref = bf16[128,256]{1,0:T(8,128)(2,1)S(1)} collective-permute-done((bf16[128,256]{1,0:T(8,128)(2,1)S(1)}, bf16[128,256]{1,0:T(8,128)(2,1)S(1)}, u32[]{:S(2)}, u32[]{:S(2)}) %collective-permute-start) | collective-permute-done | bytes 65568 | tf_op jit(solution)/shard_map/ppermute | solution.py:375
  8.1 0.8 %shard_map.119 = (bf16[512,256]{1,0:T(8,128)(2,1)S(1)}, bf16[64,512]{1,0:T(8,128)(2,1)S(1)}) custom-call(bf16[256,512]{1,0:T(8,128)(2,1)S(1)} %get-tuple-element.50.q_ref, bf16[128,256]{1,0:T(8,128)(2,1)S(1)} %get-tuple-element.51.before_ref, bf16[128,256]{1,0:T(8,128)(2,1)S(1)} %collective-permute-done.rim_ref, f32[8,128]{1,0:T(8,128)S(1)} %get-tuple-element.52.sinks_ref, ...), custom_call_target="tpu_custom_call" | custom-call | flops 67108864 | bytes 262144 | tf_op jit(solution)/shard_map/pallas_call | solution.py:403
  9.0 1.8 %collective-permute-start.1 = (bf16[64,512]{1,0:T(8,128)(2,1)S(1)}, bf16[64,512]{1,0:T(8,128)(2,1)S(1)}, u32[]{:S(2)}, u32[]{:S(2)}) collective-permute-start(bf16[64,512]{1,0:T(8,128)(2,1)S(1)} %get-tuple-element.59.rows_ref), channel_id=1, source_target_pairs={{0,2},{1,3},{2,0},{3,1},{4,6},{5,7},{6,4},{7,5},{8,10},{9,11},{10,... | collective-permute-start | bytes 196616 | tf_op jit(solution)/shard_map/ppermute | solution.py:334
  10.8 0.6 %shard_map.121.gates_ref.refs_6_.refs_5_ = bf16[4,360,720]{2,1,0:T(8,128)(2,1)S(1)} custom-call(bf16[360,2880]{1,0:T(8,128)(2,1)S(1)} %bitcast.12), custom_call_target="tpu_custom_call" | custom-call | bytes 4147200 | tf_op jit(solution)/shard_map/pallas_call | solution.py:422
  11.4 0.4 collective-permute-start.16
  11.7 0.4 %shard_map.120.refs_2_ = f32[64,720]{1,0:T(8,128)S(1)} custom-call(bf16[64,512]{1,0:T(8,128)(2,1)S(1)} %get-tuple-element.59.rows_ref, bf16[720,2048]{1,0:T(8,128)(2,1)S(1)} %get-tuple-element.60.w_ref.refs_3_.refs_2_.refs_4_, bf16[720,256]{1,0:T(8,128)(2,1)S(1)} %get-tuple-element.61.residual_ref.refs_5_, bf16[64,256]{1,0:T(8,128)(2,1)S(1)} %get-tuple-element.54.placing_ref), custom_call_target="tpu_custom_call" | custom-call | flops 47185920 | bytes 737280 | tf_op jit(solution)/shard_map/pallas_call | solution.py:414
  12.2 1.8 %collective-permute-done.1.refs_1_ = bf16[64,512]{1,0:T(8,128)(2,1)S(1)} collective-permute-done((bf16[64,512]{1,0:T(8,128)(2,1)S(1)}, bf16[64,512]{1,0:T(8,128)(2,1)S(1)}, u32[]{:S(2)}, u32[]{:S(2)}) %collective-permute-start.1) | collective-permute-done | bytes 65568 | tf_op jit(solution)/shard_map/ppermute | solution.py:334
  14.0 0.0 collective-permute-start.2
  14.0 0.0 collective-permute-done.3.refs_0_
  14.0 0.6 %shard_map.122.refs_1_ = f32[64,720]{1,0:T(8,128)S(1)} custom-call(bf16[64,512]{1,0:T(8,128)(2,1)S(1)} %collective-permute-done.3.refs_0_, bf16[64,512]{1,0:T(8,128)(2,1)S(1)} %collective-permute-done.1.refs_1_, f32[64,720]{1,0:T(8,128)S(1)} %shard_map.120.refs_2_, bf16[720,2048]{1,0:T(8,128)(2,1)S(1)} %get-tuple-element.60.w_ref.refs_3_.refs_2_.refs_4_), custom_call_target="tpu_custom_call" | custom-call | flops 47185920 | bytes 737280 | tf_op jit(solution)/shard_map/pallas_call | solution.py:425
  14.6 0.0 copy-start.3
  14.6 0.0 copy-start.1
  14.6 0.6 %collective-permute-done.2.refs_0_ = bf16[64,512]{1,0:T(8,128)(2,1)S(1)} collective-permute-done((bf16[64,512]{1,0:T(8,128)(2,1)S(1)}, bf16[64,512]{1,0:T(8,128)(2,1)S(1)}, u32[]{:S(2)}, u32[]{:S(2)}) %collective-permute-start.2) | collective-permute-done | bytes 65568 | tf_op jit(solution)/shard_map/ppermute | solution.py:334
  15.3 0.4 shard_map.123
  15.6 2.1 %collective-permute-start.4 = (bf16[16,720]{1,0:T(8,128)(2,1)S(1)}, bf16[16,720]{1,0:T(8,128)(2,1)S(1)}, u32[]{:S(2)}, u32[]{:S(2)}) collective-permute-start(bf16[16,720]{1,0:T(8,128)(2,1)S(1)} %get-tuple-element.64), channel_id=1, source_target_pairs={{0,12},{4,8},{8,4},{12,0},{1,13},{5,9},{9,5},{13,1},{2,14},{6,10},... | collective-permute-start | bytes 69128 | tf_op jit(solution)/shard_map/ppermute | solution.py:334
  17.7 2.4 %collective-permute-start.6 = (bf16[16,720]{1,0:T(8,128)(2,1)S(1)}, bf16[16,720]{1,0:T(8,128)(2,1)S(1)}, u32[]{:S(2)}, u32[]{:S(2)}) collective-permute-start(bf16[16,720]{1,0:T(8,128)(2,1)S(1)} %get-tuple-element.66), channel_id=1, source_target_pairs={{0,4},{4,0},{8,12},{12,8},{1,5},{5,1},{9,13},{13,9},{2,6},{6,2},{1... | collective-permute-start | bytes 69128 | tf_op jit(solution)/shard_map/ppermute | solution.py:334
  20.1 0.1 shard_map.125.gains_ref.refs_5_.refs_4_
  20.2 0.6 %shard_map.124.ups_ref.refs_7_.refs_6_ = bf16[4,360,720]{2,1,0:T(8,128)(2,1)S(1)} custom-call(bf16[360,2880]{1,0:T(8,128)(2,1)S(1)} %bitcast.13), custom_call_target="tpu_custom_call" | custom-call | bytes 4147200 | tf_op jit(solution)/shard_map/pallas_call | solution.py:438
  20.8 0.6 %collective-permute-done.4.refs_0_ = bf16[16,720]{1,0:T(8,128)(2,1)S(1)} collective-permute-done((bf16[16,720]{1,0:T(8,128)(2,1)S(1)}, bf16[16,720]{1,0:T(8,128)(2,1)S(1)}, u32[]{:S(2)}, u32[]{:S(2)}) %collective-permute-start.4) | collective-permute-done | bytes 23072 | tf_op jit(solution)/shard_map/ppermute | solution.py:334
  21.3 1.1 %collective-permute-done.5.refs_1_ = bf16[16,720]{1,0:T(8,128)(2,1)S(1)} collective-permute-done((bf16[16,720]{1,0:T(8,128)(2,1)S(1)}, bf16[16,720]{1,0:T(8,128)(2,1)S(1)}, u32[]{:S(2)}, u32[]{:S(2)}) %collective-permute-start.5) | collective-permute-done | bytes 23072 | tf_op jit(solution)/shard_map/ppermute | solution.py:334
  22.4 0.0 collective-permute-done.6.refs_2_
  22.5 1.6 %collective-permute-start.7 = (bf16[64,720]{1,0:T(8,128)(2,1)S(1)}, bf16[64,720]{1,0:T(8,128)(2,1)S(1)}, u32[]{:S(2)}, u32[]{:S(2)}) collective-permute-start(bf16[64,720]{1,0:T(8,128)(2,1)S(1)} %shard_map.126.block_ref), channel_id=1, source_target_pairs={{0,2},{1,3},{2,0},{3,1},{4,6},{5,7},{6,4},{7,5},{8,10},{9,11},{10,... | collective-permute-start | bytes 276488 | tf_op jit(solution)/shard_map/ppermute | solution.py:334
  24.0 0.0 collective-permute-start.9
  24.0 0.6 %shard_map.128.refs_7_.downs_ref = bf16[4,360,720]{2,1,0:T(8,128)(2,1)S(1)} custom-call(bf16[360,2880]{1,0:T(8,128)(2,1)S(1)} %bitcast.14), custom_call_target="tpu_custom_call" | custom-call | bytes 4147200 | tf_op jit(solution)/shard_map/pallas_call | solution.py:449
  24.6 0.4 %shard_map.127 = (f32[64,360]{1,0:T(8,128)S(1)}, f32[64,360]{1,0:T(8,128)S(1)}, f32[64,128]{1,0:T(8,128)S(1)}) custom-call(bf16[64,720]{1,0:T(8,128)(2,1)S(1)} %shard_map.126.block_ref, f32[4,1,720]{2,1,0:T(1,128)S(1)} %shard_map.125.gains_ref.refs_5_.refs_4_, bf16[4,360,720]{2,1,0:T(8,128)(2,1)S(1)} %shard_map.121.gates_ref.refs_6_.refs_5_, ...), custom_call_target="tpu_custom_call" | custom-call | flops 66355200 | bytes 1036800 | tf_op jit(solution)/shard_map/pallas_call | solution.py:447
  25.1 2.1 %collective-permute-done.7.refs_1_ = bf16[64,720]{1,0:T(8,128)(2,1)S(1)} collective-permute-done((bf16[64,720]{1,0:T(8,128)(2,1)S(1)}, bf16[64,720]{1,0:T(8,128)(2,1)S(1)}, u32[]{:S(2)}, u32[]{:S(2)}) %collective-permute-start.7) | collective-permute-done | bytes 92192 | tf_op jit(solution)/shard_map/ppermute | solution.py:334
  27.1 0.5 %collective-permute-start.17 = (bf16[512,256]{1,0:T(8,128)(2,1)S(1)}, bf16[512,256]{1,0:T(8,128)(2,1)S(1)}, u32[]{:S(2)}, u32[]{:S(2)}) collective-permute-start(bf16[512,256]{1,0:T(8,128)(2,1)S(1)} %get-tuple-element.94.refs_0_), channel_id=1, source_target_pairs={{0,1},{1,0},{2,3},{3,2},{4,5},{5,4},{6,7},{7,6},{8,9},{9,8},{10,11... | collective-permute-start | bytes 786440 | tf_op jit(solution)/shard_map/ppermute | solution.py:334
  27.7 0.0 collective-permute-done.16.refs_1_
  27.7 0.0 collective-permute-start.18
  27.7 0.8 %shard_map.129 = (f32[64,360]{1,0:T(8,128)S(1)}, f32[64,360]{1,0:T(8,128)S(1)}, f32[64,128]{1,0:T(8,128)S(1)}) custom-call(bf16[64,720]{1,0:T(8,128)(2,1)S(1)} %collective-permute-done.9.refs_0_, bf16[64,720]{1,0:T(8,128)(2,1)S(1)} %collective-permute-done.7.refs_1_, f32[64,360]{1,0:T(8,128)S(1)} %get-tuple-element.73.refs_2_, ...), custom_call_target="tpu_custom_call" | custom-call | flops 66355200 | bytes 1036800 | tf_op jit(solution)/shard_map/pallas_call | solution.py:455
  28.5 0.7 %shard_map.130 = (bf16[2,64,720]{2,1,0:T(8,128)(2,1)S(1)}, bf16[64,360]{1,0:T(8,128)(2,1)S(1)}) custom-call(bf16[64,720]{1,0:T(8,128)(2,1)S(1)} %collective-permute-done.8.refs_0_, f32[64,360]{1,0:T(8,128)S(1)} %get-tuple-element.78.refs_1_, f32[64,360]{1,0:T(8,128)S(1)} %get-tuple-element.79.refs_2_, f32[64,128]{1,0:T(8,128)S(1)} %get-tuple-element.80.refs_3_, ...), custom_call_target="tpu_custom_call" | custom-call | flops 66355200 | bytes 1036800 | tf_op jit(solution)/shard_map/pallas_call | solution.py:458
  29.2 0.6 %collective-permute-start.10 = (bf16[2,64,720]{2,1,0:T(8,128)(2,1)S(1)}, bf16[2,64,720]{2,1,0:T(8,128)(2,1)S(1)}, u32[]{:S(2)}, u32[]{:S(2)}) collective-permute-start(bf16[2,64,720]{2,1,0:T(8,128)(2,1)S(1)} %get-tuple-element.82), channel_id=1, source_target_pairs={{0,1},{1,0},{2,3},{3,2},{4,5},{5,4},{6,7},{7,6},{8,9},{9,8},{10,11... | collective-permute-start | bytes 552968 | tf_op jit(solution)/shard_map/ppermute | solution.py:334
  29.8 0.3 shard_map.131.kept_ref
  30.1 0.7 %collective-permute-done.10.given_ref = bf16[2,64,720]{2,1,0:T(8,128)(2,1)S(1)} collective-permute-done((bf16[2,64,720]{2,1,0:T(8,128)(2,1)S(1)}, bf16[2,64,720]{2,1,0:T(8,128)(2,1)S(1)}, u32[]{:S(2)}, u32[]{:S(2)}) %collective-permute-start.10) | collective-permute-done | bytes 184352 | tf_op jit(solution)/shard_map/ppermute | solution.py:334
  30.9 1.6 %collective-permute-start.11 = (bf16[32,720]{1,0:T(8,128)(2,1)S(1)}, bf16[32,720]{1,0:T(8,128)(2,1)S(1)}, u32[]{:S(2)}, u32[]{:S(2)}) collective-permute-start(bf16[32,720]{1,0:T(8,128)(2,1)S(1)} %get-tuple-element.84), channel_id=1, source_target_pairs={{0,2},{1,3},{2,0},{3,1},{4,6},{5,7},{6,4},{7,5},{8,10},{9,11},{10,... | collective-permute-start | bytes 138248 | tf_op jit(solution)/shard_map/ppermute | solution.py:334
  32.5 0.5 %collective-permute-start.14 = (bf16[32,720]{1,0:T(8,128)(2,1)S(1)}, bf16[32,720]{1,0:T(8,128)(2,1)S(1)}, u32[]{:S(2)}, u32[]{:S(2)}) collective-permute-start(bf16[32,720]{1,0:T(8,128)(2,1)S(1)} %get-tuple-element.88), channel_id=1, source_target_pairs={{0,2},{1,3},{2,0},{3,1},{4,6},{5,7},{6,4},{7,5},{8,10},{9,11},{10,... | collective-permute-start | bytes 138248 | tf_op jit(solution)/shard_map/ppermute | solution.py:334
  33.0 2.1 %collective-permute-done.11.refs_1_ = bf16[32,720]{1,0:T(8,128)(2,1)S(1)} collective-permute-done((bf16[32,720]{1,0:T(8,128)(2,1)S(1)}, bf16[32,720]{1,0:T(8,128)(2,1)S(1)}, u32[]{:S(2)}, u32[]{:S(2)}) %collective-permute-start.11) | collective-permute-done | bytes 46112 | tf_op jit(solution)/shard_map/ppermute | solution.py:334
  35.1 1.9 %collective-permute-start.12 = (bf16[16,720]{1,0:T(8,128)(2,1)S(1)}, bf16[16,720]{1,0:T(8,128)(2,1)S(1)}, u32[]{:S(2)}, u32[]{:S(2)}) collective-permute-start(bf16[16,720]{1,0:T(8,128)(2,1)S(1)} %get-tuple-element.85), channel_id=1, source_target_pairs={{0,12},{4,8},{8,4},{12,0},{1,13},{5,9},{9,5},{13,1},{2,14},{6,10},... | collective-permute-start | bytes 69128 | tf_op jit(solution)/shard_map/ppermute | solution.py:334
  36.9 1.1 %collective-permute-start.13 = (bf16[16,720]{1,0:T(8,128)(2,1)S(1)}, bf16[16,720]{1,0:T(8,128)(2,1)S(1)}, u32[]{:S(2)}, u32[]{:S(2)}) collective-permute-start(bf16[16,720]{1,0:T(8,128)(2,1)S(1)} %get-tuple-element.86), channel_id=1, source_target_pairs={{0,8},{4,12},{8,0},{12,4},{1,9},{5,13},{9,1},{13,5},{2,10},{6,14},... | collective-permute-start | bytes 69128 | tf_op jit(solution)/shard_map/ppermute | solution.py:334
  38.1 1.5 %collective-permute-start.15 = (bf16[16,720]{1,0:T(8,128)(2,1)S(1)}, bf16[16,720]{1,0:T(8,128)(2,1)S(1)}, u32[]{:S(2)}, u32[]{:S(2)}) collective-permute-start(bf16[16,720]{1,0:T(8,128)(2,1)S(1)} %get-tuple-element.89), channel_id=1, source_target_pairs={{0,4},{4,0},{8,12},{12,8},{1,5},{5,1},{9,13},{13,9},{2,6},{6,2},{1... | collective-permute-start | bytes 69128 | tf_op jit(solution)/shard_map/ppermute | solution.py:334
  39.6 0.9 %shard_map.135.refs_6_ = bf16[720,256]{1,0:T(8,128)(2,1)S(1)} custom-call(bf16[512,256]{1,0:T(8,128)(2,1)S(1)} %get-tuple-element.94.refs_0_, bf16[512,256]{1,0:T(8,128)(2,1)S(1)} %collective-permute-done.16.refs_1_, bf16[512,256]{1,0:T(8,128)(2,1)S(1)} %collective-permute-done.17.refs_2_, bf16[512,256]{1,0:T(8,128)(2,1)S(1)} %collective-permute-done.18.refs_3_, ...), custom_call_target="tpu_custom_call" | custom-call | flops 754974720 | bytes 2949120 | tf_op jit(solution)/shard_map/pallas_call | solution.py:465
  40.6 0.3 collective-permute-done.12.refs_0_
  40.9 0.8 %collective-permute-done.13.refs_1_ = bf16[16,720]{1,0:T(8,128)(2,1)S(1)} collective-permute-done((bf16[16,720]{1,0:T(8,128)(2,1)S(1)}, bf16[16,720]{1,0:T(8,128)(2,1)S(1)}, u32[]{:S(2)}, u32[]{:S(2)}) %collective-permute-start.13) | collective-permute-done | bytes 23072 | tf_op jit(solution)/shard_map/ppermute | solution.py:334
  41.7 0.3 collective-permute-done.15.refs_2_
  42.0 1.1 %shard_map.136 = bf16[720,256]{1,0:T(8,128)(2,1)} custom-call(bf16[16,720]{1,0:T(8,128)(2,1)S(1)} %collective-permute-done.12.refs_0_, bf16[16,720]{1,0:T(8,128)(2,1)S(1)} %collective-permute-done.13.refs_1_, bf16[16,720]{1,0:T(8,128)(2,1)S(1)} %collective-permute-done.15.refs_2_, bf16[16,720]{1,0:T(8,128)(2,1)S(1)} %get-tuple-element.90.refs_3_, ...), custom_call_target="tpu_custom_call" | custom-call | tf_op jit(solution)/shard_map/pallas_call | solution.py:485
  (18 shorter events, 0.1 us)
Async XLA Ops:
  0.8 7.3 %collective-permute-start = (bf16[128,256]{1,0:T(8,128)(2,1)S(1)}, bf16[128,256]{1,0:T(8,128)(2,1)S(1)}, u32[]{:S(2)}, u32[]{:S(2)}) collective-permute-start(bf16[128,256]{1,0:T(8,128)(2,1)S(1)} %slice.3), channel_id=1, source_target_pairs={{0,4},{4,8},{8,12},{12,0},{1,5},{5,9},{9,13},{13,1},{2,6},{6,10},{... | collective-permute-start | bytes 196616 | tf_op jit(solution)/shard_map/ppermute | solution.py:375
  3.9 6.9 %copy-start = (bf16[1,2880,360]{1,2,0:T(8,128)(2,1)S(1)}, bf16[1,2880,360]{1,2,0:T(8,128)(2,1)}, u32[]{:S(2)}) copy-start(bf16[1,2880,360]{1,2,0:T(8,128)(2,1)} %param.21) | copy-start | bytes 6220804
  9.0 5.0 %collective-permute-start.1 = (bf16[64,512]{1,0:T(8,128)(2,1)S(1)}, bf16[64,512]{1,0:T(8,128)(2,1)S(1)}, u32[]{:S(2)}, u32[]{:S(2)}) collective-permute-start(bf16[64,512]{1,0:T(8,128)(2,1)S(1)} %get-tuple-element.59.rows_ref), channel_id=1, source_target_pairs={{0,2},{1,3},{2,0},{3,1},{4,6},{5,7},{6,4},{7,5},{8,10},{9,11},{10,... | collective-permute-start | bytes 196616 | tf_op jit(solution)/shard_map/ppermute | solution.py:334
  11.4 16.3 %collective-permute-start.16 = (bf16[512,256]{1,0:T(8,128)(2,1)S(1)}, bf16[512,256]{1,0:T(8,128)(2,1)S(1)}, u32[]{:S(2)}, u32[]{:S(2)}) collective-permute-start(bf16[512,256]{1,0:T(8,128)(2,1)S(1)} %get-tuple-element.94.refs_0_), channel_id=1, source_target_pairs={{0,2},{1,3},{2,0},{3,1},{4,6},{5,7},{6,4},{7,5},{8,10},{9,11},{10,... | collective-permute-start | bytes 786440 | tf_op jit(solution)/shard_map/ppermute | solution.py:334
  11.7 2.3 %collective-permute-start.3 = (bf16[64,512]{1,0:T(8,128)(2,1)S(1)}, bf16[64,512]{1,0:T(8,128)(2,1)S(1)}, u32[]{:S(2)}, u32[]{:S(2)}) collective-permute-start(bf16[64,512]{1,0:T(8,128)(2,1)S(1)} %get-tuple-element.59.rows_ref), channel_id=1, source_target_pairs={{0,1},{1,0},{2,3},{3,2},{4,5},{5,4},{6,7},{7,6},{8,9},{9,8},{10,11... | collective-permute-start | bytes 196616 | tf_op jit(solution)/shard_map/ppermute | solution.py:334
  14.0 1.3 %collective-permute-start.2 = (bf16[64,512]{1,0:T(8,128)(2,1)S(1)}, bf16[64,512]{1,0:T(8,128)(2,1)S(1)}, u32[]{:S(2)}, u32[]{:S(2)}) collective-permute-start(bf16[64,512]{1,0:T(8,128)(2,1)S(1)} %collective-permute-done.1.refs_1_), channel_id=1, source_target_pairs={{0,1},{1,0},{2,3},{3,2},{4,5},{5,4},{6,7},{7,6},{8,9},{9,8},{10,11... | collective-permute-start | bytes 196616 | tf_op jit(solution)/shard_map/ppermute | solution.py:334
  14.6 5.5 %copy-start.3 = (f32[2880]{0:T(1024)S(1)}, f32[2880]{0:T(1024)}, u32[]{:S(2)}) copy-start(f32[2880]{0:T(1024)} %gain_ref.1) | copy-start | bytes 34564
  14.6 5.5 %copy-start.1 = (bf16[1,2880,360]{1,2,0:T(8,128)(2,1)S(1)}, bf16[1,2880,360]{1,2,0:T(8,128)(2,1)}, u32[]{:S(2)}) copy-start(bf16[1,2880,360]{1,2,0:T(8,128)(2,1)} %param.22) | copy-start | bytes 6220804
  15.6 5.7 %collective-permute-start.4 = (bf16[16,720]{1,0:T(8,128)(2,1)S(1)}, bf16[16,720]{1,0:T(8,128)(2,1)S(1)}, u32[]{:S(2)}, u32[]{:S(2)}) collective-permute-start(bf16[16,720]{1,0:T(8,128)(2,1)S(1)} %get-tuple-element.64), channel_id=1, source_target_pairs={{0,12},{4,8},{8,4},{12,0},{1,13},{5,9},{9,5},{13,1},{2,14},{6,10},... | collective-permute-start | bytes 69128 | tf_op jit(solution)/shard_map/ppermute | solution.py:334
  17.7 4.7 %collective-permute-start.5 = (bf16[16,720]{1,0:T(8,128)(2,1)S(1)}, bf16[16,720]{1,0:T(8,128)(2,1)S(1)}, u32[]{:S(2)}, u32[]{:S(2)}) collective-permute-start(bf16[16,720]{1,0:T(8,128)(2,1)S(1)} %get-tuple-element.65), channel_id=1, source_target_pairs={{0,8},{4,12},{8,0},{12,4},{1,9},{5,13},{9,1},{13,5},{2,10},{6,14},... | collective-permute-start | bytes 69128 | tf_op jit(solution)/shard_map/ppermute | solution.py:334
  17.7 4.7 %collective-permute-start.6 = (bf16[16,720]{1,0:T(8,128)(2,1)S(1)}, bf16[16,720]{1,0:T(8,128)(2,1)S(1)}, u32[]{:S(2)}, u32[]{:S(2)}) collective-permute-start(bf16[16,720]{1,0:T(8,128)(2,1)S(1)} %get-tuple-element.66), channel_id=1, source_target_pairs={{0,4},{4,0},{8,12},{12,8},{1,5},{5,1},{9,13},{13,9},{2,6},{6,2},{1... | collective-permute-start | bytes 69128 | tf_op jit(solution)/shard_map/ppermute | solution.py:334
  20.2 3.9 %copy-start.2 = (bf16[1,360,2880]{2,1,0:T(8,128)(2,1)S(1)}, bf16[1,360,2880]{2,1,0:T(8,128)(2,1)}, u32[]{:S(2)}) copy-start(bf16[1,360,2880]{2,1,0:T(8,128)(2,1)} %param.23) | copy-start | bytes 6220804
  22.5 4.7 %collective-permute-start.7 = (bf16[64,720]{1,0:T(8,128)(2,1)S(1)}, bf16[64,720]{1,0:T(8,128)(2,1)S(1)}, u32[]{:S(2)}, u32[]{:S(2)}) collective-permute-start(bf16[64,720]{1,0:T(8,128)(2,1)S(1)} %shard_map.126.block_ref), channel_id=1, source_target_pairs={{0,2},{1,3},{2,0},{3,1},{4,6},{5,7},{6,4},{7,5},{8,10},{9,11},{10,... | collective-permute-start | bytes 276488 | tf_op jit(solution)/shard_map/ppermute | solution.py:334
  24.0 3.6 %collective-permute-start.9 = (bf16[64,720]{1,0:T(8,128)(2,1)S(1)}, bf16[64,720]{1,0:T(8,128)(2,1)S(1)}, u32[]{:S(2)}, u32[]{:S(2)}) collective-permute-start(bf16[64,720]{1,0:T(8,128)(2,1)S(1)} %shard_map.126.block_ref), channel_id=1, source_target_pairs={{0,1},{1,0},{2,3},{3,2},{4,5},{5,4},{6,7},{7,6},{8,9},{9,8},{10,11... | collective-permute-start | bytes 276488 | tf_op jit(solution)/shard_map/ppermute | solution.py:334
  27.1 1.3 %collective-permute-start.8 = (bf16[64,720]{1,0:T(8,128)(2,1)S(1)}, bf16[64,720]{1,0:T(8,128)(2,1)S(1)}, u32[]{:S(2)}, u32[]{:S(2)}) collective-permute-start(bf16[64,720]{1,0:T(8,128)(2,1)S(1)} %collective-permute-done.7.refs_1_), channel_id=1, source_target_pairs={{0,1},{1,0},{2,3},{3,2},{4,5},{5,4},{6,7},{7,6},{8,9},{9,8},{10,11... | collective-permute-start | bytes 276488 | tf_op jit(solution)/shard_map/ppermute | solution.py:334
  27.1 12.5 %collective-permute-start.17 = (bf16[512,256]{1,0:T(8,128)(2,1)S(1)}, bf16[512,256]{1,0:T(8,128)(2,1)S(1)}, u32[]{:S(2)}, u32[]{:S(2)}) collective-permute-start(bf16[512,256]{1,0:T(8,128)(2,1)S(1)} %get-tuple-element.94.refs_0_), channel_id=1, source_target_pairs={{0,1},{1,0},{2,3},{3,2},{4,5},{5,4},{6,7},{7,6},{8,9},{9,8},{10,11... | collective-permute-start | bytes 786440 | tf_op jit(solution)/shard_map/ppermute | solution.py:334
  27.7 12.0 %collective-permute-start.18 = (bf16[512,256]{1,0:T(8,128)(2,1)S(1)}, bf16[512,256]{1,0:T(8,128)(2,1)S(1)}, u32[]{:S(2)}, u32[]{:S(2)}) collective-permute-start(bf16[512,256]{1,0:T(8,128)(2,1)S(1)} %collective-permute-done.16.refs_1_), channel_id=1, source_target_pairs={{0,1},{1,0},{2,3},{3,2},{4,5},{5,4},{6,7},{7,6},{8,9},{9,8},{10,11... | collective-permute-start | bytes 786440 | tf_op jit(solution)/shard_map/ppermute | solution.py:334
  29.2 1.6 %collective-permute-start.10 = (bf16[2,64,720]{2,1,0:T(8,128)(2,1)S(1)}, bf16[2,64,720]{2,1,0:T(8,128)(2,1)S(1)}, u32[]{:S(2)}, u32[]{:S(2)}) collective-permute-start(bf16[2,64,720]{2,1,0:T(8,128)(2,1)S(1)} %get-tuple-element.82), channel_id=1, source_target_pairs={{0,1},{1,0},{2,3},{3,2},{4,5},{5,4},{6,7},{7,6},{8,9},{9,8},{10,11... | collective-permute-start | bytes 552968 | tf_op jit(solution)/shard_map/ppermute | solution.py:334
  30.9 4.2 %collective-permute-start.11 = (bf16[32,720]{1,0:T(8,128)(2,1)S(1)}, bf16[32,720]{1,0:T(8,128)(2,1)S(1)}, u32[]{:S(2)}, u32[]{:S(2)}) collective-permute-start(bf16[32,720]{1,0:T(8,128)(2,1)S(1)} %get-tuple-element.84), channel_id=1, source_target_pairs={{0,2},{1,3},{2,0},{3,1},{4,6},{5,7},{6,4},{7,5},{8,10},{9,11},{10,... | collective-permute-start | bytes 138248 | tf_op jit(solution)/shard_map/ppermute | solution.py:334
  32.5 5.6 %collective-permute-start.14 = (bf16[32,720]{1,0:T(8,128)(2,1)S(1)}, bf16[32,720]{1,0:T(8,128)(2,1)S(1)}, u32[]{:S(2)}, u32[]{:S(2)}) collective-permute-start(bf16[32,720]{1,0:T(8,128)(2,1)S(1)} %get-tuple-element.88), channel_id=1, source_target_pairs={{0,2},{1,3},{2,0},{3,1},{4,6},{5,7},{6,4},{7,5},{8,10},{9,11},{10,... | collective-permute-start | bytes 138248 | tf_op jit(solution)/shard_map/ppermute | solution.py:334
  35.1 5.8 %collective-permute-start.12 = (bf16[16,720]{1,0:T(8,128)(2,1)S(1)}, bf16[16,720]{1,0:T(8,128)(2,1)S(1)}, u32[]{:S(2)}, u32[]{:S(2)}) collective-permute-start(bf16[16,720]{1,0:T(8,128)(2,1)S(1)} %get-tuple-element.85), channel_id=1, source_target_pairs={{0,12},{4,8},{8,4},{12,0},{1,13},{5,9},{9,5},{13,1},{2,14},{6,10},... | collective-permute-start | bytes 69128 | tf_op jit(solution)/shard_map/ppermute | solution.py:334
  36.9 4.7 %collective-permute-start.13 = (bf16[16,720]{1,0:T(8,128)(2,1)S(1)}, bf16[16,720]{1,0:T(8,128)(2,1)S(1)}, u32[]{:S(2)}, u32[]{:S(2)}) collective-permute-start(bf16[16,720]{1,0:T(8,128)(2,1)S(1)} %get-tuple-element.86), channel_id=1, source_target_pairs={{0,8},{4,12},{8,0},{12,4},{1,9},{5,13},{9,1},{13,5},{2,10},{6,14},... | collective-permute-start | bytes 69128 | tf_op jit(solution)/shard_map/ppermute | solution.py:334
  38.1 3.9 %collective-permute-start.15 = (bf16[16,720]{1,0:T(8,128)(2,1)S(1)}, bf16[16,720]{1,0:T(8,128)(2,1)S(1)}, u32[]{:S(2)}, u32[]{:S(2)}) collective-permute-start(bf16[16,720]{1,0:T(8,128)(2,1)S(1)} %get-tuple-element.89), channel_id=1, source_target_pairs={{0,4},{4,0},{8,12},{12,8},{1,5},{5,1},{9,13},{13,9},{2,6},{6,2},{1... | collective-permute-start | bytes 69128 | tf_op jit(solution)/shard_map/ppermute | solution.py:334

commit v11 on v10

--- a/solution.py
+++ b/solution.py
@@ -223,7 +223,7 @@
 def rows_last_kernel(steps, *refs):
     blocks, (before_ref, w_ref) = refs[: steps - 1], refs[steps - 1 : steps + 1]
     outgoing, rows_ref = refs[steps + 1 : -1], refs[-1]
-    total = add_products(before_ref[...], range(steps + 1, 2 * steps), blocks, w_ref, steps, NT)
+    total = add_products(before_ref[...], range(1, steps), blocks, w_ref, steps, NT)
     rows_ref[...] = total.astype(jnp.bfloat16).reshape(rows_ref.shape)
     me = lax.axis_index("seq")
     for k, out_ref in enumerate(outgoing):
@@ -276,7 +276,7 @@
 def expert_own_kernel(steps, block_ref, gains_ref, gates_ref, ups_ref, *out_refs):
     zeros = jnp.zeros(out_refs[0].shape, jnp.float32)
     sums = (zeros, zeros, jnp.zeros((zeros.shape[0], 1), jnp.float32))
-    store_sums(add_features(sums, [0], [block_ref], gains_ref, gates_ref, ups_ref, steps), out_refs)
+    store_sums(add_features(sums, [steps], [block_ref], gains_ref, gates_ref, ups_ref, steps), out_refs)
 
 
 def expert_more_kernel(places, steps, *refs):
@@ -297,12 +297,12 @@
     activated = ((up + 1.0) * gate * jax.nn.sigmoid(glu_alpha * gate)).astype(jnp.bfloat16)
     activated_ref[...] = activated
     for k in range(steps):
-        given_ref[k] = dot(activated, downs_ref[origin(k, True)], NN).astype(jnp.bfloat16)
+        given_ref[k] = dot(activated, downs_ref[origin(k, k > 0)], NN).astype(jnp.bfloat16)
 
 
 def expert_kept_kernel(activated_ref, downs_ref, kept_ref):
     for k in range(kept_ref.shape[0]):
-        kept_ref[k] = dot(activated_ref[...], downs_ref[origin(k, False)], NN).astype(jnp.bfloat16)
+        kept_ref[k] = dot(activated_ref[...], downs_ref[origin(k, k == 0)], NN).astype(jnp.bfloat16)
 
 
 def add_cores_kernel(kept_ref, given_ref, *out_refs):
@@ -334,8 +334,18 @@
     return lax.ppermute(block, axis, [(i, i ^ mask) for i in range(lax.axis_size(axis))])
 
 
+def to_chip(block, k):
+    return swap(block, "cuts", CORES * k + 1)
+
+
 def from_chips(block):
-    return [swap(block, "cuts", CORES * k) for k in range(1, lax.axis_size("cuts") // CORES)]
+    return [to_chip(block, k) for k in range(1, lax.axis_size("cuts") // CORES)]
+
+
+def to_seq(block, k):
+    size = lax.axis_size("seq") * lax.axis_size("cuts")
+    mask = k * lax.axis_size("cuts") + 1
+    return lax.ppermute(block, ("seq", "cuts"), [(i, i ^ mask) for i in range(size)])
 
 
 def from_sibling(block):
@@ -415,7 +425,7 @@
         rows, w_t, residual_t, placing
     )
     sibling_rows = from_sibling(rows)
-    places = [steps, *range(1, steps)]
+    places = range(steps, 2 * steps)
     spread = functools.partial(
         call, spread_kernel, bf16(cuts, hidden, feats), n_in=1, moved=4 * w_gate.size
     )
@@ -433,7 +443,7 @@
         **part,
     )(*relayed_rows, chips, w_t)
 
-    arrived = [swap(outgoing[k], "seq", k) for k in range(live - 1, 0, -1)] + [outgoing[0]]
+    arrived = [to_seq(outgoing[k], k) for k in range(live - 1, -1, -1)]
 
     ups = spread()(after(w_up[0].T, outgoing[0]))
     gains = call(spread_gain_kernel, jax.ShapeDtypeStruct((cuts, 1, feats), jnp.float32), n_in=1)(norm_gain)
@@ -448,11 +458,11 @@
     sibling_rows = from_sibling(stacked)
     downs = spread()(after(w_down[0], stacked))
     chip_blocks = from_chips(after(attended, gates))
-    blocks = [attended, *chip_blocks]
-    blocks += [from_sibling(b) for b in blocks]
+    sibling_block, *relayed_blocks = [from_sibling(b) for b in (attended, *chip_blocks)]
+    blocks = [attended, *relayed_blocks, sibling_block, *chip_blocks]
     chip_rows = after(chip_rows, (own, downs))
     relayed_rows = [from_sibling(b) for b in chip_rows]
-    chips = call(functools.partial(expert_more_kernel, places, steps), sums, n_in=steps + 6, **part)(
+    chips = call(functools.partial(expert_more_kernel, range(steps), steps), sums, n_in=steps + 6, **part)(
         sibling_rows, *chip_rows, *own, gains, gates, ups
     )
     given, activated = call(
@@ -475,13 +485,12 @@
     )
     returned = []
     for half in range(2):
-        parts = [sums[half]] + [swap(sums[2 * k + half], "cuts", CORES * k) for k in range(1, steps)]
+        parts = [sums[half]] + [to_chip(sums[2 * k + half], k) for k in range(1, steps)]
         blocks = call(functools.partial(add_chips_kernel, steps), (bf16(CAP, feats),) * (live // 2), n_in=steps)(
             *parts
         )
         for block in blocks:
-            k = live - 1 - len(returned)
-            returned.append(swap(block, "seq", k) if k else block)
+            returned.append(to_seq(block, live - 1 - len(returned)))
     out = call(
         functools.partial(combine_kernel, live),
         bf16(feats, toks),

time: 43.3 us -> 42.6 us (0.984)
  waiting for transfers between devices: 11.3 us -> 10.8 us
    ppermute x18 -> x12, starting transfers between devices: 15.9 us -> 6.52 us  [swap(): lax.ppermute(block, axis, [(i, i ^ mask) for i in range(lax.axis_size(axi...]
    ppermute x0 -> x8, starting transfers between devices: none -> 9.13 us  [to_seq(): lax.ppermute(block, ('seq', 'cuts'), [(i, i ^ mask) for i in range(size)])]
    ppermute x18 -> x12, waiting for transfers between devices: 10.4 us -> 6.81 us  [swap(): lax.ppermute(block, axis, [(i, i ^ mask) for i in range(lax.axis_size(axi...]
    ppermute x0 -> x8, waiting for transfers between devices: none -> 3.19 us  [to_seq(): lax.ppermute(block, ('seq', 'cuts'), [(i, i ^ mask) for i in range(size)])]
  transfers between devices with their start and end apart: 19 -> 21, of which waited for: 11 -> 10; matrix products, arithmetic and copies ran while one was open for 0% -> 0% of each run, Pallas kernels for 23% -> 23%
where the time goes in v11:
time: 42.6 us; the launch traced here: 42.4 us
  starting transfers between devices  18.7 us (44%)
  Pallas kernels  11.9 us (28%)
  waiting for transfers between devices  10.8 us (25%)
  local copies, waits for them, and re-layouts  0.86 us (2%)
    ppermute x8, starting transfers between devices, to_seq(): lax.ppermute(block, ('seq', 'cuts'), [(i, i ^ mask) for i in range(size)])  9.13 us
    ppermute x12, waiting for transfers between devices, swap(): lax.ppermute(block, axis, [(i, i ^ mask) for i in range(lax.axis_size(axi...  6.81 us
    ppermute x12, starting transfers between devices, swap(): lax.ppermute(block, axis, [(i, i ^ mask) for i in range(lax.axis_size(axi...  6.52 us
    pallas_call x1, Pallas kernels, shards(): call(functools.partial(first_kernel, live), (*(bf16(*a.shape) for a in lo...  3.45 us
    ppermute x8, waiting for transfers between devices, to_seq(): lax.ppermute(block, ('seq', 'cuts'), [(i, i ^ mask) for i in range(size)])  3.19 us
    ppermute x1, starting transfers between devices, shards(): rim = lax.ppermute(tail, 'seq', [(i, (i + 1) % size) for i in range(size)])  3.02 us
    pallas_call x1, Pallas kernels, shards(): call(functools.partial(combine_kernel, live), bf16(feats, toks), n_in=liv...  1.13 us
    pallas_call x1, Pallas kernels, shards(): call(functools.partial(project_kernel, steps), bf16(feats, toks), n_in=cu...  0.93 us
  transfers between devices with their start and end apart: 21, of which 10 were waited for; matrix products, arithmetic and copies ran while one was open for 0% of the time, Pallas kernels for 23%

profile of v11, /device:TPU:0, one launch (start us, length us, event | category | flops | bytes accessed | tf_op | source)
XLA Modules:
  0.0 42.4 jit_solution(2375133812216155408)
XLA Ops:
  0.0 0.8 %slice.3 = bf16[128,256]{1,0:T(8,128)(2,1)S(1)} slice(bf16[256,256]{1,0:T(8,128)(2,1)} %refs_4_.1), slice={[128:256], [0:256]} | slice | bytes 131072 | tf_op jit(solution)/shard_map/slice | solution.py:384
  0.8 3.0 %collective-permute-start = (bf16[128,256]{1,0:T(8,128)(2,1)S(1)}, bf16[128,256]{1,0:T(8,128)(2,1)S(1)}, u32[]{:S(2)}, u32[]{:S(2)}) collective-permute-start(bf16[128,256]{1,0:T(8,128)(2,1)S(1)} %slice.3), channel_id=1, source_target_pairs={{0,4},{4,8},{8,12},{12,0},{1,5},{5,9},{9,13},{13,1},{2,6},{6,10},{... | collective-permute-start | bytes 196616 | tf_op jit(solution)/shard_map/ppermute | solution.py:385
  3.9 3.5 %shard_map.118 = (bf16[256,512]{1,0:T(8,128)(2,1)S(1)}, bf16[256,256]{1,0:T(8,128)(2,1)}, bf16[128,256]{1,0:T(8,128)(2,1)S(1)}, bf16[720,2048]{1,0:T(8,128)(2,1)...) custom-call(s32[4,256]{1,0:T(4,128)} %bitcast.17, ...), custom_call_target="tpu_custom_call" | custom-call | flops 134217728 | bytes 3579904 | tf_op jit(solution)/shard_map/pallas_call | solution.py:390
  7.3 0.8 %collective-permute-done.rim_ref = bf16[128,256]{1,0:T(8,128)(2,1)S(1)} collective-permute-done((bf16[128,256]{1,0:T(8,128)(2,1)S(1)}, bf16[128,256]{1,0:T(8,128)(2,1)S(1)}, u32[]{:S(2)}, u32[]{:S(2)}) %collective-permute-start) | collective-permute-done | bytes 65568 | tf_op jit(solution)/shard_map/ppermute | solution.py:385
  8.1 0.8 %shard_map.119 = (bf16[512,256]{1,0:T(8,128)(2,1)S(1)}, bf16[64,512]{1,0:T(8,128)(2,1)S(1)}) custom-call(bf16[256,512]{1,0:T(8,128)(2,1)S(1)} %get-tuple-element.50.q_ref, bf16[128,256]{1,0:T(8,128)(2,1)S(1)} %get-tuple-element.51.before_ref, bf16[128,256]{1,0:T(8,128)(2,1)S(1)} %collective-permute-done.rim_ref, f32[8,128]{1,0:T(8,128)S(1)} %get-tuple-element.52.sinks_ref, ...), custom_call_target="tpu_custom_call" | custom-call | flops 67108864 | bytes 262144 | tf_op jit(solution)/shard_map/pallas_call | solution.py:413
  9.0 0.1 collective-permute-start.1
  9.1 0.6 %shard_map.121.gates_ref.refs_6_.refs_5_ = bf16[4,360,720]{2,1,0:T(8,128)(2,1)S(1)} custom-call(bf16[360,2880]{1,0:T(8,128)(2,1)S(1)} %bitcast.12), custom_call_target="tpu_custom_call" | custom-call | bytes 4147200 | tf_op jit(solution)/shard_map/pallas_call | solution.py:432
  9.7 1.8 %collective-permute-start.18 = (bf16[512,256]{1,0:T(8,128)(2,1)S(1)}, bf16[512,256]{1,0:T(8,128)(2,1)S(1)}, u32[]{:S(2)}, u32[]{:S(2)}) collective-permute-start(bf16[512,256]{1,0:T(8,128)(2,1)S(1)} %get-tuple-element.94.refs_0_), channel_id=1, source_target_pairs={{0,3},{1,2},{2,1},{3,0},{4,7},{5,6},{6,5},{7,4},{8,11},{9,10},{10,... | collective-permute-start | bytes 786440 | tf_op jit(solution)/shard_map/ppermute | solution.py:334
  11.5 0.1 collective-permute-start.3
  11.6 0.4 %shard_map.120.refs_2_ = f32[64,720]{1,0:T(8,128)S(1)} custom-call(bf16[64,512]{1,0:T(8,128)(2,1)S(1)} %get-tuple-element.59.rows_ref, bf16[720,2048]{1,0:T(8,128)(2,1)S(1)} %get-tuple-element.60.w_ref.refs_3_.refs_2_.refs_4_, bf16[720,256]{1,0:T(8,128)(2,1)S(1)} %get-tuple-element.61.residual_ref.refs_5_, bf16[64,256]{1,0:T(8,128)(2,1)S(1)} %get-tuple-element.54.placing_ref), custom_call_target="tpu_custom_call" | custom-call | flops 47185920 | bytes 737280 | tf_op jit(solution)/shard_map/pallas_call | solution.py:424
  12.1 1.1 %collective-permute-done.1.refs_1_ = bf16[64,512]{1,0:T(8,128)(2,1)S(1)} collective-permute-done((bf16[64,512]{1,0:T(8,128)(2,1)S(1)}, bf16[64,512]{1,0:T(8,128)(2,1)S(1)}, u32[]{:S(2)}, u32[]{:S(2)}) %collective-permute-start.1) | collective-permute-done | bytes 65568 | tf_op jit(solution)/shard_map/ppermute | solution.py:334
  13.2 0.6 %collective-permute-start.2 = (bf16[64,512]{1,0:T(8,128)(2,1)S(1)}, bf16[64,512]{1,0:T(8,128)(2,1)S(1)}, u32[]{:S(2)}, u32[]{:S(2)}) collective-permute-start(bf16[64,512]{1,0:T(8,128)(2,1)S(1)} %collective-permute-done.1.refs_1_), channel_id=1, source_target_pairs={{0,1},{1,0},{2,3},{3,2},{4,5},{5,4},{6,7},{7,6},{8,9},{9,8},{10,11... | collective-permute-start | bytes 196616 | tf_op jit(solution)/shard_map/ppermute | solution.py:334
  13.8 0.6 %shard_map.122.refs_1_ = f32[64,720]{1,0:T(8,128)S(1)} custom-call(bf16[64,512]{1,0:T(8,128)(2,1)S(1)} %collective-permute-done.3.refs_0_, bf16[64,512]{1,0:T(8,128)(2,1)S(1)} %collective-permute-done.1.refs_1_, f32[64,720]{1,0:T(8,128)S(1)} %shard_map.120.refs_2_, bf16[720,2048]{1,0:T(8,128)(2,1)S(1)} %get-tuple-element.60.w_ref.refs_3_.refs_2_.refs_4_), custom_call_target="tpu_custom_call" | custom-call | flops 47185920 | bytes 737280 | tf_op jit(solution)/shard_map/pallas_call | solution.py:435
  14.4 0.0 copy-start.3
  14.4 0.0 copy-start.1
  14.4 0.3 collective-permute-done.2.refs_0_
  14.7 0.4 shard_map.123
  15.1 1.8 %collective-permute-start.4 = (bf16[16,720]{1,0:T(8,128)(2,1)S(1)}, bf16[16,720]{1,0:T(8,128)(2,1)S(1)}, u32[]{:S(2)}, u32[]{:S(2)}) collective-permute-start(bf16[16,720]{1,0:T(8,128)(2,1)S(1)} %get-tuple-element.64), channel_id=1, source_target_pairs={{0,13},{1,12},{2,15},{3,14},{4,9},{5,8},{6,11},{7,10},{8,5},{9,4},... | collective-permute-start | bytes 69128 | tf_op jit(solution)/shard_map/ppermute | solution.py:348
  16.9 0.1 collective-permute-start.5
  17.1 2.2 %collective-permute-start.6 = (bf16[16,720]{1,0:T(8,128)(2,1)S(1)}, bf16[16,720]{1,0:T(8,128)(2,1)S(1)}, u32[]{:S(2)}, u32[]{:S(2)}) collective-permute-start(bf16[16,720]{1,0:T(8,128)(2,1)S(1)} %get-tuple-element.66), channel_id=1, source_target_pairs={{0,5},{1,4},{2,7},{3,6},{4,1},{5,0},{6,3},{7,2},{8,13},{9,12},{10,... | collective-permute-start | bytes 69128 | tf_op jit(solution)/shard_map/ppermute | solution.py:348
  19.2 0.2 collective-permute-start.7
  19.4 0.1 shard_map.125.gains_ref.refs_5_.refs_4_
  19.5 0.6 %shard_map.124.ups_ref.refs_7_.refs_6_ = bf16[4,360,720]{2,1,0:T(8,128)(2,1)S(1)} custom-call(bf16[360,2880]{1,0:T(8,128)(2,1)S(1)} %bitcast.13), custom_call_target="tpu_custom_call" | custom-call | bytes 4147200 | tf_op jit(solution)/shard_map/pallas_call | solution.py:448
  20.1 0.1 collective-permute-done.4.refs_0_
  20.2 1.5 %collective-permute-done.5.refs_1_ = bf16[16,720]{1,0:T(8,128)(2,1)S(1)} collective-permute-done((bf16[16,720]{1,0:T(8,128)(2,1)S(1)}, bf16[16,720]{1,0:T(8,128)(2,1)S(1)}, u32[]{:S(2)}, u32[]{:S(2)}) %collective-permute-start.5) | collective-permute-done | bytes 23072 | tf_op jit(solution)/shard_map/ppermute | solution.py:348
  21.7 0.5 %collective-permute-start.8 = (bf16[64,720]{1,0:T(8,128)(2,1)S(1)}, bf16[64,720]{1,0:T(8,128)(2,1)S(1)}, u32[]{:S(2)}, u32[]{:S(2)}) collective-permute-start(bf16[64,720]{1,0:T(8,128)(2,1)S(1)} %shard_map.126.block_ref), channel_id=1, source_target_pairs={{0,3},{1,2},{2,1},{3,0},{4,7},{5,6},{6,5},{7,4},{8,11},{9,10},{10,... | collective-permute-start | bytes 276488 | tf_op jit(solution)/shard_map/ppermute | solution.py:334
  22.2 0.4 collective-permute-start.10
  22.6 0.6 %shard_map.128.refs_7_.downs_ref = bf16[4,360,720]{2,1,0:T(8,128)(2,1)S(1)} custom-call(bf16[360,2880]{1,0:T(8,128)(2,1)S(1)} %bitcast.14), custom_call_target="tpu_custom_call" | custom-call | bytes 4147200 | tf_op jit(solution)/shard_map/pallas_call | solution.py:459
  23.2 0.4 %shard_map.127 = (f32[64,360]{1,0:T(8,128)S(1)}, f32[64,360]{1,0:T(8,128)S(1)}, f32[64,128]{1,0:T(8,128)S(1)}) custom-call(bf16[64,720]{1,0:T(8,128)(2,1)S(1)} %shard_map.126.block_ref, f32[4,1,720]{2,1,0:T(1,128)S(1)} %shard_map.125.gains_ref.refs_5_.refs_4_, bf16[4,360,720]{2,1,0:T(8,128)(2,1)S(1)} %shard_map.121.gates_ref.refs_6_.refs_5_, ...), custom_call_target="tpu_custom_call" | custom-call | flops 66355200 | bytes 1036800 | tf_op jit(solution)/shard_map/pallas_call | solution.py:457
  23.7 2.9 %collective-permute-done.8.refs_1_ = bf16[64,720]{1,0:T(8,128)(2,1)S(1)} collective-permute-done((bf16[64,720]{1,0:T(8,128)(2,1)S(1)}, bf16[64,720]{1,0:T(8,128)(2,1)S(1)}, u32[]{:S(2)}, u32[]{:S(2)}) %collective-permute-start.8) | collective-permute-done | bytes 92192 | tf_op jit(solution)/shard_map/ppermute | solution.py:334
  26.6 0.1 collective-permute-start.9
  26.7 0.4 collective-permute-start.20
  27.1 0.1 collective-permute-start.19
  27.2 0.8 %shard_map.129 = (f32[64,360]{1,0:T(8,128)S(1)}, f32[64,360]{1,0:T(8,128)S(1)}, f32[64,128]{1,0:T(8,128)S(1)}) custom-call(bf16[64,720]{1,0:T(8,128)(2,1)S(1)} %collective-permute-done.10.refs_0_, bf16[64,720]{1,0:T(8,128)(2,1)S(1)} %collective-permute-done.8.refs_1_, f32[64,360]{1,0:T(8,128)S(1)} %get-tuple-element.73.refs_2_, ...), custom_call_target="tpu_custom_call" | custom-call | flops 66355200 | bytes 1036800 | tf_op jit(solution)/shard_map/pallas_call | solution.py:465
  28.0 0.7 %shard_map.130 = (bf16[2,64,720]{2,1,0:T(8,128)(2,1)S(1)}, bf16[64,360]{1,0:T(8,128)(2,1)S(1)}) custom-call(bf16[64,720]{1,0:T(8,128)(2,1)S(1)} %collective-permute-done.9.refs_0_, f32[64,360]{1,0:T(8,128)S(1)} %get-tuple-element.78.refs_1_, f32[64,360]{1,0:T(8,128)S(1)} %get-tuple-element.79.refs_2_, f32[64,128]{1,0:T(8,128)S(1)} %get-tuple-element.80.refs_3_, ...), custom_call_target="tpu_custom_call" | custom-call | flops 66355200 | bytes 1036800 | tf_op jit(solution)/shard_map/pallas_call | solution.py:468
  28.7 0.5 %collective-permute-start.11 = (bf16[2,64,720]{2,1,0:T(8,128)(2,1)S(1)}, bf16[2,64,720]{2,1,0:T(8,128)(2,1)S(1)}, u32[]{:S(2)}, u32[]{:S(2)}) collective-permute-start(bf16[2,64,720]{2,1,0:T(8,128)(2,1)S(1)} %get-tuple-element.82), channel_id=1, source_target_pairs={{0,1},{1,0},{2,3},{3,2},{4,5},{5,4},{6,7},{7,6},{8,9},{9,8},{10,11... | collective-permute-start | bytes 552968 | tf_op jit(solution)/shard_map/ppermute | solution.py:334
  29.2 0.3 shard_map.131.kept_ref
  29.5 0.7 %collective-permute-done.11.given_ref = bf16[2,64,720]{2,1,0:T(8,128)(2,1)S(1)} collective-permute-done((bf16[2,64,720]{2,1,0:T(8,128)(2,1)S(1)}, bf16[2,64,720]{2,1,0:T(8,128)(2,1)S(1)}, u32[]{:S(2)}, u32[]{:S(2)}) %collective-permute-start.11) | collective-permute-done | bytes 184352 | tf_op jit(solution)/shard_map/ppermute | solution.py:334
  30.3 0.8 %collective-permute-start.12 = (bf16[32,720]{1,0:T(8,128)(2,1)S(1)}, bf16[32,720]{1,0:T(8,128)(2,1)S(1)}, u32[]{:S(2)}, u32[]{:S(2)}) collective-permute-start(bf16[32,720]{1,0:T(8,128)(2,1)S(1)} %get-tuple-element.84), channel_id=1, source_target_pairs={{0,3},{1,2},{2,1},{3,0},{4,7},{5,6},{6,5},{7,4},{8,11},{9,10},{10,... | collective-permute-start | bytes 138248 | tf_op jit(solution)/shard_map/ppermute | solution.py:334
  31.1 1.0 %collective-permute-start.15 = (bf16[32,720]{1,0:T(8,128)(2,1)S(1)}, bf16[32,720]{1,0:T(8,128)(2,1)S(1)}, u32[]{:S(2)}, u32[]{:S(2)}) collective-permute-start(bf16[32,720]{1,0:T(8,128)(2,1)S(1)} %get-tuple-element.88), channel_id=1, source_target_pairs={{0,3},{1,2},{2,1},{3,0},{4,7},{5,6},{6,5},{7,4},{8,11},{9,10},{10,... | collective-permute-start | bytes 138248 | tf_op jit(solution)/shard_map/ppermute | solution.py:334
  32.1 1.8 %collective-permute-done.12.refs_1_ = bf16[32,720]{1,0:T(8,128)(2,1)S(1)} collective-permute-done((bf16[32,720]{1,0:T(8,128)(2,1)S(1)}, bf16[32,720]{1,0:T(8,128)(2,1)S(1)}, u32[]{:S(2)}, u32[]{:S(2)}) %collective-permute-start.12) | collective-permute-done | bytes 46112 | tf_op jit(solution)/shard_map/ppermute | solution.py:334
  33.9 2.2 %collective-permute-start.13 = (bf16[16,720]{1,0:T(8,128)(2,1)S(1)}, bf16[16,720]{1,0:T(8,128)(2,1)S(1)}, u32[]{:S(2)}, u32[]{:S(2)}) collective-permute-start(bf16[16,720]{1,0:T(8,128)(2,1)S(1)} %get-tuple-element.85), channel_id=1, source_target_pairs={{0,13},{1,12},{2,15},{3,14},{4,9},{5,8},{6,11},{7,10},{8,5},{9,4},... | collective-permute-start | bytes 69128 | tf_op jit(solution)/shard_map/ppermute | solution.py:348
  36.1 0.0 collective-permute-start.14
  36.2 2.6 %collective-permute-start.16 = (bf16[16,720]{1,0:T(8,128)(2,1)S(1)}, bf16[16,720]{1,0:T(8,128)(2,1)S(1)}, u32[]{:S(2)}, u32[]{:S(2)}) collective-permute-start(bf16[16,720]{1,0:T(8,128)(2,1)S(1)} %get-tuple-element.89), channel_id=1, source_target_pairs={{0,5},{1,4},{2,7},{3,6},{4,1},{5,0},{6,3},{7,2},{8,13},{9,12},{10,... | collective-permute-start | bytes 69128 | tf_op jit(solution)/shard_map/ppermute | solution.py:348
  38.8 0.9 %shard_map.135.refs_6_ = bf16[720,256]{1,0:T(8,128)(2,1)S(1)} custom-call(bf16[512,256]{1,0:T(8,128)(2,1)S(1)} %get-tuple-element.94.refs_0_, bf16[512,256]{1,0:T(8,128)(2,1)S(1)} %collective-permute-done.19.refs_1_, bf16[512,256]{1,0:T(8,128)(2,1)S(1)} %collective-permute-done.20.refs_2_, bf16[512,256]{1,0:T(8,128)(2,1)S(1)} %collective-permute-done.18.refs_3_, ...), custom_call_target="tpu_custom_call" | custom-call | flops 754974720 | bytes 2949120 | tf_op jit(solution)/shard_map/pallas_call | solution.py:475
  39.7 1.3 %collective-permute-done.14.refs_1_ = bf16[16,720]{1,0:T(8,128)(2,1)S(1)} collective-permute-done((bf16[16,720]{1,0:T(8,128)(2,1)S(1)}, bf16[16,720]{1,0:T(8,128)(2,1)S(1)}, u32[]{:S(2)}, u32[]{:S(2)}) %collective-permute-start.14) | collective-permute-done | bytes 23072 | tf_op jit(solution)/shard_map/ppermute | solution.py:348
  41.1 0.2 collective-permute-done.16.refs_2_
  41.3 1.1 %shard_map.136 = bf16[720,256]{1,0:T(8,128)(2,1)} custom-call(bf16[16,720]{1,0:T(8,128)(2,1)S(1)} %collective-permute-done.13.refs_0_, bf16[16,720]{1,0:T(8,128)(2,1)S(1)} %collective-permute-done.14.refs_1_, bf16[16,720]{1,0:T(8,128)(2,1)S(1)} %collective-permute-done.16.refs_2_, bf16[16,720]{1,0:T(8,128)(2,1)S(1)} %collective-permute-done.17.refs_3_, ...), custom_call_target="tpu_custom_call" | custom-call | tf_op jit(solution)/shard_map/pallas_call | solution.py:494
  (22 shorter events, 0.1 us)
Async XLA Ops:
  0.8 7.3 %collective-permute-start = (bf16[128,256]{1,0:T(8,128)(2,1)S(1)}, bf16[128,256]{1,0:T(8,128)(2,1)S(1)}, u32[]{:S(2)}, u32[]{:S(2)}) collective-permute-start(bf16[128,256]{1,0:T(8,128)(2,1)S(1)} %slice.3), channel_id=1, source_target_pairs={{0,4},{4,8},{8,12},{12,0},{1,5},{5,9},{9,13},{13,1},{2,6},{6,10},{... | collective-permute-start | bytes 196616 | tf_op jit(solution)/shard_map/ppermute | solution.py:385
  3.9 5.2 %copy-start = (bf16[1,2880,360]{1,2,0:T(8,128)(2,1)S(1)}, bf16[1,2880,360]{1,2,0:T(8,128)(2,1)}, u32[]{:S(2)}) copy-start(bf16[1,2880,360]{1,2,0:T(8,128)(2,1)} %param.21) | copy-start | bytes 6220804
  9.0 4.2 %collective-permute-start.1 = (bf16[64,512]{1,0:T(8,128)(2,1)S(1)}, bf16[64,512]{1,0:T(8,128)(2,1)S(1)}, u32[]{:S(2)}, u32[]{:S(2)}) collective-permute-start(bf16[64,512]{1,0:T(8,128)(2,1)S(1)} %get-tuple-element.59.rows_ref), channel_id=1, source_target_pairs={{0,3},{1,2},{2,1},{3,0},{4,7},{5,6},{6,5},{7,4},{8,11},{9,10},{10,... | collective-permute-start | bytes 196616 | tf_op jit(solution)/shard_map/ppermute | solution.py:334
  9.7 17.4 %collective-permute-start.18 = (bf16[512,256]{1,0:T(8,128)(2,1)S(1)}, bf16[512,256]{1,0:T(8,128)(2,1)S(1)}, u32[]{:S(2)}, u32[]{:S(2)}) collective-permute-start(bf16[512,256]{1,0:T(8,128)(2,1)S(1)} %get-tuple-element.94.refs_0_), channel_id=1, source_target_pairs={{0,3},{1,2},{2,1},{3,0},{4,7},{5,6},{6,5},{7,4},{8,11},{9,10},{10,... | collective-permute-start | bytes 786440 | tf_op jit(solution)/shard_map/ppermute | solution.py:334
  11.5 2.3 %collective-permute-start.3 = (bf16[64,512]{1,0:T(8,128)(2,1)S(1)}, bf16[64,512]{1,0:T(8,128)(2,1)S(1)}, u32[]{:S(2)}, u32[]{:S(2)}) collective-permute-start(bf16[64,512]{1,0:T(8,128)(2,1)S(1)} %get-tuple-element.59.rows_ref), channel_id=1, source_target_pairs={{0,1},{1,0},{2,3},{3,2},{4,5},{5,4},{6,7},{7,6},{8,9},{9,8},{10,11... | collective-permute-start | bytes 196616 | tf_op jit(solution)/shard_map/ppermute | solution.py:334
  13.2 1.6 %collective-permute-start.2 = (bf16[64,512]{1,0:T(8,128)(2,1)S(1)}, bf16[64,512]{1,0:T(8,128)(2,1)S(1)}, u32[]{:S(2)}, u32[]{:S(2)}) collective-permute-start(bf16[64,512]{1,0:T(8,128)(2,1)S(1)} %collective-permute-done.1.refs_1_), channel_id=1, source_target_pairs={{0,1},{1,0},{2,3},{3,2},{4,5},{5,4},{6,7},{7,6},{8,9},{9,8},{10,11... | collective-permute-start | bytes 196616 | tf_op jit(solution)/shard_map/ppermute | solution.py:334
  14.4 5.0 %copy-start.3 = (f32[2880]{0:T(1024)S(1)}, f32[2880]{0:T(1024)}, u32[]{:S(2)}) copy-start(f32[2880]{0:T(1024)} %gain_ref.1) | copy-start | bytes 34564
  14.4 5.0 %copy-start.1 = (bf16[1,2880,360]{1,2,0:T(8,128)(2,1)S(1)}, bf16[1,2880,360]{1,2,0:T(8,128)(2,1)}, u32[]{:S(2)}) copy-start(bf16[1,2880,360]{1,2,0:T(8,128)(2,1)} %param.22) | copy-start | bytes 6220804
  15.1 5.1 %collective-permute-start.4 = (bf16[16,720]{1,0:T(8,128)(2,1)S(1)}, bf16[16,720]{1,0:T(8,128)(2,1)S(1)}, u32[]{:S(2)}, u32[]{:S(2)}) collective-permute-start(bf16[16,720]{1,0:T(8,128)(2,1)S(1)} %get-tuple-element.64), channel_id=1, source_target_pairs={{0,13},{1,12},{2,15},{3,14},{4,9},{5,8},{6,11},{7,10},{8,5},{9,4},... | collective-permute-start | bytes 69128 | tf_op jit(solution)/shard_map/ppermute | solution.py:348
  16.9 4.8 %collective-permute-start.5 = (bf16[16,720]{1,0:T(8,128)(2,1)S(1)}, bf16[16,720]{1,0:T(8,128)(2,1)S(1)}, u32[]{:S(2)}, u32[]{:S(2)}) collective-permute-start(bf16[16,720]{1,0:T(8,128)(2,1)S(1)} %get-tuple-element.65), channel_id=1, source_target_pairs={{0,9},{1,8},{2,11},{3,10},{4,13},{5,12},{6,15},{7,14},{8,1},{9,0},... | collective-permute-start | bytes 69128 | tf_op jit(solution)/shard_map/ppermute | solution.py:348
  17.1 4.6 %collective-permute-start.6 = (bf16[16,720]{1,0:T(8,128)(2,1)S(1)}, bf16[16,720]{1,0:T(8,128)(2,1)S(1)}, u32[]{:S(2)}, u32[]{:S(2)}) collective-permute-start(bf16[16,720]{1,0:T(8,128)(2,1)S(1)} %get-tuple-element.66), channel_id=1, source_target_pairs={{0,5},{1,4},{2,7},{3,6},{4,1},{5,0},{6,3},{7,2},{8,13},{9,12},{10,... | collective-permute-start | bytes 69128 | tf_op jit(solution)/shard_map/ppermute | solution.py:348
  19.2 2.5 %collective-permute-start.7 = (bf16[16,720]{1,0:T(8,128)(2,1)S(1)}, bf16[16,720]{1,0:T(8,128)(2,1)S(1)}, u32[]{:S(2)}, u32[]{:S(2)}) collective-permute-start(bf16[16,720]{1,0:T(8,128)(2,1)S(1)} %get-tuple-element.67), channel_id=1, source_target_pairs={{0,1},{1,0},{2,3},{3,2},{4,5},{5,4},{6,7},{7,6},{8,9},{9,8},{10,11... | collective-permute-start | bytes 69128 | tf_op jit(solution)/shard_map/ppermute | solution.py:348
  19.5 3.2 %copy-start.2 = (bf16[1,360,2880]{2,1,0:T(8,128)(2,1)S(1)}, bf16[1,360,2880]{2,1,0:T(8,128)(2,1)}, u32[]{:S(2)}) copy-start(bf16[1,360,2880]{2,1,0:T(8,128)(2,1)} %param.23) | copy-start | bytes 6220804
  21.7 4.9 %collective-permute-start.8 = (bf16[64,720]{1,0:T(8,128)(2,1)S(1)}, bf16[64,720]{1,0:T(8,128)(2,1)S(1)}, u32[]{:S(2)}, u32[]{:S(2)}) collective-permute-start(bf16[64,720]{1,0:T(8,128)(2,1)S(1)} %shard_map.126.block_ref), channel_id=1, source_target_pairs={{0,3},{1,2},{2,1},{3,0},{4,7},{5,6},{6,5},{7,4},{8,11},{9,10},{10,... | collective-permute-start | bytes 276488 | tf_op jit(solution)/shard_map/ppermute | solution.py:334
  22.2 5.0 %collective-permute-start.10 = (bf16[64,720]{1,0:T(8,128)(2,1)S(1)}, bf16[64,720]{1,0:T(8,128)(2,1)S(1)}, u32[]{:S(2)}, u32[]{:S(2)}) collective-permute-start(bf16[64,720]{1,0:T(8,128)(2,1)S(1)} %shard_map.126.block_ref), channel_id=1, source_target_pairs={{0,1},{1,0},{2,3},{3,2},{4,5},{5,4},{6,7},{7,6},{8,9},{9,8},{10,11... | collective-permute-start | bytes 276488 | tf_op jit(solution)/shard_map/ppermute | solution.py:334
  26.6 1.4 %collective-permute-start.9 = (bf16[64,720]{1,0:T(8,128)(2,1)S(1)}, bf16[64,720]{1,0:T(8,128)(2,1)S(1)}, u32[]{:S(2)}, u32[]{:S(2)}) collective-permute-start(bf16[64,720]{1,0:T(8,128)(2,1)S(1)} %collective-permute-done.8.refs_1_), channel_id=1, source_target_pairs={{0,1},{1,0},{2,3},{3,2},{4,5},{5,4},{6,7},{7,6},{8,9},{9,8},{10,11... | collective-permute-start | bytes 276488 | tf_op jit(solution)/shard_map/ppermute | solution.py:334
  26.7 12.1 %collective-permute-start.20 = (bf16[512,256]{1,0:T(8,128)(2,1)S(1)}, bf16[512,256]{1,0:T(8,128)(2,1)S(1)}, u32[]{:S(2)}, u32[]{:S(2)}) collective-permute-start(bf16[512,256]{1,0:T(8,128)(2,1)S(1)} %get-tuple-element.94.refs_0_), channel_id=1, source_target_pairs={{0,1},{1,0},{2,3},{3,2},{4,5},{5,4},{6,7},{7,6},{8,9},{9,8},{10,11... | collective-permute-start | bytes 786440 | tf_op jit(solution)/shard_map/ppermute | solution.py:334
  27.1 11.7 %collective-permute-start.19 = (bf16[512,256]{1,0:T(8,128)(2,1)S(1)}, bf16[512,256]{1,0:T(8,128)(2,1)S(1)}, u32[]{:S(2)}, u32[]{:S(2)}) collective-permute-start(bf16[512,256]{1,0:T(8,128)(2,1)S(1)} %collective-permute-done.18.refs_3_), channel_id=1, source_target_pairs={{0,1},{1,0},{2,3},{3,2},{4,5},{5,4},{6,7},{7,6},{8,9},{9,8},{10,11... | collective-permute-start | bytes 786440 | tf_op jit(solution)/shard_map/ppermute | solution.py:334
  28.7 1.5 %collective-permute-start.11 = (bf16[2,64,720]{2,1,0:T(8,128)(2,1)S(1)}, bf16[2,64,720]{2,1,0:T(8,128)(2,1)S(1)}, u32[]{:S(2)}, u32[]{:S(2)}) collective-permute-start(bf16[2,64,720]{2,1,0:T(8,128)(2,1)S(1)} %get-tuple-element.82), channel_id=1, source_target_pairs={{0,1},{1,0},{2,3},{3,2},{4,5},{5,4},{6,7},{7,6},{8,9},{9,8},{10,11... | collective-permute-start | bytes 552968 | tf_op jit(solution)/shard_map/ppermute | solution.py:334
  30.3 3.6 %collective-permute-start.12 = (bf16[32,720]{1,0:T(8,128)(2,1)S(1)}, bf16[32,720]{1,0:T(8,128)(2,1)S(1)}, u32[]{:S(2)}, u32[]{:S(2)}) collective-permute-start(bf16[32,720]{1,0:T(8,128)(2,1)S(1)} %get-tuple-element.84), channel_id=1, source_target_pairs={{0,3},{1,2},{2,1},{3,0},{4,7},{5,6},{6,5},{7,4},{8,11},{9,10},{10,... | collective-permute-start | bytes 138248 | tf_op jit(solution)/shard_map/ppermute | solution.py:334
  31.1 5.0 %collective-permute-start.15 = (bf16[32,720]{1,0:T(8,128)(2,1)S(1)}, bf16[32,720]{1,0:T(8,128)(2,1)S(1)}, u32[]{:S(2)}, u32[]{:S(2)}) collective-permute-start(bf16[32,720]{1,0:T(8,128)(2,1)S(1)} %get-tuple-element.88), channel_id=1, source_target_pairs={{0,3},{1,2},{2,1},{3,0},{4,7},{5,6},{6,5},{7,4},{8,11},{9,10},{10,... | collective-permute-start | bytes 138248 | tf_op jit(solution)/shard_map/ppermute | solution.py:334
  33.9 5.8 %collective-permute-start.13 = (bf16[16,720]{1,0:T(8,128)(2,1)S(1)}, bf16[16,720]{1,0:T(8,128)(2,1)S(1)}, u32[]{:S(2)}, u32[]{:S(2)}) collective-permute-start(bf16[16,720]{1,0:T(8,128)(2,1)S(1)} %get-tuple-element.85), channel_id=1, source_target_pairs={{0,13},{1,12},{2,15},{3,14},{4,9},{5,8},{6,11},{7,10},{8,5},{9,4},... | collective-permute-start | bytes 69128 | tf_op jit(solution)/shard_map/ppermute | solution.py:348
  36.1 5.0 %collective-permute-start.14 = (bf16[16,720]{1,0:T(8,128)(2,1)S(1)}, bf16[16,720]{1,0:T(8,128)(2,1)S(1)}, u32[]{:S(2)}, u32[]{:S(2)}) collective-permute-start(bf16[16,720]{1,0:T(8,128)(2,1)S(1)} %get-tuple-element.86), channel_id=1, source_target_pairs={{0,9},{1,8},{2,11},{3,10},{4,13},{5,12},{6,15},{7,14},{8,1},{9,0},... | collective-permute-start | bytes 69128 | tf_op jit(solution)/shard_map/ppermute | solution.py:348
  36.2 5.1 %collective-permute-start.16 = (bf16[16,720]{1,0:T(8,128)(2,1)S(1)}, bf16[16,720]{1,0:T(8,128)(2,1)S(1)}, u32[]{:S(2)}, u32[]{:S(2)}) collective-permute-start(bf16[16,720]{1,0:T(8,128)(2,1)S(1)} %get-tuple-element.89), channel_id=1, source_target_pairs={{0,5},{1,4},{2,7},{3,6},{4,1},{5,0},{6,3},{7,2},{8,13},{9,12},{10,... | collective-permute-start | bytes 69128 | tf_op jit(solution)/shard_map/ppermute | solution.py:348
  38.8 2.5 %collective-permute-start.17 = (bf16[16,720]{1,0:T(8,128)(2,1)S(1)}, bf16[16,720]{1,0:T(8,128)(2,1)S(1)}, u32[]{:S(2)}, u32[]{:S(2)}) collective-permute-start(bf16[16,720]{1,0:T(8,128)(2,1)S(1)} %get-tuple-element.90), channel_id=1, source_target_pairs={{0,1},{1,0},{2,3},{3,2},{4,5},{5,4},{6,7},{7,6},{8,9},{9,8},{10,11... | collective-permute-start | bytes 69128 | tf_op jit(solution)/shard_map/ppermute | solution.py:348

commit v12 on v11

--- a/solution.py
+++ b/solution.py
@@ -28,13 +28,13 @@
     return lax.dot_general(a, b, dims, preferred_element_type=jnp.float32)
 
 
-def call(kernel, outs, n_in, scratch=(), hbm=(), smem=(), flops=0, moved=0):
-    spaces = [pltpu.HBM if i in hbm else pltpu.SMEM if i in smem else pltpu.VMEM for i in range(n_in)]
+def call(kernel, outs, n_in, scratch=(), hbm=(), out_space=pltpu.VMEM, flops=0, moved=0):
+    spaces = [pltpu.HBM if i in hbm else pltpu.VMEM for i in range(n_in)]
     return pl.pallas_call(
         kernel,
         out_shape=outs,
         in_specs=[pl.BlockSpec(memory_space=space) for space in spaces],
-        out_specs=jax.tree.map(lambda _: pl.BlockSpec(memory_space=pltpu.VMEM), outs),
+        out_specs=jax.tree.map(lambda _: pl.BlockSpec(memory_space=out_space), outs),
         scratch_shapes=list(scratch),
         compiler_params=pltpu.CompilerParams(vmem_limit_bytes=VMEM_LIMIT),
         cost_estimate=pl.CostEstimate(flops=flops, bytes_accessed=moved, transcendentals=0),
@@ -153,7 +153,7 @@
             mixed = attend_block(pairs, kv_ref[span, g * PAIR : (g + 1) * PAIR], part, allowed)
             store_pairs(mixed, first, late_ref, slice((b - 1) * KEYS_SEEN, b * KEYS_SEEN))
     key, query = key_query(KEYS_SEEN)
-    for g in range(groups):
+    for g in range(mixed_ref.shape[0]):
         _, pairs = group_queries(q_ref, g, groups, 0)
         keys, values = split_pair(kv_ref[:KEYS_SEEN, g * PAIR : (g + 1) * PAIR])
         terms = []
@@ -168,15 +168,22 @@
         copy.wait()
 
 
-def second_kernel(q_ref, before_ref, rim_ref, sinks_ref, late_ref, placing_ref, *refs):
+def second_kernel(q_ref, kv_ref, before_ref, rim_ref, sinks_ref, late_ref, placing_ref, *refs):
     late_rows_ref, mixed_ref, peaks_ref, sums_ref, all_ref, rows_ref = refs
     rim = jnp.where(lax.axis_index("seq") == 0, before_ref[...], rim_ref[...])
-    groups = mixed_ref.shape[0]
+    groups = rim.shape[1] // PAIR
+    key, query = key_query(SPAN)
+    allowed = (key > query) & (key <= query + KEYS_SEEN)
     key, query = key_query(KEYS_SEEN)
     for g in range(groups):
         first, pairs = group_queries(q_ref, g, groups, 0)
         sinks = [sinks_ref[h : h + 1] for h in range(2 * first, 2 * (first + len(pairs)))]
-        keys, values = split_pair(rim[:, g * PAIR : (g + 1) * PAIR])
+        lanes = slice(g * PAIR, (g + 1) * PAIR)
+        if g >= mixed_ref.shape[0]:
+            both = jnp.concatenate([rim[:, lanes], kv_ref[:KEYS_SEEN, lanes]], axis=0)
+            store_pairs(attend_block(pairs, both, sinks, allowed), first, all_ref, slice(0, KEYS_SEEN))
+            continue
+        keys, values = split_pair(rim[:, lanes])
         terms, scales, inverses = [], [], []
         for i, part in enumerate(score(pairs, keys, key > query)):
             sink = sink_row(sinks, i, len(pairs))
@@ -319,15 +326,24 @@
         out_ref[...] = total[k * CAP : (k + 1) * CAP].astype(jnp.bfloat16)
 
 
-def combine_kernel(live, *refs):
+def combine_kernel(live, parts, *refs):
     blocks = refs[:live]
-    mix_hi_ref, mix_lo_ref, resid_ref, out_ref, rows_ref = refs[live:]
+    mix_hi_ref, mix_lo_ref, resid_ref, out_ref, rows_ref, held_ref, sems = refs[live:]
     me = lax.axis_index("seq")
     for k in range(live):
         rows_ref[lax.bitwise_xor(me, live - 1 - k)] = blocks[k][...]
     rows = rows_ref[...].reshape(live * CAP, -1)
-    mixed = dot(rows, mix_hi_ref[...], TN) + dot(rows, mix_lo_ref[...], TN)
-    out_ref[...] = (resid_ref[...].astype(jnp.float32) + mixed).astype(jnp.bfloat16)
+    rows = jnp.concatenate([rows, rows], axis=0)
+    mix = jnp.concatenate([mix_hi_ref[...], mix_lo_ref[...]], axis=0)
+    copies = []
+    for i, (start, stop) in enumerate(parts):
+        part = slice(start, stop)
+        mixed = dot(rows[:, part], mix, TN)
+        held_ref[part] = (resid_ref[part].astype(jnp.float32) + mixed).astype(jnp.bfloat16)
+        copies.append(pltpu.make_async_copy(held_ref.at[part], out_ref.at[part], sems.at[i]))
+        copies[-1].start()
+    for copy in copies:
+        copy.wait()
 
 
 def swap(block, axis, mask):
@@ -386,8 +402,9 @@
     loads = (queries, keyvals, preceding_keyvalues, w_out.T, residual.T)
     groups = keyvals.shape[1] // PAIR
     across = head_rows // PAIR // groups * KEYS_SEEN
-    part_sums = jax.ShapeDtypeStruct((2 * groups, across), jnp.float32)
-    q, _, before, w_t, residual_t, placing, mix_hi, mix_lo, sinks, late, *parts = call(
+    early = (groups + 1) // 2
+    part_sums = jax.ShapeDtypeStruct((2 * early, across), jnp.float32)
+    q, kv, before, w_t, residual_t, placing, mix_hi, mix_lo, sinks, late, *parts = call(
         functools.partial(first_kernel, live),
         (
             *(bf16(*a.shape) for a in loads),
@@ -395,7 +412,7 @@
             jax.ShapeDtypeStruct((heads, KEYS_SEEN), jnp.float32),
             bf16(head_rows, toks - KEYS_SEEN),
             jax.ShapeDtypeStruct((slots, head_rows), jnp.float32),
-            jax.ShapeDtypeStruct((groups, PAIR, across), jnp.float32),
+            jax.ShapeDtypeStruct((early, PAIR, across), jnp.float32),
             part_sums,
             part_sums,
         ),
@@ -413,10 +430,10 @@
     attended, rows = call(
         second_kernel,
         (bf16(head_rows, toks), bf16(slots, head_rows)),
-        n_in=10,
+        n_in=11,
         flops=2 * toks * SPAN * head_rows,
         moved=2 * queries.size,
-    )(q, before, rim, sinks, late, placing, *parts)
+    )(q, kv, before, rim, sinks, late, placing, *parts)
 
     chip_rows = from_chips(rows)
     total = jax.ShapeDtypeStruct((slots, feats), jnp.float32)
@@ -491,11 +508,18 @@
         )
         for block in blocks:
             returned.append(to_seq(block, live - 1 - len(returned)))
+    bounds = [*range(0, feats, SPAN), feats] if feats % 16 == 0 else [0, feats]
+    parts = list(zip(bounds[:-1], bounds[1:]))
     out = call(
-        functools.partial(combine_kernel, live),
+        functools.partial(combine_kernel, live, parts),
         bf16(feats, toks),
         n_in=live + 3,
-        scratch=[pltpu.VMEM((live, CAP, feats), jnp.bfloat16)],
+        scratch=[
+            pltpu.VMEM((live, CAP, feats), jnp.bfloat16),
+            pltpu.VMEM((feats, toks), jnp.bfloat16),
+            pltpu.SemaphoreType.DMA((len(parts),)),
+        ],
+        out_space=pltpu.HBM,
     )(*returned, mix_hi, mix_lo, resid)
     return out.T
 

time: 42.6 us -> 42.5 us (level)
  waiting for transfers between devices: 10.8 us -> 11.7 us
  Pallas kernels: 11.9 us -> 11.1 us
    pallas_call x1, Pallas kernels: 3.45 us -> 2.52 us  [shards(): call(functools.partial(first_kernel, live), (*(bf16(*a.shape) for a in lo...]
    ppermute x1, waiting for transfers between devices: 0.81 us -> 1.73 us  [shards(): rim = lax.ppermute(tail, 'seq', [(i, (i + 1) % size) for i in range(size)])]
  transfers between devices with their start and end apart: 21 -> 21, of which waited for: 10 -> 11; matrix products, arithmetic and copies ran while one was open for 0% -> 0% of each run, Pallas kernels for 23% -> 21%
where the time goes in v12:
time: 42.5 us; the launch traced here: 42.3 us
  starting transfers between devices  18.6 us (44%)
  waiting for transfers between devices  11.7 us (28%)
  Pallas kernels  11.1 us (26%)
  local copies, waits for them, and re-layouts  0.86 us (2%)
    ppermute x8, starting transfers between devices, to_seq(): lax.ppermute(block, ('seq', 'cuts'), [(i, i ^ mask) for i in range(size)])  9.09 us
    ppermute x12, waiting for transfers between devices, swap(): lax.ppermute(block, axis, [(i, i ^ mask) for i in range(lax.axis_size(axi...  6.82 us
    ppermute x12, starting transfers between devices, swap(): lax.ppermute(block, axis, [(i, i ^ mask) for i in range(lax.axis_size(axi...  6.46 us
    ppermute x8, waiting for transfers between devices, to_seq(): lax.ppermute(block, ('seq', 'cuts'), [(i, i ^ mask) for i in range(size)])  3.15 us
    ppermute x1, starting transfers between devices, shards(): rim = lax.ppermute(tail, 'seq', [(i, (i + 1) % size) for i in range(size)])  3.02 us
    pallas_call x1, Pallas kernels, shards(): call(functools.partial(first_kernel, live), (*(bf16(*a.shape) for a in lo...  2.52 us
    ppermute x1, waiting for transfers between devices, shards(): rim = lax.ppermute(tail, 'seq', [(i, (i + 1) % size) for i in range(size)])  1.73 us
    pallas_call x1, Pallas kernels, shards(): call(functools.partial(combine_kernel, live, parts), bf16(feats, toks), n...  1.02 us
  transfers between devices with their start and end apart: 21, of which 11 were waited for; matrix products, arithmetic and copies ran while one was open for 0% of the time, Pallas kernels for 21%

profile of v12, /device:TPU:0, one launch (start us, length us, event | category | flops | bytes accessed | tf_op | source)
XLA Modules:
  0.0 42.3 jit_solution(11333226320321622976)
XLA Ops:
  0.0 0.8 %slice.3 = bf16[128,256]{1,0:T(8,128)(2,1)S(1)} slice(bf16[256,256]{1,0:T(8,128)(2,1)} %refs_4_.1), slice={[128:256], [0:256]} | slice | bytes 131072 | tf_op jit(solution)/shard_map/slice | solution.py:400
  0.8 3.0 %collective-permute-start = (bf16[128,256]{1,0:T(8,128)(2,1)S(1)}, bf16[128,256]{1,0:T(8,128)(2,1)S(1)}, u32[]{:S(2)}, u32[]{:S(2)}) collective-permute-start(bf16[128,256]{1,0:T(8,128)(2,1)S(1)} %slice.3), channel_id=1, source_target_pairs={{0,4},{4,8},{8,12},{12,0},{1,5},{5,9},{9,13},{13,1},{2,6},{6,10},{... | collective-permute-start | bytes 196616 | tf_op jit(solution)/shard_map/ppermute | solution.py:401
  3.9 2.5 %shard_map.118 = (bf16[256,512]{1,0:T(8,128)(2,1)S(1)}, bf16[256,256]{1,0:T(8,128)(2,1)S(1)}, bf16[128,256]{1,0:T(8,128)(2,1)S(1)}, bf16[720,2048]{1,0:T(8,128)(...) custom-call(s32[4,256]{1,0:T(4,128)} %bitcast.17, ...), custom_call_target="tpu_custom_call" | custom-call | flops 134217728 | bytes 3579904 | tf_op jit(solution)/shard_map/pallas_call | solution.py:407
  6.4 1.7 %collective-permute-done.rim_ref = bf16[128,256]{1,0:T(8,128)(2,1)S(1)} collective-permute-done((bf16[128,256]{1,0:T(8,128)(2,1)S(1)}, bf16[128,256]{1,0:T(8,128)(2,1)S(1)}, u32[]{:S(2)}, u32[]{:S(2)}) %collective-permute-start) | collective-permute-done | bytes 65568 | tf_op jit(solution)/shard_map/ppermute | solution.py:401
  8.1 1.0 %shard_map.119 = (bf16[512,256]{1,0:T(8,128)(2,1)S(1)}, bf16[64,512]{1,0:T(8,128)(2,1)S(1)}) custom-call(bf16[256,512]{1,0:T(8,128)(2,1)S(1)} %get-tuple-element.51.q_ref, bf16[256,256]{1,0:T(8,128)(2,1)S(1)} %get-tuple-element.52.kv_ref, bf16[128,256]{1,0:T(8,128)(2,1)S(1)} %get-tuple-element.53.before_ref, ...), custom_call_target="tpu_custom_call" | custom-call | flops 67108864 | bytes 262144 | tf_op jit(solution)/shard_map/pallas_call | solution.py:430
  9.1 0.1 collective-permute-start.1
  9.2 0.6 %shard_map.121.gates_ref.refs_6_.refs_5_ = bf16[4,360,720]{2,1,0:T(8,128)(2,1)S(1)} custom-call(bf16[360,2880]{1,0:T(8,128)(2,1)S(1)} %bitcast.12), custom_call_target="tpu_custom_call" | custom-call | bytes 4147200 | tf_op jit(solution)/shard_map/pallas_call | solution.py:449
  9.8 1.8 %collective-permute-start.18 = (bf16[512,256]{1,0:T(8,128)(2,1)S(1)}, bf16[512,256]{1,0:T(8,128)(2,1)S(1)}, u32[]{:S(2)}, u32[]{:S(2)}) collective-permute-start(bf16[512,256]{1,0:T(8,128)(2,1)S(1)} %get-tuple-element.96.refs_0_), channel_id=1, source_target_pairs={{0,3},{1,2},{2,1},{3,0},{4,7},{5,6},{6,5},{7,4},{8,11},{9,10},{10,... | collective-permute-start | bytes 786440 | tf_op jit(solution)/shard_map/ppermute | solution.py:350
  11.6 0.1 collective-permute-start.3
  11.7 0.5 %shard_map.120.refs_2_ = f32[64,720]{1,0:T(8,128)S(1)} custom-call(bf16[64,512]{1,0:T(8,128)(2,1)S(1)} %get-tuple-element.61.rows_ref, bf16[720,2048]{1,0:T(8,128)(2,1)S(1)} %get-tuple-element.62.w_ref.refs_3_.refs_2_.refs_4_, bf16[720,256]{1,0:T(8,128)(2,1)S(1)} %get-tuple-element.63.residual_ref.refs_5_, bf16[64,256]{1,0:T(8,128)(2,1)S(1)} %get-tuple-element.56.placing_ref), custom_call_target="tpu_custom_call" | custom-call | flops 47185920 | bytes 737280 | tf_op jit(solution)/shard_map/pallas_call | solution.py:441
  12.2 1.1 %collective-permute-done.1.refs_1_ = bf16[64,512]{1,0:T(8,128)(2,1)S(1)} collective-permute-done((bf16[64,512]{1,0:T(8,128)(2,1)S(1)}, bf16[64,512]{1,0:T(8,128)(2,1)S(1)}, u32[]{:S(2)}, u32[]{:S(2)}) %collective-permute-start.1) | collective-permute-done | bytes 65568 | tf_op jit(solution)/shard_map/ppermute | solution.py:350
  13.3 0.6 %collective-permute-start.2 = (bf16[64,512]{1,0:T(8,128)(2,1)S(1)}, bf16[64,512]{1,0:T(8,128)(2,1)S(1)}, u32[]{:S(2)}, u32[]{:S(2)}) collective-permute-start(bf16[64,512]{1,0:T(8,128)(2,1)S(1)} %collective-permute-done.1.refs_1_), channel_id=1, source_target_pairs={{0,1},{1,0},{2,3},{3,2},{4,5},{5,4},{6,7},{7,6},{8,9},{9,8},{10,11... | collective-permute-start | bytes 196616 | tf_op jit(solution)/shard_map/ppermute | solution.py:350
  13.9 0.6 %shard_map.122.refs_1_ = f32[64,720]{1,0:T(8,128)S(1)} custom-call(bf16[64,512]{1,0:T(8,128)(2,1)S(1)} %collective-permute-done.3.refs_0_, bf16[64,512]{1,0:T(8,128)(2,1)S(1)} %collective-permute-done.1.refs_1_, f32[64,720]{1,0:T(8,128)S(1)} %shard_map.120.refs_2_, bf16[720,2048]{1,0:T(8,128)(2,1)S(1)} %get-tuple-element.62.w_ref.refs_3_.refs_2_.refs_4_), custom_call_target="tpu_custom_call" | custom-call | flops 47185920 | bytes 737280 | tf_op jit(solution)/shard_map/pallas_call | solution.py:452
  14.5 0.0 copy-start.3
  14.5 0.0 copy-start.1
  14.5 0.3 collective-permute-done.2.refs_0_
  14.8 0.4 shard_map.123
  15.2 1.8 %collective-permute-start.4 = (bf16[16,720]{1,0:T(8,128)(2,1)S(1)}, bf16[16,720]{1,0:T(8,128)(2,1)S(1)}, u32[]{:S(2)}, u32[]{:S(2)}) collective-permute-start(bf16[16,720]{1,0:T(8,128)(2,1)S(1)} %get-tuple-element.66), channel_id=1, source_target_pairs={{0,13},{1,12},{2,15},{3,14},{4,9},{5,8},{6,11},{7,10},{8,5},{9,4},... | collective-permute-start | bytes 69128 | tf_op jit(solution)/shard_map/ppermute | solution.py:364
  17.0 2.3 %collective-permute-start.6 = (bf16[16,720]{1,0:T(8,128)(2,1)S(1)}, bf16[16,720]{1,0:T(8,128)(2,1)S(1)}, u32[]{:S(2)}, u32[]{:S(2)}) collective-permute-start(bf16[16,720]{1,0:T(8,128)(2,1)S(1)} %get-tuple-element.68), channel_id=1, source_target_pairs={{0,5},{1,4},{2,7},{3,6},{4,1},{5,0},{6,3},{7,2},{8,13},{9,12},{10,... | collective-permute-start | bytes 69128 | tf_op jit(solution)/shard_map/ppermute | solution.py:364
  19.3 0.2 collective-permute-start.7
  19.5 0.1 shard_map.125.gains_ref.refs_5_.refs_4_
  19.5 0.6 %shard_map.124.ups_ref.refs_7_.refs_6_ = bf16[4,360,720]{2,1,0:T(8,128)(2,1)S(1)} custom-call(bf16[360,2880]{1,0:T(8,128)(2,1)S(1)} %bitcast.13), custom_call_target="tpu_custom_call" | custom-call | bytes 4147200 | tf_op jit(solution)/shard_map/pallas_call | solution.py:465
  20.1 0.1 collective-permute-done.4.refs_0_
  20.3 1.1 %collective-permute-done.5.refs_1_ = bf16[16,720]{1,0:T(8,128)(2,1)S(1)} collective-permute-done((bf16[16,720]{1,0:T(8,128)(2,1)S(1)}, bf16[16,720]{1,0:T(8,128)(2,1)S(1)}, u32[]{:S(2)}, u32[]{:S(2)}) %collective-permute-start.5) | collective-permute-done | bytes 23072 | tf_op jit(solution)/shard_map/ppermute | solution.py:364
  21.4 0.4 collective-permute-done.6.refs_2_
  21.8 0.5 %collective-permute-start.8 = (bf16[64,720]{1,0:T(8,128)(2,1)S(1)}, bf16[64,720]{1,0:T(8,128)(2,1)S(1)}, u32[]{:S(2)}, u32[]{:S(2)}) collective-permute-start(bf16[64,720]{1,0:T(8,128)(2,1)S(1)} %shard_map.126.block_ref), channel_id=1, source_target_pairs={{0,3},{1,2},{2,1},{3,0},{4,7},{5,6},{6,5},{7,4},{8,11},{9,10},{10,... | collective-permute-start | bytes 276488 | tf_op jit(solution)/shard_map/ppermute | solution.py:350
  22.3 0.4 %collective-permute-start.10 = (bf16[64,720]{1,0:T(8,128)(2,1)S(1)}, bf16[64,720]{1,0:T(8,128)(2,1)S(1)}, u32[]{:S(2)}, u32[]{:S(2)}) collective-permute-start(bf16[64,720]{1,0:T(8,128)(2,1)S(1)} %shard_map.126.block_ref), channel_id=1, source_target_pairs={{0,1},{1,0},{2,3},{3,2},{4,5},{5,4},{6,7},{7,6},{8,9},{9,8},{10,11... | collective-permute-start | bytes 276488 | tf_op jit(solution)/shard_map/ppermute | solution.py:350
  22.7 0.6 %shard_map.128.refs_7_.downs_ref = bf16[4,360,720]{2,1,0:T(8,128)(2,1)S(1)} custom-call(bf16[360,2880]{1,0:T(8,128)(2,1)S(1)} %bitcast.14), custom_call_target="tpu_custom_call" | custom-call | bytes 4147200 | tf_op jit(solution)/shard_map/pallas_call | solution.py:476
  23.3 0.4 %shard_map.127 = (f32[64,360]{1,0:T(8,128)S(1)}, f32[64,360]{1,0:T(8,128)S(1)}, f32[64,128]{1,0:T(8,128)S(1)}) custom-call(bf16[64,720]{1,0:T(8,128)(2,1)S(1)} %shard_map.126.block_ref, f32[4,1,720]{2,1,0:T(1,128)S(1)} %shard_map.125.gains_ref.refs_5_.refs_4_, bf16[4,360,720]{2,1,0:T(8,128)(2,1)S(1)} %shard_map.121.gates_ref.refs_6_.refs_5_, ...), custom_call_target="tpu_custom_call" | custom-call | flops 66355200 | bytes 1036800 | tf_op jit(solution)/shard_map/pallas_call | solution.py:474
  23.7 2.9 %collective-permute-done.8.refs_1_ = bf16[64,720]{1,0:T(8,128)(2,1)S(1)} collective-permute-done((bf16[64,720]{1,0:T(8,128)(2,1)S(1)}, bf16[64,720]{1,0:T(8,128)(2,1)S(1)}, u32[]{:S(2)}, u32[]{:S(2)}) %collective-permute-start.8) | collective-permute-done | bytes 92192 | tf_op jit(solution)/shard_map/ppermute | solution.py:350
  26.6 0.1 collective-permute-start.9
  26.7 0.4 collective-permute-start.20
  27.1 0.1 collective-permute-start.19
  27.3 0.8 %shard_map.129 = (f32[64,360]{1,0:T(8,128)S(1)}, f32[64,360]{1,0:T(8,128)S(1)}, f32[64,128]{1,0:T(8,128)S(1)}) custom-call(bf16[64,720]{1,0:T(8,128)(2,1)S(1)} %collective-permute-done.10.refs_0_, bf16[64,720]{1,0:T(8,128)(2,1)S(1)} %collective-permute-done.8.refs_1_, f32[64,360]{1,0:T(8,128)S(1)} %get-tuple-element.75.refs_2_, ...), custom_call_target="tpu_custom_call" | custom-call | flops 66355200 | bytes 1036800 | tf_op jit(solution)/shard_map/pallas_call | solution.py:482
  28.0 0.7 %shard_map.130 = (bf16[2,64,720]{2,1,0:T(8,128)(2,1)S(1)}, bf16[64,360]{1,0:T(8,128)(2,1)S(1)}) custom-call(bf16[64,720]{1,0:T(8,128)(2,1)S(1)} %collective-permute-done.9.refs_0_, f32[64,360]{1,0:T(8,128)S(1)} %get-tuple-element.80.refs_1_, f32[64,360]{1,0:T(8,128)S(1)} %get-tuple-element.81.refs_2_, f32[64,128]{1,0:T(8,128)S(1)} %get-tuple-element.82.refs_3_, ...), custom_call_target="tpu_custom_call" | custom-call | flops 66355200 | bytes 1036800 | tf_op jit(solution)/shard_map/pallas_call | solution.py:485
  28.8 0.5 %collective-permute-start.11 = (bf16[2,64,720]{2,1,0:T(8,128)(2,1)S(1)}, bf16[2,64,720]{2,1,0:T(8,128)(2,1)S(1)}, u32[]{:S(2)}, u32[]{:S(2)}) collective-permute-start(bf16[2,64,720]{2,1,0:T(8,128)(2,1)S(1)} %get-tuple-element.84), channel_id=1, source_target_pairs={{0,1},{1,0},{2,3},{3,2},{4,5},{5,4},{6,7},{7,6},{8,9},{9,8},{10,11... | collective-permute-start | bytes 552968 | tf_op jit(solution)/shard_map/ppermute | solution.py:350
  29.2 0.3 shard_map.131.kept_ref
  29.6 0.7 %collective-permute-done.11.given_ref = bf16[2,64,720]{2,1,0:T(8,128)(2,1)S(1)} collective-permute-done((bf16[2,64,720]{2,1,0:T(8,128)(2,1)S(1)}, bf16[2,64,720]{2,1,0:T(8,128)(2,1)S(1)}, u32[]{:S(2)}, u32[]{:S(2)}) %collective-permute-start.11) | collective-permute-done | bytes 184352 | tf_op jit(solution)/shard_map/ppermute | solution.py:350
  30.3 0.1 shard_map.132
  30.4 0.8 %collective-permute-start.12 = (bf16[32,720]{1,0:T(8,128)(2,1)S(1)}, bf16[32,720]{1,0:T(8,128)(2,1)S(1)}, u32[]{:S(2)}, u32[]{:S(2)}) collective-permute-start(bf16[32,720]{1,0:T(8,128)(2,1)S(1)} %get-tuple-element.86), channel_id=1, source_target_pairs={{0,3},{1,2},{2,1},{3,0},{4,7},{5,6},{6,5},{7,4},{8,11},{9,10},{10,... | collective-permute-start | bytes 138248 | tf_op jit(solution)/shard_map/ppermute | solution.py:350
  31.2 1.0 %collective-permute-start.15 = (bf16[32,720]{1,0:T(8,128)(2,1)S(1)}, bf16[32,720]{1,0:T(8,128)(2,1)S(1)}, u32[]{:S(2)}, u32[]{:S(2)}) collective-permute-start(bf16[32,720]{1,0:T(8,128)(2,1)S(1)} %get-tuple-element.90), channel_id=1, source_target_pairs={{0,3},{1,2},{2,1},{3,0},{4,7},{5,6},{6,5},{7,4},{8,11},{9,10},{10,... | collective-permute-start | bytes 138248 | tf_op jit(solution)/shard_map/ppermute | solution.py:350
  32.2 1.8 %collective-permute-done.12.refs_1_ = bf16[32,720]{1,0:T(8,128)(2,1)S(1)} collective-permute-done((bf16[32,720]{1,0:T(8,128)(2,1)S(1)}, bf16[32,720]{1,0:T(8,128)(2,1)S(1)}, u32[]{:S(2)}, u32[]{:S(2)}) %collective-permute-start.12) | collective-permute-done | bytes 46112 | tf_op jit(solution)/shard_map/ppermute | solution.py:350
  34.0 2.4 %collective-permute-start.13 = (bf16[16,720]{1,0:T(8,128)(2,1)S(1)}, bf16[16,720]{1,0:T(8,128)(2,1)S(1)}, u32[]{:S(2)}, u32[]{:S(2)}) collective-permute-start(bf16[16,720]{1,0:T(8,128)(2,1)S(1)} %get-tuple-element.87), channel_id=1, source_target_pairs={{0,13},{1,12},{2,15},{3,14},{4,9},{5,8},{6,11},{7,10},{8,5},{9,4},... | collective-permute-start | bytes 69128 | tf_op jit(solution)/shard_map/ppermute | solution.py:364
  36.4 2.4 %collective-permute-start.16 = (bf16[16,720]{1,0:T(8,128)(2,1)S(1)}, bf16[16,720]{1,0:T(8,128)(2,1)S(1)}, u32[]{:S(2)}, u32[]{:S(2)}) collective-permute-start(bf16[16,720]{1,0:T(8,128)(2,1)S(1)} %get-tuple-element.91), channel_id=1, source_target_pairs={{0,5},{1,4},{2,7},{3,6},{4,1},{5,0},{6,3},{7,2},{8,13},{9,12},{10,... | collective-permute-start | bytes 69128 | tf_op jit(solution)/shard_map/ppermute | solution.py:364
  38.8 0.9 %shard_map.135.refs_6_ = bf16[720,256]{1,0:T(8,128)(2,1)S(1)} custom-call(bf16[512,256]{1,0:T(8,128)(2,1)S(1)} %get-tuple-element.96.refs_0_, bf16[512,256]{1,0:T(8,128)(2,1)S(1)} %collective-permute-done.19.refs_1_, bf16[512,256]{1,0:T(8,128)(2,1)S(1)} %collective-permute-done.20.refs_2_, bf16[512,256]{1,0:T(8,128)(2,1)S(1)} %collective-permute-done.18.refs_3_, ...), custom_call_target="tpu_custom_call" | custom-call | flops 754974720 | bytes 2949120 | tf_op jit(solution)/shard_map/pallas_call | solution.py:492
  39.8 1.5 %collective-permute-done.14.refs_1_ = bf16[16,720]{1,0:T(8,128)(2,1)S(1)} collective-permute-done((bf16[16,720]{1,0:T(8,128)(2,1)S(1)}, bf16[16,720]{1,0:T(8,128)(2,1)S(1)}, u32[]{:S(2)}, u32[]{:S(2)}) %collective-permute-start.14) | collective-permute-done | bytes 23072 | tf_op jit(solution)/shard_map/ppermute | solution.py:364
  41.2 0.1 collective-permute-done.16.refs_2_
  41.3 1.0 %shard_map.136 = bf16[720,256]{1,0:T(8,128)(2,1)} custom-call(bf16[16,720]{1,0:T(8,128)(2,1)S(1)} %collective-permute-done.13.refs_0_, bf16[16,720]{1,0:T(8,128)(2,1)S(1)} %collective-permute-done.14.refs_1_, bf16[16,720]{1,0:T(8,128)(2,1)S(1)} %collective-permute-done.16.refs_2_, bf16[16,720]{1,0:T(8,128)(2,1)S(1)} %collective-permute-done.17.refs_3_, ...), custom_call_target="tpu_custom_call" | custom-call | tf_op jit(solution)/shard_map/pallas_call | solution.py:513
  (22 shorter events, 0.1 us)
Async XLA Ops:
  0.8 7.3 %collective-permute-start = (bf16[128,256]{1,0:T(8,128)(2,1)S(1)}, bf16[128,256]{1,0:T(8,128)(2,1)S(1)}, u32[]{:S(2)}, u32[]{:S(2)}) collective-permute-start(bf16[128,256]{1,0:T(8,128)(2,1)S(1)} %slice.3), channel_id=1, source_target_pairs={{0,4},{4,8},{8,12},{12,0},{1,5},{5,9},{9,13},{13,1},{2,6},{6,10},{... | collective-permute-start | bytes 196616 | tf_op jit(solution)/shard_map/ppermute | solution.py:401
  3.9 5.3 %copy-start = (bf16[1,2880,360]{1,2,0:T(8,128)(2,1)S(1)}, bf16[1,2880,360]{1,2,0:T(8,128)(2,1)}, u32[]{:S(2)}) copy-start(bf16[1,2880,360]{1,2,0:T(8,128)(2,1)} %param.21) | copy-start | bytes 6220804
  9.1 4.1 %collective-permute-start.1 = (bf16[64,512]{1,0:T(8,128)(2,1)S(1)}, bf16[64,512]{1,0:T(8,128)(2,1)S(1)}, u32[]{:S(2)}, u32[]{:S(2)}) collective-permute-start(bf16[64,512]{1,0:T(8,128)(2,1)S(1)} %get-tuple-element.61.rows_ref), channel_id=1, source_target_pairs={{0,3},{1,2},{2,1},{3,0},{4,7},{5,6},{6,5},{7,4},{8,11},{9,10},{10,... | collective-permute-start | bytes 196616 | tf_op jit(solution)/shard_map/ppermute | solution.py:350
  9.8 17.4 %collective-permute-start.18 = (bf16[512,256]{1,0:T(8,128)(2,1)S(1)}, bf16[512,256]{1,0:T(8,128)(2,1)S(1)}, u32[]{:S(2)}, u32[]{:S(2)}) collective-permute-start(bf16[512,256]{1,0:T(8,128)(2,1)S(1)} %get-tuple-element.96.refs_0_), channel_id=1, source_target_pairs={{0,3},{1,2},{2,1},{3,0},{4,7},{5,6},{6,5},{7,4},{8,11},{9,10},{10,... | collective-permute-start | bytes 786440 | tf_op jit(solution)/shard_map/ppermute | solution.py:350
  11.6 2.4 %collective-permute-start.3 = (bf16[64,512]{1,0:T(8,128)(2,1)S(1)}, bf16[64,512]{1,0:T(8,128)(2,1)S(1)}, u32[]{:S(2)}, u32[]{:S(2)}) collective-permute-start(bf16[64,512]{1,0:T(8,128)(2,1)S(1)} %get-tuple-element.61.rows_ref), channel_id=1, source_target_pairs={{0,1},{1,0},{2,3},{3,2},{4,5},{5,4},{6,7},{7,6},{8,9},{9,8},{10,11... | collective-permute-start | bytes 196616 | tf_op jit(solution)/shard_map/ppermute | solution.py:350
  13.3 1.6 %collective-permute-start.2 = (bf16[64,512]{1,0:T(8,128)(2,1)S(1)}, bf16[64,512]{1,0:T(8,128)(2,1)S(1)}, u32[]{:S(2)}, u32[]{:S(2)}) collective-permute-start(bf16[64,512]{1,0:T(8,128)(2,1)S(1)} %collective-permute-done.1.refs_1_), channel_id=1, source_target_pairs={{0,1},{1,0},{2,3},{3,2},{4,5},{5,4},{6,7},{7,6},{8,9},{9,8},{10,11... | collective-permute-start | bytes 196616 | tf_op jit(solution)/shard_map/ppermute | solution.py:350
  14.5 5.0 %copy-start.3 = (f32[2880]{0:T(1024)S(1)}, f32[2880]{0:T(1024)}, u32[]{:S(2)}) copy-start(f32[2880]{0:T(1024)} %gain_ref.1) | copy-start | bytes 34564
  14.5 5.0 %copy-start.1 = (bf16[1,2880,360]{1,2,0:T(8,128)(2,1)S(1)}, bf16[1,2880,360]{1,2,0:T(8,128)(2,1)}, u32[]{:S(2)}) copy-start(bf16[1,2880,360]{1,2,0:T(8,128)(2,1)} %param.22) | copy-start | bytes 6220804
  15.2 5.1 %collective-permute-start.4 = (bf16[16,720]{1,0:T(8,128)(2,1)S(1)}, bf16[16,720]{1,0:T(8,128)(2,1)S(1)}, u32[]{:S(2)}, u32[]{:S(2)}) collective-permute-start(bf16[16,720]{1,0:T(8,128)(2,1)S(1)} %get-tuple-element.66), channel_id=1, source_target_pairs={{0,13},{1,12},{2,15},{3,14},{4,9},{5,8},{6,11},{7,10},{8,5},{9,4},... | collective-permute-start | bytes 69128 | tf_op jit(solution)/shard_map/ppermute | solution.py:364
  17.0 4.4 %collective-permute-start.5 = (bf16[16,720]{1,0:T(8,128)(2,1)S(1)}, bf16[16,720]{1,0:T(8,128)(2,1)S(1)}, u32[]{:S(2)}, u32[]{:S(2)}) collective-permute-start(bf16[16,720]{1,0:T(8,128)(2,1)S(1)} %get-tuple-element.67), channel_id=1, source_target_pairs={{0,9},{1,8},{2,11},{3,10},{4,13},{5,12},{6,15},{7,14},{8,1},{9,0},... | collective-permute-start | bytes 69128 | tf_op jit(solution)/shard_map/ppermute | solution.py:364
  17.0 4.7 %collective-permute-start.6 = (bf16[16,720]{1,0:T(8,128)(2,1)S(1)}, bf16[16,720]{1,0:T(8,128)(2,1)S(1)}, u32[]{:S(2)}, u32[]{:S(2)}) collective-permute-start(bf16[16,720]{1,0:T(8,128)(2,1)S(1)} %get-tuple-element.68), channel_id=1, source_target_pairs={{0,5},{1,4},{2,7},{3,6},{4,1},{5,0},{6,3},{7,2},{8,13},{9,12},{10,... | collective-permute-start | bytes 69128 | tf_op jit(solution)/shard_map/ppermute | solution.py:364
  19.3 2.4 %collective-permute-start.7 = (bf16[16,720]{1,0:T(8,128)(2,1)S(1)}, bf16[16,720]{1,0:T(8,128)(2,1)S(1)}, u32[]{:S(2)}, u32[]{:S(2)}) collective-permute-start(bf16[16,720]{1,0:T(8,128)(2,1)S(1)} %get-tuple-element.69), channel_id=1, source_target_pairs={{0,1},{1,0},{2,3},{3,2},{4,5},{5,4},{6,7},{7,6},{8,9},{9,8},{10,11... | collective-permute-start | bytes 69128 | tf_op jit(solution)/shard_map/ppermute | solution.py:364
  19.5 3.1 %copy-start.2 = (bf16[1,360,2880]{2,1,0:T(8,128)(2,1)S(1)}, bf16[1,360,2880]{2,1,0:T(8,128)(2,1)}, u32[]{:S(2)}) copy-start(bf16[1,360,2880]{2,1,0:T(8,128)(2,1)} %param.23) | copy-start | bytes 6220804
  21.8 4.9 %collective-permute-start.8 = (bf16[64,720]{1,0:T(8,128)(2,1)S(1)}, bf16[64,720]{1,0:T(8,128)(2,1)S(1)}, u32[]{:S(2)}, u32[]{:S(2)}) collective-permute-start(bf16[64,720]{1,0:T(8,128)(2,1)S(1)} %shard_map.126.block_ref), channel_id=1, source_target_pairs={{0,3},{1,2},{2,1},{3,0},{4,7},{5,6},{6,5},{7,4},{8,11},{9,10},{10,... | collective-permute-start | bytes 276488 | tf_op jit(solution)/shard_map/ppermute | solution.py:350
  22.3 5.0 %collective-permute-start.10 = (bf16[64,720]{1,0:T(8,128)(2,1)S(1)}, bf16[64,720]{1,0:T(8,128)(2,1)S(1)}, u32[]{:S(2)}, u32[]{:S(2)}) collective-permute-start(bf16[64,720]{1,0:T(8,128)(2,1)S(1)} %shard_map.126.block_ref), channel_id=1, source_target_pairs={{0,1},{1,0},{2,3},{3,2},{4,5},{5,4},{6,7},{7,6},{8,9},{9,8},{10,11... | collective-permute-start | bytes 276488 | tf_op jit(solution)/shard_map/ppermute | solution.py:350
  26.6 1.4 %collective-permute-start.9 = (bf16[64,720]{1,0:T(8,128)(2,1)S(1)}, bf16[64,720]{1,0:T(8,128)(2,1)S(1)}, u32[]{:S(2)}, u32[]{:S(2)}) collective-permute-start(bf16[64,720]{1,0:T(8,128)(2,1)S(1)} %collective-permute-done.8.refs_1_), channel_id=1, source_target_pairs={{0,1},{1,0},{2,3},{3,2},{4,5},{5,4},{6,7},{7,6},{8,9},{9,8},{10,11... | collective-permute-start | bytes 276488 | tf_op jit(solution)/shard_map/ppermute | solution.py:350
  26.7 12.1 %collective-permute-start.20 = (bf16[512,256]{1,0:T(8,128)(2,1)S(1)}, bf16[512,256]{1,0:T(8,128)(2,1)S(1)}, u32[]{:S(2)}, u32[]{:S(2)}) collective-permute-start(bf16[512,256]{1,0:T(8,128)(2,1)S(1)} %get-tuple-element.96.refs_0_), channel_id=1, source_target_pairs={{0,1},{1,0},{2,3},{3,2},{4,5},{5,4},{6,7},{7,6},{8,9},{9,8},{10,11... | collective-permute-start | bytes 786440 | tf_op jit(solution)/shard_map/ppermute | solution.py:350
  27.1 11.7 %collective-permute-start.19 = (bf16[512,256]{1,0:T(8,128)(2,1)S(1)}, bf16[512,256]{1,0:T(8,128)(2,1)S(1)}, u32[]{:S(2)}, u32[]{:S(2)}) collective-permute-start(bf16[512,256]{1,0:T(8,128)(2,1)S(1)} %collective-permute-done.18.refs_3_), channel_id=1, source_target_pairs={{0,1},{1,0},{2,3},{3,2},{4,5},{5,4},{6,7},{7,6},{8,9},{9,8},{10,11... | collective-permute-start | bytes 786440 | tf_op jit(solution)/shard_map/ppermute | solution.py:350
  28.8 1.5 %collective-permute-start.11 = (bf16[2,64,720]{2,1,0:T(8,128)(2,1)S(1)}, bf16[2,64,720]{2,1,0:T(8,128)(2,1)S(1)}, u32[]{:S(2)}, u32[]{:S(2)}) collective-permute-start(bf16[2,64,720]{2,1,0:T(8,128)(2,1)S(1)} %get-tuple-element.84), channel_id=1, source_target_pairs={{0,1},{1,0},{2,3},{3,2},{4,5},{5,4},{6,7},{7,6},{8,9},{9,8},{10,11... | collective-permute-start | bytes 552968 | tf_op jit(solution)/shard_map/ppermute | solution.py:350
  30.4 3.6 %collective-permute-start.12 = (bf16[32,720]{1,0:T(8,128)(2,1)S(1)}, bf16[32,720]{1,0:T(8,128)(2,1)S(1)}, u32[]{:S(2)}, u32[]{:S(2)}) collective-permute-start(bf16[32,720]{1,0:T(8,128)(2,1)S(1)} %get-tuple-element.86), channel_id=1, source_target_pairs={{0,3},{1,2},{2,1},{3,0},{4,7},{5,6},{6,5},{7,4},{8,11},{9,10},{10,... | collective-permute-start | bytes 138248 | tf_op jit(solution)/shard_map/ppermute | solution.py:350
  31.2 5.1 %collective-permute-start.15 = (bf16[32,720]{1,0:T(8,128)(2,1)S(1)}, bf16[32,720]{1,0:T(8,128)(2,1)S(1)}, u32[]{:S(2)}, u32[]{:S(2)}) collective-permute-start(bf16[32,720]{1,0:T(8,128)(2,1)S(1)} %get-tuple-element.90), channel_id=1, source_target_pairs={{0,3},{1,2},{2,1},{3,0},{4,7},{5,6},{6,5},{7,4},{8,11},{9,10},{10,... | collective-permute-start | bytes 138248 | tf_op jit(solution)/shard_map/ppermute | solution.py:350
  34.0 5.8 %collective-permute-start.13 = (bf16[16,720]{1,0:T(8,128)(2,1)S(1)}, bf16[16,720]{1,0:T(8,128)(2,1)S(1)}, u32[]{:S(2)}, u32[]{:S(2)}) collective-permute-start(bf16[16,720]{1,0:T(8,128)(2,1)S(1)} %get-tuple-element.87), channel_id=1, source_target_pairs={{0,13},{1,12},{2,15},{3,14},{4,9},{5,8},{6,11},{7,10},{8,5},{9,4},... | collective-permute-start | bytes 69128 | tf_op jit(solution)/shard_map/ppermute | solution.py:364
  36.3 4.9 %collective-permute-start.14 = (bf16[16,720]{1,0:T(8,128)(2,1)S(1)}, bf16[16,720]{1,0:T(8,128)(2,1)S(1)}, u32[]{:S(2)}, u32[]{:S(2)}) collective-permute-start(bf16[16,720]{1,0:T(8,128)(2,1)S(1)} %get-tuple-element.88), channel_id=1, source_target_pairs={{0,9},{1,8},{2,11},{3,10},{4,13},{5,12},{6,15},{7,14},{8,1},{9,0},... | collective-permute-start | bytes 69128 | tf_op jit(solution)/shard_map/ppermute | solution.py:364
  36.4 4.9 %collective-permute-start.16 = (bf16[16,720]{1,0:T(8,128)(2,1)S(1)}, bf16[16,720]{1,0:T(8,128)(2,1)S(1)}, u32[]{:S(2)}, u32[]{:S(2)}) collective-permute-start(bf16[16,720]{1,0:T(8,128)(2,1)S(1)} %get-tuple-element.91), channel_id=1, source_target_pairs={{0,5},{1,4},{2,7},{3,6},{4,1},{5,0},{6,3},{7,2},{8,13},{9,12},{10,... | collective-permute-start | bytes 69128 | tf_op jit(solution)/shard_map/ppermute | solution.py:364
  38.8 2.5 %collective-permute-start.17 = (bf16[16,720]{1,0:T(8,128)(2,1)S(1)}, bf16[16,720]{1,0:T(8,128)(2,1)S(1)}, u32[]{:S(2)}, u32[]{:S(2)}) collective-permute-start(bf16[16,720]{1,0:T(8,128)(2,1)S(1)} %get-tuple-element.92), channel_id=1, source_target_pairs={{0,1},{1,0},{2,3},{3,2},{4,5},{5,4},{6,7},{7,6},{8,9},{9,8},{10,11... | collective-permute-start | bytes 69128 | tf_op jit(solution)/shard_map/ppermute | solution.py:364

commit v13 on v12

--- a/solution.py
+++ b/solution.py
@@ -296,7 +296,7 @@
     blocks, refs = refs[: steps - 1], refs[steps - 1 :]
     sums = (refs[0][...], refs[1][...], refs[2][:, :1])
     gains_ref, gates_ref, ups_ref, downs_ref, given_ref, activated_ref = refs[3:]
-    places = range(steps + 1, 2 * steps)
+    places = range(1, steps)
     gate, up, squares = add_features(sums, places, blocks, gains_ref, gates_ref, ups_ref, steps)
     cuts, _, width = gates_ref.shape
     scale = lax.rsqrt(squares / (cuts * width) + norm_eps)
@@ -350,12 +350,12 @@
     return lax.ppermute(block, axis, [(i, i ^ mask) for i in range(lax.axis_size(axis))])
 
 
-def to_chip(block, k):
-    return swap(block, "cuts", CORES * k + 1)
-
-
-def from_chips(block):
-    return [to_chip(block, k) for k in range(1, lax.axis_size("cuts") // CORES)]
+def to_chip(block, k, other=True):
+    return swap(block, "cuts", CORES * k + other)
+
+
+def from_chips(block, other=True):
+    return [to_chip(block, k, other) for k in range(1, lax.axis_size("cuts") // CORES)]
 
 
 def to_seq(block, k):
@@ -470,7 +470,7 @@
     )
     part = dict(flops=slots * w_gate.size, moved=w_gate.size)
     stacked = call(stack_kernel, bf16(slots, feats), n_in=live)(*after(arrived, (ups, gains)))
-    chip_rows = from_chips(stacked)
+    chip_rows = from_chips(stacked, False)
     own = call(functools.partial(expert_own_kernel, steps), sums, n_in=4, **part)(stacked, gains, gates, ups)
     sibling_rows = from_sibling(stacked)
     downs = spread()(after(w_down[0], stacked))
@@ -479,7 +479,7 @@
     blocks = [attended, *relayed_blocks, sibling_block, *chip_blocks]
     chip_rows = after(chip_rows, (own, downs))
     relayed_rows = [from_sibling(b) for b in chip_rows]
-    chips = call(functools.partial(expert_more_kernel, range(steps), steps), sums, n_in=steps + 6, **part)(
+    chips = call(functools.partial(expert_more_kernel, [0, *range(steps + 1, 2 * steps)], steps), sums, n_in=steps + 6, **part)(
         sibling_rows, *chip_rows, *own, gains, gates, ups
     )
     given, activated = call(

time: 42.5 us -> 42.4 us (level)
  transfers between devices with their start and end apart: 21 -> 21, of which waited for: 11 -> 10; matrix products, arithmetic and copies ran while one was open for 0% -> 0% of each run, Pallas kernels for 21% -> 21%
where the time goes in v13:
time: 42.4 us; the launch traced here: 42.3 us
  starting transfers between devices  18.5 us (44%)
  waiting for transfers between devices  11.7 us (28%)
  Pallas kernels  11.1 us (26%)
  local copies, waits for them, and re-layouts  0.86 us (2%)
    ppermute x8, starting transfers between devices, to_seq(): lax.ppermute(block, ('seq', 'cuts'), [(i, i ^ mask) for i in range(size)])  9.15 us
    ppermute x12, waiting for transfers between devices, swap(): lax.ppermute(block, axis, [(i, i ^ mask) for i in range(lax.axis_size(axi...  6.94 us
    ppermute x12, starting transfers between devices, swap(): lax.ppermute(block, axis, [(i, i ^ mask) for i in range(lax.axis_size(axi...  6.33 us
    ppermute x1, starting transfers between devices, shards(): rim = lax.ppermute(tail, 'seq', [(i, (i + 1) % size) for i in range(size)])  3.02 us
    ppermute x8, waiting for transfers between devices, to_seq(): lax.ppermute(block, ('seq', 'cuts'), [(i, i ^ mask) for i in range(size)])  3 us
    pallas_call x1, Pallas kernels, shards(): call(functools.partial(first_kernel, live), (*(bf16(*a.shape) for a in lo...  2.52 us
    ppermute x1, waiting for transfers between devices, shards(): rim = lax.ppermute(tail, 'seq', [(i, (i + 1) % size) for i in range(size)])  1.73 us
    pallas_call x1, Pallas kernels, shards(): call(functools.partial(combine_kernel, live, parts), bf16(feats, toks), n...  1.02 us
  transfers between devices with their start and end apart: 21, of which 10 were waited for; matrix products, arithmetic and copies ran while one was open for 0% of the time, Pallas kernels for 21%

profile of v13, /device:TPU:0, one launch (start us, length us, event | category | flops | bytes accessed | tf_op | source)
XLA Modules:
  0.0 42.3 jit_solution(4437996804037162966)
XLA Ops:
  0.0 0.8 %slice.3 = bf16[128,256]{1,0:T(8,128)(2,1)S(1)} slice(bf16[256,256]{1,0:T(8,128)(2,1)} %refs_4_.1), slice={[128:256], [0:256]} | slice | bytes 131072 | tf_op jit(solution)/shard_map/slice | solution.py:400
  0.8 3.0 %collective-permute-start = (bf16[128,256]{1,0:T(8,128)(2,1)S(1)}, bf16[128,256]{1,0:T(8,128)(2,1)S(1)}, u32[]{:S(2)}, u32[]{:S(2)}) collective-permute-start(bf16[128,256]{1,0:T(8,128)(2,1)S(1)} %slice.3), channel_id=1, source_target_pairs={{0,4},{4,8},{8,12},{12,0},{1,5},{5,9},{9,13},{13,1},{2,6},{6,10},{... | collective-permute-start | bytes 196616 | tf_op jit(solution)/shard_map/ppermute | solution.py:401
  3.9 2.5 %shard_map.118 = (bf16[256,512]{1,0:T(8,128)(2,1)S(1)}, bf16[256,256]{1,0:T(8,128)(2,1)S(1)}, bf16[128,256]{1,0:T(8,128)(2,1)S(1)}, bf16[720,2048]{1,0:T(8,128)(...) custom-call(s32[4,256]{1,0:T(4,128)} %bitcast.17, ...), custom_call_target="tpu_custom_call" | custom-call | flops 134217728 | bytes 3579904 | tf_op jit(solution)/shard_map/pallas_call | solution.py:407
  6.4 1.7 %collective-permute-done.rim_ref = bf16[128,256]{1,0:T(8,128)(2,1)S(1)} collective-permute-done((bf16[128,256]{1,0:T(8,128)(2,1)S(1)}, bf16[128,256]{1,0:T(8,128)(2,1)S(1)}, u32[]{:S(2)}, u32[]{:S(2)}) %collective-permute-start) | collective-permute-done | bytes 65568 | tf_op jit(solution)/shard_map/ppermute | solution.py:401
  8.1 1.0 %shard_map.119 = (bf16[512,256]{1,0:T(8,128)(2,1)S(1)}, bf16[64,512]{1,0:T(8,128)(2,1)S(1)}) custom-call(bf16[256,512]{1,0:T(8,128)(2,1)S(1)} %get-tuple-element.51.q_ref, bf16[256,256]{1,0:T(8,128)(2,1)S(1)} %get-tuple-element.52.kv_ref, bf16[128,256]{1,0:T(8,128)(2,1)S(1)} %get-tuple-element.53.before_ref, ...), custom_call_target="tpu_custom_call" | custom-call | flops 67108864 | bytes 262144 | tf_op jit(solution)/shard_map/pallas_call | solution.py:430
  9.1 0.1 collective-permute-start.1
  9.2 0.6 %shard_map.121.gates_ref.refs_6_.refs_5_ = bf16[4,360,720]{2,1,0:T(8,128)(2,1)S(1)} custom-call(bf16[360,2880]{1,0:T(8,128)(2,1)S(1)} %bitcast.12), custom_call_target="tpu_custom_call" | custom-call | bytes 4147200 | tf_op jit(solution)/shard_map/pallas_call | solution.py:449
  9.8 1.8 %collective-permute-start.18 = (bf16[512,256]{1,0:T(8,128)(2,1)S(1)}, bf16[512,256]{1,0:T(8,128)(2,1)S(1)}, u32[]{:S(2)}, u32[]{:S(2)}) collective-permute-start(bf16[512,256]{1,0:T(8,128)(2,1)S(1)} %get-tuple-element.96.refs_0_), channel_id=1, source_target_pairs={{0,3},{1,2},{2,1},{3,0},{4,7},{5,6},{6,5},{7,4},{8,11},{9,10},{10,... | collective-permute-start | bytes 786440 | tf_op jit(solution)/shard_map/ppermute | solution.py:350
  11.6 0.1 collective-permute-start.3
  11.7 0.5 %shard_map.120.refs_2_ = f32[64,720]{1,0:T(8,128)S(1)} custom-call(bf16[64,512]{1,0:T(8,128)(2,1)S(1)} %get-tuple-element.61.rows_ref, bf16[720,2048]{1,0:T(8,128)(2,1)S(1)} %get-tuple-element.62.w_ref.refs_3_.refs_2_.refs_4_, bf16[720,256]{1,0:T(8,128)(2,1)S(1)} %get-tuple-element.63.residual_ref.refs_5_, bf16[64,256]{1,0:T(8,128)(2,1)S(1)} %get-tuple-element.56.placing_ref), custom_call_target="tpu_custom_call" | custom-call | flops 47185920 | bytes 737280 | tf_op jit(solution)/shard_map/pallas_call | solution.py:441
  12.2 1.1 %collective-permute-done.1.refs_1_ = bf16[64,512]{1,0:T(8,128)(2,1)S(1)} collective-permute-done((bf16[64,512]{1,0:T(8,128)(2,1)S(1)}, bf16[64,512]{1,0:T(8,128)(2,1)S(1)}, u32[]{:S(2)}, u32[]{:S(2)}) %collective-permute-start.1) | collective-permute-done | bytes 65568 | tf_op jit(solution)/shard_map/ppermute | solution.py:350
  13.3 0.6 %collective-permute-start.2 = (bf16[64,512]{1,0:T(8,128)(2,1)S(1)}, bf16[64,512]{1,0:T(8,128)(2,1)S(1)}, u32[]{:S(2)}, u32[]{:S(2)}) collective-permute-start(bf16[64,512]{1,0:T(8,128)(2,1)S(1)} %collective-permute-done.1.refs_1_), channel_id=1, source_target_pairs={{0,1},{1,0},{2,3},{3,2},{4,5},{5,4},{6,7},{7,6},{8,9},{9,8},{10,11... | collective-permute-start | bytes 196616 | tf_op jit(solution)/shard_map/ppermute | solution.py:350
  13.9 0.0 collective-permute-done.3.refs_0_
  13.9 0.6 %shard_map.122.refs_1_ = f32[64,720]{1,0:T(8,128)S(1)} custom-call(bf16[64,512]{1,0:T(8,128)(2,1)S(1)} %collective-permute-done.3.refs_0_, bf16[64,512]{1,0:T(8,128)(2,1)S(1)} %collective-permute-done.1.refs_1_, f32[64,720]{1,0:T(8,128)S(1)} %shard_map.120.refs_2_, bf16[720,2048]{1,0:T(8,128)(2,1)S(1)} %get-tuple-element.62.w_ref.refs_3_.refs_2_.refs_4_), custom_call_target="tpu_custom_call" | custom-call | flops 47185920 | bytes 737280 | tf_op jit(solution)/shard_map/pallas_call | solution.py:452
  14.5 0.0 copy-start.3
  14.5 0.0 copy-start.1
  14.5 0.3 collective-permute-done.2.refs_0_
  14.8 0.4 shard_map.123
  15.2 1.8 %collective-permute-start.4 = (bf16[16,720]{1,0:T(8,128)(2,1)S(1)}, bf16[16,720]{1,0:T(8,128)(2,1)S(1)}, u32[]{:S(2)}, u32[]{:S(2)}) collective-permute-start(bf16[16,720]{1,0:T(8,128)(2,1)S(1)} %get-tuple-element.66), channel_id=1, source_target_pairs={{0,13},{1,12},{2,15},{3,14},{4,9},{5,8},{6,11},{7,10},{8,5},{9,4},... | collective-permute-start | bytes 69128 | tf_op jit(solution)/shard_map/ppermute | solution.py:364
  17.0 2.3 %collective-permute-start.6 = (bf16[16,720]{1,0:T(8,128)(2,1)S(1)}, bf16[16,720]{1,0:T(8,128)(2,1)S(1)}, u32[]{:S(2)}, u32[]{:S(2)}) collective-permute-start(bf16[16,720]{1,0:T(8,128)(2,1)S(1)} %get-tuple-element.68), channel_id=1, source_target_pairs={{0,5},{1,4},{2,7},{3,6},{4,1},{5,0},{6,3},{7,2},{8,13},{9,12},{10,... | collective-permute-start | bytes 69128 | tf_op jit(solution)/shard_map/ppermute | solution.py:364
  19.3 0.2 collective-permute-start.7
  19.5 0.1 shard_map.125.gains_ref.refs_5_.refs_4_
  19.5 0.6 %shard_map.124.ups_ref.refs_7_.refs_6_ = bf16[4,360,720]{2,1,0:T(8,128)(2,1)S(1)} custom-call(bf16[360,2880]{1,0:T(8,128)(2,1)S(1)} %bitcast.13), custom_call_target="tpu_custom_call" | custom-call | bytes 4147200 | tf_op jit(solution)/shard_map/pallas_call | solution.py:465
  20.1 0.1 collective-permute-done.4.refs_0_
  20.3 1.1 %collective-permute-done.5.refs_1_ = bf16[16,720]{1,0:T(8,128)(2,1)S(1)} collective-permute-done((bf16[16,720]{1,0:T(8,128)(2,1)S(1)}, bf16[16,720]{1,0:T(8,128)(2,1)S(1)}, u32[]{:S(2)}, u32[]{:S(2)}) %collective-permute-start.5) | collective-permute-done | bytes 23072 | tf_op jit(solution)/shard_map/ppermute | solution.py:364
  21.4 0.4 collective-permute-done.6.refs_2_
  21.8 0.8 %collective-permute-start.8 = (bf16[64,720]{1,0:T(8,128)(2,1)S(1)}, bf16[64,720]{1,0:T(8,128)(2,1)S(1)}, u32[]{:S(2)}, u32[]{:S(2)}) collective-permute-start(bf16[64,720]{1,0:T(8,128)(2,1)S(1)} %shard_map.126.block_ref), channel_id=1, source_target_pairs={{0,2},{1,3},{2,0},{3,1},{4,6},{5,7},{6,4},{7,5},{8,10},{9,11},{10,... | collective-permute-start | bytes 276488 | tf_op jit(solution)/shard_map/ppermute | solution.py:350
  22.6 0.6 %shard_map.128.refs_7_.downs_ref = bf16[4,360,720]{2,1,0:T(8,128)(2,1)S(1)} custom-call(bf16[360,2880]{1,0:T(8,128)(2,1)S(1)} %bitcast.14), custom_call_target="tpu_custom_call" | custom-call | bytes 4147200 | tf_op jit(solution)/shard_map/pallas_call | solution.py:476
  23.2 0.4 %shard_map.127 = (f32[64,360]{1,0:T(8,128)S(1)}, f32[64,360]{1,0:T(8,128)S(1)}, f32[64,128]{1,0:T(8,128)S(1)}) custom-call(bf16[64,720]{1,0:T(8,128)(2,1)S(1)} %shard_map.126.block_ref, f32[4,1,720]{2,1,0:T(1,128)S(1)} %shard_map.125.gains_ref.refs_5_.refs_4_, bf16[4,360,720]{2,1,0:T(8,128)(2,1)S(1)} %shard_map.121.gates_ref.refs_6_.refs_5_, ...), custom_call_target="tpu_custom_call" | custom-call | flops 66355200 | bytes 1036800 | tf_op jit(solution)/shard_map/pallas_call | solution.py:474
  23.6 3.0 %collective-permute-done.8.refs_1_ = bf16[64,720]{1,0:T(8,128)(2,1)S(1)} collective-permute-done((bf16[64,720]{1,0:T(8,128)(2,1)S(1)}, bf16[64,720]{1,0:T(8,128)(2,1)S(1)}, u32[]{:S(2)}, u32[]{:S(2)}) %collective-permute-start.8) | collective-permute-done | bytes 92192 | tf_op jit(solution)/shard_map/ppermute | solution.py:350
  26.6 0.0 collective-permute-start.9
  26.6 0.5 %collective-permute-start.20 = (bf16[512,256]{1,0:T(8,128)(2,1)S(1)}, bf16[512,256]{1,0:T(8,128)(2,1)S(1)}, u32[]{:S(2)}, u32[]{:S(2)}) collective-permute-start(bf16[512,256]{1,0:T(8,128)(2,1)S(1)} %get-tuple-element.96.refs_0_), channel_id=1, source_target_pairs={{0,1},{1,0},{2,3},{3,2},{4,5},{5,4},{6,7},{7,6},{8,9},{9,8},{10,11... | collective-permute-start | bytes 786440 | tf_op jit(solution)/shard_map/ppermute | solution.py:350
  27.2 0.0 collective-permute-start.19
  27.2 0.8 %shard_map.129 = (f32[64,360]{1,0:T(8,128)S(1)}, f32[64,360]{1,0:T(8,128)S(1)}, f32[64,128]{1,0:T(8,128)S(1)}) custom-call(bf16[64,720]{1,0:T(8,128)(2,1)S(1)} %collective-permute-done.10.refs_0_, bf16[64,720]{1,0:T(8,128)(2,1)S(1)} %collective-permute-done.8.refs_1_, f32[64,360]{1,0:T(8,128)S(1)} %get-tuple-element.75.refs_2_, ...), custom_call_target="tpu_custom_call" | custom-call | flops 66355200 | bytes 1036800 | tf_op jit(solution)/shard_map/pallas_call | solution.py:482
  28.0 0.7 %shard_map.130 = (bf16[2,64,720]{2,1,0:T(8,128)(2,1)S(1)}, bf16[64,360]{1,0:T(8,128)(2,1)S(1)}) custom-call(bf16[64,720]{1,0:T(8,128)(2,1)S(1)} %collective-permute-done.9.refs_0_, f32[64,360]{1,0:T(8,128)S(1)} %get-tuple-element.80.refs_1_, f32[64,360]{1,0:T(8,128)S(1)} %get-tuple-element.81.refs_2_, f32[64,128]{1,0:T(8,128)S(1)} %get-tuple-element.82.refs_3_, ...), custom_call_target="tpu_custom_call" | custom-call | flops 66355200 | bytes 1036800 | tf_op jit(solution)/shard_map/pallas_call | solution.py:485
  28.7 0.6 %collective-permute-start.11 = (bf16[2,64,720]{2,1,0:T(8,128)(2,1)S(1)}, bf16[2,64,720]{2,1,0:T(8,128)(2,1)S(1)}, u32[]{:S(2)}, u32[]{:S(2)}) collective-permute-start(bf16[2,64,720]{2,1,0:T(8,128)(2,1)S(1)} %get-tuple-element.84), channel_id=1, source_target_pairs={{0,1},{1,0},{2,3},{3,2},{4,5},{5,4},{6,7},{7,6},{8,9},{9,8},{10,11... | collective-permute-start | bytes 552968 | tf_op jit(solution)/shard_map/ppermute | solution.py:350
  29.3 0.3 shard_map.131.kept_ref
  29.6 0.7 %collective-permute-done.11.given_ref = bf16[2,64,720]{2,1,0:T(8,128)(2,1)S(1)} collective-permute-done((bf16[2,64,720]{2,1,0:T(8,128)(2,1)S(1)}, bf16[2,64,720]{2,1,0:T(8,128)(2,1)S(1)}, u32[]{:S(2)}, u32[]{:S(2)}) %collective-permute-start.11) | collective-permute-done | bytes 184352 | tf_op jit(solution)/shard_map/ppermute | solution.py:350
  30.3 0.1 shard_map.132
  30.4 0.8 %collective-permute-start.12 = (bf16[32,720]{1,0:T(8,128)(2,1)S(1)}, bf16[32,720]{1,0:T(8,128)(2,1)S(1)}, u32[]{:S(2)}, u32[]{:S(2)}) collective-permute-start(bf16[32,720]{1,0:T(8,128)(2,1)S(1)} %get-tuple-element.86), channel_id=1, source_target_pairs={{0,3},{1,2},{2,1},{3,0},{4,7},{5,6},{6,5},{7,4},{8,11},{9,10},{10,... | collective-permute-start | bytes 138248 | tf_op jit(solution)/shard_map/ppermute | solution.py:350
  31.2 1.0 %collective-permute-start.15 = (bf16[32,720]{1,0:T(8,128)(2,1)S(1)}, bf16[32,720]{1,0:T(8,128)(2,1)S(1)}, u32[]{:S(2)}, u32[]{:S(2)}) collective-permute-start(bf16[32,720]{1,0:T(8,128)(2,1)S(1)} %get-tuple-element.90), channel_id=1, source_target_pairs={{0,3},{1,2},{2,1},{3,0},{4,7},{5,6},{6,5},{7,4},{8,11},{9,10},{10,... | collective-permute-start | bytes 138248 | tf_op jit(solution)/shard_map/ppermute | solution.py:350
  32.2 1.8 %collective-permute-done.12.refs_1_ = bf16[32,720]{1,0:T(8,128)(2,1)S(1)} collective-permute-done((bf16[32,720]{1,0:T(8,128)(2,1)S(1)}, bf16[32,720]{1,0:T(8,128)(2,1)S(1)}, u32[]{:S(2)}, u32[]{:S(2)}) %collective-permute-start.12) | collective-permute-done | bytes 46112 | tf_op jit(solution)/shard_map/ppermute | solution.py:350
  34.0 2.2 %collective-permute-start.13 = (bf16[16,720]{1,0:T(8,128)(2,1)S(1)}, bf16[16,720]{1,0:T(8,128)(2,1)S(1)}, u32[]{:S(2)}, u32[]{:S(2)}) collective-permute-start(bf16[16,720]{1,0:T(8,128)(2,1)S(1)} %get-tuple-element.87), channel_id=1, source_target_pairs={{0,13},{1,12},{2,15},{3,14},{4,9},{5,8},{6,11},{7,10},{8,5},{9,4},... | collective-permute-start | bytes 69128 | tf_op jit(solution)/shard_map/ppermute | solution.py:364
  36.2 0.1 collective-permute-start.14
  36.4 2.5 %collective-permute-start.16 = (bf16[16,720]{1,0:T(8,128)(2,1)S(1)}, bf16[16,720]{1,0:T(8,128)(2,1)S(1)}, u32[]{:S(2)}, u32[]{:S(2)}) collective-permute-start(bf16[16,720]{1,0:T(8,128)(2,1)S(1)} %get-tuple-element.91), channel_id=1, source_target_pairs={{0,5},{1,4},{2,7},{3,6},{4,1},{5,0},{6,3},{7,2},{8,13},{9,12},{10,... | collective-permute-start | bytes 69128 | tf_op jit(solution)/shard_map/ppermute | solution.py:364
  38.9 0.9 %shard_map.135.refs_6_ = bf16[720,256]{1,0:T(8,128)(2,1)S(1)} custom-call(bf16[512,256]{1,0:T(8,128)(2,1)S(1)} %get-tuple-element.96.refs_0_, bf16[512,256]{1,0:T(8,128)(2,1)S(1)} %collective-permute-done.19.refs_1_, bf16[512,256]{1,0:T(8,128)(2,1)S(1)} %collective-permute-done.20.refs_2_, bf16[512,256]{1,0:T(8,128)(2,1)S(1)} %collective-permute-done.18.refs_3_, ...), custom_call_target="tpu_custom_call" | custom-call | flops 754974720 | bytes 2949120 | tf_op jit(solution)/shard_map/pallas_call | solution.py:492
  39.8 1.4 %collective-permute-done.14.refs_1_ = bf16[16,720]{1,0:T(8,128)(2,1)S(1)} collective-permute-done((bf16[16,720]{1,0:T(8,128)(2,1)S(1)}, bf16[16,720]{1,0:T(8,128)(2,1)S(1)}, u32[]{:S(2)}, u32[]{:S(2)}) %collective-permute-start.14) | collective-permute-done | bytes 23072 | tf_op jit(solution)/shard_map/ppermute | solution.py:364
  41.2 1.0 %shard_map.136 = bf16[720,256]{1,0:T(8,128)(2,1)} custom-call(bf16[16,720]{1,0:T(8,128)(2,1)S(1)} %collective-permute-done.13.refs_0_, bf16[16,720]{1,0:T(8,128)(2,1)S(1)} %collective-permute-done.14.refs_1_, bf16[16,720]{1,0:T(8,128)(2,1)S(1)} %collective-permute-done.16.refs_2_, bf16[16,720]{1,0:T(8,128)(2,1)S(1)} %collective-permute-done.17.refs_3_, ...), custom_call_target="tpu_custom_call" | custom-call | tf_op jit(solution)/shard_map/pallas_call | solution.py:513
  (22 shorter events, 0.1 us)
Async XLA Ops:
  0.8 7.3 %collective-permute-start = (bf16[128,256]{1,0:T(8,128)(2,1)S(1)}, bf16[128,256]{1,0:T(8,128)(2,1)S(1)}, u32[]{:S(2)}, u32[]{:S(2)}) collective-permute-start(bf16[128,256]{1,0:T(8,128)(2,1)S(1)} %slice.3), channel_id=1, source_target_pairs={{0,4},{4,8},{8,12},{12,0},{1,5},{5,9},{9,13},{13,1},{2,6},{6,10},{... | collective-permute-start | bytes 196616 | tf_op jit(solution)/shard_map/ppermute | solution.py:401
  3.9 5.3 %copy-start = (bf16[1,2880,360]{1,2,0:T(8,128)(2,1)S(1)}, bf16[1,2880,360]{1,2,0:T(8,128)(2,1)}, u32[]{:S(2)}) copy-start(bf16[1,2880,360]{1,2,0:T(8,128)(2,1)} %param.21) | copy-start | bytes 6220804
  9.1 4.1 %collective-permute-start.1 = (bf16[64,512]{1,0:T(8,128)(2,1)S(1)}, bf16[64,512]{1,0:T(8,128)(2,1)S(1)}, u32[]{:S(2)}, u32[]{:S(2)}) collective-permute-start(bf16[64,512]{1,0:T(8,128)(2,1)S(1)} %get-tuple-element.61.rows_ref), channel_id=1, source_target_pairs={{0,3},{1,2},{2,1},{3,0},{4,7},{5,6},{6,5},{7,4},{8,11},{9,10},{10,... | collective-permute-start | bytes 196616 | tf_op jit(solution)/shard_map/ppermute | solution.py:350
  9.8 17.4 %collective-permute-start.18 = (bf16[512,256]{1,0:T(8,128)(2,1)S(1)}, bf16[512,256]{1,0:T(8,128)(2,1)S(1)}, u32[]{:S(2)}, u32[]{:S(2)}) collective-permute-start(bf16[512,256]{1,0:T(8,128)(2,1)S(1)} %get-tuple-element.96.refs_0_), channel_id=1, source_target_pairs={{0,3},{1,2},{2,1},{3,0},{4,7},{5,6},{6,5},{7,4},{8,11},{9,10},{10,... | collective-permute-start | bytes 786440 | tf_op jit(solution)/shard_map/ppermute | solution.py:350
  11.6 2.4 %collective-permute-start.3 = (bf16[64,512]{1,0:T(8,128)(2,1)S(1)}, bf16[64,512]{1,0:T(8,128)(2,1)S(1)}, u32[]{:S(2)}, u32[]{:S(2)}) collective-permute-start(bf16[64,512]{1,0:T(8,128)(2,1)S(1)} %get-tuple-element.61.rows_ref), channel_id=1, source_target_pairs={{0,1},{1,0},{2,3},{3,2},{4,5},{5,4},{6,7},{7,6},{8,9},{9,8},{10,11... | collective-permute-start | bytes 196616 | tf_op jit(solution)/shard_map/ppermute | solution.py:350
  13.3 1.6 %collective-permute-start.2 = (bf16[64,512]{1,0:T(8,128)(2,1)S(1)}, bf16[64,512]{1,0:T(8,128)(2,1)S(1)}, u32[]{:S(2)}, u32[]{:S(2)}) collective-permute-start(bf16[64,512]{1,0:T(8,128)(2,1)S(1)} %collective-permute-done.1.refs_1_), channel_id=1, source_target_pairs={{0,1},{1,0},{2,3},{3,2},{4,5},{5,4},{6,7},{7,6},{8,9},{9,8},{10,11... | collective-permute-start | bytes 196616 | tf_op jit(solution)/shard_map/ppermute | solution.py:350
  14.5 5.0 %copy-start.3 = (f32[2880]{0:T(1024)S(1)}, f32[2880]{0:T(1024)}, u32[]{:S(2)}) copy-start(f32[2880]{0:T(1024)} %gain_ref.1) | copy-start | bytes 34564
  14.5 5.0 %copy-start.1 = (bf16[1,2880,360]{1,2,0:T(8,128)(2,1)S(1)}, bf16[1,2880,360]{1,2,0:T(8,128)(2,1)}, u32[]{:S(2)}) copy-start(bf16[1,2880,360]{1,2,0:T(8,128)(2,1)} %param.22) | copy-start | bytes 6220804
  15.2 5.1 %collective-permute-start.4 = (bf16[16,720]{1,0:T(8,128)(2,1)S(1)}, bf16[16,720]{1,0:T(8,128)(2,1)S(1)}, u32[]{:S(2)}, u32[]{:S(2)}) collective-permute-start(bf16[16,720]{1,0:T(8,128)(2,1)S(1)} %get-tuple-element.66), channel_id=1, source_target_pairs={{0,13},{1,12},{2,15},{3,14},{4,9},{5,8},{6,11},{7,10},{8,5},{9,4},... | collective-permute-start | bytes 69128 | tf_op jit(solution)/shard_map/ppermute | solution.py:364
  17.0 4.4 %collective-permute-start.5 = (bf16[16,720]{1,0:T(8,128)(2,1)S(1)}, bf16[16,720]{1,0:T(8,128)(2,1)S(1)}, u32[]{:S(2)}, u32[]{:S(2)}) collective-permute-start(bf16[16,720]{1,0:T(8,128)(2,1)S(1)} %get-tuple-element.67), channel_id=1, source_target_pairs={{0,9},{1,8},{2,11},{3,10},{4,13},{5,12},{6,15},{7,14},{8,1},{9,0},... | collective-permute-start | bytes 69128 | tf_op jit(solution)/shard_map/ppermute | solution.py:364
  17.0 4.7 %collective-permute-start.6 = (bf16[16,720]{1,0:T(8,128)(2,1)S(1)}, bf16[16,720]{1,0:T(8,128)(2,1)S(1)}, u32[]{:S(2)}, u32[]{:S(2)}) collective-permute-start(bf16[16,720]{1,0:T(8,128)(2,1)S(1)} %get-tuple-element.68), channel_id=1, source_target_pairs={{0,5},{1,4},{2,7},{3,6},{4,1},{5,0},{6,3},{7,2},{8,13},{9,12},{10,... | collective-permute-start | bytes 69128 | tf_op jit(solution)/shard_map/ppermute | solution.py:364
  19.3 2.4 %collective-permute-start.7 = (bf16[16,720]{1,0:T(8,128)(2,1)S(1)}, bf16[16,720]{1,0:T(8,128)(2,1)S(1)}, u32[]{:S(2)}, u32[]{:S(2)}) collective-permute-start(bf16[16,720]{1,0:T(8,128)(2,1)S(1)} %get-tuple-element.69), channel_id=1, source_target_pairs={{0,1},{1,0},{2,3},{3,2},{4,5},{5,4},{6,7},{7,6},{8,9},{9,8},{10,11... | collective-permute-start | bytes 69128 | tf_op jit(solution)/shard_map/ppermute | solution.py:364
  19.5 3.0 %copy-start.2 = (bf16[1,360,2880]{2,1,0:T(8,128)(2,1)S(1)}, bf16[1,360,2880]{2,1,0:T(8,128)(2,1)}, u32[]{:S(2)}) copy-start(bf16[1,360,2880]{2,1,0:T(8,128)(2,1)} %param.23) | copy-start | bytes 6220804
  21.8 4.9 %collective-permute-start.8 = (bf16[64,720]{1,0:T(8,128)(2,1)S(1)}, bf16[64,720]{1,0:T(8,128)(2,1)S(1)}, u32[]{:S(2)}, u32[]{:S(2)}) collective-permute-start(bf16[64,720]{1,0:T(8,128)(2,1)S(1)} %shard_map.126.block_ref), channel_id=1, source_target_pairs={{0,2},{1,3},{2,0},{3,1},{4,6},{5,7},{6,4},{7,5},{8,10},{9,11},{10,... | collective-permute-start | bytes 276488 | tf_op jit(solution)/shard_map/ppermute | solution.py:350
  22.6 4.6 %collective-permute-start.10 = (bf16[64,720]{1,0:T(8,128)(2,1)S(1)}, bf16[64,720]{1,0:T(8,128)(2,1)S(1)}, u32[]{:S(2)}, u32[]{:S(2)}) collective-permute-start(bf16[64,720]{1,0:T(8,128)(2,1)S(1)} %shard_map.126.block_ref), channel_id=1, source_target_pairs={{0,1},{1,0},{2,3},{3,2},{4,5},{5,4},{6,7},{7,6},{8,9},{9,8},{10,11... | collective-permute-start | bytes 276488 | tf_op jit(solution)/shard_map/ppermute | solution.py:350
  26.6 1.3 %collective-permute-start.9 = (bf16[64,720]{1,0:T(8,128)(2,1)S(1)}, bf16[64,720]{1,0:T(8,128)(2,1)S(1)}, u32[]{:S(2)}, u32[]{:S(2)}) collective-permute-start(bf16[64,720]{1,0:T(8,128)(2,1)S(1)} %collective-permute-done.8.refs_1_), channel_id=1, source_target_pairs={{0,1},{1,0},{2,3},{3,2},{4,5},{5,4},{6,7},{7,6},{8,9},{9,8},{10,11... | collective-permute-start | bytes 276488 | tf_op jit(solution)/shard_map/ppermute | solution.py:350
  26.6 12.2 %collective-permute-start.20 = (bf16[512,256]{1,0:T(8,128)(2,1)S(1)}, bf16[512,256]{1,0:T(8,128)(2,1)S(1)}, u32[]{:S(2)}, u32[]{:S(2)}) collective-permute-start(bf16[512,256]{1,0:T(8,128)(2,1)S(1)} %get-tuple-element.96.refs_0_), channel_id=1, source_target_pairs={{0,1},{1,0},{2,3},{3,2},{4,5},{5,4},{6,7},{7,6},{8,9},{9,8},{10,11... | collective-permute-start | bytes 786440 | tf_op jit(solution)/shard_map/ppermute | solution.py:350
  27.2 11.7 %collective-permute-start.19 = (bf16[512,256]{1,0:T(8,128)(2,1)S(1)}, bf16[512,256]{1,0:T(8,128)(2,1)S(1)}, u32[]{:S(2)}, u32[]{:S(2)}) collective-permute-start(bf16[512,256]{1,0:T(8,128)(2,1)S(1)} %collective-permute-done.18.refs_3_), channel_id=1, source_target_pairs={{0,1},{1,0},{2,3},{3,2},{4,5},{5,4},{6,7},{7,6},{8,9},{9,8},{10,11... | collective-permute-start | bytes 786440 | tf_op jit(solution)/shard_map/ppermute | solution.py:350
  28.7 1.6 %collective-permute-start.11 = (bf16[2,64,720]{2,1,0:T(8,128)(2,1)S(1)}, bf16[2,64,720]{2,1,0:T(8,128)(2,1)S(1)}, u32[]{:S(2)}, u32[]{:S(2)}) collective-permute-start(bf16[2,64,720]{2,1,0:T(8,128)(2,1)S(1)} %get-tuple-element.84), channel_id=1, source_target_pairs={{0,1},{1,0},{2,3},{3,2},{4,5},{5,4},{6,7},{7,6},{8,9},{9,8},{10,11... | collective-permute-start | bytes 552968 | tf_op jit(solution)/shard_map/ppermute | solution.py:350
  30.4 3.6 %collective-permute-start.12 = (bf16[32,720]{1,0:T(8,128)(2,1)S(1)}, bf16[32,720]{1,0:T(8,128)(2,1)S(1)}, u32[]{:S(2)}, u32[]{:S(2)}) collective-permute-start(bf16[32,720]{1,0:T(8,128)(2,1)S(1)} %get-tuple-element.86), channel_id=1, source_target_pairs={{0,3},{1,2},{2,1},{3,0},{4,7},{5,6},{6,5},{7,4},{8,11},{9,10},{10,... | collective-permute-start | bytes 138248 | tf_op jit(solution)/shard_map/ppermute | solution.py:350
  31.2 5.2 %collective-permute-start.15 = (bf16[32,720]{1,0:T(8,128)(2,1)S(1)}, bf16[32,720]{1,0:T(8,128)(2,1)S(1)}, u32[]{:S(2)}, u32[]{:S(2)}) collective-permute-start(bf16[32,720]{1,0:T(8,128)(2,1)S(1)} %get-tuple-element.90), channel_id=1, source_target_pairs={{0,3},{1,2},{2,1},{3,0},{4,7},{5,6},{6,5},{7,4},{8,11},{9,10},{10,... | collective-permute-start | bytes 138248 | tf_op jit(solution)/shard_map/ppermute | solution.py:350
  34.0 5.8 %collective-permute-start.13 = (bf16[16,720]{1,0:T(8,128)(2,1)S(1)}, bf16[16,720]{1,0:T(8,128)(2,1)S(1)}, u32[]{:S(2)}, u32[]{:S(2)}) collective-permute-start(bf16[16,720]{1,0:T(8,128)(2,1)S(1)} %get-tuple-element.87), channel_id=1, source_target_pairs={{0,13},{1,12},{2,15},{3,14},{4,9},{5,8},{6,11},{7,10},{8,5},{9,4},... | collective-permute-start | bytes 69128 | tf_op jit(solution)/shard_map/ppermute | solution.py:364
  36.2 5.0 %collective-permute-start.14 = (bf16[16,720]{1,0:T(8,128)(2,1)S(1)}, bf16[16,720]{1,0:T(8,128)(2,1)S(1)}, u32[]{:S(2)}, u32[]{:S(2)}) collective-permute-start(bf16[16,720]{1,0:T(8,128)(2,1)S(1)} %get-tuple-element.88), channel_id=1, source_target_pairs={{0,9},{1,8},{2,11},{3,10},{4,13},{5,12},{6,15},{7,14},{8,1},{9,0},... | collective-permute-start | bytes 69128 | tf_op jit(solution)/shard_map/ppermute | solution.py:364
  36.4 4.9 %collective-permute-start.16 = (bf16[16,720]{1,0:T(8,128)(2,1)S(1)}, bf16[16,720]{1,0:T(8,128)(2,1)S(1)}, u32[]{:S(2)}, u32[]{:S(2)}) collective-permute-start(bf16[16,720]{1,0:T(8,128)(2,1)S(1)} %get-tuple-element.91), channel_id=1, source_target_pairs={{0,5},{1,4},{2,7},{3,6},{4,1},{5,0},{6,3},{7,2},{8,13},{9,12},{10,... | collective-permute-start | bytes 69128 | tf_op jit(solution)/shard_map/ppermute | solution.py:364
  38.9 2.4 %collective-permute-start.17 = (bf16[16,720]{1,0:T(8,128)(2,1)S(1)}, bf16[16,720]{1,0:T(8,128)(2,1)S(1)}, u32[]{:S(2)}, u32[]{:S(2)}) collective-permute-start(bf16[16,720]{1,0:T(8,128)(2,1)S(1)} %get-tuple-element.92), channel_id=1, source_target_pairs={{0,1},{1,0},{2,3},{3,2},{4,5},{5,4},{6,7},{7,6},{8,9},{9,8},{10,11... | collective-permute-start | bytes 69128 | tf_op jit(solution)/shard_map/ppermute | solution.py:364

commit v14 on v13

--- a/solution.py
+++ b/solution.py
@@ -102,6 +102,12 @@
 
 def per_head(pair):
     return jnp.concatenate([jnp.broadcast_to(row, (HEAD_SIZE, row.shape[1])) for row in pair], axis=0)
+
+
+def tail_kernel(rows_ref, tail_ref, sem):
+    copy = pltpu.make_async_copy(rows_ref.at[rows_ref.shape[0] - KEYS_SEEN :], tail_ref, sem)
+    copy.start()
+    copy.wait()
 
 
 def fill_tables(live, ids, weights, placing_ref, mix_hi_ref, mix_lo_ref):
@@ -303,13 +309,15 @@
     gate, up = gate * scale, up * scale
     activated = ((up + 1.0) * gate * jax.nn.sigmoid(glu_alpha * gate)).astype(jnp.bfloat16)
     activated_ref[...] = activated
-    for k in range(steps):
-        given_ref[k] = dot(activated, downs_ref[origin(k, k > 0)], NN).astype(jnp.bfloat16)
-
-
-def expert_kept_kernel(activated_ref, downs_ref, kept_ref):
-    for k in range(kept_ref.shape[0]):
-        kept_ref[k] = dot(activated_ref[...], downs_ref[origin(k, k == 0)], NN).astype(jnp.bfloat16)
+    for k in range(1, steps):
+        given_ref[k - 1] = dot(activated, downs_ref[origin(k, True)], NN).astype(jnp.bfloat16)
+
+
+def expert_rest_kernel(activated_ref, downs_ref, far_ref, near_ref, given_ref):
+    for k in range(1, far_ref.shape[0] + 1):
+        far_ref[k - 1] = dot(activated_ref[...], downs_ref[origin(k, False)], NN).astype(jnp.bfloat16)
+    near_ref[0] = dot(activated_ref[...], downs_ref[origin(0, True)], NN).astype(jnp.bfloat16)
+    given_ref[0] = dot(activated_ref[...], downs_ref[origin(0, False)], NN).astype(jnp.bfloat16)
 
 
 def add_cores_kernel(kept_ref, given_ref, *out_refs):
@@ -397,7 +405,9 @@
     width = norm_gain.shape[0]
     hidden = w_gate.shape[2]
 
-    tail = keyvals[toks - KEYS_SEEN :]
+    tail = call(
+        tail_kernel, bf16(KEYS_SEEN, keyvals.shape[1]), n_in=1, hbm=(0,), scratch=[pltpu.SemaphoreType.DMA]
+    )(in_hbm(keyvals))
     rim = lax.ppermute(tail, "seq", [(i, (i + 1) % size) for i in range(size)])
     loads = (queries, keyvals, preceding_keyvalues, w_out.T, residual.T)
     groups = keyvals.shape[1] // PAIR
@@ -484,11 +494,13 @@
     )
     given, activated = call(
         functools.partial(expert_last_kernel, steps),
-        (bf16(steps, slots, feats), bf16(slots, hidden)),
+        (bf16(steps - 1, slots, feats), bf16(slots, hidden)),
         n_in=steps + 6,
         **part,
     )(*relayed_rows, *chips, gains, gates, ups, downs)
-    kept = call(expert_kept_kernel, bf16(steps, slots, feats), n_in=2, **part)(activated, downs)
+    far, near, near_given = call(
+        expert_rest_kernel, (bf16(steps - 1, slots, feats), *(bf16(1, slots, feats),) * 2), n_in=2, **part
+    )(activated, downs)
     resid = call(
         functools.partial(project_kernel, steps),
         bf16(feats, toks),
@@ -497,15 +509,17 @@
         moved=2 * w_out.size,
     )(*blocks, w_t, residual_t)
 
-    sums = call(add_cores_kernel, (bf16(slots // 2, feats),) * (2 * steps), n_in=2)(
-        kept, swap(given, "cuts", 1)
-    )
-    returned = []
+    half = bf16(slots // 2, feats)
+    far_sums = call(add_cores_kernel, (half,) * (2 * steps - 2), n_in=2)(far, from_sibling(given))
+    near_sums = call(add_cores_kernel, (half,) * 2, n_in=2)(near, from_sibling(after(near_given, far_sums)))
+    sums = [*near_sums, *far_sums]
+    returned, blocks_before = [], []
     for half in range(2):
         parts = [sums[half]] + [to_chip(sums[2 * k + half], k) for k in range(1, steps)]
         blocks = call(functools.partial(add_chips_kernel, steps), (bf16(CAP, feats),) * (live // 2), n_in=steps)(
-            *parts
+            *after(parts, blocks_before)
         )
+        blocks_before = blocks
         for block in blocks:
             returned.append(to_seq(block, live - 1 - len(returned)))
     bounds = [*range(0, feats, SPAN), feats] if feats % 16 == 0 else [0, feats]

time: 42.4 us -> 42.7 us (level)
  local copies, waits for them, and re-layouts: 0.86 us -> 0.02 us
  Pallas kernels: 11.1 us -> 11.9 us
    slice x1 -> x0, local copies, waits for them, and re-layouts: 0.84 us -> none  [shards(): tail = keyvals[toks - KEYS_SEEN:]]
    pallas_call x3 -> x5, Pallas kernels: 1.12 us -> 1.96 us  [the longest x1 0.85 us: shards(): call(tail_kernel, bf16(KEYS_SEEN, keyvals.shape[1]), n_in=1, hbm=(0,), sc...]
    ppermute x12 -> x13, starting transfers between devices: 6.33 us -> 6.65 us  [swap(): lax.ppermute(block, axis, [(i, i ^ mask) for i in range(lax.axis_size(axi...]
    ppermute x12 -> x13, waiting for transfers between devices: 6.94 us -> 6.95 us  [swap(): lax.ppermute(block, axis, [(i, i ^ mask) for i in range(lax.axis_size(axi...]
  transfers between devices with their start and end apart: 21 -> 22, of which waited for: 10 -> 11; matrix products, arithmetic and copies ran while one was open for 0% -> 0% of each run, Pallas kernels for 21% -> 21%
where the time goes in v14:
time: 42.7 us; the launch traced here: 42.5 us
  starting transfers between devices  18.6 us (44%)
  Pallas kernels  11.9 us (28%)
  waiting for transfers between devices  11.8 us (28%)
    ppermute x8, starting transfers between devices, to_seq(): lax.ppermute(block, ('seq', 'cuts'), [(i, i ^ mask) for i in range(size)])  8.91 us
    ppermute x13, waiting for transfers between devices, swap(): lax.ppermute(block, axis, [(i, i ^ mask) for i in range(lax.axis_size(axi...  6.95 us
    ppermute x13, starting transfers between devices, swap(): lax.ppermute(block, axis, [(i, i ^ mask) for i in range(lax.axis_size(axi...  6.65 us
    ppermute x8, waiting for transfers between devices, to_seq(): lax.ppermute(block, ('seq', 'cuts'), [(i, i ^ mask) for i in range(size)])  3.14 us
    ppermute x1, starting transfers between devices, shards(): rim = lax.ppermute(tail, 'seq', [(i, (i + 1) % size) for i in range(size)])  3.08 us
    pallas_call x1, Pallas kernels, shards(): call(functools.partial(first_kernel, live), (*(bf16(*a.shape) for a in lo...  2.53 us
    ppermute x1, waiting for transfers between devices, shards(): rim = lax.ppermute(tail, 'seq', [(i, (i + 1) % size) for i in range(size)])  1.73 us
    pallas_call x1, Pallas kernels, shards(): call(functools.partial(combine_kernel, live, parts), bf16(feats, toks), n...  1.02 us
  transfers between devices with their start and end apart: 22, of which 11 were waited for; matrix products, arithmetic and copies ran while one was open for 0% of the time, Pallas kernels for 21%

profile of v14, /device:TPU:0, one launch (start us, length us, event | category | flops | bytes accessed | tf_op | source)
XLA Modules:
  0.0 42.5 jit_solution(12168229482856119770)
XLA Ops:
  0.0 0.8 %shard_map.119 = bf16[128,256]{1,0:T(8,128)(2,1)S(1)} custom-call(bf16[256,256]{1,0:T(8,128)(2,1)} %rows_ref.1), custom_call_target="tpu_custom_call" | custom-call | tf_op jit(solution)/shard_map/pallas_call | solution.py:408
  0.9 3.1 %collective-permute-start = (bf16[128,256]{1,0:T(8,128)(2,1)S(1)}, bf16[128,256]{1,0:T(8,128)(2,1)S(1)}, u32[]{:S(2)}, u32[]{:S(2)}) collective-permute-start(bf16[128,256]{1,0:T(8,128)(2,1)S(1)} %shard_map.119), channel_id=1, source_target_pairs={{0,4},{4,8},{8,12},{12,0},{1,5},{5,9},{9,13},{13,1},{2,6},{6,10},{... | collective-permute-start | bytes 196616 | tf_op jit(solution)/shard_map/ppermute | solution.py:411
  3.9 2.5 %shard_map.118 = (bf16[256,512]{1,0:T(8,128)(2,1)S(1)}, bf16[256,256]{1,0:T(8,128)(2,1)S(1)}, bf16[128,256]{1,0:T(8,128)(2,1)S(1)}, bf16[720,2048]{1,0:T(8,128)(...) custom-call(s32[4,256]{1,0:T(4,128)} %bitcast.17, ...), custom_call_target="tpu_custom_call" | custom-call | flops 134217728 | bytes 3579904 | tf_op jit(solution)/shard_map/pallas_call | solution.py:417
  6.5 1.7 %collective-permute-done.rim_ref = bf16[128,256]{1,0:T(8,128)(2,1)S(1)} collective-permute-done((bf16[128,256]{1,0:T(8,128)(2,1)S(1)}, bf16[128,256]{1,0:T(8,128)(2,1)S(1)}, u32[]{:S(2)}, u32[]{:S(2)}) %collective-permute-start) | collective-permute-done | bytes 65568 | tf_op jit(solution)/shard_map/ppermute | solution.py:411
  8.2 1.0 %shard_map.120 = (bf16[512,256]{1,0:T(8,128)(2,1)S(1)}, bf16[64,512]{1,0:T(8,128)(2,1)S(1)}) custom-call(bf16[256,512]{1,0:T(8,128)(2,1)S(1)} %get-tuple-element.59.q_ref, bf16[256,256]{1,0:T(8,128)(2,1)S(1)} %get-tuple-element.60.kv_ref, bf16[128,256]{1,0:T(8,128)(2,1)S(1)} %get-tuple-element.61.before_ref, ...), custom_call_target="tpu_custom_call" | custom-call | flops 67108864 | bytes 262144 | tf_op jit(solution)/shard_map/pallas_call | solution.py:440
  9.2 0.1 collective-permute-start.1
  9.3 0.6 %shard_map.122.gates_ref.refs_6_.refs_5_ = bf16[4,360,720]{2,1,0:T(8,128)(2,1)S(1)} custom-call(bf16[360,2880]{1,0:T(8,128)(2,1)S(1)} %bitcast.12), custom_call_target="tpu_custom_call" | custom-call | bytes 4147200 | tf_op jit(solution)/shard_map/pallas_call | solution.py:459
  9.9 1.8 %collective-permute-start.19 = (bf16[512,256]{1,0:T(8,128)(2,1)S(1)}, bf16[512,256]{1,0:T(8,128)(2,1)S(1)}, u32[]{:S(2)}, u32[]{:S(2)}) collective-permute-start(bf16[512,256]{1,0:T(8,128)(2,1)S(1)} %get-tuple-element.112.refs_0_), channel_id=1, source_target_pairs={{0,3},{1,2},{2,1},{3,0},{4,7},{5,6},{6,5},{7,4},{8,11},{9,10},{10,... | collective-permute-start | bytes 786440 | tf_op jit(solution)/shard_map/ppermute | solution.py:358
  11.6 0.1 collective-permute-start.3
  11.8 0.4 %shard_map.121.refs_2_ = f32[64,720]{1,0:T(8,128)S(1)} custom-call(bf16[64,512]{1,0:T(8,128)(2,1)S(1)} %get-tuple-element.69.rows_ref, bf16[720,2048]{1,0:T(8,128)(2,1)S(1)} %get-tuple-element.70.w_ref.refs_3_.refs_2_.refs_4_, bf16[720,256]{1,0:T(8,128)(2,1)S(1)} %get-tuple-element.71.residual_ref.refs_5_, bf16[64,256]{1,0:T(8,128)(2,1)S(1)} %get-tuple-element.64.placing_ref), custom_call_target="tpu_custom_call" | custom-call | flops 47185920 | bytes 737280 | tf_op jit(solution)/shard_map/pallas_call | solution.py:451
  12.2 1.1 %collective-permute-done.1.refs_1_ = bf16[64,512]{1,0:T(8,128)(2,1)S(1)} collective-permute-done((bf16[64,512]{1,0:T(8,128)(2,1)S(1)}, bf16[64,512]{1,0:T(8,128)(2,1)S(1)}, u32[]{:S(2)}, u32[]{:S(2)}) %collective-permute-start.1) | collective-permute-done | bytes 65568 | tf_op jit(solution)/shard_map/ppermute | solution.py:358
  13.3 0.6 %collective-permute-start.2 = (bf16[64,512]{1,0:T(8,128)(2,1)S(1)}, bf16[64,512]{1,0:T(8,128)(2,1)S(1)}, u32[]{:S(2)}, u32[]{:S(2)}) collective-permute-start(bf16[64,512]{1,0:T(8,128)(2,1)S(1)} %collective-permute-done.1.refs_1_), channel_id=1, source_target_pairs={{0,1},{1,0},{2,3},{3,2},{4,5},{5,4},{6,7},{7,6},{8,9},{9,8},{10,11... | collective-permute-start | bytes 196616 | tf_op jit(solution)/shard_map/ppermute | solution.py:358
  14.0 0.0 collective-permute-done.3.refs_0_
  14.0 0.6 %shard_map.123.refs_1_ = f32[64,720]{1,0:T(8,128)S(1)} custom-call(bf16[64,512]{1,0:T(8,128)(2,1)S(1)} %collective-permute-done.3.refs_0_, bf16[64,512]{1,0:T(8,128)(2,1)S(1)} %collective-permute-done.1.refs_1_, f32[64,720]{1,0:T(8,128)S(1)} %shard_map.121.refs_2_, bf16[720,2048]{1,0:T(8,128)(2,1)S(1)} %get-tuple-element.70.w_ref.refs_3_.refs_2_.refs_4_), custom_call_target="tpu_custom_call" | custom-call | flops 47185920 | bytes 737280 | tf_op jit(solution)/shard_map/pallas_call | solution.py:462
  14.5 0.0 copy-start.3
  14.6 0.0 copy-start.1
  14.6 0.3 collective-permute-done.2.refs_0_
  14.9 0.4 shard_map.124
  15.2 1.8 %collective-permute-start.4 = (bf16[16,720]{1,0:T(8,128)(2,1)S(1)}, bf16[16,720]{1,0:T(8,128)(2,1)S(1)}, u32[]{:S(2)}, u32[]{:S(2)}) collective-permute-start(bf16[16,720]{1,0:T(8,128)(2,1)S(1)} %get-tuple-element.74), channel_id=1, source_target_pairs={{0,13},{1,12},{2,15},{3,14},{4,9},{5,8},{6,11},{7,10},{8,5},{9,4},... | collective-permute-start | bytes 69128 | tf_op jit(solution)/shard_map/ppermute | solution.py:372
  17.1 2.3 %collective-permute-start.6 = (bf16[16,720]{1,0:T(8,128)(2,1)S(1)}, bf16[16,720]{1,0:T(8,128)(2,1)S(1)}, u32[]{:S(2)}, u32[]{:S(2)}) collective-permute-start(bf16[16,720]{1,0:T(8,128)(2,1)S(1)} %get-tuple-element.76), channel_id=1, source_target_pairs={{0,5},{1,4},{2,7},{3,6},{4,1},{5,0},{6,3},{7,2},{8,13},{9,12},{10,... | collective-permute-start | bytes 69128 | tf_op jit(solution)/shard_map/ppermute | solution.py:372
  19.4 0.2 collective-permute-start.7
  19.5 0.1 shard_map.126.gains_ref.refs_5_.refs_4_
  19.6 0.6 %shard_map.125.ups_ref.refs_7_.refs_6_ = bf16[4,360,720]{2,1,0:T(8,128)(2,1)S(1)} custom-call(bf16[360,2880]{1,0:T(8,128)(2,1)S(1)} %bitcast.13), custom_call_target="tpu_custom_call" | custom-call | bytes 4147200 | tf_op jit(solution)/shard_map/pallas_call | solution.py:475
  20.2 0.1 collective-permute-done.4.refs_0_
  20.3 1.1 %collective-permute-done.5.refs_1_ = bf16[16,720]{1,0:T(8,128)(2,1)S(1)} collective-permute-done((bf16[16,720]{1,0:T(8,128)(2,1)S(1)}, bf16[16,720]{1,0:T(8,128)(2,1)S(1)}, u32[]{:S(2)}, u32[]{:S(2)}) %collective-permute-start.5) | collective-permute-done | bytes 23072 | tf_op jit(solution)/shard_map/ppermute | solution.py:372
  21.4 0.4 collective-permute-done.6.refs_2_
  21.8 0.8 %collective-permute-start.8 = (bf16[64,720]{1,0:T(8,128)(2,1)S(1)}, bf16[64,720]{1,0:T(8,128)(2,1)S(1)}, u32[]{:S(2)}, u32[]{:S(2)}) collective-permute-start(bf16[64,720]{1,0:T(8,128)(2,1)S(1)} %shard_map.127.block_ref), channel_id=1, source_target_pairs={{0,2},{1,3},{2,0},{3,1},{4,6},{5,7},{6,4},{7,5},{8,10},{9,11},{10,... | collective-permute-start | bytes 276488 | tf_op jit(solution)/shard_map/ppermute | solution.py:358
  22.6 0.6 %shard_map.129.refs_7_.downs_ref = bf16[4,360,720]{2,1,0:T(8,128)(2,1)S(1)} custom-call(bf16[360,2880]{1,0:T(8,128)(2,1)S(1)} %bitcast.14), custom_call_target="tpu_custom_call" | custom-call | bytes 4147200 | tf_op jit(solution)/shard_map/pallas_call | solution.py:486
  23.2 0.4 %shard_map.128 = (f32[64,360]{1,0:T(8,128)S(1)}, f32[64,360]{1,0:T(8,128)S(1)}, f32[64,128]{1,0:T(8,128)S(1)}) custom-call(bf16[64,720]{1,0:T(8,128)(2,1)S(1)} %shard_map.127.block_ref, f32[4,1,720]{2,1,0:T(1,128)S(1)} %shard_map.126.gains_ref.refs_5_.refs_4_, bf16[4,360,720]{2,1,0:T(8,128)(2,1)S(1)} %shard_map.122.gates_ref.refs_6_.refs_5_, ...), custom_call_target="tpu_custom_call" | custom-call | flops 66355200 | bytes 1036800 | tf_op jit(solution)/shard_map/pallas_call | solution.py:484
  23.7 3.0 %collective-permute-done.8.refs_1_ = bf16[64,720]{1,0:T(8,128)(2,1)S(1)} collective-permute-done((bf16[64,720]{1,0:T(8,128)(2,1)S(1)}, bf16[64,720]{1,0:T(8,128)(2,1)S(1)}, u32[]{:S(2)}, u32[]{:S(2)}) %collective-permute-start.8) | collective-permute-done | bytes 92192 | tf_op jit(solution)/shard_map/ppermute | solution.py:358
  26.7 0.5 %collective-permute-start.21 = (bf16[512,256]{1,0:T(8,128)(2,1)S(1)}, bf16[512,256]{1,0:T(8,128)(2,1)S(1)}, u32[]{:S(2)}, u32[]{:S(2)}) collective-permute-start(bf16[512,256]{1,0:T(8,128)(2,1)S(1)} %get-tuple-element.112.refs_0_), channel_id=1, source_target_pairs={{0,1},{1,0},{2,3},{3,2},{4,5},{5,4},{6,7},{7,6},{8,9},{9,8},{10,11... | collective-permute-start | bytes 786440 | tf_op jit(solution)/shard_map/ppermute | solution.py:358
  27.2 0.0 collective-permute-start.20
  27.2 0.8 %shard_map.130 = (f32[64,360]{1,0:T(8,128)S(1)}, f32[64,360]{1,0:T(8,128)S(1)}, f32[64,128]{1,0:T(8,128)S(1)}) custom-call(bf16[64,720]{1,0:T(8,128)(2,1)S(1)} %collective-permute-done.10.refs_0_, bf16[64,720]{1,0:T(8,128)(2,1)S(1)} %collective-permute-done.8.refs_1_, f32[64,360]{1,0:T(8,128)S(1)} %get-tuple-element.83.refs_2_, ...), custom_call_target="tpu_custom_call" | custom-call | flops 66355200 | bytes 1036800 | tf_op jit(solution)/shard_map/pallas_call | solution.py:492
  28.0 0.7 %shard_map.131 = (bf16[1,64,720]{2,1,0:T(8,128)(2,1)S(1)}, bf16[64,360]{1,0:T(8,128)(2,1)S(1)}) custom-call(bf16[64,720]{1,0:T(8,128)(2,1)S(1)} %collective-permute-done.9.refs_0_, f32[64,360]{1,0:T(8,128)S(1)} %get-tuple-element.88.refs_1_, f32[64,360]{1,0:T(8,128)S(1)} %get-tuple-element.89.refs_2_, f32[64,128]{1,0:T(8,128)S(1)} %get-tuple-element.90.refs_3_, ...), custom_call_target="tpu_custom_call" | custom-call | flops 66355200 | bytes 1036800 | tf_op jit(solution)/shard_map/pallas_call | solution.py:495
  28.7 0.6 %collective-permute-start.11 = (bf16[1,64,720]{2,1,0:T(8,128)(2,1)S(1)}, bf16[1,64,720]{2,1,0:T(8,128)(2,1)S(1)}, u32[]{:S(2)}, u32[]{:S(2)}) collective-permute-start(bf16[1,64,720]{2,1,0:T(8,128)(2,1)S(1)} %get-tuple-element.95), channel_id=1, source_target_pairs={{0,1},{1,0},{2,3},{3,2},{4,5},{5,4},{6,7},{7,6},{8,9},{9,8},{10,11... | collective-permute-start | bytes 276488 | tf_op jit(solution)/shard_map/ppermute | solution.py:358
  29.3 0.4 shard_map.132
  29.7 0.6 %collective-permute-done.11.given_ref = bf16[1,64,720]{2,1,0:T(8,128)(2,1)S(1)} collective-permute-done((bf16[1,64,720]{2,1,0:T(8,128)(2,1)S(1)}, bf16[1,64,720]{2,1,0:T(8,128)(2,1)S(1)}, u32[]{:S(2)}, u32[]{:S(2)}) %collective-permute-start.11) | collective-permute-done | bytes 92192 | tf_op jit(solution)/shard_map/ppermute | solution.py:358
  30.2 0.4 collective-permute-start.12
  30.7 0.5 %collective-permute-start.13 = (bf16[32,720]{1,0:T(8,128)(2,1)S(1)}, bf16[32,720]{1,0:T(8,128)(2,1)S(1)}, u32[]{:S(2)}, u32[]{:S(2)}) collective-permute-start(bf16[32,720]{1,0:T(8,128)(2,1)S(1)} %get-tuple-element.96), channel_id=1, source_target_pairs={{0,3},{1,2},{2,1},{3,0},{4,7},{5,6},{6,5},{7,4},{8,11},{9,10},{10,... | collective-permute-start | bytes 138248 | tf_op jit(solution)/shard_map/ppermute | solution.py:358
  31.1 1.3 %collective-permute-start.16 = (bf16[32,720]{1,0:T(8,128)(2,1)S(1)}, bf16[32,720]{1,0:T(8,128)(2,1)S(1)}, u32[]{:S(2)}, u32[]{:S(2)}) collective-permute-start(bf16[32,720]{1,0:T(8,128)(2,1)S(1)} %get-tuple-element.97), channel_id=1, source_target_pairs={{0,3},{1,2},{2,1},{3,0},{4,7},{5,6},{6,5},{7,4},{8,11},{9,10},{10,... | collective-permute-start | bytes 138248 | tf_op jit(solution)/shard_map/ppermute | solution.py:358
  32.4 1.9 %collective-permute-done.13.refs_1_ = bf16[32,720]{1,0:T(8,128)(2,1)S(1)} collective-permute-done((bf16[32,720]{1,0:T(8,128)(2,1)S(1)}, bf16[32,720]{1,0:T(8,128)(2,1)S(1)}, u32[]{:S(2)}, u32[]{:S(2)}) %collective-permute-start.13) | collective-permute-done | bytes 46112 | tf_op jit(solution)/shard_map/ppermute | solution.py:358
  34.4 2.1 %collective-permute-start.14 = (bf16[16,720]{1,0:T(8,128)(2,1)S(1)}, bf16[16,720]{1,0:T(8,128)(2,1)S(1)}, u32[]{:S(2)}, u32[]{:S(2)}) collective-permute-start(bf16[16,720]{1,0:T(8,128)(2,1)S(1)} %get-tuple-element.102), channel_id=1, source_target_pairs={{0,13},{1,12},{2,15},{3,14},{4,9},{5,8},{6,11},{7,10},{8,5},{9,4},... | collective-permute-start | bytes 69128 | tf_op jit(solution)/shard_map/ppermute | solution.py:372
  36.5 0.3 collective-permute-start.15
  36.7 2.3 %collective-permute-start.17 = (bf16[16,720]{1,0:T(8,128)(2,1)S(1)}, bf16[16,720]{1,0:T(8,128)(2,1)S(1)}, u32[]{:S(2)}, u32[]{:S(2)}) collective-permute-start(bf16[16,720]{1,0:T(8,128)(2,1)S(1)} %get-tuple-element.107), channel_id=1, source_target_pairs={{0,5},{1,4},{2,7},{3,6},{4,1},{5,0},{6,3},{7,2},{8,13},{9,12},{10,... | collective-permute-start | bytes 69128 | tf_op jit(solution)/shard_map/ppermute | solution.py:372
  39.0 0.9 %shard_map.137.refs_6_ = bf16[720,256]{1,0:T(8,128)(2,1)S(1)} custom-call(bf16[512,256]{1,0:T(8,128)(2,1)S(1)} %get-tuple-element.112.refs_0_, bf16[512,256]{1,0:T(8,128)(2,1)S(1)} %collective-permute-done.20.refs_1_, bf16[512,256]{1,0:T(8,128)(2,1)S(1)} %collective-permute-done.21.refs_2_, bf16[512,256]{1,0:T(8,128)(2,1)S(1)} %collective-permute-done.19.refs_3_, ...), custom_call_target="tpu_custom_call" | custom-call | flops 754974720 | bytes 2949120 | tf_op jit(solution)/shard_map/pallas_call | solution.py:504
  40.0 0.9 %collective-permute-done.17.refs_2_ = bf16[16,720]{1,0:T(8,128)(2,1)S(1)} collective-permute-done((bf16[16,720]{1,0:T(8,128)(2,1)S(1)}, bf16[16,720]{1,0:T(8,128)(2,1)S(1)}, u32[]{:S(2)}, u32[]{:S(2)}) %collective-permute-start.17) | collective-permute-done | bytes 23072 | tf_op jit(solution)/shard_map/ppermute | solution.py:372
  40.9 0.6 %collective-permute-done.15.refs_1_ = bf16[16,720]{1,0:T(8,128)(2,1)S(1)} collective-permute-done((bf16[16,720]{1,0:T(8,128)(2,1)S(1)}, bf16[16,720]{1,0:T(8,128)(2,1)S(1)}, u32[]{:S(2)}, u32[]{:S(2)}) %collective-permute-start.15) | collective-permute-done | bytes 23072 | tf_op jit(solution)/shard_map/ppermute | solution.py:372
  41.5 1.0 %shard_map.138 = bf16[720,256]{1,0:T(8,128)(2,1)} custom-call(bf16[16,720]{1,0:T(8,128)(2,1)S(1)} %collective-permute-done.14.refs_0_, bf16[16,720]{1,0:T(8,128)(2,1)S(1)} %collective-permute-done.15.refs_1_, bf16[16,720]{1,0:T(8,128)(2,1)S(1)} %collective-permute-done.17.refs_2_, bf16[16,720]{1,0:T(8,128)(2,1)S(1)} %collective-permute-done.18.refs_3_, ...), custom_call_target="tpu_custom_call" | custom-call | tf_op jit(solution)/shard_map/pallas_call | solution.py:527
  (25 shorter events, 0.1 us)
Async XLA Ops:
  0.9 7.3 %collective-permute-start = (bf16[128,256]{1,0:T(8,128)(2,1)S(1)}, bf16[128,256]{1,0:T(8,128)(2,1)S(1)}, u32[]{:S(2)}, u32[]{:S(2)}) collective-permute-start(bf16[128,256]{1,0:T(8,128)(2,1)S(1)} %shard_map.119), channel_id=1, source_target_pairs={{0,4},{4,8},{8,12},{12,0},{1,5},{5,9},{9,13},{13,1},{2,6},{6,10},{... | collective-permute-start | bytes 196616 | tf_op jit(solution)/shard_map/ppermute | solution.py:411
  3.9 5.3 %copy-start = (bf16[1,2880,360]{1,2,0:T(8,128)(2,1)S(1)}, bf16[1,2880,360]{1,2,0:T(8,128)(2,1)}, u32[]{:S(2)}) copy-start(bf16[1,2880,360]{1,2,0:T(8,128)(2,1)} %param.21) | copy-start | bytes 6220804
  9.2 4.1 %collective-permute-start.1 = (bf16[64,512]{1,0:T(8,128)(2,1)S(1)}, bf16[64,512]{1,0:T(8,128)(2,1)S(1)}, u32[]{:S(2)}, u32[]{:S(2)}) collective-permute-start(bf16[64,512]{1,0:T(8,128)(2,1)S(1)} %get-tuple-element.69.rows_ref), channel_id=1, source_target_pairs={{0,3},{1,2},{2,1},{3,0},{4,7},{5,6},{6,5},{7,4},{8,11},{9,10},{10,... | collective-permute-start | bytes 196616 | tf_op jit(solution)/shard_map/ppermute | solution.py:358
  9.9 17.4 %collective-permute-start.19 = (bf16[512,256]{1,0:T(8,128)(2,1)S(1)}, bf16[512,256]{1,0:T(8,128)(2,1)S(1)}, u32[]{:S(2)}, u32[]{:S(2)}) collective-permute-start(bf16[512,256]{1,0:T(8,128)(2,1)S(1)} %get-tuple-element.112.refs_0_), channel_id=1, source_target_pairs={{0,3},{1,2},{2,1},{3,0},{4,7},{5,6},{6,5},{7,4},{8,11},{9,10},{10,... | collective-permute-start | bytes 786440 | tf_op jit(solution)/shard_map/ppermute | solution.py:358
  11.6 2.3 %collective-permute-start.3 = (bf16[64,512]{1,0:T(8,128)(2,1)S(1)}, bf16[64,512]{1,0:T(8,128)(2,1)S(1)}, u32[]{:S(2)}, u32[]{:S(2)}) collective-permute-start(bf16[64,512]{1,0:T(8,128)(2,1)S(1)} %get-tuple-element.69.rows_ref), channel_id=1, source_target_pairs={{0,1},{1,0},{2,3},{3,2},{4,5},{5,4},{6,7},{7,6},{8,9},{9,8},{10,11... | collective-permute-start | bytes 196616 | tf_op jit(solution)/shard_map/ppermute | solution.py:358
  13.3 1.5 %collective-permute-start.2 = (bf16[64,512]{1,0:T(8,128)(2,1)S(1)}, bf16[64,512]{1,0:T(8,128)(2,1)S(1)}, u32[]{:S(2)}, u32[]{:S(2)}) collective-permute-start(bf16[64,512]{1,0:T(8,128)(2,1)S(1)} %collective-permute-done.1.refs_1_), channel_id=1, source_target_pairs={{0,1},{1,0},{2,3},{3,2},{4,5},{5,4},{6,7},{7,6},{8,9},{9,8},{10,11... | collective-permute-start | bytes 196616 | tf_op jit(solution)/shard_map/ppermute | solution.py:358
  14.5 5.0 %copy-start.3 = (f32[2880]{0:T(1024)S(1)}, f32[2880]{0:T(1024)}, u32[]{:S(2)}) copy-start(f32[2880]{0:T(1024)} %gain_ref.1) | copy-start | bytes 34564
  14.6 5.0 %copy-start.1 = (bf16[1,2880,360]{1,2,0:T(8,128)(2,1)S(1)}, bf16[1,2880,360]{1,2,0:T(8,128)(2,1)}, u32[]{:S(2)}) copy-start(bf16[1,2880,360]{1,2,0:T(8,128)(2,1)} %param.22) | copy-start | bytes 6220804
  15.2 5.1 %collective-permute-start.4 = (bf16[16,720]{1,0:T(8,128)(2,1)S(1)}, bf16[16,720]{1,0:T(8,128)(2,1)S(1)}, u32[]{:S(2)}, u32[]{:S(2)}) collective-permute-start(bf16[16,720]{1,0:T(8,128)(2,1)S(1)} %get-tuple-element.74), channel_id=1, source_target_pairs={{0,13},{1,12},{2,15},{3,14},{4,9},{5,8},{6,11},{7,10},{8,5},{9,4},... | collective-permute-start | bytes 69128 | tf_op jit(solution)/shard_map/ppermute | solution.py:372
  17.1 4.4 %collective-permute-start.5 = (bf16[16,720]{1,0:T(8,128)(2,1)S(1)}, bf16[16,720]{1,0:T(8,128)(2,1)S(1)}, u32[]{:S(2)}, u32[]{:S(2)}) collective-permute-start(bf16[16,720]{1,0:T(8,128)(2,1)S(1)} %get-tuple-element.75), channel_id=1, source_target_pairs={{0,9},{1,8},{2,11},{3,10},{4,13},{5,12},{6,15},{7,14},{8,1},{9,0},... | collective-permute-start | bytes 69128 | tf_op jit(solution)/shard_map/ppermute | solution.py:372
  17.1 4.8 %collective-permute-start.6 = (bf16[16,720]{1,0:T(8,128)(2,1)S(1)}, bf16[16,720]{1,0:T(8,128)(2,1)S(1)}, u32[]{:S(2)}, u32[]{:S(2)}) collective-permute-start(bf16[16,720]{1,0:T(8,128)(2,1)S(1)} %get-tuple-element.76), channel_id=1, source_target_pairs={{0,5},{1,4},{2,7},{3,6},{4,1},{5,0},{6,3},{7,2},{8,13},{9,12},{10,... | collective-permute-start | bytes 69128 | tf_op jit(solution)/shard_map/ppermute | solution.py:372
  19.4 2.5 %collective-permute-start.7 = (bf16[16,720]{1,0:T(8,128)(2,1)S(1)}, bf16[16,720]{1,0:T(8,128)(2,1)S(1)}, u32[]{:S(2)}, u32[]{:S(2)}) collective-permute-start(bf16[16,720]{1,0:T(8,128)(2,1)S(1)} %get-tuple-element.77), channel_id=1, source_target_pairs={{0,1},{1,0},{2,3},{3,2},{4,5},{5,4},{6,7},{7,6},{8,9},{9,8},{10,11... | collective-permute-start | bytes 69128 | tf_op jit(solution)/shard_map/ppermute | solution.py:372
  19.6 3.0 %copy-start.2 = (bf16[1,360,2880]{2,1,0:T(8,128)(2,1)S(1)}, bf16[1,360,2880]{2,1,0:T(8,128)(2,1)}, u32[]{:S(2)}) copy-start(bf16[1,360,2880]{2,1,0:T(8,128)(2,1)} %param.23) | copy-start | bytes 6220804
  21.8 4.9 %collective-permute-start.8 = (bf16[64,720]{1,0:T(8,128)(2,1)S(1)}, bf16[64,720]{1,0:T(8,128)(2,1)S(1)}, u32[]{:S(2)}, u32[]{:S(2)}) collective-permute-start(bf16[64,720]{1,0:T(8,128)(2,1)S(1)} %shard_map.127.block_ref), channel_id=1, source_target_pairs={{0,2},{1,3},{2,0},{3,1},{4,6},{5,7},{6,4},{7,5},{8,10},{9,11},{10,... | collective-permute-start | bytes 276488 | tf_op jit(solution)/shard_map/ppermute | solution.py:358
  22.6 4.6 %collective-permute-start.10 = (bf16[64,720]{1,0:T(8,128)(2,1)S(1)}, bf16[64,720]{1,0:T(8,128)(2,1)S(1)}, u32[]{:S(2)}, u32[]{:S(2)}) collective-permute-start(bf16[64,720]{1,0:T(8,128)(2,1)S(1)} %shard_map.127.block_ref), channel_id=1, source_target_pairs={{0,1},{1,0},{2,3},{3,2},{4,5},{5,4},{6,7},{7,6},{8,9},{9,8},{10,11... | collective-permute-start | bytes 276488 | tf_op jit(solution)/shard_map/ppermute | solution.py:358
  26.7 1.3 %collective-permute-start.9 = (bf16[64,720]{1,0:T(8,128)(2,1)S(1)}, bf16[64,720]{1,0:T(8,128)(2,1)S(1)}, u32[]{:S(2)}, u32[]{:S(2)}) collective-permute-start(bf16[64,720]{1,0:T(8,128)(2,1)S(1)} %collective-permute-done.8.refs_1_), channel_id=1, source_target_pairs={{0,1},{1,0},{2,3},{3,2},{4,5},{5,4},{6,7},{7,6},{8,9},{9,8},{10,11... | collective-permute-start | bytes 276488 | tf_op jit(solution)/shard_map/ppermute | solution.py:358
  26.7 12.3 %collective-permute-start.21 = (bf16[512,256]{1,0:T(8,128)(2,1)S(1)}, bf16[512,256]{1,0:T(8,128)(2,1)S(1)}, u32[]{:S(2)}, u32[]{:S(2)}) collective-permute-start(bf16[512,256]{1,0:T(8,128)(2,1)S(1)} %get-tuple-element.112.refs_0_), channel_id=1, source_target_pairs={{0,1},{1,0},{2,3},{3,2},{4,5},{5,4},{6,7},{7,6},{8,9},{9,8},{10,11... | collective-permute-start | bytes 786440 | tf_op jit(solution)/shard_map/ppermute | solution.py:358
  27.2 11.8 %collective-permute-start.20 = (bf16[512,256]{1,0:T(8,128)(2,1)S(1)}, bf16[512,256]{1,0:T(8,128)(2,1)S(1)}, u32[]{:S(2)}, u32[]{:S(2)}) collective-permute-start(bf16[512,256]{1,0:T(8,128)(2,1)S(1)} %collective-permute-done.19.refs_3_), channel_id=1, source_target_pairs={{0,1},{1,0},{2,3},{3,2},{4,5},{5,4},{6,7},{7,6},{8,9},{9,8},{10,11... | collective-permute-start | bytes 786440 | tf_op jit(solution)/shard_map/ppermute | solution.py:358
  28.7 1.5 %collective-permute-start.11 = (bf16[1,64,720]{2,1,0:T(8,128)(2,1)S(1)}, bf16[1,64,720]{2,1,0:T(8,128)(2,1)S(1)}, u32[]{:S(2)}, u32[]{:S(2)}) collective-permute-start(bf16[1,64,720]{2,1,0:T(8,128)(2,1)S(1)} %get-tuple-element.95), channel_id=1, source_target_pairs={{0,1},{1,0},{2,3},{3,2},{4,5},{5,4},{6,7},{7,6},{8,9},{9,8},{10,11... | collective-permute-start | bytes 276488 | tf_op jit(solution)/shard_map/ppermute | solution.py:358
  30.2 2.2 %collective-permute-start.12 = (bf16[1,64,720]{2,1,0:T(8,128)(2,1)S(1)}, bf16[1,64,720]{2,1,0:T(8,128)(2,1)S(1)}, u32[]{:S(2)}, u32[]{:S(2)}) collective-permute-start(bf16[1,64,720]{2,1,0:T(8,128)(2,1)S(1)} %get-tuple-element.98), channel_id=1, source_target_pairs={{0,1},{1,0},{2,3},{3,2},{4,5},{5,4},{6,7},{7,6},{8,9},{9,8},{10,11... | collective-permute-start | bytes 276488 | tf_op jit(solution)/shard_map/ppermute | solution.py:358
  30.7 3.7 %collective-permute-start.13 = (bf16[32,720]{1,0:T(8,128)(2,1)S(1)}, bf16[32,720]{1,0:T(8,128)(2,1)S(1)}, u32[]{:S(2)}, u32[]{:S(2)}) collective-permute-start(bf16[32,720]{1,0:T(8,128)(2,1)S(1)} %get-tuple-element.96), channel_id=1, source_target_pairs={{0,3},{1,2},{2,1},{3,0},{4,7},{5,6},{6,5},{7,4},{8,11},{9,10},{10,... | collective-permute-start | bytes 138248 | tf_op jit(solution)/shard_map/ppermute | solution.py:358
  31.1 5.6 %collective-permute-start.16 = (bf16[32,720]{1,0:T(8,128)(2,1)S(1)}, bf16[32,720]{1,0:T(8,128)(2,1)S(1)}, u32[]{:S(2)}, u32[]{:S(2)}) collective-permute-start(bf16[32,720]{1,0:T(8,128)(2,1)S(1)} %get-tuple-element.97), channel_id=1, source_target_pairs={{0,3},{1,2},{2,1},{3,0},{4,7},{5,6},{6,5},{7,4},{8,11},{9,10},{10,... | collective-permute-start | bytes 138248 | tf_op jit(solution)/shard_map/ppermute | solution.py:358
  34.4 6.5 %collective-permute-start.14 = (bf16[16,720]{1,0:T(8,128)(2,1)S(1)}, bf16[16,720]{1,0:T(8,128)(2,1)S(1)}, u32[]{:S(2)}, u32[]{:S(2)}) collective-permute-start(bf16[16,720]{1,0:T(8,128)(2,1)S(1)} %get-tuple-element.102), channel_id=1, source_target_pairs={{0,13},{1,12},{2,15},{3,14},{4,9},{5,8},{6,11},{7,10},{8,5},{9,4},... | collective-permute-start | bytes 69128 | tf_op jit(solution)/shard_map/ppermute | solution.py:372
  36.5 5.1 %collective-permute-start.15 = (bf16[16,720]{1,0:T(8,128)(2,1)S(1)}, bf16[16,720]{1,0:T(8,128)(2,1)S(1)}, u32[]{:S(2)}, u32[]{:S(2)}) collective-permute-start(bf16[16,720]{1,0:T(8,128)(2,1)S(1)} %get-tuple-element.103), channel_id=1, source_target_pairs={{0,9},{1,8},{2,11},{3,10},{4,13},{5,12},{6,15},{7,14},{8,1},{9,0},... | collective-permute-start | bytes 69128 | tf_op jit(solution)/shard_map/ppermute | solution.py:372
  36.7 4.1 %collective-permute-start.17 = (bf16[16,720]{1,0:T(8,128)(2,1)S(1)}, bf16[16,720]{1,0:T(8,128)(2,1)S(1)}, u32[]{:S(2)}, u32[]{:S(2)}) collective-permute-start(bf16[16,720]{1,0:T(8,128)(2,1)S(1)} %get-tuple-element.107), channel_id=1, source_target_pairs={{0,5},{1,4},{2,7},{3,6},{4,1},{5,0},{6,3},{7,2},{8,13},{9,12},{10,... | collective-permute-start | bytes 69128 | tf_op jit(solution)/shard_map/ppermute | solution.py:372
  39.0 1.9 %collective-permute-start.18 = (bf16[16,720]{1,0:T(8,128)(2,1)S(1)}, bf16[16,720]{1,0:T(8,128)(2,1)S(1)}, u32[]{:S(2)}, u32[]{:S(2)}) collective-permute-start(bf16[16,720]{1,0:T(8,128)(2,1)S(1)} %get-tuple-element.108), channel_id=1, source_target_pairs={{0,1},{1,0},{2,3},{3,2},{4,5},{5,4},{6,7},{7,6},{8,9},{9,8},{10,11... | collective-permute-start | bytes 69128 | tf_op jit(solution)/shard_map/ppermute | solution.py:372

commit v15 on v13

--- a/solution.py
+++ b/solution.py
@@ -98,10 +98,6 @@
 def key_query(span):
     key = lax.broadcasted_iota(jnp.int32, (span, KEYS_SEEN), 0)
     return key, lax.broadcasted_iota(jnp.int32, (span, KEYS_SEEN), 1)
-
-
-def per_head(pair):
-    return jnp.concatenate([jnp.broadcast_to(row, (HEAD_SIZE, row.shape[1])) for row in pair], axis=0)
 
 
 def fill_tables(live, ids, weights, placing_ref, mix_hi_ref, mix_lo_ref):
@@ -127,8 +123,8 @@
 
 def first_kernel(live, *refs):
     loaded, held = refs[:8], refs[8:13]
-    placing_ref, mix_hi_ref, mix_lo_ref, sinks_out, late_ref, rows_ref, mixed_ref, peaks_ref, sums_ref = refs[13:22]
-    ids_ref, weights_ref, sinks_ref, sems = refs[22:]
+    placing_ref, mix_hi_ref, mix_lo_ref, sinks_out, late_ref, rows_ref = refs[13:19]
+    ids_ref, weights_ref, sinks_ref, sems = refs[19:]
     targets = (ids_ref, weights_ref, sinks_ref, *held)
     copies = [pltpu.make_async_copy(*pair, sems.at[i]) for i, pair in enumerate(zip(loaded, targets))]
     for copy in copies:
@@ -152,52 +148,22 @@
             part = sinks[2 * first : 2 * (first + len(pairs))]
             mixed = attend_block(pairs, kv_ref[span, g * PAIR : (g + 1) * PAIR], part, allowed)
             store_pairs(mixed, first, late_ref, slice((b - 1) * KEYS_SEEN, b * KEYS_SEEN))
-    key, query = key_query(KEYS_SEEN)
-    for g in range(mixed_ref.shape[0]):
-        _, pairs = group_queries(q_ref, g, groups, 0)
-        keys, values = split_pair(kv_ref[:KEYS_SEEN, g * PAIR : (g + 1) * PAIR])
-        terms = []
-        for i, part in enumerate(score(pairs, keys, key <= query)):
-            peak = jnp.max(part, axis=0, keepdims=True)
-            terms.append(jnp.exp2(part - peak))
-            peaks_ref[2 * g + i : 2 * g + i + 1] = peak
-            sums_ref[2 * g + i : 2 * g + i + 1] = jnp.sum(terms[-1], axis=0, keepdims=True)
-        mixed_ref[g] = dot(values, jnp.concatenate(terms, axis=0).astype(jnp.bfloat16), TN)
     rows_ref[...] = dot(placing_ref[:, KEYS_SEEN:], late_ref[...], NT)
     for copy in copies[5:]:
         copy.wait()
 
 
-def second_kernel(q_ref, kv_ref, before_ref, rim_ref, sinks_ref, late_ref, placing_ref, *refs):
-    late_rows_ref, mixed_ref, peaks_ref, sums_ref, all_ref, rows_ref = refs
+def second_kernel(q_ref, kv_ref, before_ref, rim_ref, sinks_ref, late_ref, placing_ref, late_rows_ref, all_ref, rows_ref):
     rim = jnp.where(lax.axis_index("seq") == 0, before_ref[...], rim_ref[...])
     groups = rim.shape[1] // PAIR
     key, query = key_query(SPAN)
     allowed = (key > query) & (key <= query + KEYS_SEEN)
-    key, query = key_query(KEYS_SEEN)
     for g in range(groups):
         first, pairs = group_queries(q_ref, g, groups, 0)
         sinks = [sinks_ref[h : h + 1] for h in range(2 * first, 2 * (first + len(pairs)))]
         lanes = slice(g * PAIR, (g + 1) * PAIR)
-        if g >= mixed_ref.shape[0]:
-            both = jnp.concatenate([rim[:, lanes], kv_ref[:KEYS_SEEN, lanes]], axis=0)
-            store_pairs(attend_block(pairs, both, sinks, allowed), first, all_ref, slice(0, KEYS_SEEN))
-            continue
-        keys, values = split_pair(rim[:, lanes])
-        terms, scales, inverses = [], [], []
-        for i, part in enumerate(score(pairs, keys, key > query)):
-            sink = sink_row(sinks, i, len(pairs))
-            own_peak = peaks_ref[2 * g + i : 2 * g + i + 1]
-            peak = jnp.maximum(jnp.max(part, axis=0, keepdims=True), jnp.maximum(own_peak, sink))
-            scale = jnp.exp2(own_peak - peak)
-            terms.append(jnp.exp2(part - peak))
-            denom = jnp.sum(terms[-1], axis=0, keepdims=True) + jnp.exp2(sink - peak)
-            denom += sums_ref[2 * g + i : 2 * g + i + 1] * scale
-            inverses.append(1.0 / denom)
-            scales.append(scale)
-        mixed = dot(values, jnp.concatenate(terms, axis=0).astype(jnp.bfloat16), TN)
-        mixed = (mixed + mixed_ref[g] * per_head(scales)) * per_head(inverses)
-        store_pairs(mixed.astype(jnp.bfloat16), first, all_ref, slice(0, KEYS_SEEN))
+        both = jnp.concatenate([rim[:, lanes], kv_ref[:KEYS_SEEN, lanes]], axis=0)
+        store_pairs(attend_block(pairs, both, sinks, allowed), first, all_ref, slice(0, KEYS_SEEN))
     rows = late_rows_ref[...] + dot(placing_ref[:, :KEYS_SEEN], all_ref[:, :KEYS_SEEN], NT)
     rows_ref[...] = rows.astype(jnp.bfloat16)
     all_ref[:, KEYS_SEEN:] = late_ref[...]
@@ -263,44 +229,18 @@
         blocks_ref[p] = gain[:, p * width : (p + 1) * width]
 
 
-def add_features(sums, places, blocks, gains_ref, gates_ref, ups_ref, steps):
-    gate, up, squares = sums
-    for i, block in zip(places, blocks):
+def expert_kernel(places, steps, *refs):
+    blocks = refs[: 2 * steps]
+    gains_ref, gates_ref, ups_ref, downs_ref, given_ref, activated_ref = refs[2 * steps :]
+    wide = [block[...].astype(jnp.float32) for block in blocks]
+    squares = sum(jnp.sum(block * block, axis=1, keepdims=True) for block in wide)
+    scale = lax.rsqrt(squares / (len(blocks) * wide[0].shape[1]) + norm_eps)
+    gate, up = 0.0, 0.0
+    for i, block in zip(places, wide):
         p = origin(i % steps, i >= steps)
-        wide = block[...].astype(jnp.float32)
-        squares += jnp.sum(wide * wide, axis=1, keepdims=True)
-        rows = (wide * gains_ref[p]).astype(jnp.bfloat16)
+        rows = (block * scale * gains_ref[p]).astype(jnp.bfloat16)
         gate += dot(rows, gates_ref[p], NT)
         up += dot(rows, ups_ref[p], NT)
-    return gate, up, squares
-
-
-def store_sums(sums, refs):
-    for ref, value in zip(refs, sums):
-        ref[...] = jnp.broadcast_to(value, ref.shape)
-
-
-def expert_own_kernel(steps, block_ref, gains_ref, gates_ref, ups_ref, *out_refs):
-    zeros = jnp.zeros(out_refs[0].shape, jnp.float32)
-    sums = (zeros, zeros, jnp.zeros((zeros.shape[0], 1), jnp.float32))
-    store_sums(add_features(sums, [steps], [block_ref], gains_ref, gates_ref, ups_ref, steps), out_refs)
-
-
-def expert_more_kernel(places, steps, *refs):
-    blocks, refs = refs[:-9], refs[-9:]
-    sums = (refs[0][...], refs[1][...], refs[2][:, :1])
-    store_sums(add_features(sums, places, blocks, *refs[3:6], steps), refs[6:])
-
-
-def expert_last_kernel(steps, *refs):
-    blocks, refs = refs[: steps - 1], refs[steps - 1 :]
-    sums = (refs[0][...], refs[1][...], refs[2][:, :1])
-    gains_ref, gates_ref, ups_ref, downs_ref, given_ref, activated_ref = refs[3:]
-    places = range(1, steps)
-    gate, up, squares = add_features(sums, places, blocks, gains_ref, gates_ref, ups_ref, steps)
-    cuts, _, width = gates_ref.shape
-    scale = lax.rsqrt(squares / (cuts * width) + norm_eps)
-    gate, up = gate * scale, up * scale
     activated = ((up + 1.0) * gate * jax.nn.sigmoid(glu_alpha * gate)).astype(jnp.bfloat16)
     activated_ref[...] = activated
     for k in range(steps):
@@ -317,7 +257,7 @@
     for i, out_ref in enumerate(out_refs):
         rows = slice(i % 2 * half, (i % 2 + 1) * half)
         total = kept_ref[i // 2, rows].astype(jnp.float32) + given_ref[i // 2, rows].astype(jnp.float32)
-        out_ref[...] = total.astype(jnp.bfloat16)
+        out_ref[...] = total.astype(out_ref.dtype)
 
 
 def add_chips_kernel(steps, *refs):
@@ -400,11 +340,7 @@
     tail = keyvals[toks - KEYS_SEEN :]
     rim = lax.ppermute(tail, "seq", [(i, (i + 1) % size) for i in range(size)])
     loads = (queries, keyvals, preceding_keyvalues, w_out.T, residual.T)
-    groups = keyvals.shape[1] // PAIR
-    across = head_rows // PAIR // groups * KEYS_SEEN
-    early = (groups + 1) // 2
-    part_sums = jax.ShapeDtypeStruct((2 * early, across), jnp.float32)
-    q, kv, before, w_t, residual_t, placing, mix_hi, mix_lo, sinks, late, *parts = call(
+    q, kv, before, w_t, residual_t, placing, mix_hi, mix_lo, sinks, late, late_rows = call(
         functools.partial(first_kernel, live),
         (
             *(bf16(*a.shape) for a in loads),
@@ -412,9 +348,6 @@
             jax.ShapeDtypeStruct((heads, KEYS_SEEN), jnp.float32),
             bf16(head_rows, toks - KEYS_SEEN),
             jax.ShapeDtypeStruct((slots, head_rows), jnp.float32),
-            jax.ShapeDtypeStruct((early, PAIR, across), jnp.float32),
-            part_sums,
-            part_sums,
         ),
         n_in=8,
         scratch=[
@@ -430,10 +363,10 @@
     attended, rows = call(
         second_kernel,
         (bf16(head_rows, toks), bf16(slots, head_rows)),
-        n_in=11,
+        n_in=8,
         flops=2 * toks * SPAN * head_rows,
         moved=2 * queries.size,
-    )(q, kv, before, rim, sinks, late, placing, *parts)
+    )(q, kv, before, rim, sinks, late, placing, late_rows)
 
     chip_rows = from_chips(rows)
     total = jax.ShapeDtypeStruct((slots, feats), jnp.float32)
@@ -464,30 +397,22 @@
 
     ups = spread()(after(w_up[0].T, outgoing[0]))
     gains = call(spread_gain_kernel, jax.ShapeDtypeStruct((cuts, 1, feats), jnp.float32), n_in=1)(norm_gain)
-    sums = (
-        *(jax.ShapeDtypeStruct((slots, hidden), jnp.float32),) * 2,
-        jax.ShapeDtypeStruct((slots, KEYS_SEEN), jnp.float32),
-    )
     part = dict(flops=slots * w_gate.size, moved=w_gate.size)
     stacked = call(stack_kernel, bf16(slots, feats), n_in=live)(*after(arrived, (ups, gains)))
     chip_rows = from_chips(stacked, False)
-    own = call(functools.partial(expert_own_kernel, steps), sums, n_in=4, **part)(stacked, gains, gates, ups)
     sibling_rows = from_sibling(stacked)
     downs = spread()(after(w_down[0], stacked))
     chip_blocks = from_chips(after(attended, gates))
     sibling_block, *relayed_blocks = [from_sibling(b) for b in (attended, *chip_blocks)]
     blocks = [attended, *relayed_blocks, sibling_block, *chip_blocks]
-    chip_rows = after(chip_rows, (own, downs))
+    chip_rows = after(chip_rows, downs)
     relayed_rows = [from_sibling(b) for b in chip_rows]
-    chips = call(functools.partial(expert_more_kernel, [0, *range(steps + 1, 2 * steps)], steps), sums, n_in=steps + 6, **part)(
-        sibling_rows, *chip_rows, *own, gains, gates, ups
-    )
     given, activated = call(
-        functools.partial(expert_last_kernel, steps),
+        functools.partial(expert_kernel, [steps, 0, *range(steps + 1, 2 * steps), *range(1, steps)], steps),
         (bf16(steps, slots, feats), bf16(slots, hidden)),
-        n_in=steps + 6,
+        n_in=cuts + 4,
         **part,
-    )(*relayed_rows, *chips, gains, gates, ups, downs)
+    )(stacked, sibling_rows, *chip_rows, *relayed_rows, gains, gates, ups, downs)
     kept = call(expert_kept_kernel, bf16(steps, slots, feats), n_in=2, **part)(activated, downs)
     resid = call(
         functools.partial(project_kernel, steps),
@@ -497,7 +422,8 @@
         moved=2 * w_out.size,
     )(*blocks, w_t, residual_t)
 
-    sums = call(add_cores_kernel, (bf16(slots // 2, feats),) * (2 * steps), n_in=2)(
+    half = jax.ShapeDtypeStruct((slots // 2, feats), jnp.float32)
+    sums = call(add_cores_kernel, (half,) * 2 + (bf16(slots // 2, feats),) * (2 * steps - 2), n_in=2)(
         kept, swap(given, "cuts", 1)
     )
     returned = []

time: 42.4 us -> 43.7 us (1.031)
  waiting for transfers between devices: 11.7 us -> 13.6 us
  starting transfers between devices: 18.5 us -> 18 us
    ppermute x12, waiting for transfers between devices: 6.94 us -> 8.58 us  [swap(): lax.ppermute(block, axis, [(i, i ^ mask) for i in range(lax.axis_size(axi...]
    pallas_call x4 -> x2, Pallas kernels: 2.02 us -> 1.91 us  [the longest x1 1.86 us: shards(): call(functools.partial(expert_kernel, [steps, 0, *range(steps + 1, 2 * st...]
  transfers between devices with their start and end apart: 21 -> 21, of which waited for: 10 -> 11; matrix products, arithmetic and copies ran while one was open for 0% -> 0% of each run, Pallas kernels for 21% -> 20%
where the time goes in v15:
time: 43.7 us; the launch traced here: 43.6 us
  starting transfers between devices  18 us (41%)
  waiting for transfers between devices  13.6 us (31%)
  Pallas kernels  11 us (25%)
  local copies, waits for them, and re-layouts  0.86 us (2%)
    ppermute x8, starting transfers between devices, to_seq(): lax.ppermute(block, ('seq', 'cuts'), [(i, i ^ mask) for i in range(size)])  8.93 us
    ppermute x12, waiting for transfers between devices, swap(): lax.ppermute(block, axis, [(i, i ^ mask) for i in range(lax.axis_size(axi...  8.58 us
    ppermute x12, starting transfers between devices, swap(): lax.ppermute(block, axis, [(i, i ^ mask) for i in range(lax.axis_size(axi...  6.04 us
    ppermute x8, waiting for transfers between devices, to_seq(): lax.ppermute(block, ('seq', 'cuts'), [(i, i ^ mask) for i in range(size)])  3.14 us
    ppermute x1, starting transfers between devices, shards(): rim = lax.ppermute(tail, 'seq', [(i, (i + 1) % size) for i in range(size)])  3.02 us
    pallas_call x1, Pallas kernels, shards(): call(functools.partial(first_kernel, live), (*(bf16(*a.shape) for a in lo...  2.37 us
    ppermute x1, waiting for transfers between devices, shards(): rim = lax.ppermute(tail, 'seq', [(i, (i + 1) % size) for i in range(size)])  1.89 us
    pallas_call x1, Pallas kernels, shards(): call(functools.partial(expert_kernel, [steps, 0, *range(steps + 1, 2 * st...  1.86 us
  transfers between devices with their start and end apart: 21, of which 11 were waited for; matrix products, arithmetic and copies ran while one was open for 0% of the time, Pallas kernels for 20%

profile of v15, /device:TPU:0, one launch (start us, length us, event | category | flops | bytes accessed | tf_op | source)
XLA Modules:
  0.0 43.6 jit_solution(556139632744165488)
XLA Ops:
  0.0 0.8 %slice.3 = bf16[128,256]{1,0:T(8,128)(2,1)S(1)} slice(bf16[256,256]{1,0:T(8,128)(2,1)} %refs_4_.1), slice={[128:256], [0:256]} | slice | bytes 131072 | tf_op jit(solution)/shard_map/slice | solution.py:340
  0.8 3.0 %collective-permute-start = (bf16[128,256]{1,0:T(8,128)(2,1)S(1)}, bf16[128,256]{1,0:T(8,128)(2,1)S(1)}, u32[]{:S(2)}, u32[]{:S(2)}) collective-permute-start(bf16[128,256]{1,0:T(8,128)(2,1)S(1)} %slice.3), channel_id=1, source_target_pairs={{0,4},{4,8},{8,12},{12,0},{1,5},{5,9},{9,13},{13,1},{2,6},{6,10},{... | collective-permute-start | bytes 196616 | tf_op jit(solution)/shard_map/ppermute | solution.py:341
  3.9 2.4 %shard_map.118 = (bf16[256,512]{1,0:T(8,128)(2,1)S(1)}, bf16[256,256]{1,0:T(8,128)(2,1)S(1)}, bf16[128,256]{1,0:T(8,128)(2,1)S(1)}, bf16[720,2048]{1,0:T(8,128)(...) custom-call(s32[4,256]{1,0:T(4,128)} %bitcast.17, ...), custom_call_target="tpu_custom_call" | custom-call | flops 134217728 | bytes 3579904 | tf_op jit(solution)/shard_map/pallas_call | solution.py:343
  6.2 1.9 %collective-permute-done.rim_ref = bf16[128,256]{1,0:T(8,128)(2,1)S(1)} collective-permute-done((bf16[128,256]{1,0:T(8,128)(2,1)S(1)}, bf16[128,256]{1,0:T(8,128)(2,1)S(1)}, u32[]{:S(2)}, u32[]{:S(2)}) %collective-permute-start) | collective-permute-done | bytes 65568 | tf_op jit(solution)/shard_map/ppermute | solution.py:341
  8.1 1.1 %shard_map.119 = (bf16[512,256]{1,0:T(8,128)(2,1)S(1)}, bf16[64,512]{1,0:T(8,128)(2,1)S(1)}) custom-call(bf16[256,512]{1,0:T(8,128)(2,1)S(1)} %get-tuple-element.42.q_ref, bf16[256,256]{1,0:T(8,128)(2,1)S(1)} %get-tuple-element.43.kv_ref, bf16[128,256]{1,0:T(8,128)(2,1)S(1)} %get-tuple-element.44.before_ref, ...), custom_call_target="tpu_custom_call" | custom-call | flops 67108864 | bytes 262144 | tf_op jit(solution)/shard_map/pallas_call | solution.py:363
  9.3 0.1 collective-permute-start.1
  9.4 0.6 %shard_map.121.refs_5_ = bf16[4,360,720]{2,1,0:T(8,128)(2,1)S(1)} custom-call(bf16[360,2880]{1,0:T(8,128)(2,1)S(1)} %bitcast.12), custom_call_target="tpu_custom_call" | custom-call | bytes 4147200 | tf_op jit(solution)/shard_map/pallas_call | solution.py:382
  10.0 1.8 %collective-permute-start.18 = (bf16[512,256]{1,0:T(8,128)(2,1)S(1)}, bf16[512,256]{1,0:T(8,128)(2,1)S(1)}, u32[]{:S(2)}, u32[]{:S(2)}) collective-permute-start(bf16[512,256]{1,0:T(8,128)(2,1)S(1)} %get-tuple-element.78.refs_0_), channel_id=1, source_target_pairs={{0,3},{1,2},{2,1},{3,0},{4,7},{5,6},{6,5},{7,4},{8,11},{9,10},{10,... | collective-permute-start | bytes 786440 | tf_op jit(solution)/shard_map/ppermute | solution.py:290
  11.8 0.1 collective-permute-start.3
  11.9 0.5 %shard_map.120.refs_2_ = f32[64,720]{1,0:T(8,128)S(1)} custom-call(bf16[64,512]{1,0:T(8,128)(2,1)S(1)} %get-tuple-element.49.rows_ref, bf16[720,2048]{1,0:T(8,128)(2,1)S(1)} %get-tuple-element.50.w_ref.refs_3_.refs_2_.refs_4_, bf16[720,256]{1,0:T(8,128)(2,1)S(1)} %get-tuple-element.51.residual_ref.refs_5_, bf16[64,256]{1,0:T(8,128)(2,1)S(1)} %get-tuple-element.47.placing_ref), custom_call_target="tpu_custom_call" | custom-call | flops 47185920 | bytes 737280 | tf_op jit(solution)/shard_map/pallas_call | solution.py:374
  12.4 1.1 %collective-permute-done.1.refs_1_ = bf16[64,512]{1,0:T(8,128)(2,1)S(1)} collective-permute-done((bf16[64,512]{1,0:T(8,128)(2,1)S(1)}, bf16[64,512]{1,0:T(8,128)(2,1)S(1)}, u32[]{:S(2)}, u32[]{:S(2)}) %collective-permute-start.1) | collective-permute-done | bytes 65568 | tf_op jit(solution)/shard_map/ppermute | solution.py:290
  13.5 0.6 %collective-permute-start.2 = (bf16[64,512]{1,0:T(8,128)(2,1)S(1)}, bf16[64,512]{1,0:T(8,128)(2,1)S(1)}, u32[]{:S(2)}, u32[]{:S(2)}) collective-permute-start(bf16[64,512]{1,0:T(8,128)(2,1)S(1)} %collective-permute-done.1.refs_1_), channel_id=1, source_target_pairs={{0,1},{1,0},{2,3},{3,2},{4,5},{5,4},{6,7},{7,6},{8,9},{9,8},{10,11... | collective-permute-start | bytes 196616 | tf_op jit(solution)/shard_map/ppermute | solution.py:290
  14.1 0.0 collective-permute-done.3.refs_0_
  14.1 0.6 %shard_map.122.refs_1_ = f32[64,720]{1,0:T(8,128)S(1)} custom-call(bf16[64,512]{1,0:T(8,128)(2,1)S(1)} %collective-permute-done.3.refs_0_, bf16[64,512]{1,0:T(8,128)(2,1)S(1)} %collective-permute-done.1.refs_1_, f32[64,720]{1,0:T(8,128)S(1)} %shard_map.120.refs_2_, bf16[720,2048]{1,0:T(8,128)(2,1)S(1)} %get-tuple-element.50.w_ref.refs_3_.refs_2_.refs_4_), custom_call_target="tpu_custom_call" | custom-call | flops 47185920 | bytes 737280 | tf_op jit(solution)/shard_map/pallas_call | solution.py:385
  14.7 0.0 copy-start.3
  14.7 0.0 copy-start.1
  14.7 0.3 collective-permute-done.2.refs_0_
  15.0 0.4 shard_map.123
  15.4 1.8 %collective-permute-start.4 = (bf16[16,720]{1,0:T(8,128)(2,1)S(1)}, bf16[16,720]{1,0:T(8,128)(2,1)S(1)}, u32[]{:S(2)}, u32[]{:S(2)}) collective-permute-start(bf16[16,720]{1,0:T(8,128)(2,1)S(1)} %get-tuple-element.54), channel_id=1, source_target_pairs={{0,13},{1,12},{2,15},{3,14},{4,9},{5,8},{6,11},{7,10},{8,5},{9,4},... | collective-permute-start | bytes 69128 | tf_op jit(solution)/shard_map/ppermute | solution.py:304
  17.2 2.3 %collective-permute-start.6 = (bf16[16,720]{1,0:T(8,128)(2,1)S(1)}, bf16[16,720]{1,0:T(8,128)(2,1)S(1)}, u32[]{:S(2)}, u32[]{:S(2)}) collective-permute-start(bf16[16,720]{1,0:T(8,128)(2,1)S(1)} %get-tuple-element.56), channel_id=1, source_target_pairs={{0,5},{1,4},{2,7},{3,6},{4,1},{5,0},{6,3},{7,2},{8,13},{9,12},{10,... | collective-permute-start | bytes 69128 | tf_op jit(solution)/shard_map/ppermute | solution.py:304
  19.5 0.2 collective-permute-start.7
  19.7 0.1 shard_map.125.refs_4_
  19.8 0.6 %shard_map.124.refs_6_ = bf16[4,360,720]{2,1,0:T(8,128)(2,1)S(1)} custom-call(bf16[360,2880]{1,0:T(8,128)(2,1)S(1)} %bitcast.13), custom_call_target="tpu_custom_call" | custom-call | bytes 4147200 | tf_op jit(solution)/shard_map/pallas_call | solution.py:398
  20.4 0.1 collective-permute-done.4.refs_0_
  20.5 1.1 %collective-permute-done.5.refs_1_ = bf16[16,720]{1,0:T(8,128)(2,1)S(1)} collective-permute-done((bf16[16,720]{1,0:T(8,128)(2,1)S(1)}, bf16[16,720]{1,0:T(8,128)(2,1)S(1)}, u32[]{:S(2)}, u32[]{:S(2)}) %collective-permute-start.5) | collective-permute-done | bytes 23072 | tf_op jit(solution)/shard_map/ppermute | solution.py:304
  21.6 0.4 collective-permute-done.6.refs_2_
  22.0 0.0 collective-permute-done.7.refs_3_
  22.0 0.8 %collective-permute-start.9 = (bf16[64,720]{1,0:T(8,128)(2,1)S(1)}, bf16[64,720]{1,0:T(8,128)(2,1)S(1)}, u32[]{:S(2)}, u32[]{:S(2)}) collective-permute-start(bf16[64,720]{1,0:T(8,128)(2,1)S(1)} %shard_map.126.refs_0_), channel_id=1, source_target_pairs={{0,2},{1,3},{2,0},{3,1},{4,6},{5,7},{6,4},{7,5},{8,10},{9,11},{10,... | collective-permute-start | bytes 276488 | tf_op jit(solution)/shard_map/ppermute | solution.py:290
  22.8 0.6 %shard_map.127.refs_7_.downs_ref = bf16[4,360,720]{2,1,0:T(8,128)(2,1)S(1)} custom-call(bf16[360,2880]{1,0:T(8,128)(2,1)S(1)} %bitcast.14), custom_call_target="tpu_custom_call" | custom-call | bytes 4147200 | tf_op jit(solution)/shard_map/pallas_call | solution.py:404
  23.4 3.5 %collective-permute-done.9.refs_2_ = bf16[64,720]{1,0:T(8,128)(2,1)S(1)} collective-permute-done((bf16[64,720]{1,0:T(8,128)(2,1)S(1)}, bf16[64,720]{1,0:T(8,128)(2,1)S(1)}, u32[]{:S(2)}, u32[]{:S(2)}) %collective-permute-start.9) | collective-permute-done | bytes 92192 | tf_op jit(solution)/shard_map/ppermute | solution.py:290
  26.9 0.0 collective-permute-start.10
  26.9 0.5 %collective-permute-start.20 = (bf16[512,256]{1,0:T(8,128)(2,1)S(1)}, bf16[512,256]{1,0:T(8,128)(2,1)S(1)}, u32[]{:S(2)}, u32[]{:S(2)}) collective-permute-start(bf16[512,256]{1,0:T(8,128)(2,1)S(1)} %get-tuple-element.78.refs_0_), channel_id=1, source_target_pairs={{0,1},{1,0},{2,3},{3,2},{4,5},{5,4},{6,7},{7,6},{8,9},{9,8},{10,11... | collective-permute-start | bytes 786440 | tf_op jit(solution)/shard_map/ppermute | solution.py:290
  27.4 0.0 collective-permute-start.19
  27.4 0.8 %collective-permute-done.10.refs_3_ = bf16[64,720]{1,0:T(8,128)(2,1)S(1)} collective-permute-done((bf16[64,720]{1,0:T(8,128)(2,1)S(1)}, bf16[64,720]{1,0:T(8,128)(2,1)S(1)}, u32[]{:S(2)}, u32[]{:S(2)}) %collective-permute-start.10) | collective-permute-done | bytes 92192 | tf_op jit(solution)/shard_map/ppermute | solution.py:290
  28.2 1.9 %shard_map.128 = (bf16[2,64,720]{2,1,0:T(8,128)(2,1)S(1)}, bf16[64,360]{1,0:T(8,128)(2,1)S(1)}) custom-call(bf16[64,720]{1,0:T(8,128)(2,1)S(1)} %shard_map.126.refs_0_, bf16[64,720]{1,0:T(8,128)(2,1)S(1)} %collective-permute-done.8.refs_1_, bf16[64,720]{1,0:T(8,128)(2,1)S(1)} %collective-permute-done.9.refs_2_, ...), custom_call_target="tpu_custom_call" | custom-call | flops 66355200 | bytes 1036800 | tf_op jit(solution)/shard_map/pallas_call | solution.py:410
  30.0 0.2 collective-permute-start.11
  30.3 0.3 shard_map.129.kept_ref
  30.6 0.9 %collective-permute-done.11.given_ref = bf16[2,64,720]{2,1,0:T(8,128)(2,1)S(1)} collective-permute-done((bf16[2,64,720]{2,1,0:T(8,128)(2,1)S(1)}, bf16[2,64,720]{2,1,0:T(8,128)(2,1)S(1)}, u32[]{:S(2)}, u32[]{:S(2)}) %collective-permute-start.11) | collective-permute-done | bytes 184352 | tf_op jit(solution)/shard_map/ppermute | solution.py:290
  31.5 0.1 shard_map.130
  31.6 0.5 %collective-permute-start.12 = (bf16[32,720]{1,0:T(8,128)(2,1)S(1)}, bf16[32,720]{1,0:T(8,128)(2,1)S(1)}, u32[]{:S(2)}, u32[]{:S(2)}) collective-permute-start(bf16[32,720]{1,0:T(8,128)(2,1)S(1)} %get-tuple-element.68), channel_id=1, source_target_pairs={{0,3},{1,2},{2,1},{3,0},{4,7},{5,6},{6,5},{7,4},{8,11},{9,10},{10,... | collective-permute-start | bytes 138248 | tf_op jit(solution)/shard_map/ppermute | solution.py:290
  32.1 1.3 %collective-permute-start.15 = (bf16[32,720]{1,0:T(8,128)(2,1)S(1)}, bf16[32,720]{1,0:T(8,128)(2,1)S(1)}, u32[]{:S(2)}, u32[]{:S(2)}) collective-permute-start(bf16[32,720]{1,0:T(8,128)(2,1)S(1)} %get-tuple-element.72), channel_id=1, source_target_pairs={{0,3},{1,2},{2,1},{3,0},{4,7},{5,6},{6,5},{7,4},{8,11},{9,10},{10,... | collective-permute-start | bytes 138248 | tf_op jit(solution)/shard_map/ppermute | solution.py:290
  33.4 1.9 %collective-permute-done.12.refs_1_ = bf16[32,720]{1,0:T(8,128)(2,1)S(1)} collective-permute-done((bf16[32,720]{1,0:T(8,128)(2,1)S(1)}, bf16[32,720]{1,0:T(8,128)(2,1)S(1)}, u32[]{:S(2)}, u32[]{:S(2)}) %collective-permute-start.12) | collective-permute-done | bytes 46112 | tf_op jit(solution)/shard_map/ppermute | solution.py:290
  35.4 2.1 %collective-permute-start.13 = (bf16[16,720]{1,0:T(8,128)(2,1)S(1)}, bf16[16,720]{1,0:T(8,128)(2,1)S(1)}, u32[]{:S(2)}, u32[]{:S(2)}) collective-permute-start(bf16[16,720]{1,0:T(8,128)(2,1)S(1)} %get-tuple-element.69), channel_id=1, source_target_pairs={{0,13},{1,12},{2,15},{3,14},{4,9},{5,8},{6,11},{7,10},{8,5},{9,4},... | collective-permute-start | bytes 69128 | tf_op jit(solution)/shard_map/ppermute | solution.py:304
  37.5 0.3 collective-permute-start.14
  37.7 2.3 %collective-permute-start.16 = (bf16[16,720]{1,0:T(8,128)(2,1)S(1)}, bf16[16,720]{1,0:T(8,128)(2,1)S(1)}, u32[]{:S(2)}, u32[]{:S(2)}) collective-permute-start(bf16[16,720]{1,0:T(8,128)(2,1)S(1)} %get-tuple-element.73), channel_id=1, source_target_pairs={{0,5},{1,4},{2,7},{3,6},{4,1},{5,0},{6,3},{7,2},{8,13},{9,12},{10,... | collective-permute-start | bytes 69128 | tf_op jit(solution)/shard_map/ppermute | solution.py:304
  40.0 0.9 %shard_map.133.refs_6_ = bf16[720,256]{1,0:T(8,128)(2,1)S(1)} custom-call(bf16[512,256]{1,0:T(8,128)(2,1)S(1)} %get-tuple-element.78.refs_0_, bf16[512,256]{1,0:T(8,128)(2,1)S(1)} %collective-permute-done.19.refs_1_, bf16[512,256]{1,0:T(8,128)(2,1)S(1)} %collective-permute-done.20.refs_2_, bf16[512,256]{1,0:T(8,128)(2,1)S(1)} %collective-permute-done.18.refs_3_, ...), custom_call_target="tpu_custom_call" | custom-call | flops 754974720 | bytes 2949120 | tf_op jit(solution)/shard_map/pallas_call | solution.py:417
  41.0 1.5 %collective-permute-done.14.refs_1_ = bf16[16,720]{1,0:T(8,128)(2,1)S(1)} collective-permute-done((bf16[16,720]{1,0:T(8,128)(2,1)S(1)}, bf16[16,720]{1,0:T(8,128)(2,1)S(1)}, u32[]{:S(2)}, u32[]{:S(2)}) %collective-permute-start.14) | collective-permute-done | bytes 23072 | tf_op jit(solution)/shard_map/ppermute | solution.py:304
  42.5 1.0 %shard_map.134 = bf16[720,256]{1,0:T(8,128)(2,1)} custom-call(bf16[16,720]{1,0:T(8,128)(2,1)S(1)} %collective-permute-done.13.refs_0_, bf16[16,720]{1,0:T(8,128)(2,1)S(1)} %collective-permute-done.14.refs_1_, bf16[16,720]{1,0:T(8,128)(2,1)S(1)} %collective-permute-done.16.refs_2_, bf16[16,720]{1,0:T(8,128)(2,1)S(1)} %collective-permute-done.17.refs_3_, ...), custom_call_target="tpu_custom_call" | custom-call | tf_op jit(solution)/shard_map/pallas_call | solution.py:439
  (20 shorter events, 0.1 us)
Async XLA Ops:
  0.8 7.3 %collective-permute-start = (bf16[128,256]{1,0:T(8,128)(2,1)S(1)}, bf16[128,256]{1,0:T(8,128)(2,1)S(1)}, u32[]{:S(2)}, u32[]{:S(2)}) collective-permute-start(bf16[128,256]{1,0:T(8,128)(2,1)S(1)} %slice.3), channel_id=1, source_target_pairs={{0,4},{4,8},{8,12},{12,0},{1,5},{5,9},{9,13},{13,1},{2,6},{6,10},{... | collective-permute-start | bytes 196616 | tf_op jit(solution)/shard_map/ppermute | solution.py:341
  3.9 5.5 %copy-start = (bf16[1,2880,360]{1,2,0:T(8,128)(2,1)S(1)}, bf16[1,2880,360]{1,2,0:T(8,128)(2,1)}, u32[]{:S(2)}) copy-start(bf16[1,2880,360]{1,2,0:T(8,128)(2,1)} %param.21) | copy-start | bytes 6220804
  9.3 4.2 %collective-permute-start.1 = (bf16[64,512]{1,0:T(8,128)(2,1)S(1)}, bf16[64,512]{1,0:T(8,128)(2,1)S(1)}, u32[]{:S(2)}, u32[]{:S(2)}) collective-permute-start(bf16[64,512]{1,0:T(8,128)(2,1)S(1)} %get-tuple-element.49.rows_ref), channel_id=1, source_target_pairs={{0,3},{1,2},{2,1},{3,0},{4,7},{5,6},{6,5},{7,4},{8,11},{9,10},{10,... | collective-permute-start | bytes 196616 | tf_op jit(solution)/shard_map/ppermute | solution.py:290
  10.0 17.4 %collective-permute-start.18 = (bf16[512,256]{1,0:T(8,128)(2,1)S(1)}, bf16[512,256]{1,0:T(8,128)(2,1)S(1)}, u32[]{:S(2)}, u32[]{:S(2)}) collective-permute-start(bf16[512,256]{1,0:T(8,128)(2,1)S(1)} %get-tuple-element.78.refs_0_), channel_id=1, source_target_pairs={{0,3},{1,2},{2,1},{3,0},{4,7},{5,6},{6,5},{7,4},{8,11},{9,10},{10,... | collective-permute-start | bytes 786440 | tf_op jit(solution)/shard_map/ppermute | solution.py:290
  11.8 2.3 %collective-permute-start.3 = (bf16[64,512]{1,0:T(8,128)(2,1)S(1)}, bf16[64,512]{1,0:T(8,128)(2,1)S(1)}, u32[]{:S(2)}, u32[]{:S(2)}) collective-permute-start(bf16[64,512]{1,0:T(8,128)(2,1)S(1)} %get-tuple-element.49.rows_ref), channel_id=1, source_target_pairs={{0,1},{1,0},{2,3},{3,2},{4,5},{5,4},{6,7},{7,6},{8,9},{9,8},{10,11... | collective-permute-start | bytes 196616 | tf_op jit(solution)/shard_map/ppermute | solution.py:290
  13.5 1.6 %collective-permute-start.2 = (bf16[64,512]{1,0:T(8,128)(2,1)S(1)}, bf16[64,512]{1,0:T(8,128)(2,1)S(1)}, u32[]{:S(2)}, u32[]{:S(2)}) collective-permute-start(bf16[64,512]{1,0:T(8,128)(2,1)S(1)} %collective-permute-done.1.refs_1_), channel_id=1, source_target_pairs={{0,1},{1,0},{2,3},{3,2},{4,5},{5,4},{6,7},{7,6},{8,9},{9,8},{10,11... | collective-permute-start | bytes 196616 | tf_op jit(solution)/shard_map/ppermute | solution.py:290
  14.7 5.0 %copy-start.3 = (f32[2880]{0:T(1024)S(1)}, f32[2880]{0:T(1024)}, u32[]{:S(2)}) copy-start(f32[2880]{0:T(1024)} %gain_ref.1) | copy-start | bytes 34564
  14.7 5.0 %copy-start.1 = (bf16[1,2880,360]{1,2,0:T(8,128)(2,1)S(1)}, bf16[1,2880,360]{1,2,0:T(8,128)(2,1)}, u32[]{:S(2)}) copy-start(bf16[1,2880,360]{1,2,0:T(8,128)(2,1)} %param.22) | copy-start | bytes 6220804
  15.4 5.1 %collective-permute-start.4 = (bf16[16,720]{1,0:T(8,128)(2,1)S(1)}, bf16[16,720]{1,0:T(8,128)(2,1)S(1)}, u32[]{:S(2)}, u32[]{:S(2)}) collective-permute-start(bf16[16,720]{1,0:T(8,128)(2,1)S(1)} %get-tuple-element.54), channel_id=1, source_target_pairs={{0,13},{1,12},{2,15},{3,14},{4,9},{5,8},{6,11},{7,10},{8,5},{9,4},... | collective-permute-start | bytes 69128 | tf_op jit(solution)/shard_map/ppermute | solution.py:304
  17.2 4.4 %collective-permute-start.5 = (bf16[16,720]{1,0:T(8,128)(2,1)S(1)}, bf16[16,720]{1,0:T(8,128)(2,1)S(1)}, u32[]{:S(2)}, u32[]{:S(2)}) collective-permute-start(bf16[16,720]{1,0:T(8,128)(2,1)S(1)} %get-tuple-element.55), channel_id=1, source_target_pairs={{0,9},{1,8},{2,11},{3,10},{4,13},{5,12},{6,15},{7,14},{8,1},{9,0},... | collective-permute-start | bytes 69128 | tf_op jit(solution)/shard_map/ppermute | solution.py:304
  17.2 4.7 %collective-permute-start.6 = (bf16[16,720]{1,0:T(8,128)(2,1)S(1)}, bf16[16,720]{1,0:T(8,128)(2,1)S(1)}, u32[]{:S(2)}, u32[]{:S(2)}) collective-permute-start(bf16[16,720]{1,0:T(8,128)(2,1)S(1)} %get-tuple-element.56), channel_id=1, source_target_pairs={{0,5},{1,4},{2,7},{3,6},{4,1},{5,0},{6,3},{7,2},{8,13},{9,12},{10,... | collective-permute-start | bytes 69128 | tf_op jit(solution)/shard_map/ppermute | solution.py:304
  19.5 2.4 %collective-permute-start.7 = (bf16[16,720]{1,0:T(8,128)(2,1)S(1)}, bf16[16,720]{1,0:T(8,128)(2,1)S(1)}, u32[]{:S(2)}, u32[]{:S(2)}) collective-permute-start(bf16[16,720]{1,0:T(8,128)(2,1)S(1)} %get-tuple-element.57), channel_id=1, source_target_pairs={{0,1},{1,0},{2,3},{3,2},{4,5},{5,4},{6,7},{7,6},{8,9},{9,8},{10,11... | collective-permute-start | bytes 69128 | tf_op jit(solution)/shard_map/ppermute | solution.py:304
  19.8 3.0 %copy-start.2 = (bf16[1,360,2880]{2,1,0:T(8,128)(2,1)S(1)}, bf16[1,360,2880]{2,1,0:T(8,128)(2,1)}, u32[]{:S(2)}) copy-start(bf16[1,360,2880]{2,1,0:T(8,128)(2,1)} %param.23) | copy-start | bytes 6220804
  22.0 4.9 %collective-permute-start.9 = (bf16[64,720]{1,0:T(8,128)(2,1)S(1)}, bf16[64,720]{1,0:T(8,128)(2,1)S(1)}, u32[]{:S(2)}, u32[]{:S(2)}) collective-permute-start(bf16[64,720]{1,0:T(8,128)(2,1)S(1)} %shard_map.126.refs_0_), channel_id=1, source_target_pairs={{0,2},{1,3},{2,0},{3,1},{4,6},{5,7},{6,4},{7,5},{8,10},{9,11},{10,... | collective-permute-start | bytes 276488 | tf_op jit(solution)/shard_map/ppermute | solution.py:290
  22.8 4.6 %collective-permute-start.8 = (bf16[64,720]{1,0:T(8,128)(2,1)S(1)}, bf16[64,720]{1,0:T(8,128)(2,1)S(1)}, u32[]{:S(2)}, u32[]{:S(2)}) collective-permute-start(bf16[64,720]{1,0:T(8,128)(2,1)S(1)} %shard_map.126.refs_0_), channel_id=1, source_target_pairs={{0,1},{1,0},{2,3},{3,2},{4,5},{5,4},{6,7},{7,6},{8,9},{9,8},{10,11... | collective-permute-start | bytes 276488 | tf_op jit(solution)/shard_map/ppermute | solution.py:290
  26.9 1.3 %collective-permute-start.10 = (bf16[64,720]{1,0:T(8,128)(2,1)S(1)}, bf16[64,720]{1,0:T(8,128)(2,1)S(1)}, u32[]{:S(2)}, u32[]{:S(2)}) collective-permute-start(bf16[64,720]{1,0:T(8,128)(2,1)S(1)} %collective-permute-done.9.refs_2_), channel_id=1, source_target_pairs={{0,1},{1,0},{2,3},{3,2},{4,5},{5,4},{6,7},{7,6},{8,9},{9,8},{10,11... | collective-permute-start | bytes 276488 | tf_op jit(solution)/shard_map/ppermute | solution.py:290
  26.9 13.2 %collective-permute-start.20 = (bf16[512,256]{1,0:T(8,128)(2,1)S(1)}, bf16[512,256]{1,0:T(8,128)(2,1)S(1)}, u32[]{:S(2)}, u32[]{:S(2)}) collective-permute-start(bf16[512,256]{1,0:T(8,128)(2,1)S(1)} %get-tuple-element.78.refs_0_), channel_id=1, source_target_pairs={{0,1},{1,0},{2,3},{3,2},{4,5},{5,4},{6,7},{7,6},{8,9},{9,8},{10,11... | collective-permute-start | bytes 786440 | tf_op jit(solution)/shard_map/ppermute | solution.py:290
  27.4 12.7 %collective-permute-start.19 = (bf16[512,256]{1,0:T(8,128)(2,1)S(1)}, bf16[512,256]{1,0:T(8,128)(2,1)S(1)}, u32[]{:S(2)}, u32[]{:S(2)}) collective-permute-start(bf16[512,256]{1,0:T(8,128)(2,1)S(1)} %collective-permute-done.18.refs_3_), channel_id=1, source_target_pairs={{0,1},{1,0},{2,3},{3,2},{4,5},{5,4},{6,7},{7,6},{8,9},{9,8},{10,11... | collective-permute-start | bytes 786440 | tf_op jit(solution)/shard_map/ppermute | solution.py:290
  30.0 1.5 %collective-permute-start.11 = (bf16[2,64,720]{2,1,0:T(8,128)(2,1)S(1)}, bf16[2,64,720]{2,1,0:T(8,128)(2,1)S(1)}, u32[]{:S(2)}, u32[]{:S(2)}) collective-permute-start(bf16[2,64,720]{2,1,0:T(8,128)(2,1)S(1)} %get-tuple-element.66), channel_id=1, source_target_pairs={{0,1},{1,0},{2,3},{3,2},{4,5},{5,4},{6,7},{7,6},{8,9},{9,8},{10,11... | collective-permute-start | bytes 552968 | tf_op jit(solution)/shard_map/ppermute | solution.py:290
  31.6 3.8 %collective-permute-start.12 = (bf16[32,720]{1,0:T(8,128)(2,1)S(1)}, bf16[32,720]{1,0:T(8,128)(2,1)S(1)}, u32[]{:S(2)}, u32[]{:S(2)}) collective-permute-start(bf16[32,720]{1,0:T(8,128)(2,1)S(1)} %get-tuple-element.68), channel_id=1, source_target_pairs={{0,3},{1,2},{2,1},{3,0},{4,7},{5,6},{6,5},{7,4},{8,11},{9,10},{10,... | collective-permute-start | bytes 138248 | tf_op jit(solution)/shard_map/ppermute | solution.py:290
  32.1 5.6 %collective-permute-start.15 = (bf16[32,720]{1,0:T(8,128)(2,1)S(1)}, bf16[32,720]{1,0:T(8,128)(2,1)S(1)}, u32[]{:S(2)}, u32[]{:S(2)}) collective-permute-start(bf16[32,720]{1,0:T(8,128)(2,1)S(1)} %get-tuple-element.72), channel_id=1, source_target_pairs={{0,3},{1,2},{2,1},{3,0},{4,7},{5,6},{6,5},{7,4},{8,11},{9,10},{10,... | collective-permute-start | bytes 138248 | tf_op jit(solution)/shard_map/ppermute | solution.py:290
  35.4 5.6 %collective-permute-start.13 = (bf16[16,720]{1,0:T(8,128)(2,1)S(1)}, bf16[16,720]{1,0:T(8,128)(2,1)S(1)}, u32[]{:S(2)}, u32[]{:S(2)}) collective-permute-start(bf16[16,720]{1,0:T(8,128)(2,1)S(1)} %get-tuple-element.69), channel_id=1, source_target_pairs={{0,13},{1,12},{2,15},{3,14},{4,9},{5,8},{6,11},{7,10},{8,5},{9,4},... | collective-permute-start | bytes 69128 | tf_op jit(solution)/shard_map/ppermute | solution.py:304
  37.5 5.1 %collective-permute-start.14 = (bf16[16,720]{1,0:T(8,128)(2,1)S(1)}, bf16[16,720]{1,0:T(8,128)(2,1)S(1)}, u32[]{:S(2)}, u32[]{:S(2)}) collective-permute-start(bf16[16,720]{1,0:T(8,128)(2,1)S(1)} %get-tuple-element.70), channel_id=1, source_target_pairs={{0,9},{1,8},{2,11},{3,10},{4,13},{5,12},{6,15},{7,14},{8,1},{9,0},... | collective-permute-start | bytes 69128 | tf_op jit(solution)/shard_map/ppermute | solution.py:304
  37.7 4.8 %collective-permute-start.16 = (bf16[16,720]{1,0:T(8,128)(2,1)S(1)}, bf16[16,720]{1,0:T(8,128)(2,1)S(1)}, u32[]{:S(2)}, u32[]{:S(2)}) collective-permute-start(bf16[16,720]{1,0:T(8,128)(2,1)S(1)} %get-tuple-element.73), channel_id=1, source_target_pairs={{0,5},{1,4},{2,7},{3,6},{4,1},{5,0},{6,3},{7,2},{8,13},{9,12},{10,... | collective-permute-start | bytes 69128 | tf_op jit(solution)/shard_map/ppermute | solution.py:304
  40.0 2.5 %collective-permute-start.17 = (bf16[16,720]{1,0:T(8,128)(2,1)S(1)}, bf16[16,720]{1,0:T(8,128)(2,1)S(1)}, u32[]{:S(2)}, u32[]{:S(2)}) collective-permute-start(bf16[16,720]{1,0:T(8,128)(2,1)S(1)} %get-tuple-element.74), channel_id=1, source_target_pairs={{0,1},{1,0},{2,3},{3,2},{4,5},{5,4},{6,7},{7,6},{8,9},{9,8},{10,11... | collective-permute-start | bytes 69128 | tf_op jit(solution)/shard_map/ppermute | solution.py:304

commit v16 on v15

--- a/solution.py
+++ b/solution.py
@@ -229,18 +229,37 @@
         blocks_ref[p] = gain[:, p * width : (p + 1) * width]
 
 
-def expert_kernel(places, steps, *refs):
-    blocks = refs[: 2 * steps]
-    gains_ref, gates_ref, ups_ref, downs_ref, given_ref, activated_ref = refs[2 * steps :]
-    wide = [block[...].astype(jnp.float32) for block in blocks]
+def squares_kernel(mine_ref, theirs_ref, squares_ref):
+    wide = [ref[...].astype(jnp.float32) for ref in (mine_ref, theirs_ref)]
     squares = sum(jnp.sum(block * block, axis=1, keepdims=True) for block in wide)
-    scale = lax.rsqrt(squares / (len(blocks) * wide[0].shape[1]) + norm_eps)
-    gate, up = 0.0, 0.0
-    for i, block in zip(places, wide):
+    squares_ref[...] = jnp.broadcast_to(squares, squares_ref.shape)
+
+
+def add_features(gate, up, scale, places, blocks, gains_ref, gates_ref, ups_ref, steps):
+    for i, block in zip(places, blocks):
         p = origin(i % steps, i >= steps)
-        rows = (block * scale * gains_ref[p]).astype(jnp.bfloat16)
+        rows = (block[...].astype(jnp.float32) * scale * gains_ref[p]).astype(jnp.bfloat16)
         gate += dot(rows, gates_ref[p], NT)
         up += dot(rows, ups_ref[p], NT)
+    return gate, up
+
+
+def expert_most_kernel(places, steps, *refs):
+    blocks, squares = refs[: steps + 1], refs[steps + 1 : 2 * steps + 1]
+    gains_ref, gates_ref, ups_ref, gate_ref, up_ref, scale_ref = refs[2 * steps + 1 :]
+    features = 2 * steps * blocks[0].shape[1]
+    scale = lax.rsqrt(sum(ref[...] for ref in squares) / features + norm_eps)
+    scale_ref[...] = scale
+    sums = add_features(0.0, 0.0, scale[:, :1], places, blocks, gains_ref, gates_ref, ups_ref, steps)
+    gate_ref[...], up_ref[...] = sums
+
+
+def expert_last_kernel(steps, *refs):
+    blocks, refs = refs[: steps - 1], refs[steps - 1 :]
+    gate_ref, up_ref, scale_ref, gains_ref, gates_ref, ups_ref, downs_ref, given_ref, activated_ref = refs
+    gate, up = add_features(
+        gate_ref[...], up_ref[...], scale_ref[:, :1], range(1, steps), blocks, gains_ref, gates_ref, ups_ref, steps
+    )
     activated = ((up + 1.0) * gate * jax.nn.sigmoid(glu_alpha * gate)).astype(jnp.bfloat16)
     activated_ref[...] = activated
     for k in range(steps):
@@ -405,14 +424,24 @@
     chip_blocks = from_chips(after(attended, gates))
     sibling_block, *relayed_blocks = [from_sibling(b) for b in (attended, *chip_blocks)]
     blocks = [attended, *relayed_blocks, sibling_block, *chip_blocks]
-    chip_rows = after(chip_rows, downs)
+    row_sums = jax.ShapeDtypeStruct((slots, KEYS_SEEN), jnp.float32)
+    squares = call(squares_kernel, row_sums, n_in=2)(stacked, sibling_rows)
+    chip_squares = from_chips(squares)
+    chip_rows = after(chip_rows, (downs, chip_squares))
     relayed_rows = [from_sibling(b) for b in chip_rows]
+    sums = jax.ShapeDtypeStruct((slots, hidden), jnp.float32)
+    most = call(
+        functools.partial(expert_most_kernel, [steps, 0, *range(steps + 1, 2 * steps)], steps),
+        (sums, sums, row_sums),
+        n_in=2 * steps + 4,
+        **part,
+    )(stacked, sibling_rows, *chip_rows, squares, *chip_squares, gains, gates, ups)
     given, activated = call(
-        functools.partial(expert_kernel, [steps, 0, *range(steps + 1, 2 * steps), *range(1, steps)], steps),
+        functools.partial(expert_last_kernel, steps),
         (bf16(steps, slots, feats), bf16(slots, hidden)),
-        n_in=cuts + 4,
+        n_in=steps + 6,
         **part,
-    )(stacked, sibling_rows, *chip_rows, *relayed_rows, gains, gates, ups, downs)
+    )(*relayed_rows, *most, gains, gates, ups, downs)
     kept = call(expert_kept_kernel, bf16(steps, slots, feats), n_in=2, **part)(activated, downs)
     resid = call(
         functools.partial(project_kernel, steps),

time: 43.7 us -> 43.4 us (level)
  waiting for transfers between devices: 13.6 us -> 11 us
  starting transfers between devices: 18 us -> 20.1 us
    ppermute x12 -> x13, starting transfers between devices: 6.04 us -> 7.94 us  [swap(): lax.ppermute(block, axis, [(i, i ^ mask) for i in range(lax.axis_size(axi...]
    ppermute x12 -> x13, waiting for transfers between devices: 8.58 us -> 7.03 us  [swap(): lax.ppermute(block, axis, [(i, i ^ mask) for i in range(lax.axis_size(axi...]
    ppermute x8, waiting for transfers between devices: 3.14 us -> 2.09 us  [to_seq(): lax.ppermute(block, ('seq', 'cuts'), [(i, i ^ mask) for i in range(size)])]
    pallas_call x1 -> x3, Pallas kernels: 1.86 us -> 2.04 us  [the longest x1 1.14 us: shards(): call(functools.partial(expert_most_kernel, [steps, 0, *range(steps + 1, 2...]
  transfers between devices with their start and end apart: 21 -> 22, of which waited for: 11 -> 9; matrix products, arithmetic and copies ran while one was open for 0% -> 0% of each run, Pallas kernels for 20% -> 21%
where the time goes in v16:
time: 43.4 us; the launch traced here: 43.3 us
  starting transfers between devices  20.1 us (46%)
  Pallas kernels  11.1 us (26%)
  waiting for transfers between devices  11 us (25%)
  local copies, waits for them, and re-layouts  0.86 us (2%)
    ppermute x8, starting transfers between devices, to_seq(): lax.ppermute(block, ('seq', 'cuts'), [(i, i ^ mask) for i in range(size)])  9.14 us
    ppermute x13, starting transfers between devices, swap(): lax.ppermute(block, axis, [(i, i ^ mask) for i in range(lax.axis_size(axi...  7.94 us
    ppermute x13, waiting for transfers between devices, swap(): lax.ppermute(block, axis, [(i, i ^ mask) for i in range(lax.axis_size(axi...  7.03 us
    ppermute x1, starting transfers between devices, shards(): rim = lax.ppermute(tail, 'seq', [(i, (i + 1) % size) for i in range(size)])  3.02 us
    pallas_call x1, Pallas kernels, shards(): call(functools.partial(first_kernel, live), (*(bf16(*a.shape) for a in lo...  2.37 us
    ppermute x8, waiting for transfers between devices, to_seq(): lax.ppermute(block, ('seq', 'cuts'), [(i, i ^ mask) for i in range(size)])  2.09 us
    ppermute x1, waiting for transfers between devices, shards(): rim = lax.ppermute(tail, 'seq', [(i, (i + 1) % size) for i in range(size)])  1.89 us
    pallas_call x1, Pallas kernels, shards(): call(second_kernel, (bf16(head_rows, toks), bf16(slots, head_rows)), n_in...  1.14 us
  transfers between devices with their start and end apart: 22, of which 9 were waited for; matrix products, arithmetic and copies ran while one was open for 0% of the time, Pallas kernels for 21%

profile of v16, /device:TPU:0, one launch (start us, length us, event | category | flops | bytes accessed | tf_op | source)
XLA Modules:
  0.0 43.3 jit_solution(13232804262348951262)
XLA Ops:
  0.0 0.8 %slice.3 = bf16[128,256]{1,0:T(8,128)(2,1)S(1)} slice(bf16[256,256]{1,0:T(8,128)(2,1)} %refs_4_.1), slice={[128:256], [0:256]} | slice | bytes 131072 | tf_op jit(solution)/shard_map/slice | solution.py:359
  0.8 3.0 %collective-permute-start = (bf16[128,256]{1,0:T(8,128)(2,1)S(1)}, bf16[128,256]{1,0:T(8,128)(2,1)S(1)}, u32[]{:S(2)}, u32[]{:S(2)}) collective-permute-start(bf16[128,256]{1,0:T(8,128)(2,1)S(1)} %slice.3), channel_id=1, source_target_pairs={{0,4},{4,8},{8,12},{12,0},{1,5},{5,9},{9,13},{13,1},{2,6},{6,10},{... | collective-permute-start | bytes 196616 | tf_op jit(solution)/shard_map/ppermute | solution.py:360
  3.9 2.4 %shard_map.118 = (bf16[256,512]{1,0:T(8,128)(2,1)S(1)}, bf16[256,256]{1,0:T(8,128)(2,1)S(1)}, bf16[128,256]{1,0:T(8,128)(2,1)S(1)}, bf16[720,2048]{1,0:T(8,128)(...) custom-call(s32[4,256]{1,0:T(4,128)} %bitcast.17, ...), custom_call_target="tpu_custom_call" | custom-call | flops 134217728 | bytes 3579904 | tf_op jit(solution)/shard_map/pallas_call | solution.py:362
  6.2 1.9 %collective-permute-done.rim_ref = bf16[128,256]{1,0:T(8,128)(2,1)S(1)} collective-permute-done((bf16[128,256]{1,0:T(8,128)(2,1)S(1)}, bf16[128,256]{1,0:T(8,128)(2,1)S(1)}, u32[]{:S(2)}, u32[]{:S(2)}) %collective-permute-start) | collective-permute-done | bytes 65568 | tf_op jit(solution)/shard_map/ppermute | solution.py:360
  8.1 1.1 %shard_map.119 = (bf16[512,256]{1,0:T(8,128)(2,1)S(1)}, bf16[64,512]{1,0:T(8,128)(2,1)S(1)}) custom-call(bf16[256,512]{1,0:T(8,128)(2,1)S(1)} %get-tuple-element.45.q_ref, bf16[256,256]{1,0:T(8,128)(2,1)S(1)} %get-tuple-element.46.kv_ref, bf16[128,256]{1,0:T(8,128)(2,1)S(1)} %get-tuple-element.47.before_ref, ...), custom_call_target="tpu_custom_call" | custom-call | flops 67108864 | bytes 262144 | tf_op jit(solution)/shard_map/pallas_call | solution.py:382
  9.3 0.1 collective-permute-start.1
  9.4 1.8 %collective-permute-start.3 = (bf16[64,512]{1,0:T(8,128)(2,1)S(1)}, bf16[64,512]{1,0:T(8,128)(2,1)S(1)}, u32[]{:S(2)}, u32[]{:S(2)}) collective-permute-start(bf16[64,512]{1,0:T(8,128)(2,1)S(1)} %get-tuple-element.52.rows_ref), channel_id=1, source_target_pairs={{0,1},{1,0},{2,3},{3,2},{4,5},{5,4},{6,7},{7,6},{8,9},{9,8},{10,11... | collective-permute-start | bytes 196616 | tf_op jit(solution)/shard_map/ppermute | solution.py:309
  11.2 0.6 %shard_map.121.refs_6_.refs_5_ = bf16[4,360,720]{2,1,0:T(8,128)(2,1)S(1)} custom-call(bf16[360,2880]{1,0:T(8,128)(2,1)S(1)} %bitcast.12), custom_call_target="tpu_custom_call" | custom-call | bytes 4147200 | tf_op jit(solution)/shard_map/pallas_call | solution.py:401
  11.8 0.5 %shard_map.120.refs_2_ = f32[64,720]{1,0:T(8,128)S(1)} custom-call(bf16[64,512]{1,0:T(8,128)(2,1)S(1)} %get-tuple-element.52.rows_ref, bf16[720,2048]{1,0:T(8,128)(2,1)S(1)} %get-tuple-element.53.w_ref.refs_3_.refs_2_.refs_4_, bf16[720,256]{1,0:T(8,128)(2,1)S(1)} %get-tuple-element.54.residual_ref.refs_5_, bf16[64,256]{1,0:T(8,128)(2,1)S(1)} %get-tuple-element.50.placing_ref), custom_call_target="tpu_custom_call" | custom-call | flops 47185920 | bytes 737280 | tf_op jit(solution)/shard_map/pallas_call | solution.py:393
  12.2 1.2 %collective-permute-done.1.refs_1_ = bf16[64,512]{1,0:T(8,128)(2,1)S(1)} collective-permute-done((bf16[64,512]{1,0:T(8,128)(2,1)S(1)}, bf16[64,512]{1,0:T(8,128)(2,1)S(1)}, u32[]{:S(2)}, u32[]{:S(2)}) %collective-permute-start.1) | collective-permute-done | bytes 65568 | tf_op jit(solution)/shard_map/ppermute | solution.py:309
  13.5 0.1 collective-permute-start.2
  13.6 1.3 %collective-permute-start.19 = (bf16[512,256]{1,0:T(8,128)(2,1)S(1)}, bf16[512,256]{1,0:T(8,128)(2,1)S(1)}, u32[]{:S(2)}, u32[]{:S(2)}) collective-permute-start(bf16[512,256]{1,0:T(8,128)(2,1)S(1)} %get-tuple-element.84.refs_0_), channel_id=1, source_target_pairs={{0,3},{1,2},{2,1},{3,0},{4,7},{5,6},{6,5},{7,4},{8,11},{9,10},{10,... | collective-permute-start | bytes 786440 | tf_op jit(solution)/shard_map/ppermute | solution.py:309
  14.9 0.6 %shard_map.122.refs_1_ = f32[64,720]{1,0:T(8,128)S(1)} custom-call(bf16[64,512]{1,0:T(8,128)(2,1)S(1)} %collective-permute-done.3.refs_0_, bf16[64,512]{1,0:T(8,128)(2,1)S(1)} %collective-permute-done.1.refs_1_, f32[64,720]{1,0:T(8,128)S(1)} %shard_map.120.refs_2_, bf16[720,2048]{1,0:T(8,128)(2,1)S(1)} %get-tuple-element.53.w_ref.refs_3_.refs_2_.refs_4_), custom_call_target="tpu_custom_call" | custom-call | flops 47185920 | bytes 737280 | tf_op jit(solution)/shard_map/pallas_call | solution.py:404
  15.4 0.0 copy-start.3
  15.5 0.4 shard_map.123
  15.8 1.5 %collective-permute-start.4 = (bf16[16,720]{1,0:T(8,128)(2,1)S(1)}, bf16[16,720]{1,0:T(8,128)(2,1)S(1)}, u32[]{:S(2)}, u32[]{:S(2)}) collective-permute-start(bf16[16,720]{1,0:T(8,128)(2,1)S(1)} %get-tuple-element.57), channel_id=1, source_target_pairs={{0,13},{1,12},{2,15},{3,14},{4,9},{5,8},{6,11},{7,10},{8,5},{9,4},... | collective-permute-start | bytes 69128 | tf_op jit(solution)/shard_map/ppermute | solution.py:323
  17.3 2.3 %collective-permute-start.6 = (bf16[16,720]{1,0:T(8,128)(2,1)S(1)}, bf16[16,720]{1,0:T(8,128)(2,1)S(1)}, u32[]{:S(2)}, u32[]{:S(2)}) collective-permute-start(bf16[16,720]{1,0:T(8,128)(2,1)S(1)} %get-tuple-element.59), channel_id=1, source_target_pairs={{0,5},{1,4},{2,7},{3,6},{4,1},{5,0},{6,3},{7,2},{8,13},{9,12},{10,... | collective-permute-start | bytes 69128 | tf_op jit(solution)/shard_map/ppermute | solution.py:323
  19.6 0.5 %collective-permute-start.7 = (bf16[16,720]{1,0:T(8,128)(2,1)S(1)}, bf16[16,720]{1,0:T(8,128)(2,1)S(1)}, u32[]{:S(2)}, u32[]{:S(2)}) collective-permute-start(bf16[16,720]{1,0:T(8,128)(2,1)S(1)} %get-tuple-element.60), channel_id=1, source_target_pairs={{0,1},{1,0},{2,3},{3,2},{4,5},{5,4},{6,7},{7,6},{8,9},{9,8},{10,11... | collective-permute-start | bytes 69128 | tf_op jit(solution)/shard_map/ppermute | solution.py:323
  20.1 0.1 shard_map.125.refs_5_.refs_4_
  20.2 0.6 %shard_map.124.refs_7_.refs_6_ = bf16[4,360,720]{2,1,0:T(8,128)(2,1)S(1)} custom-call(bf16[360,2880]{1,0:T(8,128)(2,1)S(1)} %bitcast.13), custom_call_target="tpu_custom_call" | custom-call | bytes 4147200 | tf_op jit(solution)/shard_map/pallas_call | solution.py:417
  20.8 0.2 collective-permute-done.4.refs_0_
  21.1 1.1 %collective-permute-done.5.refs_1_ = bf16[16,720]{1,0:T(8,128)(2,1)S(1)} collective-permute-done((bf16[16,720]{1,0:T(8,128)(2,1)S(1)}, bf16[16,720]{1,0:T(8,128)(2,1)S(1)}, u32[]{:S(2)}, u32[]{:S(2)}) %collective-permute-start.5) | collective-permute-done | bytes 23072 | tf_op jit(solution)/shard_map/ppermute | solution.py:323
  22.2 0.1 collective-permute-start.9
  22.3 0.9 %collective-permute-start.8 = (bf16[64,720]{1,0:T(8,128)(2,1)S(1)}, bf16[64,720]{1,0:T(8,128)(2,1)S(1)}, u32[]{:S(2)}, u32[]{:S(2)}) collective-permute-start(bf16[64,720]{1,0:T(8,128)(2,1)S(1)} %shard_map.126.mine_ref.refs_0_), channel_id=1, source_target_pairs={{0,2},{1,3},{2,0},{3,1},{4,6},{5,7},{6,4},{7,5},{8,10},{9,11},{10,... | collective-permute-start | bytes 276488 | tf_op jit(solution)/shard_map/ppermute | solution.py:309
  23.3 0.3 collective-permute-done.9.theirs_ref.refs_1_
  23.5 0.1 shard_map.128.refs_3_
  23.7 0.7 %collective-permute-start.10 = (f32[64,128]{1,0:T(8,128)S(1)}, f32[64,128]{1,0:T(8,128)S(1)}, u32[]{:S(2)}, u32[]{:S(2)}) collective-permute-start(f32[64,128]{1,0:T(8,128)S(1)} %shard_map.128.refs_3_), channel_id=1, source_target_pairs={{0,3},{1,2},{2,1},{3,0},{4,7},{5,6},{6,5},{7,4},{8,11},{9,10},{10,... | collective-permute-start | bytes 98312 | tf_op jit(solution)/shard_map/ppermute | solution.py:309
  24.4 0.6 %shard_map.127.refs_7_.downs_ref = bf16[4,360,720]{2,1,0:T(8,128)(2,1)S(1)} custom-call(bf16[360,2880]{1,0:T(8,128)(2,1)S(1)} %bitcast.14), custom_call_target="tpu_custom_call" | custom-call | bytes 4147200 | tf_op jit(solution)/shard_map/pallas_call | solution.py:423
  25.0 2.9 %collective-permute-done.8.refs_2_ = bf16[64,720]{1,0:T(8,128)(2,1)S(1)} collective-permute-done((bf16[64,720]{1,0:T(8,128)(2,1)S(1)}, bf16[64,720]{1,0:T(8,128)(2,1)S(1)}, u32[]{:S(2)}, u32[]{:S(2)}) %collective-permute-start.8) | collective-permute-done | bytes 92192 | tf_op jit(solution)/shard_map/ppermute | solution.py:309
  27.8 0.2 collective-permute-start.11
  28.0 0.3 collective-permute-start.21
  28.3 0.2 collective-permute-start.20
  28.5 1.1 %shard_map.129 = (f32[64,360]{1,0:T(8,128)S(1)}, f32[64,360]{1,0:T(8,128)S(1)}, f32[64,128]{1,0:T(8,128)S(1)}) custom-call(bf16[64,720]{1,0:T(8,128)(2,1)S(1)} %shard_map.126.mine_ref.refs_0_, bf16[64,720]{1,0:T(8,128)(2,1)S(1)} %collective-permute-done.9.theirs_ref.refs_1_, bf16[64,720]{1,0:T(8,128)(2,1)S(1)} %collective-permute-done.8.refs_2_, ...), custom_call_target="tpu_custom_call" | custom-call | flops 66355200 | bytes 1036800 | tf_op jit(solution)/shard_map/pallas_call | solution.py:433
  29.6 0.0 collective-permute-done.11.refs_0_
  29.7 0.8 %shard_map.130 = (bf16[2,64,720]{2,1,0:T(8,128)(2,1)S(1)}, bf16[64,360]{1,0:T(8,128)(2,1)S(1)}) custom-call(bf16[64,720]{1,0:T(8,128)(2,1)S(1)} %collective-permute-done.11.refs_0_, f32[64,360]{1,0:T(8,128)S(1)} %get-tuple-element.68.refs_1_, f32[64,360]{1,0:T(8,128)S(1)} %get-tuple-element.69.refs_2_, f32[64,128]{1,0:T(8,128)S(1)} %get-tuple-element.70.refs_3_, ...), custom_call_target="tpu_custom_call" | custom-call | flops 66355200 | bytes 1036800 | tf_op jit(solution)/shard_map/pallas_call | solution.py:439
  30.5 0.4 collective-permute-start.12
  30.9 0.3 shard_map.131.kept_ref
  31.2 0.8 %collective-permute-done.12.given_ref = bf16[2,64,720]{2,1,0:T(8,128)(2,1)S(1)} collective-permute-done((bf16[2,64,720]{2,1,0:T(8,128)(2,1)S(1)}, bf16[2,64,720]{2,1,0:T(8,128)(2,1)S(1)}, u32[]{:S(2)}, u32[]{:S(2)}) %collective-permute-start.12) | collective-permute-done | bytes 184352 | tf_op jit(solution)/shard_map/ppermute | solution.py:309
  32.0 0.7 %collective-permute-start.13 = (bf16[32,720]{1,0:T(8,128)(2,1)S(1)}, bf16[32,720]{1,0:T(8,128)(2,1)S(1)}, u32[]{:S(2)}, u32[]{:S(2)}) collective-permute-start(bf16[32,720]{1,0:T(8,128)(2,1)S(1)} %get-tuple-element.74), channel_id=1, source_target_pairs={{0,3},{1,2},{2,1},{3,0},{4,7},{5,6},{6,5},{7,4},{8,11},{9,10},{10,... | collective-permute-start | bytes 138248 | tf_op jit(solution)/shard_map/ppermute | solution.py:309
  32.7 1.1 %collective-permute-start.16 = (bf16[32,720]{1,0:T(8,128)(2,1)S(1)}, bf16[32,720]{1,0:T(8,128)(2,1)S(1)}, u32[]{:S(2)}, u32[]{:S(2)}) collective-permute-start(bf16[32,720]{1,0:T(8,128)(2,1)S(1)} %get-tuple-element.78), channel_id=1, source_target_pairs={{0,3},{1,2},{2,1},{3,0},{4,7},{5,6},{6,5},{7,4},{8,11},{9,10},{10,... | collective-permute-start | bytes 138248 | tf_op jit(solution)/shard_map/ppermute | solution.py:309
  33.8 1.8 %collective-permute-done.13.refs_1_ = bf16[32,720]{1,0:T(8,128)(2,1)S(1)} collective-permute-done((bf16[32,720]{1,0:T(8,128)(2,1)S(1)}, bf16[32,720]{1,0:T(8,128)(2,1)S(1)}, u32[]{:S(2)}, u32[]{:S(2)}) %collective-permute-start.13) | collective-permute-done | bytes 46112 | tf_op jit(solution)/shard_map/ppermute | solution.py:309
  35.7 1.6 %collective-permute-start.14 = (bf16[16,720]{1,0:T(8,128)(2,1)S(1)}, bf16[16,720]{1,0:T(8,128)(2,1)S(1)}, u32[]{:S(2)}, u32[]{:S(2)}) collective-permute-start(bf16[16,720]{1,0:T(8,128)(2,1)S(1)} %get-tuple-element.75), channel_id=1, source_target_pairs={{0,13},{1,12},{2,15},{3,14},{4,9},{5,8},{6,11},{7,10},{8,5},{9,4},... | collective-permute-start | bytes 69128 | tf_op jit(solution)/shard_map/ppermute | solution.py:323
  37.3 0.8 %collective-permute-start.15 = (bf16[16,720]{1,0:T(8,128)(2,1)S(1)}, bf16[16,720]{1,0:T(8,128)(2,1)S(1)}, u32[]{:S(2)}, u32[]{:S(2)}) collective-permute-start(bf16[16,720]{1,0:T(8,128)(2,1)S(1)} %get-tuple-element.76), channel_id=1, source_target_pairs={{0,9},{1,8},{2,11},{3,10},{4,13},{5,12},{6,15},{7,14},{8,1},{9,0},... | collective-permute-start | bytes 69128 | tf_op jit(solution)/shard_map/ppermute | solution.py:323
  38.1 2.4 %collective-permute-start.17 = (bf16[16,720]{1,0:T(8,128)(2,1)S(1)}, bf16[16,720]{1,0:T(8,128)(2,1)S(1)}, u32[]{:S(2)}, u32[]{:S(2)}) collective-permute-start(bf16[16,720]{1,0:T(8,128)(2,1)S(1)} %get-tuple-element.79), channel_id=1, source_target_pairs={{0,5},{1,4},{2,7},{3,6},{4,1},{5,0},{6,3},{7,2},{8,13},{9,12},{10,... | collective-permute-start | bytes 69128 | tf_op jit(solution)/shard_map/ppermute | solution.py:323
  40.6 0.9 %shard_map.135.refs_6_ = bf16[720,256]{1,0:T(8,128)(2,1)S(1)} custom-call(bf16[512,256]{1,0:T(8,128)(2,1)S(1)} %get-tuple-element.84.refs_0_, bf16[512,256]{1,0:T(8,128)(2,1)S(1)} %collective-permute-done.20.refs_1_, bf16[512,256]{1,0:T(8,128)(2,1)S(1)} %collective-permute-done.21.refs_2_, bf16[512,256]{1,0:T(8,128)(2,1)S(1)} %collective-permute-done.19.refs_3_, ...), custom_call_target="tpu_custom_call" | custom-call | flops 754974720 | bytes 2949120 | tf_op jit(solution)/shard_map/pallas_call | solution.py:446
  41.5 0.0 collective-permute-done.15.refs_1_
  41.6 0.7 %collective-permute-done.17.refs_2_ = bf16[16,720]{1,0:T(8,128)(2,1)S(1)} collective-permute-done((bf16[16,720]{1,0:T(8,128)(2,1)S(1)}, bf16[16,720]{1,0:T(8,128)(2,1)S(1)}, u32[]{:S(2)}, u32[]{:S(2)}) %collective-permute-start.17) | collective-permute-done | bytes 23072 | tf_op jit(solution)/shard_map/ppermute | solution.py:323
  42.3 1.0 %shard_map.136 = bf16[720,256]{1,0:T(8,128)(2,1)} custom-call(bf16[16,720]{1,0:T(8,128)(2,1)S(1)} %collective-permute-done.14.refs_0_, bf16[16,720]{1,0:T(8,128)(2,1)S(1)} %collective-permute-done.15.refs_1_, bf16[16,720]{1,0:T(8,128)(2,1)S(1)} %collective-permute-done.17.refs_2_, bf16[16,720]{1,0:T(8,128)(2,1)S(1)} %collective-permute-done.18.refs_3_, ...), custom_call_target="tpu_custom_call" | custom-call | tf_op jit(solution)/shard_map/pallas_call | solution.py:468
  (24 shorter events, 0.1 us)
Async XLA Ops:
  0.8 7.3 %collective-permute-start = (bf16[128,256]{1,0:T(8,128)(2,1)S(1)}, bf16[128,256]{1,0:T(8,128)(2,1)S(1)}, u32[]{:S(2)}, u32[]{:S(2)}) collective-permute-start(bf16[128,256]{1,0:T(8,128)(2,1)S(1)} %slice.3), channel_id=1, source_target_pairs={{0,4},{4,8},{8,12},{12,0},{1,5},{5,9},{9,13},{13,1},{2,6},{6,10},{... | collective-permute-start | bytes 196616 | tf_op jit(solution)/shard_map/ppermute | solution.py:360
  3.9 7.3 %copy-start = (bf16[1,2880,360]{1,2,0:T(8,128)(2,1)S(1)}, bf16[1,2880,360]{1,2,0:T(8,128)(2,1)}, u32[]{:S(2)}) copy-start(bf16[1,2880,360]{1,2,0:T(8,128)(2,1)} %param.21) | copy-start | bytes 6220804
  9.3 4.2 %collective-permute-start.1 = (bf16[64,512]{1,0:T(8,128)(2,1)S(1)}, bf16[64,512]{1,0:T(8,128)(2,1)S(1)}, u32[]{:S(2)}, u32[]{:S(2)}) collective-permute-start(bf16[64,512]{1,0:T(8,128)(2,1)S(1)} %get-tuple-element.52.rows_ref), channel_id=1, source_target_pairs={{0,3},{1,2},{2,1},{3,0},{4,7},{5,6},{6,5},{7,4},{8,11},{9,10},{10,... | collective-permute-start | bytes 196616 | tf_op jit(solution)/shard_map/ppermute | solution.py:309
  9.4 5.5 %collective-permute-start.3 = (bf16[64,512]{1,0:T(8,128)(2,1)S(1)}, bf16[64,512]{1,0:T(8,128)(2,1)S(1)}, u32[]{:S(2)}, u32[]{:S(2)}) collective-permute-start(bf16[64,512]{1,0:T(8,128)(2,1)S(1)} %get-tuple-element.52.rows_ref), channel_id=1, source_target_pairs={{0,1},{1,0},{2,3},{3,2},{4,5},{5,4},{6,7},{7,6},{8,9},{9,8},{10,11... | collective-permute-start | bytes 196616 | tf_op jit(solution)/shard_map/ppermute | solution.py:309
  13.5 2.0 %collective-permute-start.2 = (bf16[64,512]{1,0:T(8,128)(2,1)S(1)}, bf16[64,512]{1,0:T(8,128)(2,1)S(1)}, u32[]{:S(2)}, u32[]{:S(2)}) collective-permute-start(bf16[64,512]{1,0:T(8,128)(2,1)S(1)} %collective-permute-done.1.refs_1_), channel_id=1, source_target_pairs={{0,1},{1,0},{2,3},{3,2},{4,5},{5,4},{6,7},{7,6},{8,9},{9,8},{10,11... | collective-permute-start | bytes 196616 | tf_op jit(solution)/shard_map/ppermute | solution.py:309
  13.6 14.7 %collective-permute-start.19 = (bf16[512,256]{1,0:T(8,128)(2,1)S(1)}, bf16[512,256]{1,0:T(8,128)(2,1)S(1)}, u32[]{:S(2)}, u32[]{:S(2)}) collective-permute-start(bf16[512,256]{1,0:T(8,128)(2,1)S(1)} %get-tuple-element.84.refs_0_), channel_id=1, source_target_pairs={{0,3},{1,2},{2,1},{3,0},{4,7},{5,6},{6,5},{7,4},{8,11},{9,10},{10,... | collective-permute-start | bytes 786440 | tf_op jit(solution)/shard_map/ppermute | solution.py:309
  15.4 4.7 %copy-start.3 = (f32[2880]{0:T(1024)S(1)}, f32[2880]{0:T(1024)}, u32[]{:S(2)}) copy-start(f32[2880]{0:T(1024)} %gain_ref.1) | copy-start | bytes 34564
  15.4 4.8 %copy-start.1 = (bf16[1,2880,360]{1,2,0:T(8,128)(2,1)S(1)}, bf16[1,2880,360]{1,2,0:T(8,128)(2,1)}, u32[]{:S(2)}) copy-start(bf16[1,2880,360]{1,2,0:T(8,128)(2,1)} %param.22) | copy-start | bytes 6220804
  15.8 5.2 %collective-permute-start.4 = (bf16[16,720]{1,0:T(8,128)(2,1)S(1)}, bf16[16,720]{1,0:T(8,128)(2,1)S(1)}, u32[]{:S(2)}, u32[]{:S(2)}) collective-permute-start(bf16[16,720]{1,0:T(8,128)(2,1)S(1)} %get-tuple-element.57), channel_id=1, source_target_pairs={{0,13},{1,12},{2,15},{3,14},{4,9},{5,8},{6,11},{7,10},{8,5},{9,4},... | collective-permute-start | bytes 69128 | tf_op jit(solution)/shard_map/ppermute | solution.py:323
  17.3 4.8 %collective-permute-start.5 = (bf16[16,720]{1,0:T(8,128)(2,1)S(1)}, bf16[16,720]{1,0:T(8,128)(2,1)S(1)}, u32[]{:S(2)}, u32[]{:S(2)}) collective-permute-start(bf16[16,720]{1,0:T(8,128)(2,1)S(1)} %get-tuple-element.58), channel_id=1, source_target_pairs={{0,9},{1,8},{2,11},{3,10},{4,13},{5,12},{6,15},{7,14},{8,1},{9,0},... | collective-permute-start | bytes 69128 | tf_op jit(solution)/shard_map/ppermute | solution.py:323
  17.3 4.8 %collective-permute-start.6 = (bf16[16,720]{1,0:T(8,128)(2,1)S(1)}, bf16[16,720]{1,0:T(8,128)(2,1)S(1)}, u32[]{:S(2)}, u32[]{:S(2)}) collective-permute-start(bf16[16,720]{1,0:T(8,128)(2,1)S(1)} %get-tuple-element.59), channel_id=1, source_target_pairs={{0,5},{1,4},{2,7},{3,6},{4,1},{5,0},{6,3},{7,2},{8,13},{9,12},{10,... | collective-permute-start | bytes 69128 | tf_op jit(solution)/shard_map/ppermute | solution.py:323
  19.6 2.5 %collective-permute-start.7 = (bf16[16,720]{1,0:T(8,128)(2,1)S(1)}, bf16[16,720]{1,0:T(8,128)(2,1)S(1)}, u32[]{:S(2)}, u32[]{:S(2)}) collective-permute-start(bf16[16,720]{1,0:T(8,128)(2,1)S(1)} %get-tuple-element.60), channel_id=1, source_target_pairs={{0,1},{1,0},{2,3},{3,2},{4,5},{5,4},{6,7},{7,6},{8,9},{9,8},{10,11... | collective-permute-start | bytes 69128 | tf_op jit(solution)/shard_map/ppermute | solution.py:323
  20.2 4.1 %copy-start.2 = (bf16[1,360,2880]{2,1,0:T(8,128)(2,1)S(1)}, bf16[1,360,2880]{2,1,0:T(8,128)(2,1)}, u32[]{:S(2)}) copy-start(bf16[1,360,2880]{2,1,0:T(8,128)(2,1)} %param.23) | copy-start | bytes 6220804
  22.2 1.4 %collective-permute-start.9 = (bf16[64,720]{1,0:T(8,128)(2,1)S(1)}, bf16[64,720]{1,0:T(8,128)(2,1)S(1)}, u32[]{:S(2)}, u32[]{:S(2)}) collective-permute-start(bf16[64,720]{1,0:T(8,128)(2,1)S(1)} %shard_map.126.mine_ref.refs_0_), channel_id=1, source_target_pairs={{0,1},{1,0},{2,3},{3,2},{4,5},{5,4},{6,7},{7,6},{8,9},{9,8},{10,11... | collective-permute-start | bytes 276488 | tf_op jit(solution)/shard_map/ppermute | solution.py:309
  22.3 5.5 %collective-permute-start.8 = (bf16[64,720]{1,0:T(8,128)(2,1)S(1)}, bf16[64,720]{1,0:T(8,128)(2,1)S(1)}, u32[]{:S(2)}, u32[]{:S(2)}) collective-permute-start(bf16[64,720]{1,0:T(8,128)(2,1)S(1)} %shard_map.126.mine_ref.refs_0_), channel_id=1, source_target_pairs={{0,2},{1,3},{2,0},{3,1},{4,6},{5,7},{6,4},{7,5},{8,10},{9,11},{10,... | collective-permute-start | bytes 276488 | tf_op jit(solution)/shard_map/ppermute | solution.py:309
  23.7 4.2 %collective-permute-start.10 = (f32[64,128]{1,0:T(8,128)S(1)}, f32[64,128]{1,0:T(8,128)S(1)}, u32[]{:S(2)}, u32[]{:S(2)}) collective-permute-start(f32[64,128]{1,0:T(8,128)S(1)} %shard_map.128.refs_3_), channel_id=1, source_target_pairs={{0,3},{1,2},{2,1},{3,0},{4,7},{5,6},{6,5},{7,4},{8,11},{9,10},{10,... | collective-permute-start | bytes 98312 | tf_op jit(solution)/shard_map/ppermute | solution.py:309
  27.8 1.8 %collective-permute-start.11 = (bf16[64,720]{1,0:T(8,128)(2,1)S(1)}, bf16[64,720]{1,0:T(8,128)(2,1)S(1)}, u32[]{:S(2)}, u32[]{:S(2)}) collective-permute-start(bf16[64,720]{1,0:T(8,128)(2,1)S(1)} %collective-permute-done.8.refs_2_), channel_id=1, source_target_pairs={{0,1},{1,0},{2,3},{3,2},{4,5},{5,4},{6,7},{7,6},{8,9},{9,8},{10,11... | collective-permute-start | bytes 276488 | tf_op jit(solution)/shard_map/ppermute | solution.py:309
  28.0 12.6 %collective-permute-start.21 = (bf16[512,256]{1,0:T(8,128)(2,1)S(1)}, bf16[512,256]{1,0:T(8,128)(2,1)S(1)}, u32[]{:S(2)}, u32[]{:S(2)}) collective-permute-start(bf16[512,256]{1,0:T(8,128)(2,1)S(1)} %get-tuple-element.84.refs_0_), channel_id=1, source_target_pairs={{0,1},{1,0},{2,3},{3,2},{4,5},{5,4},{6,7},{7,6},{8,9},{9,8},{10,11... | collective-permute-start | bytes 786440 | tf_op jit(solution)/shard_map/ppermute | solution.py:309
  28.3 12.2 %collective-permute-start.20 = (bf16[512,256]{1,0:T(8,128)(2,1)S(1)}, bf16[512,256]{1,0:T(8,128)(2,1)S(1)}, u32[]{:S(2)}, u32[]{:S(2)}) collective-permute-start(bf16[512,256]{1,0:T(8,128)(2,1)S(1)} %collective-permute-done.19.refs_3_), channel_id=1, source_target_pairs={{0,1},{1,0},{2,3},{3,2},{4,5},{5,4},{6,7},{7,6},{8,9},{9,8},{10,11... | collective-permute-start | bytes 786440 | tf_op jit(solution)/shard_map/ppermute | solution.py:309
  30.5 1.5 %collective-permute-start.12 = (bf16[2,64,720]{2,1,0:T(8,128)(2,1)S(1)}, bf16[2,64,720]{2,1,0:T(8,128)(2,1)S(1)}, u32[]{:S(2)}, u32[]{:S(2)}) collective-permute-start(bf16[2,64,720]{2,1,0:T(8,128)(2,1)S(1)} %get-tuple-element.72), channel_id=1, source_target_pairs={{0,1},{1,0},{2,3},{3,2},{4,5},{5,4},{6,7},{7,6},{8,9},{9,8},{10,11... | collective-permute-start | bytes 552968 | tf_op jit(solution)/shard_map/ppermute | solution.py:309
  32.0 3.7 %collective-permute-start.13 = (bf16[32,720]{1,0:T(8,128)(2,1)S(1)}, bf16[32,720]{1,0:T(8,128)(2,1)S(1)}, u32[]{:S(2)}, u32[]{:S(2)}) collective-permute-start(bf16[32,720]{1,0:T(8,128)(2,1)S(1)} %get-tuple-element.74), channel_id=1, source_target_pairs={{0,3},{1,2},{2,1},{3,0},{4,7},{5,6},{6,5},{7,4},{8,11},{9,10},{10,... | collective-permute-start | bytes 138248 | tf_op jit(solution)/shard_map/ppermute | solution.py:309
  32.7 5.4 %collective-permute-start.16 = (bf16[32,720]{1,0:T(8,128)(2,1)S(1)}, bf16[32,720]{1,0:T(8,128)(2,1)S(1)}, u32[]{:S(2)}, u32[]{:S(2)}) collective-permute-start(bf16[32,720]{1,0:T(8,128)(2,1)S(1)} %get-tuple-element.78), channel_id=1, source_target_pairs={{0,3},{1,2},{2,1},{3,0},{4,7},{5,6},{6,5},{7,4},{8,11},{9,10},{10,... | collective-permute-start | bytes 138248 | tf_op jit(solution)/shard_map/ppermute | solution.py:309
  35.7 5.8 %collective-permute-start.14 = (bf16[16,720]{1,0:T(8,128)(2,1)S(1)}, bf16[16,720]{1,0:T(8,128)(2,1)S(1)}, u32[]{:S(2)}, u32[]{:S(2)}) collective-permute-start(bf16[16,720]{1,0:T(8,128)(2,1)S(1)} %get-tuple-element.75), channel_id=1, source_target_pairs={{0,13},{1,12},{2,15},{3,14},{4,9},{5,8},{6,11},{7,10},{8,5},{9,4},... | collective-permute-start | bytes 69128 | tf_op jit(solution)/shard_map/ppermute | solution.py:323
  37.3 4.3 %collective-permute-start.15 = (bf16[16,720]{1,0:T(8,128)(2,1)S(1)}, bf16[16,720]{1,0:T(8,128)(2,1)S(1)}, u32[]{:S(2)}, u32[]{:S(2)}) collective-permute-start(bf16[16,720]{1,0:T(8,128)(2,1)S(1)} %get-tuple-element.76), channel_id=1, source_target_pairs={{0,9},{1,8},{2,11},{3,10},{4,13},{5,12},{6,15},{7,14},{8,1},{9,0},... | collective-permute-start | bytes 69128 | tf_op jit(solution)/shard_map/ppermute | solution.py:323
  38.1 4.1 %collective-permute-start.17 = (bf16[16,720]{1,0:T(8,128)(2,1)S(1)}, bf16[16,720]{1,0:T(8,128)(2,1)S(1)}, u32[]{:S(2)}, u32[]{:S(2)}) collective-permute-start(bf16[16,720]{1,0:T(8,128)(2,1)S(1)} %get-tuple-element.79), channel_id=1, source_target_pairs={{0,5},{1,4},{2,7},{3,6},{4,1},{5,0},{6,3},{7,2},{8,13},{9,12},{10,... | collective-permute-start | bytes 69128 | tf_op jit(solution)/shard_map/ppermute | solution.py:323
  40.6 1.7 %collective-permute-start.18 = (bf16[16,720]{1,0:T(8,128)(2,1)S(1)}, bf16[16,720]{1,0:T(8,128)(2,1)S(1)}, u32[]{:S(2)}, u32[]{:S(2)}) collective-permute-start(bf16[16,720]{1,0:T(8,128)(2,1)S(1)} %get-tuple-element.80), channel_id=1, source_target_pairs={{0,1},{1,0},{2,3},{3,2},{4,5},{5,4},{6,7},{7,6},{8,9},{9,8},{10,11... | collective-permute-start | bytes 69128 | tf_op jit(solution)/shard_map/ppermute | solution.py:323

commit v17 on v16

--- a/solution.py
+++ b/solution.py
@@ -222,6 +222,15 @@
         blocks_ref[p] = source_ref[:, p * width : (p + 1) * width]
 
 
+def spread_pair_kernel(start, gate_ref, up_ref, blocks_ref):
+    cuts, _, width = blocks_ref.shape
+    hidden = gate_ref.shape[0]
+    for p in range(cuts):
+        blocks_ref[p, :hidden] = gate_ref[:, p * width : (p + 1) * width]
+        blocks_ref[p, hidden:start] = jnp.zeros((start - hidden, width), jnp.bfloat16)
+        blocks_ref[p, start:] = up_ref[:, p * width : (p + 1) * width]
+
+
 def spread_gain_kernel(gain_ref, blocks_ref):
     cuts, _, width = blocks_ref.shape
     gain = gain_ref[...].reshape(1, cuts * width)
@@ -235,31 +244,30 @@
     squares_ref[...] = jnp.broadcast_to(squares, squares_ref.shape)
 
 
-def add_features(gate, up, scale, places, blocks, gains_ref, gates_ref, ups_ref, steps):
+def add_features(total, scale, places, blocks, gains_ref, weights_ref, steps):
     for i, block in zip(places, blocks):
         p = origin(i % steps, i >= steps)
         rows = (block[...].astype(jnp.float32) * scale * gains_ref[p]).astype(jnp.bfloat16)
-        gate += dot(rows, gates_ref[p], NT)
-        up += dot(rows, ups_ref[p], NT)
-    return gate, up
+        total += dot(rows, weights_ref[p], NT)
+    return total
 
 
 def expert_most_kernel(places, steps, *refs):
     blocks, squares = refs[: steps + 1], refs[steps + 1 : 2 * steps + 1]
-    gains_ref, gates_ref, ups_ref, gate_ref, up_ref, scale_ref = refs[2 * steps + 1 :]
+    gains_ref, weights_ref, total_ref, scale_ref = refs[2 * steps + 1 :]
     features = 2 * steps * blocks[0].shape[1]
     scale = lax.rsqrt(sum(ref[...] for ref in squares) / features + norm_eps)
     scale_ref[...] = scale
-    sums = add_features(0.0, 0.0, scale[:, :1], places, blocks, gains_ref, gates_ref, ups_ref, steps)
-    gate_ref[...], up_ref[...] = sums
+    total_ref[...] = add_features(0.0, scale[:, :1], places, blocks, gains_ref, weights_ref, steps)
 
 
 def expert_last_kernel(steps, *refs):
     blocks, refs = refs[: steps - 1], refs[steps - 1 :]
-    gate_ref, up_ref, scale_ref, gains_ref, gates_ref, ups_ref, downs_ref, given_ref, activated_ref = refs
-    gate, up = add_features(
-        gate_ref[...], up_ref[...], scale_ref[:, :1], range(1, steps), blocks, gains_ref, gates_ref, ups_ref, steps
-    )
+    total_ref, scale_ref, gains_ref, weights_ref, downs_ref, given_ref, activated_ref = refs
+    scale = scale_ref[:, :1]
+    total = add_features(total_ref[...], scale, range(1, steps), blocks, gains_ref, weights_ref, steps)
+    hidden = activated_ref.shape[1]
+    gate, up = total[:, :hidden], total[:, total.shape[1] - hidden :]
     activated = ((up + 1.0) * gate * jax.nn.sigmoid(glu_alpha * gate)).astype(jnp.bfloat16)
     activated_ref[...] = activated
     for k in range(steps):
@@ -398,8 +406,8 @@
     spread = functools.partial(
         call, spread_kernel, bf16(cuts, hidden, feats), n_in=1, moved=4 * w_gate.size
     )
-    gates = spread()(after(w_gate[0].T, rows))
-    chip_rows = after(chip_rows, (own, gates))
+    downs = spread()(after(w_down[0], rows))
+    chip_rows = after(chip_rows, (own, downs))
     relayed_rows = [from_sibling(b) for b in chip_rows]
     chips = call(functools.partial(rows_more_kernel, places, steps), total, n_in=steps + 2, **part)(
         sibling_rows, *chip_rows, own, w_t
@@ -414,34 +422,39 @@
 
     arrived = [to_seq(outgoing[k], k) for k in range(live - 1, -1, -1)]
 
-    ups = spread()(after(w_up[0].T, outgoing[0]))
+    start = -(-hidden // 128) * 128
+    weights = call(
+        functools.partial(spread_pair_kernel, start),
+        bf16(cuts, start + hidden, feats),
+        n_in=2,
+        moved=4 * w_gate.size,
+    )(*after((w_gate[0].T, w_up[0].T), outgoing[0]))
     gains = call(spread_gain_kernel, jax.ShapeDtypeStruct((cuts, 1, feats), jnp.float32), n_in=1)(norm_gain)
     part = dict(flops=slots * w_gate.size, moved=w_gate.size)
-    stacked = call(stack_kernel, bf16(slots, feats), n_in=live)(*after(arrived, (ups, gains)))
+    stacked = call(stack_kernel, bf16(slots, feats), n_in=live)(*after(arrived, (weights, gains)))
     chip_rows = from_chips(stacked, False)
     sibling_rows = from_sibling(stacked)
-    downs = spread()(after(w_down[0], stacked))
-    chip_blocks = from_chips(after(attended, gates))
+    chip_blocks = from_chips(after(attended, downs))
     sibling_block, *relayed_blocks = [from_sibling(b) for b in (attended, *chip_blocks)]
     blocks = [attended, *relayed_blocks, sibling_block, *chip_blocks]
     row_sums = jax.ShapeDtypeStruct((slots, KEYS_SEEN), jnp.float32)
     squares = call(squares_kernel, row_sums, n_in=2)(stacked, sibling_rows)
     chip_squares = from_chips(squares)
-    chip_rows = after(chip_rows, (downs, chip_squares))
+    chip_rows = after(chip_rows, chip_squares)
     relayed_rows = [from_sibling(b) for b in chip_rows]
-    sums = jax.ShapeDtypeStruct((slots, hidden), jnp.float32)
+    sums = jax.ShapeDtypeStruct((slots, start + hidden), jnp.float32)
     most = call(
         functools.partial(expert_most_kernel, [steps, 0, *range(steps + 1, 2 * steps)], steps),
-        (sums, sums, row_sums),
-        n_in=2 * steps + 4,
+        (sums, row_sums),
+        n_in=2 * steps + 3,
         **part,
-    )(stacked, sibling_rows, *chip_rows, squares, *chip_squares, gains, gates, ups)
+    )(stacked, sibling_rows, *chip_rows, squares, *chip_squares, gains, weights)
     given, activated = call(
         functools.partial(expert_last_kernel, steps),
         (bf16(steps, slots, feats), bf16(slots, hidden)),
-        n_in=steps + 6,
+        n_in=steps + 4,
         **part,
-    )(*relayed_rows, *most, gains, gates, ups, downs)
+    )(*relayed_rows, *most, gains, weights, downs)
     kept = call(expert_kept_kernel, bf16(steps, slots, feats), n_in=2, **part)(activated, downs)
     resid = call(
         functools.partial(project_kernel, steps),

time: 43.4 us -> 43.6 us (level)
    ppermute x13, waiting for transfers between devices: 7.03 us -> 7.64 us  [swap(): lax.ppermute(block, axis, [(i, i ^ mask) for i in range(lax.axis_size(axi...]
    ppermute x8, waiting for transfers between devices: 2.09 us -> 1.54 us  [to_seq(): lax.ppermute(block, ('seq', 'cuts'), [(i, i ^ mask) for i in range(size)])]
    pallas_call x3 -> x2, Pallas kernels: 1.77 us -> 1.72 us  [the longest x1 1.13 us: shards(): call(functools.partial(spread_pair_kernel, start), bf16(cuts, start + hid...]
where the time goes in v17:
time: 43.6 us; the launch traced here: 43.4 us
  starting transfers between devices  20.1 us (46%)
  Pallas kernels  11.2 us (26%)
  waiting for transfers between devices  11.1 us (25%)
  local copies, waits for them, and re-layouts  0.86 us (2%)
    ppermute x8, starting transfers between devices, to_seq(): lax.ppermute(block, ('seq', 'cuts'), [(i, i ^ mask) for i in range(size)])  9.14 us
    ppermute x13, starting transfers between devices, swap(): lax.ppermute(block, axis, [(i, i ^ mask) for i in range(lax.axis_size(axi...  7.94 us
    ppermute x13, waiting for transfers between devices, swap(): lax.ppermute(block, axis, [(i, i ^ mask) for i in range(lax.axis_size(axi...  7.64 us
    ppermute x1, starting transfers between devices, shards(): rim = lax.ppermute(tail, 'seq', [(i, (i + 1) % size) for i in range(size)])  3.02 us
    pallas_call x1, Pallas kernels, shards(): call(functools.partial(first_kernel, live), (*(bf16(*a.shape) for a in lo...  2.37 us
    ppermute x1, waiting for transfers between devices, shards(): rim = lax.ppermute(tail, 'seq', [(i, (i + 1) % size) for i in range(size)])  1.89 us
    ppermute x8, waiting for transfers between devices, to_seq(): lax.ppermute(block, ('seq', 'cuts'), [(i, i ^ mask) for i in range(size)])  1.54 us
    pallas_call x1, Pallas kernels, shards(): call(second_kernel, (bf16(head_rows, toks), bf16(slots, head_rows)), n_in...  1.14 us
  transfers between devices with their start and end apart: 22, of which 9 were waited for; matrix products, arithmetic and copies ran while one was open for 0% of the time, Pallas kernels for 21%

profile of v17, /device:TPU:0, one launch (start us, length us, event | category | flops | bytes accessed | tf_op | source)
XLA Modules:
  0.0 43.4 jit_solution(15169720863090108729)
XLA Ops:
  0.0 0.8 %slice.3 = bf16[128,256]{1,0:T(8,128)(2,1)S(1)} slice(bf16[256,256]{1,0:T(8,128)(2,1)} %refs_4_.1), slice={[128:256], [0:256]} | slice | bytes 131072 | tf_op jit(solution)/shard_map/slice | solution.py:367
  0.8 3.0 %collective-permute-start = (bf16[128,256]{1,0:T(8,128)(2,1)S(1)}, bf16[128,256]{1,0:T(8,128)(2,1)S(1)}, u32[]{:S(2)}, u32[]{:S(2)}) collective-permute-start(bf16[128,256]{1,0:T(8,128)(2,1)S(1)} %slice.3), channel_id=1, source_target_pairs={{0,4},{4,8},{8,12},{12,0},{1,5},{5,9},{9,13},{13,1},{2,6},{6,10},{... | collective-permute-start | bytes 196616 | tf_op jit(solution)/shard_map/ppermute | solution.py:368
  3.9 2.4 %shard_map.118 = (bf16[256,512]{1,0:T(8,128)(2,1)S(1)}, bf16[256,256]{1,0:T(8,128)(2,1)S(1)}, bf16[128,256]{1,0:T(8,128)(2,1)S(1)}, bf16[720,2048]{1,0:T(8,128)(...) custom-call(s32[4,256]{1,0:T(4,128)} %bitcast.17, ...), custom_call_target="tpu_custom_call" | custom-call | flops 134217728 | bytes 3579904 | tf_op jit(solution)/shard_map/pallas_call | solution.py:370
  6.2 1.9 %collective-permute-done.rim_ref = bf16[128,256]{1,0:T(8,128)(2,1)S(1)} collective-permute-done((bf16[128,256]{1,0:T(8,128)(2,1)S(1)}, bf16[128,256]{1,0:T(8,128)(2,1)S(1)}, u32[]{:S(2)}, u32[]{:S(2)}) %collective-permute-start) | collective-permute-done | bytes 65568 | tf_op jit(solution)/shard_map/ppermute | solution.py:368
  8.1 1.1 %shard_map.119 = (bf16[512,256]{1,0:T(8,128)(2,1)S(1)}, bf16[64,512]{1,0:T(8,128)(2,1)S(1)}) custom-call(bf16[256,512]{1,0:T(8,128)(2,1)S(1)} %get-tuple-element.44.q_ref, bf16[256,256]{1,0:T(8,128)(2,1)S(1)} %get-tuple-element.45.kv_ref, bf16[128,256]{1,0:T(8,128)(2,1)S(1)} %get-tuple-element.46.before_ref, ...), custom_call_target="tpu_custom_call" | custom-call | flops 67108864 | bytes 262144 | tf_op jit(solution)/shard_map/pallas_call | solution.py:390
  9.3 0.1 collective-permute-start.1
  9.4 1.8 %collective-permute-start.3 = (bf16[64,512]{1,0:T(8,128)(2,1)S(1)}, bf16[64,512]{1,0:T(8,128)(2,1)S(1)}, u32[]{:S(2)}, u32[]{:S(2)}) collective-permute-start(bf16[64,512]{1,0:T(8,128)(2,1)S(1)} %get-tuple-element.51.rows_ref), channel_id=1, source_target_pairs={{0,1},{1,0},{2,3},{3,2},{4,5},{5,4},{6,7},{7,6},{8,9},{9,8},{10,11... | collective-permute-start | bytes 196616 | tf_op jit(solution)/shard_map/ppermute | solution.py:317
  11.2 0.6 %shard_map.121.refs_5_.downs_ref = bf16[4,360,720]{2,1,0:T(8,128)(2,1)S(1)} custom-call(bf16[360,2880]{1,0:T(8,128)(2,1)S(1)} %bitcast.14), custom_call_target="tpu_custom_call" | custom-call | bytes 4147200 | tf_op jit(solution)/shard_map/pallas_call | solution.py:409
  11.8 0.5 %shard_map.120.refs_2_ = f32[64,720]{1,0:T(8,128)S(1)} custom-call(bf16[64,512]{1,0:T(8,128)(2,1)S(1)} %get-tuple-element.51.rows_ref, bf16[720,2048]{1,0:T(8,128)(2,1)S(1)} %get-tuple-element.52.w_ref.refs_3_.refs_2_.refs_4_, bf16[720,256]{1,0:T(8,128)(2,1)S(1)} %get-tuple-element.53.residual_ref.refs_5_, bf16[64,256]{1,0:T(8,128)(2,1)S(1)} %get-tuple-element.49.placing_ref), custom_call_target="tpu_custom_call" | custom-call | flops 47185920 | bytes 737280 | tf_op jit(solution)/shard_map/pallas_call | solution.py:401
  12.2 1.2 %collective-permute-done.1.refs_1_ = bf16[64,512]{1,0:T(8,128)(2,1)S(1)} collective-permute-done((bf16[64,512]{1,0:T(8,128)(2,1)S(1)}, bf16[64,512]{1,0:T(8,128)(2,1)S(1)}, u32[]{:S(2)}, u32[]{:S(2)}) %collective-permute-start.1) | collective-permute-done | bytes 65568 | tf_op jit(solution)/shard_map/ppermute | solution.py:317
  13.5 0.1 collective-permute-start.2
  13.6 1.3 %collective-permute-start.19 = (bf16[512,256]{1,0:T(8,128)(2,1)S(1)}, bf16[512,256]{1,0:T(8,128)(2,1)S(1)}, u32[]{:S(2)}, u32[]{:S(2)}) collective-permute-start(bf16[512,256]{1,0:T(8,128)(2,1)S(1)} %get-tuple-element.82.refs_0_), channel_id=1, source_target_pairs={{0,3},{1,2},{2,1},{3,0},{4,7},{5,6},{6,5},{7,4},{8,11},{9,10},{10,... | collective-permute-start | bytes 786440 | tf_op jit(solution)/shard_map/ppermute | solution.py:317
  14.9 0.0 collective-permute-done.3.refs_0_
  14.9 0.6 %shard_map.122.refs_1_ = f32[64,720]{1,0:T(8,128)S(1)} custom-call(bf16[64,512]{1,0:T(8,128)(2,1)S(1)} %collective-permute-done.3.refs_0_, bf16[64,512]{1,0:T(8,128)(2,1)S(1)} %collective-permute-done.1.refs_1_, f32[64,720]{1,0:T(8,128)S(1)} %shard_map.120.refs_2_, bf16[720,2048]{1,0:T(8,128)(2,1)S(1)} %get-tuple-element.52.w_ref.refs_3_.refs_2_.refs_4_), custom_call_target="tpu_custom_call" | custom-call | flops 47185920 | bytes 737280 | tf_op jit(solution)/shard_map/pallas_call | solution.py:412
  15.4 0.0 copy-start.3
  15.5 0.0 copy-start
  15.5 0.4 shard_map.123
  15.9 1.5 %collective-permute-start.4 = (bf16[16,720]{1,0:T(8,128)(2,1)S(1)}, bf16[16,720]{1,0:T(8,128)(2,1)S(1)}, u32[]{:S(2)}, u32[]{:S(2)}) collective-permute-start(bf16[16,720]{1,0:T(8,128)(2,1)S(1)} %get-tuple-element.56), channel_id=1, source_target_pairs={{0,13},{1,12},{2,15},{3,14},{4,9},{5,8},{6,11},{7,10},{8,5},{9,4},... | collective-permute-start | bytes 69128 | tf_op jit(solution)/shard_map/ppermute | solution.py:331
  17.3 2.3 %collective-permute-start.6 = (bf16[16,720]{1,0:T(8,128)(2,1)S(1)}, bf16[16,720]{1,0:T(8,128)(2,1)S(1)}, u32[]{:S(2)}, u32[]{:S(2)}) collective-permute-start(bf16[16,720]{1,0:T(8,128)(2,1)S(1)} %get-tuple-element.58), channel_id=1, source_target_pairs={{0,5},{1,4},{2,7},{3,6},{4,1},{5,0},{6,3},{7,2},{8,13},{9,12},{10,... | collective-permute-start | bytes 69128 | tf_op jit(solution)/shard_map/ppermute | solution.py:331
  19.6 0.5 %collective-permute-start.7 = (bf16[16,720]{1,0:T(8,128)(2,1)S(1)}, bf16[16,720]{1,0:T(8,128)(2,1)S(1)}, u32[]{:S(2)}, u32[]{:S(2)}) collective-permute-start(bf16[16,720]{1,0:T(8,128)(2,1)S(1)} %get-tuple-element.59), channel_id=1, source_target_pairs={{0,1},{1,0},{2,3},{3,2},{4,5},{5,4},{6,7},{7,6},{8,9},{9,8},{10,11... | collective-permute-start | bytes 69128 | tf_op jit(solution)/shard_map/ppermute | solution.py:331
  20.2 0.1 shard_map.125.refs_5_.refs_3_
  20.2 1.1 %shard_map.124.refs_6_.refs_4_ = bf16[4,744,720]{2,1,0:T(8,128)(2,1)S(1)} custom-call(bf16[360,2880]{1,0:T(8,128)(2,1)S(1)} %bitcast.12, bf16[360,2880]{1,0:T(8,128)(2,1)S(1)} %bitcast.13), custom_call_target="tpu_custom_call" | custom-call | bytes 4147200 | tf_op jit(solution)/shard_map/pallas_call | solution.py:426
  21.4 0.8 %collective-permute-done.5.refs_1_ = bf16[16,720]{1,0:T(8,128)(2,1)S(1)} collective-permute-done((bf16[16,720]{1,0:T(8,128)(2,1)S(1)}, bf16[16,720]{1,0:T(8,128)(2,1)S(1)}, u32[]{:S(2)}, u32[]{:S(2)}) %collective-permute-start.5) | collective-permute-done | bytes 23072 | tf_op jit(solution)/shard_map/ppermute | solution.py:331
  22.2 0.1 collective-permute-start.9
  22.3 0.9 %collective-permute-start.8 = (bf16[64,720]{1,0:T(8,128)(2,1)S(1)}, bf16[64,720]{1,0:T(8,128)(2,1)S(1)}, u32[]{:S(2)}, u32[]{:S(2)}) collective-permute-start(bf16[64,720]{1,0:T(8,128)(2,1)S(1)} %shard_map.126.mine_ref.refs_0_), channel_id=1, source_target_pairs={{0,2},{1,3},{2,0},{3,1},{4,6},{5,7},{6,4},{7,5},{8,10},{9,11},{10,... | collective-permute-start | bytes 276488 | tf_op jit(solution)/shard_map/ppermute | solution.py:317
  23.3 0.3 collective-permute-done.9.theirs_ref.refs_1_
  23.6 0.1 shard_map.127.refs_3_
  23.7 0.7 %collective-permute-start.10 = (f32[64,128]{1,0:T(8,128)S(1)}, f32[64,128]{1,0:T(8,128)S(1)}, u32[]{:S(2)}, u32[]{:S(2)}) collective-permute-start(f32[64,128]{1,0:T(8,128)S(1)} %shard_map.127.refs_3_), channel_id=1, source_target_pairs={{0,3},{1,2},{2,1},{3,0},{4,7},{5,6},{6,5},{7,4},{8,11},{9,10},{10,... | collective-permute-start | bytes 98312 | tf_op jit(solution)/shard_map/ppermute | solution.py:317
  24.4 3.5 %collective-permute-done.8.refs_2_ = bf16[64,720]{1,0:T(8,128)(2,1)S(1)} collective-permute-done((bf16[64,720]{1,0:T(8,128)(2,1)S(1)}, bf16[64,720]{1,0:T(8,128)(2,1)S(1)}, u32[]{:S(2)}, u32[]{:S(2)}) %collective-permute-start.8) | collective-permute-done | bytes 92192 | tf_op jit(solution)/shard_map/ppermute | solution.py:317
  27.8 0.2 collective-permute-start.11
  28.0 0.3 collective-permute-start.21
  28.4 0.2 collective-permute-start.20
  28.5 1.1 %shard_map.128 = (f32[64,744]{1,0:T(8,128)S(1)}, f32[64,128]{1,0:T(8,128)S(1)}) custom-call(bf16[64,720]{1,0:T(8,128)(2,1)S(1)} %shard_map.126.mine_ref.refs_0_, bf16[64,720]{1,0:T(8,128)(2,1)S(1)} %collective-permute-done.9.theirs_ref.refs_1_, bf16[64,720]{1,0:T(8,128)(2,1)S(1)} %collective-permute-done.8.refs_2_, f32[64,128]{1,0:T(8,128)S(1)} %shard_map.127.refs_3_, ...), custom_call_target="tpu_custom_call" | custom-call | flops 66355200 | bytes 1036800 | tf_op jit(solution)/shard_map/pallas_call | solution.py:446
  29.7 0.9 %shard_map.129 = (bf16[2,64,720]{2,1,0:T(8,128)(2,1)S(1)}, bf16[64,360]{1,0:T(8,128)(2,1)S(1)}) custom-call(bf16[64,720]{1,0:T(8,128)(2,1)S(1)} %collective-permute-done.11.refs_0_, f32[64,744]{1,0:T(8,128)S(1)} %get-tuple-element.67.refs_1_, f32[64,128]{1,0:T(8,128)S(1)} %get-tuple-element.68.refs_2_, f32[4,1,720]{2,1,0:T(1,128)S(1)} %shard_map.125.refs_5_.refs_3_, ...), custom_call_target="tpu_custom_call" | custom-call | flops 66355200 | bytes 1036800 | tf_op jit(solution)/shard_map/pallas_call | solution.py:452
  30.6 0.4 collective-permute-start.12
  31.0 0.3 shard_map.130.kept_ref
  31.4 0.8 %collective-permute-done.12.given_ref = bf16[2,64,720]{2,1,0:T(8,128)(2,1)S(1)} collective-permute-done((bf16[2,64,720]{2,1,0:T(8,128)(2,1)S(1)}, bf16[2,64,720]{2,1,0:T(8,128)(2,1)S(1)}, u32[]{:S(2)}, u32[]{:S(2)}) %collective-permute-start.12) | collective-permute-done | bytes 184352 | tf_op jit(solution)/shard_map/ppermute | solution.py:317
  32.1 0.1 shard_map.131
  32.2 0.7 %collective-permute-start.13 = (bf16[32,720]{1,0:T(8,128)(2,1)S(1)}, bf16[32,720]{1,0:T(8,128)(2,1)S(1)}, u32[]{:S(2)}, u32[]{:S(2)}) collective-permute-start(bf16[32,720]{1,0:T(8,128)(2,1)S(1)} %get-tuple-element.72), channel_id=1, source_target_pairs={{0,3},{1,2},{2,1},{3,0},{4,7},{5,6},{6,5},{7,4},{8,11},{9,10},{10,... | collective-permute-start | bytes 138248 | tf_op jit(solution)/shard_map/ppermute | solution.py:317
  32.8 1.1 %collective-permute-start.16 = (bf16[32,720]{1,0:T(8,128)(2,1)S(1)}, bf16[32,720]{1,0:T(8,128)(2,1)S(1)}, u32[]{:S(2)}, u32[]{:S(2)}) collective-permute-start(bf16[32,720]{1,0:T(8,128)(2,1)S(1)} %get-tuple-element.76), channel_id=1, source_target_pairs={{0,3},{1,2},{2,1},{3,0},{4,7},{5,6},{6,5},{7,4},{8,11},{9,10},{10,... | collective-permute-start | bytes 138248 | tf_op jit(solution)/shard_map/ppermute | solution.py:317
  34.0 1.8 %collective-permute-done.13.refs_1_ = bf16[32,720]{1,0:T(8,128)(2,1)S(1)} collective-permute-done((bf16[32,720]{1,0:T(8,128)(2,1)S(1)}, bf16[32,720]{1,0:T(8,128)(2,1)S(1)}, u32[]{:S(2)}, u32[]{:S(2)}) %collective-permute-start.13) | collective-permute-done | bytes 46112 | tf_op jit(solution)/shard_map/ppermute | solution.py:317
  35.8 1.6 %collective-permute-start.14 = (bf16[16,720]{1,0:T(8,128)(2,1)S(1)}, bf16[16,720]{1,0:T(8,128)(2,1)S(1)}, u32[]{:S(2)}, u32[]{:S(2)}) collective-permute-start(bf16[16,720]{1,0:T(8,128)(2,1)S(1)} %get-tuple-element.73), channel_id=1, source_target_pairs={{0,13},{1,12},{2,15},{3,14},{4,9},{5,8},{6,11},{7,10},{8,5},{9,4},... | collective-permute-start | bytes 69128 | tf_op jit(solution)/shard_map/ppermute | solution.py:331
  37.4 0.8 %collective-permute-start.15 = (bf16[16,720]{1,0:T(8,128)(2,1)S(1)}, bf16[16,720]{1,0:T(8,128)(2,1)S(1)}, u32[]{:S(2)}, u32[]{:S(2)}) collective-permute-start(bf16[16,720]{1,0:T(8,128)(2,1)S(1)} %get-tuple-element.74), channel_id=1, source_target_pairs={{0,9},{1,8},{2,11},{3,10},{4,13},{5,12},{6,15},{7,14},{8,1},{9,0},... | collective-permute-start | bytes 69128 | tf_op jit(solution)/shard_map/ppermute | solution.py:331
  38.3 2.4 %collective-permute-start.17 = (bf16[16,720]{1,0:T(8,128)(2,1)S(1)}, bf16[16,720]{1,0:T(8,128)(2,1)S(1)}, u32[]{:S(2)}, u32[]{:S(2)}) collective-permute-start(bf16[16,720]{1,0:T(8,128)(2,1)S(1)} %get-tuple-element.77), channel_id=1, source_target_pairs={{0,5},{1,4},{2,7},{3,6},{4,1},{5,0},{6,3},{7,2},{8,13},{9,12},{10,... | collective-permute-start | bytes 69128 | tf_op jit(solution)/shard_map/ppermute | solution.py:331
  40.7 0.9 %shard_map.134.refs_6_ = bf16[720,256]{1,0:T(8,128)(2,1)S(1)} custom-call(bf16[512,256]{1,0:T(8,128)(2,1)S(1)} %get-tuple-element.82.refs_0_, bf16[512,256]{1,0:T(8,128)(2,1)S(1)} %collective-permute-done.20.refs_1_, bf16[512,256]{1,0:T(8,128)(2,1)S(1)} %collective-permute-done.21.refs_2_, bf16[512,256]{1,0:T(8,128)(2,1)S(1)} %collective-permute-done.19.refs_3_, ...), custom_call_target="tpu_custom_call" | custom-call | flops 754974720 | bytes 2949120 | tf_op jit(solution)/shard_map/pallas_call | solution.py:459
  41.7 0.1 collective-permute-done.15.refs_1_
  41.7 0.7 %collective-permute-done.17.refs_2_ = bf16[16,720]{1,0:T(8,128)(2,1)S(1)} collective-permute-done((bf16[16,720]{1,0:T(8,128)(2,1)S(1)}, bf16[16,720]{1,0:T(8,128)(2,1)S(1)}, u32[]{:S(2)}, u32[]{:S(2)}) %collective-permute-start.17) | collective-permute-done | bytes 23072 | tf_op jit(solution)/shard_map/ppermute | solution.py:331
  42.4 1.0 %shard_map.135 = bf16[720,256]{1,0:T(8,128)(2,1)} custom-call(bf16[16,720]{1,0:T(8,128)(2,1)S(1)} %collective-permute-done.14.refs_0_, bf16[16,720]{1,0:T(8,128)(2,1)S(1)} %collective-permute-done.15.refs_1_, bf16[16,720]{1,0:T(8,128)(2,1)S(1)} %collective-permute-done.17.refs_2_, bf16[16,720]{1,0:T(8,128)(2,1)S(1)} %collective-permute-done.18.refs_3_, ...), custom_call_target="tpu_custom_call" | custom-call | tf_op jit(solution)/shard_map/pallas_call | solution.py:481
  (23 shorter events, 0.1 us)
Async XLA Ops:
  0.8 7.3 %collective-permute-start = (bf16[128,256]{1,0:T(8,128)(2,1)S(1)}, bf16[128,256]{1,0:T(8,128)(2,1)S(1)}, u32[]{:S(2)}, u32[]{:S(2)}) collective-permute-start(bf16[128,256]{1,0:T(8,128)(2,1)S(1)} %slice.3), channel_id=1, source_target_pairs={{0,4},{4,8},{8,12},{12,0},{1,5},{5,9},{9,13},{13,1},{2,6},{6,10},{... | collective-permute-start | bytes 196616 | tf_op jit(solution)/shard_map/ppermute | solution.py:368
  3.9 7.3 %copy-start.2 = (bf16[1,360,2880]{2,1,0:T(8,128)(2,1)S(1)}, bf16[1,360,2880]{2,1,0:T(8,128)(2,1)}, u32[]{:S(2)}) copy-start(bf16[1,360,2880]{2,1,0:T(8,128)(2,1)} %param.23) | copy-start | bytes 6220804
  9.3 4.2 %collective-permute-start.1 = (bf16[64,512]{1,0:T(8,128)(2,1)S(1)}, bf16[64,512]{1,0:T(8,128)(2,1)S(1)}, u32[]{:S(2)}, u32[]{:S(2)}) collective-permute-start(bf16[64,512]{1,0:T(8,128)(2,1)S(1)} %get-tuple-element.51.rows_ref), channel_id=1, source_target_pairs={{0,3},{1,2},{2,1},{3,0},{4,7},{5,6},{6,5},{7,4},{8,11},{9,10},{10,... | collective-permute-start | bytes 196616 | tf_op jit(solution)/shard_map/ppermute | solution.py:317
  9.4 5.5 %collective-permute-start.3 = (bf16[64,512]{1,0:T(8,128)(2,1)S(1)}, bf16[64,512]{1,0:T(8,128)(2,1)S(1)}, u32[]{:S(2)}, u32[]{:S(2)}) collective-permute-start(bf16[64,512]{1,0:T(8,128)(2,1)S(1)} %get-tuple-element.51.rows_ref), channel_id=1, source_target_pairs={{0,1},{1,0},{2,3},{3,2},{4,5},{5,4},{6,7},{7,6},{8,9},{9,8},{10,11... | collective-permute-start | bytes 196616 | tf_op jit(solution)/shard_map/ppermute | solution.py:317
  13.5 2.0 %collective-permute-start.2 = (bf16[64,512]{1,0:T(8,128)(2,1)S(1)}, bf16[64,512]{1,0:T(8,128)(2,1)S(1)}, u32[]{:S(2)}, u32[]{:S(2)}) collective-permute-start(bf16[64,512]{1,0:T(8,128)(2,1)S(1)} %collective-permute-done.1.refs_1_), channel_id=1, source_target_pairs={{0,1},{1,0},{2,3},{3,2},{4,5},{5,4},{6,7},{7,6},{8,9},{9,8},{10,11... | collective-permute-start | bytes 196616 | tf_op jit(solution)/shard_map/ppermute | solution.py:317
  13.6 14.8 %collective-permute-start.19 = (bf16[512,256]{1,0:T(8,128)(2,1)S(1)}, bf16[512,256]{1,0:T(8,128)(2,1)S(1)}, u32[]{:S(2)}, u32[]{:S(2)}) collective-permute-start(bf16[512,256]{1,0:T(8,128)(2,1)S(1)} %get-tuple-element.82.refs_0_), channel_id=1, source_target_pairs={{0,3},{1,2},{2,1},{3,0},{4,7},{5,6},{6,5},{7,4},{8,11},{9,10},{10,... | collective-permute-start | bytes 786440 | tf_op jit(solution)/shard_map/ppermute | solution.py:317
  14.9 5.4 %copy-start.1 = (bf16[1,2880,360]{1,2,0:T(8,128)(2,1)S(1)}, bf16[1,2880,360]{1,2,0:T(8,128)(2,1)}, u32[]{:S(2)}) copy-start(bf16[1,2880,360]{1,2,0:T(8,128)(2,1)} %param.22) | copy-start | bytes 6220804
  15.4 4.7 %copy-start.3 = (f32[2880]{0:T(1024)S(1)}, f32[2880]{0:T(1024)}, u32[]{:S(2)}) copy-start(f32[2880]{0:T(1024)} %gain_ref.1) | copy-start | bytes 34564
  15.5 4.8 %copy-start = (bf16[1,2880,360]{1,2,0:T(8,128)(2,1)S(1)}, bf16[1,2880,360]{1,2,0:T(8,128)(2,1)}, u32[]{:S(2)}) copy-start(bf16[1,2880,360]{1,2,0:T(8,128)(2,1)} %param.21) | copy-start | bytes 6220804
  15.9 5.5 %collective-permute-start.4 = (bf16[16,720]{1,0:T(8,128)(2,1)S(1)}, bf16[16,720]{1,0:T(8,128)(2,1)S(1)}, u32[]{:S(2)}, u32[]{:S(2)}) collective-permute-start(bf16[16,720]{1,0:T(8,128)(2,1)S(1)} %get-tuple-element.56), channel_id=1, source_target_pairs={{0,13},{1,12},{2,15},{3,14},{4,9},{5,8},{6,11},{7,10},{8,5},{9,4},... | collective-permute-start | bytes 69128 | tf_op jit(solution)/shard_map/ppermute | solution.py:331
  17.3 4.8 %collective-permute-start.5 = (bf16[16,720]{1,0:T(8,128)(2,1)S(1)}, bf16[16,720]{1,0:T(8,128)(2,1)S(1)}, u32[]{:S(2)}, u32[]{:S(2)}) collective-permute-start(bf16[16,720]{1,0:T(8,128)(2,1)S(1)} %get-tuple-element.57), channel_id=1, source_target_pairs={{0,9},{1,8},{2,11},{3,10},{4,13},{5,12},{6,15},{7,14},{8,1},{9,0},... | collective-permute-start | bytes 69128 | tf_op jit(solution)/shard_map/ppermute | solution.py:331
  17.3 4.8 %collective-permute-start.6 = (bf16[16,720]{1,0:T(8,128)(2,1)S(1)}, bf16[16,720]{1,0:T(8,128)(2,1)S(1)}, u32[]{:S(2)}, u32[]{:S(2)}) collective-permute-start(bf16[16,720]{1,0:T(8,128)(2,1)S(1)} %get-tuple-element.58), channel_id=1, source_target_pairs={{0,5},{1,4},{2,7},{3,6},{4,1},{5,0},{6,3},{7,2},{8,13},{9,12},{10,... | collective-permute-start | bytes 69128 | tf_op jit(solution)/shard_map/ppermute | solution.py:331
  19.6 2.5 %collective-permute-start.7 = (bf16[16,720]{1,0:T(8,128)(2,1)S(1)}, bf16[16,720]{1,0:T(8,128)(2,1)S(1)}, u32[]{:S(2)}, u32[]{:S(2)}) collective-permute-start(bf16[16,720]{1,0:T(8,128)(2,1)S(1)} %get-tuple-element.59), channel_id=1, source_target_pairs={{0,1},{1,0},{2,3},{3,2},{4,5},{5,4},{6,7},{7,6},{8,9},{9,8},{10,11... | collective-permute-start | bytes 69128 | tf_op jit(solution)/shard_map/ppermute | solution.py:331
  22.2 1.4 %collective-permute-start.9 = (bf16[64,720]{1,0:T(8,128)(2,1)S(1)}, bf16[64,720]{1,0:T(8,128)(2,1)S(1)}, u32[]{:S(2)}, u32[]{:S(2)}) collective-permute-start(bf16[64,720]{1,0:T(8,128)(2,1)S(1)} %shard_map.126.mine_ref.refs_0_), channel_id=1, source_target_pairs={{0,1},{1,0},{2,3},{3,2},{4,5},{5,4},{6,7},{7,6},{8,9},{9,8},{10,11... | collective-permute-start | bytes 276488 | tf_op jit(solution)/shard_map/ppermute | solution.py:317
  22.3 5.5 %collective-permute-start.8 = (bf16[64,720]{1,0:T(8,128)(2,1)S(1)}, bf16[64,720]{1,0:T(8,128)(2,1)S(1)}, u32[]{:S(2)}, u32[]{:S(2)}) collective-permute-start(bf16[64,720]{1,0:T(8,128)(2,1)S(1)} %shard_map.126.mine_ref.refs_0_), channel_id=1, source_target_pairs={{0,2},{1,3},{2,0},{3,1},{4,6},{5,7},{6,4},{7,5},{8,10},{9,11},{10,... | collective-permute-start | bytes 276488 | tf_op jit(solution)/shard_map/ppermute | solution.py:317
  23.7 4.2 %collective-permute-start.10 = (f32[64,128]{1,0:T(8,128)S(1)}, f32[64,128]{1,0:T(8,128)S(1)}, u32[]{:S(2)}, u32[]{:S(2)}) collective-permute-start(f32[64,128]{1,0:T(8,128)S(1)} %shard_map.127.refs_3_), channel_id=1, source_target_pairs={{0,3},{1,2},{2,1},{3,0},{4,7},{5,6},{6,5},{7,4},{8,11},{9,10},{10,... | collective-permute-start | bytes 98312 | tf_op jit(solution)/shard_map/ppermute | solution.py:317
  27.8 1.8 %collective-permute-start.11 = (bf16[64,720]{1,0:T(8,128)(2,1)S(1)}, bf16[64,720]{1,0:T(8,128)(2,1)S(1)}, u32[]{:S(2)}, u32[]{:S(2)}) collective-permute-start(bf16[64,720]{1,0:T(8,128)(2,1)S(1)} %collective-permute-done.8.refs_2_), channel_id=1, source_target_pairs={{0,1},{1,0},{2,3},{3,2},{4,5},{5,4},{6,7},{7,6},{8,9},{9,8},{10,11... | collective-permute-start | bytes 276488 | tf_op jit(solution)/shard_map/ppermute | solution.py:317
  28.0 12.7 %collective-permute-start.21 = (bf16[512,256]{1,0:T(8,128)(2,1)S(1)}, bf16[512,256]{1,0:T(8,128)(2,1)S(1)}, u32[]{:S(2)}, u32[]{:S(2)}) collective-permute-start(bf16[512,256]{1,0:T(8,128)(2,1)S(1)} %get-tuple-element.82.refs_0_), channel_id=1, source_target_pairs={{0,1},{1,0},{2,3},{3,2},{4,5},{5,4},{6,7},{7,6},{8,9},{9,8},{10,11... | collective-permute-start | bytes 786440 | tf_op jit(solution)/shard_map/ppermute | solution.py:317
  28.4 12.4 %collective-permute-start.20 = (bf16[512,256]{1,0:T(8,128)(2,1)S(1)}, bf16[512,256]{1,0:T(8,128)(2,1)S(1)}, u32[]{:S(2)}, u32[]{:S(2)}) collective-permute-start(bf16[512,256]{1,0:T(8,128)(2,1)S(1)} %collective-permute-done.19.refs_3_), channel_id=1, source_target_pairs={{0,1},{1,0},{2,3},{3,2},{4,5},{5,4},{6,7},{7,6},{8,9},{9,8},{10,11... | collective-permute-start | bytes 786440 | tf_op jit(solution)/shard_map/ppermute | solution.py:317
  30.6 1.5 %collective-permute-start.12 = (bf16[2,64,720]{2,1,0:T(8,128)(2,1)S(1)}, bf16[2,64,720]{2,1,0:T(8,128)(2,1)S(1)}, u32[]{:S(2)}, u32[]{:S(2)}) collective-permute-start(bf16[2,64,720]{2,1,0:T(8,128)(2,1)S(1)} %get-tuple-element.70), channel_id=1, source_target_pairs={{0,1},{1,0},{2,3},{3,2},{4,5},{5,4},{6,7},{7,6},{8,9},{9,8},{10,11... | collective-permute-start | bytes 552968 | tf_op jit(solution)/shard_map/ppermute | solution.py:317
  32.2 3.7 %collective-permute-start.13 = (bf16[32,720]{1,0:T(8,128)(2,1)S(1)}, bf16[32,720]{1,0:T(8,128)(2,1)S(1)}, u32[]{:S(2)}, u32[]{:S(2)}) collective-permute-start(bf16[32,720]{1,0:T(8,128)(2,1)S(1)} %get-tuple-element.72), channel_id=1, source_target_pairs={{0,3},{1,2},{2,1},{3,0},{4,7},{5,6},{6,5},{7,4},{8,11},{9,10},{10,... | collective-permute-start | bytes 138248 | tf_op jit(solution)/shard_map/ppermute | solution.py:317
  32.8 5.4 %collective-permute-start.16 = (bf16[32,720]{1,0:T(8,128)(2,1)S(1)}, bf16[32,720]{1,0:T(8,128)(2,1)S(1)}, u32[]{:S(2)}, u32[]{:S(2)}) collective-permute-start(bf16[32,720]{1,0:T(8,128)(2,1)S(1)} %get-tuple-element.76), channel_id=1, source_target_pairs={{0,3},{1,2},{2,1},{3,0},{4,7},{5,6},{6,5},{7,4},{8,11},{9,10},{10,... | collective-permute-start | bytes 138248 | tf_op jit(solution)/shard_map/ppermute | solution.py:317
  35.8 5.8 %collective-permute-start.14 = (bf16[16,720]{1,0:T(8,128)(2,1)S(1)}, bf16[16,720]{1,0:T(8,128)(2,1)S(1)}, u32[]{:S(2)}, u32[]{:S(2)}) collective-permute-start(bf16[16,720]{1,0:T(8,128)(2,1)S(1)} %get-tuple-element.73), channel_id=1, source_target_pairs={{0,13},{1,12},{2,15},{3,14},{4,9},{5,8},{6,11},{7,10},{8,5},{9,4},... | collective-permute-start | bytes 69128 | tf_op jit(solution)/shard_map/ppermute | solution.py:331
  37.4 4.3 %collective-permute-start.15 = (bf16[16,720]{1,0:T(8,128)(2,1)S(1)}, bf16[16,720]{1,0:T(8,128)(2,1)S(1)}, u32[]{:S(2)}, u32[]{:S(2)}) collective-permute-start(bf16[16,720]{1,0:T(8,128)(2,1)S(1)} %get-tuple-element.74), channel_id=1, source_target_pairs={{0,9},{1,8},{2,11},{3,10},{4,13},{5,12},{6,15},{7,14},{8,1},{9,0},... | collective-permute-start | bytes 69128 | tf_op jit(solution)/shard_map/ppermute | solution.py:331
  38.3 4.1 %collective-permute-start.17 = (bf16[16,720]{1,0:T(8,128)(2,1)S(1)}, bf16[16,720]{1,0:T(8,128)(2,1)S(1)}, u32[]{:S(2)}, u32[]{:S(2)}) collective-permute-start(bf16[16,720]{1,0:T(8,128)(2,1)S(1)} %get-tuple-element.77), channel_id=1, source_target_pairs={{0,5},{1,4},{2,7},{3,6},{4,1},{5,0},{6,3},{7,2},{8,13},{9,12},{10,... | collective-permute-start | bytes 69128 | tf_op jit(solution)/shard_map/ppermute | solution.py:331
  40.7 1.7 %collective-permute-start.18 = (bf16[16,720]{1,0:T(8,128)(2,1)S(1)}, bf16[16,720]{1,0:T(8,128)(2,1)S(1)}, u32[]{:S(2)}, u32[]{:S(2)}) collective-permute-start(bf16[16,720]{1,0:T(8,128)(2,1)S(1)} %get-tuple-element.78), channel_id=1, source_target_pairs={{0,1},{1,0},{2,3},{3,2},{4,5},{5,4},{6,7},{7,6},{8,9},{9,8},{10,11... | collective-permute-start | bytes 69128 | tf_op jit(solution)/shard_map/ppermute | solution.py:331

commit v18 on v16

--- a/solution.py
+++ b/solution.py
@@ -258,7 +258,7 @@
     blocks, refs = refs[: steps - 1], refs[steps - 1 :]
     gate_ref, up_ref, scale_ref, gains_ref, gates_ref, ups_ref, downs_ref, given_ref, activated_ref = refs
     gate, up = add_features(
-        gate_ref[...], up_ref[...], scale_ref[:, :1], range(1, steps), blocks, gains_ref, gates_ref, ups_ref, steps
+        gate_ref[...], up_ref[...], scale_ref[:, :1], range(steps + 1, 2 * steps), blocks, gains_ref, gates_ref, ups_ref, steps
     )
     activated = ((up + 1.0) * gate * jax.nn.sigmoid(glu_alpha * gate)).astype(jnp.bfloat16)
     activated_ref[...] = activated
@@ -418,7 +418,7 @@
     gains = call(spread_gain_kernel, jax.ShapeDtypeStruct((cuts, 1, feats), jnp.float32), n_in=1)(norm_gain)
     part = dict(flops=slots * w_gate.size, moved=w_gate.size)
     stacked = call(stack_kernel, bf16(slots, feats), n_in=live)(*after(arrived, (ups, gains)))
-    chip_rows = from_chips(stacked, False)
+    chip_rows = from_chips(stacked)
     sibling_rows = from_sibling(stacked)
     downs = spread()(after(w_down[0], stacked))
     chip_blocks = from_chips(after(attended, gates))
@@ -431,7 +431,7 @@
     relayed_rows = [from_sibling(b) for b in chip_rows]
     sums = jax.ShapeDtypeStruct((slots, hidden), jnp.float32)
     most = call(
-        functools.partial(expert_most_kernel, [steps, 0, *range(steps + 1, 2 * steps)], steps),
+        functools.partial(expert_most_kernel, [steps, 0, *range(1, steps)], steps),
         (sums, sums, row_sums),
         n_in=2 * steps + 4,
         **part,

time: 43.4 us -> 43.6 us (level)
  waiting for transfers between devices: 11 us -> 11.9 us
  starting transfers between devices: 20.1 us -> 19.4 us
    ppermute x8, waiting for transfers between devices: 2.09 us -> 2.66 us  [to_seq(): lax.ppermute(block, ('seq', 'cuts'), [(i, i ^ mask) for i in range(size)])]
    ppermute x8, starting transfers between devices: 9.14 us -> 8.69 us  [to_seq(): lax.ppermute(block, ('seq', 'cuts'), [(i, i ^ mask) for i in range(size)])]
  transfers between devices with their start and end apart: 22 -> 22, of which waited for: 9 -> 10; matrix products, arithmetic and copies ran while one was open for 0% -> 0% of each run, Pallas kernels for 21% -> 21%
where the time goes in v18:
time: 43.6 us; the launch traced here: 43.5 us
  starting transfers between devices  19.4 us (44%)
  waiting for transfers between devices  11.9 us (27%)
  Pallas kernels  11.1 us (25%)
  local copies, waits for them, and re-layouts  0.86 us (2%)
    ppermute x8, starting transfers between devices, to_seq(): lax.ppermute(block, ('seq', 'cuts'), [(i, i ^ mask) for i in range(size)])  8.69 us
    ppermute x13, starting transfers between devices, swap(): lax.ppermute(block, axis, [(i, i ^ mask) for i in range(lax.axis_size(axi...  7.72 us
    ppermute x13, waiting for transfers between devices, swap(): lax.ppermute(block, axis, [(i, i ^ mask) for i in range(lax.axis_size(axi...  7.34 us
    ppermute x1, starting transfers between devices, shards(): rim = lax.ppermute(tail, 'seq', [(i, (i + 1) % size) for i in range(size)])  3.02 us
    ppermute x8, waiting for transfers between devices, to_seq(): lax.ppermute(block, ('seq', 'cuts'), [(i, i ^ mask) for i in range(size)])  2.66 us
    pallas_call x1, Pallas kernels, shards(): call(functools.partial(first_kernel, live), (*(bf16(*a.shape) for a in lo...  2.37 us
    ppermute x1, waiting for transfers between devices, shards(): rim = lax.ppermute(tail, 'seq', [(i, (i + 1) % size) for i in range(size)])  1.89 us
    pallas_call x1, Pallas kernels, shards(): call(second_kernel, (bf16(head_rows, toks), bf16(slots, head_rows)), n_in...  1.14 us
  transfers between devices with their start and end apart: 22, of which 10 were waited for; matrix products, arithmetic and copies ran while one was open for 0% of the time, Pallas kernels for 21%

profile of v18, /device:TPU:0, one launch (start us, length us, event | category | flops | bytes accessed | tf_op | source)
XLA Modules:
  0.0 43.5 jit_solution(5627407594255248557)
XLA Ops:
  0.0 0.8 %slice.3 = bf16[128,256]{1,0:T(8,128)(2,1)S(1)} slice(bf16[256,256]{1,0:T(8,128)(2,1)} %refs_4_.1), slice={[128:256], [0:256]} | slice | bytes 131072 | tf_op jit(solution)/shard_map/slice | solution.py:359
  0.8 3.0 %collective-permute-start = (bf16[128,256]{1,0:T(8,128)(2,1)S(1)}, bf16[128,256]{1,0:T(8,128)(2,1)S(1)}, u32[]{:S(2)}, u32[]{:S(2)}) collective-permute-start(bf16[128,256]{1,0:T(8,128)(2,1)S(1)} %slice.3), channel_id=1, source_target_pairs={{0,4},{4,8},{8,12},{12,0},{1,5},{5,9},{9,13},{13,1},{2,6},{6,10},{... | collective-permute-start | bytes 196616 | tf_op jit(solution)/shard_map/ppermute | solution.py:360
  3.9 2.4 %shard_map.118 = (bf16[256,512]{1,0:T(8,128)(2,1)S(1)}, bf16[256,256]{1,0:T(8,128)(2,1)S(1)}, bf16[128,256]{1,0:T(8,128)(2,1)S(1)}, bf16[720,2048]{1,0:T(8,128)(...) custom-call(s32[4,256]{1,0:T(4,128)} %bitcast.17, ...), custom_call_target="tpu_custom_call" | custom-call | flops 134217728 | bytes 3579904 | tf_op jit(solution)/shard_map/pallas_call | solution.py:362
  6.2 1.9 %collective-permute-done.rim_ref = bf16[128,256]{1,0:T(8,128)(2,1)S(1)} collective-permute-done((bf16[128,256]{1,0:T(8,128)(2,1)S(1)}, bf16[128,256]{1,0:T(8,128)(2,1)S(1)}, u32[]{:S(2)}, u32[]{:S(2)}) %collective-permute-start) | collective-permute-done | bytes 65568 | tf_op jit(solution)/shard_map/ppermute | solution.py:360
  8.1 1.1 %shard_map.119 = (bf16[512,256]{1,0:T(8,128)(2,1)S(1)}, bf16[64,512]{1,0:T(8,128)(2,1)S(1)}) custom-call(bf16[256,512]{1,0:T(8,128)(2,1)S(1)} %get-tuple-element.45.q_ref, bf16[256,256]{1,0:T(8,128)(2,1)S(1)} %get-tuple-element.46.kv_ref, bf16[128,256]{1,0:T(8,128)(2,1)S(1)} %get-tuple-element.47.before_ref, ...), custom_call_target="tpu_custom_call" | custom-call | flops 67108864 | bytes 262144 | tf_op jit(solution)/shard_map/pallas_call | solution.py:382
  9.3 0.1 collective-permute-start.1
  9.4 1.8 %collective-permute-start.3 = (bf16[64,512]{1,0:T(8,128)(2,1)S(1)}, bf16[64,512]{1,0:T(8,128)(2,1)S(1)}, u32[]{:S(2)}, u32[]{:S(2)}) collective-permute-start(bf16[64,512]{1,0:T(8,128)(2,1)S(1)} %get-tuple-element.52.rows_ref), channel_id=1, source_target_pairs={{0,1},{1,0},{2,3},{3,2},{4,5},{5,4},{6,7},{7,6},{8,9},{9,8},{10,11... | collective-permute-start | bytes 196616 | tf_op jit(solution)/shard_map/ppermute | solution.py:309
  11.2 0.6 %shard_map.121.refs_6_.refs_5_ = bf16[4,360,720]{2,1,0:T(8,128)(2,1)S(1)} custom-call(bf16[360,2880]{1,0:T(8,128)(2,1)S(1)} %bitcast.12), custom_call_target="tpu_custom_call" | custom-call | bytes 4147200 | tf_op jit(solution)/shard_map/pallas_call | solution.py:401
  11.8 0.5 %shard_map.120.refs_2_ = f32[64,720]{1,0:T(8,128)S(1)} custom-call(bf16[64,512]{1,0:T(8,128)(2,1)S(1)} %get-tuple-element.52.rows_ref, bf16[720,2048]{1,0:T(8,128)(2,1)S(1)} %get-tuple-element.53.w_ref.refs_3_.refs_2_.refs_4_, bf16[720,256]{1,0:T(8,128)(2,1)S(1)} %get-tuple-element.54.residual_ref.refs_5_, bf16[64,256]{1,0:T(8,128)(2,1)S(1)} %get-tuple-element.50.placing_ref), custom_call_target="tpu_custom_call" | custom-call | flops 47185920 | bytes 737280 | tf_op jit(solution)/shard_map/pallas_call | solution.py:393
  12.2 1.2 %collective-permute-done.1.refs_1_ = bf16[64,512]{1,0:T(8,128)(2,1)S(1)} collective-permute-done((bf16[64,512]{1,0:T(8,128)(2,1)S(1)}, bf16[64,512]{1,0:T(8,128)(2,1)S(1)}, u32[]{:S(2)}, u32[]{:S(2)}) %collective-permute-start.1) | collective-permute-done | bytes 65568 | tf_op jit(solution)/shard_map/ppermute | solution.py:309
  13.5 0.1 collective-permute-start.2
  13.6 1.3 %collective-permute-start.19 = (bf16[512,256]{1,0:T(8,128)(2,1)S(1)}, bf16[512,256]{1,0:T(8,128)(2,1)S(1)}, u32[]{:S(2)}, u32[]{:S(2)}) collective-permute-start(bf16[512,256]{1,0:T(8,128)(2,1)S(1)} %get-tuple-element.84.refs_0_), channel_id=1, source_target_pairs={{0,3},{1,2},{2,1},{3,0},{4,7},{5,6},{6,5},{7,4},{8,11},{9,10},{10,... | collective-permute-start | bytes 786440 | tf_op jit(solution)/shard_map/ppermute | solution.py:309
  14.9 0.6 %shard_map.122.refs_1_ = f32[64,720]{1,0:T(8,128)S(1)} custom-call(bf16[64,512]{1,0:T(8,128)(2,1)S(1)} %collective-permute-done.3.refs_0_, bf16[64,512]{1,0:T(8,128)(2,1)S(1)} %collective-permute-done.1.refs_1_, f32[64,720]{1,0:T(8,128)S(1)} %shard_map.120.refs_2_, bf16[720,2048]{1,0:T(8,128)(2,1)S(1)} %get-tuple-element.53.w_ref.refs_3_.refs_2_.refs_4_), custom_call_target="tpu_custom_call" | custom-call | flops 47185920 | bytes 737280 | tf_op jit(solution)/shard_map/pallas_call | solution.py:404
  15.4 0.0 copy-start.3
  15.5 0.4 shard_map.123
  15.8 1.5 %collective-permute-start.4 = (bf16[16,720]{1,0:T(8,128)(2,1)S(1)}, bf16[16,720]{1,0:T(8,128)(2,1)S(1)}, u32[]{:S(2)}, u32[]{:S(2)}) collective-permute-start(bf16[16,720]{1,0:T(8,128)(2,1)S(1)} %get-tuple-element.57), channel_id=1, source_target_pairs={{0,13},{1,12},{2,15},{3,14},{4,9},{5,8},{6,11},{7,10},{8,5},{9,4},... | collective-permute-start | bytes 69128 | tf_op jit(solution)/shard_map/ppermute | solution.py:323
  17.3 2.3 %collective-permute-start.6 = (bf16[16,720]{1,0:T(8,128)(2,1)S(1)}, bf16[16,720]{1,0:T(8,128)(2,1)S(1)}, u32[]{:S(2)}, u32[]{:S(2)}) collective-permute-start(bf16[16,720]{1,0:T(8,128)(2,1)S(1)} %get-tuple-element.59), channel_id=1, source_target_pairs={{0,5},{1,4},{2,7},{3,6},{4,1},{5,0},{6,3},{7,2},{8,13},{9,12},{10,... | collective-permute-start | bytes 69128 | tf_op jit(solution)/shard_map/ppermute | solution.py:323
  19.6 0.5 %collective-permute-start.7 = (bf16[16,720]{1,0:T(8,128)(2,1)S(1)}, bf16[16,720]{1,0:T(8,128)(2,1)S(1)}, u32[]{:S(2)}, u32[]{:S(2)}) collective-permute-start(bf16[16,720]{1,0:T(8,128)(2,1)S(1)} %get-tuple-element.60), channel_id=1, source_target_pairs={{0,1},{1,0},{2,3},{3,2},{4,5},{5,4},{6,7},{7,6},{8,9},{9,8},{10,11... | collective-permute-start | bytes 69128 | tf_op jit(solution)/shard_map/ppermute | solution.py:323
  20.1 0.1 shard_map.125.refs_5_.refs_4_
  20.2 0.6 %shard_map.124.refs_7_.refs_6_ = bf16[4,360,720]{2,1,0:T(8,128)(2,1)S(1)} custom-call(bf16[360,2880]{1,0:T(8,128)(2,1)S(1)} %bitcast.13), custom_call_target="tpu_custom_call" | custom-call | bytes 4147200 | tf_op jit(solution)/shard_map/pallas_call | solution.py:417
  20.8 0.2 collective-permute-done.4.refs_0_
  21.1 1.1 %collective-permute-done.5.refs_1_ = bf16[16,720]{1,0:T(8,128)(2,1)S(1)} collective-permute-done((bf16[16,720]{1,0:T(8,128)(2,1)S(1)}, bf16[16,720]{1,0:T(8,128)(2,1)S(1)}, u32[]{:S(2)}, u32[]{:S(2)}) %collective-permute-start.5) | collective-permute-done | bytes 23072 | tf_op jit(solution)/shard_map/ppermute | solution.py:323
  22.2 0.1 collective-permute-start.9
  22.3 0.7 %collective-permute-start.8 = (bf16[64,720]{1,0:T(8,128)(2,1)S(1)}, bf16[64,720]{1,0:T(8,128)(2,1)S(1)}, u32[]{:S(2)}, u32[]{:S(2)}) collective-permute-start(bf16[64,720]{1,0:T(8,128)(2,1)S(1)} %shard_map.126.mine_ref.refs_0_), channel_id=1, source_target_pairs={{0,3},{1,2},{2,1},{3,0},{4,7},{5,6},{6,5},{7,4},{8,11},{9,10},{10,... | collective-permute-start | bytes 276488 | tf_op jit(solution)/shard_map/ppermute | solution.py:309
  23.0 0.5 %collective-permute-done.9.theirs_ref.refs_1_ = bf16[64,720]{1,0:T(8,128)(2,1)S(1)} collective-permute-done((bf16[64,720]{1,0:T(8,128)(2,1)S(1)}, bf16[64,720]{1,0:T(8,128)(2,1)S(1)}, u32[]{:S(2)}, u32[]{:S(2)}) %collective-permute-start.9) | collective-permute-done | bytes 92192 | tf_op jit(solution)/shard_map/ppermute | solution.py:309
  23.5 0.1 shard_map.128.refs_3_
  23.7 0.7 %collective-permute-start.10 = (f32[64,128]{1,0:T(8,128)S(1)}, f32[64,128]{1,0:T(8,128)S(1)}, u32[]{:S(2)}, u32[]{:S(2)}) collective-permute-start(f32[64,128]{1,0:T(8,128)S(1)} %shard_map.128.refs_3_), channel_id=1, source_target_pairs={{0,3},{1,2},{2,1},{3,0},{4,7},{5,6},{6,5},{7,4},{8,11},{9,10},{10,... | collective-permute-start | bytes 98312 | tf_op jit(solution)/shard_map/ppermute | solution.py:309
  24.4 0.6 %shard_map.127.refs_7_.downs_ref = bf16[4,360,720]{2,1,0:T(8,128)(2,1)S(1)} custom-call(bf16[360,2880]{1,0:T(8,128)(2,1)S(1)} %bitcast.14), custom_call_target="tpu_custom_call" | custom-call | bytes 4147200 | tf_op jit(solution)/shard_map/pallas_call | solution.py:423
  25.0 1.9 %collective-permute-done.8.refs_2_ = bf16[64,720]{1,0:T(8,128)(2,1)S(1)} collective-permute-done((bf16[64,720]{1,0:T(8,128)(2,1)S(1)}, bf16[64,720]{1,0:T(8,128)(2,1)S(1)}, u32[]{:S(2)}, u32[]{:S(2)}) %collective-permute-start.8) | collective-permute-done | bytes 92192 | tf_op jit(solution)/shard_map/ppermute | solution.py:309
  26.9 0.7 %collective-permute-done.10.refs_4_ = f32[64,128]{1,0:T(8,128)S(1)} collective-permute-done((f32[64,128]{1,0:T(8,128)S(1)}, f32[64,128]{1,0:T(8,128)S(1)}, u32[]{:S(2)}, u32[]{:S(2)}) %collective-permute-start.10) | collective-permute-done | bytes 32800 | tf_op jit(solution)/shard_map/ppermute | solution.py:309
  27.6 0.4 collective-permute-start.11
  27.9 0.1 collective-permute-start.21
  28.1 0.4 collective-permute-start.20
  28.5 1.1 %shard_map.129 = (f32[64,360]{1,0:T(8,128)S(1)}, f32[64,360]{1,0:T(8,128)S(1)}, f32[64,128]{1,0:T(8,128)S(1)}) custom-call(bf16[64,720]{1,0:T(8,128)(2,1)S(1)} %shard_map.126.mine_ref.refs_0_, bf16[64,720]{1,0:T(8,128)(2,1)S(1)} %collective-permute-done.9.theirs_ref.refs_1_, bf16[64,720]{1,0:T(8,128)(2,1)S(1)} %collective-permute-done.8.refs_2_, ...), custom_call_target="tpu_custom_call" | custom-call | flops 66355200 | bytes 1036800 | tf_op jit(solution)/shard_map/pallas_call | solution.py:433
  29.6 0.0 collective-permute-done.11.refs_0_
  29.6 0.8 %shard_map.130 = (bf16[2,64,720]{2,1,0:T(8,128)(2,1)S(1)}, bf16[64,360]{1,0:T(8,128)(2,1)S(1)}) custom-call(bf16[64,720]{1,0:T(8,128)(2,1)S(1)} %collective-permute-done.11.refs_0_, f32[64,360]{1,0:T(8,128)S(1)} %get-tuple-element.68.refs_1_, f32[64,360]{1,0:T(8,128)S(1)} %get-tuple-element.69.refs_2_, f32[64,128]{1,0:T(8,128)S(1)} %get-tuple-element.70.refs_3_, ...), custom_call_target="tpu_custom_call" | custom-call | flops 66355200 | bytes 1036800 | tf_op jit(solution)/shard_map/pallas_call | solution.py:439
  30.4 0.2 collective-permute-start.12
  30.6 0.3 shard_map.131.kept_ref
  30.9 1.0 %collective-permute-done.12.given_ref = bf16[2,64,720]{2,1,0:T(8,128)(2,1)S(1)} collective-permute-done((bf16[2,64,720]{2,1,0:T(8,128)(2,1)S(1)}, bf16[2,64,720]{2,1,0:T(8,128)(2,1)S(1)}, u32[]{:S(2)}, u32[]{:S(2)}) %collective-permute-start.12) | collective-permute-done | bytes 184352 | tf_op jit(solution)/shard_map/ppermute | solution.py:309
  32.0 1.0 %collective-permute-start.13 = (bf16[32,720]{1,0:T(8,128)(2,1)S(1)}, bf16[32,720]{1,0:T(8,128)(2,1)S(1)}, u32[]{:S(2)}, u32[]{:S(2)}) collective-permute-start(bf16[32,720]{1,0:T(8,128)(2,1)S(1)} %get-tuple-element.74), channel_id=1, source_target_pairs={{0,3},{1,2},{2,1},{3,0},{4,7},{5,6},{6,5},{7,4},{8,11},{9,10},{10,... | collective-permute-start | bytes 138248 | tf_op jit(solution)/shard_map/ppermute | solution.py:309
  33.0 0.8 %collective-permute-start.16 = (bf16[32,720]{1,0:T(8,128)(2,1)S(1)}, bf16[32,720]{1,0:T(8,128)(2,1)S(1)}, u32[]{:S(2)}, u32[]{:S(2)}) collective-permute-start(bf16[32,720]{1,0:T(8,128)(2,1)S(1)} %get-tuple-element.78), channel_id=1, source_target_pairs={{0,3},{1,2},{2,1},{3,0},{4,7},{5,6},{6,5},{7,4},{8,11},{9,10},{10,... | collective-permute-start | bytes 138248 | tf_op jit(solution)/shard_map/ppermute | solution.py:309
  33.8 2.0 %collective-permute-done.13.refs_1_ = bf16[32,720]{1,0:T(8,128)(2,1)S(1)} collective-permute-done((bf16[32,720]{1,0:T(8,128)(2,1)S(1)}, bf16[32,720]{1,0:T(8,128)(2,1)S(1)}, u32[]{:S(2)}, u32[]{:S(2)}) %collective-permute-start.13) | collective-permute-done | bytes 46112 | tf_op jit(solution)/shard_map/ppermute | solution.py:309
  35.8 1.6 %collective-permute-start.14 = (bf16[16,720]{1,0:T(8,128)(2,1)S(1)}, bf16[16,720]{1,0:T(8,128)(2,1)S(1)}, u32[]{:S(2)}, u32[]{:S(2)}) collective-permute-start(bf16[16,720]{1,0:T(8,128)(2,1)S(1)} %get-tuple-element.75), channel_id=1, source_target_pairs={{0,13},{1,12},{2,15},{3,14},{4,9},{5,8},{6,11},{7,10},{8,5},{9,4},... | collective-permute-start | bytes 69128 | tf_op jit(solution)/shard_map/ppermute | solution.py:323
  37.3 0.9 %collective-permute-start.15 = (bf16[16,720]{1,0:T(8,128)(2,1)S(1)}, bf16[16,720]{1,0:T(8,128)(2,1)S(1)}, u32[]{:S(2)}, u32[]{:S(2)}) collective-permute-start(bf16[16,720]{1,0:T(8,128)(2,1)S(1)} %get-tuple-element.76), channel_id=1, source_target_pairs={{0,9},{1,8},{2,11},{3,10},{4,13},{5,12},{6,15},{7,14},{8,1},{9,0},... | collective-permute-start | bytes 69128 | tf_op jit(solution)/shard_map/ppermute | solution.py:323
  38.3 1.9 %collective-permute-start.17 = (bf16[16,720]{1,0:T(8,128)(2,1)S(1)}, bf16[16,720]{1,0:T(8,128)(2,1)S(1)}, u32[]{:S(2)}, u32[]{:S(2)}) collective-permute-start(bf16[16,720]{1,0:T(8,128)(2,1)S(1)} %get-tuple-element.79), channel_id=1, source_target_pairs={{0,5},{1,4},{2,7},{3,6},{4,1},{5,0},{6,3},{7,2},{8,13},{9,12},{10,... | collective-permute-start | bytes 69128 | tf_op jit(solution)/shard_map/ppermute | solution.py:323
  40.2 0.9 %shard_map.135.refs_6_ = bf16[720,256]{1,0:T(8,128)(2,1)S(1)} custom-call(bf16[512,256]{1,0:T(8,128)(2,1)S(1)} %get-tuple-element.84.refs_0_, bf16[512,256]{1,0:T(8,128)(2,1)S(1)} %collective-permute-done.20.refs_1_, bf16[512,256]{1,0:T(8,128)(2,1)S(1)} %collective-permute-done.21.refs_2_, bf16[512,256]{1,0:T(8,128)(2,1)S(1)} %collective-permute-done.19.refs_3_, ...), custom_call_target="tpu_custom_call" | custom-call | flops 754974720 | bytes 2949120 | tf_op jit(solution)/shard_map/pallas_call | solution.py:446
  41.2 1.3 %collective-permute-done.15.refs_1_ = bf16[16,720]{1,0:T(8,128)(2,1)S(1)} collective-permute-done((bf16[16,720]{1,0:T(8,128)(2,1)S(1)}, bf16[16,720]{1,0:T(8,128)(2,1)S(1)}, u32[]{:S(2)}, u32[]{:S(2)}) %collective-permute-start.15) | collective-permute-done | bytes 23072 | tf_op jit(solution)/shard_map/ppermute | solution.py:323
  42.5 1.0 %shard_map.136 = bf16[720,256]{1,0:T(8,128)(2,1)} custom-call(bf16[16,720]{1,0:T(8,128)(2,1)S(1)} %collective-permute-done.14.refs_0_, bf16[16,720]{1,0:T(8,128)(2,1)S(1)} %collective-permute-done.15.refs_1_, bf16[16,720]{1,0:T(8,128)(2,1)S(1)} %collective-permute-done.17.refs_2_, bf16[16,720]{1,0:T(8,128)(2,1)S(1)} %collective-permute-done.18.refs_3_, ...), custom_call_target="tpu_custom_call" | custom-call | tf_op jit(solution)/shard_map/pallas_call | solution.py:468
  (24 shorter events, 0.1 us)
Async XLA Ops:
  0.8 7.3 %collective-permute-start = (bf16[128,256]{1,0:T(8,128)(2,1)S(1)}, bf16[128,256]{1,0:T(8,128)(2,1)S(1)}, u32[]{:S(2)}, u32[]{:S(2)}) collective-permute-start(bf16[128,256]{1,0:T(8,128)(2,1)S(1)} %slice.3), channel_id=1, source_target_pairs={{0,4},{4,8},{8,12},{12,0},{1,5},{5,9},{9,13},{13,1},{2,6},{6,10},{... | collective-permute-start | bytes 196616 | tf_op jit(solution)/shard_map/ppermute | solution.py:360
  3.9 7.3 %copy-start = (bf16[1,2880,360]{1,2,0:T(8,128)(2,1)S(1)}, bf16[1,2880,360]{1,2,0:T(8,128)(2,1)}, u32[]{:S(2)}) copy-start(bf16[1,2880,360]{1,2,0:T(8,128)(2,1)} %param.21) | copy-start | bytes 6220804
  9.3 4.2 %collective-permute-start.1 = (bf16[64,512]{1,0:T(8,128)(2,1)S(1)}, bf16[64,512]{1,0:T(8,128)(2,1)S(1)}, u32[]{:S(2)}, u32[]{:S(2)}) collective-permute-start(bf16[64,512]{1,0:T(8,128)(2,1)S(1)} %get-tuple-element.52.rows_ref), channel_id=1, source_target_pairs={{0,3},{1,2},{2,1},{3,0},{4,7},{5,6},{6,5},{7,4},{8,11},{9,10},{10,... | collective-permute-start | bytes 196616 | tf_op jit(solution)/shard_map/ppermute | solution.py:309
  9.4 5.5 %collective-permute-start.3 = (bf16[64,512]{1,0:T(8,128)(2,1)S(1)}, bf16[64,512]{1,0:T(8,128)(2,1)S(1)}, u32[]{:S(2)}, u32[]{:S(2)}) collective-permute-start(bf16[64,512]{1,0:T(8,128)(2,1)S(1)} %get-tuple-element.52.rows_ref), channel_id=1, source_target_pairs={{0,1},{1,0},{2,3},{3,2},{4,5},{5,4},{6,7},{7,6},{8,9},{9,8},{10,11... | collective-permute-start | bytes 196616 | tf_op jit(solution)/shard_map/ppermute | solution.py:309
  13.5 2.0 %collective-permute-start.2 = (bf16[64,512]{1,0:T(8,128)(2,1)S(1)}, bf16[64,512]{1,0:T(8,128)(2,1)S(1)}, u32[]{:S(2)}, u32[]{:S(2)}) collective-permute-start(bf16[64,512]{1,0:T(8,128)(2,1)S(1)} %collective-permute-done.1.refs_1_), channel_id=1, source_target_pairs={{0,1},{1,0},{2,3},{3,2},{4,5},{5,4},{6,7},{7,6},{8,9},{9,8},{10,11... | collective-permute-start | bytes 196616 | tf_op jit(solution)/shard_map/ppermute | solution.py:309
  13.6 14.5 %collective-permute-start.19 = (bf16[512,256]{1,0:T(8,128)(2,1)S(1)}, bf16[512,256]{1,0:T(8,128)(2,1)S(1)}, u32[]{:S(2)}, u32[]{:S(2)}) collective-permute-start(bf16[512,256]{1,0:T(8,128)(2,1)S(1)} %get-tuple-element.84.refs_0_), channel_id=1, source_target_pairs={{0,3},{1,2},{2,1},{3,0},{4,7},{5,6},{6,5},{7,4},{8,11},{9,10},{10,... | collective-permute-start | bytes 786440 | tf_op jit(solution)/shard_map/ppermute | solution.py:309
  15.4 4.7 %copy-start.3 = (f32[2880]{0:T(1024)S(1)}, f32[2880]{0:T(1024)}, u32[]{:S(2)}) copy-start(f32[2880]{0:T(1024)} %gain_ref.1) | copy-start | bytes 34564
  15.4 4.8 %copy-start.1 = (bf16[1,2880,360]{1,2,0:T(8,128)(2,1)S(1)}, bf16[1,2880,360]{1,2,0:T(8,128)(2,1)}, u32[]{:S(2)}) copy-start(bf16[1,2880,360]{1,2,0:T(8,128)(2,1)} %param.22) | copy-start | bytes 6220804
  15.8 5.2 %collective-permute-start.4 = (bf16[16,720]{1,0:T(8,128)(2,1)S(1)}, bf16[16,720]{1,0:T(8,128)(2,1)S(1)}, u32[]{:S(2)}, u32[]{:S(2)}) collective-permute-start(bf16[16,720]{1,0:T(8,128)(2,1)S(1)} %get-tuple-element.57), channel_id=1, source_target_pairs={{0,13},{1,12},{2,15},{3,14},{4,9},{5,8},{6,11},{7,10},{8,5},{9,4},... | collective-permute-start | bytes 69128 | tf_op jit(solution)/shard_map/ppermute | solution.py:323
  17.3 4.8 %collective-permute-start.5 = (bf16[16,720]{1,0:T(8,128)(2,1)S(1)}, bf16[16,720]{1,0:T(8,128)(2,1)S(1)}, u32[]{:S(2)}, u32[]{:S(2)}) collective-permute-start(bf16[16,720]{1,0:T(8,128)(2,1)S(1)} %get-tuple-element.58), channel_id=1, source_target_pairs={{0,9},{1,8},{2,11},{3,10},{4,13},{5,12},{6,15},{7,14},{8,1},{9,0},... | collective-permute-start | bytes 69128 | tf_op jit(solution)/shard_map/ppermute | solution.py:323
  17.3 4.8 %collective-permute-start.6 = (bf16[16,720]{1,0:T(8,128)(2,1)S(1)}, bf16[16,720]{1,0:T(8,128)(2,1)S(1)}, u32[]{:S(2)}, u32[]{:S(2)}) collective-permute-start(bf16[16,720]{1,0:T(8,128)(2,1)S(1)} %get-tuple-element.59), channel_id=1, source_target_pairs={{0,5},{1,4},{2,7},{3,6},{4,1},{5,0},{6,3},{7,2},{8,13},{9,12},{10,... | collective-permute-start | bytes 69128 | tf_op jit(solution)/shard_map/ppermute | solution.py:323
  19.6 2.5 %collective-permute-start.7 = (bf16[16,720]{1,0:T(8,128)(2,1)S(1)}, bf16[16,720]{1,0:T(8,128)(2,1)S(1)}, u32[]{:S(2)}, u32[]{:S(2)}) collective-permute-start(bf16[16,720]{1,0:T(8,128)(2,1)S(1)} %get-tuple-element.60), channel_id=1, source_target_pairs={{0,1},{1,0},{2,3},{3,2},{4,5},{5,4},{6,7},{7,6},{8,9},{9,8},{10,11... | collective-permute-start | bytes 69128 | tf_op jit(solution)/shard_map/ppermute | solution.py:323
  20.2 4.1 %copy-start.2 = (bf16[1,360,2880]{2,1,0:T(8,128)(2,1)S(1)}, bf16[1,360,2880]{2,1,0:T(8,128)(2,1)}, u32[]{:S(2)}) copy-start(bf16[1,360,2880]{2,1,0:T(8,128)(2,1)} %param.23) | copy-start | bytes 6220804
  22.2 1.4 %collective-permute-start.9 = (bf16[64,720]{1,0:T(8,128)(2,1)S(1)}, bf16[64,720]{1,0:T(8,128)(2,1)S(1)}, u32[]{:S(2)}, u32[]{:S(2)}) collective-permute-start(bf16[64,720]{1,0:T(8,128)(2,1)S(1)} %shard_map.126.mine_ref.refs_0_), channel_id=1, source_target_pairs={{0,1},{1,0},{2,3},{3,2},{4,5},{5,4},{6,7},{7,6},{8,9},{9,8},{10,11... | collective-permute-start | bytes 276488 | tf_op jit(solution)/shard_map/ppermute | solution.py:309
  22.3 4.5 %collective-permute-start.8 = (bf16[64,720]{1,0:T(8,128)(2,1)S(1)}, bf16[64,720]{1,0:T(8,128)(2,1)S(1)}, u32[]{:S(2)}, u32[]{:S(2)}) collective-permute-start(bf16[64,720]{1,0:T(8,128)(2,1)S(1)} %shard_map.126.mine_ref.refs_0_), channel_id=1, source_target_pairs={{0,3},{1,2},{2,1},{3,0},{4,7},{5,6},{6,5},{7,4},{8,11},{9,10},{10,... | collective-permute-start | bytes 276488 | tf_op jit(solution)/shard_map/ppermute | solution.py:309
  23.7 3.9 %collective-permute-start.10 = (f32[64,128]{1,0:T(8,128)S(1)}, f32[64,128]{1,0:T(8,128)S(1)}, u32[]{:S(2)}, u32[]{:S(2)}) collective-permute-start(f32[64,128]{1,0:T(8,128)S(1)} %shard_map.128.refs_3_), channel_id=1, source_target_pairs={{0,3},{1,2},{2,1},{3,0},{4,7},{5,6},{6,5},{7,4},{8,11},{9,10},{10,... | collective-permute-start | bytes 98312 | tf_op jit(solution)/shard_map/ppermute | solution.py:309
  27.6 2.0 %collective-permute-start.11 = (bf16[64,720]{1,0:T(8,128)(2,1)S(1)}, bf16[64,720]{1,0:T(8,128)(2,1)S(1)}, u32[]{:S(2)}, u32[]{:S(2)}) collective-permute-start(bf16[64,720]{1,0:T(8,128)(2,1)S(1)} %collective-permute-done.8.refs_2_), channel_id=1, source_target_pairs={{0,1},{1,0},{2,3},{3,2},{4,5},{5,4},{6,7},{7,6},{8,9},{9,8},{10,11... | collective-permute-start | bytes 276488 | tf_op jit(solution)/shard_map/ppermute | solution.py:309
  27.9 12.3 %collective-permute-start.21 = (bf16[512,256]{1,0:T(8,128)(2,1)S(1)}, bf16[512,256]{1,0:T(8,128)(2,1)S(1)}, u32[]{:S(2)}, u32[]{:S(2)}) collective-permute-start(bf16[512,256]{1,0:T(8,128)(2,1)S(1)} %get-tuple-element.84.refs_0_), channel_id=1, source_target_pairs={{0,1},{1,0},{2,3},{3,2},{4,5},{5,4},{6,7},{7,6},{8,9},{9,8},{10,11... | collective-permute-start | bytes 786440 | tf_op jit(solution)/shard_map/ppermute | solution.py:309
  28.1 12.1 %collective-permute-start.20 = (bf16[512,256]{1,0:T(8,128)(2,1)S(1)}, bf16[512,256]{1,0:T(8,128)(2,1)S(1)}, u32[]{:S(2)}, u32[]{:S(2)}) collective-permute-start(bf16[512,256]{1,0:T(8,128)(2,1)S(1)} %collective-permute-done.19.refs_3_), channel_id=1, source_target_pairs={{0,1},{1,0},{2,3},{3,2},{4,5},{5,4},{6,7},{7,6},{8,9},{9,8},{10,11... | collective-permute-start | bytes 786440 | tf_op jit(solution)/shard_map/ppermute | solution.py:309
  30.4 1.5 %collective-permute-start.12 = (bf16[2,64,720]{2,1,0:T(8,128)(2,1)S(1)}, bf16[2,64,720]{2,1,0:T(8,128)(2,1)S(1)}, u32[]{:S(2)}, u32[]{:S(2)}) collective-permute-start(bf16[2,64,720]{2,1,0:T(8,128)(2,1)S(1)} %get-tuple-element.72), channel_id=1, source_target_pairs={{0,1},{1,0},{2,3},{3,2},{4,5},{5,4},{6,7},{7,6},{8,9},{9,8},{10,11... | collective-permute-start | bytes 552968 | tf_op jit(solution)/shard_map/ppermute | solution.py:309
  32.0 3.8 %collective-permute-start.13 = (bf16[32,720]{1,0:T(8,128)(2,1)S(1)}, bf16[32,720]{1,0:T(8,128)(2,1)S(1)}, u32[]{:S(2)}, u32[]{:S(2)}) collective-permute-start(bf16[32,720]{1,0:T(8,128)(2,1)S(1)} %get-tuple-element.74), channel_id=1, source_target_pairs={{0,3},{1,2},{2,1},{3,0},{4,7},{5,6},{6,5},{7,4},{8,11},{9,10},{10,... | collective-permute-start | bytes 138248 | tf_op jit(solution)/shard_map/ppermute | solution.py:309
  33.0 5.3 %collective-permute-start.16 = (bf16[32,720]{1,0:T(8,128)(2,1)S(1)}, bf16[32,720]{1,0:T(8,128)(2,1)S(1)}, u32[]{:S(2)}, u32[]{:S(2)}) collective-permute-start(bf16[32,720]{1,0:T(8,128)(2,1)S(1)} %get-tuple-element.78), channel_id=1, source_target_pairs={{0,3},{1,2},{2,1},{3,0},{4,7},{5,6},{6,5},{7,4},{8,11},{9,10},{10,... | collective-permute-start | bytes 138248 | tf_op jit(solution)/shard_map/ppermute | solution.py:309
  35.8 5.4 %collective-permute-start.14 = (bf16[16,720]{1,0:T(8,128)(2,1)S(1)}, bf16[16,720]{1,0:T(8,128)(2,1)S(1)}, u32[]{:S(2)}, u32[]{:S(2)}) collective-permute-start(bf16[16,720]{1,0:T(8,128)(2,1)S(1)} %get-tuple-element.75), channel_id=1, source_target_pairs={{0,13},{1,12},{2,15},{3,14},{4,9},{5,8},{6,11},{7,10},{8,5},{9,4},... | collective-permute-start | bytes 69128 | tf_op jit(solution)/shard_map/ppermute | solution.py:323
  37.3 5.1 %collective-permute-start.15 = (bf16[16,720]{1,0:T(8,128)(2,1)S(1)}, bf16[16,720]{1,0:T(8,128)(2,1)S(1)}, u32[]{:S(2)}, u32[]{:S(2)}) collective-permute-start(bf16[16,720]{1,0:T(8,128)(2,1)S(1)} %get-tuple-element.76), channel_id=1, source_target_pairs={{0,9},{1,8},{2,11},{3,10},{4,13},{5,12},{6,15},{7,14},{8,1},{9,0},... | collective-permute-start | bytes 69128 | tf_op jit(solution)/shard_map/ppermute | solution.py:323
  38.3 4.2 %collective-permute-start.17 = (bf16[16,720]{1,0:T(8,128)(2,1)S(1)}, bf16[16,720]{1,0:T(8,128)(2,1)S(1)}, u32[]{:S(2)}, u32[]{:S(2)}) collective-permute-start(bf16[16,720]{1,0:T(8,128)(2,1)S(1)} %get-tuple-element.79), channel_id=1, source_target_pairs={{0,5},{1,4},{2,7},{3,6},{4,1},{5,0},{6,3},{7,2},{8,13},{9,12},{10,... | collective-permute-start | bytes 69128 | tf_op jit(solution)/shard_map/ppermute | solution.py:323
  40.2 2.3 %collective-permute-start.18 = (bf16[16,720]{1,0:T(8,128)(2,1)S(1)}, bf16[16,720]{1,0:T(8,128)(2,1)S(1)}, u32[]{:S(2)}, u32[]{:S(2)}) collective-permute-start(bf16[16,720]{1,0:T(8,128)(2,1)S(1)} %get-tuple-element.80), channel_id=1, source_target_pairs={{0,1},{1,0},{2,3},{3,2},{4,5},{5,4},{6,7},{7,6},{8,9},{9,8},{10,11... | collective-permute-start | bytes 69128 | tf_op jit(solution)/shard_map/ppermute | solution.py:323
